TPU v7x, 32 devices: a whole 2x2x4 slice. The times are simulated.
32 devices in a mesh: grp: 4 (over y, x), brick: 8 (over z, core).
Axes of the slice: x: 2, y: 2, z: 4, core: 2. Of those that a mesh axis runs over, the one named last changes fastest.
Arguments:
- positions: float32 [3, 1048576], P(None, ('grp', 'brick')), may hold values from -4 to 4
- charges: float32 [1048576], P(('grp', 'brick')), may hold values from -5 to 5
- cluster_fill: int32 [8192], P(('grp', 'brick')), may hold values from 1 to 128, as said below
- cluster_cell: int32 [8192], P(('grp', 'brick')), may hold values from 0 to 131071
- send_index: int32 [224, 32], P(('grp', 'brick')), may hold values from 0 to 255
- send_count: int32 [32, 7], P(('grp', 'brick')), may hold values from 1 to 32, as said below
- pair_local: int32 [32768], P(('grp', 'brick')), may hold values from 0 to 255
- pair_dir: int32 [32768], P(('grp', 'brick')), may hold values from 0 to 6, as said below
- pair_slot: int32 [32768], P(('grp', 'brick')), may hold values from 0 to 31
- ion_density: float32 [64, 256, 256], P('grp', 'brick'), may hold values from 0.2 to 2
- potential_prev: float32 [64, 256, 256], P('grp', 'brick'), may hold values from -6 to 6
- screening: float32 [64, 256, 256], P('grp', 'brick'), may hold values from 0.05 to 0.5
Outputs:
- forces: float32 [3, 1048576], P(None, ('grp', 'brick'))
- potential: float32 [64, 256, 256], P('grp', 'brick')
- ion_next: float32 [64, 256, 256], P('grp', 'brick')
Inputs may be any that keep to these rules, and one draw needn't show every extreme that they name: `cluster_fill`: live particles of a cluster; later slots are padding; some cluster is full. `send_count`: every device sends 32 live slots in some direction. `send_index`: local cluster indices; row e * 7 + k lists what device e sends to the device at minus the offset of direction k. `pair_local`: local cluster indices. `pair_dir`: a direction never names a device outside the room. `pair_slot`: slot indices; a slot at or past the sender's count carries no charge. `cluster_cell`: cell indices within a device's block.
All inputs are finite; a program needn't handle non-finite values.
Results may differ from a plain program's by a relative error of at most 0.0001.
Values sent between devices are 32-bit elements; how exact they have to be, the bound alone decides.
No kernel may reach another device: no remote copies, remote signals or barrier semaphores. Data moves between devices by JAX's collectives and lax.ppermute only.
A program may use at most 192 MiB of HBM per device.

v0:
```python
import math

import jax
import jax.numpy as jnp
from jax import lax
from jax.sharding import PartitionSpec as P

SWEEPS = 4


coulomb_scale = 0.02
softening = 0.1
field_scale = 0.5
deposit_scale = 0.2
lowest_eig = 0.01
highest_eig = 1.99
mobility = 0.3
diffusion = 0.2
time_step = 0.2


def extended(shard, sides, width):
    for axis, dim in sides:
        devices, length = (lax.axis_size(axis), shard.shape[dim])
        up = [(i, (i + 1) % devices) for i in range(devices - 1)]
        down = [(j, i) for i, j in up]
        last = lax.slice_in_dim(shard, length - width, length, axis=dim)
        initial = lax.slice_in_dim(shard, 0, width, axis=dim)
        before = lax.ppermute(last, axis, up)
        after = lax.ppermute(initial, axis, down)
        shard = jnp.concatenate([before, shard, after], axis=dim)
    return shard


def passed_along(shard, axis, by):
    devices = lax.axis_size(axis)
    pairs = [(i, i + by) for i in range(devices) if 0 <= i + by < devices]
    return lax.ppermute(shard, axis, pairs)


def stencil_core(padded, center, screen):
    beside = padded[2:, 1:-1, 1:-1] + padded[:-2, 1:-1, 1:-1]
    beside = beside + padded[1:-1, 2:, 1:-1] + padded[1:-1, :-2, 1:-1]
    beside = beside + padded[1:-1, 1:-1, 2:] + padded[1:-1, 1:-1, :-2]
    return (6.0 + screen) * center - beside


def operate_rim(field, screen):
    rimmed = extended(field, (("grp", 0), ("brick", 1)), 1)
    padded = jnp.pad(rimmed, ((0, 0), (0, 0), (1, 1)))
    return stencil_core(padded, field, screen)


def chebyshev(start, rhs, screen, operate, inside):
    middle = 0.5 * (highest_eig + lowest_eig)
    spread = 0.5 * (highest_eig - lowest_eig)
    ratio_ms = middle / spread
    weight_now = 1.0 / ratio_ms
    inverse = 1.0 / (6.0 + screen)
    solution = start
    resid = rhs - operate(solution, screen)
    update = inside * (inverse * resid / middle)
    for turn in range(SWEEPS):
        solution = solution + update
        if turn + 1 < SWEEPS:
            resid = resid - operate(update, screen)
            weight_next = 1.0 / (2.0 * ratio_ms - weight_now)
            update = inside * (
                weight_next * weight_now * update + 2.0 * weight_next / spread * (inverse * resid)
            )
            weight_now = weight_next
    return solution


def tile_forces(own, other):
    diff = own[:, :3, :, None] - other[:, :3, None, :]
    dist = jnp.sum(diff * diff, axis=1) + softening
    weight = coulomb_scale * own[:, 3, :, None] * other[:, 3, None, :] / (dist * jnp.sqrt(dist))
    pull = diff * weight[:, None]
    return (jnp.sum(pull, axis=3), jnp.sum(pull, axis=2))


def face_div(pot, ions, axis):
    inner = [slice(1, -1), slice(1, -1), slice(1, -1)]
    inner[axis] = slice(None)
    pot = pot[tuple(inner)]
    ions = ions[tuple(inner)]

    def upper(arr):
        return lax.slice_in_dim(arr, 1, arr.shape[axis], axis=axis)

    def lower(arr):
        return lax.slice_in_dim(arr, 0, arr.shape[axis] - 1, axis=axis)

    speed = -mobility * (upper(pot) - lower(pot))
    flux = (
        jnp.maximum(speed, 0.0) * lower(ions)
        + jnp.minimum(speed, 0.0) * upper(ions)
        - diffusion * (upper(ions) - lower(ions))
    )
    return upper(flux) - lower(flux)


def field_of(padded):
    along_x = -(padded[2:, 1:-1, 1:-1] - padded[:-2, 1:-1, 1:-1]) * 0.5
    along_y = -(padded[1:-1, 2:, 1:-1] - padded[1:-1, :-2, 1:-1]) * 0.5
    along_z = -(padded[1:-1, 1:-1, 2:] - padded[1:-1, 1:-1, :-2]) * 0.5
    return jnp.stack([along_x, along_y, along_z])


def shards(
    positions,
    charges,
    cluster_fill,
    cluster_cell,
    send_index,
    send_count,
    pair_local,
    pair_dir,
    pair_slot,
    ion_density,
    potential_prev,
    screening,
):
    clusters = cluster_fill.shape[0]
    psize = charges.shape[0] // clusters
    directions = send_index.shape[0]
    slots = send_index.shape[1]
    lanes = jnp.arange(psize, dtype=jnp.int32)
    qmask = charges.reshape(clusters, psize) * (lanes[None, :] < cluster_fill[:, None]).astype(
        jnp.float32
    )
    cluster_data = jnp.concatenate(
        [positions.reshape(3, clusters, psize).transpose(1, 0, 2), qmask[:, None, :]], axis=1
    )
    cells_x, cells_y, cells_z = ion_density.shape
    deposit = (
        jnp.zeros(cells_x * cells_y * cells_z, jnp.float32)
        .at[cluster_cell]
        .add(jnp.sum(qmask, axis=1))
    )
    rhs = ion_density + deposit_scale * deposit.reshape(cells_x, cells_y, cells_z)
    pairs = pair_local.shape[0]
    slot_ids = jnp.arange(slots, dtype=jnp.int32)
    slot_live = (slot_ids[None, :] < send_count.reshape(directions, 1)).astype(jnp.float32)
    outgoing = cluster_data[send_index]
    outgoing = jnp.concatenate(
        [outgoing[:, :, :3], (outgoing[:, :, 3] * slot_live[:, :, None])[:, :, None]], axis=2
    )
    pieces = [outgoing[0]]
    for offset in (-1, 1, -2, 2):
        pieces.append(passed_along(outgoing[len(pieces)], "brick", -offset))
    for offset in (-1, 1):
        pieces.append(passed_along(outgoing[len(pieces)], "grp", -offset))
    arrived = jnp.stack(pieces).reshape(directions * slots, 4, psize)
    partner_row = pair_dir * slots + pair_slot
    block = math.gcd(pairs, 32)

    def visit(carry, items):
        own_force, react = carry
        own_rows, other_rows = items
        own = cluster_data[own_rows]
        other = arrived[other_rows]
        pull_own, pull_other = tile_forces(own, other)
        return ((own_force.at[own_rows].add(pull_own), react.at[other_rows].add(-pull_other)), None)

    start_carry = (
        jnp.zeros((clusters, 3, psize), jnp.float32),
        jnp.zeros((directions * slots, 3, psize), jnp.float32),
    )
    (own_force, react), _ = lax.scan(
        visit, start_carry, (pair_local.reshape(-1, block), partner_row.reshape(-1, block))
    )
    react = react.reshape(directions, slots, 3, psize)
    backs = [react[0]]
    for offset in (-1, 1, -2, 2):
        backs.append(passed_along(react[len(backs)], "brick", offset))
    for offset in (-1, 1):
        backs.append(passed_along(react[len(backs)], "grp", offset))
    returned = jnp.stack(backs).reshape(directions * slots, 3, psize)
    coulomb = own_force.at[send_index.reshape(-1)].add(returned)
    potential = chebyshev(potential_prev, rhs, screening, operate_rim, 1.0)
    rimmed = extended(jnp.stack([potential, ion_density]), (("grp", 1), ("brick", 2)), 1)
    rimmed = jnp.pad(rimmed, ((0, 0), (0, 0), (0, 0), (1, 1)))
    padded_pot = rimmed[0]
    padded_ion = rimmed[1]
    ion_next = ion_density - time_step * (
        face_div(padded_pot, padded_ion, 0)
        + face_div(padded_pot, padded_ion, 1)
        + face_div(padded_pot, padded_ion, 2)
    )
    ecell = field_of(padded_pot).reshape(3, -1)[:, cluster_cell]
    forces = coulomb.transpose(1, 0, 2) + field_scale * qmask[None] * ecell[:, :, None]
    return (forces.reshape(3, -1), potential, ion_next)


def solution(mesh):
    in_specs = (
        P(None, ("grp", "brick")),
        P(("grp", "brick")),
        P(("grp", "brick")),
        P(("grp", "brick")),
        P(("grp", "brick"), None),
        P(("grp", "brick"), None),
        P(("grp", "brick")),
        P(("grp", "brick")),
        P(("grp", "brick")),
        P("grp", "brick", None),
        P("grp", "brick", None),
        P("grp", "brick", None),
    )
    out_specs = (P(None, ("grp", "brick")), P("grp", "brick", None), P("grp", "brick", None))
    return jax.shard_map(shards, mesh=mesh, in_specs=in_specs, out_specs=out_specs, check_vma=False)
```

profile of v0, /device:TPU:13, one launch (start us, length us, event | category | flops | bytes accessed | tf_op | source)
XLA Modules:
  0.0 649.1 jit_solution(1858514037522947903)
XLA Ops:
  1.4 3.1 collective-permute-start.13
  4.5 3.1 collective-permute-start.12
  15.1 4.5 collective-permute-start
  21.5 3.2 collective-permute-start.2
  27.8 2.7 collective-permute-start.14
  30.6 3.1 collective-permute-start.15
  36.0 2.5 collective-permute-start.3
  38.5 2.2 collective-permute-start.4
  42.5 4.0 collective-permute-start.5
  50.1 3.4 collective-permute-start.17
  55.2 466.6 %while.12 = (s32[]{:T(128)}, f32[256,3,128]{2,1,0:T(4,128)S(1)}, f32[224,3,128]{2,1,0:T(4,128)S(1)}, s32[32,32]{1,0:T(8,128)}, f32[256,4,128]{2,1,0:T(4,128)}, /...) while((s32[]{:T(128)}, f32[256,3,128]{2,1,0:T(4,128)S(1)}, f32[224,3,128]{2,1,0:T(4,128)S(1)}, ...), condition=%wide.region_6.0_spmd, body=%wide.region_0.6_spmd.sunk | while | flops 12601538 | bytes 9446745 | solution.py:171
  62.5 4.0 fusion.80
  77.1 4.0 fusion.80
  91.7 4.0 fusion.80
  106.2 4.0 fusion.80
  120.8 4.0 fusion.80
  135.4 4.0 fusion.80
  150.0 4.0 fusion.80
  164.6 4.0 fusion.80
  179.2 4.0 fusion.80
  193.8 4.0 fusion.80
  208.4 4.0 fusion.80
  222.9 4.0 fusion.80
  237.5 4.0 fusion.80
  252.1 4.0 fusion.80
  266.7 4.0 fusion.80
  281.3 4.0 fusion.80
  295.9 4.0 fusion.80
  310.4 4.0 fusion.80
  325.0 4.0 fusion.80
  339.6 4.0 fusion.80
  354.2 4.0 fusion.80
  368.7 4.0 fusion.80
  383.3 4.0 fusion.80
  397.9 4.0 fusion.80
  412.5 4.0 fusion.80
  427.1 4.0 fusion.80
  441.6 4.0 fusion.80
  456.2 4.0 fusion.80
  470.8 4.0 fusion.80
  485.4 4.0 fusion.80
  499.9 4.0 fusion.80
  514.5 4.0 fusion.80
  522.0 2.9 collective-permute-start.18
  524.9 2.7 collective-permute-start.19
  529.6 3.6 collective-permute-start.7
  533.2 2.5 collective-permute-start.8
  535.7 2.8 collective-permute-start.9
  540.4 2.8 collective-permute-start.20
  543.2 2.5 collective-permute-start.21
  545.7 3.7 collective-permute-start.10
  549.5 2.5 collective-permute-start.22
  552.1 3.0 collective-permute-start.23
  558.1 4.3 collective-permute-start.24
  564.4 3.6 collective-permute-done.25
  568.0 3.0 collective-permute-start.26
  571.0 2.9 collective-permute-start.27
  578.3 4.3 collective-permute-start.29
  583.9 5.3 collective-permute-start.30
  591.3 8.2 %scatter_fusion.2 = f32[256,3,128]{2,1,0:T(4,128)S(1)} fusion(f32[256,3,128]{2,1,0:T(4,128)S(1)} %get-tuple-element.41, s32[224]{0:T(256)S(1)} %bitcast.110, f32[224,3,128]{2,1,0:T(4,128)S(1)} %bitcast.105), kind=kCustom, calls=%fused_computation.6 | custom fusion | flops 86016 | bytes 1033088 | tf_op jit(solution)/shard_map/scatter-add | solution.py:181
  609.4 2.8 pad_maximum_fusion
  612.2 30.5 %copy.22 = f32[3,131072]{0,1:T(8,128)} copy(f32[3,131072]{1,0:T(4,128)S(1)} %pad_maximum_fusion) | data formatting | bytes 3145728 | tf_op jit(solution)/shard_map/stack | solution.py:108
  642.7 2.5 gather_fusion.3
  645.2 2.8 fusion.13
  (538 shorter events, 386.0 us)
Async XLA Ops:
  1.4 26.3 %collective-permute-start.13 = (f32[1,32,256]{2,1,0:T(8,128)S(1)}, f32[1,32,256]{2,1,0:T(8,128)S(1)}, u32[]{:S(2)}, u32[]{:S(2)}) collective-permute-start(f32[1,32,256]{2,1,0:T(8,128)S(1)} %get-tuple-element.96), channel_id=1, source_target_pairs={{0,8},{8,16},{16,24},{1,9},{9,17},{17,25},{2,10},{10,18},{18,26},{... | collective-permute-start | bytes 98312 | tf_op jit(solution)/shard_map/ppermute | solution.py:29
  4.5 23.3 %collective-permute-start.12 = (f32[1,32,256]{2,1,0:T(8,128)S(1)}, f32[1,32,256]{2,1,0:T(8,128)S(1)}, u32[]{:S(2)}, u32[]{:S(2)}) collective-permute-start(f32[1,32,256]{2,1,0:T(8,128)S(1)} %get-tuple-element.95), channel_id=1, source_target_pairs={{8,0},{16,8},{24,16},{9,1},{17,9},{25,17},{10,2},{18,10},{26,18},{... | collective-permute-start | bytes 98312 | tf_op jit(solution)/shard_map/ppermute | solution.py:30
  12.9 12.5 %copy-start.9 = (f32[256,4,128]{2,1,0:T(4,128)}, f32[256,4,128]{2,1,0:T(4,128)S(1)}, u32[]{:S(2)}) copy-start(f32[256,4,128]{2,1,0:T(4,128)S(1)} %pad_maximum_fusion.29) | copy-start | bytes 1572868
  12.9 11.8 %copy-start.12 = (f32[32768]{0:T(1024)S(1)}, f32[32768]{0:T(1024)}, u32[]{:S(2)}) copy-start(f32[32768]{0:T(1024)} %param.15) | copy-start | bytes 393220
  12.9 11.8 %copy-start.20 = (s32[256]{0:T(256)S(1)}, s32[256]{0:T(256)}, u32[]{:S(2)}) copy-start(s32[256]{0:T(256)} %param.16) | copy-start | bytes 3076
  15.1 12.5 %copy-start.22 = (s32[1024]{0:T(1024)S(1)}, s32[1024]{0:T(1024)}, u32[]{:S(2)}) copy-start(s32[1024]{0:T(1024)} %param.22) | copy-start | bytes 12292
  15.1 12.5 %copy-start.23 = (s32[1024]{0:T(1024)S(1)}, s32[1024]{0:T(1024)}, u32[]{:S(2)}) copy-start(s32[1024]{0:T(1024)} %param.21) | copy-start | bytes 12292
  15.1 12.6 %copy-start.19 = (s32[7,32]{1,0:T(8,128)S(1)}, s32[7,32]{1,0:T(8,128)}, u32[]{:S(2)}) copy-start(s32[7,32]{1,0:T(8,128)} %param.18) | copy-start | bytes 2692
  15.1 12.7 %copy-start.5 = (f32[16,32,256]{2,1,0:T(8,128)S(1)}, f32[16,32,256]{2,1,0:T(8,128)}, u32[]{:S(2)}) copy-start(f32[16,32,256]{2,1,0:T(8,128)} %param.24) | copy-start | bytes 1572868
  15.1 27.4 %collective-permute-start = (f32[32,4,128]{2,1,0:T(4,128)}, f32[32,4,128]{2,1,0:T(4,128)}, u32[]{:S(2)}, u32[]{:S(2)}) collective-permute-start(f32[32,4,128]{2,1,0:T(4,128)} %get-tuple-element.84), channel_id=1, source_target_pairs={{0,1},{1,2},{2,3},{3,4},{4,5},{5,6},{6,7},{8,9},{9,10},{10,11},{11... | collective-permute-start | bytes 196616 | tf_op jit(solution)/shard_map/ppermute | solution.py:38
  19.5 27.8 %collective-permute-start.1 = (f32[32,4,128]{2,1,0:T(4,128)}, f32[32,4,128]{2,1,0:T(4,128)}, u32[]{:S(2)}, u32[]{:S(2)}) collective-permute-start(f32[32,4,128]{2,1,0:T(4,128)} %get-tuple-element.85), channel_id=1, source_target_pairs={{1,0},{2,1},{3,2},{4,3},{5,4},{6,5},{7,6},{9,8},{10,9},{11,10},{12... | collective-permute-start | bytes 196616 | tf_op jit(solution)/shard_map/ppermute | solution.py:38
  21.5 28.7 %collective-permute-start.2 = (f32[32,4,128]{2,1,0:T(4,128)}, f32[32,4,128]{2,1,0:T(4,128)}, u32[]{:S(2)}, u32[]{:S(2)}) collective-permute-start(f32[32,4,128]{2,1,0:T(4,128)} %get-tuple-element.86), channel_id=1, source_target_pairs={{0,2},{1,3},{2,4},{3,5},{4,6},{5,7},{8,10},{9,11},{10,12},{11,13},... | collective-permute-start | bytes 196616 | tf_op jit(solution)/shard_map/ppermute | solution.py:38
  27.7 7.6 %copy-start.24 = (s32[1024]{0:T(1024)S(1)}, s32[1024]{0:T(1024)}, u32[]{:S(2)}) copy-start(s32[1024]{0:T(1024)} %param.20) | copy-start | bytes 12292
  27.8 8.1 %collective-permute-start.14 = (f32[18,1,256]{2,1,0:T(1,128)S(1)}, f32[18,1,256]{2,1,0:T(1,128)S(1)}, u32[]{:S(2)}, u32[]{:S(2)}) collective-permute-start(f32[18,1,256]{2,1,0:T(1,128)S(1)} %get-tuple-element.81), channel_id=1, source_target_pairs={{1,0},{2,1},{3,2},{4,3},{5,4},{6,5},{7,6},{9,8},{10,9},{11,10},{12... | collective-permute-start | bytes 55304 | tf_op jit(solution)/shard_map/ppermute | solution.py:30
  30.6 7.9 %collective-permute-start.15 = (f32[18,1,256]{2,1,0:T(1,128)S(1)}, f32[18,1,256]{2,1,0:T(1,128)S(1)}, u32[]{:S(2)}, u32[]{:S(2)}) collective-permute-start(f32[18,1,256]{2,1,0:T(1,128)S(1)} %get-tuple-element.80), channel_id=1, source_target_pairs={{0,1},{1,2},{2,3},{3,4},{4,5},{5,6},{6,7},{8,9},{9,10},{10,11},{11... | collective-permute-start | bytes 55304 | tf_op jit(solution)/shard_map/ppermute | solution.py:29
  35.2 6.0 copy-start
  35.2 6.0 copy-start.2
  36.0 5.3 copy-start.10
  36.0 18.4 %collective-permute-start.3 = (f32[32,4,128]{2,1,0:T(4,128)S(1)}, f32[32,4,128]{2,1,0:T(4,128)S(1)}, u32[]{:S(2)}, u32[]{:S(2)}) collective-permute-start(f32[32,4,128]{2,1,0:T(4,128)S(1)} %get-tuple-element.87), channel_id=1, source_target_pairs={{2,0},{3,1},{4,2},{5,3},{6,4},{7,5},{10,8},{11,9},{12,10},{13,11},... | collective-permute-start | bytes 196616 | tf_op jit(solution)/shard_map/ppermute | solution.py:38
  38.5 15.9 %collective-permute-start.4 = (f32[32,4,128]{2,1,0:T(4,128)S(1)}, f32[32,4,128]{2,1,0:T(4,128)S(1)}, u32[]{:S(2)}, u32[]{:S(2)}) collective-permute-start(f32[32,4,128]{2,1,0:T(4,128)S(1)} %get-tuple-element.88), channel_id=1, source_target_pairs={{0,8},{8,16},{16,24},{1,9},{9,17},{17,25},{2,10},{10,18},{18,26},{... | collective-permute-start | bytes 196616 | tf_op jit(solution)/shard_map/ppermute | solution.py:38
  41.3 5.2 copy-start.13
  41.8 498.0 %copy-start.7 = (f32[16,32,256]{2,1,0:T(8,128)}, f32[16,32,256]{2,1,0:T(8,128)S(1)}, u32[]{:S(2)}) copy-start(f32[16,32,256]{2,1,0:T(8,128)S(1)} %get-tuple-element.62) | copy-start | bytes 1572868
  42.5 11.9 %collective-permute-start.5 = (f32[32,4,128]{2,1,0:T(4,128)S(1)}, f32[32,4,128]{2,1,0:T(4,128)S(1)}, u32[]{:S(2)}, u32[]{:S(2)}) collective-permute-start(f32[32,4,128]{2,1,0:T(4,128)S(1)} %get-tuple-element.82), channel_id=1, source_target_pairs={{8,0},{16,8},{24,16},{9,1},{17,9},{25,17},{10,2},{18,10},{26,18},{... | collective-permute-start | bytes 196616 | tf_op jit(solution)/shard_map/ppermute | solution.py:38
  47.4 474.6 %collective-permute-start.16 = (f32[1,32,256]{2,1,0:T(8,128)}, f32[1,32,256]{2,1,0:T(8,128)S(1)}, u32[]{:S(2)}, u32[]{:S(2)}) collective-permute-start(f32[1,32,256]{2,1,0:T(8,128)} %get-tuple-element.94), channel_id=1, source_target_pairs={{8,0},{16,8},{24,16},{9,1},{17,9},{25,17},{10,2},{18,10},{26,18},{... | collective-permute-start | bytes 98312 | tf_op jit(solution)/shard_map/ppermute | solution.py:30
  50.1 471.8 %collective-permute-start.17 = (f32[1,32,256]{2,1,0:T(8,128)}, f32[1,32,256]{2,1,0:T(8,128)S(1)}, u32[]{:S(2)}, u32[]{:S(2)}) collective-permute-start(f32[1,32,256]{2,1,0:T(8,128)} %get-tuple-element.93), channel_id=1, source_target_pairs={{0,8},{8,16},{16,24},{1,9},{9,17},{17,25},{2,10},{10,18},{18,26},{... | collective-permute-start | bytes 98312 | tf_op jit(solution)/shard_map/ppermute | solution.py:29
  54.5 0.8 copy-start.14
  521.9 2.9 copy-start.15
  522.0 2.9 copy-start.17
  522.0 13.7 %collective-permute-start.18 = (f32[18,1,256]{2,1,0:T(1,128)S(1)}, f32[18,1,256]{2,1,0:T(1,128)S(1)}, u32[]{:S(2)}, u32[]{:S(2)}) collective-permute-start(f32[18,1,256]{2,1,0:T(1,128)S(1)} %get-tuple-element.79), channel_id=1, source_target_pairs={{1,0},{2,1},{3,2},{4,3},{5,4},{6,5},{7,6},{9,8},{10,9},{11,10},{12... | collective-permute-start | bytes 55304 | tf_op jit(solution)/shard_map/ppermute | solution.py:30
  524.9 13.6 %collective-permute-start.19 = (f32[18,1,256]{2,1,0:T(1,128)S(1)}, f32[18,1,256]{2,1,0:T(1,128)S(1)}, u32[]{:S(2)}, u32[]{:S(2)}) collective-permute-start(f32[18,1,256]{2,1,0:T(1,128)S(1)} %get-tuple-element.78), channel_id=1, source_target_pairs={{0,1},{1,2},{2,3},{3,4},{4,5},{5,6},{6,7},{8,9},{9,10},{10,11},{11... | collective-permute-start | bytes 55304 | tf_op jit(solution)/shard_map/ppermute | solution.py:29
  527.6 12.2 %copy-start.16 = (f32[1,32,256]{2,1,0:T(8,128)S(1)}, f32[1,32,256]{2,1,0:T(8,128)}, u32[]{:S(2)}) copy-start(f32[1,32,256]{2,1,0:T(8,128)} %copy-done.15) | copy-start | bytes 98308
  527.6 12.2 %copy-start.18 = (f32[1,32,256]{2,1,0:T(8,128)S(1)}, f32[1,32,256]{2,1,0:T(8,128)}, u32[]{:S(2)}) copy-start(f32[1,32,256]{2,1,0:T(8,128)} %copy-done.17) | copy-start | bytes 98308
  527.7 15.6 %collective-permute-start.6 = (f32[32,3,128]{2,1,0:T(4,128)S(1)}, f32[32,3,128]{2,1,0:T(4,128)S(1)}, u32[]{:S(2)}, u32[]{:S(2)}) collective-permute-start(f32[32,3,128]{2,1,0:T(4,128)S(1)} %get-tuple-element.102), channel_id=1, source_target_pairs={{1,0},{2,1},{3,2},{4,3},{5,4},{6,5},{7,6},{9,8},{10,9},{11,10},{12... | collective-permute-start | bytes 147464 | tf_op jit(solution)/shard_map/ppermute | solution.py:38
  529.6 22.5 %collective-permute-start.7 = (f32[32,3,128]{2,1,0:T(4,128)S(1)}, f32[32,3,128]{2,1,0:T(4,128)S(1)}, u32[]{:S(2)}, u32[]{:S(2)}) collective-permute-start(f32[32,3,128]{2,1,0:T(4,128)S(1)} %get-tuple-element.101), channel_id=1, source_target_pairs={{0,1},{1,2},{2,3},{3,4},{4,5},{5,6},{6,7},{8,9},{9,10},{10,11},{11... | collective-permute-start | bytes 147464 | tf_op jit(solution)/shard_map/ppermute | solution.py:38
  533.2 29.1 %collective-permute-start.8 = (f32[32,3,128]{2,1,0:T(4,128)S(1)}, f32[32,3,128]{2,1,0:T(4,128)S(1)}, u32[]{:S(2)}, u32[]{:S(2)}) collective-permute-start(f32[32,3,128]{2,1,0:T(4,128)S(1)} %get-tuple-element.100), channel_id=1, source_target_pairs={{2,0},{3,1},{4,2},{5,3},{6,4},{7,5},{10,8},{11,9},{12,10},{13,11},... | collective-permute-start | bytes 147464 | tf_op jit(solution)/shard_map/ppermute | solution.py:38
  535.7 38.1 %collective-permute-start.9 = (f32[32,3,128]{2,1,0:T(4,128)S(1)}, f32[32,3,128]{2,1,0:T(4,128)S(1)}, u32[]{:S(2)}, u32[]{:S(2)}) collective-permute-start(f32[32,3,128]{2,1,0:T(4,128)S(1)} %get-tuple-element.99), channel_id=1, source_target_pairs={{0,2},{1,3},{2,4},{3,5},{4,6},{5,7},{8,10},{9,11},{10,12},{11,13},... | collective-permute-start | bytes 147464 | tf_op jit(solution)/shard_map/ppermute | solution.py:38
  540.4 5.3 collective-permute-start.20
  543.2 6.2 collective-permute-start.21
  545.7 36.8 %collective-permute-start.10 = (f32[32,3,128]{2,1,0:T(4,128)S(1)}, f32[32,3,128]{2,1,0:T(4,128)S(1)}, u32[]{:S(2)}, u32[]{:S(2)}) collective-permute-start(f32[32,3,128]{2,1,0:T(4,128)S(1)} %get-tuple-element.98), channel_id=1, source_target_pairs={{8,0},{16,8},{24,16},{9,1},{17,9},{25,17},{10,2},{18,10},{26,18},{... | collective-permute-start | bytes 147464 | tf_op jit(solution)/shard_map/ppermute | solution.py:38
  549.5 5.6 collective-permute-start.22
  552.1 5.0 collective-permute-start.23
  555.1 36.1 %collective-permute-start.11 = (f32[32,3,128]{2,1,0:T(4,128)S(1)}, f32[32,3,128]{2,1,0:T(4,128)S(1)}, u32[]{:S(2)}, u32[]{:S(2)}) collective-permute-start(f32[32,3,128]{2,1,0:T(4,128)S(1)} %get-tuple-element.97), channel_id=1, source_target_pairs={{0,8},{8,16},{16,24},{1,9},{9,17},{17,25},{2,10},{10,18},{18,26},{... | collective-permute-start | bytes 147464 | tf_op jit(solution)/shard_map/ppermute | solution.py:38
  558.1 6.3 collective-permute-start.24
  562.4 5.6 collective-permute-start.25
  564.3 10.9 %copy-start.6 = (f32[16,32,256]{2,1,0:T(8,128)S(1)}, f32[16,32,256]{2,1,0:T(8,128)}, u32[]{:S(2)}) copy-start(f32[16,32,256]{2,1,0:T(8,128)} %param.24) | copy-start | bytes 1572868
  564.4 10.9 %copy-start.8 = (f32[16,32,256]{2,1,0:T(8,128)S(1)}, f32[16,32,256]{2,1,0:T(8,128)}, u32[]{:S(2)}) copy-start(f32[16,32,256]{2,1,0:T(8,128)} %copy-done.7) | copy-start | bytes 1572868
  568.0 5.9 collective-permute-start.26
  571.0 3.7 collective-permute-start.27
  576.3 23.2 %copy-start.1 = (f32[16,32,256]{2,1,0:T(8,128)}, f32[16,32,256]{2,1,0:T(8,128)S(1)}, u32[]{:S(2)}) copy-start(f32[16,32,256]{2,1,0:T(8,128)S(1)} %fusion.26) | copy-start | bytes 1572868
  576.3 14.9 %copy-start.21 = (s32[224,1]{0,1:T(1,128)S(1)}, s32[224,1]{0,1:T(1,128)}, u32[]{:S(2)}) copy-start(s32[224,1]{0,1:T(1,128)} %compare_select_fusion.4) | copy-start | bytes 2692
  576.4 6.2 collective-permute-start.28
  578.3 5.6 collective-permute-start.29
  583.9 15.6 %collective-permute-start.30 = (f32[2,18,1,256]{3,2,1,0:T(1,128)S(1)}, f32[2,18,1,256]{3,2,1,0:T(1,128)S(1)}, u32[]{:S(2)}, u32[]{:S(2)}) collective-permute-start(f32[2,18,1,256]{3,2,1,0:T(1,128)S(1)} %get-tuple-element.67), channel_id=1, source_target_pairs={{0,1},{1,2},{2,3},{3,4},{4,5},{5,6},{6,7},{8,9},{9,10},{10,11},{11... | collective-permute-start | bytes 110600 | tf_op jit(solution)/shard_map/ppermute | solution.py:29
  589.3 10.2 %collective-permute-start.31 = (f32[2,18,1,256]{3,2,1,0:T(1,128)S(1)}, f32[2,18,1,256]{3,2,1,0:T(1,128)S(1)}, u32[]{:S(2)}, u32[]{:S(2)}) collective-permute-start(f32[2,18,1,256]{3,2,1,0:T(1,128)S(1)} %get-tuple-element.68), channel_id=1, source_target_pairs={{1,0},{2,1},{3,2},{4,3},{5,4},{6,5},{7,6},{9,8},{10,9},{11,10},{12... | collective-permute-start | bytes 110600 | tf_op jit(solution)/shard_map/ppermute | solution.py:30
  599.5 1.0 copy-start.3
  645.1 2.8 copy-start.4
  645.2 2.8 copy-start.11
where the time goes:
time: 657 us; the launch traced here: 649 us
  other arithmetic  394 us (60%)
  local copies, waits for them, and re-layouts  151 us (23%)
  starting transfers between devices  93.9 us (14%)
    reduce_sum x32, other arithmetic, tile_forces(): return (jnp.sum(pull, axis=3), jnp.sum(pull, axis=2))  128 us
    reduce_sum x32, other arithmetic, tile_forces(): dist = jnp.sum(diff * diff, axis=1) + softening  66 us
    gather x32, local copies, waits for them, and re-layouts, visit(): own = cluster_data[own_rows]  52.9 us
    scatter-add x32, other arithmetic, visit(): react.at[other_rows].add(-pull_other)  52.5 us
    scatter-add x32, other arithmetic, visit(): own_force.at[own_rows].add(pull_own)  52.5 us
    gather x32, local copies, waits for them, and re-layouts, visit(): other = arrived[other_rows]  52.1 us
    div x32, other arithmetic, tile_forces(): coulomb_scale * own[:, 3, :, None] * other[:, 3, None, :]  35.6 us
    ppermute x12, starting transfers between devices, passed_along(): return lax.ppermute(shard, axis, pairs)  34.7 us
  transfers between devices with their start and end apart: 32, of which 3 were waited for; matrix products, arithmetic and copies ran while one was open for 76% of the time, Pallas kernels for 0%

commit v1 on v0

--- a/solution.py
+++ b/solution.py
@@ -1,11 +1,12 @@
-import math
-
 import jax
 import jax.numpy as jnp
 from jax import lax
+from jax.experimental import pallas as pl
+from jax.experimental.pallas import tpu as pltpu
 from jax.sharding import PartitionSpec as P
 
 SWEEPS = 4
+UNROLL = 4
 
 
 coulomb_scale = 0.02
@@ -72,12 +73,195 @@
     return solution
 
 
-def tile_forces(own, other):
-    diff = own[:, :3, :, None] - other[:, :3, None, :]
-    dist = jnp.sum(diff * diff, axis=1) + softening
-    weight = coulomb_scale * own[:, 3, :, None] * other[:, 3, None, :] / (dist * jnp.sqrt(dist))
-    pull = diff * weight[:, None]
-    return (jnp.sum(pull, axis=3), jnp.sum(pull, axis=2))
+def split3(value):
+    first = value.astype(jnp.bfloat16).astype(jnp.float32)
+    rest = value - first
+    second = rest.astype(jnp.bfloat16).astype(jnp.float32)
+    third = (rest - second).astype(jnp.bfloat16).astype(jnp.float32)
+    return (first, second, third)
+
+
+def moment_rows(comps, charge, rows_ref, base):
+    for part, charged in enumerate((*comps, None)):
+        pieces = split3(charge if charged is None else charge * charged)
+        for level, piece in enumerate(pieces):
+            rows_ref[pl.ds(base + 4 * level + part, 8, stride=16), :] = piece
+
+
+def pair_kernel(
+    own_rows_ref,
+    other_rows_ref,
+    own_ref,
+    other_ref,
+    own_out_ref,
+    other_out_ref,
+    near_ref,
+    far_ref,
+    own_moment_ref,
+    other_moment_ref,
+    own_sum_ref,
+    other_sum_ref,
+    stage_ref,
+):
+    clusters = own_ref.shape[0] // 4
+    others = other_ref.shape[0] // 4
+    pairs = own_rows_ref.shape[0]
+    ones = jnp.ones((8, 128), jnp.float32)
+    zeros = jnp.zeros((8, 128), jnp.float32)
+
+    def components(data_ref, start):
+        return [data_ref[pl.ds(4 * start + part, 8, stride=4), :] for part in range(4)]
+
+    def put(rows, base, stride):
+        for index, row in enumerate(rows):
+            stage_ref[pl.ds(base + index, 8, stride=stride), :] = row
+
+    stage_ref[...] = jnp.zeros_like(stage_ref)
+
+    def near_rows(step, _):
+        start = pl.multiple_of(step * 8, 8)
+        *comps, charge = components(own_ref, start)
+        moment_rows(comps, charge, stage_ref, 0)
+        own_moment_ref[pl.ds(pl.multiple_of(start * 16, 128), 128), :] = stage_ref[0:128, :].astype(
+            jnp.bfloat16
+        )
+        rows = []
+        square = zeros
+        for comp in comps:
+            first, second, third = split3(comp)
+            square = square + comp * comp
+            rows += [first, first, first, second, second, third]
+        rows += [*split3(square), ones, ones, ones]
+        rows += [zeros] * (32 - len(rows))
+        put(rows, 0, 32)
+        for half in range(2):
+            block = stage_ref[128 * half : 128 * half + 128, :]
+            near_ref[pl.ds(pl.multiple_of(step * 256 + half * 128, 128), 128), :] = block.T.astype(
+                jnp.bfloat16
+            )
+        return 0
+
+    def far_rows(step, _):
+        start = pl.multiple_of(step * 8, 8)
+        *comps, charge = components(other_ref, start)
+        moment_rows(comps, charge, stage_ref, 0)
+        other_moment_ref[pl.ds(pl.multiple_of(start * 16, 128), 128), :] = stage_ref[
+            0:128, :
+        ].astype(jnp.bfloat16)
+        rows = []
+        square = zeros
+        for comp in comps:
+            first, second, third = split3(-2.0 * comp)
+            square = square + comp * comp
+            rows += [first, second, third, first, second, first]
+        rows += [ones, ones, ones, *split3(square + softening)]
+        rows += [zeros] * (32 - len(rows))
+        put(rows, 0, 32)
+        for index in range(8):
+            target = pl.multiple_of((start + index) * 128, 128)
+            far_ref[pl.ds(target, 96), :] = jnp.zeros((96, 128), jnp.bfloat16)
+            far_ref[pl.ds(target + 96, 32), :] = stage_ref[32 * index : 32 * index + 32, :].astype(
+                jnp.bfloat16
+            )
+        return 0
+
+    lax.fori_loop(0, clusters // 8, near_rows, 0)
+    lax.fori_loop(0, others // 8, far_rows, 0)
+    far_ref[pl.ds(others * 128, 128), :] = jnp.zeros((128, 128), jnp.bfloat16)
+    own_sum_ref[...] = jnp.zeros_like(own_sum_ref)
+    other_sum_ref[...] = jnp.zeros_like(other_sum_ref)
+
+    def pull(pair):
+        own = own_rows_ref[pair]
+        other = other_rows_ref[pair]
+        group = lax.shift_right_logical(own, 2)
+        member = lax.bitwise_and(own, 3)
+        near = near_ref[pl.ds(pl.multiple_of(group * 128, 128), 128), :]
+        far = far_ref[pl.ds(pl.multiple_of(other * 128 + 96 - member * 32, 32), 128), :]
+        dist = jnp.dot(near, far, preferred_element_type=jnp.float32)
+        root = lax.rsqrt(dist)
+        weight = root * root * root
+        high = weight.astype(jnp.bfloat16)
+        low = (weight - high.astype(jnp.float32)).astype(jnp.bfloat16)
+        both = jnp.concatenate([high, low], axis=1)
+        own_at = pl.ds(pl.multiple_of(own * 16, 16), 16)
+        other_at = pl.ds(pl.multiple_of(other * 16, 16), 16)
+        own_moment = own_moment_ref[own_at, :]
+        other_moment = other_moment_ref[other_at, :]
+        to_own = lax.dot_general(
+            jnp.concatenate([other_moment, other_moment], axis=1),
+            both,
+            (((1,), (1,)), ((), ())),
+            preferred_element_type=jnp.float32,
+        )
+        to_other = jnp.dot(own_moment, both, preferred_element_type=jnp.float32)
+        return (own_at, other_at, to_own, to_other[:, :128] + to_other[:, 128:])
+
+    def visit(step, _):
+        results = [pull(step * UNROLL + turn) for turn in range(UNROLL)]
+        for own_at, other_at, to_own, to_other in results:
+            own_sum_ref[own_at, :] += to_own
+            other_sum_ref[other_at, :] += to_other
+        return 0
+
+    lax.fori_loop(0, pairs // UNROLL, visit, 0)
+
+    def finish(data_ref, sum_ref, out_ref):
+        def body(step, _):
+            start = pl.multiple_of(step * 8, 8)
+            *comps, charge = components(data_ref, start)
+
+            def total(part):
+                terms = [
+                    sum_ref[pl.ds(start * 16 + 4 * level + part, 8, stride=16), :]
+                    for level in range(3)
+                ]
+                return terms[0] + (terms[1] + terms[2])
+
+            weight = total(3)
+            scale = coulomb_scale * charge
+            for part, comp in enumerate(comps):
+                out_ref[pl.ds(4 * start + part, 8, stride=4), :] = scale * (
+                    comp * weight - total(part)
+                )
+            out_ref[pl.ds(4 * start + 3, 8, stride=4), :] = zeros
+            return 0
+
+        lax.fori_loop(0, data_ref.shape[0] // 32, body, 0)
+
+    finish(own_ref, own_sum_ref, own_out_ref)
+    finish(other_ref, other_sum_ref, other_out_ref)
+
+
+def pair_forces(own_rows, other_rows, own, other):
+    clusters = own.shape[0] // 4
+    others = other.shape[0] // 4
+    pairs = own_rows.shape[0]
+    smem = pl.BlockSpec(memory_space=pltpu.SMEM)
+    vmem = pl.BlockSpec(memory_space=pltpu.VMEM)
+    return pl.pallas_call(
+        pair_kernel,
+        out_shape=(
+            jax.ShapeDtypeStruct(own.shape, jnp.float32),
+            jax.ShapeDtypeStruct(other.shape, jnp.float32),
+        ),
+        in_specs=[smem, smem, vmem, vmem],
+        out_specs=(vmem, vmem),
+        scratch_shapes=[
+            pltpu.VMEM((clusters * 32, 128), jnp.bfloat16),
+            pltpu.VMEM(((others + 1) * 128, 128), jnp.bfloat16),
+            pltpu.VMEM((clusters * 16, 128), jnp.bfloat16),
+            pltpu.VMEM((others * 16, 128), jnp.bfloat16),
+            pltpu.VMEM((clusters * 16, 128), jnp.float32),
+            pltpu.VMEM((others * 16, 128), jnp.float32),
+            pltpu.VMEM((256, 128), jnp.float32),
+        ],
+        compiler_params=pltpu.CompilerParams(vmem_limit_bytes=40 * 1024 * 1024),
+        cost_estimate=pl.CostEstimate(
+            flops=pairs * 128 * 128 * 20, bytes_accessed=4 * 1024 * 1024, transcendentals=0
+        ),
+        name="pair_forces",
+    )(own_rows, other_rows, own, other)
 
 
 def face_div(pot, ions, axis):
@@ -140,7 +324,6 @@
         .add(jnp.sum(qmask, axis=1))
     )
     rhs = ion_density + deposit_scale * deposit.reshape(cells_x, cells_y, cells_z)
-    pairs = pair_local.shape[0]
     slot_ids = jnp.arange(slots, dtype=jnp.int32)
     slot_live = (slot_ids[None, :] < send_count.reshape(directions, 1)).astype(jnp.float32)
     outgoing = cluster_data[send_index]
@@ -154,24 +337,12 @@
         pieces.append(passed_along(outgoing[len(pieces)], "grp", -offset))
     arrived = jnp.stack(pieces).reshape(directions * slots, 4, psize)
     partner_row = pair_dir * slots + pair_slot
-    block = math.gcd(pairs, 32)
-
-    def visit(carry, items):
-        own_force, react = carry
-        own_rows, other_rows = items
-        own = cluster_data[own_rows]
-        other = arrived[other_rows]
-        pull_own, pull_other = tile_forces(own, other)
-        return ((own_force.at[own_rows].add(pull_own), react.at[other_rows].add(-pull_other)), None)
-
-    start_carry = (
-        jnp.zeros((clusters, 3, psize), jnp.float32),
-        jnp.zeros((directions * slots, 3, psize), jnp.float32),
-    )
-    (own_force, react), _ = lax.scan(
-        visit, start_carry, (pair_local.reshape(-1, block), partner_row.reshape(-1, block))
-    )
-    react = react.reshape(directions, slots, 3, psize)
+
+    own_force, react = pair_forces(
+        pair_local, partner_row, cluster_data.reshape(-1, psize), arrived.reshape(-1, psize)
+    )
+    own_force = own_force.reshape(clusters, 4, psize)[:, :3]
+    react = react.reshape(directions, slots, 4, psize)[:, :, :3]
     backs = [react[0]]
     for offset in (-1, 1, -2, 2):
         backs.append(passed_along(react[len(backs)], "brick", offset))

time: 657 us -> 395 us (0.60)
  other arithmetic: 394 us -> 34.7 us
  Pallas kernels: 0 us -> 211 us
  local copies, waits for them, and re-layouts: 151 us -> 45.2 us
    pallas_call x0 -> x1, Pallas kernels: none -> 211 us  [pair_forces(): pl.pallas_call(pair_kernel, out_shape=(jax.ShapeDtypeStruct(own.shape, jn...]
    reduce_sum x64 -> x0, other arithmetic: 194 us -> none  [the longest x32 128 us: tile_forces(): return (jnp.sum(pull, axis=3), jnp.sum(pull, axis=2))]
    scatter-add x64 -> x0, other arithmetic: 105 us -> none  [the longest x32 52.5 us: visit(): react.at[other_rows].add(-pull_other)]
    gather x64 -> x0, local copies, waits for them, and re-layouts: 105 us -> none  [the longest x32 52.9 us: visit(): own = cluster_data[own_rows]]
    div x32 -> x0, other arithmetic: 35.6 us -> none  [tile_forces(): coulomb_scale * own[:, 3, :, None] * other[:, 3, None, :]]
    select_n x32 -> x0, other arithmetic: 22 us -> none  [visit(): own_force.at[own_rows].add(pull_own)]
  transfers between devices with their start and end apart: 32 -> 32, of which waited for: 3 -> 3; matrix products, arithmetic and copies ran while one was open for 76% -> 7% of each run, Pallas kernels for 0% -> 54%
where the time goes in v1:
time: 395 us; the launch traced here: 392 us
  Pallas kernels  211 us (53%)
  starting transfers between devices  93.5 us (24%)
  local copies, waits for them, and re-layouts  45.2 us (11%)
  other arithmetic  34.7 us (9%)
  waiting for transfers between devices  6.26 us (2%)
    pallas_call x1, Pallas kernels, pair_forces(): pl.pallas_call(pair_kernel, out_shape=(jax.ShapeDtypeStruct(own.shape, jn...  211 us
    another operation x4, local copies, waits for them, and re-layouts, field_of(): return jnp.stack([along_x, along_y, along_z])  37.3 us
    ppermute x12, starting transfers between devices, passed_along(): return lax.ppermute(shard, axis, pairs)  34.3 us
    ppermute x10, starting transfers between devices, extended(): before = lax.ppermute(last, axis, up)  30.9 us
    ppermute x10, starting transfers between devices, extended(): after = lax.ppermute(initial, axis, down)  28.4 us
    scatter-add x1, other arithmetic, shards(): coulomb = own_force.at[send_index.reshape(-1)].add(returned)  8.23 us
  transfers between devices with their start and end apart: 32, of which 3 were waited for; matrix products, arithmetic and copies ran while one was open for 7% of the time, Pallas kernels for 54%

profile of v1, /device:TPU:13, one launch (start us, length us, event | category | flops | bytes accessed | tf_op | source)
XLA Modules:
  0.0 391.9 jit_solution(3922095228843545517)
XLA Ops:
  0.6 0.8 fusion.65
  1.4 3.1 collective-permute-start.13
  4.5 3.1 collective-permute-start.12
  7.6 0.7 compare_select_fusion.3
  8.3 0.7 compare_select_fusion.1
  9.1 0.7 fusion.57
  9.8 1.2 compare_select_fusion
  11.0 1.3 pad_maximum_fusion.29
  12.3 0.9 gather_fusion
  13.9 4.5 %collective-permute-start = (f32[32,4,128]{2,1,0:T(4,128)S(1)}, f32[32,4,128]{2,1,0:T(4,128)S(1)}, u32[]{:S(2)}, u32[]{:S(2)}) collective-permute-start(f32[32,4,128]{2,1,0:T(4,128)S(1)} %get-tuple-element.30), channel_id=1, source_target_pairs={{0,1},{1,2},{2,3},{3,4},{4,5},{5,6},{6,7},{8,9},{9,10},{10,11},{11... | collective-permute-start | bytes 196616 | tf_op jit(solution)/shard_map/ppermute | solution.py:39
  18.3 1.9 collective-permute-start.1
  20.2 3.2 collective-permute-start.2
  23.5 0.8 fusion.43
  24.2 2.1 scatter_custom_fusion.1
  27.1 0.8 constant_dynamic-update-slice_fusion.1
  28.6 1.0 fusion.61
  29.6 2.7 collective-permute-start.14
  32.3 3.1 collective-permute-start.15
  35.6 2.2 collective-permute-start.3
  37.9 2.2 collective-permute-start.4
  40.1 1.6 select_maximum_fusion.17
  41.7 1.7 fusion.58
  43.5 4.0 %collective-permute-start.5 = (f32[32,4,128]{2,1,0:T(4,128)S(1)}, f32[32,4,128]{2,1,0:T(4,128)S(1)}, u32[]{:S(2)}, u32[]{:S(2)}) collective-permute-start(f32[32,4,128]{2,1,0:T(4,128)S(1)} %get-tuple-element.28), channel_id=1, source_target_pairs={{8,0},{16,8},{24,16},{9,1},{17,9},{25,17},{10,2},{18,10},{26,18},{... | collective-permute-start | bytes 196616 | tf_op jit(solution)/shard_map/ppermute | solution.py:39
  47.5 1.9 collective-permute-start.16
  49.4 3.4 collective-permute-start.17
  52.9 210.7 %pair_forces.1 = (f32[1024,128]{1,0:T(8,128)S(1)}, f32[896,128]{1,0:T(8,128)S(1)}) custom-call(s32[1024]{0:T(1024)S(1)} %copy-done, s32[1024]{0:T(1024)S(1)} %multiply_add_fusion.2.other_rows_ref, f32[1024,128]{1,0:T(8,128)S(1)} %bitcast.81, f32[896,128]{1,0:T(8,128)S(1)} %bitcast.84), custom_call_target="tpu_custom_call" | custom-call | flops 335544320 | bytes 4194304 | tf_op jit(solution)/shard_map/pair_forces/pallas_call | solution.py:242
  263.7 2.6 collective-permute-start.18
  266.4 3.1 collective-permute-start.19
  269.5 1.9 collective-permute-start.6
  271.4 3.6 collective-permute-start.7
  275.1 2.1 collective-permute-start.8
  277.2 3.2 collective-permute-start.9
  281.4 2.7 collective-permute-start.20
  284.1 2.6 collective-permute-start.21
  286.8 3.6 collective-permute-start.10
  290.4 2.3 collective-permute-start.22
  292.7 3.3 collective-permute-start.23
  296.0 1.9 collective-permute-start.11
  299.0 4.3 %collective-permute-start.24 = (f32[1,32,256]{2,1,0:T(8,128)S(1)}, f32[1,32,256]{2,1,0:T(8,128)S(1)}, u32[]{:S(2)}, u32[]{:S(2)}) collective-permute-start(f32[1,32,256]{2,1,0:T(8,128)S(1)} %get-tuple-element.36), channel_id=1, source_target_pairs={{8,0},{16,8},{24,16},{9,1},{17,9},{25,17},{10,2},{18,10},{26,18},{... | collective-permute-start | bytes 98312 | tf_op jit(solution)/shard_map/ppermute | solution.py:31
  303.3 1.9 collective-permute-start.25
  305.3 4.1 %collective-permute-done.25 = f32[1,32,256]{2,1,0:T(8,128)S(1)} collective-permute-done((f32[1,32,256]{2,1,0:T(8,128)S(1)}, f32[1,32,256]{2,1,0:T(8,128)S(1)}, u32[]{:S(2)}, u32[]{:S(2)}) %collective-permute-start.25) | collective-permute-done | bytes 32800 | tf_op jit(solution)/shard_map/ppermute | solution.py:30
  309.4 2.4 collective-permute-start.26
  311.8 3.1 collective-permute-start.27
  315.0 0.8 collective-permute-done.27
  316.4 1.0 fusion.20
  317.4 1.9 collective-permute-start.28
  319.3 4.3 %collective-permute-start.29 = (f32[2,1,32,256]{3,2,1,0:T(8,128)S(1)}, f32[2,1,32,256]{3,2,1,0:T(8,128)S(1)}, u32[]{:S(2)}, u32[]{:S(2)}) collective-permute-start(f32[2,1,32,256]{3,2,1,0:T(8,128)S(1)} %get-tuple-element.19), channel_id=1, source_target_pairs={{8,0},{16,8},{24,16},{9,1},{17,9},{25,17},{10,2},{18,10},{26,18},{... | collective-permute-start | bytes 196616 | tf_op jit(solution)/shard_map/ppermute | solution.py:31
  323.7 1.3 collective-permute-done.29
  325.0 5.3 %collective-permute-start.30 = (f32[2,18,1,256]{3,2,1,0:T(1,128)S(1)}, f32[2,18,1,256]{3,2,1,0:T(1,128)S(1)}, u32[]{:S(2)}, u32[]{:S(2)}) collective-permute-start(f32[2,18,1,256]{3,2,1,0:T(1,128)S(1)} %get-tuple-element.13), channel_id=1, source_target_pairs={{0,1},{1,2},{2,3},{3,4},{4,5},{5,6},{6,7},{8,9},{9,10},{10,11},{11... | collective-permute-start | bytes 110600 | tf_op jit(solution)/shard_map/ppermute | solution.py:30
  330.3 2.1 collective-permute-start.31
  332.5 8.2 %scatter_fusion = f32[256,3,128]{2,1,0:T(4,128)S(1)} fusion(f32[256,3,128]{2,1,0:T(4,128)S(1)} %bitcast.82, s32[224]{0:T(256)S(1)} %bitcast.97, f32[224,3,128]{2,1,0:T(4,128)S(1)} %bitcast.93), kind=kCustom, calls=%fused_computation.2 | custom fusion | flops 86016 | bytes 1033088 | tf_op jit(solution)/shard_map/scatter-add | solution.py:352
  340.7 1.0 select_maximum_fusion
  341.9 0.7 multiply_subtract_fusion
  342.6 0.8 multiply_subtract_fusion.1
  343.4 0.7 multiply_subtract_fusion.2
  344.0 1.9 fusion.14
  345.9 2.4 stack.80
  348.3 2.4 stack.81
  350.7 2.4 stack.82
  353.0 4.2 %pad_maximum_fusion = f32[3,131072]{1,0:T(4,128)} fusion(f32[1,131072]{1,0:T(1,128)} %stack.82, f32[1,131072]{1,0:T(1,128)} %stack.81, f32[1,131072]{1,0:T(1,128)} %stack.80), kind=kLoop, calls=%fused_computation.12 | loop fusion | flops 786432 | bytes 3145728 | tf_op jit(solution)/shard_map/stack | solution.py:292
  357.2 30.2 %copy.23 = f32[3,131072]{0,1:T(8,128)} copy(f32[3,131072]{1,0:T(4,128)} %pad_maximum_fusion) | data formatting | bytes 3145728 | tf_op jit(solution)/shard_map/stack | solution.py:292
  387.4 2.3 gather_fusion.1
  389.7 1.0 fusion.7
  390.8 1.1 fusion.39
  (89 shorter events, 5.3 us)
Async XLA Ops:
  1.4 25.1 %collective-permute-start.13 = (f32[1,32,256]{2,1,0:T(8,128)S(1)}, f32[1,32,256]{2,1,0:T(8,128)S(1)}, u32[]{:S(2)}, u32[]{:S(2)}) collective-permute-start(f32[1,32,256]{2,1,0:T(8,128)S(1)} %get-tuple-element.42), channel_id=1, source_target_pairs={{0,8},{8,16},{16,24},{1,9},{9,17},{17,25},{2,10},{10,18},{18,26},{... | collective-permute-start | bytes 98312 | tf_op jit(solution)/shard_map/ppermute | solution.py:30
  4.5 23.4 %collective-permute-start.12 = (f32[1,32,256]{2,1,0:T(8,128)S(1)}, f32[1,32,256]{2,1,0:T(8,128)S(1)}, u32[]{:S(2)}, u32[]{:S(2)}) collective-permute-start(f32[1,32,256]{2,1,0:T(8,128)S(1)} %get-tuple-element.41), channel_id=1, source_target_pairs={{8,0},{16,8},{24,16},{9,1},{17,9},{25,17},{10,2},{18,10},{26,18},{... | collective-permute-start | bytes 98312 | tf_op jit(solution)/shard_map/ppermute | solution.py:31
  12.3 11.1 %copy-start.6 = (f32[32768]{0:T(1024)S(1)}, f32[32768]{0:T(1024)}, u32[]{:S(2)}) copy-start(f32[32768]{0:T(1024)} %param.13) | copy-start | bytes 393220
  12.3 11.1 %copy-start.8 = (s32[256]{0:T(256)S(1)}, s32[256]{0:T(256)}, u32[]{:S(2)}) copy-start(s32[256]{0:T(256)} %param.14) | copy-start | bytes 3076
  13.8 12.6 %copy-start.9 = (s32[1024]{0:T(1024)S(1)}, s32[1024]{0:T(1024)}, u32[]{:S(2)}) copy-start(s32[1024]{0:T(1024)} %param.20) | copy-start | bytes 12292
  13.8 12.6 %copy-start.10 = (s32[1024]{0:T(1024)S(1)}, s32[1024]{0:T(1024)}, u32[]{:S(2)}) copy-start(s32[1024]{0:T(1024)} %param.19) | copy-start | bytes 12292
  13.8 12.6 %copy-start.7 = (s32[7,32]{1,0:T(8,128)S(1)}, s32[7,32]{1,0:T(8,128)}, u32[]{:S(2)}) copy-start(s32[7,32]{1,0:T(8,128)} %param.16) | copy-start | bytes 2692
  13.8 13.3 %copy-start.4 = (f32[16,32,256]{2,1,0:T(8,128)S(1)}, f32[16,32,256]{2,1,0:T(8,128)}, u32[]{:S(2)}) copy-start(f32[16,32,256]{2,1,0:T(8,128)} %param.22) | copy-start | bytes 1572868
  13.9 29.6 %collective-permute-start = (f32[32,4,128]{2,1,0:T(4,128)S(1)}, f32[32,4,128]{2,1,0:T(4,128)S(1)}, u32[]{:S(2)}, u32[]{:S(2)}) collective-permute-start(f32[32,4,128]{2,1,0:T(4,128)S(1)} %get-tuple-element.30), channel_id=1, source_target_pairs={{0,1},{1,2},{2,3},{3,4},{4,5},{5,6},{6,7},{8,9},{9,10},{10,11},{11... | collective-permute-start | bytes 196616 | tf_op jit(solution)/shard_map/ppermute | solution.py:39
  18.3 29.2 %collective-permute-start.1 = (f32[32,4,128]{2,1,0:T(4,128)S(1)}, f32[32,4,128]{2,1,0:T(4,128)S(1)}, u32[]{:S(2)}, u32[]{:S(2)}) collective-permute-start(f32[32,4,128]{2,1,0:T(4,128)S(1)} %get-tuple-element.31), channel_id=1, source_target_pairs={{1,0},{2,1},{3,2},{4,3},{5,4},{6,5},{7,6},{9,8},{10,9},{11,10},{12... | collective-permute-start | bytes 196616 | tf_op jit(solution)/shard_map/ppermute | solution.py:39
  20.2 29.2 %collective-permute-start.2 = (f32[32,4,128]{2,1,0:T(4,128)S(1)}, f32[32,4,128]{2,1,0:T(4,128)S(1)}, u32[]{:S(2)}, u32[]{:S(2)}) collective-permute-start(f32[32,4,128]{2,1,0:T(4,128)S(1)} %get-tuple-element.32), channel_id=1, source_target_pairs={{0,2},{1,3},{2,4},{3,5},{4,6},{5,7},{8,10},{9,11},{10,12},{11,13},... | collective-permute-start | bytes 196616 | tf_op jit(solution)/shard_map/ppermute | solution.py:39
  29.6 6.1 %collective-permute-start.14 = (f32[18,1,256]{2,1,0:T(1,128)S(1)}, f32[18,1,256]{2,1,0:T(1,128)S(1)}, u32[]{:S(2)}, u32[]{:S(2)}) collective-permute-start(f32[18,1,256]{2,1,0:T(1,128)S(1)} %get-tuple-element.27), channel_id=1, source_target_pairs={{1,0},{2,1},{3,2},{4,3},{5,4},{6,5},{7,6},{9,8},{10,9},{11,10},{12... | collective-permute-start | bytes 55304 | tf_op jit(solution)/shard_map/ppermute | solution.py:31
  32.3 5.5 %collective-permute-start.15 = (f32[18,1,256]{2,1,0:T(1,128)S(1)}, f32[18,1,256]{2,1,0:T(1,128)S(1)}, u32[]{:S(2)}, u32[]{:S(2)}) collective-permute-start(f32[18,1,256]{2,1,0:T(1,128)S(1)} %get-tuple-element.26), channel_id=1, source_target_pairs={{0,1},{1,2},{2,3},{3,4},{4,5},{5,6},{6,7},{8,9},{9,10},{10,11},{11... | collective-permute-start | bytes 55304 | tf_op jit(solution)/shard_map/ppermute | solution.py:30
  35.6 6.1 %copy-start.1 = (f32[16,32,256]{2,1,0:T(8,128)S(1)}, f32[16,32,256]{2,1,0:T(8,128)}, u32[]{:S(2)}) copy-start(f32[16,32,256]{2,1,0:T(8,128)} %param.21) | copy-start | bytes 1572868
  35.6 6.1 %copy-start.3 = (f32[16,32,256]{2,1,0:T(8,128)S(1)}, f32[16,32,256]{2,1,0:T(8,128)}, u32[]{:S(2)}) copy-start(f32[16,32,256]{2,1,0:T(8,128)} %param.23) | copy-start | bytes 1572868
  35.6 17.2 %collective-permute-start.3 = (f32[32,4,128]{2,1,0:T(4,128)S(1)}, f32[32,4,128]{2,1,0:T(4,128)S(1)}, u32[]{:S(2)}, u32[]{:S(2)}) collective-permute-start(f32[32,4,128]{2,1,0:T(4,128)S(1)} %get-tuple-element.33), channel_id=1, source_target_pairs={{2,0},{3,1},{4,2},{5,3},{6,4},{7,5},{10,8},{11,9},{12,10},{13,11},... | collective-permute-start | bytes 196616 | tf_op jit(solution)/shard_map/ppermute | solution.py:39
  37.9 15.0 %collective-permute-start.4 = (f32[32,4,128]{2,1,0:T(4,128)S(1)}, f32[32,4,128]{2,1,0:T(4,128)S(1)}, u32[]{:S(2)}, u32[]{:S(2)}) collective-permute-start(f32[32,4,128]{2,1,0:T(4,128)S(1)} %get-tuple-element.34), channel_id=1, source_target_pairs={{0,8},{8,16},{16,24},{1,9},{9,17},{17,25},{2,10},{10,18},{18,26},{... | collective-permute-start | bytes 196616 | tf_op jit(solution)/shard_map/ppermute | solution.py:39
  41.7 11.2 %copy-start = (s32[1024]{0:T(1024)S(1)}, s32[1024]{0:T(1024)}, u32[]{:S(2)}) copy-start(s32[1024]{0:T(1024)} %own_rows_ref.1) | copy-start | bytes 12292
  43.5 9.4 %collective-permute-start.5 = (f32[32,4,128]{2,1,0:T(4,128)S(1)}, f32[32,4,128]{2,1,0:T(4,128)S(1)}, u32[]{:S(2)}, u32[]{:S(2)}) collective-permute-start(f32[32,4,128]{2,1,0:T(4,128)S(1)} %get-tuple-element.28), channel_id=1, source_target_pairs={{8,0},{16,8},{24,16},{9,1},{17,9},{25,17},{10,2},{18,10},{26,18},{... | collective-permute-start | bytes 196616 | tf_op jit(solution)/shard_map/ppermute | solution.py:39
  47.5 216.2 %collective-permute-start.16 = (f32[1,32,256]{2,1,0:T(8,128)S(1)}, f32[1,32,256]{2,1,0:T(8,128)S(1)}, u32[]{:S(2)}, u32[]{:S(2)}) collective-permute-start(f32[1,32,256]{2,1,0:T(8,128)S(1)} %get-tuple-element.40), channel_id=1, source_target_pairs={{8,0},{16,8},{24,16},{9,1},{17,9},{25,17},{10,2},{18,10},{26,18},{... | collective-permute-start | bytes 98312 | tf_op jit(solution)/shard_map/ppermute | solution.py:31
  49.4 214.2 %collective-permute-start.17 = (f32[1,32,256]{2,1,0:T(8,128)S(1)}, f32[1,32,256]{2,1,0:T(8,128)S(1)}, u32[]{:S(2)}, u32[]{:S(2)}) collective-permute-start(f32[1,32,256]{2,1,0:T(8,128)S(1)} %get-tuple-element.39), channel_id=1, source_target_pairs={{0,8},{8,16},{16,24},{1,9},{9,17},{17,25},{2,10},{10,18},{18,26},{... | collective-permute-start | bytes 98312 | tf_op jit(solution)/shard_map/ppermute | solution.py:30
  263.7 13.5 %collective-permute-start.18 = (f32[18,1,256]{2,1,0:T(1,128)S(1)}, f32[18,1,256]{2,1,0:T(1,128)S(1)}, u32[]{:S(2)}, u32[]{:S(2)}) collective-permute-start(f32[18,1,256]{2,1,0:T(1,128)S(1)} %get-tuple-element.25), channel_id=1, source_target_pairs={{1,0},{2,1},{3,2},{4,3},{5,4},{6,5},{7,6},{9,8},{10,9},{11,10},{12... | collective-permute-start | bytes 55304 | tf_op jit(solution)/shard_map/ppermute | solution.py:31
  266.4 14.0 %collective-permute-start.19 = (f32[18,1,256]{2,1,0:T(1,128)S(1)}, f32[18,1,256]{2,1,0:T(1,128)S(1)}, u32[]{:S(2)}, u32[]{:S(2)}) collective-permute-start(f32[18,1,256]{2,1,0:T(1,128)S(1)} %get-tuple-element.24), channel_id=1, source_target_pairs={{0,1},{1,2},{2,3},{3,4},{4,5},{5,6},{6,7},{8,9},{9,10},{10,11},{11... | collective-permute-start | bytes 55304 | tf_op jit(solution)/shard_map/ppermute | solution.py:30
  269.5 14.6 %collective-permute-start.6 = (f32[32,3,128]{2,1,0:T(4,128)S(1)}, f32[32,3,128]{2,1,0:T(4,128)S(1)}, u32[]{:S(2)}, u32[]{:S(2)}) collective-permute-start(f32[32,3,128]{2,1,0:T(4,128)S(1)} %get-tuple-element.48), channel_id=1, source_target_pairs={{1,0},{2,1},{3,2},{4,3},{5,4},{6,5},{7,6},{9,8},{10,9},{11,10},{12... | collective-permute-start | bytes 147464 | tf_op jit(solution)/shard_map/ppermute | solution.py:39
  271.4 21.2 %collective-permute-start.7 = (f32[32,3,128]{2,1,0:T(4,128)S(1)}, f32[32,3,128]{2,1,0:T(4,128)S(1)}, u32[]{:S(2)}, u32[]{:S(2)}) collective-permute-start(f32[32,3,128]{2,1,0:T(4,128)S(1)} %get-tuple-element.47), channel_id=1, source_target_pairs={{0,1},{1,2},{2,3},{3,4},{4,5},{5,6},{6,7},{8,9},{9,10},{10,11},{11... | collective-permute-start | bytes 147464 | tf_op jit(solution)/shard_map/ppermute | solution.py:39
  275.1 28.2 %collective-permute-start.8 = (f32[32,3,128]{2,1,0:T(4,128)S(1)}, f32[32,3,128]{2,1,0:T(4,128)S(1)}, u32[]{:S(2)}, u32[]{:S(2)}) collective-permute-start(f32[32,3,128]{2,1,0:T(4,128)S(1)} %get-tuple-element.46), channel_id=1, source_target_pairs={{2,0},{3,1},{4,2},{5,3},{6,4},{7,5},{10,8},{11,9},{12,10},{13,11},... | collective-permute-start | bytes 147464 | tf_op jit(solution)/shard_map/ppermute | solution.py:39
  277.2 37.8 %collective-permute-start.9 = (f32[32,3,128]{2,1,0:T(4,128)S(1)}, f32[32,3,128]{2,1,0:T(4,128)S(1)}, u32[]{:S(2)}, u32[]{:S(2)}) collective-permute-start(f32[32,3,128]{2,1,0:T(4,128)S(1)} %get-tuple-element.45), channel_id=1, source_target_pairs={{0,2},{1,3},{2,4},{3,5},{4,6},{5,7},{8,10},{9,11},{10,12},{11,13},... | collective-permute-start | bytes 147464 | tf_op jit(solution)/shard_map/ppermute | solution.py:39
  281.4 5.3 %collective-permute-start.20 = (f32[1,32,256]{2,1,0:T(8,128)S(1)}, f32[1,32,256]{2,1,0:T(8,128)S(1)}, u32[]{:S(2)}, u32[]{:S(2)}) collective-permute-start(f32[1,32,256]{2,1,0:T(8,128)S(1)} %get-tuple-element.38), channel_id=1, source_target_pairs={{8,0},{16,8},{24,16},{9,1},{17,9},{25,17},{10,2},{18,10},{26,18},{... | collective-permute-start | bytes 98312 | tf_op jit(solution)/shard_map/ppermute | solution.py:31
  284.1 6.2 %collective-permute-start.21 = (f32[1,32,256]{2,1,0:T(8,128)S(1)}, f32[1,32,256]{2,1,0:T(8,128)S(1)}, u32[]{:S(2)}, u32[]{:S(2)}) collective-permute-start(f32[1,32,256]{2,1,0:T(8,128)S(1)} %get-tuple-element.37), channel_id=1, source_target_pairs={{0,8},{8,16},{16,24},{1,9},{9,17},{17,25},{2,10},{10,18},{18,26},{... | collective-permute-start | bytes 98312 | tf_op jit(solution)/shard_map/ppermute | solution.py:30
  286.8 36.8 %collective-permute-start.10 = (f32[32,3,128]{2,1,0:T(4,128)S(1)}, f32[32,3,128]{2,1,0:T(4,128)S(1)}, u32[]{:S(2)}, u32[]{:S(2)}) collective-permute-start(f32[32,3,128]{2,1,0:T(4,128)S(1)} %get-tuple-element.44), channel_id=1, source_target_pairs={{8,0},{16,8},{24,16},{9,1},{17,9},{25,17},{10,2},{18,10},{26,18},{... | collective-permute-start | bytes 147464 | tf_op jit(solution)/shard_map/ppermute | solution.py:39
  290.4 5.6 %collective-permute-start.22 = (f32[18,1,256]{2,1,0:T(1,128)S(1)}, f32[18,1,256]{2,1,0:T(1,128)S(1)}, u32[]{:S(2)}, u32[]{:S(2)}) collective-permute-start(f32[18,1,256]{2,1,0:T(1,128)S(1)} %get-tuple-element.23), channel_id=1, source_target_pairs={{1,0},{2,1},{3,2},{4,3},{5,4},{6,5},{7,6},{9,8},{10,9},{11,10},{12... | collective-permute-start | bytes 55304 | tf_op jit(solution)/shard_map/ppermute | solution.py:31
  292.7 5.3 %collective-permute-start.23 = (f32[18,1,256]{2,1,0:T(1,128)S(1)}, f32[18,1,256]{2,1,0:T(1,128)S(1)}, u32[]{:S(2)}, u32[]{:S(2)}) collective-permute-start(f32[18,1,256]{2,1,0:T(1,128)S(1)} %get-tuple-element.22), channel_id=1, source_target_pairs={{0,1},{1,2},{2,3},{3,4},{4,5},{5,6},{6,7},{8,9},{9,10},{10,11},{11... | collective-permute-start | bytes 55304 | tf_op jit(solution)/shard_map/ppermute | solution.py:30
  296.0 36.4 %collective-permute-start.11 = (f32[32,3,128]{2,1,0:T(4,128)S(1)}, f32[32,3,128]{2,1,0:T(4,128)S(1)}, u32[]{:S(2)}, u32[]{:S(2)}) collective-permute-start(f32[32,3,128]{2,1,0:T(4,128)S(1)} %get-tuple-element.43), channel_id=1, source_target_pairs={{0,8},{8,16},{16,24},{1,9},{9,17},{17,25},{2,10},{10,18},{18,26},{... | collective-permute-start | bytes 147464 | tf_op jit(solution)/shard_map/ppermute | solution.py:39
  299.0 6.2 %collective-permute-start.24 = (f32[1,32,256]{2,1,0:T(8,128)S(1)}, f32[1,32,256]{2,1,0:T(8,128)S(1)}, u32[]{:S(2)}, u32[]{:S(2)}) collective-permute-start(f32[1,32,256]{2,1,0:T(8,128)S(1)} %get-tuple-element.36), channel_id=1, source_target_pairs={{8,0},{16,8},{24,16},{9,1},{17,9},{25,17},{10,2},{18,10},{26,18},{... | collective-permute-start | bytes 98312 | tf_op jit(solution)/shard_map/ppermute | solution.py:31
  303.3 6.1 %collective-permute-start.25 = (f32[1,32,256]{2,1,0:T(8,128)S(1)}, f32[1,32,256]{2,1,0:T(8,128)S(1)}, u32[]{:S(2)}, u32[]{:S(2)}) collective-permute-start(f32[1,32,256]{2,1,0:T(8,128)S(1)} %get-tuple-element.35), channel_id=1, source_target_pairs={{0,8},{8,16},{16,24},{1,9},{9,17},{17,25},{2,10},{10,18},{18,26},{... | collective-permute-start | bytes 98312 | tf_op jit(solution)/shard_map/ppermute | solution.py:30
  309.4 5.6 %collective-permute-start.26 = (f32[18,1,256]{2,1,0:T(1,128)S(1)}, f32[18,1,256]{2,1,0:T(1,128)S(1)}, u32[]{:S(2)}, u32[]{:S(2)}) collective-permute-start(f32[18,1,256]{2,1,0:T(1,128)S(1)} %get-tuple-element.21), channel_id=1, source_target_pairs={{1,0},{2,1},{3,2},{4,3},{5,4},{6,5},{7,6},{9,8},{10,9},{11,10},{12... | collective-permute-start | bytes 55304 | tf_op jit(solution)/shard_map/ppermute | solution.py:31
  311.8 4.0 %collective-permute-start.27 = (f32[18,1,256]{2,1,0:T(1,128)S(1)}, f32[18,1,256]{2,1,0:T(1,128)S(1)}, u32[]{:S(2)}, u32[]{:S(2)}) collective-permute-start(f32[18,1,256]{2,1,0:T(1,128)S(1)} %get-tuple-element.20), channel_id=1, source_target_pairs={{0,1},{1,2},{2,3},{3,4},{4,5},{5,6},{6,7},{8,9},{9,10},{10,11},{11... | collective-permute-start | bytes 55304 | tf_op jit(solution)/shard_map/ppermute | solution.py:30
  317.4 23.3 %copy-start.2 = (f32[16,32,256]{2,1,0:T(8,128)}, f32[16,32,256]{2,1,0:T(8,128)S(1)}, u32[]{:S(2)}) copy-start(f32[16,32,256]{2,1,0:T(8,128)S(1)} %fusion.20) | copy-start | bytes 1572868
  317.4 6.2 %collective-permute-start.28 = (f32[2,1,32,256]{3,2,1,0:T(8,128)S(1)}, f32[2,1,32,256]{3,2,1,0:T(8,128)S(1)}, u32[]{:S(2)}, u32[]{:S(2)}) collective-permute-start(f32[2,1,32,256]{3,2,1,0:T(8,128)S(1)} %get-tuple-element.18), channel_id=1, source_target_pairs={{0,8},{8,16},{16,24},{1,9},{9,17},{17,25},{2,10},{10,18},{18,26},{... | collective-permute-start | bytes 196616 | tf_op jit(solution)/shard_map/ppermute | solution.py:30
  319.3 5.6 %collective-permute-start.29 = (f32[2,1,32,256]{3,2,1,0:T(8,128)S(1)}, f32[2,1,32,256]{3,2,1,0:T(8,128)S(1)}, u32[]{:S(2)}, u32[]{:S(2)}) collective-permute-start(f32[2,1,32,256]{3,2,1,0:T(8,128)S(1)} %get-tuple-element.19), channel_id=1, source_target_pairs={{8,0},{16,8},{24,16},{9,1},{17,9},{25,17},{10,2},{18,10},{26,18},{... | collective-permute-start | bytes 196616 | tf_op jit(solution)/shard_map/ppermute | solution.py:31
  325.0 15.7 %collective-permute-start.30 = (f32[2,18,1,256]{3,2,1,0:T(1,128)S(1)}, f32[2,18,1,256]{3,2,1,0:T(1,128)S(1)}, u32[]{:S(2)}, u32[]{:S(2)}) collective-permute-start(f32[2,18,1,256]{3,2,1,0:T(1,128)S(1)} %get-tuple-element.13), channel_id=1, source_target_pairs={{0,1},{1,2},{2,3},{3,4},{4,5},{5,6},{6,7},{8,9},{9,10},{10,11},{11... | collective-permute-start | bytes 110600 | tf_op jit(solution)/shard_map/ppermute | solution.py:30
  330.3 10.4 %collective-permute-start.31 = (f32[2,18,1,256]{3,2,1,0:T(1,128)S(1)}, f32[2,18,1,256]{3,2,1,0:T(1,128)S(1)}, u32[]{:S(2)}, u32[]{:S(2)}) collective-permute-start(f32[2,18,1,256]{3,2,1,0:T(1,128)S(1)} %get-tuple-element.14), channel_id=1, source_target_pairs={{1,0},{2,1},{3,2},{4,3},{5,4},{6,5},{7,6},{9,8},{10,9},{11,10},{12... | collective-permute-start | bytes 110600 | tf_op jit(solution)/shard_map/ppermute | solution.py:31
  389.7 1.0 copy-start.5

commit v2 on v1

--- a/solution.py
+++ b/solution.py
@@ -102,12 +102,15 @@
     own_sum_ref,
     other_sum_ref,
     stage_ref,
+    dist_ref,
+    weight_ref,
 ):
     clusters = own_ref.shape[0] // 4
     others = other_ref.shape[0] // 4
-    pairs = own_rows_ref.shape[0]
+    groups = own_rows_ref.shape[0] // UNROLL
     ones = jnp.ones((8, 128), jnp.float32)
     zeros = jnp.zeros((8, 128), jnp.float32)
+    stage_ref[...] = jnp.zeros_like(stage_ref)
 
     def components(data_ref, start):
         return [data_ref[pl.ds(4 * start + part, 8, stride=4), :] for part in range(4)]
@@ -115,8 +118,6 @@
     def put(rows, base, stride):
         for index, row in enumerate(rows):
             stage_ref[pl.ds(base + index, 8, stride=stride), :] = row
-
-    stage_ref[...] = jnp.zeros_like(stage_ref)
 
     def near_rows(step, _):
         start = pl.multiple_of(step * 8, 8)
@@ -139,15 +140,17 @@
             near_ref[pl.ds(pl.multiple_of(step * 256 + half * 128, 128), 128), :] = block.T.astype(
                 jnp.bfloat16
             )
+        for index in range(8):
+            own_sum_ref[pl.ds(pl.multiple_of((start + index) * 128, 128), 128), :] = jnp.zeros(
+                (128, 128), jnp.float32
+            )
         return 0
 
     def far_rows(step, _):
         start = pl.multiple_of(step * 8, 8)
         *comps, charge = components(other_ref, start)
         moment_rows(comps, charge, stage_ref, 0)
-        other_moment_ref[pl.ds(pl.multiple_of(start * 16, 128), 128), :] = stage_ref[
-            0:128, :
-        ].astype(jnp.bfloat16)
+        columns = stage_ref[0:128, :].T
         rows = []
         square = zeros
         for comp in comps:
@@ -163,74 +166,98 @@
             far_ref[pl.ds(target + 96, 32), :] = stage_ref[32 * index : 32 * index + 32, :].astype(
                 jnp.bfloat16
             )
+            rolled = columns if index == 0 else pltpu.roll(columns, 128 - 16 * index, 1)
+            other_moment_ref[pl.ds(target, 128), :] = rolled.astype(jnp.bfloat16)
         return 0
 
     lax.fori_loop(0, clusters // 8, near_rows, 0)
     lax.fori_loop(0, others // 8, far_rows, 0)
     far_ref[pl.ds(others * 128, 128), :] = jnp.zeros((128, 128), jnp.bfloat16)
-    own_sum_ref[...] = jnp.zeros_like(own_sum_ref)
     other_sum_ref[...] = jnp.zeros_like(other_sum_ref)
-
-    def pull(pair):
+    dist_ref[...] = jnp.full(dist_ref.shape, 1e38, jnp.float32)
+    weight_ref[...] = jnp.zeros_like(weight_ref)
+
+    def distances(pair, turn):
         own = own_rows_ref[pair]
         other = other_rows_ref[pair]
         group = lax.shift_right_logical(own, 2)
         member = lax.bitwise_and(own, 3)
         near = near_ref[pl.ds(pl.multiple_of(group * 128, 128), 128), :]
         far = far_ref[pl.ds(pl.multiple_of(other * 128 + 96 - member * 32, 32), 128), :]
-        dist = jnp.dot(near, far, preferred_element_type=jnp.float32)
-        root = lax.rsqrt(dist)
+        dist_ref[turn] = jnp.dot(near, far, preferred_element_type=jnp.float32)
+
+    def weights(turn):
+        root = lax.rsqrt(dist_ref[turn])
         weight = root * root * root
         high = weight.astype(jnp.bfloat16)
-        low = (weight - high.astype(jnp.float32)).astype(jnp.bfloat16)
-        both = jnp.concatenate([high, low], axis=1)
-        own_at = pl.ds(pl.multiple_of(own * 16, 16), 16)
-        other_at = pl.ds(pl.multiple_of(other * 16, 16), 16)
-        own_moment = own_moment_ref[own_at, :]
-        other_moment = other_moment_ref[other_at, :]
-        to_own = lax.dot_general(
-            jnp.concatenate([other_moment, other_moment], axis=1),
+        weight_ref[turn, :, :128] = high
+        weight_ref[turn, :, 128:] = (weight - high.astype(jnp.float32)).astype(jnp.bfloat16)
+
+    def products(pair, turn):
+        own = own_rows_ref[pair]
+        other = other_rows_ref[pair]
+        both = weight_ref[turn]
+        moment = other_moment_ref[pl.ds(pl.multiple_of(other * 128, 128), 128), :]
+        to_own = jnp.dot(
             both,
-            (((1,), (1,)), ((), ())),
+            jnp.concatenate([moment, moment], axis=0),
             preferred_element_type=jnp.float32,
         )
-        to_other = jnp.dot(own_moment, both, preferred_element_type=jnp.float32)
-        return (own_at, other_at, to_own, to_other[:, :128] + to_other[:, 128:])
+        to_other = jnp.dot(
+            own_moment_ref[pl.ds(pl.multiple_of(own * 16, 16), 16), :],
+            both,
+            preferred_element_type=jnp.float32,
+        )
+        return (own, other, to_own, to_other[:, :128] + to_other[:, 128:])
 
     def visit(step, _):
-        results = [pull(step * UNROLL + turn) for turn in range(UNROLL)]
-        for own_at, other_at, to_own, to_other in results:
-            own_sum_ref[own_at, :] += to_own
-            other_sum_ref[other_at, :] += to_other
+        last = jnp.maximum(step - 2, 0) * UNROLL
+        first = jnp.minimum(step, groups - 1) * UNROLL
+        results = [products(last + turn, turn) for turn in range(UNROLL)]
+        for turn in range(UNROLL):
+            weights(turn)
+        for turn in range(UNROLL):
+            distances(first + turn, turn)
+        for own, other, to_own, to_other in results:
+            own_sum_ref[pl.ds(pl.multiple_of(own * 128, 128), 128), :] += to_own
+            other_sum_ref[pl.ds(pl.multiple_of(other * 16, 16), 16), :] += to_other
         return 0
 
-    lax.fori_loop(0, pairs // UNROLL, visit, 0)
-
-    def finish(data_ref, sum_ref, out_ref):
-        def body(step, _):
-            start = pl.multiple_of(step * 8, 8)
-            *comps, charge = components(data_ref, start)
-
-            def total(part):
-                terms = [
-                    sum_ref[pl.ds(start * 16 + 4 * level + part, 8, stride=16), :]
-                    for level in range(3)
-                ]
-                return terms[0] + (terms[1] + terms[2])
-
-            weight = total(3)
-            scale = coulomb_scale * charge
-            for part, comp in enumerate(comps):
-                out_ref[pl.ds(4 * start + part, 8, stride=4), :] = scale * (
-                    comp * weight - total(part)
-                )
-            out_ref[pl.ds(4 * start + 3, 8, stride=4), :] = zeros
-            return 0
-
-        lax.fori_loop(0, data_ref.shape[0] // 32, body, 0)
-
-    finish(own_ref, own_sum_ref, own_out_ref)
-    finish(other_ref, other_sum_ref, other_out_ref)
+    lax.fori_loop(0, groups + 2, visit, 0)
+
+    def finish(data_ref, out_ref, start, rows_ref, base):
+        *comps, charge = components(data_ref, start)
+
+        def total(part):
+            terms = [
+                rows_ref[pl.ds(base + 4 * level + part, 8, stride=16), :] for level in range(3)
+            ]
+            return terms[0] + (terms[1] + terms[2])
+
+        weight = total(3)
+        scale = coulomb_scale * charge
+        for part, comp in enumerate(comps):
+            out_ref[pl.ds(4 * start + part, 8, stride=4), :] = scale * (comp * weight - total(part))
+        out_ref[pl.ds(4 * start + 3, 8, stride=4), :] = zeros
+
+    def finish_own(step, _):
+        start = pl.multiple_of(step * 8, 8)
+        lane = lax.broadcasted_iota(jnp.int32, (128, 128), 1)
+        columns = own_sum_ref[pl.ds(pl.multiple_of(start * 128, 128), 128), :]
+        for index in range(1, 8):
+            block = own_sum_ref[pl.ds(pl.multiple_of((start + index) * 128, 128), 128), :]
+            columns = jnp.where(lane < 16 * index, columns, pltpu.roll(block, 16 * index, 1))
+        stage_ref[0:128, :] = columns.T
+        finish(own_ref, own_out_ref, start, stage_ref, 0)
+        return 0
+
+    def finish_other(step, _):
+        start = pl.multiple_of(step * 8, 8)
+        finish(other_ref, other_out_ref, start, other_sum_ref, start * 16)
+        return 0
+
+    lax.fori_loop(0, clusters // 8, finish_own, 0)
+    lax.fori_loop(0, others // 8, finish_other, 0)
 
 
 def pair_forces(own_rows, other_rows, own, other):
@@ -251,12 +278,14 @@
             pltpu.VMEM((clusters * 32, 128), jnp.bfloat16),
             pltpu.VMEM(((others + 1) * 128, 128), jnp.bfloat16),
             pltpu.VMEM((clusters * 16, 128), jnp.bfloat16),
-            pltpu.VMEM((others * 16, 128), jnp.bfloat16),
-            pltpu.VMEM((clusters * 16, 128), jnp.float32),
+            pltpu.VMEM((others * 128, 128), jnp.bfloat16),
+            pltpu.VMEM((clusters * 128, 128), jnp.float32),
             pltpu.VMEM((others * 16, 128), jnp.float32),
             pltpu.VMEM((256, 128), jnp.float32),
+            pltpu.VMEM((UNROLL, 128, 128), jnp.float32),
+            pltpu.VMEM((UNROLL, 128, 256), jnp.bfloat16),
         ],
-        compiler_params=pltpu.CompilerParams(vmem_limit_bytes=40 * 1024 * 1024),
+        compiler_params=pltpu.CompilerParams(vmem_limit_bytes=48 * 1024 * 1024),
         cost_estimate=pl.CostEstimate(
             flops=pairs * 128 * 128 * 20, bytes_accessed=4 * 1024 * 1024, transcendentals=0
         ),

time: 395 us -> 287 us (0.73)
  Pallas kernels: 211 us -> 102 us
    pallas_call x1, Pallas kernels: 211 us -> 102 us  [pair_forces(): pl.pallas_call(pair_kernel, out_shape=(jax.ShapeDtypeStruct(own.shape, jn...]
  transfers between devices with their start and end apart: 32 -> 32, of which waited for: 3 -> 3; matrix products, arithmetic and copies ran while one was open for 7% -> 10% of each run, Pallas kernels for 54% -> 36%
where the time goes in v2:
time: 287 us; the launch traced here: 284 us
  Pallas kernels  102 us (36%)
  starting transfers between devices  93.7 us (33%)
  local copies, waits for them, and re-layouts  45.2 us (16%)
  other arithmetic  34.7 us (12%)
  waiting for transfers between devices  6.26 us (2%)
    pallas_call x1, Pallas kernels, pair_forces(): pl.pallas_call(pair_kernel, out_shape=(jax.ShapeDtypeStruct(own.shape, jn...  102 us
    another operation x4, local copies, waits for them, and re-layouts, field_of(): return jnp.stack([along_x, along_y, along_z])  37.3 us
    ppermute x12, starting transfers between devices, passed_along(): return lax.ppermute(shard, axis, pairs)  34.6 us
    ppermute x10, starting transfers between devices, extended(): before = lax.ppermute(last, axis, up)  30.5 us
    ppermute x10, starting transfers between devices, extended(): after = lax.ppermute(initial, axis, down)  28.6 us
    scatter-add x1, other arithmetic, shards(): coulomb = own_force.at[send_index.reshape(-1)].add(returned)  8.23 us
  transfers between devices with their start and end apart: 32, of which 3 were waited for; matrix products, arithmetic and copies ran while one was open for 10% of the time, Pallas kernels for 36%

profile of v2, /device:TPU:13, one launch (start us, length us, event | category | flops | bytes accessed | tf_op | source)
XLA Modules:
  0.0 283.6 jit_solution(1224534679159549690)
XLA Ops:
  0.6 0.8 fusion.65
  1.4 3.1 %collective-permute-start.13 = (f32[1,32,256]{2,1,0:T(8,128)S(1)}, f32[1,32,256]{2,1,0:T(8,128)S(1)}, u32[]{:S(2)}, u32[]{:S(2)}) collective-permute-start(f32[1,32,256]{2,1,0:T(8,128)S(1)} %get-tuple-element.42), channel_id=1, source_target_pairs={{0,8},{8,16},{16,24},{1,9},{9,17},{17,25},{2,10},{10,18},{18,26},{... | collective-permute-start | bytes 98312 | tf_op jit(solution)/shard_map/ppermute | solution.py:30
  4.5 3.1 %collective-permute-start.12 = (f32[1,32,256]{2,1,0:T(8,128)S(1)}, f32[1,32,256]{2,1,0:T(8,128)S(1)}, u32[]{:S(2)}, u32[]{:S(2)}) collective-permute-start(f32[1,32,256]{2,1,0:T(8,128)S(1)} %get-tuple-element.41), channel_id=1, source_target_pairs={{8,0},{16,8},{24,16},{9,1},{17,9},{25,17},{10,2},{18,10},{26,18},{... | collective-permute-start | bytes 98312 | tf_op jit(solution)/shard_map/ppermute | solution.py:31
  7.6 0.7 compare_select_fusion.3
  8.3 0.7 compare_select_fusion.1
  9.1 0.7 fusion.57
  9.8 1.2 compare_select_fusion
  11.0 1.3 pad_maximum_fusion.29
  12.3 0.9 gather_fusion
  13.9 4.5 %collective-permute-start = (f32[32,4,128]{2,1,0:T(4,128)S(1)}, f32[32,4,128]{2,1,0:T(4,128)S(1)}, u32[]{:S(2)}, u32[]{:S(2)}) collective-permute-start(f32[32,4,128]{2,1,0:T(4,128)S(1)} %get-tuple-element.30), channel_id=1, source_target_pairs={{0,1},{1,2},{2,3},{3,4},{4,5},{5,6},{6,7},{8,9},{9,10},{10,11},{11... | collective-permute-start | bytes 196616 | tf_op jit(solution)/shard_map/ppermute | solution.py:39
  18.3 1.9 collective-permute-start.1
  20.2 3.2 %collective-permute-start.2 = (f32[32,4,128]{2,1,0:T(4,128)S(1)}, f32[32,4,128]{2,1,0:T(4,128)S(1)}, u32[]{:S(2)}, u32[]{:S(2)}) collective-permute-start(f32[32,4,128]{2,1,0:T(4,128)S(1)} %get-tuple-element.32), channel_id=1, source_target_pairs={{0,2},{1,3},{2,4},{3,5},{4,6},{5,7},{8,10},{9,11},{10,12},{11,13},... | collective-permute-start | bytes 196616 | tf_op jit(solution)/shard_map/ppermute | solution.py:39
  23.5 0.8 fusion.43
  24.2 2.1 scatter_custom_fusion.1
  27.1 0.8 constant_dynamic-update-slice_fusion.1
  28.6 1.0 fusion.61
  29.6 2.7 collective-permute-start.14
  32.3 3.1 %collective-permute-start.15 = (f32[18,1,256]{2,1,0:T(1,128)S(1)}, f32[18,1,256]{2,1,0:T(1,128)S(1)}, u32[]{:S(2)}, u32[]{:S(2)}) collective-permute-start(f32[18,1,256]{2,1,0:T(1,128)S(1)} %get-tuple-element.26), channel_id=1, source_target_pairs={{0,1},{1,2},{2,3},{3,4},{4,5},{5,6},{6,7},{8,9},{9,10},{10,11},{11... | collective-permute-start | bytes 55304 | tf_op jit(solution)/shard_map/ppermute | solution.py:30
  35.6 2.2 collective-permute-start.3
  37.9 2.2 collective-permute-start.4
  40.1 1.6 select_maximum_fusion.17
  41.7 1.7 fusion.58
  43.5 4.0 %collective-permute-start.5 = (f32[32,4,128]{2,1,0:T(4,128)S(1)}, f32[32,4,128]{2,1,0:T(4,128)S(1)}, u32[]{:S(2)}, u32[]{:S(2)}) collective-permute-start(f32[32,4,128]{2,1,0:T(4,128)S(1)} %get-tuple-element.28), channel_id=1, source_target_pairs={{8,0},{16,8},{24,16},{9,1},{17,9},{25,17},{10,2},{18,10},{26,18},{... | collective-permute-start | bytes 196616 | tf_op jit(solution)/shard_map/ppermute | solution.py:39
  47.5 1.9 collective-permute-start.16
  49.4 3.4 %collective-permute-start.17 = (f32[1,32,256]{2,1,0:T(8,128)S(1)}, f32[1,32,256]{2,1,0:T(8,128)S(1)}, u32[]{:S(2)}, u32[]{:S(2)}) collective-permute-start(f32[1,32,256]{2,1,0:T(8,128)S(1)} %get-tuple-element.39), channel_id=1, source_target_pairs={{0,8},{8,16},{16,24},{1,9},{9,17},{17,25},{2,10},{10,18},{18,26},{... | collective-permute-start | bytes 98312 | tf_op jit(solution)/shard_map/ppermute | solution.py:30
  52.9 102.2 %pair_forces.1 = (f32[1024,128]{1,0:T(8,128)S(1)}, f32[896,128]{1,0:T(8,128)S(1)}) custom-call(s32[1024]{0:T(1024)S(1)} %copy-done, s32[1024]{0:T(1024)S(1)} %multiply_add_fusion.2.other_rows_ref, f32[1024,128]{1,0:T(8,128)S(1)} %bitcast.81, f32[896,128]{1,0:T(8,128)S(1)} %bitcast.84), custom_call_target="tpu_custom_call" | custom-call | flops 335544320 | bytes 4194304 | tf_op jit(solution)/shard_map/pair_forces/pallas_call | solution.py:269
  155.2 2.6 collective-permute-start.18
  157.8 3.0 %collective-permute-start.19 = (f32[18,1,256]{2,1,0:T(1,128)S(1)}, f32[18,1,256]{2,1,0:T(1,128)S(1)}, u32[]{:S(2)}, u32[]{:S(2)}) collective-permute-start(f32[18,1,256]{2,1,0:T(1,128)S(1)} %get-tuple-element.24), channel_id=1, source_target_pairs={{0,1},{1,2},{2,3},{3,4},{4,5},{5,6},{6,7},{8,9},{9,10},{10,11},{11... | collective-permute-start | bytes 55304 | tf_op jit(solution)/shard_map/ppermute | solution.py:30
  160.9 1.9 collective-permute-start.6
  162.8 3.6 %collective-permute-start.7 = (f32[32,3,128]{2,1,0:T(4,128)S(1)}, f32[32,3,128]{2,1,0:T(4,128)S(1)}, u32[]{:S(2)}, u32[]{:S(2)}) collective-permute-start(f32[32,3,128]{2,1,0:T(4,128)S(1)} %get-tuple-element.47), channel_id=1, source_target_pairs={{0,1},{1,2},{2,3},{3,4},{4,5},{5,6},{6,7},{8,9},{9,10},{10,11},{11... | collective-permute-start | bytes 147464 | tf_op jit(solution)/shard_map/ppermute | solution.py:39
  166.4 2.2 collective-permute-start.8
  168.7 3.1 %collective-permute-start.9 = (f32[32,3,128]{2,1,0:T(4,128)S(1)}, f32[32,3,128]{2,1,0:T(4,128)S(1)}, u32[]{:S(2)}, u32[]{:S(2)}) collective-permute-start(f32[32,3,128]{2,1,0:T(4,128)S(1)} %get-tuple-element.45), channel_id=1, source_target_pairs={{0,2},{1,3},{2,4},{3,5},{4,6},{5,7},{8,10},{9,11},{10,12},{11,13},... | collective-permute-start | bytes 147464 | tf_op jit(solution)/shard_map/ppermute | solution.py:39
  172.8 2.9 %collective-permute-start.20 = (f32[1,32,256]{2,1,0:T(8,128)S(1)}, f32[1,32,256]{2,1,0:T(8,128)S(1)}, u32[]{:S(2)}, u32[]{:S(2)}) collective-permute-start(f32[1,32,256]{2,1,0:T(8,128)S(1)} %get-tuple-element.38), channel_id=1, source_target_pairs={{8,0},{16,8},{24,16},{9,1},{17,9},{25,17},{10,2},{18,10},{26,18},{... | collective-permute-start | bytes 98312 | tf_op jit(solution)/shard_map/ppermute | solution.py:31
  175.8 2.3 collective-permute-start.21
  178.2 3.8 %collective-permute-start.10 = (f32[32,3,128]{2,1,0:T(4,128)S(1)}, f32[32,3,128]{2,1,0:T(4,128)S(1)}, u32[]{:S(2)}, u32[]{:S(2)}) collective-permute-start(f32[32,3,128]{2,1,0:T(4,128)S(1)} %get-tuple-element.44), channel_id=1, source_target_pairs={{8,0},{16,8},{24,16},{9,1},{17,9},{25,17},{10,2},{18,10},{26,18},{... | collective-permute-start | bytes 147464 | tf_op jit(solution)/shard_map/ppermute | solution.py:39
  182.1 2.3 collective-permute-start.22
  184.3 3.3 %collective-permute-start.23 = (f32[18,1,256]{2,1,0:T(1,128)S(1)}, f32[18,1,256]{2,1,0:T(1,128)S(1)}, u32[]{:S(2)}, u32[]{:S(2)}) collective-permute-start(f32[18,1,256]{2,1,0:T(1,128)S(1)} %get-tuple-element.22), channel_id=1, source_target_pairs={{0,1},{1,2},{2,3},{3,4},{4,5},{5,6},{6,7},{8,9},{9,10},{10,11},{11... | collective-permute-start | bytes 55304 | tf_op jit(solution)/shard_map/ppermute | solution.py:30
  187.7 1.9 collective-permute-start.11
  190.7 4.3 %collective-permute-start.24 = (f32[1,32,256]{2,1,0:T(8,128)S(1)}, f32[1,32,256]{2,1,0:T(8,128)S(1)}, u32[]{:S(2)}, u32[]{:S(2)}) collective-permute-start(f32[1,32,256]{2,1,0:T(8,128)S(1)} %get-tuple-element.36), channel_id=1, source_target_pairs={{8,0},{16,8},{24,16},{9,1},{17,9},{25,17},{10,2},{18,10},{26,18},{... | collective-permute-start | bytes 98312 | tf_op jit(solution)/shard_map/ppermute | solution.py:31
  194.9 1.9 collective-permute-start.25
  196.9 4.1 %collective-permute-done.25 = f32[1,32,256]{2,1,0:T(8,128)S(1)} collective-permute-done((f32[1,32,256]{2,1,0:T(8,128)S(1)}, f32[1,32,256]{2,1,0:T(8,128)S(1)}, u32[]{:S(2)}, u32[]{:S(2)}) %collective-permute-start.25) | collective-permute-done | bytes 32800 | tf_op jit(solution)/shard_map/ppermute | solution.py:30
  201.0 2.4 collective-permute-start.26
  203.5 3.1 %collective-permute-start.27 = (f32[18,1,256]{2,1,0:T(1,128)S(1)}, f32[18,1,256]{2,1,0:T(1,128)S(1)}, u32[]{:S(2)}, u32[]{:S(2)}) collective-permute-start(f32[18,1,256]{2,1,0:T(1,128)S(1)} %get-tuple-element.20), channel_id=1, source_target_pairs={{0,1},{1,2},{2,3},{3,4},{4,5},{5,6},{6,7},{8,9},{9,10},{10,11},{11... | collective-permute-start | bytes 55304 | tf_op jit(solution)/shard_map/ppermute | solution.py:30
  206.7 0.8 collective-permute-done.27
  208.0 1.1 fusion.20
  209.1 1.9 collective-permute-start.28
  211.0 4.3 %collective-permute-start.29 = (f32[2,1,32,256]{3,2,1,0:T(8,128)S(1)}, f32[2,1,32,256]{3,2,1,0:T(8,128)S(1)}, u32[]{:S(2)}, u32[]{:S(2)}) collective-permute-start(f32[2,1,32,256]{3,2,1,0:T(8,128)S(1)} %get-tuple-element.19), channel_id=1, source_target_pairs={{8,0},{16,8},{24,16},{9,1},{17,9},{25,17},{10,2},{18,10},{26,18},{... | collective-permute-start | bytes 196616 | tf_op jit(solution)/shard_map/ppermute | solution.py:31
  215.3 1.3 collective-permute-done.29
  216.7 5.3 %collective-permute-start.30 = (f32[2,18,1,256]{3,2,1,0:T(1,128)S(1)}, f32[2,18,1,256]{3,2,1,0:T(1,128)S(1)}, u32[]{:S(2)}, u32[]{:S(2)}) collective-permute-start(f32[2,18,1,256]{3,2,1,0:T(1,128)S(1)} %get-tuple-element.13), channel_id=1, source_target_pairs={{0,1},{1,2},{2,3},{3,4},{4,5},{5,6},{6,7},{8,9},{9,10},{10,11},{11... | collective-permute-start | bytes 110600 | tf_op jit(solution)/shard_map/ppermute | solution.py:30
  222.0 2.1 collective-permute-start.31
  224.2 8.2 %scatter_fusion = f32[256,3,128]{2,1,0:T(4,128)S(1)} fusion(f32[256,3,128]{2,1,0:T(4,128)S(1)} %bitcast.82, s32[224]{0:T(256)S(1)} %bitcast.97, f32[224,3,128]{2,1,0:T(4,128)S(1)} %bitcast.93), kind=kCustom, calls=%fused_computation.2 | custom fusion | flops 86016 | bytes 1033088 | tf_op jit(solution)/shard_map/scatter-add | solution.py:381
  232.4 1.0 select_maximum_fusion
  233.6 0.7 multiply_subtract_fusion
  234.3 0.8 multiply_subtract_fusion.1
  235.1 0.7 multiply_subtract_fusion.2
  235.7 1.9 fusion.14
  237.6 2.4 stack.80
  240.0 2.4 stack.81
  242.4 2.4 stack.82
  244.7 4.2 %pad_maximum_fusion = f32[3,131072]{1,0:T(4,128)} fusion(f32[1,131072]{1,0:T(1,128)} %stack.82, f32[1,131072]{1,0:T(1,128)} %stack.81, f32[1,131072]{1,0:T(1,128)} %stack.80), kind=kLoop, calls=%fused_computation.12 | loop fusion | flops 786432 | bytes 3145728 | tf_op jit(solution)/shard_map/stack | solution.py:321
  248.9 30.2 %copy.23 = f32[3,131072]{0,1:T(8,128)} copy(f32[3,131072]{1,0:T(4,128)} %pad_maximum_fusion) | data formatting | bytes 3145728 | tf_op jit(solution)/shard_map/stack | solution.py:321
  279.1 2.3 gather_fusion.1
  281.4 1.0 fusion.7
  282.5 1.1 fusion.39
  (89 shorter events, 5.3 us)
Async XLA Ops:
  1.4 25.1 %collective-permute-start.13 = (f32[1,32,256]{2,1,0:T(8,128)S(1)}, f32[1,32,256]{2,1,0:T(8,128)S(1)}, u32[]{:S(2)}, u32[]{:S(2)}) collective-permute-start(f32[1,32,256]{2,1,0:T(8,128)S(1)} %get-tuple-element.42), channel_id=1, source_target_pairs={{0,8},{8,16},{16,24},{1,9},{9,17},{17,25},{2,10},{10,18},{18,26},{... | collective-permute-start | bytes 98312 | tf_op jit(solution)/shard_map/ppermute | solution.py:30
  4.5 23.4 %collective-permute-start.12 = (f32[1,32,256]{2,1,0:T(8,128)S(1)}, f32[1,32,256]{2,1,0:T(8,128)S(1)}, u32[]{:S(2)}, u32[]{:S(2)}) collective-permute-start(f32[1,32,256]{2,1,0:T(8,128)S(1)} %get-tuple-element.41), channel_id=1, source_target_pairs={{8,0},{16,8},{24,16},{9,1},{17,9},{25,17},{10,2},{18,10},{26,18},{... | collective-permute-start | bytes 98312 | tf_op jit(solution)/shard_map/ppermute | solution.py:31
  12.3 11.1 %copy-start.6 = (f32[32768]{0:T(1024)S(1)}, f32[32768]{0:T(1024)}, u32[]{:S(2)}) copy-start(f32[32768]{0:T(1024)} %param.13) | copy-start | bytes 393220
  12.3 11.1 %copy-start.8 = (s32[256]{0:T(256)S(1)}, s32[256]{0:T(256)}, u32[]{:S(2)}) copy-start(s32[256]{0:T(256)} %param.14) | copy-start | bytes 3076
  13.8 12.6 %copy-start.9 = (s32[1024]{0:T(1024)S(1)}, s32[1024]{0:T(1024)}, u32[]{:S(2)}) copy-start(s32[1024]{0:T(1024)} %param.20) | copy-start | bytes 12292
  13.8 12.6 %copy-start.10 = (s32[1024]{0:T(1024)S(1)}, s32[1024]{0:T(1024)}, u32[]{:S(2)}) copy-start(s32[1024]{0:T(1024)} %param.19) | copy-start | bytes 12292
  13.8 12.6 %copy-start.7 = (s32[7,32]{1,0:T(8,128)S(1)}, s32[7,32]{1,0:T(8,128)}, u32[]{:S(2)}) copy-start(s32[7,32]{1,0:T(8,128)} %param.16) | copy-start | bytes 2692
  13.8 13.3 %copy-start.4 = (f32[16,32,256]{2,1,0:T(8,128)S(1)}, f32[16,32,256]{2,1,0:T(8,128)}, u32[]{:S(2)}) copy-start(f32[16,32,256]{2,1,0:T(8,128)} %param.22) | copy-start | bytes 1572868
  13.9 29.6 %collective-permute-start = (f32[32,4,128]{2,1,0:T(4,128)S(1)}, f32[32,4,128]{2,1,0:T(4,128)S(1)}, u32[]{:S(2)}, u32[]{:S(2)}) collective-permute-start(f32[32,4,128]{2,1,0:T(4,128)S(1)} %get-tuple-element.30), channel_id=1, source_target_pairs={{0,1},{1,2},{2,3},{3,4},{4,5},{5,6},{6,7},{8,9},{9,10},{10,11},{11... | collective-permute-start | bytes 196616 | tf_op jit(solution)/shard_map/ppermute | solution.py:39
  18.3 29.2 %collective-permute-start.1 = (f32[32,4,128]{2,1,0:T(4,128)S(1)}, f32[32,4,128]{2,1,0:T(4,128)S(1)}, u32[]{:S(2)}, u32[]{:S(2)}) collective-permute-start(f32[32,4,128]{2,1,0:T(4,128)S(1)} %get-tuple-element.31), channel_id=1, source_target_pairs={{1,0},{2,1},{3,2},{4,3},{5,4},{6,5},{7,6},{9,8},{10,9},{11,10},{12... | collective-permute-start | bytes 196616 | tf_op jit(solution)/shard_map/ppermute | solution.py:39
  20.2 29.2 %collective-permute-start.2 = (f32[32,4,128]{2,1,0:T(4,128)S(1)}, f32[32,4,128]{2,1,0:T(4,128)S(1)}, u32[]{:S(2)}, u32[]{:S(2)}) collective-permute-start(f32[32,4,128]{2,1,0:T(4,128)S(1)} %get-tuple-element.32), channel_id=1, source_target_pairs={{0,2},{1,3},{2,4},{3,5},{4,6},{5,7},{8,10},{9,11},{10,12},{11,13},... | collective-permute-start | bytes 196616 | tf_op jit(solution)/shard_map/ppermute | solution.py:39
  29.6 6.1 %collective-permute-start.14 = (f32[18,1,256]{2,1,0:T(1,128)S(1)}, f32[18,1,256]{2,1,0:T(1,128)S(1)}, u32[]{:S(2)}, u32[]{:S(2)}) collective-permute-start(f32[18,1,256]{2,1,0:T(1,128)S(1)} %get-tuple-element.27), channel_id=1, source_target_pairs={{1,0},{2,1},{3,2},{4,3},{5,4},{6,5},{7,6},{9,8},{10,9},{11,10},{12... | collective-permute-start | bytes 55304 | tf_op jit(solution)/shard_map/ppermute | solution.py:31
  32.3 5.5 %collective-permute-start.15 = (f32[18,1,256]{2,1,0:T(1,128)S(1)}, f32[18,1,256]{2,1,0:T(1,128)S(1)}, u32[]{:S(2)}, u32[]{:S(2)}) collective-permute-start(f32[18,1,256]{2,1,0:T(1,128)S(1)} %get-tuple-element.26), channel_id=1, source_target_pairs={{0,1},{1,2},{2,3},{3,4},{4,5},{5,6},{6,7},{8,9},{9,10},{10,11},{11... | collective-permute-start | bytes 55304 | tf_op jit(solution)/shard_map/ppermute | solution.py:30
  35.6 6.1 %copy-start.1 = (f32[16,32,256]{2,1,0:T(8,128)S(1)}, f32[16,32,256]{2,1,0:T(8,128)}, u32[]{:S(2)}) copy-start(f32[16,32,256]{2,1,0:T(8,128)} %param.21) | copy-start | bytes 1572868
  35.6 6.1 %copy-start.3 = (f32[16,32,256]{2,1,0:T(8,128)S(1)}, f32[16,32,256]{2,1,0:T(8,128)}, u32[]{:S(2)}) copy-start(f32[16,32,256]{2,1,0:T(8,128)} %param.23) | copy-start | bytes 1572868
  35.6 17.2 %collective-permute-start.3 = (f32[32,4,128]{2,1,0:T(4,128)S(1)}, f32[32,4,128]{2,1,0:T(4,128)S(1)}, u32[]{:S(2)}, u32[]{:S(2)}) collective-permute-start(f32[32,4,128]{2,1,0:T(4,128)S(1)} %get-tuple-element.33), channel_id=1, source_target_pairs={{2,0},{3,1},{4,2},{5,3},{6,4},{7,5},{10,8},{11,9},{12,10},{13,11},... | collective-permute-start | bytes 196616 | tf_op jit(solution)/shard_map/ppermute | solution.py:39
  37.9 15.0 %collective-permute-start.4 = (f32[32,4,128]{2,1,0:T(4,128)S(1)}, f32[32,4,128]{2,1,0:T(4,128)S(1)}, u32[]{:S(2)}, u32[]{:S(2)}) collective-permute-start(f32[32,4,128]{2,1,0:T(4,128)S(1)} %get-tuple-element.34), channel_id=1, source_target_pairs={{0,8},{8,16},{16,24},{1,9},{9,17},{17,25},{2,10},{10,18},{18,26},{... | collective-permute-start | bytes 196616 | tf_op jit(solution)/shard_map/ppermute | solution.py:39
  41.7 11.2 %copy-start = (s32[1024]{0:T(1024)S(1)}, s32[1024]{0:T(1024)}, u32[]{:S(2)}) copy-start(s32[1024]{0:T(1024)} %own_rows_ref.1) | copy-start | bytes 12292
  43.5 9.4 %collective-permute-start.5 = (f32[32,4,128]{2,1,0:T(4,128)S(1)}, f32[32,4,128]{2,1,0:T(4,128)S(1)}, u32[]{:S(2)}, u32[]{:S(2)}) collective-permute-start(f32[32,4,128]{2,1,0:T(4,128)S(1)} %get-tuple-element.28), channel_id=1, source_target_pairs={{8,0},{16,8},{24,16},{9,1},{17,9},{25,17},{10,2},{18,10},{26,18},{... | collective-permute-start | bytes 196616 | tf_op jit(solution)/shard_map/ppermute | solution.py:39
  47.5 107.7 %collective-permute-start.16 = (f32[1,32,256]{2,1,0:T(8,128)S(1)}, f32[1,32,256]{2,1,0:T(8,128)S(1)}, u32[]{:S(2)}, u32[]{:S(2)}) collective-permute-start(f32[1,32,256]{2,1,0:T(8,128)S(1)} %get-tuple-element.40), channel_id=1, source_target_pairs={{8,0},{16,8},{24,16},{9,1},{17,9},{25,17},{10,2},{18,10},{26,18},{... | collective-permute-start | bytes 98312 | tf_op jit(solution)/shard_map/ppermute | solution.py:31
  49.4 105.7 %collective-permute-start.17 = (f32[1,32,256]{2,1,0:T(8,128)S(1)}, f32[1,32,256]{2,1,0:T(8,128)S(1)}, u32[]{:S(2)}, u32[]{:S(2)}) collective-permute-start(f32[1,32,256]{2,1,0:T(8,128)S(1)} %get-tuple-element.39), channel_id=1, source_target_pairs={{0,8},{8,16},{16,24},{1,9},{9,17},{17,25},{2,10},{10,18},{18,26},{... | collective-permute-start | bytes 98312 | tf_op jit(solution)/shard_map/ppermute | solution.py:30
  155.2 13.4 %collective-permute-start.18 = (f32[18,1,256]{2,1,0:T(1,128)S(1)}, f32[18,1,256]{2,1,0:T(1,128)S(1)}, u32[]{:S(2)}, u32[]{:S(2)}) collective-permute-start(f32[18,1,256]{2,1,0:T(1,128)S(1)} %get-tuple-element.25), channel_id=1, source_target_pairs={{1,0},{2,1},{3,2},{4,3},{5,4},{6,5},{7,6},{9,8},{10,9},{11,10},{12... | collective-permute-start | bytes 55304 | tf_op jit(solution)/shard_map/ppermute | solution.py:31
  157.8 13.9 %collective-permute-start.19 = (f32[18,1,256]{2,1,0:T(1,128)S(1)}, f32[18,1,256]{2,1,0:T(1,128)S(1)}, u32[]{:S(2)}, u32[]{:S(2)}) collective-permute-start(f32[18,1,256]{2,1,0:T(1,128)S(1)} %get-tuple-element.24), channel_id=1, source_target_pairs={{0,1},{1,2},{2,3},{3,4},{4,5},{5,6},{6,7},{8,9},{9,10},{10,11},{11... | collective-permute-start | bytes 55304 | tf_op jit(solution)/shard_map/ppermute | solution.py:30
  160.9 14.9 %collective-permute-start.6 = (f32[32,3,128]{2,1,0:T(4,128)S(1)}, f32[32,3,128]{2,1,0:T(4,128)S(1)}, u32[]{:S(2)}, u32[]{:S(2)}) collective-permute-start(f32[32,3,128]{2,1,0:T(4,128)S(1)} %get-tuple-element.48), channel_id=1, source_target_pairs={{1,0},{2,1},{3,2},{4,3},{5,4},{6,5},{7,6},{9,8},{10,9},{11,10},{12... | collective-permute-start | bytes 147464 | tf_op jit(solution)/shard_map/ppermute | solution.py:39
  162.8 21.5 %collective-permute-start.7 = (f32[32,3,128]{2,1,0:T(4,128)S(1)}, f32[32,3,128]{2,1,0:T(4,128)S(1)}, u32[]{:S(2)}, u32[]{:S(2)}) collective-permute-start(f32[32,3,128]{2,1,0:T(4,128)S(1)} %get-tuple-element.47), channel_id=1, source_target_pairs={{0,1},{1,2},{2,3},{3,4},{4,5},{5,6},{6,7},{8,9},{9,10},{10,11},{11... | collective-permute-start | bytes 147464 | tf_op jit(solution)/shard_map/ppermute | solution.py:39
  166.4 28.5 %collective-permute-start.8 = (f32[32,3,128]{2,1,0:T(4,128)S(1)}, f32[32,3,128]{2,1,0:T(4,128)S(1)}, u32[]{:S(2)}, u32[]{:S(2)}) collective-permute-start(f32[32,3,128]{2,1,0:T(4,128)S(1)} %get-tuple-element.46), channel_id=1, source_target_pairs={{2,0},{3,1},{4,2},{5,3},{6,4},{7,5},{10,8},{11,9},{12,10},{13,11},... | collective-permute-start | bytes 147464 | tf_op jit(solution)/shard_map/ppermute | solution.py:39
  168.7 38.0 %collective-permute-start.9 = (f32[32,3,128]{2,1,0:T(4,128)S(1)}, f32[32,3,128]{2,1,0:T(4,128)S(1)}, u32[]{:S(2)}, u32[]{:S(2)}) collective-permute-start(f32[32,3,128]{2,1,0:T(4,128)S(1)} %get-tuple-element.45), channel_id=1, source_target_pairs={{0,2},{1,3},{2,4},{3,5},{4,6},{5,7},{8,10},{9,11},{10,12},{11,13},... | collective-permute-start | bytes 147464 | tf_op jit(solution)/shard_map/ppermute | solution.py:39
  172.8 5.3 %collective-permute-start.20 = (f32[1,32,256]{2,1,0:T(8,128)S(1)}, f32[1,32,256]{2,1,0:T(8,128)S(1)}, u32[]{:S(2)}, u32[]{:S(2)}) collective-permute-start(f32[1,32,256]{2,1,0:T(8,128)S(1)} %get-tuple-element.38), channel_id=1, source_target_pairs={{8,0},{16,8},{24,16},{9,1},{17,9},{25,17},{10,2},{18,10},{26,18},{... | collective-permute-start | bytes 98312 | tf_op jit(solution)/shard_map/ppermute | solution.py:31
  175.8 6.2 %collective-permute-start.21 = (f32[1,32,256]{2,1,0:T(8,128)S(1)}, f32[1,32,256]{2,1,0:T(8,128)S(1)}, u32[]{:S(2)}, u32[]{:S(2)}) collective-permute-start(f32[1,32,256]{2,1,0:T(8,128)S(1)} %get-tuple-element.37), channel_id=1, source_target_pairs={{0,8},{8,16},{16,24},{1,9},{9,17},{17,25},{2,10},{10,18},{18,26},{... | collective-permute-start | bytes 98312 | tf_op jit(solution)/shard_map/ppermute | solution.py:30
  178.2 37.1 %collective-permute-start.10 = (f32[32,3,128]{2,1,0:T(4,128)S(1)}, f32[32,3,128]{2,1,0:T(4,128)S(1)}, u32[]{:S(2)}, u32[]{:S(2)}) collective-permute-start(f32[32,3,128]{2,1,0:T(4,128)S(1)} %get-tuple-element.44), channel_id=1, source_target_pairs={{8,0},{16,8},{24,16},{9,1},{17,9},{25,17},{10,2},{18,10},{26,18},{... | collective-permute-start | bytes 147464 | tf_op jit(solution)/shard_map/ppermute | solution.py:39
  182.1 5.6 %collective-permute-start.22 = (f32[18,1,256]{2,1,0:T(1,128)S(1)}, f32[18,1,256]{2,1,0:T(1,128)S(1)}, u32[]{:S(2)}, u32[]{:S(2)}) collective-permute-start(f32[18,1,256]{2,1,0:T(1,128)S(1)} %get-tuple-element.23), channel_id=1, source_target_pairs={{1,0},{2,1},{3,2},{4,3},{5,4},{6,5},{7,6},{9,8},{10,9},{11,10},{12... | collective-permute-start | bytes 55304 | tf_op jit(solution)/shard_map/ppermute | solution.py:31
  184.3 5.3 %collective-permute-start.23 = (f32[18,1,256]{2,1,0:T(1,128)S(1)}, f32[18,1,256]{2,1,0:T(1,128)S(1)}, u32[]{:S(2)}, u32[]{:S(2)}) collective-permute-start(f32[18,1,256]{2,1,0:T(1,128)S(1)} %get-tuple-element.22), channel_id=1, source_target_pairs={{0,1},{1,2},{2,3},{3,4},{4,5},{5,6},{6,7},{8,9},{9,10},{10,11},{11... | collective-permute-start | bytes 55304 | tf_op jit(solution)/shard_map/ppermute | solution.py:30
  187.7 36.4 %collective-permute-start.11 = (f32[32,3,128]{2,1,0:T(4,128)S(1)}, f32[32,3,128]{2,1,0:T(4,128)S(1)}, u32[]{:S(2)}, u32[]{:S(2)}) collective-permute-start(f32[32,3,128]{2,1,0:T(4,128)S(1)} %get-tuple-element.43), channel_id=1, source_target_pairs={{0,8},{8,16},{16,24},{1,9},{9,17},{17,25},{2,10},{10,18},{18,26},{... | collective-permute-start | bytes 147464 | tf_op jit(solution)/shard_map/ppermute | solution.py:39
  190.7 6.2 %collective-permute-start.24 = (f32[1,32,256]{2,1,0:T(8,128)S(1)}, f32[1,32,256]{2,1,0:T(8,128)S(1)}, u32[]{:S(2)}, u32[]{:S(2)}) collective-permute-start(f32[1,32,256]{2,1,0:T(8,128)S(1)} %get-tuple-element.36), channel_id=1, source_target_pairs={{8,0},{16,8},{24,16},{9,1},{17,9},{25,17},{10,2},{18,10},{26,18},{... | collective-permute-start | bytes 98312 | tf_op jit(solution)/shard_map/ppermute | solution.py:31
  194.9 6.1 %collective-permute-start.25 = (f32[1,32,256]{2,1,0:T(8,128)S(1)}, f32[1,32,256]{2,1,0:T(8,128)S(1)}, u32[]{:S(2)}, u32[]{:S(2)}) collective-permute-start(f32[1,32,256]{2,1,0:T(8,128)S(1)} %get-tuple-element.35), channel_id=1, source_target_pairs={{0,8},{8,16},{16,24},{1,9},{9,17},{17,25},{2,10},{10,18},{18,26},{... | collective-permute-start | bytes 98312 | tf_op jit(solution)/shard_map/ppermute | solution.py:30
  201.0 5.6 %collective-permute-start.26 = (f32[18,1,256]{2,1,0:T(1,128)S(1)}, f32[18,1,256]{2,1,0:T(1,128)S(1)}, u32[]{:S(2)}, u32[]{:S(2)}) collective-permute-start(f32[18,1,256]{2,1,0:T(1,128)S(1)} %get-tuple-element.21), channel_id=1, source_target_pairs={{1,0},{2,1},{3,2},{4,3},{5,4},{6,5},{7,6},{9,8},{10,9},{11,10},{12... | collective-permute-start | bytes 55304 | tf_op jit(solution)/shard_map/ppermute | solution.py:31
  203.5 4.0 %collective-permute-start.27 = (f32[18,1,256]{2,1,0:T(1,128)S(1)}, f32[18,1,256]{2,1,0:T(1,128)S(1)}, u32[]{:S(2)}, u32[]{:S(2)}) collective-permute-start(f32[18,1,256]{2,1,0:T(1,128)S(1)} %get-tuple-element.20), channel_id=1, source_target_pairs={{0,1},{1,2},{2,3},{3,4},{4,5},{5,6},{6,7},{8,9},{9,10},{10,11},{11... | collective-permute-start | bytes 55304 | tf_op jit(solution)/shard_map/ppermute | solution.py:30
  209.1 23.3 %copy-start.2 = (f32[16,32,256]{2,1,0:T(8,128)}, f32[16,32,256]{2,1,0:T(8,128)S(1)}, u32[]{:S(2)}) copy-start(f32[16,32,256]{2,1,0:T(8,128)S(1)} %fusion.20) | copy-start | bytes 1572868
  209.1 6.2 %collective-permute-start.28 = (f32[2,1,32,256]{3,2,1,0:T(8,128)S(1)}, f32[2,1,32,256]{3,2,1,0:T(8,128)S(1)}, u32[]{:S(2)}, u32[]{:S(2)}) collective-permute-start(f32[2,1,32,256]{3,2,1,0:T(8,128)S(1)} %get-tuple-element.18), channel_id=1, source_target_pairs={{0,8},{8,16},{16,24},{1,9},{9,17},{17,25},{2,10},{10,18},{18,26},{... | collective-permute-start | bytes 196616 | tf_op jit(solution)/shard_map/ppermute | solution.py:30
  211.0 5.6 %collective-permute-start.29 = (f32[2,1,32,256]{3,2,1,0:T(8,128)S(1)}, f32[2,1,32,256]{3,2,1,0:T(8,128)S(1)}, u32[]{:S(2)}, u32[]{:S(2)}) collective-permute-start(f32[2,1,32,256]{3,2,1,0:T(8,128)S(1)} %get-tuple-element.19), channel_id=1, source_target_pairs={{8,0},{16,8},{24,16},{9,1},{17,9},{25,17},{10,2},{18,10},{26,18},{... | collective-permute-start | bytes 196616 | tf_op jit(solution)/shard_map/ppermute | solution.py:31
  216.7 15.7 %collective-permute-start.30 = (f32[2,18,1,256]{3,2,1,0:T(1,128)S(1)}, f32[2,18,1,256]{3,2,1,0:T(1,128)S(1)}, u32[]{:S(2)}, u32[]{:S(2)}) collective-permute-start(f32[2,18,1,256]{3,2,1,0:T(1,128)S(1)} %get-tuple-element.13), channel_id=1, source_target_pairs={{0,1},{1,2},{2,3},{3,4},{4,5},{5,6},{6,7},{8,9},{9,10},{10,11},{11... | collective-permute-start | bytes 110600 | tf_op jit(solution)/shard_map/ppermute | solution.py:30
  222.0 10.4 %collective-permute-start.31 = (f32[2,18,1,256]{3,2,1,0:T(1,128)S(1)}, f32[2,18,1,256]{3,2,1,0:T(1,128)S(1)}, u32[]{:S(2)}, u32[]{:S(2)}) collective-permute-start(f32[2,18,1,256]{3,2,1,0:T(1,128)S(1)} %get-tuple-element.14), channel_id=1, source_target_pairs={{1,0},{2,1},{3,2},{4,3},{5,4},{6,5},{7,6},{9,8},{10,9},{11,10},{12... | collective-permute-start | bytes 110600 | tf_op jit(solution)/shard_map/ppermute | solution.py:31
  281.4 1.0 copy-start.5

commit v3 on v2

--- a/solution.py
+++ b/solution.py
@@ -1,3 +1,5 @@
+import functools
+
 import jax
 import jax.numpy as jnp
 from jax import lax
@@ -7,6 +9,9 @@
 
 SWEEPS = 4
 UNROLL = 4
+HALO_WIDTHS = (SWEEPS + 1, SWEEPS, SWEEPS, 1)
+MARGIN = 8
+CELL_BITS = 8
 
 
 coulomb_scale = 0.02
@@ -20,59 +25,6 @@
 time_step = 0.2
 
 
-def extended(shard, sides, width):
-    for axis, dim in sides:
-        devices, length = (lax.axis_size(axis), shard.shape[dim])
-        up = [(i, (i + 1) % devices) for i in range(devices - 1)]
-        down = [(j, i) for i, j in up]
-        last = lax.slice_in_dim(shard, length - width, length, axis=dim)
-        initial = lax.slice_in_dim(shard, 0, width, axis=dim)
-        before = lax.ppermute(last, axis, up)
-        after = lax.ppermute(initial, axis, down)
-        shard = jnp.concatenate([before, shard, after], axis=dim)
-    return shard
-
-
-def passed_along(shard, axis, by):
-    devices = lax.axis_size(axis)
-    pairs = [(i, i + by) for i in range(devices) if 0 <= i + by < devices]
-    return lax.ppermute(shard, axis, pairs)
-
-
-def stencil_core(padded, center, screen):
-    beside = padded[2:, 1:-1, 1:-1] + padded[:-2, 1:-1, 1:-1]
-    beside = beside + padded[1:-1, 2:, 1:-1] + padded[1:-1, :-2, 1:-1]
-    beside = beside + padded[1:-1, 1:-1, 2:] + padded[1:-1, 1:-1, :-2]
-    return (6.0 + screen) * center - beside
-
-
-def operate_rim(field, screen):
-    rimmed = extended(field, (("grp", 0), ("brick", 1)), 1)
-    padded = jnp.pad(rimmed, ((0, 0), (0, 0), (1, 1)))
-    return stencil_core(padded, field, screen)
-
-
-def chebyshev(start, rhs, screen, operate, inside):
-    middle = 0.5 * (highest_eig + lowest_eig)
-    spread = 0.5 * (highest_eig - lowest_eig)
-    ratio_ms = middle / spread
-    weight_now = 1.0 / ratio_ms
-    inverse = 1.0 / (6.0 + screen)
-    solution = start
-    resid = rhs - operate(solution, screen)
-    update = inside * (inverse * resid / middle)
-    for turn in range(SWEEPS):
-        solution = solution + update
-        if turn + 1 < SWEEPS:
-            resid = resid - operate(update, screen)
-            weight_next = 1.0 / (2.0 * ratio_ms - weight_now)
-            update = inside * (
-                weight_next * weight_now * update + 2.0 * weight_next / spread * (inverse * resid)
-            )
-            weight_now = weight_next
-    return solution
-
-
 def split3(value):
     first = value.astype(jnp.bfloat16).astype(jnp.float32)
     rest = value - first
@@ -92,9 +44,30 @@
     own_rows_ref,
     other_rows_ref,
     own_ref,
-    other_ref,
+    *refs,
+):
+    sources = (len(refs) - 10) // 2
+    other_refs = refs[:sources]
+    own_out_ref = refs[sources]
+    other_out_refs = refs[sources + 1 : 2 * sources + 1]
+    pair_body(
+        own_rows_ref,
+        other_rows_ref,
+        own_ref,
+        other_refs,
+        own_out_ref,
+        other_out_refs,
+        *refs[2 * sources + 1 :],
+    )
+
+
+def pair_body(
+    own_rows_ref,
+    other_rows_ref,
+    own_ref,
+    other_refs,
     own_out_ref,
-    other_out_ref,
+    other_out_refs,
     near_ref,
     far_ref,
     own_moment_ref,
@@ -106,7 +79,8 @@
     weight_ref,
 ):
     clusters = own_ref.shape[0] // 4
-    others = other_ref.shape[0] // 4
+    slots = other_out_refs[0].shape[0] // 4
+    others = slots * len(other_refs)
     groups = own_rows_ref.shape[0] // UNROLL
     ones = jnp.ones((8, 128), jnp.float32)
     zeros = jnp.zeros((8, 128), jnp.float32)
@@ -146,9 +120,10 @@
             )
         return 0
 
-    def far_rows(step, _):
-        start = pl.multiple_of(step * 8, 8)
-        *comps, charge = components(other_ref, start)
+    def far_rows(source, step, _):
+        local = pl.multiple_of(step * 8, 8)
+        start = source * slots + local
+        *comps, charge = components(other_refs[source], local)
         moment_rows(comps, charge, stage_ref, 0)
         columns = stage_ref[0:128, :].T
         rows = []
@@ -171,7 +146,8 @@
         return 0
 
     lax.fori_loop(0, clusters // 8, near_rows, 0)
-    lax.fori_loop(0, others // 8, far_rows, 0)
+    for source in range(len(other_refs)):
+        lax.fori_loop(0, slots // 8, functools.partial(far_rows, source), 0)
     far_ref[pl.ds(others * 128, 128), :] = jnp.zeros((128, 128), jnp.bfloat16)
     other_sum_ref[...] = jnp.zeros_like(other_sum_ref)
     dist_ref[...] = jnp.full(dist_ref.shape, 1e38, jnp.float32)
@@ -251,18 +227,25 @@
         finish(own_ref, own_out_ref, start, stage_ref, 0)
         return 0
 
-    def finish_other(step, _):
+    def finish_other(source, step, _):
         start = pl.multiple_of(step * 8, 8)
-        finish(other_ref, other_out_ref, start, other_sum_ref, start * 16)
+        finish(
+            other_refs[source],
+            other_out_refs[source],
+            start,
+            other_sum_ref,
+            (source * slots + start) * 16,
+        )
         return 0
 
     lax.fori_loop(0, clusters // 8, finish_own, 0)
-    lax.fori_loop(0, others // 8, finish_other, 0)
-
-
-def pair_forces(own_rows, other_rows, own, other):
+    for source in range(len(other_refs)):
+        lax.fori_loop(0, slots // 8, functools.partial(finish_other, source), 0)
+
+
+def pair_forces(own_rows, other_rows, own, arrived, slots):
     clusters = own.shape[0] // 4
-    others = other.shape[0] // 4
+    others = slots * len(arrived)
     pairs = own_rows.shape[0]
     smem = pl.BlockSpec(memory_space=pltpu.SMEM)
     vmem = pl.BlockSpec(memory_space=pltpu.VMEM)
@@ -270,10 +253,10 @@
         pair_kernel,
         out_shape=(
             jax.ShapeDtypeStruct(own.shape, jnp.float32),
-            jax.ShapeDtypeStruct(other.shape, jnp.float32),
+            *[jax.ShapeDtypeStruct((slots * 4, 128), jnp.float32)] * len(arrived),
         ),
-        in_specs=[smem, smem, vmem, vmem],
-        out_specs=(vmem, vmem),
+        in_specs=[smem, smem, vmem] + [vmem] * len(arrived),
+        out_specs=(vmem,) * (len(arrived) + 1),
         scratch_shapes=[
             pltpu.VMEM((clusters * 32, 128), jnp.bfloat16),
             pltpu.VMEM(((others + 1) * 128, 128), jnp.bfloat16),
@@ -290,35 +273,414 @@
             flops=pairs * 128 * 128 * 20, bytes_accessed=4 * 1024 * 1024, transcendentals=0
         ),
         name="pair_forces",
-    )(own_rows, other_rows, own, other)
-
-
-def face_div(pot, ions, axis):
-    inner = [slice(1, -1), slice(1, -1), slice(1, -1)]
-    inner[axis] = slice(None)
-    pot = pot[tuple(inner)]
-    ions = ions[tuple(inner)]
-
-    def upper(arr):
-        return lax.slice_in_dim(arr, 1, arr.shape[axis], axis=axis)
-
-    def lower(arr):
-        return lax.slice_in_dim(arr, 0, arr.shape[axis] - 1, axis=axis)
-
-    speed = -mobility * (upper(pot) - lower(pot))
-    flux = (
-        jnp.maximum(speed, 0.0) * lower(ions)
-        + jnp.minimum(speed, 0.0) * upper(ions)
-        - diffusion * (upper(ions) - lower(ions))
+    )(own_rows, other_rows, own, *arrived)
+
+
+def prepare_kernel(
+    fill_ref,
+    cell_ref,
+    send_index_ref,
+    send_count_ref,
+    position_ref,
+    charge_ref,
+    ion_ref,
+    start_ref,
+    screen_ref,
+    own_ref,
+    masked_ref,
+    inverse_ref,
+    source_ref,
+    *refs,
+):
+    out_refs, (sum_ref, deposit_ref) = (refs[:-2], refs[-2:])
+    clusters = charge_ref.shape[0]
+    cells_x, cells_y, _ = ion_ref.shape
+    slots = send_index_ref.shape[1]
+    lane = lax.broadcasted_iota(jnp.int32, (1, 128), 1)
+    row = lax.broadcasted_iota(jnp.int32, (4, 128), 0)
+
+    def collect(step, _):
+        for turn in range(8):
+            cluster = step * 8 + turn
+            masked = jnp.where(lane < fill_ref[cluster], charge_ref[pl.ds(cluster, 1), :], 0.0)
+            masked_ref[pl.ds(cluster, 1), :] = masked
+            place = position_ref[:, pl.ds(pl.multiple_of(cluster * 128, 128), 128)]
+            own_ref[cluster, 0:3, :] = place
+            own_ref[cluster, 3:4, :] = masked
+        at = pl.ds(pl.multiple_of(step * 8, 8), 8)
+        total = jnp.sum(masked_ref[at, :], axis=1, keepdims=True)
+        sum_ref[at, :] = jnp.broadcast_to(deposit_scale * total, (8, 128))
+        return 0
+
+    lax.fori_loop(0, clusters // 8, collect, 0)
+
+    def fill_messages(step, _):
+        for direction, out_ref in enumerate(out_refs):
+            parts = []
+            for turn in range(2):
+                slot = step * 2 + turn
+                live = jnp.where(slot < send_count_ref[0, direction], 1.0, 0.0)
+                value = own_ref[send_index_ref[direction, slot]]
+                parts.append(jnp.where(row == 3, value * live, value))
+            out_ref[pl.ds(pl.multiple_of(step * 8, 8), 8), :] = jnp.concatenate(parts, axis=0)
+        return 0
+
+    lax.fori_loop(0, slots // 2, fill_messages, 0)
+
+    deposit_ref[...] = jnp.zeros_like(deposit_ref)
+
+    def deposit(cluster, _):
+        cell = cell_ref[cluster]
+        index_x = lax.shift_right_logical(cell, CELL_BITS) // cells_y
+        index_y = lax.shift_right_logical(cell, CELL_BITS) % cells_y
+        index_z = lax.bitwise_and(cell, 255)
+        half = lax.shift_right_logical(index_z, 7)
+        added = jnp.where(
+            lane == lax.bitwise_and(index_z, 127), sum_ref[pl.ds(cluster, 1), :], 0.0
+        )
+        deposit_ref[pl.ds((index_x * 2 + half) * cells_y + index_y, 1), :] += added
+        return 0
+
+    lax.fori_loop(0, clusters, deposit, 0, unroll=4)
+    inverse_ref[...] = 1.0 / (6.0 + screen_ref[...])
+    for index in range(cells_x):
+        for half in range(2):
+            lanes = slice(128 * half, 128 * half + 128)
+            first = (index * 2 + half) * cells_y
+            source_ref[index, :, lanes] = (
+                ion_ref[index, :, lanes] + deposit_ref[first : first + cells_y, :]
+            ) * inverse_ref[index, :, lanes]
+    for out_ref, after in ((out_refs[1], True), (out_refs[2], False)):
+        for index in range(cells_x):
+            base = slots * 4 + index * 32
+            offset = 0
+            for field_ref, width in zip(
+                (start_ref, inverse_ref, source_ref, ion_ref), HALO_WIDTHS, strict=True
+            ):
+                first = cells_y - width if after else 0
+                rows = field_ref[index, first : first + width, :]
+                for half in range(2):
+                    out_ref[base + 16 * half + offset : base + 16 * half + offset + width, :] = (
+                        rows[:, 128 * half : 128 * half + 128]
+                    )
+                offset += width
+            for half in range(2):
+                out_ref[base + 16 * half + offset : base + 16 * half + 16, :] = jnp.zeros(
+                    (16 - offset, 128), jnp.float32
+                )
+
+
+def prepare(fill, cell, send_index, send_count, positions, charges, ions, start, screen):
+    clusters = charges.shape[0]
+    directions, slots = send_index.shape
+    cells_x = ions.shape[0]
+    smem = pl.BlockSpec(memory_space=pltpu.SMEM)
+    vmem = pl.BlockSpec(memory_space=pltpu.VMEM)
+    rows = [slots * 4] * directions
+    rows[1] = rows[2] = slots * 4 + cells_x * 32
+    return pl.pallas_call(
+        prepare_kernel,
+        out_shape=(
+            jax.ShapeDtypeStruct((clusters, 4, 128), jnp.float32),
+            jax.ShapeDtypeStruct((clusters, 128), jnp.float32),
+            jax.ShapeDtypeStruct(ions.shape, jnp.float32),
+            jax.ShapeDtypeStruct(ions.shape, jnp.float32),
+            *[jax.ShapeDtypeStruct((count, 128), jnp.float32) for count in rows],
+        ),
+        in_specs=[smem] * 4 + [vmem] * 5,
+        out_specs=(vmem,) * (4 + directions),
+        scratch_shapes=[
+            pltpu.VMEM((clusters, 128), jnp.float32),
+            pltpu.VMEM((ions.size // 128, 128), jnp.float32),
+        ],
+        compiler_params=pltpu.CompilerParams(vmem_limit_bytes=32 * 1024 * 1024),
+        name="prepare",
+    )(fill, cell, send_index, send_count, positions, charges, ions, start, screen)
+
+
+def put_extended(target_ref, plane, field, field_ref, index, before_ref, after_ref, base):
+    cells_y = field_ref.shape[1]
+    width = HALO_WIDTHS[field]
+    offset = sum(HALO_WIDTHS[:field])
+    target_ref[plane, MARGIN : MARGIN + cells_y, :] = field_ref[index]
+    for half in range(2):
+        lanes = slice(128 * half, 128 * half + 128)
+        first = base + index * 32 + 16 * half + offset
+        target_ref[plane, MARGIN - width : MARGIN, lanes] = before_ref[first : first + width, :]
+        target_ref[plane, MARGIN + cells_y : MARGIN + cells_y + width, lanes] = after_ref[
+            first : first + width, :
+        ]
+
+
+def planes_kernel(base, *refs):
+    field_refs, (before_ref, after_ref, down_ref, up_ref) = (refs[:4], refs[4:])
+    cells_x = field_refs[0].shape[0]
+    down_ref[...] = jnp.zeros_like(down_ref)
+    up_ref[...] = jnp.zeros_like(up_ref)
+    plane = 0
+    for field, width in enumerate(HALO_WIDTHS):
+        for index in range(width):
+            for target_ref, source in ((down_ref, index), (up_ref, cells_x - width + index)):
+                put_extended(
+                    target_ref, plane, field, field_refs[field], source, before_ref, after_ref, base
+                )
+            plane += 1
+
+
+def planes(fields, before, after, base):
+    vmem = pl.BlockSpec(memory_space=pltpu.VMEM)
+    _, cells_y, cells_z = fields[0].shape
+    shape = jax.ShapeDtypeStruct((sum(HALO_WIDTHS), cells_y + 2 * MARGIN, cells_z), jnp.float32)
+    return pl.pallas_call(
+        functools.partial(planes_kernel, base),
+        out_shape=(shape, shape),
+        in_specs=[vmem] * 6,
+        out_specs=(vmem, vmem),
+        compiler_params=pltpu.CompilerParams(vmem_limit_bytes=32 * 1024 * 1024),
+        name="planes",
+    )(*fields, before, after)
+
+
+def face_flux(pot_low, pot_high, ion_low, ion_high):
+    speed = -mobility * (pot_high - pot_low)
+    return (
+        jnp.maximum(speed, 0.0) * ion_low
+        + jnp.minimum(speed, 0.0) * ion_high
+        - diffusion * (ion_high - ion_low)
     )
-    return upper(flux) - lower(flux)
-
-
-def field_of(padded):
-    along_x = -(padded[2:, 1:-1, 1:-1] - padded[:-2, 1:-1, 1:-1]) * 0.5
-    along_y = -(padded[1:-1, 2:, 1:-1] - padded[1:-1, :-2, 1:-1]) * 0.5
-    along_z = -(padded[1:-1, 1:-1, 2:] - padded[1:-1, 1:-1, :-2]) * 0.5
-    return jnp.stack([along_x, along_y, along_z])
+
+
+def grid_kernel(base, *refs):
+    cell_ref, masked_ref = refs[:2]
+    field_refs = refs[2:6]
+    before_ref, after_ref, lower_ref, upper_ref = refs[6:10]
+    potential_ref, next_ref, force_ref = refs[10:13]
+    start_ref, inverse_ref, resid_ref, ion_ref, update_ref, line_ref, *pick_refs = refs[13:]
+    cells_x, cells_y, cells_z = field_refs[0].shape
+    rows = cells_y + 2 * MARGIN
+    depth = HALO_WIDTHS[0]
+    clusters = masked_ref.shape[0]
+    lane = lax.broadcasted_iota(jnp.int32, (rows, cells_z), 1)
+    middle = 0.5 * (highest_eig + lowest_eig)
+    spread = 0.5 * (highest_eig - lowest_eig)
+
+    plane = 0
+    for field, target_ref in enumerate((start_ref, inverse_ref, resid_ref, ion_ref)):
+        width = HALO_WIDTHS[field]
+        if field == 0 or field == 3:
+            target_ref[...] = jnp.zeros_like(target_ref)
+        else:
+            target_ref[depth : depth + cells_x, 0:MARGIN, :] = jnp.zeros(
+                (cells_x, MARGIN, cells_z), jnp.float32
+            )
+            target_ref[depth : depth + cells_x, rows - MARGIN : rows, :] = jnp.zeros(
+                (cells_x, MARGIN, cells_z), jnp.float32
+            )
+        for index in range(width):
+            target_ref[depth - width + index] = lower_ref[plane + index]
+            target_ref[depth + cells_x + index] = upper_ref[plane + index]
+        for index in range(cells_x):
+            put_extended(
+                target_ref,
+                depth + index,
+                field,
+                field_refs[field],
+                index,
+                before_ref,
+                after_ref,
+                base,
+            )
+        plane += width
+
+    def above(value):
+        return jnp.where(lane == cells_z - 1, 0.0, pltpu.roll(value, cells_z - 1, 1))
+
+    def below(value):
+        return jnp.where(lane == 0, 0.0, pltpu.roll(value, 1, 1))
+
+    def beside(value):
+        rolled = pltpu.roll(value, 1, 0) + pltpu.roll(value, rows - 1, 0)
+        return rolled + (above(value) + below(value))
+
+    def first_sweep(index, planes):
+        last, here = planes
+        after = start_ref[index + 1]
+        resid = (
+            resid_ref[index] - here + inverse_ref[index] * ((last + after) + beside(here))
+        )
+        resid_ref[index] = resid
+        update_ref[index] = resid / middle
+        return (here, after)
+
+    lax.fori_loop(1, cells_x + 2 * depth - 1, first_sweep, (start_ref[0], start_ref[1]))
+
+    ratio_ms = middle / spread
+    weight_now = 1.0 / ratio_ms
+    for turn in range(1, SWEEPS):
+        weight_next = 1.0 / (2.0 * ratio_ms - weight_now)
+        keep, gain = (weight_next * weight_now, 2.0 * weight_next / spread)
+        weight_now = weight_next
+
+        def sweep(index, planes, turn=turn, keep=keep, gain=gain):
+            last, here = planes
+            after = update_ref[index + 1]
+            resid = resid_ref[index] - here + inverse_ref[index] * ((last + after) + beside(here))
+            update = keep * here + gain * resid
+            if turn == 1:
+                start_ref[index] = start_ref[index] + here + update
+            else:
+                start_ref[index] = start_ref[index] + update
+            if turn + 1 < SWEEPS:
+                resid_ref[index] = resid
+                update_ref[index] = update
+            return (here, after)
+
+        first = 1 + turn
+        lax.fori_loop(
+            first,
+            cells_x + 2 * depth - first,
+            sweep,
+            (update_ref[first - 1], update_ref[first]),
+        )
+
+    def upper_flux(index):
+        return face_flux(start_ref[index], start_ref[index + 1], ion_ref[index], ion_ref[index + 1])
+
+    inner = slice(MARGIN, MARGIN + cells_y)
+
+    def advance(index, lower):
+        pot = start_ref[depth + index]
+        ions = ion_ref[depth + index]
+        upper = upper_flux(depth + index)
+        along_y = face_flux(pot, pltpu.roll(pot, rows - 1, 0), ions, pltpu.roll(ions, rows - 1, 0))
+        along_z = face_flux(pot, above(pot), ions, above(ions))
+        first_z = face_flux(0.0, pot, 0.0, ions)
+        total = upper - lower
+        total = total + (along_y - pltpu.roll(along_y, 1, 0))
+        total = total + (along_z - jnp.where(lane == 0, first_z, pltpu.roll(along_z, 1, 1)))
+        next_ref[index] = (ions - time_step * total)[inner]
+        potential_ref[index] = pot[inner]
+        return upper
+
+    lax.fori_loop(0, cells_x, advance, upper_flux(depth - 1))
+    for index in range(cells_x + 2):
+        for half in range(2):
+            line_ref[pl.ds((index * 2 + half) * rows, rows), :] = start_ref[
+                depth - 1 + index, :, 128 * half : 128 * half + 128
+            ]
+
+    row_lane = lax.broadcasted_iota(jnp.int32, (1, 128), 1)
+
+    def pick(cluster, _):
+        cell = cell_ref[cluster]
+        index_x = lax.shift_right_logical(cell, CELL_BITS) // cells_y + 1
+        index_y = lax.shift_right_logical(cell, CELL_BITS) % cells_y + MARGIN
+        index_z = lax.bitwise_and(cell, 255)
+        half = lax.shift_right_logical(index_z, 7)
+        here = row_lane == lax.bitwise_and(index_z, 127)
+
+        def line(plane, row, part):
+            return line_ref[pl.ds((plane * 2 + part) * rows + row, 1), :]
+
+        along_x = line(index_x - 1, index_y, half) - line(index_x + 1, index_y, half)
+        along_y = line(index_x, index_y - 1, half) - line(index_x, index_y + 1, half)
+        along_z = jnp.zeros((1, 128), jnp.float32)
+        for part in range(cells_z // 128):
+            value = line(index_x, index_y, part)
+            place = row_lane + 128 * part
+            along_z = along_z + jnp.where(place == index_z - 1, value, 0.0)
+            along_z = along_z - jnp.where(place == index_z + 1, value, 0.0)
+        at = pl.ds(cluster, 1)
+        pick_refs[0][at, :] = jnp.where(here, along_x, 0.0)
+        pick_refs[1][at, :] = jnp.where(here, along_y, 0.0)
+        pick_refs[2][at, :] = along_z
+        return 0
+
+    lax.fori_loop(0, clusters, pick, 0, unroll=4)
+
+    def spread_out(step, _):
+        start = pl.multiple_of(step * 8, 8)
+        charge = masked_ref[pl.ds(start, 8), :] * (0.5 * field_scale)
+        for part, pick_ref in enumerate(pick_refs):
+            total = jnp.sum(pick_ref[pl.ds(start, 8), :], axis=1, keepdims=True)
+            force_ref[pl.ds(4 * start + part, 8, stride=4), :] = charge * total
+        force_ref[pl.ds(4 * start + 3, 8, stride=4), :] = jnp.zeros((8, 128), jnp.float32)
+        return 0
+
+    lax.fori_loop(0, clusters // 8, spread_out, 0)
+
+
+def grid_step(cell, masked, fields, before, after, lower, upper, base):
+    smem = pl.BlockSpec(memory_space=pltpu.SMEM)
+    vmem = pl.BlockSpec(memory_space=pltpu.VMEM)
+    clusters = masked.shape[0]
+    cells_x, cells_y, cells_z = fields[0].shape
+    block = (cells_x + 2 * HALO_WIDTHS[0], cells_y + 2 * MARGIN, cells_z)
+    return pl.pallas_call(
+        functools.partial(grid_kernel, base),
+        out_shape=(
+            jax.ShapeDtypeStruct(fields[0].shape, jnp.float32),
+            jax.ShapeDtypeStruct(fields[0].shape, jnp.float32),
+            jax.ShapeDtypeStruct((clusters * 4, 128), jnp.float32),
+        ),
+        in_specs=[smem] + [vmem] * 9,
+        out_specs=(vmem,) * 3,
+        scratch_shapes=[pltpu.VMEM(block, jnp.float32)] * 5
+        + [pltpu.VMEM(((cells_x + 2) * 2 * block[1], 128), jnp.float32)]
+        + [pltpu.VMEM((clusters, 128), jnp.float32)] * 3,
+        compiler_params=pltpu.CompilerParams(vmem_limit_bytes=40 * 1024 * 1024),
+        cost_estimate=pl.CostEstimate(
+            flops=block[0] * block[1] * block[2] * 100, bytes_accessed=8 << 20, transcendentals=0
+        ),
+        name="grid_step",
+    )(cell, masked, *fields, before, after, lower, upper)
+
+
+def gather_forces_kernel(send_index_ref, own_ref, field_ref, *refs):
+    back_refs, (out_ref, sum_ref) = (refs[:-2], refs[-2:])
+    clusters = own_ref.shape[0]
+    slots = send_index_ref.shape[1]
+    sum_ref[...] = own_ref[...] + field_ref[...]
+
+    def visit(slot, _):
+        for direction, back_ref in enumerate(back_refs):
+            cluster = send_index_ref[direction, slot]
+            sum_ref[cluster] += back_ref[slot]
+        return 0
+
+    lax.fori_loop(0, slots, visit, 0)
+
+    def write(step, _):
+        for turn in range(8):
+            cluster = step * 8 + turn
+            out_ref[:, pl.ds(pl.multiple_of(cluster * 128, 128), 128)] = sum_ref[cluster][0:3]
+        return 0
+
+    lax.fori_loop(0, clusters // 8, write, 0)
+
+
+def gather_forces(send_index, own, field, backs):
+    smem = pl.BlockSpec(memory_space=pltpu.SMEM)
+    vmem = pl.BlockSpec(memory_space=pltpu.VMEM)
+    clusters = own.shape[0]
+    return pl.pallas_call(
+        gather_forces_kernel,
+        out_shape=jax.ShapeDtypeStruct((3, clusters * 128), jnp.float32),
+        in_specs=[smem] + [vmem] * (2 + len(backs)),
+        out_specs=vmem,
+        scratch_shapes=[pltpu.VMEM(own.shape, jnp.float32)],
+        compiler_params=pltpu.CompilerParams(vmem_limit_bytes=32 * 1024 * 1024),
+        name="gather_forces",
+    )(send_index, own, field, *backs)
+
+
+def passed_along(shard, axis, by):
+    devices = lax.axis_size(axis)
+    pairs = [(i, i + by) for i in range(devices) if 0 <= i + by < devices]
+    return lax.ppermute(shard, axis, pairs)
+
+
+ROUTES = (("brick", 1), ("brick", -1), ("brick", 2), ("brick", -2), ("grp", 1), ("grp", -1))
 
 
 def shards(
@@ -337,61 +699,49 @@
 ):
     clusters = cluster_fill.shape[0]
     psize = charges.shape[0] // clusters
-    directions = send_index.shape[0]
     slots = send_index.shape[1]
-    lanes = jnp.arange(psize, dtype=jnp.int32)
-    qmask = charges.reshape(clusters, psize) * (lanes[None, :] < cluster_fill[:, None]).astype(
-        jnp.float32
+    base = slots * 4
+    own, masked, inverse, source, local, *messages = prepare(
+        cluster_fill,
+        cluster_cell,
+        send_index,
+        send_count,
+        positions,
+        charges.reshape(clusters, psize),
+        ion_density,
+        potential_prev,
+        screening,
     )
-    cluster_data = jnp.concatenate(
-        [positions.reshape(3, clusters, psize).transpose(1, 0, 2), qmask[:, None, :]], axis=1
+    arrived = [local] + [
+        passed_along(message, axis, by)
+        for message, (axis, by) in zip(messages, ROUTES, strict=True)
+    ]
+    fields = (potential_prev, inverse, source, ion_density)
+    before, after = arrived[1:3]
+    down, up = planes(fields, before, after, base)
+    lower = passed_along(up, "grp", 1)
+    upper = passed_along(down, "grp", -1)
+    own_force, *reactions = pair_forces(
+        pair_local,
+        pair_dir * slots + pair_slot,
+        own.reshape(clusters * 4, psize),
+        arrived,
+        slots,
     )
-    cells_x, cells_y, cells_z = ion_density.shape
-    deposit = (
-        jnp.zeros(cells_x * cells_y * cells_z, jnp.float32)
-        .at[cluster_cell]
-        .add(jnp.sum(qmask, axis=1))
+    backs = [reactions[0]] + [
+        passed_along(reaction, axis, -by)
+        for reaction, (axis, by) in zip(reactions[1:], ROUTES, strict=True)
+    ]
+    potential, ion_next, field_force = grid_step(
+        cluster_cell, masked, fields, before, after, lower, upper, base
     )
-    rhs = ion_density + deposit_scale * deposit.reshape(cells_x, cells_y, cells_z)
-    slot_ids = jnp.arange(slots, dtype=jnp.int32)
-    slot_live = (slot_ids[None, :] < send_count.reshape(directions, 1)).astype(jnp.float32)
-    outgoing = cluster_data[send_index]
-    outgoing = jnp.concatenate(
-        [outgoing[:, :, :3], (outgoing[:, :, 3] * slot_live[:, :, None])[:, :, None]], axis=2
+    forces = gather_forces(
+        send_index,
+        own_force.reshape(clusters, 4, psize),
+        field_force.reshape(clusters, 4, psize),
+        [back.reshape(slots, 4, psize) for back in backs],
     )
-    pieces = [outgoing[0]]
-    for offset in (-1, 1, -2, 2):
-        pieces.append(passed_along(outgoing[len(pieces)], "brick", -offset))
-    for offset in (-1, 1):
-        pieces.append(passed_along(outgoing[len(pieces)], "grp", -offset))
-    arrived = jnp.stack(pieces).reshape(directions * slots, 4, psize)
-    partner_row = pair_dir * slots + pair_slot
-
-    own_force, react = pair_forces(
-        pair_local, partner_row, cluster_data.reshape(-1, psize), arrived.reshape(-1, psize)
-    )
-    own_force = own_force.reshape(clusters, 4, psize)[:, :3]
-    react = react.reshape(directions, slots, 4, psize)[:, :, :3]
-    backs = [react[0]]
-    for offset in (-1, 1, -2, 2):
-        backs.append(passed_along(react[len(backs)], "brick", offset))
-    for offset in (-1, 1):
-        backs.append(passed_along(react[len(backs)], "grp", offset))
-    returned = jnp.stack(backs).reshape(directions * slots, 3, psize)
-    coulomb = own_force.at[send_index.reshape(-1)].add(returned)
-    potential = chebyshev(potential_prev, rhs, screening, operate_rim, 1.0)
-    rimmed = extended(jnp.stack([potential, ion_density]), (("grp", 1), ("brick", 2)), 1)
-    rimmed = jnp.pad(rimmed, ((0, 0), (0, 0), (0, 0), (1, 1)))
-    padded_pot = rimmed[0]
-    padded_ion = rimmed[1]
-    ion_next = ion_density - time_step * (
-        face_div(padded_pot, padded_ion, 0)
-        + face_div(padded_pot, padded_ion, 1)
-        + face_div(padded_pot, padded_ion, 2)
-    )
-    ecell = field_of(padded_pot).reshape(3, -1)[:, cluster_cell]
-    forces = coulomb.transpose(1, 0, 2) + field_scale * qmask[None] * ecell[:, :, None]
-    return (forces.reshape(3, -1), potential, ion_next)
+    return (forces, potential, ion_next)
 
 
 def solution(mesh):

time: 287 us -> 205 us (0.71)
  starting transfers between devices: 93.7 us -> 40.4 us
  local copies, waits for them, and re-layouts: 45.2 us -> 7.81 us
  other arithmetic: 34.7 us -> 0.01 us
  Pallas kernels: 102 us -> 130 us
  waiting for transfers between devices: 6.26 us -> 24.6 us
    ppermute x20 -> x0, starting transfers between devices: 59.1 us -> none  [the longest x10 30.5 us: extended(): before = lax.ppermute(last, axis, up)]
    another operation x6 -> x0, local copies, waits for them, and re-layouts: 37.4 us -> none  [the longest x4 37.3 us: field_of(): return jnp.stack([along_x, along_y, along_z])]
    pallas_call x0 -> x4, Pallas kernels: none -> 28.1 us  [the longest x1 18.7 us: grid_step(): pl.pallas_call(functools.partial(grid_kernel, base), out_shape=(jax.Shape...]
    ppermute x12 -> x14, waiting for transfers between devices: 0.03 us -> 24.6 us  [passed_along(): return lax.ppermute(shard, axis, pairs)]
    scatter-add x2 -> x0, other arithmetic: 10.3 us -> none  [the longest x1 8.23 us: shards(): coulomb = own_force.at[send_index.reshape(-1)].add(returned)]
    ppermute x20 -> x0, waiting for transfers between devices: 6.23 us -> none  [the longest x10 4.94 us: extended(): before = lax.ppermute(last, axis, up)]
    unnamed x34 -> x30, local copies, waits for them, and re-layouts: 1.68 us -> 7.81 us
    mul x6 -> x0, other arithmetic: 5.98 us -> none  [the longest x1 1.89 us: field_of(): along_x = -(padded[2:, 1:-1, 1:-1] - padded[:-2, 1:-1, 1:-1]) * 0.5]
  transfers between devices with their start and end apart: 32 -> 14, of which waited for: 3 -> 3; matrix products, arithmetic and copies ran while one was open for 10% -> 0% of each run, Pallas kernels for 36% -> 59%
where the time goes in v3:
time: 205 us; the launch traced here: 204 us
  Pallas kernels  130 us (63%)
  starting transfers between devices  40.4 us (20%)
  waiting for transfers between devices  24.6 us (12%)
  local copies, waits for them, and re-layouts  7.81 us (4%)
    pallas_call x1, Pallas kernels, pair_forces(): pl.pallas_call(pair_kernel, out_shape=(jax.ShapeDtypeStruct(own.shape, jn...  102 us
    ppermute x14, starting transfers between devices, passed_along(): return lax.ppermute(shard, axis, pairs)  40.4 us
    ppermute x14, waiting for transfers between devices, passed_along(): return lax.ppermute(shard, axis, pairs)  24.6 us
    pallas_call x1, Pallas kernels, grid_step(): pl.pallas_call(functools.partial(grid_kernel, base), out_shape=(jax.Shape...  18.7 us
    unnamed x30, local copies, waits for them, and re-layouts  7.81 us
    pallas_call x1, Pallas kernels, prepare(): pl.pallas_call(prepare_kernel, out_shape=(jax.ShapeDtypeStruct((clusters,...  6.56 us
  transfers between devices with their start and end apart: 14, of which 3 were waited for; matrix products, arithmetic and copies ran while one was open for 0% of the time, Pallas kernels for 59%

profile of v3, /device:TPU:13, one launch (start us, length us, event | category | flops | bytes accessed | tf_op | source)
XLA Modules:
  0.0 204.2 jit_solution(15404679510693150694)
XLA Ops:
  0.6 0.0 copy-start.10
  0.6 0.0 copy-start.12
  0.7 0.7 copy-done.10
  1.3 0.0 copy-done.12
  1.3 0.0 copy-start
  1.3 1.0 copy-done
  2.4 0.0 copy-start.2
  2.4 1.0 copy-done.2
  3.4 0.0 copy-start.4
  3.4 1.0 copy-done.4
  4.4 0.0 copy-start.5
  4.4 1.0 copy-done.5
  5.5 0.0 copy-start.6
  5.5 0.9 copy-done.6
  6.4 0.0 copy-start.7
  6.4 0.7 copy-done.7
  7.1 0.0 copy-start.11
  7.1 0.7 copy-done.11
  7.8 0.0 copy-start.1
  7.8 0.0 copy-start.3
  7.8 6.6 %prepare.1 = (f32[256,4,128]{2,1,0:T(4,128)S(1)}, f32[256,128]{1,0:T(8,128)S(1)}, f32[16,32,256]{2,1,0:T(8,128)S(1)}, f32[16,32,256]{2,1,0:T(8,128)S(1)}, f32[12...) custom-call(s32[256]{0:T(256)S(1)} %copy-done.11, ...), custom_call_target="tpu_custom_call" | custom-call | tf_op jit(solution)/shard_map/prepare/pallas_call | solution.py:381
  14.3 3.8 %collective-permute-start = (f32[640,128]{1,0:T(8,128)S(1)}, f32[640,128]{1,0:T(8,128)S(1)}, u32[]{:S(2)}, u32[]{:S(2)}) collective-permute-start(f32[640,128]{1,0:T(8,128)S(1)} %get-tuple-element.29), channel_id=1, source_target_pairs={{0,1},{1,2},{2,3},{3,4},{4,5},{5,6},{6,7},{8,9},{9,10},{10,11},{11... | collective-permute-start | bytes 983048 | tf_op jit(solution)/shard_map/ppermute | solution.py:680
  18.1 1.9 collective-permute-start.1
  20.0 2.1 %collective-permute-done.refs_1_.refs_4_.refs_6_ = f32[640,128]{1,0:T(8,128)S(1)} collective-permute-done((f32[640,128]{1,0:T(8,128)S(1)}, f32[640,128]{1,0:T(8,128)S(1)}, u32[]{:S(2)}, u32[]{:S(2)}) %collective-permute-start) | collective-permute-done | bytes 327712 | tf_op jit(solution)/shard_map/ppermute | solution.py:680
  22.1 4.4 %collective-permute-done.1.refs_2_.refs_5_.refs_7_ = f32[640,128]{1,0:T(8,128)S(1)} collective-permute-done((f32[640,128]{1,0:T(8,128)S(1)}, f32[640,128]{1,0:T(8,128)S(1)}, u32[]{:S(2)}, u32[]{:S(2)}) %collective-permute-start.1) | collective-permute-done | bytes 327712 | tf_op jit(solution)/shard_map/ppermute | solution.py:680
  26.5 0.0 copy-done.1
  26.5 0.0 copy-done.3
  26.5 0.1 planes.1
  26.6 3.1 %collective-permute-start.6 = (f32[14,48,256]{2,1,0:T(8,128)S(1)}, f32[14,48,256]{2,1,0:T(8,128)S(1)}, u32[]{:S(2)}, u32[]{:S(2)}) collective-permute-start(f32[14,48,256]{2,1,0:T(8,128)S(1)} %get-tuple-element.39), channel_id=1, source_target_pairs={{0,8},{8,16},{16,24},{1,9},{9,17},{17,25},{2,10},{10,18},{18,26},{... | collective-permute-start | bytes 2064392 | tf_op jit(solution)/shard_map/ppermute | solution.py:680
  29.8 0.0 copy-start.14
  29.8 0.0 copy-start.13
  29.8 3.1 %collective-permute-start.7 = (f32[14,48,256]{2,1,0:T(8,128)S(1)}, f32[14,48,256]{2,1,0:T(8,128)S(1)}, u32[]{:S(2)}, u32[]{:S(2)}) collective-permute-start(f32[14,48,256]{2,1,0:T(8,128)S(1)} %get-tuple-element.40), channel_id=1, source_target_pairs={{8,0},{16,8},{24,16},{9,1},{17,9},{25,17},{10,2},{18,10},{26,18},{... | collective-permute-start | bytes 2064392 | tf_op jit(solution)/shard_map/ppermute | solution.py:680
  32.8 3.2 %collective-permute-start.2 = (f32[128,128]{1,0:T(8,128)S(1)}, f32[128,128]{1,0:T(8,128)S(1)}, u32[]{:S(2)}, u32[]{:S(2)}) collective-permute-start(f32[128,128]{1,0:T(8,128)S(1)} %get-tuple-element.31), channel_id=1, source_target_pairs={{0,2},{1,3},{2,4},{3,5},{4,6},{5,7},{8,10},{9,11},{10,12},{11,13},... | collective-permute-start | bytes 196616 | tf_op jit(solution)/shard_map/ppermute | solution.py:680
  36.1 2.1 %collective-permute-start.3 = (f32[128,128]{1,0:T(8,128)S(1)}, f32[128,128]{1,0:T(8,128)S(1)}, u32[]{:S(2)}, u32[]{:S(2)}) collective-permute-start(f32[128,128]{1,0:T(8,128)S(1)} %get-tuple-element.32), channel_id=1, source_target_pairs={{2,0},{3,1},{4,2},{5,3},{6,4},{7,5},{10,8},{11,9},{12,10},{13,11},... | collective-permute-start | bytes 196616 | tf_op jit(solution)/shard_map/ppermute | solution.py:680
  38.1 2.3 %collective-permute-start.4 = (f32[128,128]{1,0:T(8,128)S(1)}, f32[128,128]{1,0:T(8,128)S(1)}, u32[]{:S(2)}, u32[]{:S(2)}) collective-permute-start(f32[128,128]{1,0:T(8,128)S(1)} %get-tuple-element.33), channel_id=1, source_target_pairs={{0,8},{8,16},{16,24},{1,9},{9,17},{17,25},{2,10},{10,18},{18,26},{... | collective-permute-start | bytes 196616 | tf_op jit(solution)/shard_map/ppermute | solution.py:680
  40.4 0.0 collective-permute-done.2.refs_3_
  40.4 3.9 %collective-permute-start.5 = (f32[128,128]{1,0:T(8,128)S(1)}, f32[128,128]{1,0:T(8,128)S(1)}, u32[]{:S(2)}, u32[]{:S(2)}) collective-permute-start(f32[128,128]{1,0:T(8,128)S(1)} %get-tuple-element.34), channel_id=1, source_target_pairs={{8,0},{16,8},{24,16},{9,1},{17,9},{25,17},{10,2},{18,10},{26,18},{... | collective-permute-start | bytes 196616 | tf_op jit(solution)/shard_map/ppermute | solution.py:680
  44.3 0.0 copy-done.14
  44.4 0.0 copy-done.13
  44.4 0.0 copy-start.9
  44.4 0.0 collective-permute-done.3.refs_4_
  44.4 18.1 %collective-permute-done.4.refs_5_ = f32[128,128]{1,0:T(8,128)S(1)} collective-permute-done((f32[128,128]{1,0:T(8,128)S(1)}, f32[128,128]{1,0:T(8,128)S(1)}, u32[]{:S(2)}, u32[]{:S(2)}) %collective-permute-start.4) | collective-permute-done | bytes 65568 | tf_op jit(solution)/shard_map/ppermute | solution.py:680
  62.5 0.0 collective-permute-done.5.refs_6_
  62.5 0.0 copy-done.9
  62.6 102.4 %pair_forces.1 = (f32[1024,128]{1,0:T(8,128)S(1)}, f32[128,128]{1,0:T(8,128)S(1)}, f32[128,128]{1,0:T(8,128)S(1)}, f32[128,128]{1,0:T(8,128)S(1)}, f32[128,128]{...) custom-call(s32[1024]{0:T(1024)S(1)} %copy-done.9, ...), custom_call_target="tpu_custom_call" | custom-call | flops 335544320 | bytes 4194304 | tf_op jit(solution)/shard_map/pair_forces/pallas_call | solution.py:252
  164.9 2.3 %collective-permute-start.13 = (f32[128,128]{1,0:T(8,128)S(1)}, f32[128,128]{1,0:T(8,128)S(1)}, u32[]{:S(2)}, u32[]{:S(2)}) collective-permute-start(f32[128,128]{1,0:T(8,128)S(1)} %get-tuple-element.48), channel_id=1, source_target_pairs={{0,8},{8,16},{16,24},{1,9},{9,17},{17,25},{2,10},{10,18},{18,26},{... | collective-permute-start | bytes 196616 | tf_op jit(solution)/shard_map/ppermute | solution.py:680
  167.2 1.9 collective-permute-start.8
  169.1 3.6 %collective-permute-start.9 = (f32[128,128]{1,0:T(8,128)S(1)}, f32[128,128]{1,0:T(8,128)S(1)}, u32[]{:S(2)}, u32[]{:S(2)}) collective-permute-start(f32[128,128]{1,0:T(8,128)S(1)} %get-tuple-element.44), channel_id=1, source_target_pairs={{0,1},{1,2},{2,3},{3,4},{4,5},{5,6},{6,7},{8,9},{9,10},{10,11},{11... | collective-permute-start | bytes 196616 | tf_op jit(solution)/shard_map/ppermute | solution.py:680
  172.8 0.0 collective-permute-done.13
  172.8 1.9 collective-permute-start.10
  174.7 0.0 collective-permute-done.6.refs_8_
  174.7 3.4 %collective-permute-start.11 = (f32[128,128]{1,0:T(8,128)S(1)}, f32[128,128]{1,0:T(8,128)S(1)}, u32[]{:S(2)}, u32[]{:S(2)}) collective-permute-start(f32[128,128]{1,0:T(8,128)S(1)} %get-tuple-element.46), channel_id=1, source_target_pairs={{0,2},{1,3},{2,4},{3,5},{4,6},{5,7},{8,10},{9,11},{10,12},{11,13},... | collective-permute-start | bytes 196616 | tf_op jit(solution)/shard_map/ppermute | solution.py:680
  178.1 0.0 collective-permute-done.7.refs_9_
  178.1 3.9 %collective-permute-start.12 = (f32[128,128]{1,0:T(8,128)S(1)}, f32[128,128]{1,0:T(8,128)S(1)}, u32[]{:S(2)}, u32[]{:S(2)}) collective-permute-start(f32[128,128]{1,0:T(8,128)S(1)} %get-tuple-element.47), channel_id=1, source_target_pairs={{8,0},{16,8},{24,16},{9,1},{17,9},{25,17},{10,2},{18,10},{26,18},{... | collective-permute-start | bytes 196616 | tf_op jit(solution)/shard_map/ppermute | solution.py:680
  182.0 18.7 %grid_step.1 = (f32[16,32,256]{2,1,0:T(8,128)}, f32[16,32,256]{2,1,0:T(8,128)}, f32[1024,128]{1,0:T(8,128)S(1)}) custom-call(s32[256]{0:T(256)S(1)} %copy-done.10, f32[256,128]{1,0:T(8,128)S(1)} %get-tuple-element.36.refs_1_, f32[16,32,256]{2,1,0:T(8,128)S(1)} %copy-done.3, f32[16,32,256]{2,1,0:T(8,128)S(1)} %get-tuple-element.37.refs_1_.refs_3_, ...), custom_call_target="tpu_custom_call" | custom-call | flops 31948800 | bytes 8388608 | tf_op jit(solution)/shard_map/grid_step/pallas_call | solution.py:619
  200.7 0.0 collective-permute-done.8
  200.7 0.0 collective-permute-done.9
  200.7 0.0 collective-permute-done.10
  200.7 0.0 collective-permute-done.11
  200.7 0.0 collective-permute-done.12
  200.7 0.0 copy-start.8
  200.7 0.7 copy-done.8
  201.4 2.8 %gather_forces.1 = f32[3,32768]{1,0:T(4,128)} custom-call(s32[7,32]{1,0:T(8,128)S(1)} %copy-done.8, f32[256,4,128]{2,1,0:T(4,128)S(1)} %bitcast.12, f32[256,4,128]{2,1,0:T(4,128)S(1)} %bitcast.13, f32[32,4,128]{2,1,0:T(4,128)S(1)} %bitcast.15, f32[32,4,128]{2,1,0:T(4,128)S(1)} %bitcast.17, f32[32,4,128]{2,1,0:T(4,128)S(1)} %bitcast.18, ...), custom_call_target="tpu_custom_call" | custom-call | tf_op jit(solution)/shard_map/gather_forces/pallas_call | solution.py:666
  (1 shorter events, 0.0 us)
Async XLA Ops:
  0.6 0.7 copy-start.10
  0.6 0.7 copy-start.12
  1.3 1.0 copy-start
  2.4 1.0 copy-start.2
  3.4 1.0 copy-start.4
  4.4 1.0 copy-start.5
  5.5 0.9 copy-start.6
  6.4 0.7 copy-start.7
  7.1 0.7 copy-start.11
  7.8 18.7 %copy-start.1 = (f32[16,32,256]{2,1,0:T(8,128)S(1)}, f32[16,32,256]{2,1,0:T(8,128)}, u32[]{:S(2)}) copy-start(f32[16,32,256]{2,1,0:T(8,128)} %refs_5_.1) | copy-start | bytes 1572868
  7.8 18.7 %copy-start.3 = (f32[16,32,256]{2,1,0:T(8,128)S(1)}, f32[16,32,256]{2,1,0:T(8,128)}, u32[]{:S(2)}) copy-start(f32[16,32,256]{2,1,0:T(8,128)} %refs_2_.1) | copy-start | bytes 1572868
  14.3 7.8 %collective-permute-start = (f32[640,128]{1,0:T(8,128)S(1)}, f32[640,128]{1,0:T(8,128)S(1)}, u32[]{:S(2)}, u32[]{:S(2)}) collective-permute-start(f32[640,128]{1,0:T(8,128)S(1)} %get-tuple-element.29), channel_id=1, source_target_pairs={{0,1},{1,2},{2,3},{3,4},{4,5},{5,6},{6,7},{8,9},{9,10},{10,11},{11... | collective-permute-start | bytes 983048 | tf_op jit(solution)/shard_map/ppermute | solution.py:680
  18.1 8.4 %collective-permute-start.1 = (f32[640,128]{1,0:T(8,128)S(1)}, f32[640,128]{1,0:T(8,128)S(1)}, u32[]{:S(2)}, u32[]{:S(2)}) collective-permute-start(f32[640,128]{1,0:T(8,128)S(1)} %get-tuple-element.30), channel_id=1, source_target_pairs={{1,0},{2,1},{3,2},{4,3},{5,4},{6,5},{7,6},{9,8},{10,9},{11,10},{12... | collective-permute-start | bytes 983048 | tf_op jit(solution)/shard_map/ppermute | solution.py:680
  26.6 148.1 %collective-permute-start.6 = (f32[14,48,256]{2,1,0:T(8,128)S(1)}, f32[14,48,256]{2,1,0:T(8,128)S(1)}, u32[]{:S(2)}, u32[]{:S(2)}) collective-permute-start(f32[14,48,256]{2,1,0:T(8,128)S(1)} %get-tuple-element.39), channel_id=1, source_target_pairs={{0,8},{8,16},{16,24},{1,9},{9,17},{17,25},{2,10},{10,18},{18,26},{... | collective-permute-start | bytes 2064392 | tf_op jit(solution)/shard_map/ppermute | solution.py:680
  29.8 14.6 %copy-start.14 = (s32[1024]{0:T(1024)S(1)}, s32[1024]{0:T(1024)}, u32[]{:S(2)}) copy-start(s32[1024]{0:T(1024)} %param.19) | copy-start | bytes 12292
  29.8 14.6 %copy-start.13 = (s32[1024]{0:T(1024)S(1)}, s32[1024]{0:T(1024)}, u32[]{:S(2)}) copy-start(s32[1024]{0:T(1024)} %param.20) | copy-start | bytes 12292
  29.8 148.3 %collective-permute-start.7 = (f32[14,48,256]{2,1,0:T(8,128)S(1)}, f32[14,48,256]{2,1,0:T(8,128)S(1)}, u32[]{:S(2)}, u32[]{:S(2)}) collective-permute-start(f32[14,48,256]{2,1,0:T(8,128)S(1)} %get-tuple-element.40), channel_id=1, source_target_pairs={{8,0},{16,8},{24,16},{9,1},{17,9},{25,17},{10,2},{18,10},{26,18},{... | collective-permute-start | bytes 2064392 | tf_op jit(solution)/shard_map/ppermute | solution.py:680
  32.8 7.6 %collective-permute-start.2 = (f32[128,128]{1,0:T(8,128)S(1)}, f32[128,128]{1,0:T(8,128)S(1)}, u32[]{:S(2)}, u32[]{:S(2)}) collective-permute-start(f32[128,128]{1,0:T(8,128)S(1)} %get-tuple-element.31), channel_id=1, source_target_pairs={{0,2},{1,3},{2,4},{3,5},{4,6},{5,7},{8,10},{9,11},{10,12},{11,13},... | collective-permute-start | bytes 196616 | tf_op jit(solution)/shard_map/ppermute | solution.py:680
  36.1 8.3 %collective-permute-start.3 = (f32[128,128]{1,0:T(8,128)S(1)}, f32[128,128]{1,0:T(8,128)S(1)}, u32[]{:S(2)}, u32[]{:S(2)}) collective-permute-start(f32[128,128]{1,0:T(8,128)S(1)} %get-tuple-element.32), channel_id=1, source_target_pairs={{2,0},{3,1},{4,2},{5,3},{6,4},{7,5},{10,8},{11,9},{12,10},{13,11},... | collective-permute-start | bytes 196616 | tf_op jit(solution)/shard_map/ppermute | solution.py:680
  38.1 24.4 %collective-permute-start.4 = (f32[128,128]{1,0:T(8,128)S(1)}, f32[128,128]{1,0:T(8,128)S(1)}, u32[]{:S(2)}, u32[]{:S(2)}) collective-permute-start(f32[128,128]{1,0:T(8,128)S(1)} %get-tuple-element.33), channel_id=1, source_target_pairs={{0,8},{8,16},{16,24},{1,9},{9,17},{17,25},{2,10},{10,18},{18,26},{... | collective-permute-start | bytes 196616 | tf_op jit(solution)/shard_map/ppermute | solution.py:680
  40.4 22.1 %collective-permute-start.5 = (f32[128,128]{1,0:T(8,128)S(1)}, f32[128,128]{1,0:T(8,128)S(1)}, u32[]{:S(2)}, u32[]{:S(2)}) collective-permute-start(f32[128,128]{1,0:T(8,128)S(1)} %get-tuple-element.34), channel_id=1, source_target_pairs={{8,0},{16,8},{24,16},{9,1},{17,9},{25,17},{10,2},{18,10},{26,18},{... | collective-permute-start | bytes 196616 | tf_op jit(solution)/shard_map/ppermute | solution.py:680
  44.4 18.2 %copy-start.9 = (s32[1024]{0:T(1024)S(1)}, s32[1024]{0:T(1024)}, u32[]{:S(2)}) copy-start(s32[1024]{0:T(1024)} %own_rows_ref.1) | copy-start | bytes 12292
  164.9 7.9 %collective-permute-start.13 = (f32[128,128]{1,0:T(8,128)S(1)}, f32[128,128]{1,0:T(8,128)S(1)}, u32[]{:S(2)}, u32[]{:S(2)}) collective-permute-start(f32[128,128]{1,0:T(8,128)S(1)} %get-tuple-element.48), channel_id=1, source_target_pairs={{0,8},{8,16},{16,24},{1,9},{9,17},{17,25},{2,10},{10,18},{18,26},{... | collective-permute-start | bytes 196616 | tf_op jit(solution)/shard_map/ppermute | solution.py:680
  167.2 33.5 %collective-permute-start.8 = (f32[128,128]{1,0:T(8,128)S(1)}, f32[128,128]{1,0:T(8,128)S(1)}, u32[]{:S(2)}, u32[]{:S(2)}) collective-permute-start(f32[128,128]{1,0:T(8,128)S(1)} %get-tuple-element.43), channel_id=1, source_target_pairs={{1,0},{2,1},{3,2},{4,3},{5,4},{6,5},{7,6},{9,8},{10,9},{11,10},{12... | collective-permute-start | bytes 196616 | tf_op jit(solution)/shard_map/ppermute | solution.py:680
  169.1 31.6 %collective-permute-start.9 = (f32[128,128]{1,0:T(8,128)S(1)}, f32[128,128]{1,0:T(8,128)S(1)}, u32[]{:S(2)}, u32[]{:S(2)}) collective-permute-start(f32[128,128]{1,0:T(8,128)S(1)} %get-tuple-element.44), channel_id=1, source_target_pairs={{0,1},{1,2},{2,3},{3,4},{4,5},{5,6},{6,7},{8,9},{9,10},{10,11},{11... | collective-permute-start | bytes 196616 | tf_op jit(solution)/shard_map/ppermute | solution.py:680
  172.8 27.9 %collective-permute-start.10 = (f32[128,128]{1,0:T(8,128)S(1)}, f32[128,128]{1,0:T(8,128)S(1)}, u32[]{:S(2)}, u32[]{:S(2)}) collective-permute-start(f32[128,128]{1,0:T(8,128)S(1)} %get-tuple-element.45), channel_id=1, source_target_pairs={{2,0},{3,1},{4,2},{5,3},{6,4},{7,5},{10,8},{11,9},{12,10},{13,11},... | collective-permute-start | bytes 196616 | tf_op jit(solution)/shard_map/ppermute | solution.py:680
  174.7 26.0 %collective-permute-start.11 = (f32[128,128]{1,0:T(8,128)S(1)}, f32[128,128]{1,0:T(8,128)S(1)}, u32[]{:S(2)}, u32[]{:S(2)}) collective-permute-start(f32[128,128]{1,0:T(8,128)S(1)} %get-tuple-element.46), channel_id=1, source_target_pairs={{0,2},{1,3},{2,4},{3,5},{4,6},{5,7},{8,10},{9,11},{10,12},{11,13},... | collective-permute-start | bytes 196616 | tf_op jit(solution)/shard_map/ppermute | solution.py:680
  178.1 22.6 %collective-permute-start.12 = (f32[128,128]{1,0:T(8,128)S(1)}, f32[128,128]{1,0:T(8,128)S(1)}, u32[]{:S(2)}, u32[]{:S(2)}) collective-permute-start(f32[128,128]{1,0:T(8,128)S(1)} %get-tuple-element.47), channel_id=1, source_target_pairs={{8,0},{16,8},{24,16},{9,1},{17,9},{25,17},{10,2},{18,10},{26,18},{... | collective-permute-start | bytes 196616 | tf_op jit(solution)/shard_map/ppermute | solution.py:680
  200.7 0.7 copy-start.8

commit v4 on v3

--- a/solution.py
+++ b/solution.py
@@ -33,58 +33,36 @@
     return (first, second, third)
 
 
-def moment_rows(comps, charge, rows_ref, base):
+def moment_rows(comps, charge):
+    rows = [None] * 12
     for part, charged in enumerate((*comps, None)):
-        pieces = split3(charge if charged is None else charge * charged)
-        for level, piece in enumerate(pieces):
-            rows_ref[pl.ds(base + 4 * level + part, 8, stride=16), :] = piece
-
-
-def pair_kernel(
-    own_rows_ref,
-    other_rows_ref,
-    own_ref,
-    *refs,
-):
+        for level, piece in enumerate(split3(charge if charged is None else charge * charged)):
+            rows[4 * level + part] = piece
+    return rows
+
+
+def pair_kernel(own_rows_ref, other_rows_ref, own_ref, *refs):
     sources = (len(refs) - 10) // 2
     other_refs = refs[:sources]
     own_out_ref = refs[sources]
     other_out_refs = refs[sources + 1 : 2 * sources + 1]
-    pair_body(
-        own_rows_ref,
-        other_rows_ref,
-        own_ref,
-        other_refs,
-        own_out_ref,
-        other_out_refs,
-        *refs[2 * sources + 1 :],
-    )
-
-
-def pair_body(
-    own_rows_ref,
-    other_rows_ref,
-    own_ref,
-    other_refs,
-    own_out_ref,
-    other_out_refs,
-    near_ref,
-    far_ref,
-    own_moment_ref,
-    other_moment_ref,
-    own_sum_ref,
-    other_sum_ref,
-    stage_ref,
-    dist_ref,
-    weight_ref,
-):
+    (
+        near_ref,
+        far_ref,
+        own_moment_ref,
+        other_moment_ref,
+        own_sum_ref,
+        other_sum_ref,
+        stage_ref,
+        dist_ref,
+        weight_ref,
+    ) = refs[2 * sources + 1 :]
     clusters = own_ref.shape[0] // 4
     slots = other_out_refs[0].shape[0] // 4
-    others = slots * len(other_refs)
     groups = own_rows_ref.shape[0] // UNROLL
+    units = UNROLL // 2
     ones = jnp.ones((8, 128), jnp.float32)
     zeros = jnp.zeros((8, 128), jnp.float32)
-    stage_ref[...] = jnp.zeros_like(stage_ref)
 
     def components(data_ref, start):
         return [data_ref[pl.ds(4 * start + part, 8, stride=4), :] for part in range(4)]
@@ -96,10 +74,10 @@
     def near_rows(step, _):
         start = pl.multiple_of(step * 8, 8)
         *comps, charge = components(own_ref, start)
-        moment_rows(comps, charge, stage_ref, 0)
-        own_moment_ref[pl.ds(pl.multiple_of(start * 16, 128), 128), :] = stage_ref[0:128, :].astype(
-            jnp.bfloat16
-        )
+        put(moment_rows(comps, charge) + [zeros] * 4, 256, 16)
+        own_moment_ref[pl.ds(pl.multiple_of(start * 16, 128), 128), :] = stage_ref[
+            256:384, :
+        ].astype(jnp.bfloat16)
         rows = []
         square = zeros
         for comp in comps:
@@ -110,22 +88,26 @@
         rows += [zeros] * (32 - len(rows))
         put(rows, 0, 32)
         for half in range(2):
-            block = stage_ref[128 * half : 128 * half + 128, :]
-            near_ref[pl.ds(pl.multiple_of(step * 256 + half * 128, 128), 128), :] = block.T.astype(
-                jnp.bfloat16
-            )
-        for index in range(8):
-            own_sum_ref[pl.ds(pl.multiple_of((start + index) * 128, 128), 128), :] = jnp.zeros(
-                (128, 128), jnp.float32
-            )
+            columns = stage_ref[128 * half : 128 * half + 128, :].T
+            for index in range(4):
+                at = pl.ds(pl.multiple_of((start + 4 * half + index) * 128, 128), 128)
+                rolled = columns if index == 0 else pltpu.roll(columns, 128 - 32 * index, 1)
+                near_ref[at, :] = rolled.astype(jnp.bfloat16)
+                own_sum_ref[at, :] = jnp.zeros((128, 128), jnp.float32)
         return 0
 
     def far_rows(source, step, _):
         local = pl.multiple_of(step * 8, 8)
         start = source * slots + local
         *comps, charge = components(other_refs[source], local)
-        moment_rows(comps, charge, stage_ref, 0)
-        columns = stage_ref[0:128, :].T
+        moments = moment_rows(comps, charge) + [zeros] * 4
+        put(moments + moments, 0, 32)
+        for half in range(2):
+            columns = stage_ref[128 * half : 128 * half + 128, :].T
+            for index in range(4):
+                at = pl.ds(pl.multiple_of((start + 4 * half + index) * 128, 128), 128)
+                rolled = columns if index == 0 else pltpu.roll(columns, 128 - 32 * index, 1)
+                other_moment_ref[at, :] = rolled.astype(jnp.bfloat16)
         rows = []
         square = zeros
         for comp in comps:
@@ -135,80 +117,93 @@
         rows += [ones, ones, ones, *split3(square + softening)]
         rows += [zeros] * (32 - len(rows))
         put(rows, 0, 32)
-        for index in range(8):
-            target = pl.multiple_of((start + index) * 128, 128)
-            far_ref[pl.ds(target, 96), :] = jnp.zeros((96, 128), jnp.bfloat16)
-            far_ref[pl.ds(target + 96, 32), :] = stage_ref[32 * index : 32 * index + 32, :].astype(
-                jnp.bfloat16
-            )
-            rolled = columns if index == 0 else pltpu.roll(columns, 128 - 16 * index, 1)
-            other_moment_ref[pl.ds(target, 128), :] = rolled.astype(jnp.bfloat16)
+        far_ref[pl.ds(pl.multiple_of(start * 32, 256), 256), :] = stage_ref[0:256, :].astype(
+            jnp.bfloat16
+        )
         return 0
 
     lax.fori_loop(0, clusters // 8, near_rows, 0)
-    for source in range(len(other_refs)):
+    for source in range(sources):
         lax.fori_loop(0, slots // 8, functools.partial(far_rows, source), 0)
-    far_ref[pl.ds(others * 128, 128), :] = jnp.zeros((128, 128), jnp.bfloat16)
     other_sum_ref[...] = jnp.zeros_like(other_sum_ref)
     dist_ref[...] = jnp.full(dist_ref.shape, 1e38, jnp.float32)
     weight_ref[...] = jnp.zeros_like(weight_ref)
 
+    lane = lax.broadcasted_iota(jnp.int32, (128, 128), 1)
+    lane_row = lax.broadcasted_iota(jnp.int32, (1, 128), 1)
+    left_mask = jnp.where(lane_row < 16, 1.0, 0.0).astype(jnp.bfloat16)
+    right_mask = jnp.where((lane_row >= 16) & (lane_row < 32), 1.0, 0.0).astype(jnp.bfloat16)
+
     def distances(pair, turn):
         own = own_rows_ref[pair]
         other = other_rows_ref[pair]
-        group = lax.shift_right_logical(own, 2)
-        member = lax.bitwise_and(own, 3)
-        near = near_ref[pl.ds(pl.multiple_of(group * 128, 128), 128), :]
-        far = far_ref[pl.ds(pl.multiple_of(other * 128 + 96 - member * 32, 32), 128), :]
+        near = near_ref[pl.ds(pl.multiple_of(own * 128, 128), 128), 0:32]
+        far = far_ref[pl.ds(pl.multiple_of(other * 32, 32), 32), :]
         dist_ref[turn] = jnp.dot(near, far, preferred_element_type=jnp.float32)
 
     def weights(turn):
         root = lax.rsqrt(dist_ref[turn])
         weight = root * root * root
         high = weight.astype(jnp.bfloat16)
-        weight_ref[turn, :, :128] = high
-        weight_ref[turn, :, 128:] = (weight - high.astype(jnp.float32)).astype(jnp.bfloat16)
-
-    def products(pair, turn):
-        own = own_rows_ref[pair]
-        other = other_rows_ref[pair]
-        both = weight_ref[turn]
-        moment = other_moment_ref[pl.ds(pl.multiple_of(other * 128, 128), 128), :]
-        to_own = jnp.dot(
-            both,
-            jnp.concatenate([moment, moment], axis=0),
-            preferred_element_type=jnp.float32,
-        )
-        to_other = jnp.dot(
-            own_moment_ref[pl.ds(pl.multiple_of(own * 16, 16), 16), :],
-            both,
-            preferred_element_type=jnp.float32,
-        )
-        return (own, other, to_own, to_other[:, :128] + to_other[:, 128:])
+        lanes = slice(128 * (turn % 2), 128 * (turn % 2) + 128)
+        weight_ref[2 * (turn // 2), :, lanes] = high
+        weight_ref[2 * (turn // 2) + 1, :, lanes] = (weight - high.astype(jnp.float32)).astype(
+            jnp.bfloat16
+        )
+
+    def moment_of(moment_ref, row, size):
+        return moment_ref[pl.ds(pl.multiple_of(row * size, size), size), :]
+
+    def products(pair, unit):
+        owns = [own_rows_ref[pair + turn] for turn in range(2)]
+        others = [other_rows_ref[pair + turn] for turn in range(2)]
+        high = weight_ref[2 * unit]
+        low = weight_ref[2 * unit + 1]
+        columns = jnp.concatenate(
+            [
+                moment_of(other_moment_ref, others[0], 128) * left_mask,
+                moment_of(other_moment_ref, others[1], 128) * right_mask,
+            ],
+            axis=0,
+        )
+        rows = jnp.concatenate(
+            [moment_of(own_moment_ref, owns[0], 16), moment_of(own_moment_ref, owns[1], 16)], axis=0
+        )
+        to_own = jnp.dot(high, columns, preferred_element_type=jnp.float32) + jnp.dot(
+            low, columns, preferred_element_type=jnp.float32
+        )
+        to_other = jnp.dot(rows, high, preferred_element_type=jnp.float32) + jnp.dot(
+            rows, low, preferred_element_type=jnp.float32
+        )
+        return (owns, others, to_own, (to_other[:16, :128], to_other[16:, 128:]))
 
     def visit(step, _):
         last = jnp.maximum(step - 2, 0) * UNROLL
         first = jnp.minimum(step, groups - 1) * UNROLL
-        results = [products(last + turn, turn) for turn in range(UNROLL)]
+        results = [products(last + 2 * unit, unit) for unit in range(units)]
         for turn in range(UNROLL):
             weights(turn)
         for turn in range(UNROLL):
             distances(first + turn, turn)
-        for own, other, to_own, to_other in results:
-            own_sum_ref[pl.ds(pl.multiple_of(own * 128, 128), 128), :] += to_own
-            other_sum_ref[pl.ds(pl.multiple_of(other * 16, 16), 16), :] += to_other
+        for owns, others, to_own, to_other in results:
+            for turn in range(2):
+                kept = jnp.where(lane < 16 if turn == 0 else lane >= 16, to_own, 0.0)
+                own_sum_ref[pl.ds(pl.multiple_of(owns[turn] * 128, 128), 128), :] += kept
+                other_sum_ref[pl.ds(pl.multiple_of(others[turn] * 16, 16), 16), :] += to_other[turn]
         return 0
 
     lax.fori_loop(0, groups + 2, visit, 0)
 
-    def finish(data_ref, out_ref, start, rows_ref, base):
+    def finish(data_ref, out_ref, start, rows_ref, bases, stride):
         *comps, charge = components(data_ref, start)
 
         def total(part):
             terms = [
-                rows_ref[pl.ds(base + 4 * level + part, 8, stride=16), :] for level in range(3)
+                rows_ref[pl.ds(base + 4 * level + part, 8, stride=stride), :]
+                for level in range(3)
+                for base in bases
             ]
-            return terms[0] + (terms[1] + terms[2])
+            return functools.reduce(lambda left, right: right + left, terms[::-1])
 
         weight = total(3)
         scale = coulomb_scale * charge
@@ -218,13 +213,18 @@
 
     def finish_own(step, _):
         start = pl.multiple_of(step * 8, 8)
-        lane = lax.broadcasted_iota(jnp.int32, (128, 128), 1)
-        columns = own_sum_ref[pl.ds(pl.multiple_of(start * 128, 128), 128), :]
-        for index in range(1, 8):
-            block = own_sum_ref[pl.ds(pl.multiple_of((start + index) * 128, 128), 128), :]
-            columns = jnp.where(lane < 16 * index, columns, pltpu.roll(block, 16 * index, 1))
-        stage_ref[0:128, :] = columns.T
-        finish(own_ref, own_out_ref, start, stage_ref, 0)
+        for half in range(2):
+            columns = None
+            for index in range(4):
+                at = pl.ds(pl.multiple_of((start + 4 * half + index) * 128, 128), 128)
+                block = own_sum_ref[at, :]
+                if index:
+                    rolled = pltpu.roll(block, 32 * index, 1)
+                    columns = jnp.where(lane < 32 * index, columns, rolled)
+                else:
+                    columns = block
+            stage_ref[128 * half : 128 * half + 128, :] = columns.T
+        finish(own_ref, own_out_ref, start, stage_ref, (0, 16), 32)
         return 0
 
     def finish_other(source, step, _):
@@ -234,12 +234,13 @@
             other_out_refs[source],
             start,
             other_sum_ref,
-            (source * slots + start) * 16,
+            ((source * slots + start) * 16,),
+            16,
         )
         return 0
 
     lax.fori_loop(0, clusters // 8, finish_own, 0)
-    for source in range(len(other_refs)):
+    for source in range(sources):
         lax.fori_loop(0, slots // 8, functools.partial(finish_other, source), 0)
 
 
@@ -258,17 +259,17 @@
         in_specs=[smem, smem, vmem] + [vmem] * len(arrived),
         out_specs=(vmem,) * (len(arrived) + 1),
         scratch_shapes=[
-            pltpu.VMEM((clusters * 32, 128), jnp.bfloat16),
-            pltpu.VMEM(((others + 1) * 128, 128), jnp.bfloat16),
+            pltpu.VMEM((clusters * 128, 128), jnp.bfloat16),
+            pltpu.VMEM((others * 32, 128), jnp.bfloat16),
             pltpu.VMEM((clusters * 16, 128), jnp.bfloat16),
             pltpu.VMEM((others * 128, 128), jnp.bfloat16),
             pltpu.VMEM((clusters * 128, 128), jnp.float32),
             pltpu.VMEM((others * 16, 128), jnp.float32),
-            pltpu.VMEM((256, 128), jnp.float32),
+            pltpu.VMEM((384, 128), jnp.float32),
             pltpu.VMEM((UNROLL, 128, 128), jnp.float32),
             pltpu.VMEM((UNROLL, 128, 256), jnp.bfloat16),
         ],
-        compiler_params=pltpu.CompilerParams(vmem_limit_bytes=48 * 1024 * 1024),
+        compiler_params=pltpu.CompilerParams(vmem_limit_bytes=46 * 1024 * 1024),
         cost_estimate=pl.CostEstimate(
             flops=pairs * 128 * 128 * 20, bytes_accessed=4 * 1024 * 1024, transcendentals=0
         ),
@@ -281,18 +282,36 @@
     cell_ref,
     send_index_ref,
     send_count_ref,
-    position_ref,
-    charge_ref,
-    ion_ref,
-    start_ref,
-    screen_ref,
+    position_hbm,
+    charge_hbm,
+    ion_hbm,
+    start_hbm,
+    screen_hbm,
     own_ref,
     masked_ref,
     inverse_ref,
     source_ref,
     *refs,
 ):
-    out_refs, (sum_ref, deposit_ref) = (refs[:-2], refs[-2:])
+    out_refs, scratch = (refs[:-8], refs[-8:])
+    sum_ref, deposit_ref, position_ref, charge_ref, ion_ref, start_ref, screen_ref, sems = scratch
+    copies = [
+        pltpu.make_async_copy(source, target, sems.at[index])
+        for index, (source, target) in enumerate(
+            (
+                (position_hbm, position_ref),
+                (charge_hbm, charge_ref),
+                (ion_hbm, ion_ref),
+                (start_hbm, start_ref),
+                (screen_hbm, screen_ref),
+            )
+        )
+    ]
+    for copy in copies:
+        copy.start()
+    deposit_ref[...] = jnp.zeros_like(deposit_ref)
+    copies[0].wait()
+    copies[1].wait()
     clusters = charge_ref.shape[0]
     cells_x, cells_y, _ = ion_ref.shape
     slots = send_index_ref.shape[1]
@@ -327,8 +346,6 @@
 
     lax.fori_loop(0, slots // 2, fill_messages, 0)
 
-    deposit_ref[...] = jnp.zeros_like(deposit_ref)
-
     def deposit(cluster, _):
         cell = cell_ref[cluster]
         index_x = lax.shift_right_logical(cell, CELL_BITS) // cells_y
@@ -342,6 +359,8 @@
         return 0
 
     lax.fori_loop(0, clusters, deposit, 0, unroll=4)
+    for copy in copies[2:]:
+        copy.wait()
     inverse_ref[...] = 1.0 / (6.0 + screen_ref[...])
     for index in range(cells_x):
         for half in range(2):
@@ -387,13 +406,18 @@
             jax.ShapeDtypeStruct(ions.shape, jnp.float32),
             *[jax.ShapeDtypeStruct((count, 128), jnp.float32) for count in rows],
         ),
-        in_specs=[smem] * 4 + [vmem] * 5,
+        in_specs=[smem] * 4 + [pl.BlockSpec(memory_space=pltpu.HBM)] * 5,
         out_specs=(vmem,) * (4 + directions),
         scratch_shapes=[
             pltpu.VMEM((clusters, 128), jnp.float32),
             pltpu.VMEM((ions.size // 128, 128), jnp.float32),
+            *[
+                pltpu.VMEM(operand.shape, jnp.float32)
+                for operand in (positions, charges, ions, start, screen)
+            ],
+            pltpu.SemaphoreType.DMA((5,)),
         ],
-        compiler_params=pltpu.CompilerParams(vmem_limit_bytes=32 * 1024 * 1024),
+        compiler_params=pltpu.CompilerParams(vmem_limit_bytes=60 * 1024 * 1024),
         name="prepare",
     )(fill, cell, send_index, send_count, positions, charges, ions, start, screen)
 
@@ -717,6 +741,7 @@
         for message, (axis, by) in zip(messages, ROUTES, strict=True)
     ]
     fields = (potential_prev, inverse, source, ion_density)
+    arrived = lax.optimization_barrier(arrived)
     before, after = arrived[1:3]
     down, up = planes(fields, before, after, base)
     lower = passed_along(up, "grp", 1)

time: 205 us -> 187 us (0.912)
  waiting for transfers between devices: 24.6 us -> 2.16 us
  Pallas kernels: 130 us -> 136 us
  local copies, waits for them, and re-layouts: 7.81 us -> 3.45 us
  starting transfers between devices: 40.4 us -> 43.3 us
    ppermute x14, waiting for transfers between devices: 24.6 us -> 2.16 us  [passed_along(): return lax.ppermute(shard, axis, pairs)]
    unnamed x30 -> x28, local copies, waits for them, and re-layouts: 7.81 us -> 3.45 us
    pallas_call x1, Pallas kernels: 102 us -> 106 us  [pair_forces(): pl.pallas_call(pair_kernel, out_shape=(jax.ShapeDtypeStruct(own.shape, jn...]
    ppermute x14, starting transfers between devices: 40.4 us -> 43.3 us  [passed_along(): return lax.ppermute(shard, axis, pairs)]
    pallas_call x1, Pallas kernels: 6.56 us -> 9.1 us  [prepare(): pl.pallas_call(prepare_kernel, out_shape=(jax.ShapeDtypeStruct((clusters,...]
  transfers between devices with their start and end apart: 14 -> 14, of which waited for: 3 -> 1; matrix products, arithmetic and copies ran while one was open for 0% -> 0% of each run, Pallas kernels for 59% -> 67%
where the time goes in v4:
time: 187 us; the launch traced here: 186 us
  Pallas kernels  136 us (73%)
  starting transfers between devices  43.3 us (23%)
  local copies, waits for them, and re-layouts  3.45 us (2%)
  waiting for transfers between devices  2.16 us (1%)
    pallas_call x1, Pallas kernels, pair_forces(): pl.pallas_call(pair_kernel, out_shape=(jax.ShapeDtypeStruct(own.shape, jn...  106 us
    ppermute x14, starting transfers between devices, passed_along(): return lax.ppermute(shard, axis, pairs)  43.3 us
    pallas_call x1, Pallas kernels, grid_step(): pl.pallas_call(functools.partial(grid_kernel, base), out_shape=(jax.Shape...  18.7 us
    pallas_call x1, Pallas kernels, prepare(): pl.pallas_call(prepare_kernel, out_shape=(jax.ShapeDtypeStruct((clusters,...  9.1 us
  transfers between devices with their start and end apart: 14, of which 1 were waited for; matrix products, arithmetic and copies ran while one was open for 0% of the time, Pallas kernels for 67%

profile of v4, /device:TPU:13, one launch (start us, length us, event | category | flops | bytes accessed | tf_op | source)
XLA Modules:
  0.0 186.2 jit_solution(12827960569720421225)
XLA Ops:
  0.6 0.0 copy-start
  0.6 0.0 copy-start.1
  0.7 9.1 %prepare.1 = (f32[256,4,128]{2,1,0:T(4,128)}, f32[256,128]{1,0:T(8,128)}, f32[16,32,256]{2,1,0:T(8,128)}, f32[16,32,256]{2,1,0:T(8,128)}, f32[128,128]{1,0:T(8,1...) custom-call(s32[256]{0:T(256)} %fill_ref.1, ...), custom_call_target="tpu_custom_call" | custom-call | tf_op jit(solution)/shard_map/prepare/pallas_call | solution.py:400
  9.8 3.8 %collective-permute-start = (f32[640,128]{1,0:T(8,128)}, f32[640,128]{1,0:T(8,128)S(1)}, u32[]{:S(2)}, u32[]{:S(2)}) collective-permute-start(f32[640,128]{1,0:T(8,128)} %get-tuple-element.36), channel_id=1, source_target_pairs={{0,1},{1,2},{2,3},{3,4},{4,5},{5,6},{6,7},{8,9},{9,10},{10,11},{11... | collective-permute-start | bytes 983048 | tf_op jit(solution)/shard_map/ppermute | solution.py:704
  13.5 1.9 %collective-permute-start.1 = (f32[640,128]{1,0:T(8,128)}, f32[640,128]{1,0:T(8,128)S(1)}, u32[]{:S(2)}, u32[]{:S(2)}) collective-permute-start(f32[640,128]{1,0:T(8,128)} %get-tuple-element.37), channel_id=1, source_target_pairs={{1,0},{2,1},{3,2},{4,3},{5,4},{6,5},{7,6},{9,8},{10,9},{11,10},{12... | collective-permute-start | bytes 983048 | tf_op jit(solution)/shard_map/ppermute | solution.py:704
  15.5 3.2 %collective-permute-start.2 = (f32[128,128]{1,0:T(8,128)}, f32[128,128]{1,0:T(8,128)S(1)}, u32[]{:S(2)}, u32[]{:S(2)}) collective-permute-start(f32[128,128]{1,0:T(8,128)} %get-tuple-element.38), channel_id=1, source_target_pairs={{0,2},{1,3},{2,4},{3,5},{4,6},{5,7},{8,10},{9,11},{10,12},{11,13},... | collective-permute-start | bytes 196616 | tf_op jit(solution)/shard_map/ppermute | solution.py:704
  18.7 2.1 %collective-permute-start.3 = (f32[128,128]{1,0:T(8,128)}, f32[128,128]{1,0:T(8,128)S(1)}, u32[]{:S(2)}, u32[]{:S(2)}) collective-permute-start(f32[128,128]{1,0:T(8,128)} %get-tuple-element.39), channel_id=1, source_target_pairs={{2,0},{3,1},{4,2},{5,3},{6,4},{7,5},{10,8},{11,9},{12,10},{13,11},... | collective-permute-start | bytes 196616 | tf_op jit(solution)/shard_map/ppermute | solution.py:704
  20.8 3.1 %collective-permute-start.4 = (f32[128,128]{1,0:T(8,128)}, f32[128,128]{1,0:T(8,128)S(1)}, u32[]{:S(2)}, u32[]{:S(2)}) collective-permute-start(f32[128,128]{1,0:T(8,128)} %get-tuple-element.40), channel_id=1, source_target_pairs={{0,8},{8,16},{16,24},{1,9},{9,17},{17,25},{2,10},{10,18},{18,26},{... | collective-permute-start | bytes 196616 | tf_op jit(solution)/shard_map/ppermute | solution.py:704
  23.9 0.0 collective-permute-done.2.refs_3_
  23.9 3.1 %collective-permute-start.5 = (f32[128,128]{1,0:T(8,128)}, f32[128,128]{1,0:T(8,128)S(1)}, u32[]{:S(2)}, u32[]{:S(2)}) collective-permute-start(f32[128,128]{1,0:T(8,128)} %get-tuple-element.41), channel_id=1, source_target_pairs={{8,0},{16,8},{24,16},{9,1},{17,9},{25,17},{10,2},{18,10},{26,18},{... | collective-permute-start | bytes 196616 | tf_op jit(solution)/shard_map/ppermute | solution.py:704
  27.0 0.0 collective-permute-done.3.refs_4_
  27.0 0.0 collective-permute-done.4.refs_5_
  27.0 2.1 %collective-permute-done.5.refs_6_ = f32[128,128]{1,0:T(8,128)S(1)} collective-permute-done((f32[128,128]{1,0:T(8,128)}, f32[128,128]{1,0:T(8,128)S(1)}, u32[]{:S(2)}, u32[]{:S(2)}) %collective-permute-start.5) | collective-permute-done | bytes 65568 | tf_op jit(solution)/shard_map/ppermute | solution.py:704
  29.1 0.0 collective-permute-done.refs_1_.refs_4_.refs_6_
  29.1 0.0 collective-permute-done.1.refs_2_.refs_5_.refs_7_
  29.1 0.0 copy-done
  29.1 0.0 copy-done.1
  29.1 0.0 copy-start.2
  29.2 1.0 copy-done.2
  30.2 0.0 copy-start.4
  30.2 1.0 copy-done.4
  31.2 0.0 copy-start.12
  31.2 0.0 copy-start.13
  31.2 0.0 copy-start.6
  31.2 0.0 copy-start.8
  31.2 0.1 planes.1
  31.4 2.1 %collective-permute-start.6 = (f32[14,48,256]{2,1,0:T(8,128)S(1)}, f32[14,48,256]{2,1,0:T(8,128)S(1)}, u32[]{:S(2)}, u32[]{:S(2)}) collective-permute-start(f32[14,48,256]{2,1,0:T(8,128)S(1)} %get-tuple-element.53), channel_id=1, source_target_pairs={{0,8},{8,16},{16,24},{1,9},{9,17},{17,25},{2,10},{10,18},{18,26},{... | collective-permute-start | bytes 2064392 | tf_op jit(solution)/shard_map/ppermute | solution.py:704
  33.4 4.3 %collective-permute-start.7 = (f32[14,48,256]{2,1,0:T(8,128)S(1)}, f32[14,48,256]{2,1,0:T(8,128)S(1)}, u32[]{:S(2)}, u32[]{:S(2)}) collective-permute-start(f32[14,48,256]{2,1,0:T(8,128)S(1)} %get-tuple-element.54), channel_id=1, source_target_pairs={{8,0},{16,8},{24,16},{9,1},{17,9},{25,17},{10,2},{18,10},{26,18},{... | collective-permute-start | bytes 2064392 | tf_op jit(solution)/shard_map/ppermute | solution.py:704
  37.7 0.0 copy-done.12
  37.7 0.0 copy-done.13
  37.7 0.0 copy-start.10
  37.8 0.0 copy-done.6
  37.8 0.0 copy-done.8
  37.8 0.6 copy-done.10
  38.4 0.0 copy-start.3
  38.4 0.0 copy-start.5
  38.4 0.0 copy-start.7
  38.4 105.6 %pair_forces.1 = (f32[1024,128]{1,0:T(8,128)S(1)}, f32[128,128]{1,0:T(8,128)S(1)}, f32[128,128]{1,0:T(8,128)S(1)}, f32[128,128]{1,0:T(8,128)S(1)}, f32[128,128]{...) custom-call(s32[1024]{0:T(1024)S(1)} %copy-done.10, ...), custom_call_target="tpu_custom_call" | custom-call | flops 335544320 | bytes 4194304 | tf_op jit(solution)/shard_map/pair_forces/pallas_call | solution.py:253
  144.0 1.9 %collective-permute-start.13 = (f32[128,128]{1,0:T(8,128)S(1)}, f32[128,128]{1,0:T(8,128)S(1)}, u32[]{:S(2)}, u32[]{:S(2)}) collective-permute-start(f32[128,128]{1,0:T(8,128)S(1)} %get-tuple-element.62), channel_id=1, source_target_pairs={{0,8},{8,16},{16,24},{1,9},{9,17},{17,25},{2,10},{10,18},{18,26},{... | collective-permute-start | bytes 196616 | tf_op jit(solution)/shard_map/ppermute | solution.py:704
  146.0 5.0 %collective-permute-start.8 = (f32[128,128]{1,0:T(8,128)S(1)}, f32[128,128]{1,0:T(8,128)S(1)}, u32[]{:S(2)}, u32[]{:S(2)}) collective-permute-start(f32[128,128]{1,0:T(8,128)S(1)} %get-tuple-element.57), channel_id=1, source_target_pairs={{1,0},{2,1},{3,2},{4,3},{5,4},{6,5},{7,6},{9,8},{10,9},{11,10},{12... | collective-permute-start | bytes 196616 | tf_op jit(solution)/shard_map/ppermute | solution.py:704
  151.0 3.1 %collective-permute-start.9 = (f32[128,128]{1,0:T(8,128)S(1)}, f32[128,128]{1,0:T(8,128)S(1)}, u32[]{:S(2)}, u32[]{:S(2)}) collective-permute-start(f32[128,128]{1,0:T(8,128)S(1)} %get-tuple-element.58), channel_id=1, source_target_pairs={{0,1},{1,2},{2,3},{3,4},{4,5},{5,6},{6,7},{8,9},{9,10},{10,11},{11... | collective-permute-start | bytes 196616 | tf_op jit(solution)/shard_map/ppermute | solution.py:704
  154.1 0.0 collective-permute-done.13
  154.1 2.1 %collective-permute-start.10 = (f32[128,128]{1,0:T(8,128)S(1)}, f32[128,128]{1,0:T(8,128)S(1)}, u32[]{:S(2)}, u32[]{:S(2)}) collective-permute-start(f32[128,128]{1,0:T(8,128)S(1)} %get-tuple-element.59), channel_id=1, source_target_pairs={{2,0},{3,1},{4,2},{5,3},{6,4},{7,5},{10,8},{11,9},{12,10},{13,11},... | collective-permute-start | bytes 196616 | tf_op jit(solution)/shard_map/ppermute | solution.py:704
  156.2 0.0 collective-permute-done.6.refs_8_
  156.2 3.2 %collective-permute-start.11 = (f32[128,128]{1,0:T(8,128)S(1)}, f32[128,128]{1,0:T(8,128)S(1)}, u32[]{:S(2)}, u32[]{:S(2)}) collective-permute-start(f32[128,128]{1,0:T(8,128)S(1)} %get-tuple-element.60), channel_id=1, source_target_pairs={{0,2},{1,3},{2,4},{3,5},{4,6},{5,7},{8,10},{9,11},{10,12},{11,13},... | collective-permute-start | bytes 196616 | tf_op jit(solution)/shard_map/ppermute | solution.py:704
  159.4 0.0 collective-permute-done.7.refs_9_
  159.4 0.0 copy-start.11
  159.4 4.5 %collective-permute-start.12 = (f32[128,128]{1,0:T(8,128)S(1)}, f32[128,128]{1,0:T(8,128)S(1)}, u32[]{:S(2)}, u32[]{:S(2)}) collective-permute-start(f32[128,128]{1,0:T(8,128)S(1)} %get-tuple-element.61), channel_id=1, source_target_pairs={{8,0},{16,8},{24,16},{9,1},{17,9},{25,17},{10,2},{18,10},{26,18},{... | collective-permute-start | bytes 196616 | tf_op jit(solution)/shard_map/ppermute | solution.py:704
  164.0 0.0 copy-done.3
  164.0 0.0 copy-done.5
  164.0 0.0 copy-done.7
  164.0 0.0 copy-done.11
  164.0 18.7 %grid_step.1 = (f32[16,32,256]{2,1,0:T(8,128)}, f32[16,32,256]{2,1,0:T(8,128)}, f32[1024,128]{1,0:T(8,128)S(1)}) custom-call(s32[256]{0:T(256)S(1)} %copy-done.11, f32[256,128]{1,0:T(8,128)S(1)} %copy-done.7, f32[16,32,256]{2,1,0:T(8,128)S(1)} %copy-done.1, f32[16,32,256]{2,1,0:T(8,128)S(1)} %copy-done.3, f32[16,32,256]{2,1,0:T(8,128)S(1)} %copy-done.5, ...), custom_call_target="tpu_custom_call" | custom-call | flops 31948800 | bytes 8388608 | tf_op jit(solution)/shard_map/grid_step/pallas_call | solution.py:643
  182.7 0.0 collective-permute-done.8
  182.7 0.0 collective-permute-done.9
  182.7 0.0 collective-permute-done.10
  182.7 0.0 collective-permute-done.11
  182.7 0.0 collective-permute-done.12
  182.7 0.0 copy-start.9
  182.7 0.7 copy-done.9
  183.4 2.8 %gather_forces.1 = f32[3,32768]{1,0:T(4,128)} custom-call(s32[7,32]{1,0:T(8,128)S(1)} %copy-done.9, f32[256,4,128]{2,1,0:T(4,128)S(1)} %bitcast.12, f32[256,4,128]{2,1,0:T(4,128)S(1)} %bitcast.13, f32[32,4,128]{2,1,0:T(4,128)S(1)} %bitcast.14, f32[32,4,128]{2,1,0:T(4,128)S(1)} %bitcast.16, f32[32,4,128]{2,1,0:T(4,128)S(1)} %bitcast.17, ...), custom_call_target="tpu_custom_call" | custom-call | tf_op jit(solution)/shard_map/gather_forces/pallas_call | solution.py:690
  (1 shorter events, 0.0 us)
Async XLA Ops:
  0.6 28.5 %copy-start = (f32[16,32,256]{2,1,0:T(8,128)S(1)}, f32[16,32,256]{2,1,0:T(8,128)}, u32[]{:S(2)}) copy-start(f32[16,32,256]{2,1,0:T(8,128)} %refs_5_.1) | copy-start | bytes 1572868
  0.6 28.5 %copy-start.1 = (f32[16,32,256]{2,1,0:T(8,128)S(1)}, f32[16,32,256]{2,1,0:T(8,128)}, u32[]{:S(2)}) copy-start(f32[16,32,256]{2,1,0:T(8,128)} %refs_2_.1) | copy-start | bytes 1572868
  9.8 19.4 %collective-permute-start = (f32[640,128]{1,0:T(8,128)}, f32[640,128]{1,0:T(8,128)S(1)}, u32[]{:S(2)}, u32[]{:S(2)}) collective-permute-start(f32[640,128]{1,0:T(8,128)} %get-tuple-element.36), channel_id=1, source_target_pairs={{0,1},{1,2},{2,3},{3,4},{4,5},{5,6},{6,7},{8,9},{9,10},{10,11},{11... | collective-permute-start | bytes 983048 | tf_op jit(solution)/shard_map/ppermute | solution.py:704
  13.5 15.6 %collective-permute-start.1 = (f32[640,128]{1,0:T(8,128)}, f32[640,128]{1,0:T(8,128)S(1)}, u32[]{:S(2)}, u32[]{:S(2)}) collective-permute-start(f32[640,128]{1,0:T(8,128)} %get-tuple-element.37), channel_id=1, source_target_pairs={{1,0},{2,1},{3,2},{4,3},{5,4},{6,5},{7,6},{9,8},{10,9},{11,10},{12... | collective-permute-start | bytes 983048 | tf_op jit(solution)/shard_map/ppermute | solution.py:704
  15.5 8.4 %collective-permute-start.2 = (f32[128,128]{1,0:T(8,128)}, f32[128,128]{1,0:T(8,128)S(1)}, u32[]{:S(2)}, u32[]{:S(2)}) collective-permute-start(f32[128,128]{1,0:T(8,128)} %get-tuple-element.38), channel_id=1, source_target_pairs={{0,2},{1,3},{2,4},{3,5},{4,6},{5,7},{8,10},{9,11},{10,12},{11,13},... | collective-permute-start | bytes 196616 | tf_op jit(solution)/shard_map/ppermute | solution.py:704
  18.7 8.3 %collective-permute-start.3 = (f32[128,128]{1,0:T(8,128)}, f32[128,128]{1,0:T(8,128)S(1)}, u32[]{:S(2)}, u32[]{:S(2)}) collective-permute-start(f32[128,128]{1,0:T(8,128)} %get-tuple-element.39), channel_id=1, source_target_pairs={{2,0},{3,1},{4,2},{5,3},{6,4},{7,5},{10,8},{11,9},{12,10},{13,11},... | collective-permute-start | bytes 196616 | tf_op jit(solution)/shard_map/ppermute | solution.py:704
  20.8 6.2 %collective-permute-start.4 = (f32[128,128]{1,0:T(8,128)}, f32[128,128]{1,0:T(8,128)S(1)}, u32[]{:S(2)}, u32[]{:S(2)}) collective-permute-start(f32[128,128]{1,0:T(8,128)} %get-tuple-element.40), channel_id=1, source_target_pairs={{0,8},{8,16},{16,24},{1,9},{9,17},{17,25},{2,10},{10,18},{18,26},{... | collective-permute-start | bytes 196616 | tf_op jit(solution)/shard_map/ppermute | solution.py:704
  23.9 5.2 %collective-permute-start.5 = (f32[128,128]{1,0:T(8,128)}, f32[128,128]{1,0:T(8,128)S(1)}, u32[]{:S(2)}, u32[]{:S(2)}) collective-permute-start(f32[128,128]{1,0:T(8,128)} %get-tuple-element.41), channel_id=1, source_target_pairs={{8,0},{16,8},{24,16},{9,1},{17,9},{25,17},{10,2},{18,10},{26,18},{... | collective-permute-start | bytes 196616 | tf_op jit(solution)/shard_map/ppermute | solution.py:704
  29.1 1.0 copy-start.2
  30.2 1.0 copy-start.4
  31.2 6.5 %copy-start.12 = (s32[1024]{0:T(1024)S(1)}, s32[1024]{0:T(1024)}, u32[]{:S(2)}) copy-start(s32[1024]{0:T(1024)} %param.20) | copy-start | bytes 12292
  31.2 6.5 %copy-start.13 = (s32[1024]{0:T(1024)S(1)}, s32[1024]{0:T(1024)}, u32[]{:S(2)}) copy-start(s32[1024]{0:T(1024)} %param.19) | copy-start | bytes 12292
  31.2 6.5 %copy-start.6 = (f32[256,4,128]{2,1,0:T(4,128)S(1)}, f32[256,4,128]{2,1,0:T(4,128)}, u32[]{:S(2)}) copy-start(f32[256,4,128]{2,1,0:T(4,128)} %get-tuple-element.34) | copy-start | bytes 1572868
  31.2 6.5 %copy-start.8 = (f32[128,128]{1,0:T(8,128)S(1)}, f32[128,128]{1,0:T(8,128)}, u32[]{:S(2)}) copy-start(f32[128,128]{1,0:T(8,128)} %get-tuple-element.42.refs_0_) | copy-start | bytes 196612
  31.4 124.8 %collective-permute-start.6 = (f32[14,48,256]{2,1,0:T(8,128)S(1)}, f32[14,48,256]{2,1,0:T(8,128)S(1)}, u32[]{:S(2)}, u32[]{:S(2)}) collective-permute-start(f32[14,48,256]{2,1,0:T(8,128)S(1)} %get-tuple-element.53), channel_id=1, source_target_pairs={{0,8},{8,16},{16,24},{1,9},{9,17},{17,25},{2,10},{10,18},{18,26},{... | collective-permute-start | bytes 2064392 | tf_op jit(solution)/shard_map/ppermute | solution.py:704
  33.4 126.0 %collective-permute-start.7 = (f32[14,48,256]{2,1,0:T(8,128)S(1)}, f32[14,48,256]{2,1,0:T(8,128)S(1)}, u32[]{:S(2)}, u32[]{:S(2)}) collective-permute-start(f32[14,48,256]{2,1,0:T(8,128)S(1)} %get-tuple-element.54), channel_id=1, source_target_pairs={{8,0},{16,8},{24,16},{9,1},{17,9},{25,17},{10,2},{18,10},{26,18},{... | collective-permute-start | bytes 2064392 | tf_op jit(solution)/shard_map/ppermute | solution.py:704
  37.7 0.7 copy-start.10
  38.4 125.6 %copy-start.3 = (f32[16,32,256]{2,1,0:T(8,128)S(1)}, f32[16,32,256]{2,1,0:T(8,128)}, u32[]{:S(2)}) copy-start(f32[16,32,256]{2,1,0:T(8,128)} %get-tuple-element.51.refs_1_.refs_3_) | copy-start | bytes 1572868
  38.4 125.6 %copy-start.5 = (f32[16,32,256]{2,1,0:T(8,128)S(1)}, f32[16,32,256]{2,1,0:T(8,128)}, u32[]{:S(2)}) copy-start(f32[16,32,256]{2,1,0:T(8,128)} %get-tuple-element.52.refs_2_.refs_4_) | copy-start | bytes 1572868
  38.4 125.6 %copy-start.7 = (f32[256,128]{1,0:T(8,128)S(1)}, f32[256,128]{1,0:T(8,128)}, u32[]{:S(2)}) copy-start(f32[256,128]{1,0:T(8,128)} %get-tuple-element.50.refs_1_) | copy-start | bytes 393220
  144.0 10.1 %collective-permute-start.13 = (f32[128,128]{1,0:T(8,128)S(1)}, f32[128,128]{1,0:T(8,128)S(1)}, u32[]{:S(2)}, u32[]{:S(2)}) collective-permute-start(f32[128,128]{1,0:T(8,128)S(1)} %get-tuple-element.62), channel_id=1, source_target_pairs={{0,8},{8,16},{16,24},{1,9},{9,17},{17,25},{2,10},{10,18},{18,26},{... | collective-permute-start | bytes 196616 | tf_op jit(solution)/shard_map/ppermute | solution.py:704
  146.0 36.7 %collective-permute-start.8 = (f32[128,128]{1,0:T(8,128)S(1)}, f32[128,128]{1,0:T(8,128)S(1)}, u32[]{:S(2)}, u32[]{:S(2)}) collective-permute-start(f32[128,128]{1,0:T(8,128)S(1)} %get-tuple-element.57), channel_id=1, source_target_pairs={{1,0},{2,1},{3,2},{4,3},{5,4},{6,5},{7,6},{9,8},{10,9},{11,10},{12... | collective-permute-start | bytes 196616 | tf_op jit(solution)/shard_map/ppermute | solution.py:704
  151.0 31.7 %collective-permute-start.9 = (f32[128,128]{1,0:T(8,128)S(1)}, f32[128,128]{1,0:T(8,128)S(1)}, u32[]{:S(2)}, u32[]{:S(2)}) collective-permute-start(f32[128,128]{1,0:T(8,128)S(1)} %get-tuple-element.58), channel_id=1, source_target_pairs={{0,1},{1,2},{2,3},{3,4},{4,5},{5,6},{6,7},{8,9},{9,10},{10,11},{11... | collective-permute-start | bytes 196616 | tf_op jit(solution)/shard_map/ppermute | solution.py:704
  154.1 28.6 %collective-permute-start.10 = (f32[128,128]{1,0:T(8,128)S(1)}, f32[128,128]{1,0:T(8,128)S(1)}, u32[]{:S(2)}, u32[]{:S(2)}) collective-permute-start(f32[128,128]{1,0:T(8,128)S(1)} %get-tuple-element.59), channel_id=1, source_target_pairs={{2,0},{3,1},{4,2},{5,3},{6,4},{7,5},{10,8},{11,9},{12,10},{13,11},... | collective-permute-start | bytes 196616 | tf_op jit(solution)/shard_map/ppermute | solution.py:704
  156.2 26.5 %collective-permute-start.11 = (f32[128,128]{1,0:T(8,128)S(1)}, f32[128,128]{1,0:T(8,128)S(1)}, u32[]{:S(2)}, u32[]{:S(2)}) collective-permute-start(f32[128,128]{1,0:T(8,128)S(1)} %get-tuple-element.60), channel_id=1, source_target_pairs={{0,2},{1,3},{2,4},{3,5},{4,6},{5,7},{8,10},{9,11},{10,12},{11,13},... | collective-permute-start | bytes 196616 | tf_op jit(solution)/shard_map/ppermute | solution.py:704
  159.4 4.6 %copy-start.11 = (s32[256]{0:T(256)S(1)}, s32[256]{0:T(256)}, u32[]{:S(2)}) copy-start(s32[256]{0:T(256)} %refs_0_.3) | copy-start | bytes 3076
  159.4 23.3 %collective-permute-start.12 = (f32[128,128]{1,0:T(8,128)S(1)}, f32[128,128]{1,0:T(8,128)S(1)}, u32[]{:S(2)}, u32[]{:S(2)}) collective-permute-start(f32[128,128]{1,0:T(8,128)S(1)} %get-tuple-element.61), channel_id=1, source_target_pairs={{8,0},{16,8},{24,16},{9,1},{17,9},{25,17},{10,2},{18,10},{26,18},{... | collective-permute-start | bytes 196616 | tf_op jit(solution)/shard_map/ppermute | solution.py:704
  182.7 0.7 copy-start.9

commit v5 on v4

--- a/solution.py
+++ b/solution.py
@@ -8,7 +8,8 @@
 from jax.sharding import PartitionSpec as P
 
 SWEEPS = 4
-UNROLL = 4
+QUAD = 4
+UNROLL = 8
 HALO_WIDTHS = (SWEEPS + 1, SWEEPS, SWEEPS, 1)
 MARGIN = 8
 CELL_BITS = 8
@@ -59,8 +60,11 @@
     ) = refs[2 * sources + 1 :]
     clusters = own_ref.shape[0] // 4
     slots = other_out_refs[0].shape[0] // 4
+    others = slots * sources
     groups = own_rows_ref.shape[0] // UNROLL
-    units = UNROLL // 2
+    units = UNROLL // QUAD
+    groups_of_own = clusters // QUAD
+    groups_of_other = others // QUAD
     ones = jnp.ones((8, 128), jnp.float32)
     zeros = jnp.zeros((8, 128), jnp.float32)
 
@@ -70,6 +74,12 @@
     def put(rows, base, stride):
         for index, row in enumerate(rows):
             stage_ref[pl.ds(base + index, 8, stride=stride), :] = row
+
+    def put_turned(target_ref, columns, group, groups_in_all):
+        for turn in range(QUAD):
+            rolled = columns if turn == 0 else pltpu.roll(columns, 32 * turn, 1)
+            at = pl.multiple_of((turn * groups_in_all + group) * 128, 128)
+            target_ref[pl.ds(at, 128), :] = rolled.astype(jnp.bfloat16)
 
     def near_rows(step, _):
         start = pl.multiple_of(step * 8, 8)
@@ -89,11 +99,10 @@
         put(rows, 0, 32)
         for half in range(2):
             columns = stage_ref[128 * half : 128 * half + 128, :].T
-            for index in range(4):
-                at = pl.ds(pl.multiple_of((start + 4 * half + index) * 128, 128), 128)
-                rolled = columns if index == 0 else pltpu.roll(columns, 128 - 32 * index, 1)
-                near_ref[at, :] = rolled.astype(jnp.bfloat16)
-                own_sum_ref[at, :] = jnp.zeros((128, 128), jnp.float32)
+            put_turned(near_ref, columns, step * 2 + half, groups_of_own)
+        for index in range(8):
+            at = pl.ds(pl.multiple_of((start + index) * 128, 128), 128)
+            own_sum_ref[at, :] = jnp.zeros((128, 128), jnp.float32)
         return 0
 
     def far_rows(source, step, _):
@@ -101,13 +110,10 @@
         start = source * slots + local
         *comps, charge = components(other_refs[source], local)
         moments = moment_rows(comps, charge) + [zeros] * 4
-        put(moments + moments, 0, 32)
+        put(moments + [zeros] * 16, 0, 32)
         for half in range(2):
             columns = stage_ref[128 * half : 128 * half + 128, :].T
-            for index in range(4):
-                at = pl.ds(pl.multiple_of((start + 4 * half + index) * 128, 128), 128)
-                rolled = columns if index == 0 else pltpu.roll(columns, 128 - 32 * index, 1)
-                other_moment_ref[at, :] = rolled.astype(jnp.bfloat16)
+            put_turned(other_moment_ref, columns, (start // 8) * 2 + half, groups_of_other)
         rows = []
         square = zeros
         for comp in comps:
@@ -130,80 +136,93 @@
     weight_ref[...] = jnp.zeros_like(weight_ref)
 
     lane = lax.broadcasted_iota(jnp.int32, (128, 128), 1)
-    lane_row = lax.broadcasted_iota(jnp.int32, (1, 128), 1)
-    left_mask = jnp.where(lane_row < 16, 1.0, 0.0).astype(jnp.bfloat16)
-    right_mask = jnp.where((lane_row >= 16) & (lane_row < 32), 1.0, 0.0).astype(jnp.bfloat16)
-
-    def distances(pair, turn):
-        own = own_rows_ref[pair]
-        other = other_rows_ref[pair]
-        near = near_ref[pl.ds(pl.multiple_of(own * 128, 128), 128), 0:32]
-        far = far_ref[pl.ds(pl.multiple_of(other * 32, 32), 32), :]
-        dist_ref[turn] = jnp.dot(near, far, preferred_element_type=jnp.float32)
-
-    def weights(turn):
-        root = lax.rsqrt(dist_ref[turn])
+    quarter = lax.shift_right_logical(lane, 5)
+    quarter_row = lax.shift_right_logical(lax.broadcasted_iota(jnp.int32, (1, 128), 1), 5)
+    masks = [jnp.where(quarter_row == turn, 1.0, 0.0).astype(jnp.bfloat16) for turn in range(QUAD)]
+    empty = jnp.zeros((32, 128), jnp.bfloat16)
+
+    def turned(source_ref, index, turn, groups_in_all):
+        rotation = lax.bitwise_and(turn - index, 3)
+        group = rotation * groups_in_all + lax.shift_right_logical(index, 2)
+        return source_ref[pl.ds(pl.multiple_of(group * 128, 128), 128), :] * masks[turn]
+
+    def block_diagonal(blocks):
+        blank = empty[: blocks[0].shape[0]]
+        lines = [
+            jnp.concatenate([block if turn == at else blank for turn in range(QUAD)], axis=1)
+            for at, block in enumerate(blocks)
+        ]
+        return jnp.concatenate(lines, axis=0)
+
+    def distances(pair, unit):
+        near = None
+        far = []
+        for turn in range(QUAD):
+            tile = turned(near_ref, own_rows_ref[pair + turn], turn, groups_of_own)
+            near = tile if near is None else near + tile
+            at = pl.multiple_of(other_rows_ref[pair + turn] * 32, 32)
+            far.append(far_ref[pl.ds(at, 32), :])
+        dist_ref[unit] = jnp.dot(near, block_diagonal(far), preferred_element_type=jnp.float32)
+
+    def weights(unit, turn):
+        root = lax.rsqrt(dist_ref[unit, :, 128 * turn : 128 * turn + 128])
         weight = root * root * root
         high = weight.astype(jnp.bfloat16)
-        lanes = slice(128 * (turn % 2), 128 * (turn % 2) + 128)
-        weight_ref[2 * (turn // 2), :, lanes] = high
-        weight_ref[2 * (turn // 2) + 1, :, lanes] = (weight - high.astype(jnp.float32)).astype(
-            jnp.bfloat16
-        )
-
-    def moment_of(moment_ref, row, size):
-        return moment_ref[pl.ds(pl.multiple_of(row * size, size), size), :]
+        weight_ref[unit, 128 * turn : 128 * turn + 128, :128] = high
+        weight_ref[unit, 128 * turn : 128 * turn + 128, 128:] = (
+            weight - high.astype(jnp.float32)
+        ).astype(jnp.bfloat16)
 
     def products(pair, unit):
-        owns = [own_rows_ref[pair + turn] for turn in range(2)]
-        others = [other_rows_ref[pair + turn] for turn in range(2)]
-        high = weight_ref[2 * unit]
-        low = weight_ref[2 * unit + 1]
+        owns = [own_rows_ref[pair + turn] for turn in range(QUAD)]
+        others = [other_rows_ref[pair + turn] for turn in range(QUAD)]
+        both = weight_ref[unit]
+        levels = [
+            jnp.concatenate(
+                [both[128 * turn : 128 * turn + 128, lanes] for turn in range(QUAD)], axis=1
+            )
+            for lanes in (slice(0, 128), slice(128, 256))
+        ]
         columns = jnp.concatenate(
-            [
-                moment_of(other_moment_ref, others[0], 128) * left_mask,
-                moment_of(other_moment_ref, others[1], 128) * right_mask,
-            ],
+            [turned(other_moment_ref, others[turn], turn, groups_of_other) for turn in range(QUAD)],
             axis=0,
         )
-        rows = jnp.concatenate(
-            [moment_of(own_moment_ref, owns[0], 16), moment_of(own_moment_ref, owns[1], 16)], axis=0
+        to_own = jnp.dot(
+            jnp.concatenate(levels, axis=0), columns, preferred_element_type=jnp.float32
         )
-        to_own = jnp.dot(high, columns, preferred_element_type=jnp.float32) + jnp.dot(
-            low, columns, preferred_element_type=jnp.float32
+        rows = block_diagonal(
+            [own_moment_ref[pl.ds(pl.multiple_of(own * 16, 16), 16), :] for own in owns]
         )
-        to_other = jnp.dot(rows, high, preferred_element_type=jnp.float32) + jnp.dot(
-            rows, low, preferred_element_type=jnp.float32
-        )
-        return (owns, others, to_own, (to_other[:16, :128], to_other[16:, 128:]))
+        to_other = jnp.dot(rows, both, preferred_element_type=jnp.float32)
+        return (owns, others, to_own[:128] + to_own[128:], to_other[:, :128] + to_other[:, 128:])
 
     def visit(step, _):
         last = jnp.maximum(step - 2, 0) * UNROLL
         first = jnp.minimum(step, groups - 1) * UNROLL
-        results = [products(last + 2 * unit, unit) for unit in range(units)]
-        for turn in range(UNROLL):
-            weights(turn)
-        for turn in range(UNROLL):
-            distances(first + turn, turn)
+        results = [products(last + QUAD * unit, unit) for unit in range(units)]
+        for unit in range(units):
+            for turn in range(QUAD):
+                weights(unit, turn)
+        for unit in range(units):
+            distances(first + QUAD * unit, unit)
         for owns, others, to_own, to_other in results:
-            for turn in range(2):
-                kept = jnp.where(lane < 16 if turn == 0 else lane >= 16, to_own, 0.0)
-                own_sum_ref[pl.ds(pl.multiple_of(owns[turn] * 128, 128), 128), :] += kept
-                other_sum_ref[pl.ds(pl.multiple_of(others[turn] * 16, 16), 16), :] += to_other[turn]
+            for turn in range(QUAD):
+                own_at = pl.ds(pl.multiple_of(owns[turn] * 128, 128), 128)
+                other_at = pl.ds(pl.multiple_of(others[turn] * 16, 16), 16)
+                own_sum_ref[own_at, :] += jnp.where(quarter == turn, to_own, 0.0)
+                other_sum_ref[other_at, :] += to_other[16 * turn : 16 * turn + 16]
         return 0
 
     lax.fori_loop(0, groups + 2, visit, 0)
 
-    def finish(data_ref, out_ref, start, rows_ref, bases, stride):
+    def finish(data_ref, out_ref, start, rows_ref, base, stride):
         *comps, charge = components(data_ref, start)
 
         def total(part):
             terms = [
-                rows_ref[pl.ds(base + 4 * level + part, 8, stride=stride), :]
-                for level in range(3)
-                for base in bases
+                rows_ref[pl.ds(base + 4 * level + part, 8, stride=stride), :] for level in range(3)
             ]
-            return functools.reduce(lambda left, right: right + left, terms[::-1])
+            return terms[0] + (terms[1] + terms[2])
 
         weight = total(3)
         scale = coulomb_scale * charge
@@ -218,13 +237,11 @@
             for index in range(4):
                 at = pl.ds(pl.multiple_of((start + 4 * half + index) * 128, 128), 128)
                 block = own_sum_ref[at, :]
-                if index:
-                    rolled = pltpu.roll(block, 32 * index, 1)
-                    columns = jnp.where(lane < 32 * index, columns, rolled)
-                else:
-                    columns = block
+                block = block + pltpu.roll(block, 64, 1)
+                block = block + pltpu.roll(block, 32, 1)
+                columns = block if index == 0 else jnp.where(quarter < index, columns, block)
             stage_ref[128 * half : 128 * half + 128, :] = columns.T
-        finish(own_ref, own_out_ref, start, stage_ref, (0, 16), 32)
+        finish(own_ref, own_out_ref, start, stage_ref, 0, 32)
         return 0
 
     def finish_other(source, step, _):
@@ -234,7 +251,7 @@
             other_out_refs[source],
             start,
             other_sum_ref,
-            ((source * slots + start) * 16,),
+            (source * slots + start) * 16,
             16,
         )
         return 0
@@ -266,8 +283,8 @@
             pltpu.VMEM((clusters * 128, 128), jnp.float32),
             pltpu.VMEM((others * 16, 128), jnp.float32),
             pltpu.VMEM((384, 128), jnp.float32),
-            pltpu.VMEM((UNROLL, 128, 128), jnp.float32),
-            pltpu.VMEM((UNROLL, 128, 256), jnp.bfloat16),
+            pltpu.VMEM((UNROLL // QUAD, 128, 128 * QUAD), jnp.float32),
+            pltpu.VMEM((UNROLL // QUAD, 128 * QUAD, 256), jnp.bfloat16),
         ],
         compiler_params=pltpu.CompilerParams(vmem_limit_bytes=46 * 1024 * 1024),
         cost_estimate=pl.CostEstimate(

time: 187 us -> 190 us (1.016)
  Pallas kernels: 136 us -> 140 us
    pallas_call x1, Pallas kernels: 106 us -> 109 us  [pair_forces(): pl.pallas_call(pair_kernel, out_shape=(jax.ShapeDtypeStruct(own.shape, jn...]
where the time goes in v5:
time: 190 us
  Pallas kernels  140 us (74%)
  starting transfers between devices  43.3 us (23%)
  local copies, waits for them, and re-layouts  3.45 us (2%)
  waiting for transfers between devices  2.16 us (1%)
    pallas_call x1, Pallas kernels, pair_forces(): pl.pallas_call(pair_kernel, out_shape=(jax.ShapeDtypeStruct(own.shape, jn...  109 us
    ppermute x14, starting transfers between devices, passed_along(): return lax.ppermute(shard, axis, pairs)  43.3 us
    pallas_call x1, Pallas kernels, grid_step(): pl.pallas_call(functools.partial(grid_kernel, base), out_shape=(jax.Shape...  18.7 us
    pallas_call x1, Pallas kernels, prepare(): pl.pallas_call(prepare_kernel, out_shape=(jax.ShapeDtypeStruct((clusters,...  9.1 us
  transfers between devices with their start and end apart: 14, of which 1 were waited for; matrix products, arithmetic and copies ran while one was open for 0% of the time, Pallas kernels for 67%

profile of v5, /device:TPU:13, one launch (start us, length us, event | category | flops | bytes accessed | tf_op | source)
XLA Modules:
  0.0 189.8 jit_solution(16651144504258563518)
XLA Ops:
  0.6 0.0 copy-start
  0.6 0.0 copy-start.1
  0.7 9.1 %prepare.1 = (f32[256,4,128]{2,1,0:T(4,128)}, f32[256,128]{1,0:T(8,128)}, f32[16,32,256]{2,1,0:T(8,128)}, f32[16,32,256]{2,1,0:T(8,128)}, f32[128,128]{1,0:T(8,1...) custom-call(s32[256]{0:T(256)} %fill_ref.1, ...), custom_call_target="tpu_custom_call" | custom-call | tf_op jit(solution)/shard_map/prepare/pallas_call | solution.py:417
  9.8 3.8 %collective-permute-start = (f32[640,128]{1,0:T(8,128)}, f32[640,128]{1,0:T(8,128)S(1)}, u32[]{:S(2)}, u32[]{:S(2)}) collective-permute-start(f32[640,128]{1,0:T(8,128)} %get-tuple-element.36), channel_id=1, source_target_pairs={{0,1},{1,2},{2,3},{3,4},{4,5},{5,6},{6,7},{8,9},{9,10},{10,11},{11... | collective-permute-start | bytes 983048 | tf_op jit(solution)/shard_map/ppermute | solution.py:721
  13.5 1.9 %collective-permute-start.1 = (f32[640,128]{1,0:T(8,128)}, f32[640,128]{1,0:T(8,128)S(1)}, u32[]{:S(2)}, u32[]{:S(2)}) collective-permute-start(f32[640,128]{1,0:T(8,128)} %get-tuple-element.37), channel_id=1, source_target_pairs={{1,0},{2,1},{3,2},{4,3},{5,4},{6,5},{7,6},{9,8},{10,9},{11,10},{12... | collective-permute-start | bytes 983048 | tf_op jit(solution)/shard_map/ppermute | solution.py:721
  15.5 3.2 %collective-permute-start.2 = (f32[128,128]{1,0:T(8,128)}, f32[128,128]{1,0:T(8,128)S(1)}, u32[]{:S(2)}, u32[]{:S(2)}) collective-permute-start(f32[128,128]{1,0:T(8,128)} %get-tuple-element.38), channel_id=1, source_target_pairs={{0,2},{1,3},{2,4},{3,5},{4,6},{5,7},{8,10},{9,11},{10,12},{11,13},... | collective-permute-start | bytes 196616 | tf_op jit(solution)/shard_map/ppermute | solution.py:721
  18.7 2.1 %collective-permute-start.3 = (f32[128,128]{1,0:T(8,128)}, f32[128,128]{1,0:T(8,128)S(1)}, u32[]{:S(2)}, u32[]{:S(2)}) collective-permute-start(f32[128,128]{1,0:T(8,128)} %get-tuple-element.39), channel_id=1, source_target_pairs={{2,0},{3,1},{4,2},{5,3},{6,4},{7,5},{10,8},{11,9},{12,10},{13,11},... | collective-permute-start | bytes 196616 | tf_op jit(solution)/shard_map/ppermute | solution.py:721
  20.8 3.1 %collective-permute-start.4 = (f32[128,128]{1,0:T(8,128)}, f32[128,128]{1,0:T(8,128)S(1)}, u32[]{:S(2)}, u32[]{:S(2)}) collective-permute-start(f32[128,128]{1,0:T(8,128)} %get-tuple-element.40), channel_id=1, source_target_pairs={{0,8},{8,16},{16,24},{1,9},{9,17},{17,25},{2,10},{10,18},{18,26},{... | collective-permute-start | bytes 196616 | tf_op jit(solution)/shard_map/ppermute | solution.py:721
  23.9 0.0 collective-permute-done.2.refs_3_
  23.9 3.1 %collective-permute-start.5 = (f32[128,128]{1,0:T(8,128)}, f32[128,128]{1,0:T(8,128)S(1)}, u32[]{:S(2)}, u32[]{:S(2)}) collective-permute-start(f32[128,128]{1,0:T(8,128)} %get-tuple-element.41), channel_id=1, source_target_pairs={{8,0},{16,8},{24,16},{9,1},{17,9},{25,17},{10,2},{18,10},{26,18},{... | collective-permute-start | bytes 196616 | tf_op jit(solution)/shard_map/ppermute | solution.py:721
  27.0 0.0 collective-permute-done.3.refs_4_
  27.0 0.0 collective-permute-done.4.refs_5_
  27.0 2.1 %collective-permute-done.5.refs_6_ = f32[128,128]{1,0:T(8,128)S(1)} collective-permute-done((f32[128,128]{1,0:T(8,128)}, f32[128,128]{1,0:T(8,128)S(1)}, u32[]{:S(2)}, u32[]{:S(2)}) %collective-permute-start.5) | collective-permute-done | bytes 65568 | tf_op jit(solution)/shard_map/ppermute | solution.py:721
  29.1 0.0 collective-permute-done.refs_1_.refs_4_.refs_6_
  29.1 0.0 collective-permute-done.1.refs_2_.refs_5_.refs_7_
  29.1 0.0 copy-done
  29.1 0.0 copy-done.1
  29.1 0.0 copy-start.2
  29.2 1.0 copy-done.2
  30.2 0.0 copy-start.4
  30.2 1.0 copy-done.4
  31.2 0.0 copy-start.12
  31.2 0.0 copy-start.13
  31.2 0.0 copy-start.6
  31.2 0.0 copy-start.8
  31.2 0.1 planes.1
  31.4 2.1 %collective-permute-start.6 = (f32[14,48,256]{2,1,0:T(8,128)S(1)}, f32[14,48,256]{2,1,0:T(8,128)S(1)}, u32[]{:S(2)}, u32[]{:S(2)}) collective-permute-start(f32[14,48,256]{2,1,0:T(8,128)S(1)} %get-tuple-element.53), channel_id=1, source_target_pairs={{0,8},{8,16},{16,24},{1,9},{9,17},{17,25},{2,10},{10,18},{18,26},{... | collective-permute-start | bytes 2064392 | tf_op jit(solution)/shard_map/ppermute | solution.py:721
  33.4 4.3 %collective-permute-start.7 = (f32[14,48,256]{2,1,0:T(8,128)S(1)}, f32[14,48,256]{2,1,0:T(8,128)S(1)}, u32[]{:S(2)}, u32[]{:S(2)}) collective-permute-start(f32[14,48,256]{2,1,0:T(8,128)S(1)} %get-tuple-element.54), channel_id=1, source_target_pairs={{8,0},{16,8},{24,16},{9,1},{17,9},{25,17},{10,2},{18,10},{26,18},{... | collective-permute-start | bytes 2064392 | tf_op jit(solution)/shard_map/ppermute | solution.py:721
  37.7 0.0 copy-done.12
  37.7 0.0 copy-done.13
  37.7 0.0 copy-start.10
  37.8 0.0 copy-done.6
  37.8 0.0 copy-done.8
  37.8 0.6 copy-done.10
  38.4 0.0 copy-start.3
  38.4 0.0 copy-start.5
  38.4 0.0 copy-start.7
  38.4 109.2 %pair_forces.1 = (f32[1024,128]{1,0:T(8,128)S(1)}, f32[128,128]{1,0:T(8,128)S(1)}, f32[128,128]{1,0:T(8,128)S(1)}, f32[128,128]{1,0:T(8,128)S(1)}, f32[128,128]{...) custom-call(s32[1024]{0:T(1024)S(1)} %copy-done.10, ...), custom_call_target="tpu_custom_call" | custom-call | flops 335544320 | bytes 4194304 | tf_op jit(solution)/shard_map/pair_forces/pallas_call | solution.py:270
  147.6 1.9 %collective-permute-start.13 = (f32[128,128]{1,0:T(8,128)S(1)}, f32[128,128]{1,0:T(8,128)S(1)}, u32[]{:S(2)}, u32[]{:S(2)}) collective-permute-start(f32[128,128]{1,0:T(8,128)S(1)} %get-tuple-element.62), channel_id=1, source_target_pairs={{0,8},{8,16},{16,24},{1,9},{9,17},{17,25},{2,10},{10,18},{18,26},{... | collective-permute-start | bytes 196616 | tf_op jit(solution)/shard_map/ppermute | solution.py:721
  149.5 5.0 %collective-permute-start.8 = (f32[128,128]{1,0:T(8,128)S(1)}, f32[128,128]{1,0:T(8,128)S(1)}, u32[]{:S(2)}, u32[]{:S(2)}) collective-permute-start(f32[128,128]{1,0:T(8,128)S(1)} %get-tuple-element.57), channel_id=1, source_target_pairs={{1,0},{2,1},{3,2},{4,3},{5,4},{6,5},{7,6},{9,8},{10,9},{11,10},{12... | collective-permute-start | bytes 196616 | tf_op jit(solution)/shard_map/ppermute | solution.py:721
  154.5 3.1 %collective-permute-start.9 = (f32[128,128]{1,0:T(8,128)S(1)}, f32[128,128]{1,0:T(8,128)S(1)}, u32[]{:S(2)}, u32[]{:S(2)}) collective-permute-start(f32[128,128]{1,0:T(8,128)S(1)} %get-tuple-element.58), channel_id=1, source_target_pairs={{0,1},{1,2},{2,3},{3,4},{4,5},{5,6},{6,7},{8,9},{9,10},{10,11},{11... | collective-permute-start | bytes 196616 | tf_op jit(solution)/shard_map/ppermute | solution.py:721
  157.6 0.0 collective-permute-done.13
  157.7 2.1 %collective-permute-start.10 = (f32[128,128]{1,0:T(8,128)S(1)}, f32[128,128]{1,0:T(8,128)S(1)}, u32[]{:S(2)}, u32[]{:S(2)}) collective-permute-start(f32[128,128]{1,0:T(8,128)S(1)} %get-tuple-element.59), channel_id=1, source_target_pairs={{2,0},{3,1},{4,2},{5,3},{6,4},{7,5},{10,8},{11,9},{12,10},{13,11},... | collective-permute-start | bytes 196616 | tf_op jit(solution)/shard_map/ppermute | solution.py:721
  159.7 0.0 collective-permute-done.6.refs_8_
  159.8 3.2 %collective-permute-start.11 = (f32[128,128]{1,0:T(8,128)S(1)}, f32[128,128]{1,0:T(8,128)S(1)}, u32[]{:S(2)}, u32[]{:S(2)}) collective-permute-start(f32[128,128]{1,0:T(8,128)S(1)} %get-tuple-element.60), channel_id=1, source_target_pairs={{0,2},{1,3},{2,4},{3,5},{4,6},{5,7},{8,10},{9,11},{10,12},{11,13},... | collective-permute-start | bytes 196616 | tf_op jit(solution)/shard_map/ppermute | solution.py:721
  163.0 0.0 collective-permute-done.7.refs_9_
  163.0 0.0 copy-start.11
  163.0 4.5 %collective-permute-start.12 = (f32[128,128]{1,0:T(8,128)S(1)}, f32[128,128]{1,0:T(8,128)S(1)}, u32[]{:S(2)}, u32[]{:S(2)}) collective-permute-start(f32[128,128]{1,0:T(8,128)S(1)} %get-tuple-element.61), channel_id=1, source_target_pairs={{8,0},{16,8},{24,16},{9,1},{17,9},{25,17},{10,2},{18,10},{26,18},{... | collective-permute-start | bytes 196616 | tf_op jit(solution)/shard_map/ppermute | solution.py:721
  167.5 0.0 copy-done.3
  167.6 0.0 copy-done.5
  167.6 0.0 copy-done.7
  167.6 0.0 copy-done.11
  167.6 18.7 %grid_step.1 = (f32[16,32,256]{2,1,0:T(8,128)}, f32[16,32,256]{2,1,0:T(8,128)}, f32[1024,128]{1,0:T(8,128)S(1)}) custom-call(s32[256]{0:T(256)S(1)} %copy-done.11, f32[256,128]{1,0:T(8,128)S(1)} %copy-done.7, f32[16,32,256]{2,1,0:T(8,128)S(1)} %copy-done.1, f32[16,32,256]{2,1,0:T(8,128)S(1)} %copy-done.3, f32[16,32,256]{2,1,0:T(8,128)S(1)} %copy-done.5, ...), custom_call_target="tpu_custom_call" | custom-call | flops 31948800 | bytes 8388608 | tf_op jit(solution)/shard_map/grid_step/pallas_call | solution.py:660
  186.3 0.0 collective-permute-done.8
  186.3 0.0 collective-permute-done.9
  186.3 0.0 collective-permute-done.10
  186.3 0.0 collective-permute-done.11
  186.3 0.0 collective-permute-done.12
  186.3 0.0 copy-start.9
  186.3 0.7 copy-done.9
  187.0 2.8 %gather_forces.1 = f32[3,32768]{1,0:T(4,128)} custom-call(s32[7,32]{1,0:T(8,128)S(1)} %copy-done.9, f32[256,4,128]{2,1,0:T(4,128)S(1)} %bitcast.12, f32[256,4,128]{2,1,0:T(4,128)S(1)} %bitcast.13, f32[32,4,128]{2,1,0:T(4,128)S(1)} %bitcast.14, f32[32,4,128]{2,1,0:T(4,128)S(1)} %bitcast.16, f32[32,4,128]{2,1,0:T(4,128)S(1)} %bitcast.17, ...), custom_call_target="tpu_custom_call" | custom-call | tf_op jit(solution)/shard_map/gather_forces/pallas_call | solution.py:707
  (1 shorter events, 0.0 us)
Async XLA Ops:
  0.6 28.5 %copy-start = (f32[16,32,256]{2,1,0:T(8,128)S(1)}, f32[16,32,256]{2,1,0:T(8,128)}, u32[]{:S(2)}) copy-start(f32[16,32,256]{2,1,0:T(8,128)} %refs_5_.1) | copy-start | bytes 1572868
  0.6 28.5 %copy-start.1 = (f32[16,32,256]{2,1,0:T(8,128)S(1)}, f32[16,32,256]{2,1,0:T(8,128)}, u32[]{:S(2)}) copy-start(f32[16,32,256]{2,1,0:T(8,128)} %refs_2_.1) | copy-start | bytes 1572868
  9.8 19.4 %collective-permute-start = (f32[640,128]{1,0:T(8,128)}, f32[640,128]{1,0:T(8,128)S(1)}, u32[]{:S(2)}, u32[]{:S(2)}) collective-permute-start(f32[640,128]{1,0:T(8,128)} %get-tuple-element.36), channel_id=1, source_target_pairs={{0,1},{1,2},{2,3},{3,4},{4,5},{5,6},{6,7},{8,9},{9,10},{10,11},{11... | collective-permute-start | bytes 983048 | tf_op jit(solution)/shard_map/ppermute | solution.py:721
  13.5 15.6 %collective-permute-start.1 = (f32[640,128]{1,0:T(8,128)}, f32[640,128]{1,0:T(8,128)S(1)}, u32[]{:S(2)}, u32[]{:S(2)}) collective-permute-start(f32[640,128]{1,0:T(8,128)} %get-tuple-element.37), channel_id=1, source_target_pairs={{1,0},{2,1},{3,2},{4,3},{5,4},{6,5},{7,6},{9,8},{10,9},{11,10},{12... | collective-permute-start | bytes 983048 | tf_op jit(solution)/shard_map/ppermute | solution.py:721
  15.5 8.4 %collective-permute-start.2 = (f32[128,128]{1,0:T(8,128)}, f32[128,128]{1,0:T(8,128)S(1)}, u32[]{:S(2)}, u32[]{:S(2)}) collective-permute-start(f32[128,128]{1,0:T(8,128)} %get-tuple-element.38), channel_id=1, source_target_pairs={{0,2},{1,3},{2,4},{3,5},{4,6},{5,7},{8,10},{9,11},{10,12},{11,13},... | collective-permute-start | bytes 196616 | tf_op jit(solution)/shard_map/ppermute | solution.py:721
  18.7 8.3 %collective-permute-start.3 = (f32[128,128]{1,0:T(8,128)}, f32[128,128]{1,0:T(8,128)S(1)}, u32[]{:S(2)}, u32[]{:S(2)}) collective-permute-start(f32[128,128]{1,0:T(8,128)} %get-tuple-element.39), channel_id=1, source_target_pairs={{2,0},{3,1},{4,2},{5,3},{6,4},{7,5},{10,8},{11,9},{12,10},{13,11},... | collective-permute-start | bytes 196616 | tf_op jit(solution)/shard_map/ppermute | solution.py:721
  20.8 6.2 %collective-permute-start.4 = (f32[128,128]{1,0:T(8,128)}, f32[128,128]{1,0:T(8,128)S(1)}, u32[]{:S(2)}, u32[]{:S(2)}) collective-permute-start(f32[128,128]{1,0:T(8,128)} %get-tuple-element.40), channel_id=1, source_target_pairs={{0,8},{8,16},{16,24},{1,9},{9,17},{17,25},{2,10},{10,18},{18,26},{... | collective-permute-start | bytes 196616 | tf_op jit(solution)/shard_map/ppermute | solution.py:721
  23.9 5.2 %collective-permute-start.5 = (f32[128,128]{1,0:T(8,128)}, f32[128,128]{1,0:T(8,128)S(1)}, u32[]{:S(2)}, u32[]{:S(2)}) collective-permute-start(f32[128,128]{1,0:T(8,128)} %get-tuple-element.41), channel_id=1, source_target_pairs={{8,0},{16,8},{24,16},{9,1},{17,9},{25,17},{10,2},{18,10},{26,18},{... | collective-permute-start | bytes 196616 | tf_op jit(solution)/shard_map/ppermute | solution.py:721
  29.1 1.0 copy-start.2
  30.2 1.0 copy-start.4
  31.2 6.5 %copy-start.12 = (s32[1024]{0:T(1024)S(1)}, s32[1024]{0:T(1024)}, u32[]{:S(2)}) copy-start(s32[1024]{0:T(1024)} %param.20) | copy-start | bytes 12292
  31.2 6.5 %copy-start.13 = (s32[1024]{0:T(1024)S(1)}, s32[1024]{0:T(1024)}, u32[]{:S(2)}) copy-start(s32[1024]{0:T(1024)} %param.19) | copy-start | bytes 12292
  31.2 6.5 %copy-start.6 = (f32[256,4,128]{2,1,0:T(4,128)S(1)}, f32[256,4,128]{2,1,0:T(4,128)}, u32[]{:S(2)}) copy-start(f32[256,4,128]{2,1,0:T(4,128)} %get-tuple-element.34) | copy-start | bytes 1572868
  31.2 6.5 %copy-start.8 = (f32[128,128]{1,0:T(8,128)S(1)}, f32[128,128]{1,0:T(8,128)}, u32[]{:S(2)}) copy-start(f32[128,128]{1,0:T(8,128)} %get-tuple-element.42.refs_0_) | copy-start | bytes 196612
  31.4 128.4 %collective-permute-start.6 = (f32[14,48,256]{2,1,0:T(8,128)S(1)}, f32[14,48,256]{2,1,0:T(8,128)S(1)}, u32[]{:S(2)}, u32[]{:S(2)}) collective-permute-start(f32[14,48,256]{2,1,0:T(8,128)S(1)} %get-tuple-element.53), channel_id=1, source_target_pairs={{0,8},{8,16},{16,24},{1,9},{9,17},{17,25},{2,10},{10,18},{18,26},{... | collective-permute-start | bytes 2064392 | tf_op jit(solution)/shard_map/ppermute | solution.py:721
  33.4 129.5 %collective-permute-start.7 = (f32[14,48,256]{2,1,0:T(8,128)S(1)}, f32[14,48,256]{2,1,0:T(8,128)S(1)}, u32[]{:S(2)}, u32[]{:S(2)}) collective-permute-start(f32[14,48,256]{2,1,0:T(8,128)S(1)} %get-tuple-element.54), channel_id=1, source_target_pairs={{8,0},{16,8},{24,16},{9,1},{17,9},{25,17},{10,2},{18,10},{26,18},{... | collective-permute-start | bytes 2064392 | tf_op jit(solution)/shard_map/ppermute | solution.py:721
  37.7 0.7 copy-start.10
  38.4 129.1 %copy-start.3 = (f32[16,32,256]{2,1,0:T(8,128)S(1)}, f32[16,32,256]{2,1,0:T(8,128)}, u32[]{:S(2)}) copy-start(f32[16,32,256]{2,1,0:T(8,128)} %get-tuple-element.51.refs_1_.refs_3_) | copy-start | bytes 1572868
  38.4 129.1 %copy-start.5 = (f32[16,32,256]{2,1,0:T(8,128)S(1)}, f32[16,32,256]{2,1,0:T(8,128)}, u32[]{:S(2)}) copy-start(f32[16,32,256]{2,1,0:T(8,128)} %get-tuple-element.52.refs_2_.refs_4_) | copy-start | bytes 1572868
  38.4 129.1 %copy-start.7 = (f32[256,128]{1,0:T(8,128)S(1)}, f32[256,128]{1,0:T(8,128)}, u32[]{:S(2)}) copy-start(f32[256,128]{1,0:T(8,128)} %get-tuple-element.50.refs_1_) | copy-start | bytes 393220
  147.6 10.1 %collective-permute-start.13 = (f32[128,128]{1,0:T(8,128)S(1)}, f32[128,128]{1,0:T(8,128)S(1)}, u32[]{:S(2)}, u32[]{:S(2)}) collective-permute-start(f32[128,128]{1,0:T(8,128)S(1)} %get-tuple-element.62), channel_id=1, source_target_pairs={{0,8},{8,16},{16,24},{1,9},{9,17},{17,25},{2,10},{10,18},{18,26},{... | collective-permute-start | bytes 196616 | tf_op jit(solution)/shard_map/ppermute | solution.py:721
  149.5 36.7 %collective-permute-start.8 = (f32[128,128]{1,0:T(8,128)S(1)}, f32[128,128]{1,0:T(8,128)S(1)}, u32[]{:S(2)}, u32[]{:S(2)}) collective-permute-start(f32[128,128]{1,0:T(8,128)S(1)} %get-tuple-element.57), channel_id=1, source_target_pairs={{1,0},{2,1},{3,2},{4,3},{5,4},{6,5},{7,6},{9,8},{10,9},{11,10},{12... | collective-permute-start | bytes 196616 | tf_op jit(solution)/shard_map/ppermute | solution.py:721
  154.5 31.7 %collective-permute-start.9 = (f32[128,128]{1,0:T(8,128)S(1)}, f32[128,128]{1,0:T(8,128)S(1)}, u32[]{:S(2)}, u32[]{:S(2)}) collective-permute-start(f32[128,128]{1,0:T(8,128)S(1)} %get-tuple-element.58), channel_id=1, source_target_pairs={{0,1},{1,2},{2,3},{3,4},{4,5},{5,6},{6,7},{8,9},{9,10},{10,11},{11... | collective-permute-start | bytes 196616 | tf_op jit(solution)/shard_map/ppermute | solution.py:721
  157.7 28.6 %collective-permute-start.10 = (f32[128,128]{1,0:T(8,128)S(1)}, f32[128,128]{1,0:T(8,128)S(1)}, u32[]{:S(2)}, u32[]{:S(2)}) collective-permute-start(f32[128,128]{1,0:T(8,128)S(1)} %get-tuple-element.59), channel_id=1, source_target_pairs={{2,0},{3,1},{4,2},{5,3},{6,4},{7,5},{10,8},{11,9},{12,10},{13,11},... | collective-permute-start | bytes 196616 | tf_op jit(solution)/shard_map/ppermute | solution.py:721
  159.8 26.5 %collective-permute-start.11 = (f32[128,128]{1,0:T(8,128)S(1)}, f32[128,128]{1,0:T(8,128)S(1)}, u32[]{:S(2)}, u32[]{:S(2)}) collective-permute-start(f32[128,128]{1,0:T(8,128)S(1)} %get-tuple-element.60), channel_id=1, source_target_pairs={{0,2},{1,3},{2,4},{3,5},{4,6},{5,7},{8,10},{9,11},{10,12},{11,13},... | collective-permute-start | bytes 196616 | tf_op jit(solution)/shard_map/ppermute | solution.py:721
  163.0 4.6 %copy-start.11 = (s32[256]{0:T(256)S(1)}, s32[256]{0:T(256)}, u32[]{:S(2)}) copy-start(s32[256]{0:T(256)} %refs_0_.3) | copy-start | bytes 3076
  163.0 23.3 %collective-permute-start.12 = (f32[128,128]{1,0:T(8,128)S(1)}, f32[128,128]{1,0:T(8,128)S(1)}, u32[]{:S(2)}, u32[]{:S(2)}) collective-permute-start(f32[128,128]{1,0:T(8,128)S(1)} %get-tuple-element.61), channel_id=1, source_target_pairs={{8,0},{16,8},{24,16},{9,1},{17,9},{25,17},{10,2},{18,10},{26,18},{... | collective-permute-start | bytes 196616 | tf_op jit(solution)/shard_map/ppermute | solution.py:721
  186.3 0.7 copy-start.9

commit v6 on v5

--- a/solution.py
+++ b/solution.py
@@ -43,7 +43,7 @@
 
 
 def pair_kernel(own_rows_ref, other_rows_ref, own_ref, *refs):
-    sources = (len(refs) - 10) // 2
+    sources = (len(refs) - 12) // 2
     other_refs = refs[:sources]
     own_out_ref = refs[sources]
     other_out_refs = refs[sources + 1 : 2 * sources + 1]
@@ -55,8 +55,7 @@
         own_sum_ref,
         other_sum_ref,
         stage_ref,
-        dist_ref,
-        weight_ref,
+        *passed_refs,
     ) = refs[2 * sources + 1 :]
     clusters = own_ref.shape[0] // 4
     slots = other_out_refs[0].shape[0] // 4
@@ -132,8 +131,9 @@
     for source in range(sources):
         lax.fori_loop(0, slots // 8, functools.partial(far_rows, source), 0)
     other_sum_ref[...] = jnp.zeros_like(other_sum_ref)
-    dist_ref[...] = jnp.full(dist_ref.shape, 1e38, jnp.float32)
-    weight_ref[...] = jnp.zeros_like(weight_ref)
+    dist_refs, weight_refs = (passed_refs[:2], passed_refs[2:])
+    dist_refs[0][...] = jnp.full(dist_refs[0].shape, 1e38, jnp.float32)
+    weight_refs[0][...] = jnp.zeros_like(weight_refs[0])
 
     lane = lax.broadcasted_iota(jnp.int32, (128, 128), 1)
     quarter = lax.shift_right_logical(lane, 5)
@@ -154,7 +154,7 @@
         ]
         return jnp.concatenate(lines, axis=0)
 
-    def distances(pair, unit):
+    def distances(pair, unit, dist_ref):
         near = None
         far = []
         for turn in range(QUAD):
@@ -164,7 +164,7 @@
             far.append(far_ref[pl.ds(at, 32), :])
         dist_ref[unit] = jnp.dot(near, block_diagonal(far), preferred_element_type=jnp.float32)
 
-    def weights(unit, turn):
+    def weights(unit, turn, dist_ref, weight_ref):
         root = lax.rsqrt(dist_ref[unit, :, 128 * turn : 128 * turn + 128])
         weight = root * root * root
         high = weight.astype(jnp.bfloat16)
@@ -173,7 +173,7 @@
             weight - high.astype(jnp.float32)
         ).astype(jnp.bfloat16)
 
-    def products(pair, unit):
+    def products(pair, unit, weight_ref):
         owns = [own_rows_ref[pair + turn] for turn in range(QUAD)]
         others = [other_rows_ref[pair + turn] for turn in range(QUAD)]
         both = weight_ref[unit]
@@ -196,24 +196,28 @@
         to_other = jnp.dot(rows, both, preferred_element_type=jnp.float32)
         return (owns, others, to_own[:128] + to_own[128:], to_other[:, :128] + to_other[:, 128:])
 
-    def visit(step, _):
+    def half_step(step, side):
         last = jnp.maximum(step - 2, 0) * UNROLL
         first = jnp.minimum(step, groups - 1) * UNROLL
-        results = [products(last + QUAD * unit, unit) for unit in range(units)]
+        results = [products(last + QUAD * unit, unit, weight_refs[side]) for unit in range(units)]
         for unit in range(units):
             for turn in range(QUAD):
-                weights(unit, turn)
+                weights(unit, turn, dist_refs[side], weight_refs[1 - side])
         for unit in range(units):
-            distances(first + QUAD * unit, unit)
+            distances(first + QUAD * unit, unit, dist_refs[1 - side])
         for owns, others, to_own, to_other in results:
             for turn in range(QUAD):
                 own_at = pl.ds(pl.multiple_of(owns[turn] * 128, 128), 128)
                 other_at = pl.ds(pl.multiple_of(others[turn] * 16, 16), 16)
                 own_sum_ref[own_at, :] += jnp.where(quarter == turn, to_own, 0.0)
                 other_sum_ref[other_at, :] += to_other[16 * turn : 16 * turn + 16]
-        return 0
-
-    lax.fori_loop(0, groups + 2, visit, 0)
+
+    def visit(step, _):
+        for side in range(2):
+            half_step(step * 2 + side, side)
+        return 0
+
+    lax.fori_loop(0, (groups + 2) // 2, visit, 0)
 
     def finish(data_ref, out_ref, start, rows_ref, base, stride):
         *comps, charge = components(data_ref, start)
@@ -283,8 +287,8 @@
             pltpu.VMEM((clusters * 128, 128), jnp.float32),
             pltpu.VMEM((others * 16, 128), jnp.float32),
             pltpu.VMEM((384, 128), jnp.float32),
-            pltpu.VMEM((UNROLL // QUAD, 128, 128 * QUAD), jnp.float32),
-            pltpu.VMEM((UNROLL // QUAD, 128 * QUAD, 256), jnp.bfloat16),
+            *[pltpu.VMEM((UNROLL // QUAD, 128, 128 * QUAD), jnp.float32)] * 2,
+            *[pltpu.VMEM((UNROLL // QUAD, 128 * QUAD, 256), jnp.bfloat16)] * 2,
         ],
         compiler_params=pltpu.CompilerParams(vmem_limit_bytes=46 * 1024 * 1024),
         cost_estimate=pl.CostEstimate(

time: 190 us -> 186 us (0.979)
  Pallas kernels: 140 us -> 136 us
    pallas_call x1, Pallas kernels: 109 us -> 105 us  [pair_forces(): pl.pallas_call(pair_kernel, out_shape=(jax.ShapeDtypeStruct(own.shape, jn...]
where the time goes in v6:
time: 186 us
  Pallas kernels  136 us (73%)
  starting transfers between devices  43.3 us (23%)
  local copies, waits for them, and re-layouts  3.45 us (2%)
  waiting for transfers between devices  2.16 us (1%)
    pallas_call x1, Pallas kernels, pair_forces(): pl.pallas_call(pair_kernel, out_shape=(jax.ShapeDtypeStruct(own.shape, jn...  105 us
    ppermute x14, starting transfers between devices, passed_along(): return lax.ppermute(shard, axis, pairs)  43.3 us
    pallas_call x1, Pallas kernels, grid_step(): pl.pallas_call(functools.partial(grid_kernel, base), out_shape=(jax.Shape...  18.7 us
    pallas_call x1, Pallas kernels, prepare(): pl.pallas_call(prepare_kernel, out_shape=(jax.ShapeDtypeStruct((clusters,...  9.1 us
  transfers between devices with their start and end apart: 14, of which 1 were waited for; matrix products, arithmetic and copies ran while one was open for 0% of the time, Pallas kernels for 67%

profile of v6, /device:TPU:13, one launch (start us, length us, event | category | flops | bytes accessed | tf_op | source)
XLA Modules:
  0.0 185.5 jit_solution(937105727808713257)
XLA Ops:
  0.6 0.0 copy-start
  0.6 0.0 copy-start.1
  0.7 9.1 %prepare.1 = (f32[256,4,128]{2,1,0:T(4,128)}, f32[256,128]{1,0:T(8,128)}, f32[16,32,256]{2,1,0:T(8,128)}, f32[16,32,256]{2,1,0:T(8,128)}, f32[128,128]{1,0:T(8,1...) custom-call(s32[256]{0:T(256)} %fill_ref.1, ...), custom_call_target="tpu_custom_call" | custom-call | tf_op jit(solution)/shard_map/prepare/pallas_call | solution.py:421
  9.8 3.8 %collective-permute-start = (f32[640,128]{1,0:T(8,128)}, f32[640,128]{1,0:T(8,128)S(1)}, u32[]{:S(2)}, u32[]{:S(2)}) collective-permute-start(f32[640,128]{1,0:T(8,128)} %get-tuple-element.36), channel_id=1, source_target_pairs={{0,1},{1,2},{2,3},{3,4},{4,5},{5,6},{6,7},{8,9},{9,10},{10,11},{11... | collective-permute-start | bytes 983048 | tf_op jit(solution)/shard_map/ppermute | solution.py:725
  13.5 1.9 %collective-permute-start.1 = (f32[640,128]{1,0:T(8,128)}, f32[640,128]{1,0:T(8,128)S(1)}, u32[]{:S(2)}, u32[]{:S(2)}) collective-permute-start(f32[640,128]{1,0:T(8,128)} %get-tuple-element.37), channel_id=1, source_target_pairs={{1,0},{2,1},{3,2},{4,3},{5,4},{6,5},{7,6},{9,8},{10,9},{11,10},{12... | collective-permute-start | bytes 983048 | tf_op jit(solution)/shard_map/ppermute | solution.py:725
  15.5 3.2 %collective-permute-start.2 = (f32[128,128]{1,0:T(8,128)}, f32[128,128]{1,0:T(8,128)S(1)}, u32[]{:S(2)}, u32[]{:S(2)}) collective-permute-start(f32[128,128]{1,0:T(8,128)} %get-tuple-element.38), channel_id=1, source_target_pairs={{0,2},{1,3},{2,4},{3,5},{4,6},{5,7},{8,10},{9,11},{10,12},{11,13},... | collective-permute-start | bytes 196616 | tf_op jit(solution)/shard_map/ppermute | solution.py:725
  18.7 2.1 %collective-permute-start.3 = (f32[128,128]{1,0:T(8,128)}, f32[128,128]{1,0:T(8,128)S(1)}, u32[]{:S(2)}, u32[]{:S(2)}) collective-permute-start(f32[128,128]{1,0:T(8,128)} %get-tuple-element.39), channel_id=1, source_target_pairs={{2,0},{3,1},{4,2},{5,3},{6,4},{7,5},{10,8},{11,9},{12,10},{13,11},... | collective-permute-start | bytes 196616 | tf_op jit(solution)/shard_map/ppermute | solution.py:725
  20.8 3.1 %collective-permute-start.4 = (f32[128,128]{1,0:T(8,128)}, f32[128,128]{1,0:T(8,128)S(1)}, u32[]{:S(2)}, u32[]{:S(2)}) collective-permute-start(f32[128,128]{1,0:T(8,128)} %get-tuple-element.40), channel_id=1, source_target_pairs={{0,8},{8,16},{16,24},{1,9},{9,17},{17,25},{2,10},{10,18},{18,26},{... | collective-permute-start | bytes 196616 | tf_op jit(solution)/shard_map/ppermute | solution.py:725
  23.9 0.0 collective-permute-done.2.refs_3_
  23.9 3.1 %collective-permute-start.5 = (f32[128,128]{1,0:T(8,128)}, f32[128,128]{1,0:T(8,128)S(1)}, u32[]{:S(2)}, u32[]{:S(2)}) collective-permute-start(f32[128,128]{1,0:T(8,128)} %get-tuple-element.41), channel_id=1, source_target_pairs={{8,0},{16,8},{24,16},{9,1},{17,9},{25,17},{10,2},{18,10},{26,18},{... | collective-permute-start | bytes 196616 | tf_op jit(solution)/shard_map/ppermute | solution.py:725
  27.0 0.0 collective-permute-done.3.refs_4_
  27.0 0.0 collective-permute-done.4.refs_5_
  27.0 2.1 %collective-permute-done.5.refs_6_ = f32[128,128]{1,0:T(8,128)S(1)} collective-permute-done((f32[128,128]{1,0:T(8,128)}, f32[128,128]{1,0:T(8,128)S(1)}, u32[]{:S(2)}, u32[]{:S(2)}) %collective-permute-start.5) | collective-permute-done | bytes 65568 | tf_op jit(solution)/shard_map/ppermute | solution.py:725
  29.1 0.0 collective-permute-done.refs_1_.refs_4_.refs_6_
  29.1 0.0 collective-permute-done.1.refs_2_.refs_5_.refs_7_
  29.1 0.0 copy-done
  29.1 0.0 copy-done.1
  29.1 0.0 copy-start.2
  29.2 1.0 copy-done.2
  30.2 0.0 copy-start.4
  30.2 1.0 copy-done.4
  31.2 0.0 copy-start.12
  31.2 0.0 copy-start.13
  31.2 0.0 copy-start.6
  31.2 0.0 copy-start.8
  31.2 0.1 planes.1
  31.4 2.1 %collective-permute-start.6 = (f32[14,48,256]{2,1,0:T(8,128)S(1)}, f32[14,48,256]{2,1,0:T(8,128)S(1)}, u32[]{:S(2)}, u32[]{:S(2)}) collective-permute-start(f32[14,48,256]{2,1,0:T(8,128)S(1)} %get-tuple-element.53), channel_id=1, source_target_pairs={{0,8},{8,16},{16,24},{1,9},{9,17},{17,25},{2,10},{10,18},{18,26},{... | collective-permute-start | bytes 2064392 | tf_op jit(solution)/shard_map/ppermute | solution.py:725
  33.4 4.3 %collective-permute-start.7 = (f32[14,48,256]{2,1,0:T(8,128)S(1)}, f32[14,48,256]{2,1,0:T(8,128)S(1)}, u32[]{:S(2)}, u32[]{:S(2)}) collective-permute-start(f32[14,48,256]{2,1,0:T(8,128)S(1)} %get-tuple-element.54), channel_id=1, source_target_pairs={{8,0},{16,8},{24,16},{9,1},{17,9},{25,17},{10,2},{18,10},{26,18},{... | collective-permute-start | bytes 2064392 | tf_op jit(solution)/shard_map/ppermute | solution.py:725
  37.7 0.0 copy-done.12
  37.7 0.0 copy-done.13
  37.7 0.0 copy-start.10
  37.8 0.0 copy-done.6
  37.8 0.0 copy-done.8
  37.8 0.6 copy-done.10
  38.4 0.0 copy-start.3
  38.4 0.0 copy-start.5
  38.4 0.0 copy-start.7
  38.4 104.9 %pair_forces.1 = (f32[1024,128]{1,0:T(8,128)S(1)}, f32[128,128]{1,0:T(8,128)S(1)}, f32[128,128]{1,0:T(8,128)S(1)}, f32[128,128]{1,0:T(8,128)S(1)}, f32[128,128]{...) custom-call(s32[1024]{0:T(1024)S(1)} %copy-done.10, ...), custom_call_target="tpu_custom_call" | custom-call | flops 335544320 | bytes 4194304 | tf_op jit(solution)/shard_map/pair_forces/pallas_call | solution.py:274
  143.3 1.9 %collective-permute-start.13 = (f32[128,128]{1,0:T(8,128)S(1)}, f32[128,128]{1,0:T(8,128)S(1)}, u32[]{:S(2)}, u32[]{:S(2)}) collective-permute-start(f32[128,128]{1,0:T(8,128)S(1)} %get-tuple-element.62), channel_id=1, source_target_pairs={{0,8},{8,16},{16,24},{1,9},{9,17},{17,25},{2,10},{10,18},{18,26},{... | collective-permute-start | bytes 196616 | tf_op jit(solution)/shard_map/ppermute | solution.py:725
  145.3 5.0 %collective-permute-start.8 = (f32[128,128]{1,0:T(8,128)S(1)}, f32[128,128]{1,0:T(8,128)S(1)}, u32[]{:S(2)}, u32[]{:S(2)}) collective-permute-start(f32[128,128]{1,0:T(8,128)S(1)} %get-tuple-element.57), channel_id=1, source_target_pairs={{1,0},{2,1},{3,2},{4,3},{5,4},{6,5},{7,6},{9,8},{10,9},{11,10},{12... | collective-permute-start | bytes 196616 | tf_op jit(solution)/shard_map/ppermute | solution.py:725
  150.3 3.1 %collective-permute-start.9 = (f32[128,128]{1,0:T(8,128)S(1)}, f32[128,128]{1,0:T(8,128)S(1)}, u32[]{:S(2)}, u32[]{:S(2)}) collective-permute-start(f32[128,128]{1,0:T(8,128)S(1)} %get-tuple-element.58), channel_id=1, source_target_pairs={{0,1},{1,2},{2,3},{3,4},{4,5},{5,6},{6,7},{8,9},{9,10},{10,11},{11... | collective-permute-start | bytes 196616 | tf_op jit(solution)/shard_map/ppermute | solution.py:725
  153.4 0.0 collective-permute-done.13
  153.4 2.1 %collective-permute-start.10 = (f32[128,128]{1,0:T(8,128)S(1)}, f32[128,128]{1,0:T(8,128)S(1)}, u32[]{:S(2)}, u32[]{:S(2)}) collective-permute-start(f32[128,128]{1,0:T(8,128)S(1)} %get-tuple-element.59), channel_id=1, source_target_pairs={{2,0},{3,1},{4,2},{5,3},{6,4},{7,5},{10,8},{11,9},{12,10},{13,11},... | collective-permute-start | bytes 196616 | tf_op jit(solution)/shard_map/ppermute | solution.py:725
  155.5 0.0 collective-permute-done.6.refs_8_
  155.5 3.2 %collective-permute-start.11 = (f32[128,128]{1,0:T(8,128)S(1)}, f32[128,128]{1,0:T(8,128)S(1)}, u32[]{:S(2)}, u32[]{:S(2)}) collective-permute-start(f32[128,128]{1,0:T(8,128)S(1)} %get-tuple-element.60), channel_id=1, source_target_pairs={{0,2},{1,3},{2,4},{3,5},{4,6},{5,7},{8,10},{9,11},{10,12},{11,13},... | collective-permute-start | bytes 196616 | tf_op jit(solution)/shard_map/ppermute | solution.py:725
  158.7 0.0 collective-permute-done.7.refs_9_
  158.7 0.0 copy-start.11
  158.8 4.5 %collective-permute-start.12 = (f32[128,128]{1,0:T(8,128)S(1)}, f32[128,128]{1,0:T(8,128)S(1)}, u32[]{:S(2)}, u32[]{:S(2)}) collective-permute-start(f32[128,128]{1,0:T(8,128)S(1)} %get-tuple-element.61), channel_id=1, source_target_pairs={{8,0},{16,8},{24,16},{9,1},{17,9},{25,17},{10,2},{18,10},{26,18},{... | collective-permute-start | bytes 196616 | tf_op jit(solution)/shard_map/ppermute | solution.py:725
  163.3 0.0 copy-done.3
  163.3 0.0 copy-done.5
  163.3 0.0 copy-done.7
  163.3 0.0 copy-done.11
  163.3 18.7 %grid_step.1 = (f32[16,32,256]{2,1,0:T(8,128)}, f32[16,32,256]{2,1,0:T(8,128)}, f32[1024,128]{1,0:T(8,128)S(1)}) custom-call(s32[256]{0:T(256)S(1)} %copy-done.11, f32[256,128]{1,0:T(8,128)S(1)} %copy-done.7, f32[16,32,256]{2,1,0:T(8,128)S(1)} %copy-done.1, f32[16,32,256]{2,1,0:T(8,128)S(1)} %copy-done.3, f32[16,32,256]{2,1,0:T(8,128)S(1)} %copy-done.5, ...), custom_call_target="tpu_custom_call" | custom-call | flops 31948800 | bytes 8388608 | tf_op jit(solution)/shard_map/grid_step/pallas_call | solution.py:664
  182.0 0.0 collective-permute-done.8
  182.0 0.0 collective-permute-done.9
  182.0 0.0 collective-permute-done.10
  182.0 0.0 collective-permute-done.11
  182.0 0.0 collective-permute-done.12
  182.0 0.0 copy-start.9
  182.1 0.7 copy-done.9
  182.7 2.8 %gather_forces.1 = f32[3,32768]{1,0:T(4,128)} custom-call(s32[7,32]{1,0:T(8,128)S(1)} %copy-done.9, f32[256,4,128]{2,1,0:T(4,128)S(1)} %bitcast.12, f32[256,4,128]{2,1,0:T(4,128)S(1)} %bitcast.13, f32[32,4,128]{2,1,0:T(4,128)S(1)} %bitcast.14, f32[32,4,128]{2,1,0:T(4,128)S(1)} %bitcast.16, f32[32,4,128]{2,1,0:T(4,128)S(1)} %bitcast.17, ...), custom_call_target="tpu_custom_call" | custom-call | tf_op jit(solution)/shard_map/gather_forces/pallas_call | solution.py:711
  (1 shorter events, 0.0 us)
Async XLA Ops:
  0.6 28.5 %copy-start = (f32[16,32,256]{2,1,0:T(8,128)S(1)}, f32[16,32,256]{2,1,0:T(8,128)}, u32[]{:S(2)}) copy-start(f32[16,32,256]{2,1,0:T(8,128)} %refs_5_.1) | copy-start | bytes 1572868
  0.6 28.5 %copy-start.1 = (f32[16,32,256]{2,1,0:T(8,128)S(1)}, f32[16,32,256]{2,1,0:T(8,128)}, u32[]{:S(2)}) copy-start(f32[16,32,256]{2,1,0:T(8,128)} %refs_2_.1) | copy-start | bytes 1572868
  9.8 19.4 %collective-permute-start = (f32[640,128]{1,0:T(8,128)}, f32[640,128]{1,0:T(8,128)S(1)}, u32[]{:S(2)}, u32[]{:S(2)}) collective-permute-start(f32[640,128]{1,0:T(8,128)} %get-tuple-element.36), channel_id=1, source_target_pairs={{0,1},{1,2},{2,3},{3,4},{4,5},{5,6},{6,7},{8,9},{9,10},{10,11},{11... | collective-permute-start | bytes 983048 | tf_op jit(solution)/shard_map/ppermute | solution.py:725
  13.5 15.6 %collective-permute-start.1 = (f32[640,128]{1,0:T(8,128)}, f32[640,128]{1,0:T(8,128)S(1)}, u32[]{:S(2)}, u32[]{:S(2)}) collective-permute-start(f32[640,128]{1,0:T(8,128)} %get-tuple-element.37), channel_id=1, source_target_pairs={{1,0},{2,1},{3,2},{4,3},{5,4},{6,5},{7,6},{9,8},{10,9},{11,10},{12... | collective-permute-start | bytes 983048 | tf_op jit(solution)/shard_map/ppermute | solution.py:725
  15.5 8.4 %collective-permute-start.2 = (f32[128,128]{1,0:T(8,128)}, f32[128,128]{1,0:T(8,128)S(1)}, u32[]{:S(2)}, u32[]{:S(2)}) collective-permute-start(f32[128,128]{1,0:T(8,128)} %get-tuple-element.38), channel_id=1, source_target_pairs={{0,2},{1,3},{2,4},{3,5},{4,6},{5,7},{8,10},{9,11},{10,12},{11,13},... | collective-permute-start | bytes 196616 | tf_op jit(solution)/shard_map/ppermute | solution.py:725
  18.7 8.3 %collective-permute-start.3 = (f32[128,128]{1,0:T(8,128)}, f32[128,128]{1,0:T(8,128)S(1)}, u32[]{:S(2)}, u32[]{:S(2)}) collective-permute-start(f32[128,128]{1,0:T(8,128)} %get-tuple-element.39), channel_id=1, source_target_pairs={{2,0},{3,1},{4,2},{5,3},{6,4},{7,5},{10,8},{11,9},{12,10},{13,11},... | collective-permute-start | bytes 196616 | tf_op jit(solution)/shard_map/ppermute | solution.py:725
  20.8 6.2 %collective-permute-start.4 = (f32[128,128]{1,0:T(8,128)}, f32[128,128]{1,0:T(8,128)S(1)}, u32[]{:S(2)}, u32[]{:S(2)}) collective-permute-start(f32[128,128]{1,0:T(8,128)} %get-tuple-element.40), channel_id=1, source_target_pairs={{0,8},{8,16},{16,24},{1,9},{9,17},{17,25},{2,10},{10,18},{18,26},{... | collective-permute-start | bytes 196616 | tf_op jit(solution)/shard_map/ppermute | solution.py:725
  23.9 5.2 %collective-permute-start.5 = (f32[128,128]{1,0:T(8,128)}, f32[128,128]{1,0:T(8,128)S(1)}, u32[]{:S(2)}, u32[]{:S(2)}) collective-permute-start(f32[128,128]{1,0:T(8,128)} %get-tuple-element.41), channel_id=1, source_target_pairs={{8,0},{16,8},{24,16},{9,1},{17,9},{25,17},{10,2},{18,10},{26,18},{... | collective-permute-start | bytes 196616 | tf_op jit(solution)/shard_map/ppermute | solution.py:725
  29.1 1.0 copy-start.2
  30.2 1.0 copy-start.4
  31.2 6.5 %copy-start.12 = (s32[1024]{0:T(1024)S(1)}, s32[1024]{0:T(1024)}, u32[]{:S(2)}) copy-start(s32[1024]{0:T(1024)} %param.20) | copy-start | bytes 12292
  31.2 6.5 %copy-start.13 = (s32[1024]{0:T(1024)S(1)}, s32[1024]{0:T(1024)}, u32[]{:S(2)}) copy-start(s32[1024]{0:T(1024)} %param.19) | copy-start | bytes 12292
  31.2 6.5 %copy-start.6 = (f32[256,4,128]{2,1,0:T(4,128)S(1)}, f32[256,4,128]{2,1,0:T(4,128)}, u32[]{:S(2)}) copy-start(f32[256,4,128]{2,1,0:T(4,128)} %get-tuple-element.34) | copy-start | bytes 1572868
  31.2 6.5 %copy-start.8 = (f32[128,128]{1,0:T(8,128)S(1)}, f32[128,128]{1,0:T(8,128)}, u32[]{:S(2)}) copy-start(f32[128,128]{1,0:T(8,128)} %get-tuple-element.42.refs_0_) | copy-start | bytes 196612
  31.4 124.1 %collective-permute-start.6 = (f32[14,48,256]{2,1,0:T(8,128)S(1)}, f32[14,48,256]{2,1,0:T(8,128)S(1)}, u32[]{:S(2)}, u32[]{:S(2)}) collective-permute-start(f32[14,48,256]{2,1,0:T(8,128)S(1)} %get-tuple-element.53), channel_id=1, source_target_pairs={{0,8},{8,16},{16,24},{1,9},{9,17},{17,25},{2,10},{10,18},{18,26},{... | collective-permute-start | bytes 2064392 | tf_op jit(solution)/shard_map/ppermute | solution.py:725
  33.4 125.3 %collective-permute-start.7 = (f32[14,48,256]{2,1,0:T(8,128)S(1)}, f32[14,48,256]{2,1,0:T(8,128)S(1)}, u32[]{:S(2)}, u32[]{:S(2)}) collective-permute-start(f32[14,48,256]{2,1,0:T(8,128)S(1)} %get-tuple-element.54), channel_id=1, source_target_pairs={{8,0},{16,8},{24,16},{9,1},{17,9},{25,17},{10,2},{18,10},{26,18},{... | collective-permute-start | bytes 2064392 | tf_op jit(solution)/shard_map/ppermute | solution.py:725
  37.7 0.7 copy-start.10
  38.4 124.9 %copy-start.3 = (f32[16,32,256]{2,1,0:T(8,128)S(1)}, f32[16,32,256]{2,1,0:T(8,128)}, u32[]{:S(2)}) copy-start(f32[16,32,256]{2,1,0:T(8,128)} %get-tuple-element.51.refs_1_.refs_3_) | copy-start | bytes 1572868
  38.4 124.9 %copy-start.5 = (f32[16,32,256]{2,1,0:T(8,128)S(1)}, f32[16,32,256]{2,1,0:T(8,128)}, u32[]{:S(2)}) copy-start(f32[16,32,256]{2,1,0:T(8,128)} %get-tuple-element.52.refs_2_.refs_4_) | copy-start | bytes 1572868
  38.4 124.9 %copy-start.7 = (f32[256,128]{1,0:T(8,128)S(1)}, f32[256,128]{1,0:T(8,128)}, u32[]{:S(2)}) copy-start(f32[256,128]{1,0:T(8,128)} %get-tuple-element.50.refs_1_) | copy-start | bytes 393220
  143.3 10.1 %collective-permute-start.13 = (f32[128,128]{1,0:T(8,128)S(1)}, f32[128,128]{1,0:T(8,128)S(1)}, u32[]{:S(2)}, u32[]{:S(2)}) collective-permute-start(f32[128,128]{1,0:T(8,128)S(1)} %get-tuple-element.62), channel_id=1, source_target_pairs={{0,8},{8,16},{16,24},{1,9},{9,17},{17,25},{2,10},{10,18},{18,26},{... | collective-permute-start | bytes 196616 | tf_op jit(solution)/shard_map/ppermute | solution.py:725
  145.3 36.8 %collective-permute-start.8 = (f32[128,128]{1,0:T(8,128)S(1)}, f32[128,128]{1,0:T(8,128)S(1)}, u32[]{:S(2)}, u32[]{:S(2)}) collective-permute-start(f32[128,128]{1,0:T(8,128)S(1)} %get-tuple-element.57), channel_id=1, source_target_pairs={{1,0},{2,1},{3,2},{4,3},{5,4},{6,5},{7,6},{9,8},{10,9},{11,10},{12... | collective-permute-start | bytes 196616 | tf_op jit(solution)/shard_map/ppermute | solution.py:725
  150.3 31.7 %collective-permute-start.9 = (f32[128,128]{1,0:T(8,128)S(1)}, f32[128,128]{1,0:T(8,128)S(1)}, u32[]{:S(2)}, u32[]{:S(2)}) collective-permute-start(f32[128,128]{1,0:T(8,128)S(1)} %get-tuple-element.58), channel_id=1, source_target_pairs={{0,1},{1,2},{2,3},{3,4},{4,5},{5,6},{6,7},{8,9},{9,10},{10,11},{11... | collective-permute-start | bytes 196616 | tf_op jit(solution)/shard_map/ppermute | solution.py:725
  153.4 28.6 %collective-permute-start.10 = (f32[128,128]{1,0:T(8,128)S(1)}, f32[128,128]{1,0:T(8,128)S(1)}, u32[]{:S(2)}, u32[]{:S(2)}) collective-permute-start(f32[128,128]{1,0:T(8,128)S(1)} %get-tuple-element.59), channel_id=1, source_target_pairs={{2,0},{3,1},{4,2},{5,3},{6,4},{7,5},{10,8},{11,9},{12,10},{13,11},... | collective-permute-start | bytes 196616 | tf_op jit(solution)/shard_map/ppermute | solution.py:725
  155.5 26.5 %collective-permute-start.11 = (f32[128,128]{1,0:T(8,128)S(1)}, f32[128,128]{1,0:T(8,128)S(1)}, u32[]{:S(2)}, u32[]{:S(2)}) collective-permute-start(f32[128,128]{1,0:T(8,128)S(1)} %get-tuple-element.60), channel_id=1, source_target_pairs={{0,2},{1,3},{2,4},{3,5},{4,6},{5,7},{8,10},{9,11},{10,12},{11,13},... | collective-permute-start | bytes 196616 | tf_op jit(solution)/shard_map/ppermute | solution.py:725
  158.7 4.6 %copy-start.11 = (s32[256]{0:T(256)S(1)}, s32[256]{0:T(256)}, u32[]{:S(2)}) copy-start(s32[256]{0:T(256)} %refs_0_.3) | copy-start | bytes 3076
  158.8 23.3 %collective-permute-start.12 = (f32[128,128]{1,0:T(8,128)S(1)}, f32[128,128]{1,0:T(8,128)S(1)}, u32[]{:S(2)}, u32[]{:S(2)}) collective-permute-start(f32[128,128]{1,0:T(8,128)S(1)} %get-tuple-element.61), channel_id=1, source_target_pairs={{8,0},{16,8},{24,16},{9,1},{17,9},{25,17},{10,2},{18,10},{26,18},{... | collective-permute-start | bytes 196616 | tf_op jit(solution)/shard_map/ppermute | solution.py:725
  182.0 0.7 copy-start.9

commit v7 on v6

--- a/solution.py
+++ b/solution.py
@@ -2,6 +2,7 @@
 
 import jax
 import jax.numpy as jnp
+import numpy as np
 from jax import lax
 from jax.experimental import pallas as pl
 from jax.experimental.pallas import tpu as pltpu
@@ -34,7 +35,7 @@
     return (first, second, third)
 
 
-def moment_rows(comps, charge):
+def moment_pieces(comps, charge):
     rows = [None] * 12
     for part, charged in enumerate((*comps, None)):
         for level, piece in enumerate(split3(charge if charged is None else charge * charged)):
@@ -42,8 +43,35 @@
     return rows
 
 
-def pair_kernel(own_rows_ref, other_rows_ref, own_ref, *refs):
-    sources = (len(refs) - 12) // 2
+def selections():
+    near_kinds, far_kinds = ([], [])
+    for part in range(3):
+        near_kinds += [3 * part + level for level in (0, 0, 0, 1, 1, 2)]
+        far_kinds += [3 * part + level for level in (0, 1, 2, 0, 1, 0)]
+    near_kinds += [9, 10, 11, 12, 12, 12]
+    far_kinds += [12, 12, 12, 9, 10, 11]
+    near = np.zeros((128, 256), np.float32)
+    far = np.zeros((256, 128), np.float32)
+    own_moment = np.zeros((128, 128), np.float32)
+    other_moment = np.zeros((128, QUAD * 256), np.float32)
+    for cluster in range(8):
+        for index, kind in enumerate(near_kinds):
+            near[kind * 8 + cluster, cluster * 32 + index] = 1.0
+        for index, kind in enumerate(far_kinds):
+            far[cluster * 32 + index, kind * 8 + cluster] = 1.0
+        for kind in range(12):
+            own_moment[cluster * 16 + kind, kind * 8 + cluster] = 1.0
+            for turn in range(QUAD):
+                lane = (cluster % QUAD + turn) % QUAD * 32 + kind
+                column = turn * 256 + cluster // QUAD * 128 + lane
+                other_moment[kind * 8 + cluster, column] = 1.0
+    return tuple(jnp.asarray(part, jnp.bfloat16) for part in (near, far, own_moment, other_moment))
+
+
+def pair_kernel(own_rows_ref, other_rows_ref, *refs):
+    near_sel_ref, far_sel_ref, own_moment_sel_ref, other_moment_sel_ref, own_ref = refs[:5]
+    refs = refs[5:]
+    sources = (len(refs) - 11) // 2
     other_refs = refs[:sources]
     own_out_ref = refs[sources]
     other_out_refs = refs[sources + 1 : 2 * sources + 1]
@@ -54,7 +82,6 @@
         other_moment_ref,
         own_sum_ref,
         other_sum_ref,
-        stage_ref,
         *passed_refs,
     ) = refs[2 * sources + 1 :]
     clusters = own_ref.shape[0] // 4
@@ -62,7 +89,6 @@
     others = slots * sources
     groups = own_rows_ref.shape[0] // UNROLL
     units = UNROLL // QUAD
-    groups_of_own = clusters // QUAD
     groups_of_other = others // QUAD
     ones = jnp.ones((8, 128), jnp.float32)
     zeros = jnp.zeros((8, 128), jnp.float32)
@@ -70,99 +96,91 @@
     def components(data_ref, start):
         return [data_ref[pl.ds(4 * start + part, 8, stride=4), :] for part in range(4)]
 
-    def put(rows, base, stride):
-        for index, row in enumerate(rows):
-            stage_ref[pl.ds(base + index, 8, stride=stride), :] = row
-
-    def put_turned(target_ref, columns, group, groups_in_all):
-        for turn in range(QUAD):
-            rolled = columns if turn == 0 else pltpu.roll(columns, 32 * turn, 1)
-            at = pl.multiple_of((turn * groups_in_all + group) * 128, 128)
-            target_ref[pl.ds(at, 128), :] = rolled.astype(jnp.bfloat16)
+    def place_pieces(comps, factor, offset):
+        pieces = []
+        square = zeros
+        for comp in comps:
+            square = square + comp * comp
+            pieces += split3(factor * comp)
+        pieces += [*split3(square + offset), ones]
+        return jnp.concatenate(pieces + [zeros] * (16 - len(pieces)), axis=0)
+
+    def selected(left, right):
+        return jnp.dot(
+            left.astype(jnp.bfloat16), right, preferred_element_type=jnp.float32
+        ).astype(jnp.bfloat16)
 
     def near_rows(step, _):
         start = pl.multiple_of(step * 8, 8)
         *comps, charge = components(own_ref, start)
-        put(moment_rows(comps, charge) + [zeros] * 4, 256, 16)
-        own_moment_ref[pl.ds(pl.multiple_of(start * 16, 128), 128), :] = stage_ref[
-            256:384, :
-        ].astype(jnp.bfloat16)
-        rows = []
-        square = zeros
-        for comp in comps:
-            first, second, third = split3(comp)
-            square = square + comp * comp
-            rows += [first, first, first, second, second, third]
-        rows += [*split3(square), ones, ones, ones]
-        rows += [zeros] * (32 - len(rows))
-        put(rows, 0, 32)
+        moments = jnp.concatenate(moment_pieces(comps, charge) + [zeros] * 4, axis=0)
+        own_moment_ref[pl.ds(pl.multiple_of(start * 16, 128), 128), :] = selected(
+            own_moment_sel_ref[...], moments.astype(jnp.bfloat16)
+        )
+        tiles = selected(place_pieces(comps, 1.0, 0.0).T, near_sel_ref[...])
         for half in range(2):
-            columns = stage_ref[128 * half : 128 * half + 128, :].T
-            put_turned(near_ref, columns, step * 2 + half, groups_of_own)
-        for index in range(8):
-            at = pl.ds(pl.multiple_of((start + index) * 128, 128), 128)
-            own_sum_ref[at, :] = jnp.zeros((128, 128), jnp.float32)
+            at = pl.ds(pl.multiple_of(step * 256 + half * 128, 128), 128)
+            near_ref[at, :] = tiles[:, 128 * half : 128 * half + 128]
         return 0
 
     def far_rows(source, step, _):
         local = pl.multiple_of(step * 8, 8)
         start = source * slots + local
         *comps, charge = components(other_refs[source], local)
-        moments = moment_rows(comps, charge) + [zeros] * 4
-        put(moments + [zeros] * 16, 0, 32)
-        for half in range(2):
-            columns = stage_ref[128 * half : 128 * half + 128, :].T
-            put_turned(other_moment_ref, columns, (start // 8) * 2 + half, groups_of_other)
-        rows = []
-        square = zeros
-        for comp in comps:
-            first, second, third = split3(-2.0 * comp)
-            square = square + comp * comp
-            rows += [first, second, third, first, second, first]
-        rows += [ones, ones, ones, *split3(square + softening)]
-        rows += [zeros] * (32 - len(rows))
-        put(rows, 0, 32)
-        far_ref[pl.ds(pl.multiple_of(start * 32, 256), 256), :] = stage_ref[0:256, :].astype(
-            jnp.bfloat16
-        )
-        return 0
-
-    lax.fori_loop(0, clusters // 8, near_rows, 0)
+        rows = selected(far_sel_ref[...], place_pieces(comps, -2.0, softening).astype(jnp.bfloat16))
+        for index in range(8):
+            at = pl.multiple_of((start + index) * 128, 128)
+            far_ref[pl.ds(at, 96), :] = jnp.zeros((96, 128), jnp.bfloat16)
+            far_ref[pl.ds(at + 96, 32), :] = rows[32 * index : 32 * index + 32]
+        moments = jnp.concatenate(moment_pieces(comps, charge) + [zeros] * 4, axis=0)
+        tiles = selected(moments.T, other_moment_sel_ref[...])
+        for turn in range(QUAD):
+            for half in range(2):
+                group = turn * groups_of_other + source * (slots // QUAD) + step * 2 + half
+                column = 256 * turn + 128 * half
+                other_moment_ref[pl.ds(pl.multiple_of(group * 128, 128), 128), :] = tiles[
+                    :, column : column + 128
+                ]
+        return 0
+
+    lax.fori_loop(0, clusters // 8, near_rows, 0, unroll=2)
     for source in range(sources):
-        lax.fori_loop(0, slots // 8, functools.partial(far_rows, source), 0)
+        lax.fori_loop(0, slots // 8, functools.partial(far_rows, source), 0, unroll=2)
+    far_ref[pl.ds(others * 128, 128), :] = jnp.zeros((128, 128), jnp.bfloat16)
+    own_sum_ref[...] = jnp.zeros_like(own_sum_ref)
     other_sum_ref[...] = jnp.zeros_like(other_sum_ref)
     dist_refs, weight_refs = (passed_refs[:2], passed_refs[2:])
     dist_refs[0][...] = jnp.full(dist_refs[0].shape, 1e38, jnp.float32)
     weight_refs[0][...] = jnp.zeros_like(weight_refs[0])
 
-    lane = lax.broadcasted_iota(jnp.int32, (128, 128), 1)
-    quarter = lax.shift_right_logical(lane, 5)
     quarter_row = lax.shift_right_logical(lax.broadcasted_iota(jnp.int32, (1, 128), 1), 5)
     masks = [jnp.where(quarter_row == turn, 1.0, 0.0).astype(jnp.bfloat16) for turn in range(QUAD)]
-    empty = jnp.zeros((32, 128), jnp.bfloat16)
-
-    def turned(source_ref, index, turn, groups_in_all):
-        rotation = lax.bitwise_and(turn - index, 3)
-        group = rotation * groups_in_all + lax.shift_right_logical(index, 2)
-        return source_ref[pl.ds(pl.multiple_of(group * 128, 128), 128), :] * masks[turn]
 
     def block_diagonal(blocks):
-        blank = empty[: blocks[0].shape[0]]
+        blank = jnp.zeros_like(blocks[0])
         lines = [
-            jnp.concatenate([block if turn == at else blank for turn in range(QUAD)], axis=1)
+            jnp.concatenate(
+                [block if turn == at else blank for turn in range(len(blocks))], axis=1
+            )
             for at, block in enumerate(blocks)
         ]
         return jnp.concatenate(lines, axis=0)
 
     def distances(pair, unit, dist_ref):
-        near = None
-        far = []
-        for turn in range(QUAD):
-            tile = turned(near_ref, own_rows_ref[pair + turn], turn, groups_of_own)
-            near = tile if near is None else near + tile
-            at = pl.multiple_of(other_rows_ref[pair + turn] * 32, 32)
-            far.append(far_ref[pl.ds(at, 32), :])
-        dist_ref[unit] = jnp.dot(near, block_diagonal(far), preferred_element_type=jnp.float32)
+        for couple in range(QUAD // 2):
+            near, far = ([], [])
+            for turn in range(2):
+                own = own_rows_ref[pair + 2 * couple + turn]
+                other = other_rows_ref[pair + 2 * couple + turn]
+                tile = pl.multiple_of(lax.shift_right_logical(own, 2) * 128, 128)
+                near.append(near_ref[pl.ds(tile, 128), :])
+                first = pl.multiple_of(other * 128 + 96 - lax.bitwise_and(own, 3) * 32, 32)
+                far.append(far_ref[pl.ds(first, 128), :])
+            dist_ref[unit, :, 256 * couple : 256 * couple + 256] = jnp.dot(
+                jnp.concatenate(near, axis=1),
+                block_diagonal(far),
+                preferred_element_type=jnp.float32,
+            )
 
     def weights(unit, turn, dist_ref, weight_ref):
         root = lax.rsqrt(dist_ref[unit, :, 128 * turn : 128 * turn + 128])
@@ -172,6 +190,11 @@
         weight_ref[unit, 128 * turn : 128 * turn + 128, 128:] = (
             weight - high.astype(jnp.float32)
         ).astype(jnp.bfloat16)
+
+    def turned(index, turn):
+        rotation = lax.bitwise_and(turn - index, 3)
+        group = rotation * groups_of_other + lax.shift_right_logical(index, 2)
+        return other_moment_ref[pl.ds(pl.multiple_of(group * 128, 128), 128), :] * masks[turn]
 
     def products(pair, unit, weight_ref):
         owns = [own_rows_ref[pair + turn] for turn in range(QUAD)]
@@ -183,10 +206,7 @@
             )
             for lanes in (slice(0, 128), slice(128, 256))
         ]
-        columns = jnp.concatenate(
-            [turned(other_moment_ref, others[turn], turn, groups_of_other) for turn in range(QUAD)],
-            axis=0,
-        )
+        columns = jnp.concatenate([turned(others[turn], turn) for turn in range(QUAD)], axis=0)
         to_own = jnp.dot(
             jnp.concatenate(levels, axis=0), columns, preferred_element_type=jnp.float32
         )
@@ -194,7 +214,12 @@
             [own_moment_ref[pl.ds(pl.multiple_of(own * 16, 16), 16), :] for own in owns]
         )
         to_other = jnp.dot(rows, both, preferred_element_type=jnp.float32)
-        return (owns, others, to_own[:128] + to_own[128:], to_other[:, :128] + to_other[:, 128:])
+        return (
+            owns,
+            others,
+            (to_own[:128] + to_own[128:]).T,
+            to_other[:, :128] + to_other[:, 128:],
+        )
 
     def half_step(step, side):
         last = jnp.maximum(step - 2, 0) * UNROLL
@@ -207,9 +232,9 @@
             distances(first + QUAD * unit, unit, dist_refs[1 - side])
         for owns, others, to_own, to_other in results:
             for turn in range(QUAD):
-                own_at = pl.ds(pl.multiple_of(owns[turn] * 128, 128), 128)
+                own_at = pl.ds(pl.multiple_of(owns[turn] * 16, 16), 16)
                 other_at = pl.ds(pl.multiple_of(others[turn] * 16, 16), 16)
-                own_sum_ref[own_at, :] += jnp.where(quarter == turn, to_own, 0.0)
+                own_sum_ref[own_at, :] += to_own[32 * turn : 32 * turn + 16]
                 other_sum_ref[other_at, :] += to_other[16 * turn : 16 * turn + 16]
 
     def visit(step, _):
@@ -219,12 +244,14 @@
 
     lax.fori_loop(0, (groups + 2) // 2, visit, 0)
 
-    def finish(data_ref, out_ref, start, rows_ref, base, stride):
+    def finish(data_ref, out_ref, sum_ref, base, step, _):
+        start = pl.multiple_of(step * 8, 8)
         *comps, charge = components(data_ref, start)
 
         def total(part):
             terms = [
-                rows_ref[pl.ds(base + 4 * level + part, 8, stride=stride), :] for level in range(3)
+                sum_ref[pl.ds(base + start * 16 + 4 * level + part, 8, stride=16), :]
+                for level in range(3)
             ]
             return terms[0] + (terms[1] + terms[2])
 
@@ -233,36 +260,20 @@
         for part, comp in enumerate(comps):
             out_ref[pl.ds(4 * start + part, 8, stride=4), :] = scale * (comp * weight - total(part))
         out_ref[pl.ds(4 * start + 3, 8, stride=4), :] = zeros
-
-    def finish_own(step, _):
-        start = pl.multiple_of(step * 8, 8)
-        for half in range(2):
-            columns = None
-            for index in range(4):
-                at = pl.ds(pl.multiple_of((start + 4 * half + index) * 128, 128), 128)
-                block = own_sum_ref[at, :]
-                block = block + pltpu.roll(block, 64, 1)
-                block = block + pltpu.roll(block, 32, 1)
-                columns = block if index == 0 else jnp.where(quarter < index, columns, block)
-            stage_ref[128 * half : 128 * half + 128, :] = columns.T
-        finish(own_ref, own_out_ref, start, stage_ref, 0, 32)
-        return 0
-
-    def finish_other(source, step, _):
-        start = pl.multiple_of(step * 8, 8)
-        finish(
+        return 0
+
+    lax.fori_loop(
+        0, clusters // 8, functools.partial(finish, own_ref, own_out_ref, own_sum_ref, 0), 0
+    )
+    for source in range(sources):
+        body = functools.partial(
+            finish,
             other_refs[source],
             other_out_refs[source],
-            start,
             other_sum_ref,
-            (source * slots + start) * 16,
-            16,
+            source * slots * 16,
         )
-        return 0
-
-    lax.fori_loop(0, clusters // 8, finish_own, 0)
-    for source in range(sources):
-        lax.fori_loop(0, slots // 8, functools.partial(finish_other, source), 0)
+        lax.fori_loop(0, slots // 8, body, 0)
 
 
 def pair_forces(own_rows, other_rows, own, arrived, slots):
@@ -277,25 +288,24 @@
             jax.ShapeDtypeStruct(own.shape, jnp.float32),
             *[jax.ShapeDtypeStruct((slots * 4, 128), jnp.float32)] * len(arrived),
         ),
-        in_specs=[smem, smem, vmem] + [vmem] * len(arrived),
+        in_specs=[smem, smem] + [vmem] * (5 + len(arrived)),
         out_specs=(vmem,) * (len(arrived) + 1),
         scratch_shapes=[
-            pltpu.VMEM((clusters * 128, 128), jnp.bfloat16),
-            pltpu.VMEM((others * 32, 128), jnp.bfloat16),
+            pltpu.VMEM((clusters * 32, 128), jnp.bfloat16),
+            pltpu.VMEM(((others + 1) * 128, 128), jnp.bfloat16),
             pltpu.VMEM((clusters * 16, 128), jnp.bfloat16),
             pltpu.VMEM((others * 128, 128), jnp.bfloat16),
-            pltpu.VMEM((clusters * 128, 128), jnp.float32),
+            pltpu.VMEM((clusters * 16, 128), jnp.float32),
             pltpu.VMEM((others * 16, 128), jnp.float32),
-            pltpu.VMEM((384, 128), jnp.float32),
             *[pltpu.VMEM((UNROLL // QUAD, 128, 128 * QUAD), jnp.float32)] * 2,
             *[pltpu.VMEM((UNROLL // QUAD, 128 * QUAD, 256), jnp.bfloat16)] * 2,
         ],
-        compiler_params=pltpu.CompilerParams(vmem_limit_bytes=46 * 1024 * 1024),
+        compiler_params=pltpu.CompilerParams(vmem_limit_bytes=40 * 1024 * 1024),
         cost_estimate=pl.CostEstimate(
             flops=pairs * 128 * 128 * 20, bytes_accessed=4 * 1024 * 1024, transcendentals=0
         ),
         name="pair_forces",
-    )(own_rows, other_rows, own, *arrived)
+    )(own_rows, other_rows, *selections(), own, *arrived)
 
 
 def prepare_kernel(

time: 186 us -> 152 us (0.82)
  Pallas kernels: 136 us -> 101 us
    pallas_call x1, Pallas kernels: 105 us -> 70.5 us  [pair_forces(): pl.pallas_call(pair_kernel, out_shape=(jax.ShapeDtypeStruct(own.shape, jn...]
  transfers between devices with their start and end apart: 14 -> 14, of which waited for: 1 -> 1; matrix products, arithmetic and copies ran while one was open for 0% -> 0% of each run, Pallas kernels for 67% -> 59%
where the time goes in v7:
time: 152 us; the launch traced here: 151 us
  Pallas kernels  101 us (66%)
  starting transfers between devices  43.3 us (28%)
  local copies, waits for them, and re-layouts  3.44 us (2%)
  waiting for transfers between devices  2.16 us (1%)
    pallas_call x1, Pallas kernels, pair_forces(): pl.pallas_call(pair_kernel, out_shape=(jax.ShapeDtypeStruct(own.shape, jn...  70.5 us
    ppermute x14, starting transfers between devices, passed_along(): return lax.ppermute(shard, axis, pairs)  43.3 us
    pallas_call x1, Pallas kernels, grid_step(): pl.pallas_call(functools.partial(grid_kernel, base), out_shape=(jax.Shape...  18.7 us
    pallas_call x1, Pallas kernels, prepare(): pl.pallas_call(prepare_kernel, out_shape=(jax.ShapeDtypeStruct((clusters,...  9.11 us
    unnamed x36, local copies, waits for them, and re-layouts  3.44 us
  transfers between devices with their start and end apart: 14, of which 1 were waited for; matrix products, arithmetic and copies ran while one was open for 0% of the time, Pallas kernels for 59%

profile of v7, /device:TPU:13, one launch (start us, length us, event | category | flops | bytes accessed | tf_op | source)
XLA Modules:
  0.0 151.2 jit_solution(8328155650757189782)
XLA Ops:
  0.6 0.0 copy-start
  0.6 0.0 copy-start.1
  0.7 9.1 %prepare.1 = (f32[256,4,128]{2,1,0:T(4,128)}, f32[256,128]{1,0:T(8,128)}, f32[16,32,256]{2,1,0:T(8,128)}, f32[16,32,256]{2,1,0:T(8,128)}, f32[128,128]{1,0:T(8,1...) custom-call(s32[256]{0:T(256)} %fill_ref.1, ...), custom_call_target="tpu_custom_call" | custom-call | tf_op jit(solution)/shard_map/prepare/pallas_call | solution.py:431
  9.8 3.8 %collective-permute-start = (f32[640,128]{1,0:T(8,128)}, f32[640,128]{1,0:T(8,128)S(1)}, u32[]{:S(2)}, u32[]{:S(2)}) collective-permute-start(f32[640,128]{1,0:T(8,128)} %get-tuple-element.36), channel_id=1, source_target_pairs={{0,1},{1,2},{2,3},{3,4},{4,5},{5,6},{6,7},{8,9},{9,10},{10,11},{11... | collective-permute-start | bytes 983048 | tf_op jit(solution)/shard_map/ppermute | solution.py:735
  13.5 1.9 %collective-permute-start.1 = (f32[640,128]{1,0:T(8,128)}, f32[640,128]{1,0:T(8,128)S(1)}, u32[]{:S(2)}, u32[]{:S(2)}) collective-permute-start(f32[640,128]{1,0:T(8,128)} %get-tuple-element.37), channel_id=1, source_target_pairs={{1,0},{2,1},{3,2},{4,3},{5,4},{6,5},{7,6},{9,8},{10,9},{11,10},{12... | collective-permute-start | bytes 983048 | tf_op jit(solution)/shard_map/ppermute | solution.py:735
  15.5 3.2 %collective-permute-start.2 = (f32[128,128]{1,0:T(8,128)}, f32[128,128]{1,0:T(8,128)S(1)}, u32[]{:S(2)}, u32[]{:S(2)}) collective-permute-start(f32[128,128]{1,0:T(8,128)} %get-tuple-element.38), channel_id=1, source_target_pairs={{0,2},{1,3},{2,4},{3,5},{4,6},{5,7},{8,10},{9,11},{10,12},{11,13},... | collective-permute-start | bytes 196616 | tf_op jit(solution)/shard_map/ppermute | solution.py:735
  18.7 2.1 %collective-permute-start.3 = (f32[128,128]{1,0:T(8,128)}, f32[128,128]{1,0:T(8,128)S(1)}, u32[]{:S(2)}, u32[]{:S(2)}) collective-permute-start(f32[128,128]{1,0:T(8,128)} %get-tuple-element.39), channel_id=1, source_target_pairs={{2,0},{3,1},{4,2},{5,3},{6,4},{7,5},{10,8},{11,9},{12,10},{13,11},... | collective-permute-start | bytes 196616 | tf_op jit(solution)/shard_map/ppermute | solution.py:735
  20.8 3.1 %collective-permute-start.4 = (f32[128,128]{1,0:T(8,128)}, f32[128,128]{1,0:T(8,128)S(1)}, u32[]{:S(2)}, u32[]{:S(2)}) collective-permute-start(f32[128,128]{1,0:T(8,128)} %get-tuple-element.40), channel_id=1, source_target_pairs={{0,8},{8,16},{16,24},{1,9},{9,17},{17,25},{2,10},{10,18},{18,26},{... | collective-permute-start | bytes 196616 | tf_op jit(solution)/shard_map/ppermute | solution.py:735
  23.9 0.0 collective-permute-done.2.refs_8_
  23.9 3.1 %collective-permute-start.5 = (f32[128,128]{1,0:T(8,128)}, f32[128,128]{1,0:T(8,128)S(1)}, u32[]{:S(2)}, u32[]{:S(2)}) collective-permute-start(f32[128,128]{1,0:T(8,128)} %get-tuple-element.41), channel_id=1, source_target_pairs={{8,0},{16,8},{24,16},{9,1},{17,9},{25,17},{10,2},{18,10},{26,18},{... | collective-permute-start | bytes 196616 | tf_op jit(solution)/shard_map/ppermute | solution.py:735
  27.0 0.0 collective-permute-done.3.refs_9_
  27.0 0.0 collective-permute-done.4.refs_10_
  27.0 2.1 %collective-permute-done.5.refs_11_ = f32[128,128]{1,0:T(8,128)S(1)} collective-permute-done((f32[128,128]{1,0:T(8,128)}, f32[128,128]{1,0:T(8,128)S(1)}, u32[]{:S(2)}, u32[]{:S(2)}) %collective-permute-start.5) | collective-permute-done | bytes 65568 | tf_op jit(solution)/shard_map/ppermute | solution.py:735
  29.1 0.0 collective-permute-done.refs_6_.refs_4_
  29.1 0.0 collective-permute-done.1.refs_7_.refs_5_
  29.1 0.0 copy-done
  29.1 0.0 copy-done.1
  29.2 0.0 copy-start.2
  29.2 1.0 copy-done.2
  30.2 0.0 copy-start.4
  30.2 1.0 copy-done.4
  31.2 0.0 copy-start.16
  31.2 0.0 copy-start.17
  31.2 0.0 copy-start.9
  31.3 0.0 copy-start.10
  31.3 0.0 copy-start.11
  31.3 0.0 copy-start.12
  31.3 0.1 planes.1
  31.4 2.1 %collective-permute-start.6 = (f32[14,48,256]{2,1,0:T(8,128)S(1)}, f32[14,48,256]{2,1,0:T(8,128)S(1)}, u32[]{:S(2)}, u32[]{:S(2)}) collective-permute-start(f32[14,48,256]{2,1,0:T(8,128)S(1)} %get-tuple-element.53), channel_id=1, source_target_pairs={{0,8},{8,16},{16,24},{1,9},{9,17},{17,25},{2,10},{10,18},{18,26},{... | collective-permute-start | bytes 2064392 | tf_op jit(solution)/shard_map/ppermute | solution.py:735
  33.5 4.3 %collective-permute-start.7 = (f32[14,48,256]{2,1,0:T(8,128)S(1)}, f32[14,48,256]{2,1,0:T(8,128)S(1)}, u32[]{:S(2)}, u32[]{:S(2)}) collective-permute-start(f32[14,48,256]{2,1,0:T(8,128)S(1)} %get-tuple-element.54), channel_id=1, source_target_pairs={{8,0},{16,8},{24,16},{9,1},{17,9},{25,17},{10,2},{18,10},{26,18},{... | collective-permute-start | bytes 2064392 | tf_op jit(solution)/shard_map/ppermute | solution.py:735
  37.8 0.0 copy-done.16
  37.8 0.0 copy-done.17
  37.8 0.0 copy-start.14
  37.8 0.0 copy-done.6
  37.8 0.0 copy-done.7
  37.8 0.0 copy-done.9
  37.8 0.0 copy-done.10
  37.9 0.0 copy-done.11
  37.9 0.0 copy-done.12
  37.9 0.6 copy-done.14
  38.5 70.5 %pair_forces.1 = (f32[1024,128]{1,0:T(8,128)S(1)}, f32[128,128]{1,0:T(8,128)S(1)}, f32[128,128]{1,0:T(8,128)S(1)}, f32[128,128]{1,0:T(8,128)S(1)}, f32[128,128]{...) custom-call(s32[1024]{0:T(1024)S(1)} %copy-done.14, ...), custom_call_target="tpu_custom_call" | custom-call | flops 335544320 | bytes 4194304 | tf_op jit(solution)/shard_map/pair_forces/pallas_call | solution.py:285
  109.0 1.9 %collective-permute-start.13 = (f32[128,128]{1,0:T(8,128)S(1)}, f32[128,128]{1,0:T(8,128)S(1)}, u32[]{:S(2)}, u32[]{:S(2)}) collective-permute-start(f32[128,128]{1,0:T(8,128)S(1)} %get-tuple-element.62), channel_id=1, source_target_pairs={{0,8},{8,16},{16,24},{1,9},{9,17},{17,25},{2,10},{10,18},{18,26},{... | collective-permute-start | bytes 196616 | tf_op jit(solution)/shard_map/ppermute | solution.py:735
  110.9 4.9 %collective-permute-start.8 = (f32[128,128]{1,0:T(8,128)S(1)}, f32[128,128]{1,0:T(8,128)S(1)}, u32[]{:S(2)}, u32[]{:S(2)}) collective-permute-start(f32[128,128]{1,0:T(8,128)S(1)} %get-tuple-element.57), channel_id=1, source_target_pairs={{1,0},{2,1},{3,2},{4,3},{5,4},{6,5},{7,6},{9,8},{10,9},{11,10},{12... | collective-permute-start | bytes 196616 | tf_op jit(solution)/shard_map/ppermute | solution.py:735
  115.9 3.2 %collective-permute-start.9 = (f32[128,128]{1,0:T(8,128)S(1)}, f32[128,128]{1,0:T(8,128)S(1)}, u32[]{:S(2)}, u32[]{:S(2)}) collective-permute-start(f32[128,128]{1,0:T(8,128)S(1)} %get-tuple-element.58), channel_id=1, source_target_pairs={{0,1},{1,2},{2,3},{3,4},{4,5},{5,6},{6,7},{8,9},{9,10},{10,11},{11... | collective-permute-start | bytes 196616 | tf_op jit(solution)/shard_map/ppermute | solution.py:735
  119.1 0.0 collective-permute-done.13
  119.1 2.0 %collective-permute-start.10 = (f32[128,128]{1,0:T(8,128)S(1)}, f32[128,128]{1,0:T(8,128)S(1)}, u32[]{:S(2)}, u32[]{:S(2)}) collective-permute-start(f32[128,128]{1,0:T(8,128)S(1)} %get-tuple-element.59), channel_id=1, source_target_pairs={{2,0},{3,1},{4,2},{5,3},{6,4},{7,5},{10,8},{11,9},{12,10},{13,11},... | collective-permute-start | bytes 196616 | tf_op jit(solution)/shard_map/ppermute | solution.py:735
  121.1 0.0 collective-permute-done.6.refs_8_
  121.1 3.3 %collective-permute-start.11 = (f32[128,128]{1,0:T(8,128)S(1)}, f32[128,128]{1,0:T(8,128)S(1)}, u32[]{:S(2)}, u32[]{:S(2)}) collective-permute-start(f32[128,128]{1,0:T(8,128)S(1)} %get-tuple-element.60), channel_id=1, source_target_pairs={{0,2},{1,3},{2,4},{3,5},{4,6},{5,7},{8,10},{9,11},{10,12},{11,13},... | collective-permute-start | bytes 196616 | tf_op jit(solution)/shard_map/ppermute | solution.py:735
  124.4 0.0 collective-permute-done.7.refs_9_
  124.4 0.0 copy-start.15
  124.4 4.5 %collective-permute-start.12 = (f32[128,128]{1,0:T(8,128)S(1)}, f32[128,128]{1,0:T(8,128)S(1)}, u32[]{:S(2)}, u32[]{:S(2)}) collective-permute-start(f32[128,128]{1,0:T(8,128)S(1)} %get-tuple-element.61), channel_id=1, source_target_pairs={{8,0},{16,8},{24,16},{9,1},{17,9},{25,17},{10,2},{18,10},{26,18},{... | collective-permute-start | bytes 196616 | tf_op jit(solution)/shard_map/ppermute | solution.py:735
  129.0 0.0 copy-done.3
  129.0 0.0 copy-done.5
  129.0 0.0 copy-done.8
  129.0 0.0 copy-done.15
  129.0 18.7 %grid_step.1 = (f32[16,32,256]{2,1,0:T(8,128)}, f32[16,32,256]{2,1,0:T(8,128)}, f32[1024,128]{1,0:T(8,128)S(1)}) custom-call(s32[256]{0:T(256)S(1)} %copy-done.15, f32[256,128]{1,0:T(8,128)S(1)} %copy-done.8, f32[16,32,256]{2,1,0:T(8,128)S(1)} %copy-done.1, f32[16,32,256]{2,1,0:T(8,128)S(1)} %copy-done.3, f32[16,32,256]{2,1,0:T(8,128)S(1)} %copy-done.5, ...), custom_call_target="tpu_custom_call" | custom-call | flops 31948800 | bytes 8388608 | tf_op jit(solution)/shard_map/grid_step/pallas_call | solution.py:674
  147.7 0.0 collective-permute-done.8
  147.7 0.0 collective-permute-done.9
  147.7 0.0 collective-permute-done.10
  147.7 0.0 collective-permute-done.11
  147.7 0.0 collective-permute-done.12
  147.7 0.0 copy-start.13
  147.7 0.7 copy-done.13
  148.4 2.8 %gather_forces.1 = f32[3,32768]{1,0:T(4,128)} custom-call(s32[7,32]{1,0:T(8,128)S(1)} %copy-done.13, f32[256,4,128]{2,1,0:T(4,128)S(1)} %bitcast.11, f32[256,4,128]{2,1,0:T(4,128)S(1)} %bitcast.13, f32[32,4,128]{2,1,0:T(4,128)S(1)} %bitcast.14, f32[32,4,128]{2,1,0:T(4,128)S(1)} %bitcast.16, f32[32,4,128]{2,1,0:T(4,128)S(1)} %bitcast.17, ...), custom_call_target="tpu_custom_call" | custom-call | tf_op jit(solution)/shard_map/gather_forces/pallas_call | solution.py:721
  (6 shorter events, 0.0 us)
Async XLA Ops:
  0.6 28.5 %copy-start = (f32[16,32,256]{2,1,0:T(8,128)S(1)}, f32[16,32,256]{2,1,0:T(8,128)}, u32[]{:S(2)}) copy-start(f32[16,32,256]{2,1,0:T(8,128)} %refs_5_.1) | copy-start | bytes 1572868
  0.6 28.5 %copy-start.1 = (f32[16,32,256]{2,1,0:T(8,128)S(1)}, f32[16,32,256]{2,1,0:T(8,128)}, u32[]{:S(2)}) copy-start(f32[16,32,256]{2,1,0:T(8,128)} %refs_2_.2) | copy-start | bytes 1572868
  9.8 19.4 %collective-permute-start = (f32[640,128]{1,0:T(8,128)}, f32[640,128]{1,0:T(8,128)S(1)}, u32[]{:S(2)}, u32[]{:S(2)}) collective-permute-start(f32[640,128]{1,0:T(8,128)} %get-tuple-element.36), channel_id=1, source_target_pairs={{0,1},{1,2},{2,3},{3,4},{4,5},{5,6},{6,7},{8,9},{9,10},{10,11},{11... | collective-permute-start | bytes 983048 | tf_op jit(solution)/shard_map/ppermute | solution.py:735
  13.5 15.6 %collective-permute-start.1 = (f32[640,128]{1,0:T(8,128)}, f32[640,128]{1,0:T(8,128)S(1)}, u32[]{:S(2)}, u32[]{:S(2)}) collective-permute-start(f32[640,128]{1,0:T(8,128)} %get-tuple-element.37), channel_id=1, source_target_pairs={{1,0},{2,1},{3,2},{4,3},{5,4},{6,5},{7,6},{9,8},{10,9},{11,10},{12... | collective-permute-start | bytes 983048 | tf_op jit(solution)/shard_map/ppermute | solution.py:735
  15.5 8.4 %collective-permute-start.2 = (f32[128,128]{1,0:T(8,128)}, f32[128,128]{1,0:T(8,128)S(1)}, u32[]{:S(2)}, u32[]{:S(2)}) collective-permute-start(f32[128,128]{1,0:T(8,128)} %get-tuple-element.38), channel_id=1, source_target_pairs={{0,2},{1,3},{2,4},{3,5},{4,6},{5,7},{8,10},{9,11},{10,12},{11,13},... | collective-permute-start | bytes 196616 | tf_op jit(solution)/shard_map/ppermute | solution.py:735
  18.7 8.3 %collective-permute-start.3 = (f32[128,128]{1,0:T(8,128)}, f32[128,128]{1,0:T(8,128)S(1)}, u32[]{:S(2)}, u32[]{:S(2)}) collective-permute-start(f32[128,128]{1,0:T(8,128)} %get-tuple-element.39), channel_id=1, source_target_pairs={{2,0},{3,1},{4,2},{5,3},{6,4},{7,5},{10,8},{11,9},{12,10},{13,11},... | collective-permute-start | bytes 196616 | tf_op jit(solution)/shard_map/ppermute | solution.py:735
  20.8 6.2 %collective-permute-start.4 = (f32[128,128]{1,0:T(8,128)}, f32[128,128]{1,0:T(8,128)S(1)}, u32[]{:S(2)}, u32[]{:S(2)}) collective-permute-start(f32[128,128]{1,0:T(8,128)} %get-tuple-element.40), channel_id=1, source_target_pairs={{0,8},{8,16},{16,24},{1,9},{9,17},{17,25},{2,10},{10,18},{18,26},{... | collective-permute-start | bytes 196616 | tf_op jit(solution)/shard_map/ppermute | solution.py:735
  23.9 5.2 %collective-permute-start.5 = (f32[128,128]{1,0:T(8,128)}, f32[128,128]{1,0:T(8,128)S(1)}, u32[]{:S(2)}, u32[]{:S(2)}) collective-permute-start(f32[128,128]{1,0:T(8,128)} %get-tuple-element.41), channel_id=1, source_target_pairs={{8,0},{16,8},{24,16},{9,1},{17,9},{25,17},{10,2},{18,10},{26,18},{... | collective-permute-start | bytes 196616 | tf_op jit(solution)/shard_map/ppermute | solution.py:735
  29.2 1.0 copy-start.2
  30.2 1.0 copy-start.4
  31.2 6.5 %copy-start.16 = (s32[1024]{0:T(1024)S(1)}, s32[1024]{0:T(1024)}, u32[]{:S(2)}) copy-start(s32[1024]{0:T(1024)} %param.24) | copy-start | bytes 12292
  31.2 6.5 %copy-start.17 = (s32[1024]{0:T(1024)S(1)}, s32[1024]{0:T(1024)}, u32[]{:S(2)}) copy-start(s32[1024]{0:T(1024)} %param.23) | copy-start | bytes 12292
  31.2 6.6 %copy-start.6 = (f32[256,4,128]{2,1,0:T(4,128)S(1)}, f32[256,4,128]{2,1,0:T(4,128)}, u32[]{:S(2)}) copy-start(f32[256,4,128]{2,1,0:T(4,128)} %get-tuple-element.34) | copy-start | bytes 1572868
  31.2 6.6 %copy-start.7 = (bf16[128,1024]{1,0:T(8,128)(2,1)S(1)}, bf16[128,1024]{1,0:T(8,128)(2,1)}, u32[]{:S(2)}) copy-start(bf16[128,1024]{1,0:T(8,128)(2,1)} %constant.13.clone.refs_3_) | copy-start | bytes 786436
  31.2 6.6 %copy-start.9 = (bf16[128,256]{1,0:T(8,128)(2,1)S(1)}, bf16[128,256]{1,0:T(8,128)(2,1)}, u32[]{:S(2)}) copy-start(bf16[128,256]{1,0:T(8,128)(2,1)} %constant.10.clone.refs_0_) | copy-start | bytes 196612
  31.3 6.6 %copy-start.10 = (bf16[256,128]{1,0:T(8,128)(2,1)S(1)}, bf16[256,128]{1,0:T(8,128)(2,1)}, u32[]{:S(2)}) copy-start(bf16[256,128]{1,0:T(8,128)(2,1)} %constant.11.clone.refs_1_) | copy-start | bytes 196612
  31.3 6.6 %copy-start.11 = (f32[128,128]{1,0:T(8,128)S(1)}, f32[128,128]{1,0:T(8,128)}, u32[]{:S(2)}) copy-start(f32[128,128]{1,0:T(8,128)} %get-tuple-element.42.refs_5_) | copy-start | bytes 196612
  31.3 6.6 %copy-start.12 = (bf16[128,128]{1,0:T(8,128)(2,1)S(1)}, bf16[128,128]{1,0:T(8,128)(2,1)}, u32[]{:S(2)}) copy-start(bf16[128,128]{1,0:T(8,128)(2,1)} %constant.12.clone.refs_2_) | copy-start | bytes 98308
  31.4 89.7 %collective-permute-start.6 = (f32[14,48,256]{2,1,0:T(8,128)S(1)}, f32[14,48,256]{2,1,0:T(8,128)S(1)}, u32[]{:S(2)}, u32[]{:S(2)}) collective-permute-start(f32[14,48,256]{2,1,0:T(8,128)S(1)} %get-tuple-element.53), channel_id=1, source_target_pairs={{0,8},{8,16},{16,24},{1,9},{9,17},{17,25},{2,10},{10,18},{18,26},{... | collective-permute-start | bytes 2064392 | tf_op jit(solution)/shard_map/ppermute | solution.py:735
  33.5 90.9 %collective-permute-start.7 = (f32[14,48,256]{2,1,0:T(8,128)S(1)}, f32[14,48,256]{2,1,0:T(8,128)S(1)}, u32[]{:S(2)}, u32[]{:S(2)}) collective-permute-start(f32[14,48,256]{2,1,0:T(8,128)S(1)} %get-tuple-element.54), channel_id=1, source_target_pairs={{8,0},{16,8},{24,16},{9,1},{17,9},{25,17},{10,2},{18,10},{26,18},{... | collective-permute-start | bytes 2064392 | tf_op jit(solution)/shard_map/ppermute | solution.py:735
  37.8 0.7 copy-start.14
  38.5 90.5 %copy-start.3 = (f32[16,32,256]{2,1,0:T(8,128)S(1)}, f32[16,32,256]{2,1,0:T(8,128)}, u32[]{:S(2)}) copy-start(f32[16,32,256]{2,1,0:T(8,128)} %get-tuple-element.51.refs_1_.refs_3_) | copy-start | bytes 1572868
  38.5 90.5 %copy-start.5 = (f32[16,32,256]{2,1,0:T(8,128)S(1)}, f32[16,32,256]{2,1,0:T(8,128)}, u32[]{:S(2)}) copy-start(f32[16,32,256]{2,1,0:T(8,128)} %get-tuple-element.52.refs_2_.refs_4_) | copy-start | bytes 1572868
  38.5 90.5 %copy-start.8 = (f32[256,128]{1,0:T(8,128)S(1)}, f32[256,128]{1,0:T(8,128)}, u32[]{:S(2)}) copy-start(f32[256,128]{1,0:T(8,128)} %get-tuple-element.50.refs_1_) | copy-start | bytes 393220
  109.0 10.1 %collective-permute-start.13 = (f32[128,128]{1,0:T(8,128)S(1)}, f32[128,128]{1,0:T(8,128)S(1)}, u32[]{:S(2)}, u32[]{:S(2)}) collective-permute-start(f32[128,128]{1,0:T(8,128)S(1)} %get-tuple-element.62), channel_id=1, source_target_pairs={{0,8},{8,16},{16,24},{1,9},{9,17},{17,25},{2,10},{10,18},{18,26},{... | collective-permute-start | bytes 196616 | tf_op jit(solution)/shard_map/ppermute | solution.py:735
  110.9 36.8 %collective-permute-start.8 = (f32[128,128]{1,0:T(8,128)S(1)}, f32[128,128]{1,0:T(8,128)S(1)}, u32[]{:S(2)}, u32[]{:S(2)}) collective-permute-start(f32[128,128]{1,0:T(8,128)S(1)} %get-tuple-element.57), channel_id=1, source_target_pairs={{1,0},{2,1},{3,2},{4,3},{5,4},{6,5},{7,6},{9,8},{10,9},{11,10},{12... | collective-permute-start | bytes 196616 | tf_op jit(solution)/shard_map/ppermute | solution.py:735
  115.9 31.8 %collective-permute-start.9 = (f32[128,128]{1,0:T(8,128)S(1)}, f32[128,128]{1,0:T(8,128)S(1)}, u32[]{:S(2)}, u32[]{:S(2)}) collective-permute-start(f32[128,128]{1,0:T(8,128)S(1)} %get-tuple-element.58), channel_id=1, source_target_pairs={{0,1},{1,2},{2,3},{3,4},{4,5},{5,6},{6,7},{8,9},{9,10},{10,11},{11... | collective-permute-start | bytes 196616 | tf_op jit(solution)/shard_map/ppermute | solution.py:735
  119.1 28.6 %collective-permute-start.10 = (f32[128,128]{1,0:T(8,128)S(1)}, f32[128,128]{1,0:T(8,128)S(1)}, u32[]{:S(2)}, u32[]{:S(2)}) collective-permute-start(f32[128,128]{1,0:T(8,128)S(1)} %get-tuple-element.59), channel_id=1, source_target_pairs={{2,0},{3,1},{4,2},{5,3},{6,4},{7,5},{10,8},{11,9},{12,10},{13,11},... | collective-permute-start | bytes 196616 | tf_op jit(solution)/shard_map/ppermute | solution.py:735
  121.1 26.6 %collective-permute-start.11 = (f32[128,128]{1,0:T(8,128)S(1)}, f32[128,128]{1,0:T(8,128)S(1)}, u32[]{:S(2)}, u32[]{:S(2)}) collective-permute-start(f32[128,128]{1,0:T(8,128)S(1)} %get-tuple-element.60), channel_id=1, source_target_pairs={{0,2},{1,3},{2,4},{3,5},{4,6},{5,7},{8,10},{9,11},{10,12},{11,13},... | collective-permute-start | bytes 196616 | tf_op jit(solution)/shard_map/ppermute | solution.py:735
  124.4 4.6 %copy-start.15 = (s32[256]{0:T(256)S(1)}, s32[256]{0:T(256)}, u32[]{:S(2)}) copy-start(s32[256]{0:T(256)} %refs_0_.4) | copy-start | bytes 3076
  124.4 23.3 %collective-permute-start.12 = (f32[128,128]{1,0:T(8,128)S(1)}, f32[128,128]{1,0:T(8,128)S(1)}, u32[]{:S(2)}, u32[]{:S(2)}) collective-permute-start(f32[128,128]{1,0:T(8,128)S(1)} %get-tuple-element.61), channel_id=1, source_target_pairs={{8,0},{16,8},{24,16},{9,1},{17,9},{25,17},{10,2},{18,10},{26,18},{... | collective-permute-start | bytes 196616 | tf_op jit(solution)/shard_map/ppermute | solution.py:735
  147.7 0.7 copy-start.13

commit v8 on v7

--- a/solution.py
+++ b/solution.py
@@ -14,6 +14,7 @@
 HALO_WIDTHS = (SWEEPS + 1, SWEEPS, SWEEPS, 1)
 MARGIN = 8
 CELL_BITS = 8
+ROUTES = (("brick", 1), ("brick", -1), ("brick", 2), ("brick", -2), ("grp", 1), ("grp", -1))
 
 
 coulomb_scale = 0.02
@@ -71,10 +72,9 @@
 def pair_kernel(own_rows_ref, other_rows_ref, *refs):
     near_sel_ref, far_sel_ref, own_moment_sel_ref, other_moment_sel_ref, own_ref = refs[:5]
     refs = refs[5:]
-    sources = (len(refs) - 11) // 2
+    sources = len(ROUTES) + 1
     other_refs = refs[:sources]
-    own_out_ref = refs[sources]
-    other_out_refs = refs[sources + 1 : 2 * sources + 1]
+    own_out_ref, local_out_ref, brick_out_ref, grp_out_ref = refs[sources : sources + 4]
     (
         near_ref,
         far_ref,
@@ -83,9 +83,9 @@
         own_sum_ref,
         other_sum_ref,
         *passed_refs,
-    ) = refs[2 * sources + 1 :]
+    ) = refs[sources + 4 :]
     clusters = own_ref.shape[0] // 4
-    slots = other_out_refs[0].shape[0] // 4
+    slots = local_out_ref.shape[0] // 4
     others = slots * sources
     groups = own_rows_ref.shape[0] // UNROLL
     units = UNROLL // QUAD
@@ -244,7 +244,7 @@
 
     lax.fori_loop(0, (groups + 2) // 2, visit, 0)
 
-    def finish(data_ref, out_ref, sum_ref, base, step, _):
+    def finish(data_ref, out_ref, out_base, sum_ref, base, step, _):
         start = pl.multiple_of(step * 8, 8)
         *comps, charge = components(data_ref, start)
 
@@ -258,18 +258,23 @@
         weight = total(3)
         scale = coulomb_scale * charge
         for part, comp in enumerate(comps):
-            out_ref[pl.ds(4 * start + part, 8, stride=4), :] = scale * (comp * weight - total(part))
-        out_ref[pl.ds(4 * start + 3, 8, stride=4), :] = zeros
+            out_ref[pl.ds(out_base + 4 * start + part, 8, stride=4), :] = scale * (
+                comp * weight - total(part)
+            )
+        out_ref[pl.ds(out_base + 4 * start + 3, 8, stride=4), :] = zeros
         return 0
 
     lax.fori_loop(
-        0, clusters // 8, functools.partial(finish, own_ref, own_out_ref, own_sum_ref, 0), 0
+        0, clusters // 8, functools.partial(finish, own_ref, own_out_ref, 0, own_sum_ref, 0), 0
     )
+    targets = [(local_out_ref, 0)]
+    targets += [(brick_out_ref, slots * 4 * index) for index in range(4)]
+    targets += [(grp_out_ref, slots * 4 * index) for index in range(2)]
     for source in range(sources):
         body = functools.partial(
             finish,
             other_refs[source],
-            other_out_refs[source],
+            *targets[source],
             other_sum_ref,
             source * slots * 16,
         )
@@ -286,10 +291,10 @@
         pair_kernel,
         out_shape=(
             jax.ShapeDtypeStruct(own.shape, jnp.float32),
-            *[jax.ShapeDtypeStruct((slots * 4, 128), jnp.float32)] * len(arrived),
+            *[jax.ShapeDtypeStruct((slots * 4 * count, 128), jnp.float32) for count in (1, 4, 2)],
         ),
         in_specs=[smem, smem] + [vmem] * (5 + len(arrived)),
-        out_specs=(vmem,) * (len(arrived) + 1),
+        out_specs=(vmem,) * 4,
         scratch_shapes=[
             pltpu.VMEM((clusters * 32, 128), jnp.bfloat16),
             pltpu.VMEM(((others + 1) * 128, 128), jnp.bfloat16),
@@ -691,16 +696,44 @@
     )(cell, masked, *fields, before, after, lower, upper)
 
 
-def gather_forces_kernel(send_index_ref, own_ref, field_ref, *refs):
-    back_refs, (out_ref, sum_ref) = (refs[:-2], refs[-2:])
+def gather_forces_kernel(
+    send_index_ref,
+    own_ref,
+    field_ref,
+    local_ref,
+    brick_hbm,
+    grp_hbm,
+    out_ref,
+    sum_ref,
+    back_ref,
+    sems,
+):
     clusters = own_ref.shape[0]
     slots = send_index_ref.shape[1]
+    shares = []
+    for index, (axis, by) in enumerate(ROUTES):
+        hbm = brick_hbm if axis == "brick" else grp_hbm
+        first, count = (0, 4) if axis == "brick" else (4, 2)
+        devices = hbm.shape[0] // (slots * count)
+        source = lax.axis_index(axis) + by
+        inside = (source >= 0) & (source < devices)
+        block = jnp.clip(source, 0, devices - 1) * count + index - first
+        copy = pltpu.make_async_copy(
+            hbm.at[pl.ds(block * slots, slots)],
+            back_ref.at[pl.ds(index * slots, slots)],
+            sems.at[index],
+        )
+        copy.start()
+        shares.append((copy, jnp.where(inside, 1.0, 0.0)))
     sum_ref[...] = own_ref[...] + field_ref[...]
+    for copy, _ in shares:
+        copy.wait()
 
     def visit(slot, _):
-        for direction, back_ref in enumerate(back_refs):
-            cluster = send_index_ref[direction, slot]
-            sum_ref[cluster] += back_ref[slot]
+        sum_ref[send_index_ref[0, slot]] += local_ref[slot]
+        for index, (_, share) in enumerate(shares):
+            cluster = send_index_ref[index + 1, slot]
+            sum_ref[cluster] += back_ref[index * slots + slot] * share
         return 0
 
     lax.fori_loop(0, slots, visit, 0)
@@ -714,28 +747,31 @@
     lax.fori_loop(0, clusters // 8, write, 0)
 
 
-def gather_forces(send_index, own, field, backs):
+def gather_forces(send_index, own, field, local, brick_all, grp_all):
     smem = pl.BlockSpec(memory_space=pltpu.SMEM)
     vmem = pl.BlockSpec(memory_space=pltpu.VMEM)
+    hbm = pl.BlockSpec(memory_space=pltpu.HBM)
     clusters = own.shape[0]
+    slots = send_index.shape[1]
     return pl.pallas_call(
         gather_forces_kernel,
         out_shape=jax.ShapeDtypeStruct((3, clusters * 128), jnp.float32),
-        in_specs=[smem] + [vmem] * (2 + len(backs)),
+        in_specs=[smem, vmem, vmem, vmem, hbm, hbm],
         out_specs=vmem,
-        scratch_shapes=[pltpu.VMEM(own.shape, jnp.float32)],
-        compiler_params=pltpu.CompilerParams(vmem_limit_bytes=32 * 1024 * 1024),
+        scratch_shapes=[
+            pltpu.VMEM(own.shape, jnp.float32),
+            pltpu.VMEM((len(ROUTES) * slots, 4, 128), jnp.float32),
+            pltpu.SemaphoreType.DMA((len(ROUTES),)),
+        ],
+        compiler_params=pltpu.CompilerParams(vmem_limit_bytes=60 * 1024 * 1024),
         name="gather_forces",
-    )(send_index, own, field, *backs)
+    )(send_index, own, field, local, brick_all, grp_all)
 
 
 def passed_along(shard, axis, by):
     devices = lax.axis_size(axis)
     pairs = [(i, i + by) for i in range(devices) if 0 <= i + by < devices]
     return lax.ppermute(shard, axis, pairs)
-
-
-ROUTES = (("brick", 1), ("brick", -1), ("brick", 2), ("brick", -2), ("grp", 1), ("grp", -1))
 
 
 def shards(
@@ -777,17 +813,18 @@
     down, up = planes(fields, before, after, base)
     lower = passed_along(up, "grp", 1)
     upper = passed_along(down, "grp", -1)
-    own_force, *reactions = pair_forces(
+    own_force, local_back, brick_back, grp_back = pair_forces(
         pair_local,
         pair_dir * slots + pair_slot,
         own.reshape(clusters * 4, psize),
         arrived,
         slots,
     )
-    backs = [reactions[0]] + [
-        passed_along(reaction, axis, -by)
-        for reaction, (axis, by) in zip(reactions[1:], ROUTES, strict=True)
-    ]
+    brick_back, grp_back, lower, upper = lax.optimization_barrier(
+        (brick_back, grp_back, lower, upper)
+    )
+    brick_all = lax.all_gather(brick_back, "brick")
+    grp_all = lax.all_gather(grp_back, "grp")
     potential, ion_next, field_force = grid_step(
         cluster_cell, masked, fields, before, after, lower, upper, base
     )
@@ -795,7 +832,9 @@
         send_index,
         own_force.reshape(clusters, 4, psize),
         field_force.reshape(clusters, 4, psize),
-        [back.reshape(slots, 4, psize) for back in backs],
+        local_back.reshape(slots, 4, psize),
+        brick_all.reshape(-1, 4, psize),
+        grp_all.reshape(-1, 4, psize),
     )
     return (forces, potential, ion_next)
 

time: 152 us -> 166 us (1.092)
  the two profiles are of different devices: /device:TPU:13 before, /device:TPU:0 now
where the time goes in v8:
time: 166 us; the launch traced here: 165 us
  Pallas kernels  103 us (62%)
  starting transfers between devices  22.3 us (13%)
  between operations  14.4 us (9%)
  blocking collectives  12.3 us (7%)
  local copies, waits for them, and re-layouts  8.55 us (5%)
  waiting for transfers between devices  5.1 us (3%)
    pallas_call x1, Pallas kernels, pair_forces(): pl.pallas_call(pair_kernel, out_shape=(jax.ShapeDtypeStruct(own.shape, jn...  70.4 us
    ppermute x8, starting transfers between devices, passed_along(): return lax.ppermute(shard, axis, pairs)  22.2 us
    pallas_call x1, Pallas kernels, grid_step(): pl.pallas_call(functools.partial(grid_kernel, base), out_shape=(jax.Shape...  18.7 us
    all_gather x1, blocking collectives, shards(): grp_all = lax.all_gather(grp_back, 'grp')  12.3 us
    pallas_call x1, Pallas kernels, prepare(): pl.pallas_call(prepare_kernel, out_shape=(jax.ShapeDtypeStruct((clusters,...  9.13 us
    unnamed x50, local copies, waits for them, and re-layouts  8.55 us
    ppermute x8, waiting for transfers between devices, passed_along(): return lax.ppermute(shard, axis, pairs)  5.08 us
    pallas_call x1, Pallas kernels, gather_forces(): pl.pallas_call(gather_forces_kernel, out_shape=jax.ShapeDtypeStruct((3, c...  4.34 us
  transfers between devices with their start and end apart: 9, of which 3 were waited for; matrix products, arithmetic and copies ran while one was open for 0% of the time, Pallas kernels for 54%

profile of v8, /device:TPU:0, one launch (start us, length us, event | category | flops | bytes accessed | tf_op | source)
XLA Modules:
  0.0 165.4 jit_solution(6439105152226118439)
XLA Ops:
  7.2 0.0 copy-start.1
  7.2 0.0 copy-start
  7.2 0.0 all-gather.4.cloned.1.call-start
  7.2 0.0 copy-start.23
  7.2 0.0 copy-start.24
  7.3 0.0 copy-start.12
  7.3 0.0 copy-start.17
  7.3 0.0 copy-start.18
  7.3 0.0 copy-start.20
  7.3 0.0 copy-start.21
  7.3 9.1 %prepare.1 = (f32[256,4,128]{2,1,0:T(4,128)}, f32[256,128]{1,0:T(8,128)}, f32[16,32,256]{2,1,0:T(8,128)}, f32[16,32,256]{2,1,0:T(8,128)}, f32[128,128]{1,0:T(8,1...) custom-call(s32[256]{0:T(256)} %fill_ref.1, ...), custom_call_target="tpu_custom_call" | custom-call | tf_op jit(solution)/shard_map/prepare/pallas_call | solution.py:436
  16.4 2.4 %collective-permute-start = (f32[640,128]{1,0:T(8,128)}, f32[640,128]{1,0:T(8,128)S(1)}, u32[]{:S(2)}, u32[]{:S(2)}) collective-permute-start(f32[640,128]{1,0:T(8,128)} %get-tuple-element.36), channel_id=1, source_target_pairs={{0,1},{1,2},{2,3},{3,4},{4,5},{5,6},{6,7},{8,9},{9,10},{10,11},{11... | collective-permute-start | bytes 983048 | tf_op jit(solution)/shard_map/ppermute | solution.py:774
  18.8 1.3 collective-permute-start.1
  20.1 6.8 %collective-permute-start.2 = (f32[128,128]{1,0:T(8,128)}, f32[128,128]{1,0:T(8,128)S(1)}, u32[]{:S(2)}, u32[]{:S(2)}) collective-permute-start(f32[128,128]{1,0:T(8,128)} %get-tuple-element.38), channel_id=1, source_target_pairs={{0,2},{1,3},{2,4},{3,5},{4,6},{5,7},{8,10},{9,11},{10,12},{11,13},... | collective-permute-start | bytes 196616 | tf_op jit(solution)/shard_map/ppermute | solution.py:774
  27.0 1.3 collective-permute-start.3
  28.3 3.4 %collective-permute-start.4 = (f32[128,128]{1,0:T(8,128)}, f32[128,128]{1,0:T(8,128)S(1)}, u32[]{:S(2)}, u32[]{:S(2)}) collective-permute-start(f32[128,128]{1,0:T(8,128)} %get-tuple-element.40), channel_id=1, source_target_pairs={{0,8},{8,16},{16,24},{1,9},{9,17},{17,25},{2,10},{10,18},{18,26},{... | collective-permute-start | bytes 196616 | tf_op jit(solution)/shard_map/ppermute | solution.py:774
  31.7 0.0 collective-permute-done.2.refs_8_
  31.7 1.3 collective-permute-start.5
  33.0 0.4 collective-permute-done.3.refs_9_
  33.3 0.5 collective-permute-done.4.refs_10_
  33.9 4.2 %collective-permute-done.5.refs_11_ = f32[128,128]{1,0:T(8,128)S(1)} collective-permute-done((f32[128,128]{1,0:T(8,128)}, f32[128,128]{1,0:T(8,128)S(1)}, u32[]{:S(2)}, u32[]{:S(2)}) %collective-permute-start.5) | collective-permute-done | bytes 65568 | tf_op jit(solution)/shard_map/ppermute | solution.py:774
  38.1 0.0 collective-permute-done.refs_6_.refs_4_
  38.1 0.0 collective-permute-done.1.refs_7_.refs_5_
  38.1 0.0 copy-done.1
  38.1 0.0 copy-done
  38.1 0.0 copy-start.2
  38.1 1.0 copy-done.2
  39.1 1.0 copy-done.4
  40.2 0.0 copy-start.10
  40.2 0.0 copy-start.19
  40.2 0.0 copy-start.22
  40.2 0.1 planes.1
  40.3 4.5 %collective-permute-start.6 = (f32[14,48,256]{2,1,0:T(8,128)S(1)}, f32[14,48,256]{2,1,0:T(8,128)S(1)}, u32[]{:S(2)}, u32[]{:S(2)}) collective-permute-start(f32[14,48,256]{2,1,0:T(8,128)S(1)} %get-tuple-element.55), channel_id=1, source_target_pairs={{0,8},{8,16},{16,24},{1,9},{9,17},{17,25},{2,10},{10,18},{18,26},{... | collective-permute-start | bytes 2064392 | tf_op jit(solution)/shard_map/ppermute | solution.py:774
  44.8 1.3 collective-permute-start.7
  46.1 0.0 copy-done.23
  46.1 0.0 copy-done.24
  46.1 0.0 copy-done.12
  46.1 0.0 copy-done.17
  46.1 0.0 copy-done.18
  46.2 0.0 copy-done.20
  46.2 0.0 copy-done.21
  46.2 0.0 copy-done.10
  46.2 0.0 copy-done.19
  46.2 70.4 %pair_forces.1 = (f32[1024,128]{1,0:T(8,128)S(1)}, f32[128,128]{1,0:T(8,128)S(1)}, f32[512,128]{1,0:T(8,128)S(1)}, f32[256,128]{1,0:T(8,128)S(1)}) custom-call(s32[1024]{0:T(1024)S(1)} %copy-done.21, s32[1024]{0:T(1024)S(1)} %multiply_add_fusion.other_rows_ref, bf16[128,256]{1,0:T(8,128)(2,1)S(1)} %copy-done.18, bf16[256,128]{1,0:T(8,128)(2,1)S(1)} %copy-done.17, ...), custom_call_target="tpu_custom_call" | custom-call | flops 335544320 | bytes 4194304 | tf_op jit(solution)/shard_map/pair_forces/pallas_call | solution.py:290
  116.6 0.0 copy-start.8
  116.7 0.8 copy-done.8
  117.4 0.7 copy-done.11
  118.1 0.6 copy-done.14
  118.8 0.6 copy-done.16
  119.4 0.0 collective-permute-done.6.refs_8_
  119.4 0.0 collective-permute-done.7.refs_9_
  119.4 0.9 copy-done.6
  120.3 0.0 all-gather.4.cloned.1.call-update
  120.3 0.0 copy-done.3
  120.3 0.0 copy-done.5
  120.3 0.0 copy-done.22
  120.3 0.0 copy-start.7
  120.3 1.1 copy-done.7
  121.4 0.9 copy-done.13
  122.3 18.7 %grid_step.1 = (f32[16,32,256]{2,1,0:T(8,128)}, f32[16,32,256]{2,1,0:T(8,128)}, f32[1024,128]{1,0:T(8,128)S(1)}) custom-call(s32[256]{0:T(256)S(1)} %copy-done.22, f32[256,128]{1,0:T(8,128)S(1)} %copy-done.13, f32[16,32,256]{2,1,0:T(8,128)S(1)} %copy-done.1, f32[16,32,256]{2,1,0:T(8,128)S(1)} %copy-done.3, f32[16,32,256]{2,1,0:T(8,128)S(1)} %copy-done.5, ...), custom_call_target="tpu_custom_call" | custom-call | flops 31948800 | bytes 8388608 | tf_op jit(solution)/shard_map/grid_step/pallas_call | solution.py:679
  141.0 0.8 copy-done.9
  141.8 0.0 copy-done.15
  141.8 12.3 %all-gather.1 = f32[1024,128]{1,0:T(8,128)} all-gather(f32[256,128]{1,0:T(8,128)S(1)} %copy-done.15), channel_id=3, replica_groups=mesh['grp'=4,'brick'=8] {'grp'}, dimensions={0}, use_global_device_ids=true | all-gather | bytes 655360 | tf_op jit(solution)/shard_map/all_gather | solution.py:827
  154.1 4.3 %gather_forces.1 = f32[3,32768]{1,0:T(4,128)} custom-call(s32[7,32]{1,0:T(8,128)} %send_index_ref.3, f32[256,4,128]{2,1,0:T(4,128)} %bitcast.7, f32[256,4,128]{2,1,0:T(4,128)} %bitcast.8, f32[32,4,128]{2,1,0:T(4,128)} %bitcast.10, f32[1024,4,128]{2,1,0:T(4,128)} %bitcast.12, f32[256,4,128]{2,1,0:T(4,128)} %bitcast.11), custom_call_target="tpu_custom_call" | custom-call | tf_op jit(solution)/shard_map/gather_forces/pallas_call | solution.py:756
  (12 shorter events, 0.0 us)
Async XLA Ops:
  7.2 30.9 %copy-start.1 = (f32[16,32,256]{2,1,0:T(8,128)S(1)}, f32[16,32,256]{2,1,0:T(8,128)}, u32[]{:S(2)}) copy-start(f32[16,32,256]{2,1,0:T(8,128)} %refs_2_.2) | copy-start | bytes 1572868
  7.2 30.9 %copy-start = (f32[16,32,256]{2,1,0:T(8,128)S(1)}, f32[16,32,256]{2,1,0:T(8,128)}, u32[]{:S(2)}) copy-start(f32[16,32,256]{2,1,0:T(8,128)} %refs_5_.1) | copy-start | bytes 1572868
  7.2 147.0 %all-gather.4.cloned.1.call-start = ((), (), s32[]{:S(2)}) async-start(), calls=%async_computation | async-start | bytes 2359296 | tf_op jit(solution)/shard_map/all_gather | solution.py:826
  7.2 38.9 %copy-start.23 = (s32[1024]{0:T(1024)S(1)}, s32[1024]{0:T(1024)}, u32[]{:S(2)}) copy-start(s32[1024]{0:T(1024)} %param.24) | copy-start | bytes 12292
  7.2 38.9 %copy-start.24 = (s32[1024]{0:T(1024)S(1)}, s32[1024]{0:T(1024)}, u32[]{:S(2)}) copy-start(s32[1024]{0:T(1024)} %param.23) | copy-start | bytes 12292
  7.3 38.9 %copy-start.12 = (bf16[128,1024]{1,0:T(8,128)(2,1)S(1)}, bf16[128,1024]{1,0:T(8,128)(2,1)}, u32[]{:S(2)}) copy-start(bf16[128,1024]{1,0:T(8,128)(2,1)} %constant.13.clone.refs_3_) | copy-start | bytes 786436
  7.3 38.9 %copy-start.17 = (bf16[256,128]{1,0:T(8,128)(2,1)S(1)}, bf16[256,128]{1,0:T(8,128)(2,1)}, u32[]{:S(2)}) copy-start(bf16[256,128]{1,0:T(8,128)(2,1)} %constant.11.clone.refs_1_) | copy-start | bytes 196612
  7.3 38.9 %copy-start.18 = (bf16[128,256]{1,0:T(8,128)(2,1)S(1)}, bf16[128,256]{1,0:T(8,128)(2,1)}, u32[]{:S(2)}) copy-start(bf16[128,256]{1,0:T(8,128)(2,1)} %constant.10.clone.refs_0_) | copy-start | bytes 196612
  7.3 38.9 %copy-start.20 = (bf16[128,128]{1,0:T(8,128)(2,1)S(1)}, bf16[128,128]{1,0:T(8,128)(2,1)}, u32[]{:S(2)}) copy-start(bf16[128,128]{1,0:T(8,128)(2,1)} %constant.12.clone.refs_2_) | copy-start | bytes 98308
  7.3 38.9 %copy-start.21 = (s32[1024]{0:T(1024)S(1)}, s32[1024]{0:T(1024)}, u32[]{:S(2)}) copy-start(s32[1024]{0:T(1024)} %own_rows_ref.1) | copy-start | bytes 12292
  16.4 21.6 %collective-permute-start = (f32[640,128]{1,0:T(8,128)}, f32[640,128]{1,0:T(8,128)S(1)}, u32[]{:S(2)}, u32[]{:S(2)}) collective-permute-start(f32[640,128]{1,0:T(8,128)} %get-tuple-element.36), channel_id=1, source_target_pairs={{0,1},{1,2},{2,3},{3,4},{4,5},{5,6},{6,7},{8,9},{9,10},{10,11},{11... | collective-permute-start | bytes 983048 | tf_op jit(solution)/shard_map/ppermute | solution.py:774
  18.8 19.2 %collective-permute-start.1 = (f32[640,128]{1,0:T(8,128)}, f32[640,128]{1,0:T(8,128)S(1)}, u32[]{:S(2)}, u32[]{:S(2)}) collective-permute-start(f32[640,128]{1,0:T(8,128)} %get-tuple-element.37), channel_id=1, source_target_pairs={{1,0},{2,1},{3,2},{4,3},{5,4},{6,5},{7,6},{9,8},{10,9},{11,10},{12... | collective-permute-start | bytes 983048 | tf_op jit(solution)/shard_map/ppermute | solution.py:774
  20.1 11.5 %collective-permute-start.2 = (f32[128,128]{1,0:T(8,128)}, f32[128,128]{1,0:T(8,128)S(1)}, u32[]{:S(2)}, u32[]{:S(2)}) collective-permute-start(f32[128,128]{1,0:T(8,128)} %get-tuple-element.38), channel_id=1, source_target_pairs={{0,2},{1,3},{2,4},{3,5},{4,6},{5,7},{8,10},{9,11},{10,12},{11,13},... | collective-permute-start | bytes 196616 | tf_op jit(solution)/shard_map/ppermute | solution.py:774
  27.0 6.4 %collective-permute-start.3 = (f32[128,128]{1,0:T(8,128)}, f32[128,128]{1,0:T(8,128)S(1)}, u32[]{:S(2)}, u32[]{:S(2)}) collective-permute-start(f32[128,128]{1,0:T(8,128)} %get-tuple-element.39), channel_id=1, source_target_pairs={{2,0},{3,1},{4,2},{5,3},{6,4},{7,5},{10,8},{11,9},{12,10},{13,11},... | collective-permute-start | bytes 196616 | tf_op jit(solution)/shard_map/ppermute | solution.py:774
  28.3 5.6 %collective-permute-start.4 = (f32[128,128]{1,0:T(8,128)}, f32[128,128]{1,0:T(8,128)S(1)}, u32[]{:S(2)}, u32[]{:S(2)}) collective-permute-start(f32[128,128]{1,0:T(8,128)} %get-tuple-element.40), channel_id=1, source_target_pairs={{0,8},{8,16},{16,24},{1,9},{9,17},{17,25},{2,10},{10,18},{18,26},{... | collective-permute-start | bytes 196616 | tf_op jit(solution)/shard_map/ppermute | solution.py:774
  31.7 6.4 %collective-permute-start.5 = (f32[128,128]{1,0:T(8,128)}, f32[128,128]{1,0:T(8,128)S(1)}, u32[]{:S(2)}, u32[]{:S(2)}) collective-permute-start(f32[128,128]{1,0:T(8,128)} %get-tuple-element.41), channel_id=1, source_target_pairs={{8,0},{16,8},{24,16},{9,1},{17,9},{25,17},{10,2},{18,10},{26,18},{... | collective-permute-start | bytes 196616 | tf_op jit(solution)/shard_map/ppermute | solution.py:774
  38.1 1.0 copy-start.2
  39.1 1.0 copy-start.4
  40.2 6.0 %copy-start.10 = (f32[256,4,128]{2,1,0:T(4,128)S(1)}, f32[256,4,128]{2,1,0:T(4,128)}, u32[]{:S(2)}) copy-start(f32[256,4,128]{2,1,0:T(4,128)} %get-tuple-element.34) | copy-start | bytes 1572868
  40.2 6.0 %copy-start.19 = (f32[128,128]{1,0:T(8,128)S(1)}, f32[128,128]{1,0:T(8,128)}, u32[]{:S(2)}) copy-start(f32[128,128]{1,0:T(8,128)} %get-tuple-element.42.refs_5_) | copy-start | bytes 196612
  40.2 80.1 %copy-start.3 = (f32[16,32,256]{2,1,0:T(8,128)S(1)}, f32[16,32,256]{2,1,0:T(8,128)}, u32[]{:S(2)}) copy-start(f32[16,32,256]{2,1,0:T(8,128)} %get-tuple-element.51.refs_1_.refs_3_) | copy-start | bytes 1572868
  40.2 80.1 %copy-start.5 = (f32[16,32,256]{2,1,0:T(8,128)S(1)}, f32[16,32,256]{2,1,0:T(8,128)}, u32[]{:S(2)}) copy-start(f32[16,32,256]{2,1,0:T(8,128)} %get-tuple-element.52.refs_2_.refs_4_) | copy-start | bytes 1572868
  40.2 80.1 %copy-start.22 = (s32[256]{0:T(256)S(1)}, s32[256]{0:T(256)}, u32[]{:S(2)}) copy-start(s32[256]{0:T(256)} %refs_0_.4) | copy-start | bytes 3076
  40.3 79.1 %collective-permute-start.6 = (f32[14,48,256]{2,1,0:T(8,128)S(1)}, f32[14,48,256]{2,1,0:T(8,128)S(1)}, u32[]{:S(2)}, u32[]{:S(2)}) collective-permute-start(f32[14,48,256]{2,1,0:T(8,128)S(1)} %get-tuple-element.55), channel_id=1, source_target_pairs={{0,8},{8,16},{16,24},{1,9},{9,17},{17,25},{2,10},{10,18},{18,26},{... | collective-permute-start | bytes 2064392 | tf_op jit(solution)/shard_map/ppermute | solution.py:774
  44.8 74.6 %collective-permute-start.7 = (f32[14,48,256]{2,1,0:T(8,128)S(1)}, f32[14,48,256]{2,1,0:T(8,128)S(1)}, u32[]{:S(2)}, u32[]{:S(2)}) collective-permute-start(f32[14,48,256]{2,1,0:T(8,128)S(1)} %get-tuple-element.56), channel_id=1, source_target_pairs={{8,0},{16,8},{24,16},{9,1},{17,9},{25,17},{10,2},{18,10},{26,18},{... | collective-permute-start | bytes 2064392 | tf_op jit(solution)/shard_map/ppermute | solution.py:774
  116.6 0.8 copy-start.8
  117.4 0.7 copy-start.11
  118.1 0.6 copy-start.14
  118.8 0.6 copy-start.16
  119.4 0.9 copy-start.6
  120.3 1.1 copy-start.7
  121.4 0.9 copy-start.13
  122.3 19.5 %copy-start.15 = (f32[256,128]{1,0:T(8,128)S(1)}, f32[256,128]{1,0:T(8,128)}, u32[]{:S(2)}) copy-start(f32[256,128]{1,0:T(8,128)} %copy-done.14) | copy-start | bytes 393220
  141.0 0.8 copy-start.9
Sparse Core Ops, SparseCore 0:
  120.4 31.5 all-gather.3

commit v9 on v7

--- a/solution.py
+++ b/solution.py
@@ -52,25 +52,20 @@
     far_kinds += [12, 12, 12, 9, 10, 11]
     near = np.zeros((128, 256), np.float32)
     far = np.zeros((256, 128), np.float32)
-    own_moment = np.zeros((128, 128), np.float32)
-    other_moment = np.zeros((128, QUAD * 256), np.float32)
+    moment = np.zeros((128, 128), np.float32)
     for cluster in range(8):
         for index, kind in enumerate(near_kinds):
             near[kind * 8 + cluster, cluster * 32 + index] = 1.0
         for index, kind in enumerate(far_kinds):
             far[cluster * 32 + index, kind * 8 + cluster] = 1.0
         for kind in range(12):
-            own_moment[cluster * 16 + kind, kind * 8 + cluster] = 1.0
-            for turn in range(QUAD):
-                lane = (cluster % QUAD + turn) % QUAD * 32 + kind
-                column = turn * 256 + cluster // QUAD * 128 + lane
-                other_moment[kind * 8 + cluster, column] = 1.0
-    return tuple(jnp.asarray(part, jnp.bfloat16) for part in (near, far, own_moment, other_moment))
+            moment[cluster * 16 + kind, kind * 8 + cluster] = 1.0
+    return tuple(jnp.asarray(part, jnp.bfloat16) for part in (near, far, moment))
 
 
 def pair_kernel(own_rows_ref, other_rows_ref, *refs):
-    near_sel_ref, far_sel_ref, own_moment_sel_ref, other_moment_sel_ref, own_ref = refs[:5]
-    refs = refs[5:]
+    near_sel_ref, far_sel_ref, moment_sel_ref, own_ref = refs[:4]
+    refs = refs[4:]
     sources = (len(refs) - 11) // 2
     other_refs = refs[:sources]
     own_out_ref = refs[sources]
@@ -89,7 +84,6 @@
     others = slots * sources
     groups = own_rows_ref.shape[0] // UNROLL
     units = UNROLL // QUAD
-    groups_of_other = others // QUAD
     ones = jnp.ones((8, 128), jnp.float32)
     zeros = jnp.zeros((8, 128), jnp.float32)
 
@@ -115,7 +109,7 @@
         *comps, charge = components(own_ref, start)
         moments = jnp.concatenate(moment_pieces(comps, charge) + [zeros] * 4, axis=0)
         own_moment_ref[pl.ds(pl.multiple_of(start * 16, 128), 128), :] = selected(
-            own_moment_sel_ref[...], moments.astype(jnp.bfloat16)
+            moment_sel_ref[...], moments.astype(jnp.bfloat16)
         )
         tiles = selected(place_pieces(comps, 1.0, 0.0).T, near_sel_ref[...])
         for half in range(2):
@@ -133,14 +127,9 @@
             far_ref[pl.ds(at, 96), :] = jnp.zeros((96, 128), jnp.bfloat16)
             far_ref[pl.ds(at + 96, 32), :] = rows[32 * index : 32 * index + 32]
         moments = jnp.concatenate(moment_pieces(comps, charge) + [zeros] * 4, axis=0)
-        tiles = selected(moments.T, other_moment_sel_ref[...])
-        for turn in range(QUAD):
-            for half in range(2):
-                group = turn * groups_of_other + source * (slots // QUAD) + step * 2 + half
-                column = 256 * turn + 128 * half
-                other_moment_ref[pl.ds(pl.multiple_of(group * 128, 128), 128), :] = tiles[
-                    :, column : column + 128
-                ]
+        other_moment_ref[pl.ds(pl.multiple_of(start * 16, 128), 128), :] = selected(
+            moment_sel_ref[...], moments.astype(jnp.bfloat16)
+        )
         return 0
 
     lax.fori_loop(0, clusters // 8, near_rows, 0, unroll=2)
@@ -152,9 +141,6 @@
     dist_refs, weight_refs = (passed_refs[:2], passed_refs[2:])
     dist_refs[0][...] = jnp.full(dist_refs[0].shape, 1e38, jnp.float32)
     weight_refs[0][...] = jnp.zeros_like(weight_refs[0])
-
-    quarter_row = lax.shift_right_logical(lax.broadcasted_iota(jnp.int32, (1, 128), 1), 5)
-    masks = [jnp.where(quarter_row == turn, 1.0, 0.0).astype(jnp.bfloat16) for turn in range(QUAD)]
 
     def block_diagonal(blocks):
         blank = jnp.zeros_like(blocks[0])
@@ -191,10 +177,10 @@
             weight - high.astype(jnp.float32)
         ).astype(jnp.bfloat16)
 
-    def turned(index, turn):
-        rotation = lax.bitwise_and(turn - index, 3)
-        group = rotation * groups_of_other + lax.shift_right_logical(index, 2)
-        return other_moment_ref[pl.ds(pl.multiple_of(group * 128, 128), 128), :] * masks[turn]
+    def moments_of(moment_ref, indices):
+        return block_diagonal(
+            [moment_ref[pl.ds(pl.multiple_of(index * 16, 16), 16), :] for index in indices]
+        )
 
     def products(pair, unit, weight_ref):
         owns = [own_rows_ref[pair + turn] for turn in range(QUAD)]
@@ -206,20 +192,16 @@
             )
             for lanes in (slice(0, 128), slice(128, 256))
         ]
-        columns = jnp.concatenate([turned(others[turn], turn) for turn in range(QUAD)], axis=0)
-        to_own = jnp.dot(
-            jnp.concatenate(levels, axis=0), columns, preferred_element_type=jnp.float32
-        )
-        rows = block_diagonal(
-            [own_moment_ref[pl.ds(pl.multiple_of(own * 16, 16), 16), :] for own in owns]
-        )
-        to_other = jnp.dot(rows, both, preferred_element_type=jnp.float32)
-        return (
-            owns,
-            others,
-            (to_own[:128] + to_own[128:]).T,
-            to_other[:, :128] + to_other[:, 128:],
-        )
+        to_own = lax.dot_general(
+            moments_of(other_moment_ref, others),
+            jnp.concatenate(levels, axis=0),
+            (((1,), (1,)), ((), ())),
+            preferred_element_type=jnp.float32,
+        )
+        to_other = jnp.dot(
+            moments_of(own_moment_ref, owns), both, preferred_element_type=jnp.float32
+        )
+        return (owns, others, *(part[:, :128] + part[:, 128:] for part in (to_own, to_other)))
 
     def half_step(step, side):
         last = jnp.maximum(step - 2, 0) * UNROLL
@@ -234,7 +216,7 @@
             for turn in range(QUAD):
                 own_at = pl.ds(pl.multiple_of(owns[turn] * 16, 16), 16)
                 other_at = pl.ds(pl.multiple_of(others[turn] * 16, 16), 16)
-                own_sum_ref[own_at, :] += to_own[32 * turn : 32 * turn + 16]
+                own_sum_ref[own_at, :] += to_own[16 * turn : 16 * turn + 16]
                 other_sum_ref[other_at, :] += to_other[16 * turn : 16 * turn + 16]
 
     def visit(step, _):
@@ -288,13 +270,13 @@
             jax.ShapeDtypeStruct(own.shape, jnp.float32),
             *[jax.ShapeDtypeStruct((slots * 4, 128), jnp.float32)] * len(arrived),
         ),
-        in_specs=[smem, smem] + [vmem] * (5 + len(arrived)),
+        in_specs=[smem, smem] + [vmem] * (4 + len(arrived)),
         out_specs=(vmem,) * (len(arrived) + 1),
         scratch_shapes=[
             pltpu.VMEM((clusters * 32, 128), jnp.bfloat16),
             pltpu.VMEM(((others + 1) * 128, 128), jnp.bfloat16),
             pltpu.VMEM((clusters * 16, 128), jnp.bfloat16),
-            pltpu.VMEM((others * 128, 128), jnp.bfloat16),
+            pltpu.VMEM((others * 16, 128), jnp.bfloat16),
             pltpu.VMEM((clusters * 16, 128), jnp.float32),
             pltpu.VMEM((others * 16, 128), jnp.float32),
             *[pltpu.VMEM((UNROLL // QUAD, 128, 128 * QUAD), jnp.float32)] * 2,

time: 152 us -> 147 us (0.967)
  Pallas kernels: 101 us -> 96.7 us
    pallas_call x1, Pallas kernels: 70.5 us -> 66 us  [pair_forces(): pl.pallas_call(pair_kernel, out_shape=(jax.ShapeDtypeStruct(own.shape, jn...]
    unnamed x36 -> x34, local copies, waits for them, and re-layouts: 3.44 us -> 3.44 us
  transfers between devices with their start and end apart: 14 -> 14, of which waited for: 1 -> 1; matrix products, arithmetic and copies ran while one was open for 0% -> 0% of each run, Pallas kernels for 59% -> 58%
where the time goes in v9:
time: 147 us
  Pallas kernels  96.7 us (66%)
  starting transfers between devices  43.3 us (29%)
  local copies, waits for them, and re-layouts  3.44 us (2%)
  waiting for transfers between devices  2.16 us (1%)
    pallas_call x1, Pallas kernels, pair_forces(): pl.pallas_call(pair_kernel, out_shape=(jax.ShapeDtypeStruct(own.shape, jn...  66 us
    ppermute x14, starting transfers between devices, passed_along(): return lax.ppermute(shard, axis, pairs)  43.3 us
    pallas_call x1, Pallas kernels, grid_step(): pl.pallas_call(functools.partial(grid_kernel, base), out_shape=(jax.Shape...  18.7 us
    pallas_call x1, Pallas kernels, prepare(): pl.pallas_call(prepare_kernel, out_shape=(jax.ShapeDtypeStruct((clusters,...  9.11 us
    unnamed x34, local copies, waits for them, and re-layouts  3.44 us
  transfers between devices with their start and end apart: 14, of which 1 were waited for; matrix products, arithmetic and copies ran while one was open for 0% of the time, Pallas kernels for 58%

profile of v9, /device:TPU:13, one launch (start us, length us, event | category | flops | bytes accessed | tf_op | source)
XLA Modules:
  0.0 146.6 jit_solution(11827720159275282129)
XLA Ops:
  0.6 0.0 copy-start
  0.6 0.0 copy-start.1
  0.7 9.1 %prepare.1 = (f32[256,4,128]{2,1,0:T(4,128)}, f32[256,128]{1,0:T(8,128)}, f32[16,32,256]{2,1,0:T(8,128)}, f32[16,32,256]{2,1,0:T(8,128)}, f32[128,128]{1,0:T(8,1...) custom-call(s32[256]{0:T(256)} %fill_ref.1, ...), custom_call_target="tpu_custom_call" | custom-call | tf_op jit(solution)/shard_map/prepare/pallas_call | solution.py:413
  9.8 3.8 %collective-permute-start = (f32[640,128]{1,0:T(8,128)}, f32[640,128]{1,0:T(8,128)S(1)}, u32[]{:S(2)}, u32[]{:S(2)}) collective-permute-start(f32[640,128]{1,0:T(8,128)} %get-tuple-element.36), channel_id=1, source_target_pairs={{0,1},{1,2},{2,3},{3,4},{4,5},{5,6},{6,7},{8,9},{9,10},{10,11},{11... | collective-permute-start | bytes 983048 | tf_op jit(solution)/shard_map/ppermute | solution.py:717
  13.5 1.9 %collective-permute-start.1 = (f32[640,128]{1,0:T(8,128)}, f32[640,128]{1,0:T(8,128)S(1)}, u32[]{:S(2)}, u32[]{:S(2)}) collective-permute-start(f32[640,128]{1,0:T(8,128)} %get-tuple-element.37), channel_id=1, source_target_pairs={{1,0},{2,1},{3,2},{4,3},{5,4},{6,5},{7,6},{9,8},{10,9},{11,10},{12... | collective-permute-start | bytes 983048 | tf_op jit(solution)/shard_map/ppermute | solution.py:717
  15.5 3.2 %collective-permute-start.2 = (f32[128,128]{1,0:T(8,128)}, f32[128,128]{1,0:T(8,128)S(1)}, u32[]{:S(2)}, u32[]{:S(2)}) collective-permute-start(f32[128,128]{1,0:T(8,128)} %get-tuple-element.38), channel_id=1, source_target_pairs={{0,2},{1,3},{2,4},{3,5},{4,6},{5,7},{8,10},{9,11},{10,12},{11,13},... | collective-permute-start | bytes 196616 | tf_op jit(solution)/shard_map/ppermute | solution.py:717
  18.7 2.1 %collective-permute-start.3 = (f32[128,128]{1,0:T(8,128)}, f32[128,128]{1,0:T(8,128)S(1)}, u32[]{:S(2)}, u32[]{:S(2)}) collective-permute-start(f32[128,128]{1,0:T(8,128)} %get-tuple-element.39), channel_id=1, source_target_pairs={{2,0},{3,1},{4,2},{5,3},{6,4},{7,5},{10,8},{11,9},{12,10},{13,11},... | collective-permute-start | bytes 196616 | tf_op jit(solution)/shard_map/ppermute | solution.py:717
  20.8 3.1 %collective-permute-start.4 = (f32[128,128]{1,0:T(8,128)}, f32[128,128]{1,0:T(8,128)S(1)}, u32[]{:S(2)}, u32[]{:S(2)}) collective-permute-start(f32[128,128]{1,0:T(8,128)} %get-tuple-element.40), channel_id=1, source_target_pairs={{0,8},{8,16},{16,24},{1,9},{9,17},{17,25},{2,10},{10,18},{18,26},{... | collective-permute-start | bytes 196616 | tf_op jit(solution)/shard_map/ppermute | solution.py:717
  23.9 0.0 collective-permute-done.2.refs_7_
  23.9 3.1 %collective-permute-start.5 = (f32[128,128]{1,0:T(8,128)}, f32[128,128]{1,0:T(8,128)S(1)}, u32[]{:S(2)}, u32[]{:S(2)}) collective-permute-start(f32[128,128]{1,0:T(8,128)} %get-tuple-element.41), channel_id=1, source_target_pairs={{8,0},{16,8},{24,16},{9,1},{17,9},{25,17},{10,2},{18,10},{26,18},{... | collective-permute-start | bytes 196616 | tf_op jit(solution)/shard_map/ppermute | solution.py:717
  27.0 0.0 collective-permute-done.3.refs_8_
  27.0 0.0 collective-permute-done.4.refs_9_
  27.0 2.1 %collective-permute-done.5.refs_10_ = f32[128,128]{1,0:T(8,128)S(1)} collective-permute-done((f32[128,128]{1,0:T(8,128)}, f32[128,128]{1,0:T(8,128)S(1)}, u32[]{:S(2)}, u32[]{:S(2)}) %collective-permute-start.5) | collective-permute-done | bytes 65568 | tf_op jit(solution)/shard_map/ppermute | solution.py:717
  29.1 0.0 collective-permute-done.refs_5_.refs_4_.refs_6_
  29.1 0.0 collective-permute-done.1.refs_6_.refs_5_.refs_7_
  29.1 0.0 copy-done
  29.1 0.0 copy-done.1
  29.1 0.0 copy-start.2
  29.2 1.0 copy-done.2
  30.2 0.0 copy-start.4
  30.2 1.0 copy-done.4
  31.2 0.0 copy-start.15
  31.2 0.0 copy-start.16
  31.2 0.0 copy-start.6
  31.2 0.0 copy-start.8
  31.2 0.0 copy-start.9
  31.3 0.0 copy-start.10
  31.3 0.0 copy-start.11
  31.3 0.1 planes.1
  31.4 2.1 %collective-permute-start.6 = (f32[14,48,256]{2,1,0:T(8,128)S(1)}, f32[14,48,256]{2,1,0:T(8,128)S(1)}, u32[]{:S(2)}, u32[]{:S(2)}) collective-permute-start(f32[14,48,256]{2,1,0:T(8,128)S(1)} %get-tuple-element.53), channel_id=1, source_target_pairs={{0,8},{8,16},{16,24},{1,9},{9,17},{17,25},{2,10},{10,18},{18,26},{... | collective-permute-start | bytes 2064392 | tf_op jit(solution)/shard_map/ppermute | solution.py:717
  33.5 4.3 %collective-permute-start.7 = (f32[14,48,256]{2,1,0:T(8,128)S(1)}, f32[14,48,256]{2,1,0:T(8,128)S(1)}, u32[]{:S(2)}, u32[]{:S(2)}) collective-permute-start(f32[14,48,256]{2,1,0:T(8,128)S(1)} %get-tuple-element.54), channel_id=1, source_target_pairs={{8,0},{16,8},{24,16},{9,1},{17,9},{25,17},{10,2},{18,10},{26,18},{... | collective-permute-start | bytes 2064392 | tf_op jit(solution)/shard_map/ppermute | solution.py:717
  37.8 0.0 copy-done.15
  37.8 0.0 copy-done.16
  37.8 0.0 copy-start.13
  37.8 0.0 copy-done.6
  37.8 0.0 copy-done.8
  37.8 0.0 copy-done.9
  37.8 0.0 copy-done.10
  37.8 0.0 copy-done.11
  37.8 0.6 copy-done.13
  38.5 66.0 %pair_forces.1 = (f32[1024,128]{1,0:T(8,128)S(1)}, f32[128,128]{1,0:T(8,128)S(1)}, f32[128,128]{1,0:T(8,128)S(1)}, f32[128,128]{1,0:T(8,128)S(1)}, f32[128,128]{...) custom-call(s32[1024]{0:T(1024)S(1)} %copy-done.13, ...), custom_call_target="tpu_custom_call" | custom-call | flops 335544320 | bytes 4194304 | tf_op jit(solution)/shard_map/pair_forces/pallas_call | solution.py:267
  104.5 1.9 %collective-permute-start.13 = (f32[128,128]{1,0:T(8,128)S(1)}, f32[128,128]{1,0:T(8,128)S(1)}, u32[]{:S(2)}, u32[]{:S(2)}) collective-permute-start(f32[128,128]{1,0:T(8,128)S(1)} %get-tuple-element.62), channel_id=1, source_target_pairs={{0,8},{8,16},{16,24},{1,9},{9,17},{17,25},{2,10},{10,18},{18,26},{... | collective-permute-start | bytes 196616 | tf_op jit(solution)/shard_map/ppermute | solution.py:717
  106.4 5.1 %collective-permute-start.8 = (f32[128,128]{1,0:T(8,128)S(1)}, f32[128,128]{1,0:T(8,128)S(1)}, u32[]{:S(2)}, u32[]{:S(2)}) collective-permute-start(f32[128,128]{1,0:T(8,128)S(1)} %get-tuple-element.57), channel_id=1, source_target_pairs={{1,0},{2,1},{3,2},{4,3},{5,4},{6,5},{7,6},{9,8},{10,9},{11,10},{12... | collective-permute-start | bytes 196616 | tf_op jit(solution)/shard_map/ppermute | solution.py:717
  111.5 3.0 %collective-permute-start.9 = (f32[128,128]{1,0:T(8,128)S(1)}, f32[128,128]{1,0:T(8,128)S(1)}, u32[]{:S(2)}, u32[]{:S(2)}) collective-permute-start(f32[128,128]{1,0:T(8,128)S(1)} %get-tuple-element.58), channel_id=1, source_target_pairs={{0,1},{1,2},{2,3},{3,4},{4,5},{5,6},{6,7},{8,9},{9,10},{10,11},{11... | collective-permute-start | bytes 196616 | tf_op jit(solution)/shard_map/ppermute | solution.py:717
  114.5 0.0 collective-permute-done.13
  114.5 2.2 %collective-permute-start.10 = (f32[128,128]{1,0:T(8,128)S(1)}, f32[128,128]{1,0:T(8,128)S(1)}, u32[]{:S(2)}, u32[]{:S(2)}) collective-permute-start(f32[128,128]{1,0:T(8,128)S(1)} %get-tuple-element.59), channel_id=1, source_target_pairs={{2,0},{3,1},{4,2},{5,3},{6,4},{7,5},{10,8},{11,9},{12,10},{13,11},... | collective-permute-start | bytes 196616 | tf_op jit(solution)/shard_map/ppermute | solution.py:717
  116.7 0.0 collective-permute-done.6.refs_8_
  116.7 3.1 %collective-permute-start.11 = (f32[128,128]{1,0:T(8,128)S(1)}, f32[128,128]{1,0:T(8,128)S(1)}, u32[]{:S(2)}, u32[]{:S(2)}) collective-permute-start(f32[128,128]{1,0:T(8,128)S(1)} %get-tuple-element.60), channel_id=1, source_target_pairs={{0,2},{1,3},{2,4},{3,5},{4,6},{5,7},{8,10},{9,11},{10,12},{11,13},... | collective-permute-start | bytes 196616 | tf_op jit(solution)/shard_map/ppermute | solution.py:717
  119.8 0.0 collective-permute-done.7.refs_9_
  119.8 0.0 copy-start.14
  119.8 4.5 %collective-permute-start.12 = (f32[128,128]{1,0:T(8,128)S(1)}, f32[128,128]{1,0:T(8,128)S(1)}, u32[]{:S(2)}, u32[]{:S(2)}) collective-permute-start(f32[128,128]{1,0:T(8,128)S(1)} %get-tuple-element.61), channel_id=1, source_target_pairs={{8,0},{16,8},{24,16},{9,1},{17,9},{25,17},{10,2},{18,10},{26,18},{... | collective-permute-start | bytes 196616 | tf_op jit(solution)/shard_map/ppermute | solution.py:717
  124.4 0.0 copy-done.3
  124.4 0.0 copy-done.5
  124.4 0.0 copy-done.7
  124.4 0.0 copy-done.14
  124.4 18.7 %grid_step.1 = (f32[16,32,256]{2,1,0:T(8,128)}, f32[16,32,256]{2,1,0:T(8,128)}, f32[1024,128]{1,0:T(8,128)S(1)}) custom-call(s32[256]{0:T(256)S(1)} %copy-done.14, f32[256,128]{1,0:T(8,128)S(1)} %copy-done.7, f32[16,32,256]{2,1,0:T(8,128)S(1)} %copy-done.1, f32[16,32,256]{2,1,0:T(8,128)S(1)} %copy-done.3, f32[16,32,256]{2,1,0:T(8,128)S(1)} %copy-done.5, ...), custom_call_target="tpu_custom_call" | custom-call | flops 31948800 | bytes 8388608 | tf_op jit(solution)/shard_map/grid_step/pallas_call | solution.py:656
  143.1 0.0 collective-permute-done.8
  143.1 0.0 collective-permute-done.9
  143.1 0.0 collective-permute-done.10
  143.1 0.0 collective-permute-done.11
  143.1 0.0 collective-permute-done.12
  143.1 0.0 copy-start.12
  143.2 0.7 copy-done.12
  143.8 2.8 %gather_forces.1 = f32[3,32768]{1,0:T(4,128)} custom-call(s32[7,32]{1,0:T(8,128)S(1)} %copy-done.12, f32[256,4,128]{2,1,0:T(4,128)S(1)} %bitcast.12, f32[256,4,128]{2,1,0:T(4,128)S(1)} %bitcast.13, f32[32,4,128]{2,1,0:T(4,128)S(1)} %bitcast.14, f32[32,4,128]{2,1,0:T(4,128)S(1)} %bitcast.16, f32[32,4,128]{2,1,0:T(4,128)S(1)} %bitcast.17, ...), custom_call_target="tpu_custom_call" | custom-call | tf_op jit(solution)/shard_map/gather_forces/pallas_call | solution.py:703
  (4 shorter events, 0.0 us)
Async XLA Ops:
  0.6 28.5 %copy-start = (f32[16,32,256]{2,1,0:T(8,128)S(1)}, f32[16,32,256]{2,1,0:T(8,128)}, u32[]{:S(2)}) copy-start(f32[16,32,256]{2,1,0:T(8,128)} %refs_5_.1) | copy-start | bytes 1572868
  0.6 28.5 %copy-start.1 = (f32[16,32,256]{2,1,0:T(8,128)S(1)}, f32[16,32,256]{2,1,0:T(8,128)}, u32[]{:S(2)}) copy-start(f32[16,32,256]{2,1,0:T(8,128)} %refs_2_.2) | copy-start | bytes 1572868
  9.8 19.4 %collective-permute-start = (f32[640,128]{1,0:T(8,128)}, f32[640,128]{1,0:T(8,128)S(1)}, u32[]{:S(2)}, u32[]{:S(2)}) collective-permute-start(f32[640,128]{1,0:T(8,128)} %get-tuple-element.36), channel_id=1, source_target_pairs={{0,1},{1,2},{2,3},{3,4},{4,5},{5,6},{6,7},{8,9},{9,10},{10,11},{11... | collective-permute-start | bytes 983048 | tf_op jit(solution)/shard_map/ppermute | solution.py:717
  13.5 15.6 %collective-permute-start.1 = (f32[640,128]{1,0:T(8,128)}, f32[640,128]{1,0:T(8,128)S(1)}, u32[]{:S(2)}, u32[]{:S(2)}) collective-permute-start(f32[640,128]{1,0:T(8,128)} %get-tuple-element.37), channel_id=1, source_target_pairs={{1,0},{2,1},{3,2},{4,3},{5,4},{6,5},{7,6},{9,8},{10,9},{11,10},{12... | collective-permute-start | bytes 983048 | tf_op jit(solution)/shard_map/ppermute | solution.py:717
  15.5 8.4 %collective-permute-start.2 = (f32[128,128]{1,0:T(8,128)}, f32[128,128]{1,0:T(8,128)S(1)}, u32[]{:S(2)}, u32[]{:S(2)}) collective-permute-start(f32[128,128]{1,0:T(8,128)} %get-tuple-element.38), channel_id=1, source_target_pairs={{0,2},{1,3},{2,4},{3,5},{4,6},{5,7},{8,10},{9,11},{10,12},{11,13},... | collective-permute-start | bytes 196616 | tf_op jit(solution)/shard_map/ppermute | solution.py:717
  18.7 8.3 %collective-permute-start.3 = (f32[128,128]{1,0:T(8,128)}, f32[128,128]{1,0:T(8,128)S(1)}, u32[]{:S(2)}, u32[]{:S(2)}) collective-permute-start(f32[128,128]{1,0:T(8,128)} %get-tuple-element.39), channel_id=1, source_target_pairs={{2,0},{3,1},{4,2},{5,3},{6,4},{7,5},{10,8},{11,9},{12,10},{13,11},... | collective-permute-start | bytes 196616 | tf_op jit(solution)/shard_map/ppermute | solution.py:717
  20.8 6.2 %collective-permute-start.4 = (f32[128,128]{1,0:T(8,128)}, f32[128,128]{1,0:T(8,128)S(1)}, u32[]{:S(2)}, u32[]{:S(2)}) collective-permute-start(f32[128,128]{1,0:T(8,128)} %get-tuple-element.40), channel_id=1, source_target_pairs={{0,8},{8,16},{16,24},{1,9},{9,17},{17,25},{2,10},{10,18},{18,26},{... | collective-permute-start | bytes 196616 | tf_op jit(solution)/shard_map/ppermute | solution.py:717
  23.9 5.2 %collective-permute-start.5 = (f32[128,128]{1,0:T(8,128)}, f32[128,128]{1,0:T(8,128)S(1)}, u32[]{:S(2)}, u32[]{:S(2)}) collective-permute-start(f32[128,128]{1,0:T(8,128)} %get-tuple-element.41), channel_id=1, source_target_pairs={{8,0},{16,8},{24,16},{9,1},{17,9},{25,17},{10,2},{18,10},{26,18},{... | collective-permute-start | bytes 196616 | tf_op jit(solution)/shard_map/ppermute | solution.py:717
  29.1 1.0 copy-start.2
  30.2 1.0 copy-start.4
  31.2 6.5 %copy-start.15 = (s32[1024]{0:T(1024)S(1)}, s32[1024]{0:T(1024)}, u32[]{:S(2)}) copy-start(s32[1024]{0:T(1024)} %param.23) | copy-start | bytes 12292
  31.2 6.5 %copy-start.16 = (s32[1024]{0:T(1024)S(1)}, s32[1024]{0:T(1024)}, u32[]{:S(2)}) copy-start(s32[1024]{0:T(1024)} %param.22) | copy-start | bytes 12292
  31.2 6.6 %copy-start.6 = (f32[256,4,128]{2,1,0:T(4,128)S(1)}, f32[256,4,128]{2,1,0:T(4,128)}, u32[]{:S(2)}) copy-start(f32[256,4,128]{2,1,0:T(4,128)} %get-tuple-element.34) | copy-start | bytes 1572868
  31.2 6.6 %copy-start.8 = (bf16[128,256]{1,0:T(8,128)(2,1)S(1)}, bf16[128,256]{1,0:T(8,128)(2,1)}, u32[]{:S(2)}) copy-start(bf16[128,256]{1,0:T(8,128)(2,1)} %constant.8.clone.refs_0_) | copy-start | bytes 196612
  31.2 6.6 %copy-start.9 = (bf16[256,128]{1,0:T(8,128)(2,1)S(1)}, bf16[256,128]{1,0:T(8,128)(2,1)}, u32[]{:S(2)}) copy-start(bf16[256,128]{1,0:T(8,128)(2,1)} %constant.9.clone.refs_1_) | copy-start | bytes 196612
  31.3 6.6 %copy-start.10 = (f32[128,128]{1,0:T(8,128)S(1)}, f32[128,128]{1,0:T(8,128)}, u32[]{:S(2)}) copy-start(f32[128,128]{1,0:T(8,128)} %get-tuple-element.42.refs_4_) | copy-start | bytes 196612
  31.3 6.6 %copy-start.11 = (bf16[128,128]{1,0:T(8,128)(2,1)S(1)}, bf16[128,128]{1,0:T(8,128)(2,1)}, u32[]{:S(2)}) copy-start(bf16[128,128]{1,0:T(8,128)(2,1)} %constant.10.clone.refs_2_) | copy-start | bytes 98308
  31.4 85.3 %collective-permute-start.6 = (f32[14,48,256]{2,1,0:T(8,128)S(1)}, f32[14,48,256]{2,1,0:T(8,128)S(1)}, u32[]{:S(2)}, u32[]{:S(2)}) collective-permute-start(f32[14,48,256]{2,1,0:T(8,128)S(1)} %get-tuple-element.53), channel_id=1, source_target_pairs={{0,8},{8,16},{16,24},{1,9},{9,17},{17,25},{2,10},{10,18},{18,26},{... | collective-permute-start | bytes 2064392 | tf_op jit(solution)/shard_map/ppermute | solution.py:717
  33.5 86.3 %collective-permute-start.7 = (f32[14,48,256]{2,1,0:T(8,128)S(1)}, f32[14,48,256]{2,1,0:T(8,128)S(1)}, u32[]{:S(2)}, u32[]{:S(2)}) collective-permute-start(f32[14,48,256]{2,1,0:T(8,128)S(1)} %get-tuple-element.54), channel_id=1, source_target_pairs={{8,0},{16,8},{24,16},{9,1},{17,9},{25,17},{10,2},{18,10},{26,18},{... | collective-permute-start | bytes 2064392 | tf_op jit(solution)/shard_map/ppermute | solution.py:717
  37.8 0.7 copy-start.13
  38.5 85.9 %copy-start.3 = (f32[16,32,256]{2,1,0:T(8,128)S(1)}, f32[16,32,256]{2,1,0:T(8,128)}, u32[]{:S(2)}) copy-start(f32[16,32,256]{2,1,0:T(8,128)} %get-tuple-element.51.refs_1_.refs_3_) | copy-start | bytes 1572868
  38.5 85.9 %copy-start.5 = (f32[16,32,256]{2,1,0:T(8,128)S(1)}, f32[16,32,256]{2,1,0:T(8,128)}, u32[]{:S(2)}) copy-start(f32[16,32,256]{2,1,0:T(8,128)} %get-tuple-element.52.refs_2_.refs_4_) | copy-start | bytes 1572868
  38.5 86.0 %copy-start.7 = (f32[256,128]{1,0:T(8,128)S(1)}, f32[256,128]{1,0:T(8,128)}, u32[]{:S(2)}) copy-start(f32[256,128]{1,0:T(8,128)} %get-tuple-element.50.refs_1_) | copy-start | bytes 393220
  104.5 10.0 %collective-permute-start.13 = (f32[128,128]{1,0:T(8,128)S(1)}, f32[128,128]{1,0:T(8,128)S(1)}, u32[]{:S(2)}, u32[]{:S(2)}) collective-permute-start(f32[128,128]{1,0:T(8,128)S(1)} %get-tuple-element.62), channel_id=1, source_target_pairs={{0,8},{8,16},{16,24},{1,9},{9,17},{17,25},{2,10},{10,18},{18,26},{... | collective-permute-start | bytes 196616 | tf_op jit(solution)/shard_map/ppermute | solution.py:717
  106.4 36.7 %collective-permute-start.8 = (f32[128,128]{1,0:T(8,128)S(1)}, f32[128,128]{1,0:T(8,128)S(1)}, u32[]{:S(2)}, u32[]{:S(2)}) collective-permute-start(f32[128,128]{1,0:T(8,128)S(1)} %get-tuple-element.57), channel_id=1, source_target_pairs={{1,0},{2,1},{3,2},{4,3},{5,4},{6,5},{7,6},{9,8},{10,9},{11,10},{12... | collective-permute-start | bytes 196616 | tf_op jit(solution)/shard_map/ppermute | solution.py:717
  111.5 31.6 %collective-permute-start.9 = (f32[128,128]{1,0:T(8,128)S(1)}, f32[128,128]{1,0:T(8,128)S(1)}, u32[]{:S(2)}, u32[]{:S(2)}) collective-permute-start(f32[128,128]{1,0:T(8,128)S(1)} %get-tuple-element.58), channel_id=1, source_target_pairs={{0,1},{1,2},{2,3},{3,4},{4,5},{5,6},{6,7},{8,9},{9,10},{10,11},{11... | collective-permute-start | bytes 196616 | tf_op jit(solution)/shard_map/ppermute | solution.py:717
  114.5 28.6 %collective-permute-start.10 = (f32[128,128]{1,0:T(8,128)S(1)}, f32[128,128]{1,0:T(8,128)S(1)}, u32[]{:S(2)}, u32[]{:S(2)}) collective-permute-start(f32[128,128]{1,0:T(8,128)S(1)} %get-tuple-element.59), channel_id=1, source_target_pairs={{2,0},{3,1},{4,2},{5,3},{6,4},{7,5},{10,8},{11,9},{12,10},{13,11},... | collective-permute-start | bytes 196616 | tf_op jit(solution)/shard_map/ppermute | solution.py:717
  116.7 26.4 %collective-permute-start.11 = (f32[128,128]{1,0:T(8,128)S(1)}, f32[128,128]{1,0:T(8,128)S(1)}, u32[]{:S(2)}, u32[]{:S(2)}) collective-permute-start(f32[128,128]{1,0:T(8,128)S(1)} %get-tuple-element.60), channel_id=1, source_target_pairs={{0,2},{1,3},{2,4},{3,5},{4,6},{5,7},{8,10},{9,11},{10,12},{11,13},... | collective-permute-start | bytes 196616 | tf_op jit(solution)/shard_map/ppermute | solution.py:717
  119.8 4.6 %copy-start.14 = (s32[256]{0:T(256)S(1)}, s32[256]{0:T(256)}, u32[]{:S(2)}) copy-start(s32[256]{0:T(256)} %refs_0_.4) | copy-start | bytes 3076
  119.8 23.3 %collective-permute-start.12 = (f32[128,128]{1,0:T(8,128)S(1)}, f32[128,128]{1,0:T(8,128)S(1)}, u32[]{:S(2)}, u32[]{:S(2)}) collective-permute-start(f32[128,128]{1,0:T(8,128)S(1)} %get-tuple-element.61), channel_id=1, source_target_pairs={{8,0},{16,8},{24,16},{9,1},{17,9},{25,17},{10,2},{18,10},{26,18},{... | collective-permute-start | bytes 196616 | tf_op jit(solution)/shard_map/ppermute | solution.py:717
  143.1 0.7 copy-start.12

commit v10 on v9

--- a/solution.py
+++ b/solution.py
@@ -12,7 +12,7 @@
 QUAD = 4
 UNROLL = 8
 HALO_WIDTHS = (SWEEPS + 1, SWEEPS, SWEEPS, 1)
-MARGIN = 8
+DEPTH = SWEEPS + 1
 CELL_BITS = 8
 
 
@@ -50,12 +50,12 @@
         far_kinds += [3 * part + level for level in (0, 1, 2, 0, 1, 0)]
     near_kinds += [9, 10, 11, 12, 12, 12]
     far_kinds += [12, 12, 12, 9, 10, 11]
-    near = np.zeros((128, 256), np.float32)
+    near = np.zeros((128, 1024), np.float32)
     far = np.zeros((256, 128), np.float32)
     moment = np.zeros((128, 128), np.float32)
     for cluster in range(8):
         for index, kind in enumerate(near_kinds):
-            near[kind * 8 + cluster, cluster * 32 + index] = 1.0
+            near[kind * 8 + cluster, cluster * 128 + index] = 1.0
         for index, kind in enumerate(far_kinds):
             far[cluster * 32 + index, kind * 8 + cluster] = 1.0
         for kind in range(12):
@@ -112,30 +112,27 @@
             moment_sel_ref[...], moments.astype(jnp.bfloat16)
         )
         tiles = selected(place_pieces(comps, 1.0, 0.0).T, near_sel_ref[...])
-        for half in range(2):
-            at = pl.ds(pl.multiple_of(step * 256 + half * 128, 128), 128)
-            near_ref[at, :] = tiles[:, 128 * half : 128 * half + 128]
+        for index in range(8):
+            at = pl.ds(pl.multiple_of((start + index) * 128, 128), 128)
+            near_ref[at, :] = tiles[:, 128 * index : 128 * index + 128]
         return 0
 
     def far_rows(source, step, _):
         local = pl.multiple_of(step * 8, 8)
         start = source * slots + local
         *comps, charge = components(other_refs[source], local)
-        rows = selected(far_sel_ref[...], place_pieces(comps, -2.0, softening).astype(jnp.bfloat16))
-        for index in range(8):
-            at = pl.multiple_of((start + index) * 128, 128)
-            far_ref[pl.ds(at, 96), :] = jnp.zeros((96, 128), jnp.bfloat16)
-            far_ref[pl.ds(at + 96, 32), :] = rows[32 * index : 32 * index + 32]
+        far_ref[pl.ds(pl.multiple_of(start * 32, 256), 256), :] = selected(
+            far_sel_ref[...], place_pieces(comps, -2.0, softening).astype(jnp.bfloat16)
+        )
         moments = jnp.concatenate(moment_pieces(comps, charge) + [zeros] * 4, axis=0)
         other_moment_ref[pl.ds(pl.multiple_of(start * 16, 128), 128), :] = selected(
             moment_sel_ref[...], moments.astype(jnp.bfloat16)
         )
         return 0
 
-    lax.fori_loop(0, clusters // 8, near_rows, 0, unroll=2)
+    lax.fori_loop(0, clusters // 8, near_rows, 0, unroll=4)
     for source in range(sources):
-        lax.fori_loop(0, slots // 8, functools.partial(far_rows, source), 0, unroll=2)
-    far_ref[pl.ds(others * 128, 128), :] = jnp.zeros((128, 128), jnp.bfloat16)
+        lax.fori_loop(0, slots // 8, functools.partial(far_rows, source), 0, unroll=4)
     own_sum_ref[...] = jnp.zeros_like(own_sum_ref)
     other_sum_ref[...] = jnp.zeros_like(other_sum_ref)
     dist_refs, weight_refs = (passed_refs[:2], passed_refs[2:])
@@ -153,18 +150,12 @@
         return jnp.concatenate(lines, axis=0)
 
     def distances(pair, unit, dist_ref):
-        for couple in range(QUAD // 2):
-            near, far = ([], [])
-            for turn in range(2):
-                own = own_rows_ref[pair + 2 * couple + turn]
-                other = other_rows_ref[pair + 2 * couple + turn]
-                tile = pl.multiple_of(lax.shift_right_logical(own, 2) * 128, 128)
-                near.append(near_ref[pl.ds(tile, 128), :])
-                first = pl.multiple_of(other * 128 + 96 - lax.bitwise_and(own, 3) * 32, 32)
-                far.append(far_ref[pl.ds(first, 128), :])
-            dist_ref[unit, :, 256 * couple : 256 * couple + 256] = jnp.dot(
-                jnp.concatenate(near, axis=1),
-                block_diagonal(far),
+        for turn in range(QUAD):
+            own = own_rows_ref[pair + turn]
+            other = other_rows_ref[pair + turn]
+            dist_ref[unit, :, 128 * turn : 128 * turn + 128] = jnp.dot(
+                near_ref[pl.ds(pl.multiple_of(own * 128, 128), 128), 0:32],
+                far_ref[pl.ds(pl.multiple_of(other * 32, 32), 32), :],
                 preferred_element_type=jnp.float32,
             )
 
@@ -245,7 +236,7 @@
         return 0
 
     lax.fori_loop(
-        0, clusters // 8, functools.partial(finish, own_ref, own_out_ref, own_sum_ref, 0), 0
+        0, clusters // 8, functools.partial(finish, own_ref, own_out_ref, own_sum_ref, 0), 0, unroll=4
     )
     for source in range(sources):
         body = functools.partial(
@@ -255,7 +246,7 @@
             other_sum_ref,
             source * slots * 16,
         )
-        lax.fori_loop(0, slots // 8, body, 0)
+        lax.fori_loop(0, slots // 8, body, 0, unroll=4)
 
 
 def pair_forces(own_rows, other_rows, own, arrived, slots):
@@ -273,8 +264,8 @@
         in_specs=[smem, smem] + [vmem] * (4 + len(arrived)),
         out_specs=(vmem,) * (len(arrived) + 1),
         scratch_shapes=[
-            pltpu.VMEM((clusters * 32, 128), jnp.bfloat16),
-            pltpu.VMEM(((others + 1) * 128, 128), jnp.bfloat16),
+            pltpu.VMEM((clusters * 128, 128), jnp.bfloat16),
+            pltpu.VMEM((others * 32, 128), jnp.bfloat16),
             pltpu.VMEM((clusters * 16, 128), jnp.bfloat16),
             pltpu.VMEM((others * 16, 128), jnp.bfloat16),
             pltpu.VMEM((clusters * 16, 128), jnp.float32),
@@ -295,6 +286,7 @@
     cell_ref,
     send_index_ref,
     send_count_ref,
+    cell_row_ref,
     position_hbm,
     charge_hbm,
     ion_hbm,
@@ -322,7 +314,6 @@
     ]
     for copy in copies:
         copy.start()
-    deposit_ref[...] = jnp.zeros_like(deposit_ref)
     copies[0].wait()
     copies[1].wait()
     clusters = charge_ref.shape[0]
@@ -344,7 +335,7 @@
         sum_ref[at, :] = jnp.broadcast_to(deposit_scale * total, (8, 128))
         return 0
 
-    lax.fori_loop(0, clusters // 8, collect, 0)
+    lax.fori_loop(0, clusters // 8, collect, 0, unroll=4)
 
     def fill_messages(step, _):
         for direction, out_ref in enumerate(out_refs):
@@ -359,19 +350,28 @@
 
     lax.fori_loop(0, slots // 2, fill_messages, 0)
 
-    def deposit(cluster, _):
-        cell = cell_ref[cluster]
-        index_x = lax.shift_right_logical(cell, CELL_BITS) // cells_y
-        index_y = lax.shift_right_logical(cell, CELL_BITS) % cells_y
-        index_z = lax.bitwise_and(cell, 255)
-        half = lax.shift_right_logical(index_z, 7)
-        added = jnp.where(
-            lane == lax.bitwise_and(index_z, 127), sum_ref[pl.ds(cluster, 1), :], 0.0
+    def place(step, _):
+        for turn in range(8):
+            cluster = step * 8 + turn
+            index_z = lax.bitwise_and(cell_ref[cluster], 127)
+            at = pl.ds(cluster, 1)
+            sum_ref[at, :] = jnp.where(lane == index_z, sum_ref[at, :], 0.0)
+        return 0
+
+    lax.fori_loop(0, clusters // 8, place, 0)
+    cell = cell_row_ref[...]
+    line = lax.shift_right_logical(cell, CELL_BITS)
+    line = (line // cells_y * 2 + lax.shift_right_logical(lax.bitwise_and(cell, 255), 7)) * cells_y
+    line = line + lax.shift_right_logical(cell, CELL_BITS) % cells_y
+    sums = jnp.concatenate([part.astype(jnp.bfloat16) for part in split3(sum_ref[...])], axis=1)
+    block = 128
+    for first in range(0, deposit_ref.shape[0], block):
+        rows = lax.broadcasted_iota(jnp.int32, (block, clusters), 0) + first
+        hot = jnp.where(rows == line, 1.0, 0.0).astype(jnp.bfloat16)
+        added = jnp.dot(hot, sums, preferred_element_type=jnp.float32)
+        deposit_ref[first : first + block, :] = added[:, :128] + (
+            added[:, 128:256] + added[:, 256:]
         )
-        deposit_ref[pl.ds((index_x * 2 + half) * cells_y + index_y, 1), :] += added
-        return 0
-
-    lax.fori_loop(0, clusters, deposit, 0, unroll=4)
     for copy in copies[2:]:
         copy.wait()
     inverse_ref[...] = 1.0 / (6.0 + screen_ref[...])
@@ -419,7 +419,7 @@
             jax.ShapeDtypeStruct(ions.shape, jnp.float32),
             *[jax.ShapeDtypeStruct((count, 128), jnp.float32) for count in rows],
         ),
-        in_specs=[smem] * 4 + [pl.BlockSpec(memory_space=pltpu.HBM)] * 5,
+        in_specs=[smem] * 4 + [vmem] + [pl.BlockSpec(memory_space=pltpu.HBM)] * 5,
         out_specs=(vmem,) * (4 + directions),
         scratch_shapes=[
             pltpu.VMEM((clusters, 128), jnp.float32),
@@ -432,42 +432,62 @@
         ],
         compiler_params=pltpu.CompilerParams(vmem_limit_bytes=60 * 1024 * 1024),
         name="prepare",
-    )(fill, cell, send_index, send_count, positions, charges, ions, start, screen)
-
-
-def put_extended(target_ref, plane, field, field_ref, index, before_ref, after_ref, base):
+    )(
+        fill,
+        cell,
+        send_index,
+        send_count,
+        cell.reshape(1, clusters),
+        positions,
+        charges,
+        ions,
+        start,
+        screen,
+    )
+
+
+def line_rows(cells_y):
+    return (cells_y + 2 * DEPTH + 7) // 8 * 8
+
+
+def fill_lines(target_ref, plane, field, field_ref, index, before_ref, after_ref, base):
     cells_y = field_ref.shape[1]
     width = HALO_WIDTHS[field]
-    offset = sum(HALO_WIDTHS[:field])
-    target_ref[plane, MARGIN : MARGIN + cells_y, :] = field_ref[index]
     for half in range(2):
-        lanes = slice(128 * half, 128 * half + 128)
-        first = base + index * 32 + 16 * half + offset
-        target_ref[plane, MARGIN - width : MARGIN, lanes] = before_ref[first : first + width, :]
-        target_ref[plane, MARGIN + cells_y : MARGIN + cells_y + width, lanes] = after_ref[
-            first : first + width, :
-        ]
+        at = (plane * 2 + half) * line_rows(cells_y) + DEPTH
+        first = base + index * 32 + 16 * half + sum(HALO_WIDTHS[:field])
+        target_ref[pl.ds(at - width, width), :] = before_ref[pl.ds(first, width), :]
+        target_ref[pl.ds(at, cells_y), :] = field_ref[index, :, 128 * half : 128 * half + 128]
+        target_ref[pl.ds(at + cells_y, width), :] = after_ref[pl.ds(first, width), :]
 
 
 def planes_kernel(base, *refs):
     field_refs, (before_ref, after_ref, down_ref, up_ref) = (refs[:4], refs[4:])
     cells_x = field_refs[0].shape[0]
-    down_ref[...] = jnp.zeros_like(down_ref)
-    up_ref[...] = jnp.zeros_like(up_ref)
-    plane = 0
     for field, width in enumerate(HALO_WIDTHS):
-        for index in range(width):
-            for target_ref, source in ((down_ref, index), (up_ref, cells_x - width + index)):
-                put_extended(
-                    target_ref, plane, field, field_refs[field], source, before_ref, after_ref, base
+        plane = sum(HALO_WIDTHS[:field])
+
+        def fill(step, _, field=field, plane=plane, width=width):
+            for target_ref, source in ((down_ref, step), (up_ref, cells_x - width + step)):
+                fill_lines(
+                    target_ref,
+                    plane + step,
+                    field,
+                    field_refs[field],
+                    source,
+                    before_ref,
+                    after_ref,
+                    base,
                 )
-            plane += 1
+            return 0
+
+        lax.fori_loop(0, width, fill, 0)
 
 
 def planes(fields, before, after, base):
     vmem = pl.BlockSpec(memory_space=pltpu.VMEM)
-    _, cells_y, cells_z = fields[0].shape
-    shape = jax.ShapeDtypeStruct((sum(HALO_WIDTHS), cells_y + 2 * MARGIN, cells_z), jnp.float32)
+    rows = sum(HALO_WIDTHS) * 2 * line_rows(fields[0].shape[1])
+    shape = jax.ShapeDtypeStruct((rows, 128), jnp.float32)
     return pl.pallas_call(
         functools.partial(planes_kernel, base),
         out_shape=(shape, shape),
@@ -492,34 +512,27 @@
     field_refs = refs[2:6]
     before_ref, after_ref, lower_ref, upper_ref = refs[6:10]
     potential_ref, next_ref, force_ref = refs[10:13]
-    start_ref, inverse_ref, resid_ref, ion_ref, update_ref, line_ref, *pick_refs = refs[13:]
-    cells_x, cells_y, cells_z = field_refs[0].shape
-    rows = cells_y + 2 * MARGIN
-    depth = HALO_WIDTHS[0]
+    start_ref, inverse_ref, source_ref, ion_ref = refs[13:17]
+    updates, resids, final_ref, pick_refs = (refs[17:20], refs[20:22], refs[22], refs[23:26])
+    cells_x, cells_y, _ = field_refs[0].shape
+    rows = line_rows(cells_y)
+    inner = cells_y + 2 * DEPTH - 2
     clusters = masked_ref.shape[0]
-    lane = lax.broadcasted_iota(jnp.int32, (rows, cells_z), 1)
-    middle = 0.5 * (highest_eig + lowest_eig)
-    spread = 0.5 * (highest_eig - lowest_eig)
-
-    plane = 0
-    for field, target_ref in enumerate((start_ref, inverse_ref, resid_ref, ion_ref)):
+
+    for field, target_ref in enumerate((start_ref, inverse_ref, source_ref, ion_ref)):
         width = HALO_WIDTHS[field]
-        if field == 0 or field == 3:
-            target_ref[...] = jnp.zeros_like(target_ref)
-        else:
-            target_ref[depth : depth + cells_x, 0:MARGIN, :] = jnp.zeros(
-                (cells_x, MARGIN, cells_z), jnp.float32
-            )
-            target_ref[depth : depth + cells_x, rows - MARGIN : rows, :] = jnp.zeros(
-                (cells_x, MARGIN, cells_z), jnp.float32
-            )
-        for index in range(width):
-            target_ref[depth - width + index] = lower_ref[plane + index]
-            target_ref[depth + cells_x + index] = upper_ref[plane + index]
-        for index in range(cells_x):
-            put_extended(
+        size = width * 2 * rows
+        first = sum(HALO_WIDTHS[:field]) * 2 * rows
+        low = (DEPTH - width) * 2 * rows
+        high = (DEPTH + cells_x) * 2 * rows
+        target_ref[low : low + size, :] = lower_ref[first : first + size, :]
+        target_ref[high : high + size, :] = upper_ref[first : first + size, :]
+
+    def fill(index, _):
+        for field, target_ref in enumerate((start_ref, inverse_ref, source_ref, ion_ref)):
+            fill_lines(
                 target_ref,
-                depth + index,
+                DEPTH + index,
                 field,
                 field_refs[field],
                 index,
@@ -527,29 +540,44 @@
                 after_ref,
                 base,
             )
-        plane += width
-
-    def above(value):
-        return jnp.where(lane == cells_z - 1, 0.0, pltpu.roll(value, cells_z - 1, 1))
-
-    def below(value):
-        return jnp.where(lane == 0, 0.0, pltpu.roll(value, 1, 1))
-
-    def beside(value):
-        rolled = pltpu.roll(value, 1, 0) + pltpu.roll(value, rows - 1, 0)
-        return rolled + (above(value) + below(value))
-
-    def first_sweep(index, planes):
-        last, here = planes
-        after = start_ref[index + 1]
-        resid = (
-            resid_ref[index] - here + inverse_ref[index] * ((last + after) + beside(here))
-        )
-        resid_ref[index] = resid
-        update_ref[index] = resid / middle
-        return (here, after)
-
-    lax.fori_loop(1, cells_x + 2 * depth - 1, first_sweep, (start_ref[0], start_ref[1]))
+        return 0
+
+    lax.fori_loop(0, cells_x, fill, 0, unroll=2)
+
+    def beyond(values):
+        lane = lax.broadcasted_iota(jnp.int32, values[0].shape, 1)
+        right = [pltpu.roll(value, 127, 1) for value in values]
+        left = [pltpu.roll(value, 1, 1) for value in values]
+        above = [jnp.where(lane == 127, right[1], right[0]), jnp.where(lane == 127, 0.0, right[1])]
+        below = [jnp.where(lane == 0, 0.0, left[0]), jnp.where(lane == 0, left[0], left[1])]
+        return (below, above)
+
+    def wide(plane, half, shift=0):
+        return pl.ds((plane * 2 + half) * rows + 1 + shift, inner)
+
+    def around(ref, plane):
+        here = [ref[wide(plane, half), :] for half in range(2)]
+        below, above = beyond(here)
+        sums = [
+            (ref[wide(plane - 1, half), :] + ref[wide(plane + 1, half), :])
+            + (ref[wide(plane, half, -1), :] + ref[wide(plane, half, 1), :])
+            + (below[half] + above[half])
+            for half in range(2)
+        ]
+        return (here, sums)
+
+    middle = 0.5 * (highest_eig + lowest_eig)
+    spread = 0.5 * (highest_eig - lowest_eig)
+    assert middle == 1.0 and SWEEPS == 4
+
+    def sweep_first(plane, _):
+        here, sums = around(start_ref, plane)
+        for half in range(2):
+            at = wide(plane, half)
+            updates[0][at, :] = source_ref[at, :] - here[half] + inverse_ref[at, :] * sums[half]
+        return 0
+
+    lax.fori_loop(1, cells_x + 2 * DEPTH - 1, sweep_first, 0, unroll=2)
 
     ratio_ms = middle / spread
     weight_now = 1.0 / ratio_ms
@@ -558,71 +586,76 @@
         keep, gain = (weight_next * weight_now, 2.0 * weight_next / spread)
         weight_now = weight_next
 
-        def sweep(index, planes, turn=turn, keep=keep, gain=gain):
-            last, here = planes
-            after = update_ref[index + 1]
-            resid = resid_ref[index] - here + inverse_ref[index] * ((last + after) + beside(here))
-            update = keep * here + gain * resid
-            if turn == 1:
-                start_ref[index] = start_ref[index] + here + update
-            else:
-                start_ref[index] = start_ref[index] + update
-            if turn + 1 < SWEEPS:
-                resid_ref[index] = resid
-                update_ref[index] = update
-            return (here, after)
+        def sweep(plane, _, turn=turn, keep=keep, gain=gain):
+            here, sums = around(updates[turn - 1], plane)
+            for half in range(2):
+                at = wide(plane, half)
+                resid = inverse_ref[at, :] * sums[half]
+                if turn > 1:
+                    resid = resid + (resids[turn - 2][at, :] - here[half])
+                update = keep * here[half] + gain * resid
+                if turn + 1 < SWEEPS:
+                    resids[turn - 1][at, :] = resid
+                    updates[turn][at, :] = update
+                else:
+                    final_ref[at, :] = (start_ref[at, :] + updates[0][at, :]) + (
+                        (updates[1][at, :] + here[half]) + update
+                    )
+            return 0
 
         first = 1 + turn
-        lax.fori_loop(
-            first,
-            cells_x + 2 * depth - first,
-            sweep,
-            (update_ref[first - 1], update_ref[first]),
-        )
-
-    def upper_flux(index):
-        return face_flux(start_ref[index], start_ref[index + 1], ion_ref[index], ion_ref[index + 1])
-
-    inner = slice(MARGIN, MARGIN + cells_y)
-
-    def advance(index, lower):
-        pot = start_ref[depth + index]
-        ions = ion_ref[depth + index]
-        upper = upper_flux(depth + index)
-        along_y = face_flux(pot, pltpu.roll(pot, rows - 1, 0), ions, pltpu.roll(ions, rows - 1, 0))
-        along_z = face_flux(pot, above(pot), ions, above(ions))
-        first_z = face_flux(0.0, pot, 0.0, ions)
-        total = upper - lower
-        total = total + (along_y - pltpu.roll(along_y, 1, 0))
-        total = total + (along_z - jnp.where(lane == 0, first_z, pltpu.roll(along_z, 1, 1)))
-        next_ref[index] = (ions - time_step * total)[inner]
-        potential_ref[index] = pot[inner]
-        return upper
-
-    lax.fori_loop(0, cells_x, advance, upper_flux(depth - 1))
-    for index in range(cells_x + 2):
+        lax.fori_loop(first, cells_x + 2 * DEPTH - first, sweep, 0, unroll=2)
+
+    def local(plane, half, shift=0):
+        return pl.ds((plane * 2 + half) * rows + DEPTH + shift, cells_y)
+
+    def advance(index, _):
+        plane = index + DEPTH
+        pots = [final_ref[local(plane, half), :] for half in range(2)]
+        ions = [ion_ref[local(plane, half), :] for half in range(2)]
+        pot_below, pot_above = beyond(pots)
+        ion_below, ion_above = beyond(ions)
         for half in range(2):
-            line_ref[pl.ds((index * 2 + half) * rows, rows), :] = start_ref[
-                depth - 1 + index, :, 128 * half : 128 * half + 128
+            pot, ion = (pots[half], ions[half])
+            steps = [
+                (final_ref[at, :], ion_ref[at, :])
+                for at in (
+                    local(plane - 1, half),
+                    local(plane + 1, half),
+                    local(plane, half, -1),
+                    local(plane, half, 1),
+                )
             ]
+            steps += [(pot_below[half], ion_below[half]), (pot_above[half], ion_above[half])]
+            total = 0.0
+            for low, high in zip(steps[0::2], steps[1::2], strict=True):
+                total = total + (
+                    face_flux(pot, high[0], ion, high[1]) - face_flux(low[0], pot, low[1], ion)
+                )
+            lanes = slice(128 * half, 128 * half + 128)
+            next_ref[index, :, lanes] = ion - time_step * total
+            potential_ref[index, :, lanes] = pot
+        return 0
+
+    lax.fori_loop(0, cells_x, advance, 0)
 
     row_lane = lax.broadcasted_iota(jnp.int32, (1, 128), 1)
 
     def pick(cluster, _):
         cell = cell_ref[cluster]
-        index_x = lax.shift_right_logical(cell, CELL_BITS) // cells_y + 1
-        index_y = lax.shift_right_logical(cell, CELL_BITS) % cells_y + MARGIN
+        index_x = lax.shift_right_logical(cell, CELL_BITS) // cells_y + DEPTH
+        index_y = lax.shift_right_logical(cell, CELL_BITS) % cells_y + DEPTH
         index_z = lax.bitwise_and(cell, 255)
         half = lax.shift_right_logical(index_z, 7)
         here = row_lane == lax.bitwise_and(index_z, 127)
 
         def line(plane, row, part):
-            return line_ref[pl.ds((plane * 2 + part) * rows + row, 1), :]
+            return final_ref[pl.ds((plane * 2 + part) * rows + row, 1), :]
 
         along_x = line(index_x - 1, index_y, half) - line(index_x + 1, index_y, half)
         along_y = line(index_x, index_y - 1, half) - line(index_x, index_y + 1, half)
         along_z = jnp.zeros((1, 128), jnp.float32)
-        for part in range(cells_z // 128):
+        for part in range(2):
             value = line(index_x, index_y, part)
             place = row_lane + 128 * part
             along_z = along_z + jnp.where(place == index_z - 1, value, 0.0)
@@ -633,7 +666,7 @@
         pick_refs[2][at, :] = along_z
         return 0
 
-    lax.fori_loop(0, clusters, pick, 0, unroll=4)
+    lax.fori_loop(0, clusters, pick, 0, unroll=8)
 
     def spread_out(step, _):
         start = pl.multiple_of(step * 8, 8)
@@ -644,15 +677,15 @@
         force_ref[pl.ds(4 * start + 3, 8, stride=4), :] = jnp.zeros((8, 128), jnp.float32)
         return 0
 
-    lax.fori_loop(0, clusters // 8, spread_out, 0)
+    lax.fori_loop(0, clusters // 8, spread_out, 0, unroll=4)
 
 
 def grid_step(cell, masked, fields, before, after, lower, upper, base):
     smem = pl.BlockSpec(memory_space=pltpu.SMEM)
     vmem = pl.BlockSpec(memory_space=pltpu.VMEM)
     clusters = masked.shape[0]
-    cells_x, cells_y, cells_z = fields[0].shape
-    block = (cells_x + 2 * HALO_WIDTHS[0], cells_y + 2 * MARGIN, cells_z)
+    cells_x, cells_y, _ = fields[0].shape
+    block = ((cells_x + 2 * DEPTH) * 2 * line_rows(cells_y), 128)
     return pl.pallas_call(
         functools.partial(grid_kernel, base),
         out_shape=(
@@ -662,12 +695,11 @@
         ),
         in_specs=[smem] + [vmem] * 9,
         out_specs=(vmem,) * 3,
-        scratch_shapes=[pltpu.VMEM(block, jnp.float32)] * 5
-        + [pltpu.VMEM(((cells_x + 2) * 2 * block[1], 128), jnp.float32)]
+        scratch_shapes=[pltpu.VMEM(block, jnp.float32)] * 10
         + [pltpu.VMEM((clusters, 128), jnp.float32)] * 3,
         compiler_params=pltpu.CompilerParams(vmem_limit_bytes=40 * 1024 * 1024),
         cost_estimate=pl.CostEstimate(
-            flops=block[0] * block[1] * block[2] * 100, bytes_accessed=8 << 20, transcendentals=0
+            flops=block[0] * block[1] * 100, bytes_accessed=8 << 20, transcendentals=0
         ),
         name="grid_step",
     )(cell, masked, *fields, before, after, lower, upper)

time: 147 us -> 134 us (0.912)
  Pallas kernels: 96.7 us -> 83 us
    pallas_call x1, Pallas kernels: 18.7 us -> 11.5 us  [grid_step(): pl.pallas_call(functools.partial(grid_kernel, base), out_shape=(jax.Shape...]
    pallas_call x1, Pallas kernels: 66 us -> 62.6 us  [pair_forces(): pl.pallas_call(pair_kernel, out_shape=(jax.ShapeDtypeStruct(own.shape, jn...]
    pallas_call x1, Pallas kernels: 9.11 us -> 6.06 us  [prepare(): pl.pallas_call(prepare_kernel, out_shape=(jax.ShapeDtypeStruct((clusters,...]
  transfers between devices with their start and end apart: 14 -> 14, of which waited for: 1 -> 1; matrix products, arithmetic and copies ran while one was open for 0% -> 0% of each run, Pallas kernels for 58% -> 56%
where the time goes in v10:
time: 134 us; the launch traced here: 132 us
  Pallas kernels  83 us (62%)
  starting transfers between devices  42.7 us (32%)
  local copies, waits for them, and re-layouts  3.44 us (3%)
  waiting for transfers between devices  2.16 us (2%)
    pallas_call x1, Pallas kernels, pair_forces(): pl.pallas_call(pair_kernel, out_shape=(jax.ShapeDtypeStruct(own.shape, jn...  62.6 us
    ppermute x14, starting transfers between devices, passed_along(): return lax.ppermute(shard, axis, pairs)  42.7 us
    pallas_call x1, Pallas kernels, grid_step(): pl.pallas_call(functools.partial(grid_kernel, base), out_shape=(jax.Shape...  11.5 us
    pallas_call x1, Pallas kernels, prepare(): pl.pallas_call(prepare_kernel, out_shape=(jax.ShapeDtypeStruct((clusters,...  6.06 us
    unnamed x34, local copies, waits for them, and re-layouts  3.44 us
    pallas_call x1, Pallas kernels, gather_forces(): pl.pallas_call(gather_forces_kernel, out_shape=jax.ShapeDtypeStruct((3, c...  2.77 us
  transfers between devices with their start and end apart: 14, of which 1 were waited for; matrix products, arithmetic and copies ran while one was open for 0% of the time, Pallas kernels for 56%

profile of v10, /device:TPU:13, one launch (start us, length us, event | category | flops | bytes accessed | tf_op | source)
XLA Modules:
  0.0 132.4 jit_solution(2627945530294014137)
XLA Ops:
  0.6 0.0 copy-start
  0.6 0.0 copy-start.1
  0.7 6.1 %prepare.1 = (f32[256,4,128]{2,1,0:T(4,128)}, f32[256,128]{1,0:T(8,128)}, f32[16,32,256]{2,1,0:T(8,128)}, f32[16,32,256]{2,1,0:T(8,128)}, f32[128,128]{1,0:T(8,1...) custom-call(s32[256]{0:T(256)} %fill_ref.1, ...), custom_call_target="tpu_custom_call" | custom-call | tf_op jit(solution)/shard_map/prepare/pallas_call | solution.py:413
  6.7 3.8 %collective-permute-start = (f32[640,128]{1,0:T(8,128)}, f32[640,128]{1,0:T(8,128)S(1)}, u32[]{:S(2)}, u32[]{:S(2)}) collective-permute-start(f32[640,128]{1,0:T(8,128)} %get-tuple-element.36), channel_id=1, source_target_pairs={{0,1},{1,2},{2,3},{3,4},{4,5},{5,6},{6,7},{8,9},{9,10},{10,11},{11... | collective-permute-start | bytes 983048 | tf_op jit(solution)/shard_map/ppermute | solution.py:749
  10.5 1.9 %collective-permute-start.1 = (f32[640,128]{1,0:T(8,128)}, f32[640,128]{1,0:T(8,128)S(1)}, u32[]{:S(2)}, u32[]{:S(2)}) collective-permute-start(f32[640,128]{1,0:T(8,128)} %get-tuple-element.37), channel_id=1, source_target_pairs={{1,0},{2,1},{3,2},{4,3},{5,4},{6,5},{7,6},{9,8},{10,9},{11,10},{12... | collective-permute-start | bytes 983048 | tf_op jit(solution)/shard_map/ppermute | solution.py:749
  12.4 3.2 %collective-permute-start.2 = (f32[128,128]{1,0:T(8,128)}, f32[128,128]{1,0:T(8,128)S(1)}, u32[]{:S(2)}, u32[]{:S(2)}) collective-permute-start(f32[128,128]{1,0:T(8,128)} %get-tuple-element.38), channel_id=1, source_target_pairs={{0,2},{1,3},{2,4},{3,5},{4,6},{5,7},{8,10},{9,11},{10,12},{11,13},... | collective-permute-start | bytes 196616 | tf_op jit(solution)/shard_map/ppermute | solution.py:749
  15.6 2.1 %collective-permute-start.3 = (f32[128,128]{1,0:T(8,128)}, f32[128,128]{1,0:T(8,128)S(1)}, u32[]{:S(2)}, u32[]{:S(2)}) collective-permute-start(f32[128,128]{1,0:T(8,128)} %get-tuple-element.39), channel_id=1, source_target_pairs={{2,0},{3,1},{4,2},{5,3},{6,4},{7,5},{10,8},{11,9},{12,10},{13,11},... | collective-permute-start | bytes 196616 | tf_op jit(solution)/shard_map/ppermute | solution.py:749
  17.7 3.1 %collective-permute-start.4 = (f32[128,128]{1,0:T(8,128)}, f32[128,128]{1,0:T(8,128)S(1)}, u32[]{:S(2)}, u32[]{:S(2)}) collective-permute-start(f32[128,128]{1,0:T(8,128)} %get-tuple-element.40), channel_id=1, source_target_pairs={{0,8},{8,16},{16,24},{1,9},{9,17},{17,25},{2,10},{10,18},{18,26},{... | collective-permute-start | bytes 196616 | tf_op jit(solution)/shard_map/ppermute | solution.py:749
  20.8 0.0 collective-permute-done.2.refs_7_
  20.9 3.1 %collective-permute-start.5 = (f32[128,128]{1,0:T(8,128)}, f32[128,128]{1,0:T(8,128)S(1)}, u32[]{:S(2)}, u32[]{:S(2)}) collective-permute-start(f32[128,128]{1,0:T(8,128)} %get-tuple-element.41), channel_id=1, source_target_pairs={{8,0},{16,8},{24,16},{9,1},{17,9},{25,17},{10,2},{18,10},{26,18},{... | collective-permute-start | bytes 196616 | tf_op jit(solution)/shard_map/ppermute | solution.py:749
  23.9 0.0 collective-permute-done.3.refs_8_
  23.9 0.0 collective-permute-done.4.refs_9_
  23.9 2.1 %collective-permute-done.5.refs_10_ = f32[128,128]{1,0:T(8,128)S(1)} collective-permute-done((f32[128,128]{1,0:T(8,128)}, f32[128,128]{1,0:T(8,128)S(1)}, u32[]{:S(2)}, u32[]{:S(2)}) %collective-permute-start.5) | collective-permute-done | bytes 65568 | tf_op jit(solution)/shard_map/ppermute | solution.py:749
  26.1 0.0 collective-permute-done.refs_5_.refs_4_.refs_6_
  26.1 0.0 collective-permute-done.1.refs_6_.refs_5_.refs_7_
  26.1 0.0 copy-done
  26.1 0.0 copy-done.1
  26.1 0.0 copy-start.2
  26.1 1.0 copy-done.2
  27.1 0.0 copy-start.4
  27.1 1.0 copy-done.4
  28.2 0.0 copy-start.16
  28.2 0.0 copy-start.6
  28.2 0.0 copy-start.7
  28.2 0.0 copy-start.9
  28.2 0.0 copy-start.10
  28.2 0.0 copy-start.11
  28.2 0.1 planes.1
  28.4 2.1 %collective-permute-start.6 = (f32[1344,128]{1,0:T(8,128)S(1)}, f32[1344,128]{1,0:T(8,128)S(1)}, u32[]{:S(2)}, u32[]{:S(2)}) collective-permute-start(f32[1344,128]{1,0:T(8,128)S(1)} %get-tuple-element.53), channel_id=1, source_target_pairs={{0,8},{8,16},{16,24},{1,9},{9,17},{17,25},{2,10},{10,18},{18,26},{... | collective-permute-start | bytes 2064392 | tf_op jit(solution)/shard_map/ppermute | solution.py:749
  30.4 4.3 %collective-permute-start.7 = (f32[1344,128]{1,0:T(8,128)S(1)}, f32[1344,128]{1,0:T(8,128)S(1)}, u32[]{:S(2)}, u32[]{:S(2)}) collective-permute-start(f32[1344,128]{1,0:T(8,128)S(1)} %get-tuple-element.54), channel_id=1, source_target_pairs={{8,0},{16,8},{24,16},{9,1},{17,9},{25,17},{10,2},{18,10},{26,18},{... | collective-permute-start | bytes 2064392 | tf_op jit(solution)/shard_map/ppermute | solution.py:749
  34.7 0.0 copy-done.15
  34.7 0.0 copy-done.16
  34.7 0.0 copy-start.14
  34.7 0.0 copy-done.6
  34.7 0.0 copy-done.7
  34.8 0.0 copy-done.9
  34.8 0.0 copy-done.10
  34.8 0.0 copy-done.11
  34.8 0.6 copy-done.14
  35.4 0.0 copy-start.3
  35.4 62.6 %pair_forces.1 = (f32[1024,128]{1,0:T(8,128)S(1)}, f32[128,128]{1,0:T(8,128)S(1)}, f32[128,128]{1,0:T(8,128)S(1)}, f32[128,128]{1,0:T(8,128)S(1)}, f32[128,128]{...) custom-call(s32[1024]{0:T(1024)S(1)} %copy-done.14, ...), custom_call_target="tpu_custom_call" | custom-call | flops 335544320 | bytes 4194304 | tf_op jit(solution)/shard_map/pair_forces/pallas_call | solution.py:258
  98.0 3.1 %collective-permute-start.12 = (f32[128,128]{1,0:T(8,128)S(1)}, f32[128,128]{1,0:T(8,128)S(1)}, u32[]{:S(2)}, u32[]{:S(2)}) collective-permute-start(f32[128,128]{1,0:T(8,128)S(1)} %get-tuple-element.61), channel_id=1, source_target_pairs={{8,0},{16,8},{24,16},{9,1},{17,9},{25,17},{10,2},{18,10},{26,18},{... | collective-permute-start | bytes 196616 | tf_op jit(solution)/shard_map/ppermute | solution.py:749
  101.1 2.1 %collective-permute-start.13 = (f32[128,128]{1,0:T(8,128)S(1)}, f32[128,128]{1,0:T(8,128)S(1)}, u32[]{:S(2)}, u32[]{:S(2)}) collective-permute-start(f32[128,128]{1,0:T(8,128)S(1)} %get-tuple-element.62), channel_id=1, source_target_pairs={{0,8},{8,16},{16,24},{1,9},{9,17},{17,25},{2,10},{10,18},{18,26},{... | collective-permute-start | bytes 196616 | tf_op jit(solution)/shard_map/ppermute | solution.py:749
  103.3 5.6 %collective-permute-start.8 = (f32[128,128]{1,0:T(8,128)S(1)}, f32[128,128]{1,0:T(8,128)S(1)}, u32[]{:S(2)}, u32[]{:S(2)}) collective-permute-start(f32[128,128]{1,0:T(8,128)S(1)} %get-tuple-element.57), channel_id=1, source_target_pairs={{1,0},{2,1},{3,2},{4,3},{5,4},{6,5},{7,6},{9,8},{10,9},{11,10},{12... | collective-permute-start | bytes 196616 | tf_op jit(solution)/shard_map/ppermute | solution.py:749
  108.9 0.0 collective-permute-done.12
  108.9 3.1 %collective-permute-start.9 = (f32[128,128]{1,0:T(8,128)S(1)}, f32[128,128]{1,0:T(8,128)S(1)}, u32[]{:S(2)}, u32[]{:S(2)}) collective-permute-start(f32[128,128]{1,0:T(8,128)S(1)} %get-tuple-element.58), channel_id=1, source_target_pairs={{0,1},{1,2},{2,3},{3,4},{4,5},{5,6},{6,7},{8,9},{9,10},{10,11},{11... | collective-permute-start | bytes 196616 | tf_op jit(solution)/shard_map/ppermute | solution.py:749
  112.0 0.0 collective-permute-done.6.refs_8_
  112.0 2.1 %collective-permute-start.10 = (f32[128,128]{1,0:T(8,128)S(1)}, f32[128,128]{1,0:T(8,128)S(1)}, u32[]{:S(2)}, u32[]{:S(2)}) collective-permute-start(f32[128,128]{1,0:T(8,128)S(1)} %get-tuple-element.59), channel_id=1, source_target_pairs={{2,0},{3,1},{4,2},{5,3},{6,4},{7,5},{10,8},{11,9},{12,10},{13,11},... | collective-permute-start | bytes 196616 | tf_op jit(solution)/shard_map/ppermute | solution.py:749
  114.1 0.0 collective-permute-done.7.refs_9_
  114.1 0.0 copy-start.13
  114.1 3.2 %collective-permute-start.11 = (f32[128,128]{1,0:T(8,128)S(1)}, f32[128,128]{1,0:T(8,128)S(1)}, u32[]{:S(2)}, u32[]{:S(2)}) collective-permute-start(f32[128,128]{1,0:T(8,128)S(1)} %get-tuple-element.60), channel_id=1, source_target_pairs={{0,2},{1,3},{2,4},{3,5},{4,6},{5,7},{8,10},{9,11},{10,12},{11,13},... | collective-permute-start | bytes 196616 | tf_op jit(solution)/shard_map/ppermute | solution.py:749
  117.3 0.0 copy-done.3
  117.3 0.0 copy-done.5
  117.4 0.0 copy-done.8
  117.4 0.0 copy-done.13
  117.4 11.5 %grid_step.1 = (f32[16,32,256]{2,1,0:T(8,128)}, f32[16,32,256]{2,1,0:T(8,128)}, f32[1024,128]{1,0:T(8,128)S(1)}) custom-call(s32[256]{0:T(256)S(1)} %copy-done.13, f32[256,128]{1,0:T(8,128)S(1)} %copy-done.8, f32[16,32,256]{2,1,0:T(8,128)S(1)} %copy-done.1, f32[16,32,256]{2,1,0:T(8,128)S(1)} %copy-done.3, f32[16,32,256]{2,1,0:T(8,128)S(1)} %copy-done.5, ...), custom_call_target="tpu_custom_call" | custom-call | flops 31948800 | bytes 8388608 | tf_op jit(solution)/shard_map/grid_step/pallas_call | solution.py:689
  128.9 0.0 collective-permute-done.13
  128.9 0.0 collective-permute-done.8
  128.9 0.0 collective-permute-done.9
  128.9 0.0 collective-permute-done.10
  128.9 0.0 collective-permute-done.11
  128.9 0.0 copy-start.12
  128.9 0.7 copy-done.12
  129.6 2.8 %gather_forces.1 = f32[3,32768]{1,0:T(4,128)} custom-call(s32[7,32]{1,0:T(8,128)S(1)} %copy-done.12, f32[256,4,128]{2,1,0:T(4,128)S(1)} %bitcast.13, f32[256,4,128]{2,1,0:T(4,128)S(1)} %bitcast.14, f32[32,4,128]{2,1,0:T(4,128)S(1)} %bitcast.15, f32[32,4,128]{2,1,0:T(4,128)S(1)} %bitcast.18, f32[32,4,128]{2,1,0:T(4,128)S(1)} %bitcast.19, ...), custom_call_target="tpu_custom_call" | custom-call | tf_op jit(solution)/shard_map/gather_forces/pallas_call | solution.py:735
  (4 shorter events, 0.0 us)
Async XLA Ops:
  0.6 25.5 %copy-start = (f32[16,32,256]{2,1,0:T(8,128)S(1)}, f32[16,32,256]{2,1,0:T(8,128)}, u32[]{:S(2)}) copy-start(f32[16,32,256]{2,1,0:T(8,128)} %refs_5_.1) | copy-start | bytes 1572868
  0.6 25.4 %copy-start.1 = (f32[16,32,256]{2,1,0:T(8,128)S(1)}, f32[16,32,256]{2,1,0:T(8,128)}, u32[]{:S(2)}) copy-start(f32[16,32,256]{2,1,0:T(8,128)} %refs_2_.2) | copy-start | bytes 1572868
  6.7 19.4 %collective-permute-start = (f32[640,128]{1,0:T(8,128)}, f32[640,128]{1,0:T(8,128)S(1)}, u32[]{:S(2)}, u32[]{:S(2)}) collective-permute-start(f32[640,128]{1,0:T(8,128)} %get-tuple-element.36), channel_id=1, source_target_pairs={{0,1},{1,2},{2,3},{3,4},{4,5},{5,6},{6,7},{8,9},{9,10},{10,11},{11... | collective-permute-start | bytes 983048 | tf_op jit(solution)/shard_map/ppermute | solution.py:749
  10.5 15.6 %collective-permute-start.1 = (f32[640,128]{1,0:T(8,128)}, f32[640,128]{1,0:T(8,128)S(1)}, u32[]{:S(2)}, u32[]{:S(2)}) collective-permute-start(f32[640,128]{1,0:T(8,128)} %get-tuple-element.37), channel_id=1, source_target_pairs={{1,0},{2,1},{3,2},{4,3},{5,4},{6,5},{7,6},{9,8},{10,9},{11,10},{12... | collective-permute-start | bytes 983048 | tf_op jit(solution)/shard_map/ppermute | solution.py:749
  12.4 8.4 %collective-permute-start.2 = (f32[128,128]{1,0:T(8,128)}, f32[128,128]{1,0:T(8,128)S(1)}, u32[]{:S(2)}, u32[]{:S(2)}) collective-permute-start(f32[128,128]{1,0:T(8,128)} %get-tuple-element.38), channel_id=1, source_target_pairs={{0,2},{1,3},{2,4},{3,5},{4,6},{5,7},{8,10},{9,11},{10,12},{11,13},... | collective-permute-start | bytes 196616 | tf_op jit(solution)/shard_map/ppermute | solution.py:749
  15.6 8.3 %collective-permute-start.3 = (f32[128,128]{1,0:T(8,128)}, f32[128,128]{1,0:T(8,128)S(1)}, u32[]{:S(2)}, u32[]{:S(2)}) collective-permute-start(f32[128,128]{1,0:T(8,128)} %get-tuple-element.39), channel_id=1, source_target_pairs={{2,0},{3,1},{4,2},{5,3},{6,4},{7,5},{10,8},{11,9},{12,10},{13,11},... | collective-permute-start | bytes 196616 | tf_op jit(solution)/shard_map/ppermute | solution.py:749
  17.7 6.2 %collective-permute-start.4 = (f32[128,128]{1,0:T(8,128)}, f32[128,128]{1,0:T(8,128)S(1)}, u32[]{:S(2)}, u32[]{:S(2)}) collective-permute-start(f32[128,128]{1,0:T(8,128)} %get-tuple-element.40), channel_id=1, source_target_pairs={{0,8},{8,16},{16,24},{1,9},{9,17},{17,25},{2,10},{10,18},{18,26},{... | collective-permute-start | bytes 196616 | tf_op jit(solution)/shard_map/ppermute | solution.py:749
  20.9 5.2 %collective-permute-start.5 = (f32[128,128]{1,0:T(8,128)}, f32[128,128]{1,0:T(8,128)S(1)}, u32[]{:S(2)}, u32[]{:S(2)}) collective-permute-start(f32[128,128]{1,0:T(8,128)} %get-tuple-element.41), channel_id=1, source_target_pairs={{8,0},{16,8},{24,16},{9,1},{17,9},{25,17},{10,2},{18,10},{26,18},{... | collective-permute-start | bytes 196616 | tf_op jit(solution)/shard_map/ppermute | solution.py:749
  26.1 1.0 copy-start.2
  27.1 1.0 copy-start.4
  28.2 6.5 %copy-start.15 = (s32[1024]{0:T(1024)S(1)}, s32[1024]{0:T(1024)}, u32[]{:S(2)}) copy-start(s32[1024]{0:T(1024)} %param.23) | copy-start | bytes 12292
  28.2 6.5 %copy-start.16 = (s32[1024]{0:T(1024)S(1)}, s32[1024]{0:T(1024)}, u32[]{:S(2)}) copy-start(s32[1024]{0:T(1024)} %param.22) | copy-start | bytes 12292
  28.2 6.5 %copy-start.6 = (f32[256,4,128]{2,1,0:T(4,128)S(1)}, f32[256,4,128]{2,1,0:T(4,128)}, u32[]{:S(2)}) copy-start(f32[256,4,128]{2,1,0:T(4,128)} %get-tuple-element.34) | copy-start | bytes 1572868
  28.2 6.6 %copy-start.7 = (bf16[128,1024]{1,0:T(8,128)(2,1)S(1)}, bf16[128,1024]{1,0:T(8,128)(2,1)}, u32[]{:S(2)}) copy-start(bf16[128,1024]{1,0:T(8,128)(2,1)} %constant.8.clone.refs_0_) | copy-start | bytes 786436
  28.2 6.6 %copy-start.9 = (bf16[256,128]{1,0:T(8,128)(2,1)S(1)}, bf16[256,128]{1,0:T(8,128)(2,1)}, u32[]{:S(2)}) copy-start(bf16[256,128]{1,0:T(8,128)(2,1)} %constant.9.clone.refs_1_) | copy-start | bytes 196612
  28.2 6.6 %copy-start.10 = (f32[128,128]{1,0:T(8,128)S(1)}, f32[128,128]{1,0:T(8,128)}, u32[]{:S(2)}) copy-start(f32[128,128]{1,0:T(8,128)} %get-tuple-element.42.refs_4_) | copy-start | bytes 196612
  28.2 6.6 %copy-start.11 = (bf16[128,128]{1,0:T(8,128)(2,1)S(1)}, bf16[128,128]{1,0:T(8,128)(2,1)}, u32[]{:S(2)}) copy-start(bf16[128,128]{1,0:T(8,128)(2,1)} %constant.10.clone.refs_2_) | copy-start | bytes 98308
  28.4 83.6 %collective-permute-start.6 = (f32[1344,128]{1,0:T(8,128)S(1)}, f32[1344,128]{1,0:T(8,128)S(1)}, u32[]{:S(2)}, u32[]{:S(2)}) collective-permute-start(f32[1344,128]{1,0:T(8,128)S(1)} %get-tuple-element.53), channel_id=1, source_target_pairs={{0,8},{8,16},{16,24},{1,9},{9,17},{17,25},{2,10},{10,18},{18,26},{... | collective-permute-start | bytes 2064392 | tf_op jit(solution)/shard_map/ppermute | solution.py:749
  30.4 83.7 %collective-permute-start.7 = (f32[1344,128]{1,0:T(8,128)S(1)}, f32[1344,128]{1,0:T(8,128)S(1)}, u32[]{:S(2)}, u32[]{:S(2)}) collective-permute-start(f32[1344,128]{1,0:T(8,128)S(1)} %get-tuple-element.54), channel_id=1, source_target_pairs={{8,0},{16,8},{24,16},{9,1},{17,9},{25,17},{10,2},{18,10},{26,18},{... | collective-permute-start | bytes 2064392 | tf_op jit(solution)/shard_map/ppermute | solution.py:749
  34.7 0.7 copy-start.14
  35.4 81.9 %copy-start.3 = (f32[16,32,256]{2,1,0:T(8,128)S(1)}, f32[16,32,256]{2,1,0:T(8,128)}, u32[]{:S(2)}) copy-start(f32[16,32,256]{2,1,0:T(8,128)} %get-tuple-element.51.refs_1_.refs_3_) | copy-start | bytes 1572868
  35.4 81.9 %copy-start.5 = (f32[16,32,256]{2,1,0:T(8,128)S(1)}, f32[16,32,256]{2,1,0:T(8,128)}, u32[]{:S(2)}) copy-start(f32[16,32,256]{2,1,0:T(8,128)} %get-tuple-element.52.refs_2_.refs_4_) | copy-start | bytes 1572868
  35.4 81.9 %copy-start.8 = (f32[256,128]{1,0:T(8,128)S(1)}, f32[256,128]{1,0:T(8,128)}, u32[]{:S(2)}) copy-start(f32[256,128]{1,0:T(8,128)} %get-tuple-element.50.refs_1_) | copy-start | bytes 393220
  98.0 10.9 %collective-permute-start.12 = (f32[128,128]{1,0:T(8,128)S(1)}, f32[128,128]{1,0:T(8,128)S(1)}, u32[]{:S(2)}, u32[]{:S(2)}) collective-permute-start(f32[128,128]{1,0:T(8,128)S(1)} %get-tuple-element.61), channel_id=1, source_target_pairs={{8,0},{16,8},{24,16},{9,1},{17,9},{25,17},{10,2},{18,10},{26,18},{... | collective-permute-start | bytes 196616 | tf_op jit(solution)/shard_map/ppermute | solution.py:749
  101.1 27.8 %collective-permute-start.13 = (f32[128,128]{1,0:T(8,128)S(1)}, f32[128,128]{1,0:T(8,128)S(1)}, u32[]{:S(2)}, u32[]{:S(2)}) collective-permute-start(f32[128,128]{1,0:T(8,128)S(1)} %get-tuple-element.62), channel_id=1, source_target_pairs={{0,8},{8,16},{16,24},{1,9},{9,17},{17,25},{2,10},{10,18},{18,26},{... | collective-permute-start | bytes 196616 | tf_op jit(solution)/shard_map/ppermute | solution.py:749
  103.3 25.6 %collective-permute-start.8 = (f32[128,128]{1,0:T(8,128)S(1)}, f32[128,128]{1,0:T(8,128)S(1)}, u32[]{:S(2)}, u32[]{:S(2)}) collective-permute-start(f32[128,128]{1,0:T(8,128)S(1)} %get-tuple-element.57), channel_id=1, source_target_pairs={{1,0},{2,1},{3,2},{4,3},{5,4},{6,5},{7,6},{9,8},{10,9},{11,10},{12... | collective-permute-start | bytes 196616 | tf_op jit(solution)/shard_map/ppermute | solution.py:749
  108.9 20.0 %collective-permute-start.9 = (f32[128,128]{1,0:T(8,128)S(1)}, f32[128,128]{1,0:T(8,128)S(1)}, u32[]{:S(2)}, u32[]{:S(2)}) collective-permute-start(f32[128,128]{1,0:T(8,128)S(1)} %get-tuple-element.58), channel_id=1, source_target_pairs={{0,1},{1,2},{2,3},{3,4},{4,5},{5,6},{6,7},{8,9},{9,10},{10,11},{11... | collective-permute-start | bytes 196616 | tf_op jit(solution)/shard_map/ppermute | solution.py:749
  112.0 16.9 %collective-permute-start.10 = (f32[128,128]{1,0:T(8,128)S(1)}, f32[128,128]{1,0:T(8,128)S(1)}, u32[]{:S(2)}, u32[]{:S(2)}) collective-permute-start(f32[128,128]{1,0:T(8,128)S(1)} %get-tuple-element.59), channel_id=1, source_target_pairs={{2,0},{3,1},{4,2},{5,3},{6,4},{7,5},{10,8},{11,9},{12,10},{13,11},... | collective-permute-start | bytes 196616 | tf_op jit(solution)/shard_map/ppermute | solution.py:749
  114.1 3.2 %copy-start.13 = (s32[256]{0:T(256)S(1)}, s32[256]{0:T(256)}, u32[]{:S(2)}) copy-start(s32[256]{0:T(256)} %refs_0_.4) | copy-start | bytes 3076
  114.1 14.8 %collective-permute-start.11 = (f32[128,128]{1,0:T(8,128)S(1)}, f32[128,128]{1,0:T(8,128)S(1)}, u32[]{:S(2)}, u32[]{:S(2)}) collective-permute-start(f32[128,128]{1,0:T(8,128)S(1)} %get-tuple-element.60), channel_id=1, source_target_pairs={{0,2},{1,3},{2,4},{3,5},{4,6},{5,7},{8,10},{9,11},{10,12},{11,13},... | collective-permute-start | bytes 196616 | tf_op jit(solution)/shard_map/ppermute | solution.py:749
  128.9 0.7 copy-start.12

commit v11 on v10

--- a/solution.py
+++ b/solution.py
@@ -136,7 +136,7 @@
     own_sum_ref[...] = jnp.zeros_like(own_sum_ref)
     other_sum_ref[...] = jnp.zeros_like(other_sum_ref)
     dist_refs, weight_refs = (passed_refs[:2], passed_refs[2:])
-    dist_refs[0][...] = jnp.full(dist_refs[0].shape, 1e38, jnp.float32)
+    dist_refs[0][...] = jnp.full(dist_refs[0].shape, 1e30, jnp.float32)
     weight_refs[0][...] = jnp.zeros_like(weight_refs[0])
 
     def block_diagonal(blocks):
@@ -160,8 +160,11 @@
             )
 
     def weights(unit, turn, dist_ref, weight_ref):
-        root = lax.rsqrt(dist_ref[unit, :, 128 * turn : 128 * turn + 128])
-        weight = root * root * root
+        dist = dist_ref[unit, :, 128 * turn : 128 * turn + 128]
+        root = lax.rsqrt(dist.astype(jnp.bfloat16)).astype(jnp.float32)
+        square = root * root
+        error = 1.0 - dist * square
+        weight = (square * root) * (1.0 + error * (1.5 + 1.875 * error))
         high = weight.astype(jnp.bfloat16)
         weight_ref[unit, 128 * turn : 128 * turn + 128, :128] = high
         weight_ref[unit, 128 * turn : 128 * turn + 128, 128:] = (

time: 134 us -> 149 us (1.11)
  Pallas kernels: 83 us -> 98.2 us
    pallas_call x1, Pallas kernels: 62.6 us -> 77.8 us  [pair_forces(): pl.pallas_call(pair_kernel, out_shape=(jax.ShapeDtypeStruct(own.shape, jn...]
  transfers between devices with their start and end apart: 14 -> 14, of which waited for: 1 -> 1; matrix products, arithmetic and copies ran while one was open for 0% -> 0% of each run, Pallas kernels for 56% -> 61%
where the time goes in v11:
time: 149 us; the launch traced here: 148 us
  Pallas kernels  98.2 us (66%)
  starting transfers between devices  42.7 us (29%)
  local copies, waits for them, and re-layouts  3.44 us (2%)
  waiting for transfers between devices  2.16 us (1%)
    pallas_call x1, Pallas kernels, pair_forces(): pl.pallas_call(pair_kernel, out_shape=(jax.ShapeDtypeStruct(own.shape, jn...  77.8 us
    ppermute x14, starting transfers between devices, passed_along(): return lax.ppermute(shard, axis, pairs)  42.7 us
    pallas_call x1, Pallas kernels, grid_step(): pl.pallas_call(functools.partial(grid_kernel, base), out_shape=(jax.Shape...  11.5 us
    pallas_call x1, Pallas kernels, prepare(): pl.pallas_call(prepare_kernel, out_shape=(jax.ShapeDtypeStruct((clusters,...  6.06 us
    unnamed x34, local copies, waits for them, and re-layouts  3.44 us
  transfers between devices with their start and end apart: 14, of which 1 were waited for; matrix products, arithmetic and copies ran while one was open for 0% of the time, Pallas kernels for 61%

profile of v11, /device:TPU:13, one launch (start us, length us, event | category | flops | bytes accessed | tf_op | source)
XLA Modules:
  0.0 147.5 jit_solution(15794084669431391254)
XLA Ops:
  0.6 0.0 copy-start
  0.6 0.0 copy-start.1
  0.7 6.1 %prepare.1 = (f32[256,4,128]{2,1,0:T(4,128)}, f32[256,128]{1,0:T(8,128)}, f32[16,32,256]{2,1,0:T(8,128)}, f32[16,32,256]{2,1,0:T(8,128)}, f32[128,128]{1,0:T(8,1...) custom-call(s32[256]{0:T(256)} %fill_ref.1, ...), custom_call_target="tpu_custom_call" | custom-call | tf_op jit(solution)/shard_map/prepare/pallas_call | solution.py:416
  6.7 3.8 %collective-permute-start = (f32[640,128]{1,0:T(8,128)}, f32[640,128]{1,0:T(8,128)S(1)}, u32[]{:S(2)}, u32[]{:S(2)}) collective-permute-start(f32[640,128]{1,0:T(8,128)} %get-tuple-element.36), channel_id=1, source_target_pairs={{0,1},{1,2},{2,3},{3,4},{4,5},{5,6},{6,7},{8,9},{9,10},{10,11},{11... | collective-permute-start | bytes 983048 | tf_op jit(solution)/shard_map/ppermute | solution.py:752
  10.5 1.9 %collective-permute-start.1 = (f32[640,128]{1,0:T(8,128)}, f32[640,128]{1,0:T(8,128)S(1)}, u32[]{:S(2)}, u32[]{:S(2)}) collective-permute-start(f32[640,128]{1,0:T(8,128)} %get-tuple-element.37), channel_id=1, source_target_pairs={{1,0},{2,1},{3,2},{4,3},{5,4},{6,5},{7,6},{9,8},{10,9},{11,10},{12... | collective-permute-start | bytes 983048 | tf_op jit(solution)/shard_map/ppermute | solution.py:752
  12.4 3.2 %collective-permute-start.2 = (f32[128,128]{1,0:T(8,128)}, f32[128,128]{1,0:T(8,128)S(1)}, u32[]{:S(2)}, u32[]{:S(2)}) collective-permute-start(f32[128,128]{1,0:T(8,128)} %get-tuple-element.38), channel_id=1, source_target_pairs={{0,2},{1,3},{2,4},{3,5},{4,6},{5,7},{8,10},{9,11},{10,12},{11,13},... | collective-permute-start | bytes 196616 | tf_op jit(solution)/shard_map/ppermute | solution.py:752
  15.6 2.1 %collective-permute-start.3 = (f32[128,128]{1,0:T(8,128)}, f32[128,128]{1,0:T(8,128)S(1)}, u32[]{:S(2)}, u32[]{:S(2)}) collective-permute-start(f32[128,128]{1,0:T(8,128)} %get-tuple-element.39), channel_id=1, source_target_pairs={{2,0},{3,1},{4,2},{5,3},{6,4},{7,5},{10,8},{11,9},{12,10},{13,11},... | collective-permute-start | bytes 196616 | tf_op jit(solution)/shard_map/ppermute | solution.py:752
  17.7 3.1 %collective-permute-start.4 = (f32[128,128]{1,0:T(8,128)}, f32[128,128]{1,0:T(8,128)S(1)}, u32[]{:S(2)}, u32[]{:S(2)}) collective-permute-start(f32[128,128]{1,0:T(8,128)} %get-tuple-element.40), channel_id=1, source_target_pairs={{0,8},{8,16},{16,24},{1,9},{9,17},{17,25},{2,10},{10,18},{18,26},{... | collective-permute-start | bytes 196616 | tf_op jit(solution)/shard_map/ppermute | solution.py:752
  20.8 0.0 collective-permute-done.2.refs_7_
  20.9 3.1 %collective-permute-start.5 = (f32[128,128]{1,0:T(8,128)}, f32[128,128]{1,0:T(8,128)S(1)}, u32[]{:S(2)}, u32[]{:S(2)}) collective-permute-start(f32[128,128]{1,0:T(8,128)} %get-tuple-element.41), channel_id=1, source_target_pairs={{8,0},{16,8},{24,16},{9,1},{17,9},{25,17},{10,2},{18,10},{26,18},{... | collective-permute-start | bytes 196616 | tf_op jit(solution)/shard_map/ppermute | solution.py:752
  23.9 0.0 collective-permute-done.3.refs_8_
  23.9 0.0 collective-permute-done.4.refs_9_
  23.9 2.1 %collective-permute-done.5.refs_10_ = f32[128,128]{1,0:T(8,128)S(1)} collective-permute-done((f32[128,128]{1,0:T(8,128)}, f32[128,128]{1,0:T(8,128)S(1)}, u32[]{:S(2)}, u32[]{:S(2)}) %collective-permute-start.5) | collective-permute-done | bytes 65568 | tf_op jit(solution)/shard_map/ppermute | solution.py:752
  26.1 0.0 collective-permute-done.refs_5_.refs_4_.refs_6_
  26.1 0.0 collective-permute-done.1.refs_6_.refs_5_.refs_7_
  26.1 0.0 copy-done
  26.1 0.0 copy-done.1
  26.1 0.0 copy-start.2
  26.1 1.0 copy-done.2
  27.1 0.0 copy-start.4
  27.1 1.0 copy-done.4
  28.2 0.0 copy-start.15
  28.2 0.0 copy-start.16
  28.2 0.0 copy-start.6
  28.2 0.0 copy-start.7
  28.2 0.0 copy-start.9
  28.2 0.0 copy-start.10
  28.2 0.0 copy-start.11
  28.2 0.1 planes.1
  28.4 2.1 %collective-permute-start.6 = (f32[1344,128]{1,0:T(8,128)S(1)}, f32[1344,128]{1,0:T(8,128)S(1)}, u32[]{:S(2)}, u32[]{:S(2)}) collective-permute-start(f32[1344,128]{1,0:T(8,128)S(1)} %get-tuple-element.53), channel_id=1, source_target_pairs={{0,8},{8,16},{16,24},{1,9},{9,17},{17,25},{2,10},{10,18},{18,26},{... | collective-permute-start | bytes 2064392 | tf_op jit(solution)/shard_map/ppermute | solution.py:752
  30.4 4.3 %collective-permute-start.7 = (f32[1344,128]{1,0:T(8,128)S(1)}, f32[1344,128]{1,0:T(8,128)S(1)}, u32[]{:S(2)}, u32[]{:S(2)}) collective-permute-start(f32[1344,128]{1,0:T(8,128)S(1)} %get-tuple-element.54), channel_id=1, source_target_pairs={{8,0},{16,8},{24,16},{9,1},{17,9},{25,17},{10,2},{18,10},{26,18},{... | collective-permute-start | bytes 2064392 | tf_op jit(solution)/shard_map/ppermute | solution.py:752
  34.7 0.0 copy-done.15
  34.7 0.0 copy-done.16
  34.7 0.0 copy-start.14
  34.7 0.0 copy-done.6
  34.7 0.0 copy-done.7
  34.8 0.0 copy-done.9
  34.8 0.0 copy-done.10
  34.8 0.0 copy-done.11
  34.8 0.6 copy-done.14
  35.4 77.8 %pair_forces.1 = (f32[1024,128]{1,0:T(8,128)S(1)}, f32[128,128]{1,0:T(8,128)S(1)}, f32[128,128]{1,0:T(8,128)S(1)}, f32[128,128]{1,0:T(8,128)S(1)}, f32[128,128]{...) custom-call(s32[1024]{0:T(1024)S(1)} %copy-done.14, ...), custom_call_target="tpu_custom_call" | custom-call | flops 335544320 | bytes 4194304 | tf_op jit(solution)/shard_map/pair_forces/pallas_call | solution.py:261
  113.2 3.1 %collective-permute-start.12 = (f32[128,128]{1,0:T(8,128)S(1)}, f32[128,128]{1,0:T(8,128)S(1)}, u32[]{:S(2)}, u32[]{:S(2)}) collective-permute-start(f32[128,128]{1,0:T(8,128)S(1)} %get-tuple-element.61), channel_id=1, source_target_pairs={{8,0},{16,8},{24,16},{9,1},{17,9},{25,17},{10,2},{18,10},{26,18},{... | collective-permute-start | bytes 196616 | tf_op jit(solution)/shard_map/ppermute | solution.py:752
  116.3 2.2 %collective-permute-start.13 = (f32[128,128]{1,0:T(8,128)S(1)}, f32[128,128]{1,0:T(8,128)S(1)}, u32[]{:S(2)}, u32[]{:S(2)}) collective-permute-start(f32[128,128]{1,0:T(8,128)S(1)} %get-tuple-element.62), channel_id=1, source_target_pairs={{0,8},{8,16},{16,24},{1,9},{9,17},{17,25},{2,10},{10,18},{18,26},{... | collective-permute-start | bytes 196616 | tf_op jit(solution)/shard_map/ppermute | solution.py:752
  118.5 5.6 %collective-permute-start.8 = (f32[128,128]{1,0:T(8,128)S(1)}, f32[128,128]{1,0:T(8,128)S(1)}, u32[]{:S(2)}, u32[]{:S(2)}) collective-permute-start(f32[128,128]{1,0:T(8,128)S(1)} %get-tuple-element.57), channel_id=1, source_target_pairs={{1,0},{2,1},{3,2},{4,3},{5,4},{6,5},{7,6},{9,8},{10,9},{11,10},{12... | collective-permute-start | bytes 196616 | tf_op jit(solution)/shard_map/ppermute | solution.py:752
  124.1 0.0 collective-permute-done.12
  124.1 3.1 %collective-permute-start.9 = (f32[128,128]{1,0:T(8,128)S(1)}, f32[128,128]{1,0:T(8,128)S(1)}, u32[]{:S(2)}, u32[]{:S(2)}) collective-permute-start(f32[128,128]{1,0:T(8,128)S(1)} %get-tuple-element.58), channel_id=1, source_target_pairs={{0,1},{1,2},{2,3},{3,4},{4,5},{5,6},{6,7},{8,9},{9,10},{10,11},{11... | collective-permute-start | bytes 196616 | tf_op jit(solution)/shard_map/ppermute | solution.py:752
  127.2 0.0 collective-permute-done.6.refs_8_
  127.2 2.1 %collective-permute-start.10 = (f32[128,128]{1,0:T(8,128)S(1)}, f32[128,128]{1,0:T(8,128)S(1)}, u32[]{:S(2)}, u32[]{:S(2)}) collective-permute-start(f32[128,128]{1,0:T(8,128)S(1)} %get-tuple-element.59), channel_id=1, source_target_pairs={{2,0},{3,1},{4,2},{5,3},{6,4},{7,5},{10,8},{11,9},{12,10},{13,11},... | collective-permute-start | bytes 196616 | tf_op jit(solution)/shard_map/ppermute | solution.py:752
  129.3 0.0 collective-permute-done.7.refs_9_
  129.3 0.0 copy-start.13
  129.3 3.2 %collective-permute-start.11 = (f32[128,128]{1,0:T(8,128)S(1)}, f32[128,128]{1,0:T(8,128)S(1)}, u32[]{:S(2)}, u32[]{:S(2)}) collective-permute-start(f32[128,128]{1,0:T(8,128)S(1)} %get-tuple-element.60), channel_id=1, source_target_pairs={{0,2},{1,3},{2,4},{3,5},{4,6},{5,7},{8,10},{9,11},{10,12},{11,13},... | collective-permute-start | bytes 196616 | tf_op jit(solution)/shard_map/ppermute | solution.py:752
  132.5 0.0 copy-done.3
  132.5 0.0 copy-done.5
  132.5 0.0 copy-done.8
  132.5 0.0 copy-done.13
  132.5 11.5 %grid_step.1 = (f32[16,32,256]{2,1,0:T(8,128)}, f32[16,32,256]{2,1,0:T(8,128)}, f32[1024,128]{1,0:T(8,128)S(1)}) custom-call(s32[256]{0:T(256)S(1)} %copy-done.13, f32[256,128]{1,0:T(8,128)S(1)} %copy-done.8, f32[16,32,256]{2,1,0:T(8,128)S(1)} %copy-done.1, f32[16,32,256]{2,1,0:T(8,128)S(1)} %copy-done.3, f32[16,32,256]{2,1,0:T(8,128)S(1)} %copy-done.5, ...), custom_call_target="tpu_custom_call" | custom-call | flops 31948800 | bytes 8388608 | tf_op jit(solution)/shard_map/grid_step/pallas_call | solution.py:692
  144.0 0.0 collective-permute-done.13
  144.0 0.0 collective-permute-done.8
  144.0 0.0 collective-permute-done.9
  144.0 0.0 collective-permute-done.10
  144.1 0.0 collective-permute-done.11
  144.1 0.0 copy-start.12
  144.1 0.7 copy-done.12
  144.8 2.8 %gather_forces.1 = f32[3,32768]{1,0:T(4,128)} custom-call(s32[7,32]{1,0:T(8,128)S(1)} %copy-done.12, f32[256,4,128]{2,1,0:T(4,128)S(1)} %bitcast.13, f32[256,4,128]{2,1,0:T(4,128)S(1)} %bitcast.14, f32[32,4,128]{2,1,0:T(4,128)S(1)} %bitcast.15, f32[32,4,128]{2,1,0:T(4,128)S(1)} %bitcast.18, f32[32,4,128]{2,1,0:T(4,128)S(1)} %bitcast.19, ...), custom_call_target="tpu_custom_call" | custom-call | tf_op jit(solution)/shard_map/gather_forces/pallas_call | solution.py:738
  (4 shorter events, 0.0 us)
Async XLA Ops:
  0.6 25.5 %copy-start = (f32[16,32,256]{2,1,0:T(8,128)S(1)}, f32[16,32,256]{2,1,0:T(8,128)}, u32[]{:S(2)}) copy-start(f32[16,32,256]{2,1,0:T(8,128)} %refs_5_.1) | copy-start | bytes 1572868
  0.6 25.4 %copy-start.1 = (f32[16,32,256]{2,1,0:T(8,128)S(1)}, f32[16,32,256]{2,1,0:T(8,128)}, u32[]{:S(2)}) copy-start(f32[16,32,256]{2,1,0:T(8,128)} %refs_2_.2) | copy-start | bytes 1572868
  6.7 19.4 %collective-permute-start = (f32[640,128]{1,0:T(8,128)}, f32[640,128]{1,0:T(8,128)S(1)}, u32[]{:S(2)}, u32[]{:S(2)}) collective-permute-start(f32[640,128]{1,0:T(8,128)} %get-tuple-element.36), channel_id=1, source_target_pairs={{0,1},{1,2},{2,3},{3,4},{4,5},{5,6},{6,7},{8,9},{9,10},{10,11},{11... | collective-permute-start | bytes 983048 | tf_op jit(solution)/shard_map/ppermute | solution.py:752
  10.5 15.6 %collective-permute-start.1 = (f32[640,128]{1,0:T(8,128)}, f32[640,128]{1,0:T(8,128)S(1)}, u32[]{:S(2)}, u32[]{:S(2)}) collective-permute-start(f32[640,128]{1,0:T(8,128)} %get-tuple-element.37), channel_id=1, source_target_pairs={{1,0},{2,1},{3,2},{4,3},{5,4},{6,5},{7,6},{9,8},{10,9},{11,10},{12... | collective-permute-start | bytes 983048 | tf_op jit(solution)/shard_map/ppermute | solution.py:752
  12.4 8.4 %collective-permute-start.2 = (f32[128,128]{1,0:T(8,128)}, f32[128,128]{1,0:T(8,128)S(1)}, u32[]{:S(2)}, u32[]{:S(2)}) collective-permute-start(f32[128,128]{1,0:T(8,128)} %get-tuple-element.38), channel_id=1, source_target_pairs={{0,2},{1,3},{2,4},{3,5},{4,6},{5,7},{8,10},{9,11},{10,12},{11,13},... | collective-permute-start | bytes 196616 | tf_op jit(solution)/shard_map/ppermute | solution.py:752
  15.6 8.3 %collective-permute-start.3 = (f32[128,128]{1,0:T(8,128)}, f32[128,128]{1,0:T(8,128)S(1)}, u32[]{:S(2)}, u32[]{:S(2)}) collective-permute-start(f32[128,128]{1,0:T(8,128)} %get-tuple-element.39), channel_id=1, source_target_pairs={{2,0},{3,1},{4,2},{5,3},{6,4},{7,5},{10,8},{11,9},{12,10},{13,11},... | collective-permute-start | bytes 196616 | tf_op jit(solution)/shard_map/ppermute | solution.py:752
  17.7 6.2 %collective-permute-start.4 = (f32[128,128]{1,0:T(8,128)}, f32[128,128]{1,0:T(8,128)S(1)}, u32[]{:S(2)}, u32[]{:S(2)}) collective-permute-start(f32[128,128]{1,0:T(8,128)} %get-tuple-element.40), channel_id=1, source_target_pairs={{0,8},{8,16},{16,24},{1,9},{9,17},{17,25},{2,10},{10,18},{18,26},{... | collective-permute-start | bytes 196616 | tf_op jit(solution)/shard_map/ppermute | solution.py:752
  20.9 5.2 %collective-permute-start.5 = (f32[128,128]{1,0:T(8,128)}, f32[128,128]{1,0:T(8,128)S(1)}, u32[]{:S(2)}, u32[]{:S(2)}) collective-permute-start(f32[128,128]{1,0:T(8,128)} %get-tuple-element.41), channel_id=1, source_target_pairs={{8,0},{16,8},{24,16},{9,1},{17,9},{25,17},{10,2},{18,10},{26,18},{... | collective-permute-start | bytes 196616 | tf_op jit(solution)/shard_map/ppermute | solution.py:752
  26.1 1.0 copy-start.2
  27.1 1.0 copy-start.4
  28.2 6.5 %copy-start.15 = (s32[1024]{0:T(1024)S(1)}, s32[1024]{0:T(1024)}, u32[]{:S(2)}) copy-start(s32[1024]{0:T(1024)} %param.23) | copy-start | bytes 12292
  28.2 6.5 %copy-start.16 = (s32[1024]{0:T(1024)S(1)}, s32[1024]{0:T(1024)}, u32[]{:S(2)}) copy-start(s32[1024]{0:T(1024)} %param.22) | copy-start | bytes 12292
  28.2 6.5 %copy-start.6 = (f32[256,4,128]{2,1,0:T(4,128)S(1)}, f32[256,4,128]{2,1,0:T(4,128)}, u32[]{:S(2)}) copy-start(f32[256,4,128]{2,1,0:T(4,128)} %get-tuple-element.34) | copy-start | bytes 1572868
  28.2 6.6 %copy-start.7 = (bf16[128,1024]{1,0:T(8,128)(2,1)S(1)}, bf16[128,1024]{1,0:T(8,128)(2,1)}, u32[]{:S(2)}) copy-start(bf16[128,1024]{1,0:T(8,128)(2,1)} %constant.8.clone.refs_0_) | copy-start | bytes 786436
  28.2 6.6 %copy-start.9 = (bf16[256,128]{1,0:T(8,128)(2,1)S(1)}, bf16[256,128]{1,0:T(8,128)(2,1)}, u32[]{:S(2)}) copy-start(bf16[256,128]{1,0:T(8,128)(2,1)} %constant.9.clone.refs_1_) | copy-start | bytes 196612
  28.2 6.6 %copy-start.10 = (f32[128,128]{1,0:T(8,128)S(1)}, f32[128,128]{1,0:T(8,128)}, u32[]{:S(2)}) copy-start(f32[128,128]{1,0:T(8,128)} %get-tuple-element.42.refs_4_) | copy-start | bytes 196612
  28.2 6.6 %copy-start.11 = (bf16[128,128]{1,0:T(8,128)(2,1)S(1)}, bf16[128,128]{1,0:T(8,128)(2,1)}, u32[]{:S(2)}) copy-start(bf16[128,128]{1,0:T(8,128)(2,1)} %constant.10.clone.refs_2_) | copy-start | bytes 98308
  28.4 98.8 %collective-permute-start.6 = (f32[1344,128]{1,0:T(8,128)S(1)}, f32[1344,128]{1,0:T(8,128)S(1)}, u32[]{:S(2)}, u32[]{:S(2)}) collective-permute-start(f32[1344,128]{1,0:T(8,128)S(1)} %get-tuple-element.53), channel_id=1, source_target_pairs={{0,8},{8,16},{16,24},{1,9},{9,17},{17,25},{2,10},{10,18},{18,26},{... | collective-permute-start | bytes 2064392 | tf_op jit(solution)/shard_map/ppermute | solution.py:752
  30.4 98.9 %collective-permute-start.7 = (f32[1344,128]{1,0:T(8,128)S(1)}, f32[1344,128]{1,0:T(8,128)S(1)}, u32[]{:S(2)}, u32[]{:S(2)}) collective-permute-start(f32[1344,128]{1,0:T(8,128)S(1)} %get-tuple-element.54), channel_id=1, source_target_pairs={{8,0},{16,8},{24,16},{9,1},{17,9},{25,17},{10,2},{18,10},{26,18},{... | collective-permute-start | bytes 2064392 | tf_op jit(solution)/shard_map/ppermute | solution.py:752
  34.7 0.7 copy-start.14
  35.4 97.1 %copy-start.3 = (f32[16,32,256]{2,1,0:T(8,128)S(1)}, f32[16,32,256]{2,1,0:T(8,128)}, u32[]{:S(2)}) copy-start(f32[16,32,256]{2,1,0:T(8,128)} %get-tuple-element.51.refs_1_.refs_3_) | copy-start | bytes 1572868
  35.4 97.1 %copy-start.5 = (f32[16,32,256]{2,1,0:T(8,128)S(1)}, f32[16,32,256]{2,1,0:T(8,128)}, u32[]{:S(2)}) copy-start(f32[16,32,256]{2,1,0:T(8,128)} %get-tuple-element.52.refs_2_.refs_4_) | copy-start | bytes 1572868
  35.4 97.1 %copy-start.8 = (f32[256,128]{1,0:T(8,128)S(1)}, f32[256,128]{1,0:T(8,128)}, u32[]{:S(2)}) copy-start(f32[256,128]{1,0:T(8,128)} %get-tuple-element.50.refs_1_) | copy-start | bytes 393220
  113.2 10.9 %collective-permute-start.12 = (f32[128,128]{1,0:T(8,128)S(1)}, f32[128,128]{1,0:T(8,128)S(1)}, u32[]{:S(2)}, u32[]{:S(2)}) collective-permute-start(f32[128,128]{1,0:T(8,128)S(1)} %get-tuple-element.61), channel_id=1, source_target_pairs={{8,0},{16,8},{24,16},{9,1},{17,9},{25,17},{10,2},{18,10},{26,18},{... | collective-permute-start | bytes 196616 | tf_op jit(solution)/shard_map/ppermute | solution.py:752
  116.3 27.8 %collective-permute-start.13 = (f32[128,128]{1,0:T(8,128)S(1)}, f32[128,128]{1,0:T(8,128)S(1)}, u32[]{:S(2)}, u32[]{:S(2)}) collective-permute-start(f32[128,128]{1,0:T(8,128)S(1)} %get-tuple-element.62), channel_id=1, source_target_pairs={{0,8},{8,16},{16,24},{1,9},{9,17},{17,25},{2,10},{10,18},{18,26},{... | collective-permute-start | bytes 196616 | tf_op jit(solution)/shard_map/ppermute | solution.py:752
  118.5 25.6 %collective-permute-start.8 = (f32[128,128]{1,0:T(8,128)S(1)}, f32[128,128]{1,0:T(8,128)S(1)}, u32[]{:S(2)}, u32[]{:S(2)}) collective-permute-start(f32[128,128]{1,0:T(8,128)S(1)} %get-tuple-element.57), channel_id=1, source_target_pairs={{1,0},{2,1},{3,2},{4,3},{5,4},{6,5},{7,6},{9,8},{10,9},{11,10},{12... | collective-permute-start | bytes 196616 | tf_op jit(solution)/shard_map/ppermute | solution.py:752
  124.1 20.0 %collective-permute-start.9 = (f32[128,128]{1,0:T(8,128)S(1)}, f32[128,128]{1,0:T(8,128)S(1)}, u32[]{:S(2)}, u32[]{:S(2)}) collective-permute-start(f32[128,128]{1,0:T(8,128)S(1)} %get-tuple-element.58), channel_id=1, source_target_pairs={{0,1},{1,2},{2,3},{3,4},{4,5},{5,6},{6,7},{8,9},{9,10},{10,11},{11... | collective-permute-start | bytes 196616 | tf_op jit(solution)/shard_map/ppermute | solution.py:752
  127.2 16.9 %collective-permute-start.10 = (f32[128,128]{1,0:T(8,128)S(1)}, f32[128,128]{1,0:T(8,128)S(1)}, u32[]{:S(2)}, u32[]{:S(2)}) collective-permute-start(f32[128,128]{1,0:T(8,128)S(1)} %get-tuple-element.59), channel_id=1, source_target_pairs={{2,0},{3,1},{4,2},{5,3},{6,4},{7,5},{10,8},{11,9},{12,10},{13,11},... | collective-permute-start | bytes 196616 | tf_op jit(solution)/shard_map/ppermute | solution.py:752
  129.3 3.2 %copy-start.13 = (s32[256]{0:T(256)S(1)}, s32[256]{0:T(256)}, u32[]{:S(2)}) copy-start(s32[256]{0:T(256)} %refs_0_.4) | copy-start | bytes 3076
  129.3 14.8 %collective-permute-start.11 = (f32[128,128]{1,0:T(8,128)S(1)}, f32[128,128]{1,0:T(8,128)S(1)}, u32[]{:S(2)}, u32[]{:S(2)}) collective-permute-start(f32[128,128]{1,0:T(8,128)S(1)} %get-tuple-element.60), channel_id=1, source_target_pairs={{0,2},{1,3},{2,4},{3,5},{4,6},{5,7},{8,10},{9,11},{10,12},{11,13},... | collective-permute-start | bytes 196616 | tf_op jit(solution)/shard_map/ppermute | solution.py:752
  144.1 0.7 copy-start.12

commit v12 on v10

--- a/solution.py
+++ b/solution.py
@@ -149,15 +149,14 @@
         ]
         return jnp.concatenate(lines, axis=0)
 
-    def distances(pair, unit, dist_ref):
-        for turn in range(QUAD):
-            own = own_rows_ref[pair + turn]
-            other = other_rows_ref[pair + turn]
-            dist_ref[unit, :, 128 * turn : 128 * turn + 128] = jnp.dot(
-                near_ref[pl.ds(pl.multiple_of(own * 128, 128), 128), 0:32],
-                far_ref[pl.ds(pl.multiple_of(other * 32, 32), 32), :],
-                preferred_element_type=jnp.float32,
-            )
+    def distances(pair, unit, turn, dist_ref):
+        own = own_rows_ref[pair + turn]
+        other = other_rows_ref[pair + turn]
+        dist_ref[unit, :, 128 * turn : 128 * turn + 128] = jnp.dot(
+            near_ref[pl.ds(pl.multiple_of(own * 128, 128), 128), 0:32],
+            far_ref[pl.ds(pl.multiple_of(other * 32, 32), 32), :],
+            preferred_element_type=jnp.float32,
+        )
 
     def weights(unit, turn, dist_ref, weight_ref):
         root = lax.rsqrt(dist_ref[unit, :, 128 * turn : 128 * turn + 128])
@@ -173,42 +172,47 @@
             [moment_ref[pl.ds(pl.multiple_of(index * 16, 16), 16), :] for index in indices]
         )
 
-    def products(pair, unit, weight_ref):
-        owns = [own_rows_ref[pair + turn] for turn in range(QUAD)]
-        others = [other_rows_ref[pair + turn] for turn in range(QUAD)]
-        both = weight_ref[unit]
+    def own_products(others, weight_ref, unit):
         levels = [
             jnp.concatenate(
-                [both[128 * turn : 128 * turn + 128, lanes] for turn in range(QUAD)], axis=1
+                [weight_ref[unit, 128 * turn : 128 * turn + 128, lanes] for turn in range(QUAD)],
+                axis=1,
             )
             for lanes in (slice(0, 128), slice(128, 256))
         ]
-        to_own = lax.dot_general(
+        return lax.dot_general(
             moments_of(other_moment_ref, others),
             jnp.concatenate(levels, axis=0),
             (((1,), (1,)), ((), ())),
             preferred_element_type=jnp.float32,
         )
-        to_other = jnp.dot(
-            moments_of(own_moment_ref, owns), both, preferred_element_type=jnp.float32
-        )
-        return (owns, others, *(part[:, :128] + part[:, 128:] for part in (to_own, to_other)))
+
+    def other_products(owns, weight_ref, unit):
+        return jnp.dot(
+            moments_of(own_moment_ref, owns), weight_ref[unit], preferred_element_type=jnp.float32
+        )
+
+    def add_rows(sum_ref, indices, values):
+        values = values[:, :128] + values[:, 128:]
+        for turn, index in enumerate(indices):
+            at = pl.ds(pl.multiple_of(index * 16, 16), 16)
+            sum_ref[at, :] += values[16 * turn : 16 * turn + 16]
 
     def half_step(step, side):
         last = jnp.maximum(step - 2, 0) * UNROLL
         first = jnp.minimum(step, groups - 1) * UNROLL
-        results = [products(last + QUAD * unit, unit, weight_refs[side]) for unit in range(units)]
         for unit in range(units):
+            owns = [own_rows_ref[last + QUAD * unit + turn] for turn in range(QUAD)]
+            others = [other_rows_ref[last + QUAD * unit + turn] for turn in range(QUAD)]
             for turn in range(QUAD):
+                distances(first + QUAD * unit, unit, turn, dist_refs[1 - side])
+                if turn == 0:
+                    to_own = own_products(others, weight_refs[side], unit)
+                if turn == 2:
+                    to_other = other_products(owns, weight_refs[side], unit)
                 weights(unit, turn, dist_refs[side], weight_refs[1 - side])
-        for unit in range(units):
-            distances(first + QUAD * unit, unit, dist_refs[1 - side])
-        for owns, others, to_own, to_other in results:
-            for turn in range(QUAD):
-                own_at = pl.ds(pl.multiple_of(owns[turn] * 16, 16), 16)
-                other_at = pl.ds(pl.multiple_of(others[turn] * 16, 16), 16)
-                own_sum_ref[own_at, :] += to_own[16 * turn : 16 * turn + 16]
-                other_sum_ref[other_at, :] += to_other[16 * turn : 16 * turn + 16]
+            add_rows(own_sum_ref, owns, to_own)
+            add_rows(other_sum_ref, others, to_other)
 
     def visit(step, _):
         for side in range(2):

time: 134 us -> 125 us (0.933)
  Pallas kernels: 83 us -> 74.4 us
    pallas_call x1, Pallas kernels: 62.6 us -> 53.9 us  [pair_forces(): pl.pallas_call(pair_kernel, out_shape=(jax.ShapeDtypeStruct(own.shape, jn...]
  transfers between devices with their start and end apart: 14 -> 14, of which waited for: 1 -> 1; matrix products, arithmetic and copies ran while one was open for 0% -> 0% of each run, Pallas kernels for 56% -> 53%
where the time goes in v12:
time: 125 us; the launch traced here: 124 us
  Pallas kernels  74.4 us (60%)
  starting transfers between devices  42.8 us (34%)
  local copies, waits for them, and re-layouts  3.44 us (3%)
  waiting for transfers between devices  2.16 us (2%)
    pallas_call x1, Pallas kernels, pair_forces(): pl.pallas_call(pair_kernel, out_shape=(jax.ShapeDtypeStruct(own.shape, jn...  53.9 us
    ppermute x14, starting transfers between devices, passed_along(): return lax.ppermute(shard, axis, pairs)  42.8 us
    pallas_call x1, Pallas kernels, grid_step(): pl.pallas_call(functools.partial(grid_kernel, base), out_shape=(jax.Shape...  11.5 us
    pallas_call x1, Pallas kernels, prepare(): pl.pallas_call(prepare_kernel, out_shape=(jax.ShapeDtypeStruct((clusters,...  6.06 us
    unnamed x34, local copies, waits for them, and re-layouts  3.44 us
    pallas_call x1, Pallas kernels, gather_forces(): pl.pallas_call(gather_forces_kernel, out_shape=jax.ShapeDtypeStruct((3, c...  2.77 us
  transfers between devices with their start and end apart: 14, of which 1 were waited for; matrix products, arithmetic and copies ran while one was open for 0% of the time, Pallas kernels for 53%

profile of v12, /device:TPU:13, one launch (start us, length us, event | category | flops | bytes accessed | tf_op | source)
XLA Modules:
  0.0 123.8 jit_solution(10248792476789231724)
XLA Ops:
  0.6 0.0 copy-start
  0.6 0.0 copy-start.1
  0.7 6.1 %prepare.1 = (f32[256,4,128]{2,1,0:T(4,128)}, f32[256,128]{1,0:T(8,128)}, f32[16,32,256]{2,1,0:T(8,128)}, f32[16,32,256]{2,1,0:T(8,128)}, f32[128,128]{1,0:T(8,1...) custom-call(s32[256]{0:T(256)} %fill_ref.1, ...), custom_call_target="tpu_custom_call" | custom-call | tf_op jit(solution)/shard_map/prepare/pallas_call | solution.py:417
  6.7 3.8 %collective-permute-start = (f32[640,128]{1,0:T(8,128)}, f32[640,128]{1,0:T(8,128)S(1)}, u32[]{:S(2)}, u32[]{:S(2)}) collective-permute-start(f32[640,128]{1,0:T(8,128)} %get-tuple-element.36), channel_id=1, source_target_pairs={{0,1},{1,2},{2,3},{3,4},{4,5},{5,6},{6,7},{8,9},{9,10},{10,11},{11... | collective-permute-start | bytes 983048 | tf_op jit(solution)/shard_map/ppermute | solution.py:753
  10.5 1.9 %collective-permute-start.1 = (f32[640,128]{1,0:T(8,128)}, f32[640,128]{1,0:T(8,128)S(1)}, u32[]{:S(2)}, u32[]{:S(2)}) collective-permute-start(f32[640,128]{1,0:T(8,128)} %get-tuple-element.37), channel_id=1, source_target_pairs={{1,0},{2,1},{3,2},{4,3},{5,4},{6,5},{7,6},{9,8},{10,9},{11,10},{12... | collective-permute-start | bytes 983048 | tf_op jit(solution)/shard_map/ppermute | solution.py:753
  12.4 3.2 %collective-permute-start.2 = (f32[128,128]{1,0:T(8,128)}, f32[128,128]{1,0:T(8,128)S(1)}, u32[]{:S(2)}, u32[]{:S(2)}) collective-permute-start(f32[128,128]{1,0:T(8,128)} %get-tuple-element.38), channel_id=1, source_target_pairs={{0,2},{1,3},{2,4},{3,5},{4,6},{5,7},{8,10},{9,11},{10,12},{11,13},... | collective-permute-start | bytes 196616 | tf_op jit(solution)/shard_map/ppermute | solution.py:753
  15.6 2.1 %collective-permute-start.3 = (f32[128,128]{1,0:T(8,128)}, f32[128,128]{1,0:T(8,128)S(1)}, u32[]{:S(2)}, u32[]{:S(2)}) collective-permute-start(f32[128,128]{1,0:T(8,128)} %get-tuple-element.39), channel_id=1, source_target_pairs={{2,0},{3,1},{4,2},{5,3},{6,4},{7,5},{10,8},{11,9},{12,10},{13,11},... | collective-permute-start | bytes 196616 | tf_op jit(solution)/shard_map/ppermute | solution.py:753
  17.7 3.1 %collective-permute-start.4 = (f32[128,128]{1,0:T(8,128)}, f32[128,128]{1,0:T(8,128)S(1)}, u32[]{:S(2)}, u32[]{:S(2)}) collective-permute-start(f32[128,128]{1,0:T(8,128)} %get-tuple-element.40), channel_id=1, source_target_pairs={{0,8},{8,16},{16,24},{1,9},{9,17},{17,25},{2,10},{10,18},{18,26},{... | collective-permute-start | bytes 196616 | tf_op jit(solution)/shard_map/ppermute | solution.py:753
  20.8 0.0 collective-permute-done.2.refs_7_
  20.9 3.1 %collective-permute-start.5 = (f32[128,128]{1,0:T(8,128)}, f32[128,128]{1,0:T(8,128)S(1)}, u32[]{:S(2)}, u32[]{:S(2)}) collective-permute-start(f32[128,128]{1,0:T(8,128)} %get-tuple-element.41), channel_id=1, source_target_pairs={{8,0},{16,8},{24,16},{9,1},{17,9},{25,17},{10,2},{18,10},{26,18},{... | collective-permute-start | bytes 196616 | tf_op jit(solution)/shard_map/ppermute | solution.py:753
  23.9 0.0 collective-permute-done.3.refs_8_
  23.9 0.0 collective-permute-done.4.refs_9_
  23.9 2.1 %collective-permute-done.5.refs_10_ = f32[128,128]{1,0:T(8,128)S(1)} collective-permute-done((f32[128,128]{1,0:T(8,128)}, f32[128,128]{1,0:T(8,128)S(1)}, u32[]{:S(2)}, u32[]{:S(2)}) %collective-permute-start.5) | collective-permute-done | bytes 65568 | tf_op jit(solution)/shard_map/ppermute | solution.py:753
  26.1 0.0 collective-permute-done.refs_5_.refs_4_.refs_6_
  26.1 0.0 collective-permute-done.1.refs_6_.refs_5_.refs_7_
  26.1 0.0 copy-done
  26.1 0.0 copy-done.1
  26.1 0.0 copy-start.2
  26.1 1.0 copy-done.2
  27.1 0.0 copy-start.4
  27.1 1.0 copy-done.4
  28.2 0.0 copy-start.15
  28.2 0.0 copy-start.16
  28.2 0.0 copy-start.6
  28.2 0.0 copy-start.7
  28.2 0.0 copy-start.9
  28.2 0.0 copy-start.10
  28.2 0.0 copy-start.11
  28.2 0.1 planes.1
  28.4 2.1 %collective-permute-start.6 = (f32[1344,128]{1,0:T(8,128)S(1)}, f32[1344,128]{1,0:T(8,128)S(1)}, u32[]{:S(2)}, u32[]{:S(2)}) collective-permute-start(f32[1344,128]{1,0:T(8,128)S(1)} %get-tuple-element.53), channel_id=1, source_target_pairs={{0,8},{8,16},{16,24},{1,9},{9,17},{17,25},{2,10},{10,18},{18,26},{... | collective-permute-start | bytes 2064392 | tf_op jit(solution)/shard_map/ppermute | solution.py:753
  30.4 4.3 %collective-permute-start.7 = (f32[1344,128]{1,0:T(8,128)S(1)}, f32[1344,128]{1,0:T(8,128)S(1)}, u32[]{:S(2)}, u32[]{:S(2)}) collective-permute-start(f32[1344,128]{1,0:T(8,128)S(1)} %get-tuple-element.54), channel_id=1, source_target_pairs={{8,0},{16,8},{24,16},{9,1},{17,9},{25,17},{10,2},{18,10},{26,18},{... | collective-permute-start | bytes 2064392 | tf_op jit(solution)/shard_map/ppermute | solution.py:753
  34.7 0.0 copy-done.15
  34.7 0.0 copy-done.16
  34.7 0.0 copy-start.14
  34.7 0.0 copy-done.6
  34.7 0.0 copy-done.7
  34.8 0.0 copy-done.9
  34.8 0.0 copy-done.10
  34.8 0.0 copy-done.11
  34.8 0.6 copy-done.14
  35.4 53.9 %pair_forces.1 = (f32[1024,128]{1,0:T(8,128)S(1)}, f32[128,128]{1,0:T(8,128)S(1)}, f32[128,128]{1,0:T(8,128)S(1)}, f32[128,128]{1,0:T(8,128)S(1)}, f32[128,128]{...) custom-call(s32[1024]{0:T(1024)S(1)} %copy-done.14, ...), custom_call_target="tpu_custom_call" | custom-call | flops 335544320 | bytes 4194304 | tf_op jit(solution)/shard_map/pair_forces/pallas_call | solution.py:262
  89.4 3.1 %collective-permute-start.12 = (f32[128,128]{1,0:T(8,128)S(1)}, f32[128,128]{1,0:T(8,128)S(1)}, u32[]{:S(2)}, u32[]{:S(2)}) collective-permute-start(f32[128,128]{1,0:T(8,128)S(1)} %get-tuple-element.61), channel_id=1, source_target_pairs={{8,0},{16,8},{24,16},{9,1},{17,9},{25,17},{10,2},{18,10},{26,18},{... | collective-permute-start | bytes 196616 | tf_op jit(solution)/shard_map/ppermute | solution.py:753
  92.5 2.1 %collective-permute-start.13 = (f32[128,128]{1,0:T(8,128)S(1)}, f32[128,128]{1,0:T(8,128)S(1)}, u32[]{:S(2)}, u32[]{:S(2)}) collective-permute-start(f32[128,128]{1,0:T(8,128)S(1)} %get-tuple-element.62), channel_id=1, source_target_pairs={{0,8},{8,16},{16,24},{1,9},{9,17},{17,25},{2,10},{10,18},{18,26},{... | collective-permute-start | bytes 196616 | tf_op jit(solution)/shard_map/ppermute | solution.py:753
  94.7 5.7 %collective-permute-start.8 = (f32[128,128]{1,0:T(8,128)S(1)}, f32[128,128]{1,0:T(8,128)S(1)}, u32[]{:S(2)}, u32[]{:S(2)}) collective-permute-start(f32[128,128]{1,0:T(8,128)S(1)} %get-tuple-element.57), channel_id=1, source_target_pairs={{1,0},{2,1},{3,2},{4,3},{5,4},{6,5},{7,6},{9,8},{10,9},{11,10},{12... | collective-permute-start | bytes 196616 | tf_op jit(solution)/shard_map/ppermute | solution.py:753
  100.3 0.0 collective-permute-done.12
  100.3 3.1 %collective-permute-start.9 = (f32[128,128]{1,0:T(8,128)S(1)}, f32[128,128]{1,0:T(8,128)S(1)}, u32[]{:S(2)}, u32[]{:S(2)}) collective-permute-start(f32[128,128]{1,0:T(8,128)S(1)} %get-tuple-element.58), channel_id=1, source_target_pairs={{0,1},{1,2},{2,3},{3,4},{4,5},{5,6},{6,7},{8,9},{9,10},{10,11},{11... | collective-permute-start | bytes 196616 | tf_op jit(solution)/shard_map/ppermute | solution.py:753
  103.5 0.0 collective-permute-done.6.refs_8_
  103.5 2.1 %collective-permute-start.10 = (f32[128,128]{1,0:T(8,128)S(1)}, f32[128,128]{1,0:T(8,128)S(1)}, u32[]{:S(2)}, u32[]{:S(2)}) collective-permute-start(f32[128,128]{1,0:T(8,128)S(1)} %get-tuple-element.59), channel_id=1, source_target_pairs={{2,0},{3,1},{4,2},{5,3},{6,4},{7,5},{10,8},{11,9},{12,10},{13,11},... | collective-permute-start | bytes 196616 | tf_op jit(solution)/shard_map/ppermute | solution.py:753
  105.5 0.0 collective-permute-done.7.refs_9_
  105.5 0.0 copy-start.13
  105.6 3.2 %collective-permute-start.11 = (f32[128,128]{1,0:T(8,128)S(1)}, f32[128,128]{1,0:T(8,128)S(1)}, u32[]{:S(2)}, u32[]{:S(2)}) collective-permute-start(f32[128,128]{1,0:T(8,128)S(1)} %get-tuple-element.60), channel_id=1, source_target_pairs={{0,2},{1,3},{2,4},{3,5},{4,6},{5,7},{8,10},{9,11},{10,12},{11,13},... | collective-permute-start | bytes 196616 | tf_op jit(solution)/shard_map/ppermute | solution.py:753
  108.8 0.0 copy-done.3
  108.8 0.0 copy-done.5
  108.8 0.0 copy-done.8
  108.8 0.0 copy-done.13
  108.8 11.5 %grid_step.1 = (f32[16,32,256]{2,1,0:T(8,128)}, f32[16,32,256]{2,1,0:T(8,128)}, f32[1024,128]{1,0:T(8,128)S(1)}) custom-call(s32[256]{0:T(256)S(1)} %copy-done.13, f32[256,128]{1,0:T(8,128)S(1)} %copy-done.8, f32[16,32,256]{2,1,0:T(8,128)S(1)} %copy-done.1, f32[16,32,256]{2,1,0:T(8,128)S(1)} %copy-done.3, f32[16,32,256]{2,1,0:T(8,128)S(1)} %copy-done.5, ...), custom_call_target="tpu_custom_call" | custom-call | flops 31948800 | bytes 8388608 | tf_op jit(solution)/shard_map/grid_step/pallas_call | solution.py:693
  120.3 0.0 collective-permute-done.13
  120.3 0.0 collective-permute-done.8
  120.3 0.0 collective-permute-done.9
  120.3 0.0 collective-permute-done.10
  120.3 0.0 collective-permute-done.11
  120.4 0.0 copy-start.12
  120.4 0.7 copy-done.12
  121.0 2.8 %gather_forces.1 = f32[3,32768]{1,0:T(4,128)} custom-call(s32[7,32]{1,0:T(8,128)S(1)} %copy-done.12, f32[256,4,128]{2,1,0:T(4,128)S(1)} %bitcast.13, f32[256,4,128]{2,1,0:T(4,128)S(1)} %bitcast.14, f32[32,4,128]{2,1,0:T(4,128)S(1)} %bitcast.15, f32[32,4,128]{2,1,0:T(4,128)S(1)} %bitcast.18, f32[32,4,128]{2,1,0:T(4,128)S(1)} %bitcast.19, ...), custom_call_target="tpu_custom_call" | custom-call | tf_op jit(solution)/shard_map/gather_forces/pallas_call | solution.py:739
  (4 shorter events, 0.0 us)
Async XLA Ops:
  0.6 25.5 %copy-start = (f32[16,32,256]{2,1,0:T(8,128)S(1)}, f32[16,32,256]{2,1,0:T(8,128)}, u32[]{:S(2)}) copy-start(f32[16,32,256]{2,1,0:T(8,128)} %refs_5_.1) | copy-start | bytes 1572868
  0.6 25.4 %copy-start.1 = (f32[16,32,256]{2,1,0:T(8,128)S(1)}, f32[16,32,256]{2,1,0:T(8,128)}, u32[]{:S(2)}) copy-start(f32[16,32,256]{2,1,0:T(8,128)} %refs_2_.2) | copy-start | bytes 1572868
  6.7 19.4 %collective-permute-start = (f32[640,128]{1,0:T(8,128)}, f32[640,128]{1,0:T(8,128)S(1)}, u32[]{:S(2)}, u32[]{:S(2)}) collective-permute-start(f32[640,128]{1,0:T(8,128)} %get-tuple-element.36), channel_id=1, source_target_pairs={{0,1},{1,2},{2,3},{3,4},{4,5},{5,6},{6,7},{8,9},{9,10},{10,11},{11... | collective-permute-start | bytes 983048 | tf_op jit(solution)/shard_map/ppermute | solution.py:753
  10.5 15.6 %collective-permute-start.1 = (f32[640,128]{1,0:T(8,128)}, f32[640,128]{1,0:T(8,128)S(1)}, u32[]{:S(2)}, u32[]{:S(2)}) collective-permute-start(f32[640,128]{1,0:T(8,128)} %get-tuple-element.37), channel_id=1, source_target_pairs={{1,0},{2,1},{3,2},{4,3},{5,4},{6,5},{7,6},{9,8},{10,9},{11,10},{12... | collective-permute-start | bytes 983048 | tf_op jit(solution)/shard_map/ppermute | solution.py:753
  12.4 8.4 %collective-permute-start.2 = (f32[128,128]{1,0:T(8,128)}, f32[128,128]{1,0:T(8,128)S(1)}, u32[]{:S(2)}, u32[]{:S(2)}) collective-permute-start(f32[128,128]{1,0:T(8,128)} %get-tuple-element.38), channel_id=1, source_target_pairs={{0,2},{1,3},{2,4},{3,5},{4,6},{5,7},{8,10},{9,11},{10,12},{11,13},... | collective-permute-start | bytes 196616 | tf_op jit(solution)/shard_map/ppermute | solution.py:753
  15.6 8.3 %collective-permute-start.3 = (f32[128,128]{1,0:T(8,128)}, f32[128,128]{1,0:T(8,128)S(1)}, u32[]{:S(2)}, u32[]{:S(2)}) collective-permute-start(f32[128,128]{1,0:T(8,128)} %get-tuple-element.39), channel_id=1, source_target_pairs={{2,0},{3,1},{4,2},{5,3},{6,4},{7,5},{10,8},{11,9},{12,10},{13,11},... | collective-permute-start | bytes 196616 | tf_op jit(solution)/shard_map/ppermute | solution.py:753
  17.7 6.2 %collective-permute-start.4 = (f32[128,128]{1,0:T(8,128)}, f32[128,128]{1,0:T(8,128)S(1)}, u32[]{:S(2)}, u32[]{:S(2)}) collective-permute-start(f32[128,128]{1,0:T(8,128)} %get-tuple-element.40), channel_id=1, source_target_pairs={{0,8},{8,16},{16,24},{1,9},{9,17},{17,25},{2,10},{10,18},{18,26},{... | collective-permute-start | bytes 196616 | tf_op jit(solution)/shard_map/ppermute | solution.py:753
  20.9 5.2 %collective-permute-start.5 = (f32[128,128]{1,0:T(8,128)}, f32[128,128]{1,0:T(8,128)S(1)}, u32[]{:S(2)}, u32[]{:S(2)}) collective-permute-start(f32[128,128]{1,0:T(8,128)} %get-tuple-element.41), channel_id=1, source_target_pairs={{8,0},{16,8},{24,16},{9,1},{17,9},{25,17},{10,2},{18,10},{26,18},{... | collective-permute-start | bytes 196616 | tf_op jit(solution)/shard_map/ppermute | solution.py:753
  26.1 1.0 copy-start.2
  27.1 1.0 copy-start.4
  28.2 6.5 %copy-start.15 = (s32[1024]{0:T(1024)S(1)}, s32[1024]{0:T(1024)}, u32[]{:S(2)}) copy-start(s32[1024]{0:T(1024)} %param.23) | copy-start | bytes 12292
  28.2 6.5 %copy-start.16 = (s32[1024]{0:T(1024)S(1)}, s32[1024]{0:T(1024)}, u32[]{:S(2)}) copy-start(s32[1024]{0:T(1024)} %param.22) | copy-start | bytes 12292
  28.2 6.5 %copy-start.6 = (f32[256,4,128]{2,1,0:T(4,128)S(1)}, f32[256,4,128]{2,1,0:T(4,128)}, u32[]{:S(2)}) copy-start(f32[256,4,128]{2,1,0:T(4,128)} %get-tuple-element.34) | copy-start | bytes 1572868
  28.2 6.6 %copy-start.7 = (bf16[128,1024]{1,0:T(8,128)(2,1)S(1)}, bf16[128,1024]{1,0:T(8,128)(2,1)}, u32[]{:S(2)}) copy-start(bf16[128,1024]{1,0:T(8,128)(2,1)} %constant.8.clone.refs_0_) | copy-start | bytes 786436
  28.2 6.6 %copy-start.9 = (bf16[256,128]{1,0:T(8,128)(2,1)S(1)}, bf16[256,128]{1,0:T(8,128)(2,1)}, u32[]{:S(2)}) copy-start(bf16[256,128]{1,0:T(8,128)(2,1)} %constant.9.clone.refs_1_) | copy-start | bytes 196612
  28.2 6.6 %copy-start.10 = (f32[128,128]{1,0:T(8,128)S(1)}, f32[128,128]{1,0:T(8,128)}, u32[]{:S(2)}) copy-start(f32[128,128]{1,0:T(8,128)} %get-tuple-element.42.refs_4_) | copy-start | bytes 196612
  28.2 6.6 %copy-start.11 = (bf16[128,128]{1,0:T(8,128)(2,1)S(1)}, bf16[128,128]{1,0:T(8,128)(2,1)}, u32[]{:S(2)}) copy-start(bf16[128,128]{1,0:T(8,128)(2,1)} %constant.10.clone.refs_2_) | copy-start | bytes 98308
  28.4 75.1 %collective-permute-start.6 = (f32[1344,128]{1,0:T(8,128)S(1)}, f32[1344,128]{1,0:T(8,128)S(1)}, u32[]{:S(2)}, u32[]{:S(2)}) collective-permute-start(f32[1344,128]{1,0:T(8,128)S(1)} %get-tuple-element.53), channel_id=1, source_target_pairs={{0,8},{8,16},{16,24},{1,9},{9,17},{17,25},{2,10},{10,18},{18,26},{... | collective-permute-start | bytes 2064392 | tf_op jit(solution)/shard_map/ppermute | solution.py:753
  30.4 75.1 %collective-permute-start.7 = (f32[1344,128]{1,0:T(8,128)S(1)}, f32[1344,128]{1,0:T(8,128)S(1)}, u32[]{:S(2)}, u32[]{:S(2)}) collective-permute-start(f32[1344,128]{1,0:T(8,128)S(1)} %get-tuple-element.54), channel_id=1, source_target_pairs={{8,0},{16,8},{24,16},{9,1},{17,9},{25,17},{10,2},{18,10},{26,18},{... | collective-permute-start | bytes 2064392 | tf_op jit(solution)/shard_map/ppermute | solution.py:753
  34.7 0.7 copy-start.14
  35.4 73.4 %copy-start.3 = (f32[16,32,256]{2,1,0:T(8,128)S(1)}, f32[16,32,256]{2,1,0:T(8,128)}, u32[]{:S(2)}) copy-start(f32[16,32,256]{2,1,0:T(8,128)} %get-tuple-element.51.refs_1_.refs_3_) | copy-start | bytes 1572868
  35.4 73.4 %copy-start.5 = (f32[16,32,256]{2,1,0:T(8,128)S(1)}, f32[16,32,256]{2,1,0:T(8,128)}, u32[]{:S(2)}) copy-start(f32[16,32,256]{2,1,0:T(8,128)} %get-tuple-element.52.refs_2_.refs_4_) | copy-start | bytes 1572868
  35.4 73.4 %copy-start.8 = (f32[256,128]{1,0:T(8,128)S(1)}, f32[256,128]{1,0:T(8,128)}, u32[]{:S(2)}) copy-start(f32[256,128]{1,0:T(8,128)} %get-tuple-element.50.refs_1_) | copy-start | bytes 393220
  89.4 11.0 %collective-permute-start.12 = (f32[128,128]{1,0:T(8,128)S(1)}, f32[128,128]{1,0:T(8,128)S(1)}, u32[]{:S(2)}, u32[]{:S(2)}) collective-permute-start(f32[128,128]{1,0:T(8,128)S(1)} %get-tuple-element.61), channel_id=1, source_target_pairs={{8,0},{16,8},{24,16},{9,1},{17,9},{25,17},{10,2},{18,10},{26,18},{... | collective-permute-start | bytes 196616 | tf_op jit(solution)/shard_map/ppermute | solution.py:753
  92.5 27.8 %collective-permute-start.13 = (f32[128,128]{1,0:T(8,128)S(1)}, f32[128,128]{1,0:T(8,128)S(1)}, u32[]{:S(2)}, u32[]{:S(2)}) collective-permute-start(f32[128,128]{1,0:T(8,128)S(1)} %get-tuple-element.62), channel_id=1, source_target_pairs={{0,8},{8,16},{16,24},{1,9},{9,17},{17,25},{2,10},{10,18},{18,26},{... | collective-permute-start | bytes 196616 | tf_op jit(solution)/shard_map/ppermute | solution.py:753
  94.7 25.7 %collective-permute-start.8 = (f32[128,128]{1,0:T(8,128)S(1)}, f32[128,128]{1,0:T(8,128)S(1)}, u32[]{:S(2)}, u32[]{:S(2)}) collective-permute-start(f32[128,128]{1,0:T(8,128)S(1)} %get-tuple-element.57), channel_id=1, source_target_pairs={{1,0},{2,1},{3,2},{4,3},{5,4},{6,5},{7,6},{9,8},{10,9},{11,10},{12... | collective-permute-start | bytes 196616 | tf_op jit(solution)/shard_map/ppermute | solution.py:753
  100.3 20.0 %collective-permute-start.9 = (f32[128,128]{1,0:T(8,128)S(1)}, f32[128,128]{1,0:T(8,128)S(1)}, u32[]{:S(2)}, u32[]{:S(2)}) collective-permute-start(f32[128,128]{1,0:T(8,128)S(1)} %get-tuple-element.58), channel_id=1, source_target_pairs={{0,1},{1,2},{2,3},{3,4},{4,5},{5,6},{6,7},{8,9},{9,10},{10,11},{11... | collective-permute-start | bytes 196616 | tf_op jit(solution)/shard_map/ppermute | solution.py:753
  103.5 16.9 %collective-permute-start.10 = (f32[128,128]{1,0:T(8,128)S(1)}, f32[128,128]{1,0:T(8,128)S(1)}, u32[]{:S(2)}, u32[]{:S(2)}) collective-permute-start(f32[128,128]{1,0:T(8,128)S(1)} %get-tuple-element.59), channel_id=1, source_target_pairs={{2,0},{3,1},{4,2},{5,3},{6,4},{7,5},{10,8},{11,9},{12,10},{13,11},... | collective-permute-start | bytes 196616 | tf_op jit(solution)/shard_map/ppermute | solution.py:753
  105.5 3.3 %copy-start.13 = (s32[256]{0:T(256)S(1)}, s32[256]{0:T(256)}, u32[]{:S(2)}) copy-start(s32[256]{0:T(256)} %refs_0_.4) | copy-start | bytes 3076
  105.6 14.8 %collective-permute-start.11 = (f32[128,128]{1,0:T(8,128)S(1)}, f32[128,128]{1,0:T(8,128)S(1)}, u32[]{:S(2)}, u32[]{:S(2)}) collective-permute-start(f32[128,128]{1,0:T(8,128)S(1)} %get-tuple-element.60), channel_id=1, source_target_pairs={{0,2},{1,3},{2,4},{3,5},{4,6},{5,7},{8,10},{9,11},{10,12},{11,13},... | collective-permute-start | bytes 196616 | tf_op jit(solution)/shard_map/ppermute | solution.py:753
  120.4 0.7 copy-start.12

commit v13 on v12

--- a/solution.py
+++ b/solution.py
@@ -11,9 +11,13 @@
 SWEEPS = 4
 QUAD = 4
 UNROLL = 8
+CHUNKS = 4
 HALO_WIDTHS = (SWEEPS + 1, SWEEPS, SWEEPS, 1)
 DEPTH = SWEEPS + 1
 CELL_BITS = 8
+SWAPS = tuple(
+    (*way, phase) for way in (("brick", 1), ("brick", 2), ("grp", 1)) for phase in (0, 1)
+)
 
 
 coulomb_scale = 0.02
@@ -25,6 +29,27 @@
 mobility = 0.3
 diffusion = 0.2
 time_step = 0.2
+
+
+def upward():
+    brick, grp = (lax.axis_index("brick"), lax.axis_index("grp"))
+    bits = (brick, lax.shift_right_logical(brick, 1), grp)
+    return [1 - lax.bitwise_and(bit, 1) for bit in bits]
+
+
+def sent_row(position, ups):
+    way, phase = ((position - 1) // 2, (position - 1) % 2)
+    return 1 + 2 * way + (ups[way] if phase else 1 - ups[way])
+
+
+def swapped(shard, axis, distance, phase):
+    devices = lax.axis_size(axis)
+    pairs = []
+    for index in range(devices):
+        step = distance if (index // distance + phase) % 2 == 0 else -distance
+        if 0 <= index + step < devices:
+            pairs.append((index, index + step))
+    return lax.ppermute(shard, axis, pairs)
 
 
 def split3(value):
@@ -139,16 +164,6 @@
     dist_refs[0][...] = jnp.full(dist_refs[0].shape, 1e38, jnp.float32)
     weight_refs[0][...] = jnp.zeros_like(weight_refs[0])
 
-    def block_diagonal(blocks):
-        blank = jnp.zeros_like(blocks[0])
-        lines = [
-            jnp.concatenate(
-                [block if turn == at else blank for turn in range(len(blocks))], axis=1
-            )
-            for at, block in enumerate(blocks)
-        ]
-        return jnp.concatenate(lines, axis=0)
-
     def distances(pair, unit, turn, dist_ref):
         own = own_rows_ref[pair + turn]
         other = other_rows_ref[pair + turn]
@@ -158,61 +173,62 @@
             preferred_element_type=jnp.float32,
         )
 
-    def weights(unit, turn, dist_ref, weight_ref):
-        root = lax.rsqrt(dist_ref[unit, :, 128 * turn : 128 * turn + 128])
+    def weights(unit, turn, chunk, dist_ref, weight_ref):
+        rows = 128 // CHUNKS
+        first = rows * chunk
+        dist = dist_ref[unit, first : first + rows, 128 * turn : 128 * turn + 128]
+        root = lax.rsqrt(dist)
         weight = root * root * root
         high = weight.astype(jnp.bfloat16)
-        weight_ref[unit, 128 * turn : 128 * turn + 128, :128] = high
-        weight_ref[unit, 128 * turn : 128 * turn + 128, 128:] = (
-            weight - high.astype(jnp.float32)
-        ).astype(jnp.bfloat16)
-
-    def moments_of(moment_ref, indices):
-        return block_diagonal(
-            [moment_ref[pl.ds(pl.multiple_of(index * 16, 16), 16), :] for index in indices]
-        )
-
-    def own_products(others, weight_ref, unit):
-        levels = [
-            jnp.concatenate(
-                [weight_ref[unit, 128 * turn : 128 * turn + 128, lanes] for turn in range(QUAD)],
-                axis=1,
-            )
-            for lanes in (slice(0, 128), slice(128, 256))
-        ]
+        low = (weight - high.astype(jnp.float32)).astype(jnp.bfloat16)
+        at = slice(128 * turn + first, 128 * turn + first + rows)
+        weight_ref[unit, at, :128] = high
+        weight_ref[unit, at, 128:] = low
+
+    def row_block(index):
+        return pl.ds(pl.multiple_of(index * 16, 16), 16)
+
+    def own_product(other, weight_ref, unit, turn):
+        both = weight_ref[unit, 128 * turn : 128 * turn + 128]
         return lax.dot_general(
-            moments_of(other_moment_ref, others),
-            jnp.concatenate(levels, axis=0),
+            other_moment_ref[row_block(other), :],
+            jnp.concatenate([both[:, :128], both[:, 128:]], axis=0),
             (((1,), (1,)), ((), ())),
             preferred_element_type=jnp.float32,
         )
 
-    def other_products(owns, weight_ref, unit):
+    def other_product(own, weight_ref, unit, turn):
         return jnp.dot(
-            moments_of(own_moment_ref, owns), weight_ref[unit], preferred_element_type=jnp.float32
+            own_moment_ref[row_block(own), :],
+            weight_ref[unit, 128 * turn : 128 * turn + 128],
+            preferred_element_type=jnp.float32,
         )
 
-    def add_rows(sum_ref, indices, values):
-        values = values[:, :128] + values[:, 128:]
-        for turn, index in enumerate(indices):
-            at = pl.ds(pl.multiple_of(index * 16, 16), 16)
-            sum_ref[at, :] += values[16 * turn : 16 * turn + 16]
+    def add_rows(own, other, to_own, to_other):
+        own_sum_ref[row_block(own), :] += to_own[:, :128] + to_own[:, 128:]
+        other_sum_ref[row_block(other), :] += to_other[:, :128] + to_other[:, 128:]
 
     def half_step(step, side):
         last = jnp.maximum(step - 2, 0) * UNROLL
         first = jnp.minimum(step, groups - 1) * UNROLL
-        for unit in range(units):
-            owns = [own_rows_ref[last + QUAD * unit + turn] for turn in range(QUAD)]
-            others = [other_rows_ref[last + QUAD * unit + turn] for turn in range(QUAD)]
-            for turn in range(QUAD):
-                distances(first + QUAD * unit, unit, turn, dist_refs[1 - side])
-                if turn == 0:
-                    to_own = own_products(others, weight_refs[side], unit)
-                if turn == 2:
-                    to_other = other_products(owns, weight_refs[side], unit)
-                weights(unit, turn, dist_refs[side], weight_refs[1 - side])
-            add_rows(own_sum_ref, owns, to_own)
-            add_rows(other_sum_ref, others, to_other)
+        waiting = []
+        for index in range(UNROLL):
+            unit, turn = (index // QUAD, index % QUAD)
+            own = own_rows_ref[last + index]
+            other = other_rows_ref[last + index]
+            passed = (dist_refs[side], weight_refs[1 - side])
+            distances(first + QUAD * unit, unit, turn, dist_refs[1 - side])
+            weights(unit, turn, 0, *passed)
+            to_own = own_product(other, weight_refs[side], unit, turn)
+            weights(unit, turn, 1, *passed)
+            weights(unit, turn, 2, *passed)
+            to_other = other_product(own, weight_refs[side], unit, turn)
+            weights(unit, turn, 3, *passed)
+            waiting.append((own, other, to_own, to_other))
+            if len(waiting) > 2:
+                add_rows(*waiting.pop(0))
+        for entry in waiting:
+            add_rows(*entry)
 
     def visit(step, _):
         for side in range(2):
@@ -341,8 +357,11 @@
 
     lax.fori_loop(0, clusters // 8, collect, 0, unroll=4)
 
+    ups = upward()
+
     def fill_messages(step, _):
-        for direction, out_ref in enumerate(out_refs):
+        for position, out_ref in enumerate(out_refs):
+            direction = sent_row(position, ups) if position else 0
             parts = []
             for turn in range(2):
                 slot = step * 2 + turn
@@ -386,7 +405,7 @@
             source_ref[index, :, lanes] = (
                 ion_ref[index, :, lanes] + deposit_ref[first : first + cells_y, :]
             ) * inverse_ref[index, :, lanes]
-    for out_ref, after in ((out_refs[1], True), (out_refs[2], False)):
+    def fill_rows(out_ref, after):
         for index in range(cells_x):
             base = slots * 4 + index * 32
             offset = 0
@@ -404,6 +423,13 @@
                 out_ref[base + 16 * half + offset : base + 16 * half + 16, :] = jnp.zeros(
                     (16 - offset, 128), jnp.float32
                 )
+
+    for up in range(2):
+
+        @pl.when(ups[0] == up)
+        def _(up=up):
+            fill_rows(out_refs[1], up == 1)
+            fill_rows(out_refs[2], up == 0)
 
 
 def prepare(fill, cell, send_index, send_count, positions, charges, ions, start, screen):
@@ -454,52 +480,59 @@
     return (cells_y + 2 * DEPTH + 7) // 8 * 8
 
 
-def fill_lines(target_ref, plane, field, field_ref, index, before_ref, after_ref, base):
-    cells_y = field_ref.shape[1]
+def collect_rows(rim_ref, first_ref, second_ref, base):
+    size = rim_ref.shape[0] // 2
+    up = upward()[0]
+    rim_ref[pl.ds(pl.multiple_of(up * size, size), size), :] = first_ref[base : base + size, :]
+    rim_ref[pl.ds(pl.multiple_of((1 - up) * size, size), size), :] = second_ref[
+        base : base + size, :
+    ]
+
+
+def fill_lines(target_ref, plane, field, field_ref, index, rim_ref):
+    cells_x, cells_y, _ = field_ref.shape
     width = HALO_WIDTHS[field]
     for half in range(2):
         at = (plane * 2 + half) * line_rows(cells_y) + DEPTH
-        first = base + index * 32 + 16 * half + sum(HALO_WIDTHS[:field])
-        target_ref[pl.ds(at - width, width), :] = before_ref[pl.ds(first, width), :]
+        first = index * 32 + 16 * half + sum(HALO_WIDTHS[:field])
+        target_ref[pl.ds(at - width, width), :] = rim_ref[pl.ds(first, width), :]
         target_ref[pl.ds(at, cells_y), :] = field_ref[index, :, 128 * half : 128 * half + 128]
-        target_ref[pl.ds(at + cells_y, width), :] = after_ref[pl.ds(first, width), :]
+        first = first + cells_x * 32
+        target_ref[pl.ds(at + cells_y, width), :] = rim_ref[pl.ds(first, width), :]
 
 
 def planes_kernel(base, *refs):
-    field_refs, (before_ref, after_ref, down_ref, up_ref) = (refs[:4], refs[4:])
+    field_refs, (first_ref, second_ref, *out_refs, rim_ref) = (refs[:4], refs[4:])
     cells_x = field_refs[0].shape[0]
+    collect_rows(rim_ref, first_ref, second_ref, base)
+    up = upward()[2]
     for field, width in enumerate(HALO_WIDTHS):
         plane = sum(HALO_WIDTHS[:field])
 
         def fill(step, _, field=field, plane=plane, width=width):
-            for target_ref, source in ((down_ref, step), (up_ref, cells_x - width + step)):
-                fill_lines(
-                    target_ref,
-                    plane + step,
-                    field,
-                    field_refs[field],
-                    source,
-                    before_ref,
-                    after_ref,
-                    base,
-                )
+            for phase, out_ref in enumerate(out_refs):
+                last = up if phase == 0 else 1 - up
+                source = last * (cells_x - width) + step
+                fill_lines(out_ref, plane + step, field, field_refs[field], source, rim_ref)
             return 0
 
         lax.fori_loop(0, width, fill, 0)
 
 
-def planes(fields, before, after, base):
+def planes(fields, first, second, base):
     vmem = pl.BlockSpec(memory_space=pltpu.VMEM)
-    rows = sum(HALO_WIDTHS) * 2 * line_rows(fields[0].shape[1])
+    cells_x, cells_y, _ = fields[0].shape
+    rows = sum(HALO_WIDTHS) * 2 * line_rows(cells_y)
     shape = jax.ShapeDtypeStruct((rows, 128), jnp.float32)
     return pl.pallas_call(
         functools.partial(planes_kernel, base),
         out_shape=(shape, shape),
         in_specs=[vmem] * 6,
         out_specs=(vmem, vmem),
+        scratch_shapes=[pltpu.VMEM((cells_x * 64, 128), jnp.float32)],
         compiler_params=pltpu.CompilerParams(vmem_limit_bytes=32 * 1024 * 1024),
         name="planes",
-    )(*fields, before, after)
+    )(*fields, first, second)
 
 
 def face_flux(pot_low, pot_high, ion_low, ion_high):
@@ -514,36 +547,31 @@
 def grid_kernel(base, *refs):
     cell_ref, masked_ref = refs[:2]
     field_refs = refs[2:6]
-    before_ref, after_ref, lower_ref, upper_ref = refs[6:10]
+    first_ref, second_ref, *plane_refs = refs[6:10]
     potential_ref, next_ref, force_ref = refs[10:13]
     start_ref, inverse_ref, source_ref, ion_ref = refs[13:17]
     updates, resids, final_ref, pick_refs = (refs[17:20], refs[20:22], refs[22], refs[23:26])
+    rim_ref = refs[26]
     cells_x, cells_y, _ = field_refs[0].shape
     rows = line_rows(cells_y)
     inner = cells_y + 2 * DEPTH - 2
     clusters = masked_ref.shape[0]
+    up = upward()[2]
+    collect_rows(rim_ref, first_ref, second_ref, base)
 
     for field, target_ref in enumerate((start_ref, inverse_ref, source_ref, ion_ref)):
         width = HALO_WIDTHS[field]
         size = width * 2 * rows
         first = sum(HALO_WIDTHS[:field]) * 2 * rows
-        low = (DEPTH - width) * 2 * rows
-        high = (DEPTH + cells_x) * 2 * rows
-        target_ref[low : low + size, :] = lower_ref[first : first + size, :]
-        target_ref[high : high + size, :] = upper_ref[first : first + size, :]
+        for phase, plane_ref in enumerate(plane_refs):
+            higher = up if phase == 0 else 1 - up
+            plane = (DEPTH - width) + higher * (cells_x + width)
+            at = pl.ds(pl.multiple_of(plane * 2 * rows, 2 * rows), size)
+            target_ref[at, :] = plane_ref[first : first + size, :]
 
     def fill(index, _):
         for field, target_ref in enumerate((start_ref, inverse_ref, source_ref, ion_ref)):
-            fill_lines(
-                target_ref,
-                DEPTH + index,
-                field,
-                field_refs[field],
-                index,
-                before_ref,
-                after_ref,
-                base,
-            )
+            fill_lines(target_ref, DEPTH + index, field, field_refs[field], index, rim_ref)
         return 0
 
     lax.fori_loop(0, cells_x, fill, 0, unroll=2)
@@ -684,7 +712,7 @@
     lax.fori_loop(0, clusters // 8, spread_out, 0, unroll=4)
 
 
-def grid_step(cell, masked, fields, before, after, lower, upper, base):
+def grid_step(cell, masked, fields, rims, edges, base):
     smem = pl.BlockSpec(memory_space=pltpu.SMEM)
     vmem = pl.BlockSpec(memory_space=pltpu.VMEM)
     clusters = masked.shape[0]
@@ -700,13 +728,14 @@
         in_specs=[smem] + [vmem] * 9,
         out_specs=(vmem,) * 3,
         scratch_shapes=[pltpu.VMEM(block, jnp.float32)] * 10
-        + [pltpu.VMEM((clusters, 128), jnp.float32)] * 3,
+        + [pltpu.VMEM((clusters, 128), jnp.float32)] * 3
+        + [pltpu.VMEM((cells_x * 64, 128), jnp.float32)],
         compiler_params=pltpu.CompilerParams(vmem_limit_bytes=40 * 1024 * 1024),
         cost_estimate=pl.CostEstimate(
             flops=block[0] * block[1] * 100, bytes_accessed=8 << 20, transcendentals=0
         ),
         name="grid_step",
-    )(cell, masked, *fields, before, after, lower, upper)
+    )(cell, masked, *fields, *rims, *edges)
 
 
 def gather_forces_kernel(send_index_ref, own_ref, field_ref, *refs):
@@ -714,10 +743,11 @@
     clusters = own_ref.shape[0]
     slots = send_index_ref.shape[1]
     sum_ref[...] = own_ref[...] + field_ref[...]
+    ups = upward()
 
     def visit(slot, _):
-        for direction, back_ref in enumerate(back_refs):
-            cluster = send_index_ref[direction, slot]
+        for position, back_ref in enumerate(back_refs):
+            cluster = send_index_ref[sent_row(position, ups) if position else 0, slot]
             sum_ref[cluster] += back_ref[slot]
         return 0
 
@@ -745,15 +775,6 @@
         compiler_params=pltpu.CompilerParams(vmem_limit_bytes=32 * 1024 * 1024),
         name="gather_forces",
     )(send_index, own, field, *backs)
-
-
-def passed_along(shard, axis, by):
-    devices = lax.axis_size(axis)
-    pairs = [(i, i + by) for i in range(devices) if 0 <= i + by < devices]
-    return lax.ppermute(shard, axis, pairs)
-
-
-ROUTES = (("brick", 1), ("brick", -1), ("brick", 2), ("brick", -2), ("grp", 1), ("grp", -1))
 
 
 def shards(
@@ -786,29 +807,29 @@
         screening,
     )
     arrived = [local] + [
-        passed_along(message, axis, by)
-        for message, (axis, by) in zip(messages, ROUTES, strict=True)
+        swapped(message, *swap) for message, swap in zip(messages, SWAPS, strict=True)
     ]
     fields = (potential_prev, inverse, source, ion_density)
     arrived = lax.optimization_barrier(arrived)
-    before, after = arrived[1:3]
-    down, up = planes(fields, before, after, base)
-    lower = passed_along(up, "grp", 1)
-    upper = passed_along(down, "grp", -1)
+    rims = arrived[1:3]
+    edges = [
+        swapped(edge, "grp", 1, phase) for phase, edge in enumerate(planes(fields, *rims, base))
+    ]
+    way = lax.shift_right_arithmetic(pair_dir - 1, 1)
+    ups = upward()
+    flip = jnp.where(way == 0, ups[0], jnp.where(way == 1, ups[1], ups[2]))
+    position = 1 + 2 * way + lax.bitwise_xor(lax.bitwise_and(pair_dir - 1, 1), flip)
     own_force, *reactions = pair_forces(
         pair_local,
-        pair_dir * slots + pair_slot,
+        jnp.where(pair_dir == 0, 0, position) * slots + pair_slot,
         own.reshape(clusters * 4, psize),
         arrived,
         slots,
     )
     backs = [reactions[0]] + [
-        passed_along(reaction, axis, -by)
-        for reaction, (axis, by) in zip(reactions[1:], ROUTES, strict=True)
+        swapped(reaction, *swap) for reaction, swap in zip(reactions[1:], SWAPS, strict=True)
     ]
-    potential, ion_next, field_force = grid_step(
-        cluster_cell, masked, fields, before, after, lower, upper, base
-    )
+    potential, ion_next, field_force = grid_step(cluster_cell, masked, fields, rims, edges, base)
     forces = gather_forces(
         send_index,
         own_force.reshape(clusters, 4, psize),

time: 125 us -> 116 us (0.928)
  starting transfers between devices: 42.8 us -> 25.5 us
  local copies, waits for them, and re-layouts: 3.44 us -> 8.47 us
  waiting for transfers between devices: 2.16 us -> 5.95 us
    ppermute x14, starting transfers between devices: 42.8 us -> 25.5 us  [swapped(): return lax.ppermute(shard, axis, pairs)]
    unnamed x34 -> x46, local copies, waits for them, and re-layouts: 3.44 us -> 8.47 us
    ppermute x14, waiting for transfers between devices: 2.16 us -> 5.95 us  [swapped(): return lax.ppermute(shard, axis, pairs)]
    pallas_call x1, Pallas kernels: 53.9 us -> 51.4 us  [pair_forces(): pl.pallas_call(pair_kernel, out_shape=(jax.ShapeDtypeStruct(own.shape, jn...]
  transfers between devices with their start and end apart: 14 -> 14, of which waited for: 1 -> 2; matrix products, arithmetic and copies ran while one was open for 0% -> 0% of each run, Pallas kernels for 53% -> 55%
where the time goes in v13:
time: 116 us; the launch traced here: 114 us
  Pallas kernels  73.5 us (63%)
  starting transfers between devices  25.5 us (22%)
  local copies, waits for them, and re-layouts  8.47 us (7%)
  waiting for transfers between devices  5.95 us (5%)
    pallas_call x1, Pallas kernels, pair_forces(): pl.pallas_call(pair_kernel, out_shape=(jax.ShapeDtypeStruct(own.shape, jn...  51.4 us
    ppermute x14, starting transfers between devices, swapped(): return lax.ppermute(shard, axis, pairs)  25.5 us
    pallas_call x1, Pallas kernels, grid_step(): pl.pallas_call(functools.partial(grid_kernel, base), out_shape=(jax.Shape...  11.5 us
    unnamed x46, local copies, waits for them, and re-layouts  8.47 us
    pallas_call x1, Pallas kernels, prepare(): pl.pallas_call(prepare_kernel, out_shape=(jax.ShapeDtypeStruct((clusters,...  6.37 us
    ppermute x14, waiting for transfers between devices, swapped(): return lax.ppermute(shard, axis, pairs)  5.95 us
    pallas_call x1, Pallas kernels, gather_forces(): pl.pallas_call(gather_forces_kernel, out_shape=jax.ShapeDtypeStruct((3, c...  2.86 us
  transfers between devices with their start and end apart: 14, of which 2 were waited for; matrix products, arithmetic and copies ran while one was open for 0% of the time, Pallas kernels for 55%

profile of v13, /device:TPU:13, one launch (start us, length us, event | category | flops | bytes accessed | tf_op | source)
XLA Modules:
  0.0 114.4 jit_solution(13077848399855423462)
XLA Ops:
  0.6 0.0 copy-start
  0.6 0.0 copy-start.1
  0.7 6.4 %prepare.1 = (f32[256,4,128]{2,1,0:T(4,128)}, f32[256,128]{1,0:T(8,128)}, f32[16,32,256]{2,1,0:T(8,128)}, f32[16,32,256]{2,1,0:T(8,128)}, f32[128,128]{1,0:T(8,1...) custom-call(s32[256]{0:T(256)} %fill_ref.1, ...), custom_call_target="tpu_custom_call" | custom-call | tf_op jit(solution)/shard_map/prepare/pallas_call | solution.py:443
  7.0 0.7 collective-permute-start
  7.8 3.1 %collective-permute-start.1 = (f32[640,128]{1,0:T(8,128)}, f32[640,128]{1,0:T(8,128)S(1)}, u32[]{:S(2)}, u32[]{:S(2)}) collective-permute-start(f32[640,128]{1,0:T(8,128)} %get-tuple-element.37), channel_id=1, source_target_pairs={{1,2},{2,1},{3,4},{4,3},{5,6},{6,5},{9,10},{10,9},{11,12},{12,11},... | collective-permute-start | bytes 983048 | tf_op jit(solution)/shard_map/ppermute | solution.py:52
  10.9 0.2 collective-permute-start.2
  11.1 3.0 %collective-permute-start.3 = (f32[128,128]{1,0:T(8,128)}, f32[128,128]{1,0:T(8,128)S(1)}, u32[]{:S(2)}, u32[]{:S(2)}) collective-permute-start(f32[128,128]{1,0:T(8,128)} %get-tuple-element.39), channel_id=1, source_target_pairs={{2,4},{3,5},{4,2},{5,3},{10,12},{11,13},{12,10},{13,11},{18,20},{1... | collective-permute-start | bytes 196616 | tf_op jit(solution)/shard_map/ppermute | solution.py:52
  14.2 1.3 %collective-permute-start.4 = (f32[128,128]{1,0:T(8,128)}, f32[128,128]{1,0:T(8,128)S(1)}, u32[]{:S(2)}, u32[]{:S(2)}) collective-permute-start(f32[128,128]{1,0:T(8,128)} %get-tuple-element.40), channel_id=1, source_target_pairs={{0,8},{8,0},{16,24},{24,16},{1,9},{9,1},{17,25},{25,17},{2,10},{10... | collective-permute-start | bytes 196616 | tf_op jit(solution)/shard_map/ppermute | solution.py:52
  15.5 1.9 %collective-permute-done.2.refs_7_ = f32[128,128]{1,0:T(8,128)S(1)} collective-permute-done((f32[128,128]{1,0:T(8,128)}, f32[128,128]{1,0:T(8,128)S(1)}, u32[]{:S(2)}, u32[]{:S(2)}) %collective-permute-start.2) | collective-permute-done | bytes 65568 | tf_op jit(solution)/shard_map/ppermute | solution.py:52
  17.4 3.0 %collective-permute-start.5 = (f32[128,128]{1,0:T(8,128)}, f32[128,128]{1,0:T(8,128)S(1)}, u32[]{:S(2)}, u32[]{:S(2)}) collective-permute-start(f32[128,128]{1,0:T(8,128)} %get-tuple-element.41), channel_id=1, source_target_pairs={{8,16},{16,8},{9,17},{17,9},{10,18},{18,10},{11,19},{19,11},{12,20... | collective-permute-start | bytes 196616 | tf_op jit(solution)/shard_map/ppermute | solution.py:52
  20.5 0.0 collective-permute-done.3.refs_8_
  20.5 0.0 copy-start.11
  20.5 0.0 collective-permute-done.4.refs_9_
  20.5 0.0 copy-start.13
  20.5 4.0 %collective-permute-done.5.refs_10_ = f32[128,128]{1,0:T(8,128)S(1)} collective-permute-done((f32[128,128]{1,0:T(8,128)}, f32[128,128]{1,0:T(8,128)S(1)}, u32[]{:S(2)}, u32[]{:S(2)}) %collective-permute-start.5) | collective-permute-done | bytes 65568 | tf_op jit(solution)/shard_map/ppermute | solution.py:52
  24.5 0.0 collective-permute-done.refs_5_.refs_4_.refs_6_
  24.5 0.0 collective-permute-done.1.refs_6_.refs_5_.refs_7_
  24.5 0.0 copy-done
  24.5 0.0 copy-done.1
  24.5 0.0 copy-start.2
  24.5 1.0 copy-done.2
  25.6 1.0 copy-done.4
  26.6 1.3 %planes.1 = (f32[1344,128]{1,0:T(8,128)}, f32[1344,128]{1,0:T(8,128)}) custom-call(f32[16,32,256]{2,1,0:T(8,128)S(1)} %copy-done.1, f32[16,32,256]{2,1,0:T(8,128)S(1)} %copy-done.2, f32[16,32,256]{2,1,0:T(8,128)S(1)} %copy-done.4, f32[16,32,256]{2,1,0:T(8,128)S(1)} %copy-done, f32[640,128]{1,0:T(8,128)S(1)} %collective-permute-done.refs_5_.refs_4_.refs_6_, ...), custom_call_target="tpu_custom_call" | custom-call | tf_op jit(solution)/shard_map/planes/pallas_call | solution.py:527
  27.9 0.0 copy-done.11
  27.9 0.0 copy-done.13
  27.9 0.0 copy-done.15
  27.9 0.1 collective-permute-start.6
  28.0 2.4 %collective-permute-start.7 = (f32[1344,128]{1,0:T(8,128)}, f32[1344,128]{1,0:T(8,128)S(1)}, u32[]{:S(2)}, u32[]{:S(2)}) collective-permute-start(f32[1344,128]{1,0:T(8,128)} %get-tuple-element.54), channel_id=1, source_target_pairs={{8,16},{16,8},{9,17},{17,9},{10,18},{18,10},{11,19},{19,11},{12,20... | collective-permute-start | bytes 2064392 | tf_op jit(solution)/shard_map/ppermute | solution.py:52
  30.4 0.0 copy-start.22
  30.4 0.0 copy-start.21
  30.4 0.7 copy-done.22
  31.1 0.0 copy-done.21
  31.1 0.0 copy-done.7
  31.1 0.0 copy-done.9
  31.1 0.0 copy-done.10
  31.2 0.6 copy-done.20
  31.8 1.0 copy-done.6
  32.8 0.8 copy-done.12
  33.7 0.8 copy-done.14
  34.5 0.8 copy-done.16
  35.4 0.8 copy-done.17
  36.1 51.4 %pair_forces.1 = (f32[1024,128]{1,0:T(8,128)S(1)}, f32[128,128]{1,0:T(8,128)S(1)}, f32[128,128]{1,0:T(8,128)S(1)}, f32[128,128]{1,0:T(8,128)S(1)}, f32[128,128]{...) custom-call(s32[1024]{0:T(1024)S(1)} %copy-done.20, ...), custom_call_target="tpu_custom_call" | custom-call | flops 335544320 | bytes 4194304 | tf_op jit(solution)/shard_map/pair_forces/pallas_call | solution.py:278
  87.6 0.1 collective-permute-start.12
  87.6 3.8 %collective-permute-start.13 = (f32[128,128]{1,0:T(8,128)S(1)}, f32[128,128]{1,0:T(8,128)S(1)}, u32[]{:S(2)}, u32[]{:S(2)}) collective-permute-start(f32[128,128]{1,0:T(8,128)S(1)} %get-tuple-element.62), channel_id=1, source_target_pairs={{8,16},{16,8},{9,17},{17,9},{10,18},{18,10},{11,19},{19,11},{12,20... | collective-permute-start | bytes 196616 | tf_op jit(solution)/shard_map/ppermute | solution.py:52
  91.4 1.0 collective-permute-start.8
  92.5 0.0 collective-permute-done.12
  92.5 4.7 %collective-permute-start.9 = (f32[128,128]{1,0:T(8,128)S(1)}, f32[128,128]{1,0:T(8,128)S(1)}, u32[]{:S(2)}, u32[]{:S(2)}) collective-permute-start(f32[128,128]{1,0:T(8,128)S(1)} %get-tuple-element.58), channel_id=1, source_target_pairs={{1,2},{2,1},{3,4},{4,3},{5,6},{6,5},{9,10},{10,9},{11,12},{12,11},... | collective-permute-start | bytes 196616 | tf_op jit(solution)/shard_map/ppermute | solution.py:52
  97.2 0.0 collective-permute-done.6.refs_8_
  97.2 0.1 collective-permute-start.10
  97.3 0.0 collective-permute-done.7.refs_9_
  97.3 0.0 copy-start.19
  97.3 1.9 %collective-permute-start.11 = (f32[128,128]{1,0:T(8,128)S(1)}, f32[128,128]{1,0:T(8,128)S(1)}, u32[]{:S(2)}, u32[]{:S(2)}) collective-permute-start(f32[128,128]{1,0:T(8,128)S(1)} %get-tuple-element.60), channel_id=1, source_target_pairs={{2,4},{3,5},{4,2},{5,3},{10,12},{11,13},{12,10},{13,11},{18,20},{1... | collective-permute-start | bytes 196616 | tf_op jit(solution)/shard_map/ppermute | solution.py:52
  99.2 0.0 copy-done.3
  99.2 0.0 copy-done.5
  99.2 0.0 copy-done.8
  99.3 11.5 %grid_step.1 = (f32[16,32,256]{2,1,0:T(8,128)}, f32[16,32,256]{2,1,0:T(8,128)}, f32[1024,128]{1,0:T(8,128)S(1)}) custom-call(s32[256]{0:T(256)S(1)} %copy-done.19, f32[256,128]{1,0:T(8,128)S(1)} %copy-done.8, f32[16,32,256]{2,1,0:T(8,128)S(1)} %copy-done.1, f32[16,32,256]{2,1,0:T(8,128)S(1)} %copy-done.3, f32[16,32,256]{2,1,0:T(8,128)S(1)} %copy-done.5, ...), custom_call_target="tpu_custom_call" | custom-call | flops 31948800 | bytes 8388608 | tf_op jit(solution)/shard_map/grid_step/pallas_call | solution.py:721
  110.8 0.0 collective-permute-done.13
  110.8 0.0 collective-permute-done.8
  110.8 0.0 collective-permute-done.9
  110.8 0.0 collective-permute-done.10
  110.8 0.0 collective-permute-done.11
  110.8 0.0 copy-start.18
  110.8 0.7 copy-done.18
  111.5 2.9 %gather_forces.1 = f32[3,32768]{1,0:T(4,128)} custom-call(s32[7,32]{1,0:T(8,128)S(1)} %copy-done.18, f32[256,4,128]{2,1,0:T(4,128)S(1)} %bitcast.13, f32[256,4,128]{2,1,0:T(4,128)S(1)} %bitcast.14, f32[32,4,128]{2,1,0:T(4,128)S(1)} %bitcast.15, f32[32,4,128]{2,1,0:T(4,128)S(1)} %bitcast.18, f32[32,4,128]{2,1,0:T(4,128)S(1)} %bitcast.19, ...), custom_call_target="tpu_custom_call" | custom-call | tf_op jit(solution)/shard_map/gather_forces/pallas_call | solution.py:769
  (16 shorter events, 0.0 us)
Async XLA Ops:
  0.6 23.9 %copy-start = (f32[16,32,256]{2,1,0:T(8,128)S(1)}, f32[16,32,256]{2,1,0:T(8,128)}, u32[]{:S(2)}) copy-start(f32[16,32,256]{2,1,0:T(8,128)} %refs_5_.1) | copy-start | bytes 1572868
  0.6 23.9 %copy-start.1 = (f32[16,32,256]{2,1,0:T(8,128)S(1)}, f32[16,32,256]{2,1,0:T(8,128)}, u32[]{:S(2)}) copy-start(f32[16,32,256]{2,1,0:T(8,128)} %refs_2_.2) | copy-start | bytes 1572868
  7.0 17.4 %collective-permute-start = (f32[640,128]{1,0:T(8,128)}, f32[640,128]{1,0:T(8,128)S(1)}, u32[]{:S(2)}, u32[]{:S(2)}) collective-permute-start(f32[640,128]{1,0:T(8,128)} %get-tuple-element.36), channel_id=1, source_target_pairs={{0,1},{1,0},{2,3},{3,2},{4,5},{5,4},{6,7},{7,6},{8,9},{9,8},{10,11... | collective-permute-start | bytes 983048 | tf_op jit(solution)/shard_map/ppermute | solution.py:52
  7.8 16.7 %collective-permute-start.1 = (f32[640,128]{1,0:T(8,128)}, f32[640,128]{1,0:T(8,128)S(1)}, u32[]{:S(2)}, u32[]{:S(2)}) collective-permute-start(f32[640,128]{1,0:T(8,128)} %get-tuple-element.37), channel_id=1, source_target_pairs={{1,2},{2,1},{3,4},{4,3},{5,6},{6,5},{9,10},{10,9},{11,12},{12,11},... | collective-permute-start | bytes 983048 | tf_op jit(solution)/shard_map/ppermute | solution.py:52
  10.9 6.5 %collective-permute-start.2 = (f32[128,128]{1,0:T(8,128)}, f32[128,128]{1,0:T(8,128)S(1)}, u32[]{:S(2)}, u32[]{:S(2)}) collective-permute-start(f32[128,128]{1,0:T(8,128)} %get-tuple-element.38), channel_id=1, source_target_pairs={{0,2},{1,3},{2,0},{3,1},{4,6},{5,7},{6,4},{7,5},{8,10},{9,11},{10,... | collective-permute-start | bytes 196616 | tf_op jit(solution)/shard_map/ppermute | solution.py:52
  11.1 9.3 %collective-permute-start.3 = (f32[128,128]{1,0:T(8,128)}, f32[128,128]{1,0:T(8,128)S(1)}, u32[]{:S(2)}, u32[]{:S(2)}) collective-permute-start(f32[128,128]{1,0:T(8,128)} %get-tuple-element.39), channel_id=1, source_target_pairs={{2,4},{3,5},{4,2},{5,3},{10,12},{11,13},{12,10},{13,11},{18,20},{1... | collective-permute-start | bytes 196616 | tf_op jit(solution)/shard_map/ppermute | solution.py:52
  14.2 6.3 %collective-permute-start.4 = (f32[128,128]{1,0:T(8,128)}, f32[128,128]{1,0:T(8,128)S(1)}, u32[]{:S(2)}, u32[]{:S(2)}) collective-permute-start(f32[128,128]{1,0:T(8,128)} %get-tuple-element.40), channel_id=1, source_target_pairs={{0,8},{8,0},{16,24},{24,16},{1,9},{9,1},{17,25},{25,17},{2,10},{10... | collective-permute-start | bytes 196616 | tf_op jit(solution)/shard_map/ppermute | solution.py:52
  17.4 7.1 %collective-permute-start.5 = (f32[128,128]{1,0:T(8,128)}, f32[128,128]{1,0:T(8,128)S(1)}, u32[]{:S(2)}, u32[]{:S(2)}) collective-permute-start(f32[128,128]{1,0:T(8,128)} %get-tuple-element.41), channel_id=1, source_target_pairs={{8,16},{16,8},{9,17},{17,9},{10,18},{18,10},{11,19},{19,11},{12,20... | collective-permute-start | bytes 196616 | tf_op jit(solution)/shard_map/ppermute | solution.py:52
  20.5 7.4 %copy-start.11 = (f32[128,128]{1,0:T(8,128)}, f32[128,128]{1,0:T(8,128)S(1)}, u32[]{:S(2)}) copy-start(f32[128,128]{1,0:T(8,128)S(1)} %collective-permute-done.3.refs_8_) | copy-start | bytes 196612
  20.5 7.4 %copy-start.13 = (f32[128,128]{1,0:T(8,128)}, f32[128,128]{1,0:T(8,128)S(1)}, u32[]{:S(2)}) copy-start(f32[128,128]{1,0:T(8,128)S(1)} %collective-permute-done.4.refs_9_) | copy-start | bytes 196612
  24.5 3.4 %copy-start.15 = (f32[128,128]{1,0:T(8,128)}, f32[128,128]{1,0:T(8,128)S(1)}, u32[]{:S(2)}) copy-start(f32[128,128]{1,0:T(8,128)S(1)} %collective-permute-done.5.refs_10_) | copy-start | bytes 196612
  24.5 1.1 copy-start.2
  25.6 1.0 copy-start.4
  26.6 4.5 %copy-start.7 = (bf16[128,1024]{1,0:T(8,128)(2,1)S(1)}, bf16[128,1024]{1,0:T(8,128)(2,1)}, u32[]{:S(2)}) copy-start(bf16[128,1024]{1,0:T(8,128)(2,1)} %constant.26.clone.refs_0_) | copy-start | bytes 786436
  26.6 4.5 %copy-start.9 = (bf16[256,128]{1,0:T(8,128)(2,1)S(1)}, bf16[256,128]{1,0:T(8,128)(2,1)}, u32[]{:S(2)}) copy-start(bf16[256,128]{1,0:T(8,128)(2,1)} %constant.27.clone.refs_1_) | copy-start | bytes 196612
  26.6 4.5 %copy-start.10 = (f32[128,128]{1,0:T(8,128)S(1)}, f32[128,128]{1,0:T(8,128)}, u32[]{:S(2)}) copy-start(f32[128,128]{1,0:T(8,128)} %get-tuple-element.42.refs_4_) | copy-start | bytes 196612
  27.9 69.3 %collective-permute-start.6 = (f32[1344,128]{1,0:T(8,128)}, f32[1344,128]{1,0:T(8,128)S(1)}, u32[]{:S(2)}, u32[]{:S(2)}) collective-permute-start(f32[1344,128]{1,0:T(8,128)} %get-tuple-element.53), channel_id=1, source_target_pairs={{0,8},{8,0},{16,24},{24,16},{1,9},{9,1},{17,25},{25,17},{2,10},{10... | collective-permute-start | bytes 2064392 | tf_op jit(solution)/shard_map/ppermute | solution.py:52
  28.0 69.3 %collective-permute-start.7 = (f32[1344,128]{1,0:T(8,128)}, f32[1344,128]{1,0:T(8,128)S(1)}, u32[]{:S(2)}, u32[]{:S(2)}) collective-permute-start(f32[1344,128]{1,0:T(8,128)} %get-tuple-element.54), channel_id=1, source_target_pairs={{8,16},{16,8},{9,17},{17,9},{10,18},{18,10},{11,19},{19,11},{12,20... | collective-permute-start | bytes 2064392 | tf_op jit(solution)/shard_map/ppermute | solution.py:52
  30.4 0.7 copy-start.22
  30.4 0.7 copy-start.21
  31.1 0.7 copy-start.20
  31.8 1.0 copy-start.6
  32.8 0.8 copy-start.12
  33.7 0.8 copy-start.14
  34.5 0.8 copy-start.16
  35.4 0.8 copy-start.17
  36.1 63.1 %copy-start.3 = (f32[16,32,256]{2,1,0:T(8,128)S(1)}, f32[16,32,256]{2,1,0:T(8,128)}, u32[]{:S(2)}) copy-start(f32[16,32,256]{2,1,0:T(8,128)} %get-tuple-element.51.refs_1_.refs_3_) | copy-start | bytes 1572868
  36.1 63.1 %copy-start.5 = (f32[16,32,256]{2,1,0:T(8,128)S(1)}, f32[16,32,256]{2,1,0:T(8,128)}, u32[]{:S(2)}) copy-start(f32[16,32,256]{2,1,0:T(8,128)} %get-tuple-element.52.refs_2_.refs_4_) | copy-start | bytes 1572868
  36.1 63.1 %copy-start.8 = (f32[256,128]{1,0:T(8,128)S(1)}, f32[256,128]{1,0:T(8,128)}, u32[]{:S(2)}) copy-start(f32[256,128]{1,0:T(8,128)} %get-tuple-element.50.refs_1_) | copy-start | bytes 393220
  87.6 4.9 %collective-permute-start.12 = (f32[128,128]{1,0:T(8,128)S(1)}, f32[128,128]{1,0:T(8,128)S(1)}, u32[]{:S(2)}, u32[]{:S(2)}) collective-permute-start(f32[128,128]{1,0:T(8,128)S(1)} %get-tuple-element.61), channel_id=1, source_target_pairs={{0,8},{8,0},{16,24},{24,16},{1,9},{9,1},{17,25},{25,17},{2,10},{10... | collective-permute-start | bytes 196616 | tf_op jit(solution)/shard_map/ppermute | solution.py:52
  87.6 23.1 %collective-permute-start.13 = (f32[128,128]{1,0:T(8,128)S(1)}, f32[128,128]{1,0:T(8,128)S(1)}, u32[]{:S(2)}, u32[]{:S(2)}) collective-permute-start(f32[128,128]{1,0:T(8,128)S(1)} %get-tuple-element.62), channel_id=1, source_target_pairs={{8,16},{16,8},{9,17},{17,9},{10,18},{18,10},{11,19},{19,11},{12,20... | collective-permute-start | bytes 196616 | tf_op jit(solution)/shard_map/ppermute | solution.py:52
  91.4 19.4 %collective-permute-start.8 = (f32[128,128]{1,0:T(8,128)S(1)}, f32[128,128]{1,0:T(8,128)S(1)}, u32[]{:S(2)}, u32[]{:S(2)}) collective-permute-start(f32[128,128]{1,0:T(8,128)S(1)} %get-tuple-element.57), channel_id=1, source_target_pairs={{0,1},{1,0},{2,3},{3,2},{4,5},{5,4},{6,7},{7,6},{8,9},{9,8},{10,11... | collective-permute-start | bytes 196616 | tf_op jit(solution)/shard_map/ppermute | solution.py:52
  92.5 18.3 %collective-permute-start.9 = (f32[128,128]{1,0:T(8,128)S(1)}, f32[128,128]{1,0:T(8,128)S(1)}, u32[]{:S(2)}, u32[]{:S(2)}) collective-permute-start(f32[128,128]{1,0:T(8,128)S(1)} %get-tuple-element.58), channel_id=1, source_target_pairs={{1,2},{2,1},{3,4},{4,3},{5,6},{6,5},{9,10},{10,9},{11,12},{12,11},... | collective-permute-start | bytes 196616 | tf_op jit(solution)/shard_map/ppermute | solution.py:52
  97.2 13.6 %collective-permute-start.10 = (f32[128,128]{1,0:T(8,128)S(1)}, f32[128,128]{1,0:T(8,128)S(1)}, u32[]{:S(2)}, u32[]{:S(2)}) collective-permute-start(f32[128,128]{1,0:T(8,128)S(1)} %get-tuple-element.59), channel_id=1, source_target_pairs={{0,2},{1,3},{2,0},{3,1},{4,6},{5,7},{6,4},{7,5},{8,10},{9,11},{10,... | collective-permute-start | bytes 196616 | tf_op jit(solution)/shard_map/ppermute | solution.py:52
  97.3 2.0 %copy-start.19 = (s32[256]{0:T(256)S(1)}, s32[256]{0:T(256)}, u32[]{:S(2)}) copy-start(s32[256]{0:T(256)} %refs_0_.4) | copy-start | bytes 3076
  97.3 13.5 %collective-permute-start.11 = (f32[128,128]{1,0:T(8,128)S(1)}, f32[128,128]{1,0:T(8,128)S(1)}, u32[]{:S(2)}, u32[]{:S(2)}) collective-permute-start(f32[128,128]{1,0:T(8,128)S(1)} %get-tuple-element.60), channel_id=1, source_target_pairs={{2,4},{3,5},{4,2},{5,3},{10,12},{11,13},{12,10},{13,11},{18,20},{1... | collective-permute-start | bytes 196616 | tf_op jit(solution)/shard_map/ppermute | solution.py:52
  110.8 0.7 copy-start.18

commit v14 on v13

--- a/solution.py
+++ b/solution.py
@@ -9,7 +9,6 @@
 from jax.sharding import PartitionSpec as P
 
 SWEEPS = 4
-QUAD = 4
 UNROLL = 8
 CHUNKS = 4
 HALO_WIDTHS = (SWEEPS + 1, SWEEPS, SWEEPS, 1)
@@ -29,6 +28,19 @@
 mobility = 0.3
 diffusion = 0.2
 time_step = 0.2
+
+
+VMEM_LIMIT = 60 * 1024 * 1024
+
+
+def start_copies(pairs, sems):
+    copies = [
+        pltpu.make_async_copy(source, target, sems.at[index])
+        for index, (source, target) in enumerate(pairs)
+    ]
+    for copy in copies:
+        copy.start()
+    return copies
 
 
 def upward():
@@ -89,12 +101,22 @@
 
 
 def pair_kernel(own_rows_ref, other_rows_ref, *refs):
+    sources = len(SWAPS) + 1
+    fetched = sources + 4
+    hbm_refs = refs[:fetched]
+    own_out_ref = refs[fetched]
+    other_out_refs = refs[fetched + 1 : fetched + 1 + sources]
+    refs = refs[fetched + 1 + sources :]
     near_sel_ref, far_sel_ref, moment_sel_ref, own_ref = refs[:4]
-    refs = refs[4:]
-    sources = (len(refs) - 11) // 2
-    other_refs = refs[:sources]
-    own_out_ref = refs[sources]
-    other_out_refs = refs[sources + 1 : 2 * sources + 1]
+    other_refs = refs[4:fetched]
+    sems = refs[fetched]
+    copies = start_copies(
+        [
+            (source.at[0 : target.shape[0]], target)
+            for source, target in zip(hbm_refs, refs[:fetched], strict=True)
+        ],
+        sems,
+    )
     (
         near_ref,
         far_ref,
@@ -102,13 +124,13 @@
         other_moment_ref,
         own_sum_ref,
         other_sum_ref,
-        *passed_refs,
-    ) = refs[2 * sources + 1 :]
+        dist_ref,
+        *weight_refs,
+    ) = refs[fetched + 1 :]
     clusters = own_ref.shape[0] // 4
     slots = other_out_refs[0].shape[0] // 4
     others = slots * sources
     groups = own_rows_ref.shape[0] // UNROLL
-    units = UNROLL // QUAD
     ones = jnp.ones((8, 128), jnp.float32)
     zeros = jnp.zeros((8, 128), jnp.float32)
 
@@ -155,41 +177,41 @@
         )
         return 0
 
+    own_sum_ref[...] = jnp.zeros_like(own_sum_ref)
+    other_sum_ref[...] = jnp.zeros_like(other_sum_ref)
+    weight_refs[0][...] = jnp.zeros_like(weight_refs[0])
+    for copy in copies[:4]:
+        copy.wait()
     lax.fori_loop(0, clusters // 8, near_rows, 0, unroll=4)
+    for copy in copies[4:]:
+        copy.wait()
     for source in range(sources):
         lax.fori_loop(0, slots // 8, functools.partial(far_rows, source), 0, unroll=4)
-    own_sum_ref[...] = jnp.zeros_like(own_sum_ref)
-    other_sum_ref[...] = jnp.zeros_like(other_sum_ref)
-    dist_refs, weight_refs = (passed_refs[:2], passed_refs[2:])
-    dist_refs[0][...] = jnp.full(dist_refs[0].shape, 1e38, jnp.float32)
-    weight_refs[0][...] = jnp.zeros_like(weight_refs[0])
-
-    def distances(pair, unit, turn, dist_ref):
-        own = own_rows_ref[pair + turn]
-        other = other_rows_ref[pair + turn]
-        dist_ref[unit, :, 128 * turn : 128 * turn + 128] = jnp.dot(
+    def distances(pair):
+        own = own_rows_ref[pair]
+        other = other_rows_ref[pair]
+        return jnp.dot(
             near_ref[pl.ds(pl.multiple_of(own * 128, 128), 128), 0:32],
             far_ref[pl.ds(pl.multiple_of(other * 32, 32), 32), :],
             preferred_element_type=jnp.float32,
         )
 
-    def weights(unit, turn, chunk, dist_ref, weight_ref):
+    def weights(dist, index, chunk, weight_ref):
         rows = 128 // CHUNKS
         first = rows * chunk
-        dist = dist_ref[unit, first : first + rows, 128 * turn : 128 * turn + 128]
-        root = lax.rsqrt(dist)
+        root = lax.rsqrt(dist[first : first + rows])
         weight = root * root * root
         high = weight.astype(jnp.bfloat16)
         low = (weight - high.astype(jnp.float32)).astype(jnp.bfloat16)
-        at = slice(128 * turn + first, 128 * turn + first + rows)
-        weight_ref[unit, at, :128] = high
-        weight_ref[unit, at, 128:] = low
+        at = slice(128 * index + first, 128 * index + first + rows)
+        weight_ref[at, :128] = high
+        weight_ref[at, 128:] = low
 
     def row_block(index):
         return pl.ds(pl.multiple_of(index * 16, 16), 16)
 
-    def own_product(other, weight_ref, unit, turn):
-        both = weight_ref[unit, 128 * turn : 128 * turn + 128]
+    def own_product(other, weight_ref, index):
+        both = weight_ref[128 * index : 128 * index + 128]
         return lax.dot_general(
             other_moment_ref[row_block(other), :],
             jnp.concatenate([both[:, :128], both[:, 128:]], axis=0),
@@ -197,10 +219,10 @@
             preferred_element_type=jnp.float32,
         )
 
-    def other_product(own, weight_ref, unit, turn):
+    def other_product(own, weight_ref, index):
         return jnp.dot(
             own_moment_ref[row_block(own), :],
-            weight_ref[unit, 128 * turn : 128 * turn + 128],
+            weight_ref[128 * index : 128 * index + 128],
             preferred_element_type=jnp.float32,
         )
 
@@ -208,34 +230,37 @@
         own_sum_ref[row_block(own), :] += to_own[:, :128] + to_own[:, 128:]
         other_sum_ref[row_block(other), :] += to_other[:, :128] + to_other[:, 128:]
 
-    def half_step(step, side):
-        last = jnp.maximum(step - 2, 0) * UNROLL
-        first = jnp.minimum(step, groups - 1) * UNROLL
+    def half_step(step, side, dist):
+        last = jnp.maximum(step - 1, 0) * UNROLL
         waiting = []
         for index in range(UNROLL):
-            unit, turn = (index // QUAD, index % QUAD)
             own = own_rows_ref[last + index]
             other = other_rows_ref[last + index]
-            passed = (dist_refs[side], weight_refs[1 - side])
-            distances(first + QUAD * unit, unit, turn, dist_refs[1 - side])
-            weights(unit, turn, 0, *passed)
-            to_own = own_product(other, weight_refs[side], unit, turn)
-            weights(unit, turn, 1, *passed)
-            weights(unit, turn, 2, *passed)
-            to_other = other_product(own, weight_refs[side], unit, turn)
-            weights(unit, turn, 3, *passed)
+            later = distances(jnp.minimum(step * UNROLL + index + 1, groups * UNROLL - 1))
+            weights(dist, index, 0, weight_refs[1 - side])
+            to_own = own_product(other, weight_refs[side], index)
+            weights(dist, index, 1, weight_refs[1 - side])
+            weights(dist, index, 2, weight_refs[1 - side])
+            to_other = other_product(own, weight_refs[side], index)
+            weights(dist, index, 3, weight_refs[1 - side])
+            dist = later
             waiting.append((own, other, to_own, to_other))
             if len(waiting) > 2:
                 add_rows(*waiting.pop(0))
         for entry in waiting:
             add_rows(*entry)
+        return dist
 
     def visit(step, _):
+        dist = dist_ref[...]
         for side in range(2):
-            half_step(step * 2 + side, side)
-        return 0
-
-    lax.fori_loop(0, (groups + 2) // 2, visit, 0)
+            dist = half_step(step * 2 + side, side, dist)
+        dist_ref[...] = dist
+        return 0
+
+    dist_ref[...] = distances(0)
+    lax.fori_loop(0, groups // 2, visit, 0)
+    half_step(groups, 0, dist_ref[...])
 
     def finish(data_ref, out_ref, sum_ref, base, step, _):
         start = pl.multiple_of(step * 8, 8)
@@ -275,30 +300,35 @@
     pairs = own_rows.shape[0]
     smem = pl.BlockSpec(memory_space=pltpu.SMEM)
     vmem = pl.BlockSpec(memory_space=pltpu.VMEM)
+    hbm = pl.BlockSpec(memory_space=pltpu.HBM)
+    operands = (*selections(), own)
     return pl.pallas_call(
         pair_kernel,
         out_shape=(
             jax.ShapeDtypeStruct(own.shape, jnp.float32),
             *[jax.ShapeDtypeStruct((slots * 4, 128), jnp.float32)] * len(arrived),
         ),
-        in_specs=[smem, smem] + [vmem] * (4 + len(arrived)),
+        in_specs=[smem, smem] + [hbm] * (4 + len(arrived)),
         out_specs=(vmem,) * (len(arrived) + 1),
         scratch_shapes=[
+            *[pltpu.VMEM(operand.shape, operand.dtype) for operand in operands],
+            *[pltpu.VMEM((slots * 4, 128), jnp.float32)] * len(arrived),
+            pltpu.SemaphoreType.DMA((len(operands) + len(arrived),)),
             pltpu.VMEM((clusters * 128, 128), jnp.bfloat16),
             pltpu.VMEM((others * 32, 128), jnp.bfloat16),
             pltpu.VMEM((clusters * 16, 128), jnp.bfloat16),
             pltpu.VMEM((others * 16, 128), jnp.bfloat16),
             pltpu.VMEM((clusters * 16, 128), jnp.float32),
             pltpu.VMEM((others * 16, 128), jnp.float32),
-            *[pltpu.VMEM((UNROLL // QUAD, 128, 128 * QUAD), jnp.float32)] * 2,
-            *[pltpu.VMEM((UNROLL // QUAD, 128 * QUAD, 256), jnp.bfloat16)] * 2,
+            pltpu.VMEM((128, 128), jnp.float32),
+            *[pltpu.VMEM((128 * UNROLL, 256), jnp.bfloat16)] * 2,
         ],
-        compiler_params=pltpu.CompilerParams(vmem_limit_bytes=40 * 1024 * 1024),
+        compiler_params=pltpu.CompilerParams(vmem_limit_bytes=VMEM_LIMIT),
         cost_estimate=pl.CostEstimate(
             flops=pairs * 128 * 128 * 20, bytes_accessed=4 * 1024 * 1024, transcendentals=0
         ),
         name="pair_forces",
-    )(own_rows, other_rows, *selections(), own, *arrived)
+    )(own_rows, other_rows, *operands, *arrived)
 
 
 def prepare_kernel(
@@ -307,11 +337,14 @@
     send_index_ref,
     send_count_ref,
     cell_row_ref,
+    pair_dir_ref,
+    pair_slot_ref,
     position_hbm,
     charge_hbm,
     ion_hbm,
     start_hbm,
     screen_hbm,
+    row_ref,
     own_ref,
     masked_ref,
     inverse_ref,
@@ -320,20 +353,16 @@
 ):
     out_refs, scratch = (refs[:-8], refs[-8:])
     sum_ref, deposit_ref, position_ref, charge_ref, ion_ref, start_ref, screen_ref, sems = scratch
-    copies = [
-        pltpu.make_async_copy(source, target, sems.at[index])
-        for index, (source, target) in enumerate(
-            (
-                (position_hbm, position_ref),
-                (charge_hbm, charge_ref),
-                (ion_hbm, ion_ref),
-                (start_hbm, start_ref),
-                (screen_hbm, screen_ref),
-            )
-        )
-    ]
-    for copy in copies:
-        copy.start()
+    copies = start_copies(
+        (
+            (position_hbm, position_ref),
+            (charge_hbm, charge_ref),
+            (ion_hbm, ion_ref),
+            (start_hbm, start_ref),
+            (screen_hbm, screen_ref),
+        ),
+        sems,
+    )
     copies[0].wait()
     copies[1].wait()
     clusters = charge_ref.shape[0]
@@ -358,6 +387,11 @@
     lax.fori_loop(0, clusters // 8, collect, 0, unroll=4)
 
     ups = upward()
+    direction = pair_dir_ref[...]
+    way = lax.shift_right_arithmetic(direction - 1, 1)
+    flip = jnp.where(way == 0, ups[0], jnp.where(way == 1, ups[1], ups[2]))
+    position = 1 + 2 * way + lax.bitwise_xor(lax.bitwise_and(direction - 1, 1), flip)
+    row_ref[...] = jnp.where(direction == 0, 0, position) * slots + pair_slot_ref[...]
 
     def fill_messages(step, _):
         for position, out_ref in enumerate(out_refs):
@@ -432,7 +466,19 @@
             fill_rows(out_refs[2], up == 0)
 
 
-def prepare(fill, cell, send_index, send_count, positions, charges, ions, start, screen):
+def prepare(
+    fill,
+    cell,
+    send_index,
+    send_count,
+    pair_dir,
+    pair_slot,
+    positions,
+    charges,
+    ions,
+    start,
+    screen,
+):
     clusters = charges.shape[0]
     directions, slots = send_index.shape
     cells_x = ions.shape[0]
@@ -443,14 +489,15 @@
     return pl.pallas_call(
         prepare_kernel,
         out_shape=(
+            jax.ShapeDtypeStruct(pair_dir.shape, jnp.int32),
             jax.ShapeDtypeStruct((clusters, 4, 128), jnp.float32),
             jax.ShapeDtypeStruct((clusters, 128), jnp.float32),
             jax.ShapeDtypeStruct(ions.shape, jnp.float32),
             jax.ShapeDtypeStruct(ions.shape, jnp.float32),
             *[jax.ShapeDtypeStruct((count, 128), jnp.float32) for count in rows],
         ),
-        in_specs=[smem] * 4 + [vmem] + [pl.BlockSpec(memory_space=pltpu.HBM)] * 5,
-        out_specs=(vmem,) * (4 + directions),
+        in_specs=[smem] * 4 + [vmem] * 3 + [pl.BlockSpec(memory_space=pltpu.HBM)] * 5,
+        out_specs=(vmem,) * (5 + directions),
         scratch_shapes=[
             pltpu.VMEM((clusters, 128), jnp.float32),
             pltpu.VMEM((ions.size // 128, 128), jnp.float32),
@@ -460,7 +507,7 @@
             ],
             pltpu.SemaphoreType.DMA((5,)),
         ],
-        compiler_params=pltpu.CompilerParams(vmem_limit_bytes=60 * 1024 * 1024),
+        compiler_params=pltpu.CompilerParams(vmem_limit_bytes=VMEM_LIMIT),
         name="prepare",
     )(
         fill,
@@ -468,6 +515,8 @@
         send_index,
         send_count,
         cell.reshape(1, clusters),
+        pair_dir,
+        pair_slot,
         positions,
         charges,
         ions,
@@ -480,40 +529,49 @@
     return (cells_y + 2 * DEPTH + 7) // 8 * 8
 
 
-def collect_rows(rim_ref, first_ref, second_ref, base):
-    size = rim_ref.shape[0] // 2
-    up = upward()[0]
-    rim_ref[pl.ds(pl.multiple_of(up * size, size), size), :] = first_ref[base : base + size, :]
-    rim_ref[pl.ds(pl.multiple_of((1 - up) * size, size), size), :] = second_ref[
-        base : base + size, :
-    ]
-
-
-def fill_lines(target_ref, plane, field, field_ref, index, rim_ref):
-    cells_x, cells_y, _ = field_ref.shape
+def fill_lines(target_ref, plane, field, field_ref, index, rim_ref, source):
+    cells_y = field_ref.shape[1]
     width = HALO_WIDTHS[field]
     for half in range(2):
         at = (plane * 2 + half) * line_rows(cells_y) + DEPTH
-        first = index * 32 + 16 * half + sum(HALO_WIDTHS[:field])
+        first = source * 32 + 16 * half + sum(HALO_WIDTHS[:field])
         target_ref[pl.ds(at - width, width), :] = rim_ref[pl.ds(first, width), :]
         target_ref[pl.ds(at, cells_y), :] = field_ref[index, :, 128 * half : 128 * half + 128]
-        first = first + cells_x * 32
+        first = first + rim_ref.shape[0] // 2
         target_ref[pl.ds(at + cells_y, width), :] = rim_ref[pl.ds(first, width), :]
 
 
 def planes_kernel(base, *refs):
-    field_refs, (first_ref, second_ref, *out_refs, rim_ref) = (refs[:4], refs[4:])
+    field_refs, rims, out_refs = (refs[:4], refs[4:6], refs[6:8])
+    edge_refs, rim_ref, sems = (refs[8:12], refs[12], refs[13])
     cells_x = field_refs[0].shape[0]
-    collect_rows(rim_ref, first_ref, second_ref, base)
-    up = upward()[2]
+    size = cells_x * 32
+    ups = upward()
+    moves = [
+        (rim.at[base : base + size], rim_ref.at[pl.ds(pl.multiple_of(side * size, size), size)])
+        for rim, side in zip(rims, (ups[0], 1 - ups[0]), strict=True)
+    ]
+    for field_ref, edge_ref, width in zip(field_refs, edge_refs, HALO_WIDTHS, strict=True):
+        moves.append((field_ref.at[0:width], edge_ref.at[0:width]))
+        moves.append((field_ref.at[cells_x - width : cells_x], edge_ref.at[width : 2 * width]))
+    for copy in start_copies(moves, sems):
+        copy.wait()
     for field, width in enumerate(HALO_WIDTHS):
         plane = sum(HALO_WIDTHS[:field])
 
         def fill(step, _, field=field, plane=plane, width=width):
             for phase, out_ref in enumerate(out_refs):
-                last = up if phase == 0 else 1 - up
+                last = ups[2] if phase == 0 else 1 - ups[2]
                 source = last * (cells_x - width) + step
-                fill_lines(out_ref, plane + step, field, field_refs[field], source, rim_ref)
+                fill_lines(
+                    out_ref,
+                    plane + step,
+                    field,
+                    edge_refs[field],
+                    last * width + step,
+                    rim_ref,
+                    source,
+                )
             return 0
 
         lax.fori_loop(0, width, fill, 0)
@@ -521,16 +579,20 @@
 
 def planes(fields, first, second, base):
     vmem = pl.BlockSpec(memory_space=pltpu.VMEM)
-    cells_x, cells_y, _ = fields[0].shape
+    cells_x, cells_y, cells_z = fields[0].shape
     rows = sum(HALO_WIDTHS) * 2 * line_rows(cells_y)
     shape = jax.ShapeDtypeStruct((rows, 128), jnp.float32)
     return pl.pallas_call(
         functools.partial(planes_kernel, base),
         out_shape=(shape, shape),
-        in_specs=[vmem] * 6,
+        in_specs=[pl.BlockSpec(memory_space=pltpu.HBM)] * 6,
         out_specs=(vmem, vmem),
-        scratch_shapes=[pltpu.VMEM((cells_x * 64, 128), jnp.float32)],
-        compiler_params=pltpu.CompilerParams(vmem_limit_bytes=32 * 1024 * 1024),
+        scratch_shapes=[
+            *[pltpu.VMEM((2 * width, cells_y, cells_z), jnp.float32) for width in HALO_WIDTHS],
+            pltpu.VMEM((cells_x * 64, 128), jnp.float32),
+            pltpu.SemaphoreType.DMA((2 + 2 * len(HALO_WIDTHS),)),
+        ],
+        compiler_params=pltpu.CompilerParams(vmem_limit_bytes=VMEM_LIMIT),
         name="planes",
     )(*fields, first, second)
 
@@ -545,36 +607,46 @@
 
 
 def grid_kernel(base, *refs):
-    cell_ref, masked_ref = refs[:2]
-    field_refs = refs[2:6]
-    first_ref, second_ref, *plane_refs = refs[6:10]
+    cell_ref, masked_hbm = refs[:2]
+    hbm_refs, plane_hbms = (refs[2:6], refs[8:10])
     potential_ref, next_ref, force_ref = refs[10:13]
     start_ref, inverse_ref, source_ref, ion_ref = refs[13:17]
     updates, resids, final_ref, pick_refs = (refs[17:20], refs[20:22], refs[22], refs[23:26])
-    rim_ref = refs[26]
+    rim_ref, field_refs, masked_ref, sems = (refs[26], refs[27:31], refs[31], refs[32])
     cells_x, cells_y, _ = field_refs[0].shape
     rows = line_rows(cells_y)
     inner = cells_y + 2 * DEPTH - 2
     clusters = masked_ref.shape[0]
-    up = upward()[2]
-    collect_rows(rim_ref, first_ref, second_ref, base)
-
+    ups = upward()
+    size = cells_x * 32
+    moves = [
+        (rim.at[base : base + size], rim_ref.at[pl.ds(pl.multiple_of(side * size, size), size)])
+        for rim, side in zip(refs[6:8], (ups[0], 1 - ups[0]), strict=True)
+    ]
+    moves += zip(hbm_refs, field_refs, strict=True)
+    moves.append((masked_hbm, masked_ref))
+    near = len(moves)
     for field, target_ref in enumerate((start_ref, inverse_ref, source_ref, ion_ref)):
         width = HALO_WIDTHS[field]
         size = width * 2 * rows
         first = sum(HALO_WIDTHS[:field]) * 2 * rows
-        for phase, plane_ref in enumerate(plane_refs):
-            higher = up if phase == 0 else 1 - up
+        for phase, plane_ref in enumerate(plane_hbms):
+            higher = ups[2] if phase == 0 else 1 - ups[2]
             plane = (DEPTH - width) + higher * (cells_x + width)
             at = pl.ds(pl.multiple_of(plane * 2 * rows, 2 * rows), size)
-            target_ref[at, :] = plane_ref[first : first + size, :]
+            moves.append((plane_ref.at[first : first + size], target_ref.at[at]))
+    copies = start_copies(moves, sems)
+    for copy in copies[:near]:
+        copy.wait()
 
     def fill(index, _):
         for field, target_ref in enumerate((start_ref, inverse_ref, source_ref, ion_ref)):
-            fill_lines(target_ref, DEPTH + index, field, field_refs[field], index, rim_ref)
+            fill_lines(target_ref, DEPTH + index, field, field_refs[field], index, rim_ref, index)
         return 0
 
     lax.fori_loop(0, cells_x, fill, 0, unroll=2)
+    for copy in copies[near:]:
+        copy.wait()
 
     def beyond(values):
         lane = lax.broadcasted_iota(jnp.int32, values[0].shape, 1)
@@ -725,12 +797,14 @@
             jax.ShapeDtypeStruct(fields[0].shape, jnp.float32),
             jax.ShapeDtypeStruct((clusters * 4, 128), jnp.float32),
         ),
-        in_specs=[smem] + [vmem] * 9,
+        in_specs=[smem] + [pl.BlockSpec(memory_space=pltpu.HBM)] * 9,
         out_specs=(vmem,) * 3,
         scratch_shapes=[pltpu.VMEM(block, jnp.float32)] * 10
         + [pltpu.VMEM((clusters, 128), jnp.float32)] * 3
-        + [pltpu.VMEM((cells_x * 64, 128), jnp.float32)],
-        compiler_params=pltpu.CompilerParams(vmem_limit_bytes=40 * 1024 * 1024),
+        + [pltpu.VMEM((cells_x * 64, 128), jnp.float32)]
+        + [pltpu.VMEM(field.shape, jnp.float32) for field in fields]
+        + [pltpu.VMEM(masked.shape, jnp.float32), pltpu.SemaphoreType.DMA((15,))],
+        compiler_params=pltpu.CompilerParams(vmem_limit_bytes=VMEM_LIMIT),
         cost_estimate=pl.CostEstimate(
             flops=block[0] * block[1] * 100, bytes_accessed=8 << 20, transcendentals=0
         ),
@@ -738,8 +812,13 @@
     )(cell, masked, *fields, *rims, *edges)
 
 
-def gather_forces_kernel(send_index_ref, own_ref, field_ref, *refs):
-    back_refs, (out_ref, sum_ref) = (refs[:-2], refs[-2:])
+def gather_forces_kernel(send_index_ref, *refs):
+    fetched = len(SWAPS) + 3
+    out_ref, sum_ref = refs[fetched : fetched + 2]
+    own_ref, field_ref, *back_refs = refs[fetched + 2 : -1]
+    copies = start_copies(zip(refs[:fetched], refs[fetched + 2 : -1], strict=True), refs[-1])
+    for copy in copies:
+        copy.wait()
     clusters = own_ref.shape[0]
     slots = send_index_ref.shape[1]
     sum_ref[...] = own_ref[...] + field_ref[...]
@@ -769,10 +848,13 @@
     return pl.pallas_call(
         gather_forces_kernel,
         out_shape=jax.ShapeDtypeStruct((3, clusters * 128), jnp.float32),
-        in_specs=[smem] + [vmem] * (2 + len(backs)),
+        in_specs=[smem] + [pl.BlockSpec(memory_space=pltpu.HBM)] * (2 + len(backs)),
         out_specs=vmem,
-        scratch_shapes=[pltpu.VMEM(own.shape, jnp.float32)],
-        compiler_params=pltpu.CompilerParams(vmem_limit_bytes=32 * 1024 * 1024),
+        scratch_shapes=[
+            *[pltpu.VMEM(part.shape, jnp.float32) for part in (own, own, field, *backs)],
+            pltpu.SemaphoreType.DMA((2 + len(backs),)),
+        ],
+        compiler_params=pltpu.CompilerParams(vmem_limit_bytes=VMEM_LIMIT),
         name="gather_forces",
     )(send_index, own, field, *backs)
 
@@ -795,11 +877,13 @@
     psize = charges.shape[0] // clusters
     slots = send_index.shape[1]
     base = slots * 4
-    own, masked, inverse, source, local, *messages = prepare(
+    other_rows, own, masked, inverse, source, local, *messages = prepare(
         cluster_fill,
         cluster_cell,
         send_index,
         send_count,
+        pair_dir.reshape(-1, 128),
+        pair_slot.reshape(-1, 128),
         positions,
         charges.reshape(clusters, psize),
         ion_density,
@@ -815,13 +899,9 @@
     edges = [
         swapped(edge, "grp", 1, phase) for phase, edge in enumerate(planes(fields, *rims, base))
     ]
-    way = lax.shift_right_arithmetic(pair_dir - 1, 1)
-    ups = upward()
-    flip = jnp.where(way == 0, ups[0], jnp.where(way == 1, ups[1], ups[2]))
-    position = 1 + 2 * way + lax.bitwise_xor(lax.bitwise_and(pair_dir - 1, 1), flip)
     own_force, *reactions = pair_forces(
         pair_local,
-        jnp.where(pair_dir == 0, 0, position) * slots + pair_slot,
+        other_rows.reshape(-1),
         own.reshape(clusters * 4, psize),
         arrived,
         slots,

time: 116 us -> 112 us (0.966)
  local copies, waits for them, and re-layouts: 8.47 us -> 1.53 us
  Pallas kernels: 73.5 us -> 77.5 us
    unnamed x46 -> x28, local copies, waits for them, and re-layouts: 8.47 us -> 1.53 us
    pallas_call x1, Pallas kernels: 11.5 us -> 13.7 us  [grid_step(): pl.pallas_call(functools.partial(grid_kernel, base), out_shape=(jax.Shape...]
    pallas_call x1, Pallas kernels: 2.86 us -> 4.31 us  [gather_forces(): pl.pallas_call(gather_forces_kernel, out_shape=jax.ShapeDtypeStruct((3, c...]
    pallas_call x1, Pallas kernels: 1.31 us -> 2.6 us  [planes(): pl.pallas_call(functools.partial(planes_kernel, base), out_shape=(shape,...]
  transfers between devices with their start and end apart: 14 -> 14, of which waited for: 2 -> 3; matrix products, arithmetic and copies ran while one was open for 0% -> 0% of each run, Pallas kernels for 55% -> 58%
where the time goes in v14:
time: 112 us; the launch traced here: 111 us
  Pallas kernels  77.5 us (69%)
  starting transfers between devices  25.2 us (22%)
  waiting for transfers between devices  6.09 us (5%)
  local copies, waits for them, and re-layouts  1.53 us (1%)
    pallas_call x1, Pallas kernels, pair_forces(): pl.pallas_call(pair_kernel, out_shape=(jax.ShapeDtypeStruct(own.shape, jn...  50.5 us
    ppermute x14, starting transfers between devices, swapped(): return lax.ppermute(shard, axis, pairs)  25.2 us
    pallas_call x1, Pallas kernels, grid_step(): pl.pallas_call(functools.partial(grid_kernel, base), out_shape=(jax.Shape...  13.7 us
    pallas_call x1, Pallas kernels, prepare(): pl.pallas_call(prepare_kernel, out_shape=(jax.ShapeDtypeStruct(pair_dir.s...  6.41 us
    ppermute x14, waiting for transfers between devices, swapped(): return lax.ppermute(shard, axis, pairs)  6.09 us
    pallas_call x1, Pallas kernels, gather_forces(): pl.pallas_call(gather_forces_kernel, out_shape=jax.ShapeDtypeStruct((3, c...  4.31 us
    pallas_call x1, Pallas kernels, planes(): pl.pallas_call(functools.partial(planes_kernel, base), out_shape=(shape,...  2.6 us
  transfers between devices with their start and end apart: 14, of which 3 were waited for; matrix products, arithmetic and copies ran while one was open for 0% of the time, Pallas kernels for 58%

profile of v14, /device:TPU:13, one launch (start us, length us, event | category | flops | bytes accessed | tf_op | source)
XLA Modules:
  0.0 111.3 jit_solution(15194939886669844450)
XLA Ops:
  0.6 6.4 %prepare.1 = (s32[8,128]{1,0:T(8,128)}, f32[256,4,128]{2,1,0:T(4,128)}, f32[256,128]{1,0:T(8,128)}, f32[16,32,256]{2,1,0:T(8,128)}, f32[16,32,256]{2,1,0:T(8,128...) custom-call(s32[256]{0:T(256)} %fill_ref.1, ...), custom_call_target="tpu_custom_call" | custom-call | tf_op jit(solution)/shard_map/prepare/pallas_call | solution.py:489
  7.0 0.7 collective-permute-start
  7.8 3.1 %collective-permute-start.1 = (f32[640,128]{1,0:T(8,128)}, f32[640,128]{1,0:T(8,128)S(1)}, u32[]{:S(2)}, u32[]{:S(2)}) collective-permute-start(f32[640,128]{1,0:T(8,128)} %get-tuple-element.39), channel_id=1, source_target_pairs={{1,2},{2,1},{3,4},{4,3},{5,6},{6,5},{9,10},{10,9},{11,12},{12,11},... | collective-permute-start | bytes 983048 | tf_op jit(solution)/shard_map/ppermute | solution.py:64
  10.9 0.2 collective-permute-start.2
  11.1 3.0 %collective-permute-start.3 = (f32[128,128]{1,0:T(8,128)}, f32[128,128]{1,0:T(8,128)S(1)}, u32[]{:S(2)}, u32[]{:S(2)}) collective-permute-start(f32[128,128]{1,0:T(8,128)} %get-tuple-element.41), channel_id=1, source_target_pairs={{2,4},{3,5},{4,2},{5,3},{10,12},{11,13},{12,10},{13,11},{18,20},{1... | collective-permute-start | bytes 196616 | tf_op jit(solution)/shard_map/ppermute | solution.py:64
  14.2 1.3 %collective-permute-start.4 = (f32[128,128]{1,0:T(8,128)}, f32[128,128]{1,0:T(8,128)S(1)}, u32[]{:S(2)}, u32[]{:S(2)}) collective-permute-start(f32[128,128]{1,0:T(8,128)} %get-tuple-element.42), channel_id=1, source_target_pairs={{0,8},{8,0},{16,24},{24,16},{1,9},{9,1},{17,25},{25,17},{2,10},{10... | collective-permute-start | bytes 196616 | tf_op jit(solution)/shard_map/ppermute | solution.py:64
  15.5 1.9 %collective-permute-done.2.refs_7_ = f32[128,128]{1,0:T(8,128)S(1)} collective-permute-done((f32[128,128]{1,0:T(8,128)}, f32[128,128]{1,0:T(8,128)S(1)}, u32[]{:S(2)}, u32[]{:S(2)}) %collective-permute-start.2) | collective-permute-done | bytes 65568 | tf_op jit(solution)/shard_map/ppermute | solution.py:64
  17.4 0.0 copy-start.6
  17.4 3.0 %collective-permute-start.5 = (f32[128,128]{1,0:T(8,128)}, f32[128,128]{1,0:T(8,128)S(1)}, u32[]{:S(2)}, u32[]{:S(2)}) collective-permute-start(f32[128,128]{1,0:T(8,128)} %get-tuple-element.43), channel_id=1, source_target_pairs={{8,16},{16,8},{9,17},{17,9},{10,18},{18,10},{11,19},{19,11},{12,20... | collective-permute-start | bytes 196616 | tf_op jit(solution)/shard_map/ppermute | solution.py:64
  20.5 0.0 collective-permute-done.3.refs_8_
  20.5 0.0 copy-start.8
  20.5 0.0 collective-permute-done.4.refs_9_
  20.5 0.0 copy-start.9
  20.5 4.0 %collective-permute-done.5.refs_10_ = f32[128,128]{1,0:T(8,128)S(1)} collective-permute-done((f32[128,128]{1,0:T(8,128)}, f32[128,128]{1,0:T(8,128)S(1)}, u32[]{:S(2)}, u32[]{:S(2)}) %collective-permute-start.5) | collective-permute-done | bytes 65568 | tf_op jit(solution)/shard_map/ppermute | solution.py:64
  24.5 0.0 copy-start.11
  24.5 0.0 collective-permute-done.refs_5_.refs_4_.refs_6_
  24.5 0.0 copy-start
  24.5 0.0 collective-permute-done.1.refs_6_.refs_5_.refs_7_
  24.5 0.0 copy-start.1
  24.5 0.7 copy-done
  25.2 0.1 copy-done.1
  25.3 2.6 %planes.1 = (f32[1344,128]{1,0:T(8,128)}, f32[1344,128]{1,0:T(8,128)}) custom-call(f32[16,32,256]{2,1,0:T(8,128)} %refs_2_.2, f32[16,32,256]{2,1,0:T(8,128)} %get-tuple-element.53.refs_1_.refs_3_, f32[16,32,256]{2,1,0:T(8,128)} %get-tuple-element.54.refs_2_.refs_4_, f32[16,32,256]{2,1,0:T(8,128)} %refs_5_.1, f32[640,128]{1,0:T(8,128)} %copy-done, ...), custom_call_target="tpu_custom_call" | custom-call | tf_op jit(solution)/shard_map/planes/pallas_call | solution.py:585
  28.0 0.0 copy-done.6
  28.0 0.0 copy-done.8
  28.0 0.0 copy-done.9
  28.0 0.0 copy-done.11
  28.0 0.1 collective-permute-start.6
  28.1 2.4 %collective-permute-start.7 = (f32[1344,128]{1,0:T(8,128)}, f32[1344,128]{1,0:T(8,128)S(1)}, u32[]{:S(2)}, u32[]{:S(2)}) collective-permute-start(f32[1344,128]{1,0:T(8,128)} %get-tuple-element.56), channel_id=1, source_target_pairs={{8,16},{16,8},{9,17},{17,9},{10,18},{18,10},{11,19},{19,11},{12,20... | collective-permute-start | bytes 2064392 | tf_op jit(solution)/shard_map/ppermute | solution.py:64
  30.5 50.5 %pair_forces.1 = (f32[1024,128]{1,0:T(8,128)}, f32[128,128]{1,0:T(8,128)}, f32[128,128]{1,0:T(8,128)}, f32[128,128]{1,0:T(8,128)}, f32[128,128]{1,0:T(8,128)}, /...) custom-call(s32[1024]{0:T(1024)} %own_rows_ref.1, s32[1024]{0:T(1024)} %bitcast.29, ...), custom_call_target="tpu_custom_call" | custom-call | flops 335544320 | bytes 4194304 | tf_op jit(solution)/shard_map/pair_forces/pallas_call | solution.py:305
  81.0 5.3 %collective-permute-start.9 = (f32[128,128]{1,0:T(8,128)}, f32[128,128]{1,0:T(8,128)S(1)}, u32[]{:S(2)}, u32[]{:S(2)}) collective-permute-start(f32[128,128]{1,0:T(8,128)} %get-tuple-element.60), channel_id=1, source_target_pairs={{1,2},{2,1},{3,4},{4,3},{5,6},{6,5},{9,10},{10,9},{11,12},{12,11},... | collective-permute-start | bytes 196616 | tf_op jit(solution)/shard_map/ppermute | solution.py:64
  86.3 0.1 collective-permute-start.10
  86.4 1.9 %collective-permute-start.11 = (f32[128,128]{1,0:T(8,128)}, f32[128,128]{1,0:T(8,128)S(1)}, u32[]{:S(2)}, u32[]{:S(2)}) collective-permute-start(f32[128,128]{1,0:T(8,128)} %get-tuple-element.62), channel_id=1, source_target_pairs={{2,4},{3,5},{4,2},{5,3},{10,12},{11,13},{12,10},{13,11},{18,20},{1... | collective-permute-start | bytes 196616 | tf_op jit(solution)/shard_map/ppermute | solution.py:64
  88.3 0.1 collective-permute-done.9
  88.4 0.0 copy-start.4
  88.4 0.0 collective-permute-start.12
  88.4 0.0 collective-permute-done.6.refs_8_
  88.4 0.0 copy-start.2
  88.4 3.1 %collective-permute-start.13 = (f32[128,128]{1,0:T(8,128)}, f32[128,128]{1,0:T(8,128)S(1)}, u32[]{:S(2)}, u32[]{:S(2)}) collective-permute-start(f32[128,128]{1,0:T(8,128)} %get-tuple-element.64), channel_id=1, source_target_pairs={{8,16},{16,8},{9,17},{17,9},{10,18},{18,10},{11,19},{19,11},{12,20... | collective-permute-start | bytes 196616 | tf_op jit(solution)/shard_map/ppermute | solution.py:64
  91.6 0.0 collective-permute-done.7.refs_9_
  91.6 0.0 copy-start.3
  91.6 0.9 collective-permute-start.8
  92.5 0.0 copy-done.2
  92.5 0.0 copy-done.3
  92.5 13.7 %grid_step.1 = (f32[16,32,256]{2,1,0:T(8,128)}, f32[16,32,256]{2,1,0:T(8,128)}, f32[1024,128]{1,0:T(8,128)}) custom-call(s32[256]{0:T(256)} %refs_0_.4, f32[256,128]{1,0:T(8,128)} %get-tuple-element.52.refs_1_, f32[16,32,256]{2,1,0:T(8,128)} %refs_2_.2, f32[16,32,256]{2,1,0:T(8,128)} %get-tuple-element.53.refs_1_.refs_3_, ...), custom_call_target="tpu_custom_call" | custom-call | flops 31948800 | bytes 8388608 | tf_op jit(solution)/shard_map/grid_step/pallas_call | solution.py:793
  106.2 0.0 copy-done.4
  106.2 0.0 collective-permute-done.10
  106.2 0.0 copy-start.5
  106.2 0.0 collective-permute-done.11
  106.2 0.0 copy-start.7
  106.2 0.0 collective-permute-done.12
  106.2 0.0 copy-start.10
  106.3 0.0 collective-permute-done.13
  106.3 0.0 copy-start.12
  106.3 0.0 collective-permute-done.8
  106.3 0.0 copy-start.13
  106.3 0.5 copy-done.5
  106.8 0.0 copy-done.7
  106.9 0.0 copy-done.10
  106.9 0.0 copy-done.12
  106.9 0.0 copy-done.13
  107.0 4.3 %gather_forces.1 = f32[3,32768]{1,0:T(4,128)} custom-call(s32[7,32]{1,0:T(8,128)} %send_index_ref.3, f32[256,4,128]{2,1,0:T(4,128)} %bitcast.16, f32[256,4,128]{2,1,0:T(4,128)} %bitcast.17, f32[32,4,128]{2,1,0:T(4,128)} %bitcast.19, f32[32,4,128]{2,1,0:T(4,128)} %bitcast.25, f32[32,4,128]{2,1,0:T(4,128)} %bitcast.20, f32[32,4,128]{2,1,0:T(4,128)} %bitcast.21, ...), custom_call_target="tpu_custom_call" | custom-call | tf_op jit(solution)/shard_map/gather_forces/pallas_call | solution.py:848
Async XLA Ops:
  7.0 17.4 %collective-permute-start = (f32[640,128]{1,0:T(8,128)}, f32[640,128]{1,0:T(8,128)S(1)}, u32[]{:S(2)}, u32[]{:S(2)}) collective-permute-start(f32[640,128]{1,0:T(8,128)} %get-tuple-element.38), channel_id=1, source_target_pairs={{0,1},{1,0},{2,3},{3,2},{4,5},{5,4},{6,7},{7,6},{8,9},{9,8},{10,11... | collective-permute-start | bytes 983048 | tf_op jit(solution)/shard_map/ppermute | solution.py:64
  7.8 16.7 %collective-permute-start.1 = (f32[640,128]{1,0:T(8,128)}, f32[640,128]{1,0:T(8,128)S(1)}, u32[]{:S(2)}, u32[]{:S(2)}) collective-permute-start(f32[640,128]{1,0:T(8,128)} %get-tuple-element.39), channel_id=1, source_target_pairs={{1,2},{2,1},{3,4},{4,3},{5,6},{6,5},{9,10},{10,9},{11,12},{12,11},... | collective-permute-start | bytes 983048 | tf_op jit(solution)/shard_map/ppermute | solution.py:64
  10.9 6.5 %collective-permute-start.2 = (f32[128,128]{1,0:T(8,128)}, f32[128,128]{1,0:T(8,128)S(1)}, u32[]{:S(2)}, u32[]{:S(2)}) collective-permute-start(f32[128,128]{1,0:T(8,128)} %get-tuple-element.40), channel_id=1, source_target_pairs={{0,2},{1,3},{2,0},{3,1},{4,6},{5,7},{6,4},{7,5},{8,10},{9,11},{10,... | collective-permute-start | bytes 196616 | tf_op jit(solution)/shard_map/ppermute | solution.py:64
  11.1 9.3 %collective-permute-start.3 = (f32[128,128]{1,0:T(8,128)}, f32[128,128]{1,0:T(8,128)S(1)}, u32[]{:S(2)}, u32[]{:S(2)}) collective-permute-start(f32[128,128]{1,0:T(8,128)} %get-tuple-element.41), channel_id=1, source_target_pairs={{2,4},{3,5},{4,2},{5,3},{10,12},{11,13},{12,10},{13,11},{18,20},{1... | collective-permute-start | bytes 196616 | tf_op jit(solution)/shard_map/ppermute | solution.py:64
  14.2 6.3 %collective-permute-start.4 = (f32[128,128]{1,0:T(8,128)}, f32[128,128]{1,0:T(8,128)S(1)}, u32[]{:S(2)}, u32[]{:S(2)}) collective-permute-start(f32[128,128]{1,0:T(8,128)} %get-tuple-element.42), channel_id=1, source_target_pairs={{0,8},{8,0},{16,24},{24,16},{1,9},{9,1},{17,25},{25,17},{2,10},{10... | collective-permute-start | bytes 196616 | tf_op jit(solution)/shard_map/ppermute | solution.py:64
  17.4 10.5 %copy-start.6 = (f32[128,128]{1,0:T(8,128)}, f32[128,128]{1,0:T(8,128)S(1)}, u32[]{:S(2)}) copy-start(f32[128,128]{1,0:T(8,128)S(1)} %collective-permute-done.2.refs_7_) | copy-start | bytes 196612
  17.4 7.1 %collective-permute-start.5 = (f32[128,128]{1,0:T(8,128)}, f32[128,128]{1,0:T(8,128)S(1)}, u32[]{:S(2)}, u32[]{:S(2)}) collective-permute-start(f32[128,128]{1,0:T(8,128)} %get-tuple-element.43), channel_id=1, source_target_pairs={{8,16},{16,8},{9,17},{17,9},{10,18},{18,10},{11,19},{19,11},{12,20... | collective-permute-start | bytes 196616 | tf_op jit(solution)/shard_map/ppermute | solution.py:64
  20.5 7.5 %copy-start.8 = (f32[128,128]{1,0:T(8,128)}, f32[128,128]{1,0:T(8,128)S(1)}, u32[]{:S(2)}) copy-start(f32[128,128]{1,0:T(8,128)S(1)} %collective-permute-done.3.refs_8_) | copy-start | bytes 196612
  20.5 7.5 %copy-start.9 = (f32[128,128]{1,0:T(8,128)}, f32[128,128]{1,0:T(8,128)S(1)}, u32[]{:S(2)}) copy-start(f32[128,128]{1,0:T(8,128)S(1)} %collective-permute-done.4.refs_9_) | copy-start | bytes 196612
  24.5 3.5 %copy-start.11 = (f32[128,128]{1,0:T(8,128)}, f32[128,128]{1,0:T(8,128)S(1)}, u32[]{:S(2)}) copy-start(f32[128,128]{1,0:T(8,128)S(1)} %collective-permute-done.5.refs_10_) | copy-start | bytes 196612
  24.5 0.7 copy-start
  24.5 0.8 copy-start.1
  28.0 60.4 %collective-permute-start.6 = (f32[1344,128]{1,0:T(8,128)}, f32[1344,128]{1,0:T(8,128)S(1)}, u32[]{:S(2)}, u32[]{:S(2)}) collective-permute-start(f32[1344,128]{1,0:T(8,128)} %get-tuple-element.55), channel_id=1, source_target_pairs={{0,8},{8,0},{16,24},{24,16},{1,9},{9,1},{17,25},{25,17},{2,10},{10... | collective-permute-start | bytes 2064392 | tf_op jit(solution)/shard_map/ppermute | solution.py:64
  28.1 63.5 %collective-permute-start.7 = (f32[1344,128]{1,0:T(8,128)}, f32[1344,128]{1,0:T(8,128)S(1)}, u32[]{:S(2)}, u32[]{:S(2)}) collective-permute-start(f32[1344,128]{1,0:T(8,128)} %get-tuple-element.56), channel_id=1, source_target_pairs={{8,16},{16,8},{9,17},{17,9},{10,18},{18,10},{11,19},{19,11},{12,20... | collective-permute-start | bytes 2064392 | tf_op jit(solution)/shard_map/ppermute | solution.py:64
  81.0 7.4 %collective-permute-start.9 = (f32[128,128]{1,0:T(8,128)}, f32[128,128]{1,0:T(8,128)S(1)}, u32[]{:S(2)}, u32[]{:S(2)}) collective-permute-start(f32[128,128]{1,0:T(8,128)} %get-tuple-element.60), channel_id=1, source_target_pairs={{1,2},{2,1},{3,4},{4,3},{5,6},{6,5},{9,10},{10,9},{11,12},{12,11},... | collective-permute-start | bytes 196616 | tf_op jit(solution)/shard_map/ppermute | solution.py:64
  86.3 19.9 %collective-permute-start.10 = (f32[128,128]{1,0:T(8,128)}, f32[128,128]{1,0:T(8,128)S(1)}, u32[]{:S(2)}, u32[]{:S(2)}) collective-permute-start(f32[128,128]{1,0:T(8,128)} %get-tuple-element.61), channel_id=1, source_target_pairs={{0,2},{1,3},{2,0},{3,1},{4,6},{5,7},{6,4},{7,5},{8,10},{9,11},{10,... | collective-permute-start | bytes 196616 | tf_op jit(solution)/shard_map/ppermute | solution.py:64
  86.4 19.9 %collective-permute-start.11 = (f32[128,128]{1,0:T(8,128)}, f32[128,128]{1,0:T(8,128)S(1)}, u32[]{:S(2)}, u32[]{:S(2)}) collective-permute-start(f32[128,128]{1,0:T(8,128)} %get-tuple-element.62), channel_id=1, source_target_pairs={{2,4},{3,5},{4,2},{5,3},{10,12},{11,13},{12,10},{13,11},{18,20},{1... | collective-permute-start | bytes 196616 | tf_op jit(solution)/shard_map/ppermute | solution.py:64
  88.4 17.8 %copy-start.4 = (f32[128,128]{1,0:T(8,128)}, f32[128,128]{1,0:T(8,128)S(1)}, u32[]{:S(2)}) copy-start(f32[128,128]{1,0:T(8,128)S(1)} %collective-permute-done.9) | copy-start | bytes 196612
  88.4 17.8 %collective-permute-start.12 = (f32[128,128]{1,0:T(8,128)}, f32[128,128]{1,0:T(8,128)S(1)}, u32[]{:S(2)}, u32[]{:S(2)}) collective-permute-start(f32[128,128]{1,0:T(8,128)} %get-tuple-element.63), channel_id=1, source_target_pairs={{0,8},{8,0},{16,24},{24,16},{1,9},{9,1},{17,25},{25,17},{2,10},{10... | collective-permute-start | bytes 196616 | tf_op jit(solution)/shard_map/ppermute | solution.py:64
  88.4 4.1 %copy-start.2 = (f32[1344,128]{1,0:T(8,128)}, f32[1344,128]{1,0:T(8,128)S(1)}, u32[]{:S(2)}) copy-start(f32[1344,128]{1,0:T(8,128)S(1)} %collective-permute-done.6.refs_8_) | copy-start | bytes 2064388
  88.4 17.8 %collective-permute-start.13 = (f32[128,128]{1,0:T(8,128)}, f32[128,128]{1,0:T(8,128)S(1)}, u32[]{:S(2)}, u32[]{:S(2)}) collective-permute-start(f32[128,128]{1,0:T(8,128)} %get-tuple-element.64), channel_id=1, source_target_pairs={{8,16},{16,8},{9,17},{17,9},{10,18},{18,10},{11,19},{19,11},{12,20... | collective-permute-start | bytes 196616 | tf_op jit(solution)/shard_map/ppermute | solution.py:64
  91.6 0.9 copy-start.3
  91.6 14.7 %collective-permute-start.8 = (f32[128,128]{1,0:T(8,128)}, f32[128,128]{1,0:T(8,128)S(1)}, u32[]{:S(2)}, u32[]{:S(2)}) collective-permute-start(f32[128,128]{1,0:T(8,128)} %get-tuple-element.59), channel_id=1, source_target_pairs={{0,1},{1,0},{2,3},{3,2},{4,5},{5,4},{6,7},{7,6},{8,9},{9,8},{10,11... | collective-permute-start | bytes 196616 | tf_op jit(solution)/shard_map/ppermute | solution.py:64
  106.2 0.6 copy-start.5
  106.2 0.6 copy-start.7
  106.2 0.6 copy-start.10
  106.3 0.7 copy-start.12
  106.3 0.7 copy-start.13

commit v15 on v14

--- a/solution.py
+++ b/solution.py
@@ -351,7 +351,7 @@
     source_ref,
     *refs,
 ):
-    out_refs, scratch = (refs[:-8], refs[-8:])
+    out_refs, edge_refs, scratch = (refs[:-10], refs[-10:-8], refs[-8:])
     sum_ref, deposit_ref, position_ref, charge_ref, ion_ref, start_ref, screen_ref, sems = scratch
     copies = start_copies(
         (
@@ -439,31 +439,17 @@
             source_ref[index, :, lanes] = (
                 ion_ref[index, :, lanes] + deposit_ref[first : first + cells_y, :]
             ) * inverse_ref[index, :, lanes]
-    def fill_rows(out_ref, after):
-        for index in range(cells_x):
-            base = slots * 4 + index * 32
-            offset = 0
-            for field_ref, width in zip(
-                (start_ref, inverse_ref, source_ref, ion_ref), HALO_WIDTHS, strict=True
-            ):
-                first = cells_y - width if after else 0
-                rows = field_ref[index, first : first + width, :]
+    edge = 0
+    for field_ref, width in zip(
+        (start_ref, inverse_ref, source_ref, ion_ref), HALO_WIDTHS, strict=True
+    ):
+        for step in range(width):
+            for phase, edge_ref in enumerate(edge_refs):
+                last = ups[2] if phase == 0 else 1 - ups[2]
+                plane = field_ref[last * (cells_x - width) + step]
                 for half in range(2):
-                    out_ref[base + 16 * half + offset : base + 16 * half + offset + width, :] = (
-                        rows[:, 128 * half : 128 * half + 128]
-                    )
-                offset += width
-            for half in range(2):
-                out_ref[base + 16 * half + offset : base + 16 * half + 16, :] = jnp.zeros(
-                    (16 - offset, 128), jnp.float32
-                )
-
-    for up in range(2):
-
-        @pl.when(ups[0] == up)
-        def _(up=up):
-            fill_rows(out_refs[1], up == 1)
-            fill_rows(out_refs[2], up == 0)
+                    edge_ref[2 * edge + half] = plane[:, 128 * half : 128 * half + 128]
+            edge += 1
 
 
 def prepare(
@@ -481,11 +467,9 @@
 ):
     clusters = charges.shape[0]
     directions, slots = send_index.shape
-    cells_x = ions.shape[0]
+    cells_y = ions.shape[1]
     smem = pl.BlockSpec(memory_space=pltpu.SMEM)
     vmem = pl.BlockSpec(memory_space=pltpu.VMEM)
-    rows = [slots * 4] * directions
-    rows[1] = rows[2] = slots * 4 + cells_x * 32
     return pl.pallas_call(
         prepare_kernel,
         out_shape=(
@@ -494,10 +478,11 @@
             jax.ShapeDtypeStruct((clusters, 128), jnp.float32),
             jax.ShapeDtypeStruct(ions.shape, jnp.float32),
             jax.ShapeDtypeStruct(ions.shape, jnp.float32),
-            *[jax.ShapeDtypeStruct((count, 128), jnp.float32) for count in rows],
+            *[jax.ShapeDtypeStruct((slots * 4, 128), jnp.float32)] * directions,
+            *[jax.ShapeDtypeStruct((2 * sum(HALO_WIDTHS), cells_y, 128), jnp.float32)] * 2,
         ),
         in_specs=[smem] * 4 + [vmem] * 3 + [pl.BlockSpec(memory_space=pltpu.HBM)] * 5,
-        out_specs=(vmem,) * (5 + directions),
+        out_specs=(vmem,) * (7 + directions),
         scratch_shapes=[
             pltpu.VMEM((clusters, 128), jnp.float32),
             pltpu.VMEM((ions.size // 128, 128), jnp.float32),
@@ -529,72 +514,78 @@
     return (cells_y + 2 * DEPTH + 7) // 8 * 8
 
 
-def fill_lines(target_ref, plane, field, field_ref, index, rim_ref, source):
-    cells_y = field_ref.shape[1]
-    width = HALO_WIDTHS[field]
-    for half in range(2):
-        at = (plane * 2 + half) * line_rows(cells_y) + DEPTH
-        first = source * 32 + 16 * half + sum(HALO_WIDTHS[:field])
-        target_ref[pl.ds(at - width, width), :] = rim_ref[pl.ds(first, width), :]
-        target_ref[pl.ds(at, cells_y), :] = field_ref[index, :, 128 * half : 128 * half + 128]
-        first = first + rim_ref.shape[0] // 2
-        target_ref[pl.ds(at + cells_y, width), :] = rim_ref[pl.ds(first, width), :]
-
-
-def planes_kernel(base, *refs):
-    field_refs, rims, out_refs = (refs[:4], refs[4:6], refs[6:8])
-    edge_refs, rim_ref, sems = (refs[8:12], refs[12], refs[13])
-    cells_x = field_refs[0].shape[0]
-    size = cells_x * 32
+def pack_rows_kernel(*refs):
+    field_hbms, edge_hbms, reaction_hbms, out_refs = (refs[:4], refs[4:6], refs[6:8], refs[8:10])
+    near_refs, edge_refs, sems = (refs[10:14], refs[14:16], refs[16])
+    cells_x, cells_y, _ = field_hbms[0].shape
+    base = reaction_hbms[0].shape[0]
     ups = upward()
     moves = [
-        (rim.at[base : base + size], rim_ref.at[pl.ds(pl.multiple_of(side * size, size), size)])
-        for rim, side in zip(rims, (ups[0], 1 - ups[0]), strict=True)
+        (reaction, out_ref.at[0:base])
+        for reaction, out_ref in zip(reaction_hbms, out_refs, strict=True)
     ]
-    for field_ref, edge_ref, width in zip(field_refs, edge_refs, HALO_WIDTHS, strict=True):
-        moves.append((field_ref.at[0:width], edge_ref.at[0:width]))
-        moves.append((field_ref.at[cells_x - width : cells_x], edge_ref.at[width : 2 * width]))
+    for source, target in zip(field_hbms + edge_hbms, near_refs + edge_refs, strict=True):
+        moves.append((source.at[:, 0:8], target.at[0]))
+        moves.append((source.at[:, cells_y - 8 : cells_y], target.at[1]))
     for copy in start_copies(moves, sems):
         copy.wait()
-    for field, width in enumerate(HALO_WIDTHS):
-        plane = sum(HALO_WIDTHS[:field])
-
-        def fill(step, _, field=field, plane=plane, width=width):
-            for phase, out_ref in enumerate(out_refs):
-                last = ups[2] if phase == 0 else 1 - ups[2]
-                source = last * (cells_x - width) + step
-                fill_lines(
-                    out_ref,
-                    plane + step,
-                    field,
-                    edge_refs[field],
-                    last * width + step,
-                    rim_ref,
-                    source,
-                )
-            return 0
-
-        lax.fori_loop(0, width, fill, 0)
-
-
-def planes(fields, first, second, base):
+
+    def fill(out_ref, after):
+        for field, width in enumerate(HALO_WIDTHS):
+            offset = sum(HALO_WIDTHS[:field])
+            rows = slice(8 - width, 8) if after else slice(0, width)
+            for index in range(cells_x):
+                value = near_refs[field][after, index, rows, :]
+                for half in range(2):
+                    at = base + ((DEPTH + index) * 2 + half) * 16 + offset
+                    out_ref[at : at + width, :] = value[:, 128 * half : 128 * half + 128]
+            if width == 1:
+                continue
+            for phase, edge_ref in enumerate(edge_refs):
+                higher = ups[2] if phase == 0 else 1 - ups[2]
+                for step in range(width):
+                    plane = (DEPTH - width) + higher * (cells_x + width) + step
+                    for half in range(2):
+                        at = pl.ds(base + (plane * 2 + half) * 16 + offset, width)
+                        out_ref[at, :] = edge_ref[after, 2 * (offset + step) + half, rows, :]
+
+    for up in range(2):
+
+        @pl.when(ups[0] == up)
+        def _(up=up):
+            fill(out_refs[0], up)
+            fill(out_refs[1], 1 - up)
+
+
+def pack_rows(fields, edges, reactions):
     vmem = pl.BlockSpec(memory_space=pltpu.VMEM)
-    cells_x, cells_y, cells_z = fields[0].shape
-    rows = sum(HALO_WIDTHS) * 2 * line_rows(cells_y)
+    cells_x, _, cells_z = fields[0].shape
+    rows = reactions[0].shape[0] + (cells_x + 2 * DEPTH) * 32
     shape = jax.ShapeDtypeStruct((rows, 128), jnp.float32)
     return pl.pallas_call(
-        functools.partial(planes_kernel, base),
+        pack_rows_kernel,
         out_shape=(shape, shape),
-        in_specs=[pl.BlockSpec(memory_space=pltpu.HBM)] * 6,
+        in_specs=[pl.BlockSpec(memory_space=pltpu.HBM)] * 8,
         out_specs=(vmem, vmem),
         scratch_shapes=[
-            *[pltpu.VMEM((2 * width, cells_y, cells_z), jnp.float32) for width in HALO_WIDTHS],
-            pltpu.VMEM((cells_x * 64, 128), jnp.float32),
-            pltpu.SemaphoreType.DMA((2 + 2 * len(HALO_WIDTHS),)),
+            *[pltpu.VMEM((2, cells_x, 8, cells_z), jnp.float32)] * 4,
+            *[pltpu.VMEM((2, edges[0].shape[0], 8, 128), jnp.float32)] * 2,
+            pltpu.SemaphoreType.DMA((14,)),
         ],
         compiler_params=pltpu.CompilerParams(vmem_limit_bytes=VMEM_LIMIT),
-        name="planes",
-    )(*fields, first, second)
+        name="pack_rows",
+    )(*fields, *edges, *reactions)
+
+
+def fill_line(target_ref, plane, half, field, value, rim_ref):
+    cells_y = value.shape[0]
+    width = HALO_WIDTHS[field]
+    at = (plane * 2 + half) * line_rows(cells_y) + DEPTH
+    target_ref[pl.ds(at, cells_y), :] = value
+    first = (plane * 2 + half) * 16 + sum(HALO_WIDTHS[:field])
+    target_ref[pl.ds(at - width, width), :] = rim_ref[pl.ds(first, width), :]
+    first = first + rim_ref.shape[0] // 2
+    target_ref[pl.ds(at + cells_y, width), :] = rim_ref[pl.ds(first, width), :]
 
 
 def face_flux(pot_low, pot_high, ion_low, ion_high):
@@ -608,45 +599,52 @@
 
 def grid_kernel(base, *refs):
     cell_ref, masked_hbm = refs[:2]
-    hbm_refs, plane_hbms = (refs[2:6], refs[8:10])
+    hbm_refs, edge_hbms = (refs[2:6], refs[8:10])
     potential_ref, next_ref, force_ref = refs[10:13]
     start_ref, inverse_ref, source_ref, ion_ref = refs[13:17]
     updates, resids, final_ref, pick_refs = (refs[17:20], refs[20:22], refs[22], refs[23:26])
     rim_ref, field_refs, masked_ref, sems = (refs[26], refs[27:31], refs[31], refs[32])
+    edge_refs = refs[33:35]
     cells_x, cells_y, _ = field_refs[0].shape
     rows = line_rows(cells_y)
     inner = cells_y + 2 * DEPTH - 2
     clusters = masked_ref.shape[0]
     ups = upward()
-    size = cells_x * 32
+    size = (cells_x + 2 * DEPTH) * 32
     moves = [
         (rim.at[base : base + size], rim_ref.at[pl.ds(pl.multiple_of(side * size, size), size)])
         for rim, side in zip(refs[6:8], (ups[0], 1 - ups[0]), strict=True)
     ]
     moves += zip(hbm_refs, field_refs, strict=True)
+    moves += zip(edge_hbms, edge_refs, strict=True)
     moves.append((masked_hbm, masked_ref))
-    near = len(moves)
-    for field, target_ref in enumerate((start_ref, inverse_ref, source_ref, ion_ref)):
+    for copy in start_copies(moves, sems):
+        copy.wait()
+    extended = (start_ref, inverse_ref, source_ref, ion_ref)
+
+    def fill(index, _):
+        for field, target_ref in enumerate(extended):
+            plane = field_refs[field][index]
+            for half in range(2):
+                value = plane[:, 128 * half : 128 * half + 128]
+                fill_line(target_ref, DEPTH + index, half, field, value, rim_ref)
+        return 0
+
+    lax.fori_loop(0, cells_x, fill, 0, unroll=2)
+    for field, target_ref in enumerate(extended):
         width = HALO_WIDTHS[field]
-        size = width * 2 * rows
-        first = sum(HALO_WIDTHS[:field]) * 2 * rows
-        for phase, plane_ref in enumerate(plane_hbms):
+        for phase, edge_ref in enumerate(edge_refs):
             higher = ups[2] if phase == 0 else 1 - ups[2]
-            plane = (DEPTH - width) + higher * (cells_x + width)
-            at = pl.ds(pl.multiple_of(plane * 2 * rows, 2 * rows), size)
-            moves.append((plane_ref.at[first : first + size], target_ref.at[at]))
-    copies = start_copies(moves, sems)
-    for copy in copies[:near]:
-        copy.wait()
-
-    def fill(index, _):
-        for field, target_ref in enumerate((start_ref, inverse_ref, source_ref, ion_ref)):
-            fill_lines(target_ref, DEPTH + index, field, field_refs[field], index, rim_ref, index)
-        return 0
-
-    lax.fori_loop(0, cells_x, fill, 0, unroll=2)
-    for copy in copies[near:]:
-        copy.wait()
+
+            def fill_edge(step, _, field=field, target_ref=target_ref, edge_ref=edge_ref):
+                width = HALO_WIDTHS[field]
+                plane = (DEPTH - width) + higher * (cells_x + width) + step
+                for half in range(2):
+                    value = edge_ref[2 * (sum(HALO_WIDTHS[:field]) + step) + half]
+                    fill_line(target_ref, plane, half, field, value, rim_ref)
+                return 0
+
+            lax.fori_loop(0, width, fill_edge, 0, unroll=True)
 
     def beyond(values):
         lane = lax.broadcasted_iota(jnp.int32, values[0].shape, 1)
@@ -801,9 +799,10 @@
         out_specs=(vmem,) * 3,
         scratch_shapes=[pltpu.VMEM(block, jnp.float32)] * 10
         + [pltpu.VMEM((clusters, 128), jnp.float32)] * 3
-        + [pltpu.VMEM((cells_x * 64, 128), jnp.float32)]
+        + [pltpu.VMEM(((cells_x + 2 * DEPTH) * 64, 128), jnp.float32)]
         + [pltpu.VMEM(field.shape, jnp.float32) for field in fields]
-        + [pltpu.VMEM(masked.shape, jnp.float32), pltpu.SemaphoreType.DMA((15,))],
+        + [pltpu.VMEM(masked.shape, jnp.float32), pltpu.SemaphoreType.DMA((9,))]
+        + [pltpu.VMEM(edge.shape, jnp.float32) for edge in edges],
         compiler_params=pltpu.CompilerParams(vmem_limit_bytes=VMEM_LIMIT),
         cost_estimate=pl.CostEstimate(
             flops=block[0] * block[1] * 100, bytes_accessed=8 << 20, transcendentals=0
@@ -816,7 +815,13 @@
     fetched = len(SWAPS) + 3
     out_ref, sum_ref = refs[fetched : fetched + 2]
     own_ref, field_ref, *back_refs = refs[fetched + 2 : -1]
-    copies = start_copies(zip(refs[:fetched], refs[fetched + 2 : -1], strict=True), refs[-1])
+    copies = start_copies(
+        [
+            (source.at[0 : target.shape[0]], target)
+            for source, target in zip(refs[:fetched], refs[fetched + 2 : -1], strict=True)
+        ],
+        refs[-1],
+    )
     for copy in copies:
         copy.wait()
     clusters = own_ref.shape[0]
@@ -851,7 +856,8 @@
         in_specs=[smem] + [pl.BlockSpec(memory_space=pltpu.HBM)] * (2 + len(backs)),
         out_specs=vmem,
         scratch_shapes=[
-            *[pltpu.VMEM(part.shape, jnp.float32) for part in (own, own, field, *backs)],
+            *[pltpu.VMEM(part.shape, jnp.float32) for part in (own, own, field)],
+            *[pltpu.VMEM((send_index.shape[1], 4, 128), jnp.float32)] * len(backs),
             pltpu.SemaphoreType.DMA((2 + len(backs),)),
         ],
         compiler_params=pltpu.CompilerParams(vmem_limit_bytes=VMEM_LIMIT),
@@ -890,15 +896,14 @@
         potential_prev,
         screening,
     )
+    edges = messages[len(SWAPS) :]
     arrived = [local] + [
-        swapped(message, *swap) for message, swap in zip(messages, SWAPS, strict=True)
+        swapped(message, *swap)
+        for message, swap in zip(messages[: len(SWAPS)], SWAPS, strict=True)
     ]
     fields = (potential_prev, inverse, source, ion_density)
-    arrived = lax.optimization_barrier(arrived)
-    rims = arrived[1:3]
-    edges = [
-        swapped(edge, "grp", 1, phase) for phase, edge in enumerate(planes(fields, *rims, base))
-    ]
+    arrived, edges = lax.optimization_barrier((arrived, edges))
+    edges = [swapped(edge, "grp", 1, phase) for phase, edge in enumerate(edges)]
     own_force, *reactions = pair_forces(
         pair_local,
         other_rows.reshape(-1),
@@ -906,15 +911,20 @@
         arrived,
         slots,
     )
-    backs = [reactions[0]] + [
-        swapped(reaction, *swap) for reaction, swap in zip(reactions[1:], SWAPS, strict=True)
+    local_back, *reactions = reactions
+    rims = pack_rows(fields, edges, reactions[:2])
+    backs = [
+        swapped(reaction, *swap)
+        for reaction, swap in zip((*rims, *reactions[2:]), SWAPS, strict=True)
     ]
-    potential, ion_next, field_force = grid_step(cluster_cell, masked, fields, rims, edges, base)
+    potential, ion_next, field_force = grid_step(
+        cluster_cell, masked, fields, backs[:2], edges, base
+    )
     forces = gather_forces(
         send_index,
         own_force.reshape(clusters, 4, psize),
         field_force.reshape(clusters, 4, psize),
-        [back.reshape(slots, 4, psize) for back in backs],
+        [back.reshape(-1, 4, psize) for back in (local_back, *backs)],
     )
     return (forces, potential, ion_next)
 

time: 112 us -> 114 us (1.018); the launches traced: 111 us -> 112 us
    unnamed x28 -> x36, local copies, waits for them, and re-layouts: 1.53 us -> 2.34 us
  transfers between devices with their start and end apart: 14 -> 14, of which waited for: 3 -> 2; matrix products, arithmetic and copies ran while one was open for 0% -> 0% of each run, Pallas kernels for 58% -> 58%
where the time goes in v15:
time: 114 us; the launch traced here: 112 us
  Pallas kernels  77.8 us (68%)
  starting transfers between devices  25.4 us (22%)
  waiting for transfers between devices  5.18 us (5%)
  local copies, waits for them, and re-layouts  2.34 us (2%)
    pallas_call x1, Pallas kernels, pair_forces(): pl.pallas_call(pair_kernel, out_shape=(jax.ShapeDtypeStruct(own.shape, jn...  50.6 us
    ppermute x14, starting transfers between devices, swapped(): return lax.ppermute(shard, axis, pairs)  25.4 us
    pallas_call x1, Pallas kernels, grid_step(): pl.pallas_call(functools.partial(grid_kernel, base), out_shape=(jax.Shape...  13.9 us
    pallas_call x1, Pallas kernels, prepare(): pl.pallas_call(prepare_kernel, out_shape=(jax.ShapeDtypeStruct(pair_dir.s...  6.34 us
    ppermute x14, waiting for transfers between devices, swapped(): return lax.ppermute(shard, axis, pairs)  5.18 us
    pallas_call x1, Pallas kernels, gather_forces(): pl.pallas_call(gather_forces_kernel, out_shape=jax.ShapeDtypeStruct((3, c...  4.31 us
    pallas_call x1, Pallas kernels, pack_rows(): pl.pallas_call(pack_rows_kernel, out_shape=(shape, shape), in_specs=[pl.B...  2.71 us
    unnamed x36, local copies, waits for them, and re-layouts  2.34 us
  transfers between devices with their start and end apart: 14, of which 2 were waited for; matrix products, arithmetic and copies ran while one was open for 0% of the time, Pallas kernels for 58%

profile of v15, /device:TPU:13, one launch (start us, length us, event | category | flops | bytes accessed | tf_op | source)
XLA Modules:
  0.0 111.7 jit_solution(8748744636733033337)
XLA Ops:
  0.6 6.3 %prepare.1 = (s32[8,128]{1,0:T(8,128)}, f32[256,4,128]{2,1,0:T(4,128)}, f32[256,128]{1,0:T(8,128)}, f32[16,32,256]{2,1,0:T(8,128)}, f32[16,32,256]{2,1,0:T(8,128...) custom-call(s32[256]{0:T(256)} %fill_ref.1, ...), custom_call_target="tpu_custom_call" | custom-call | tf_op jit(solution)/shard_map/prepare/pallas_call | solution.py:473
  7.0 0.7 collective-permute-start
  7.7 3.1 %collective-permute-start.1 = (f32[128,128]{1,0:T(8,128)}, f32[128,128]{1,0:T(8,128)S(1)}, u32[]{:S(2)}, u32[]{:S(2)}) collective-permute-start(f32[128,128]{1,0:T(8,128)} %get-tuple-element.43), channel_id=1, source_target_pairs={{1,2},{2,1},{3,4},{4,3},{5,6},{6,5},{9,10},{10,9},{11,12},{12,11},... | collective-permute-start | bytes 196616 | tf_op jit(solution)/shard_map/ppermute | solution.py:64
  10.8 0.2 collective-permute-start.2
  11.1 3.0 %collective-permute-start.3 = (f32[128,128]{1,0:T(8,128)}, f32[128,128]{1,0:T(8,128)S(1)}, u32[]{:S(2)}, u32[]{:S(2)}) collective-permute-start(f32[128,128]{1,0:T(8,128)} %get-tuple-element.45), channel_id=1, source_target_pairs={{2,4},{3,5},{4,2},{5,3},{10,12},{11,13},{12,10},{13,11},{18,20},{1... | collective-permute-start | bytes 196616 | tf_op jit(solution)/shard_map/ppermute | solution.py:64
  14.1 1.3 %collective-permute-start.4 = (f32[128,128]{1,0:T(8,128)}, f32[128,128]{1,0:T(8,128)S(1)}, u32[]{:S(2)}, u32[]{:S(2)}) collective-permute-start(f32[128,128]{1,0:T(8,128)} %get-tuple-element.46), channel_id=1, source_target_pairs={{0,8},{8,0},{16,24},{24,16},{1,9},{9,1},{17,25},{25,17},{2,10},{10... | collective-permute-start | bytes 196616 | tf_op jit(solution)/shard_map/ppermute | solution.py:64
  15.4 0.0 collective-permute-done.refs_5_
  15.4 0.0 copy-start.8
  15.4 2.1 %collective-permute-start.5 = (f32[128,128]{1,0:T(8,128)}, f32[128,128]{1,0:T(8,128)S(1)}, u32[]{:S(2)}, u32[]{:S(2)}) collective-permute-start(f32[128,128]{1,0:T(8,128)} %get-tuple-element.47), channel_id=1, source_target_pairs={{8,16},{16,8},{9,17},{17,9},{10,18},{18,10},{11,19},{19,11},{12,20... | collective-permute-start | bytes 196616 | tf_op jit(solution)/shard_map/ppermute | solution.py:64
  17.5 0.0 collective-permute-done.1.refs_6_
  17.5 0.0 copy-start.9
  17.5 0.0 collective-permute-done.2.refs_7_
  17.5 0.0 copy-start.10
  17.5 0.0 collective-permute-done.3.refs_8_
  17.6 0.0 copy-start.11
  17.6 0.0 collective-permute-done.4.refs_9_
  17.6 0.0 copy-start.12
  17.6 3.9 %collective-permute-done.5.refs_10_ = f32[128,128]{1,0:T(8,128)S(1)} collective-permute-done((f32[128,128]{1,0:T(8,128)}, f32[128,128]{1,0:T(8,128)S(1)}, u32[]{:S(2)}, u32[]{:S(2)}) %collective-permute-start.5) | collective-permute-done | bytes 65568 | tf_op jit(solution)/shard_map/ppermute | solution.py:64
  21.5 0.0 copy-start.13
  21.5 0.0 collective-permute-start.6
  21.5 2.4 %collective-permute-start.7 = (f32[28,32,128]{2,1,0:T(8,128)}, f32[28,32,128]{2,1,0:T(8,128)S(1)}, u32[]{:S(2)}, u32[]{:S(2)}) collective-permute-start(f32[28,32,128]{2,1,0:T(8,128)} %get-tuple-element.62), channel_id=1, source_target_pairs={{8,16},{16,8},{9,17},{17,9},{10,18},{18,10},{11,19},{19,11},{12,20... | collective-permute-start | bytes 1376264 | tf_op jit(solution)/shard_map/ppermute | solution.py:64
  23.9 0.0 copy-done.8
  23.9 0.0 copy-done.9
  23.9 0.0 copy-done.10
  23.9 0.0 copy-done.11
  23.9 0.0 copy-done.12
  23.9 0.0 copy-done.13
  23.9 50.6 %pair_forces.1 = (f32[1024,128]{1,0:T(8,128)}, f32[128,128]{1,0:T(8,128)}, f32[128,128]{1,0:T(8,128)}, f32[128,128]{1,0:T(8,128)}, f32[128,128]{1,0:T(8,128)}, /...) custom-call(s32[1024]{0:T(1024)} %own_rows_ref.1, s32[1024]{0:T(1024)} %bitcast.29, ...), custom_call_target="tpu_custom_call" | custom-call | flops 335544320 | bytes 4194304 | tf_op jit(solution)/shard_map/pair_forces/pallas_call | solution.py:305
  74.5 0.0 collective-permute-done.6.refs_4_.refs_8_
  74.5 0.0 copy-start.2
  74.5 0.0 collective-permute-done.7.refs_5_.refs_9_
  74.5 0.0 copy-start.3
  74.6 0.7 copy-done.2
  75.3 0.1 copy-done.3
  75.5 0.0 copy-start.17
  75.5 2.7 %pack_rows.1 = (f32[960,128]{1,0:T(8,128)}, f32[960,128]{1,0:T(8,128)}) custom-call(f32[16,32,256]{2,1,0:T(8,128)} %refs_2_.2, f32[16,32,256]{2,1,0:T(8,128)} %get-tuple-element.59.refs_1_.refs_3_, f32[16,32,256]{2,1,0:T(8,128)} %get-tuple-element.60.refs_2_.refs_4_, f32[16,32,256]{2,1,0:T(8,128)} %refs_5_.1, f32[28,32,128]{2,1,0:T(8,128)} %copy-done.2, ...), custom_call_target="tpu_custom_call" | custom-call | tf_op jit(solution)/shard_map/pack_rows/pallas_call | solution.py:565
  78.2 2.7 %collective-permute-start.8 = (f32[960,128]{1,0:T(8,128)}, f32[960,128]{1,0:T(8,128)S(1)}, u32[]{:S(2)}, u32[]{:S(2)}) collective-permute-start(f32[960,128]{1,0:T(8,128)} %get-tuple-element.65), channel_id=1, source_target_pairs={{0,1},{1,0},{2,3},{3,2},{4,5},{5,4},{6,7},{7,6},{8,9},{9,8},{10,11... | collective-permute-start | bytes 1474568 | tf_op jit(solution)/shard_map/ppermute | solution.py:64
  80.9 1.9 %collective-permute-start.9 = (f32[960,128]{1,0:T(8,128)}, f32[960,128]{1,0:T(8,128)S(1)}, u32[]{:S(2)}, u32[]{:S(2)}) collective-permute-start(f32[960,128]{1,0:T(8,128)} %get-tuple-element.66), channel_id=1, source_target_pairs={{1,2},{2,1},{3,4},{4,3},{5,6},{6,5},{9,10},{10,9},{11,12},{12,11},... | collective-permute-start | bytes 1474568 | tf_op jit(solution)/shard_map/ppermute | solution.py:64
  82.8 0.0 copy-done.17
  82.8 1.4 %collective-permute-start.10 = (f32[128,128]{1,0:T(8,128)S(1)}, f32[128,128]{1,0:T(8,128)S(1)}, u32[]{:S(2)}, u32[]{:S(2)}) collective-permute-start(f32[128,128]{1,0:T(8,128)S(1)} %copy-done.17), channel_id=1, source_target_pairs={{0,2},{1,3},{2,0},{3,1},{4,6},{5,7},{6,4},{7,5},{8,10},{9,11},{10,... | collective-permute-start | bytes 196616 | tf_op jit(solution)/shard_map/ppermute | solution.py:64
  84.3 0.0 copy-done.16
  84.3 1.9 %collective-permute-start.11 = (f32[128,128]{1,0:T(8,128)S(1)}, f32[128,128]{1,0:T(8,128)S(1)}, u32[]{:S(2)}, u32[]{:S(2)}) collective-permute-start(f32[128,128]{1,0:T(8,128)S(1)} %copy-done.16), channel_id=1, source_target_pairs={{2,4},{3,5},{4,2},{5,3},{10,12},{11,13},{12,10},{13,11},{18,20},{1... | collective-permute-start | bytes 196616 | tf_op jit(solution)/shard_map/ppermute | solution.py:64
  86.2 0.0 copy-done.15
  86.2 0.5 collective-permute-start.12
  86.7 0.0 collective-permute-done.8.refs_6_
  86.7 0.0 copy-done.14
  86.7 4.0 %collective-permute-start.13 = (f32[128,128]{1,0:T(8,128)S(1)}, f32[128,128]{1,0:T(8,128)S(1)}, u32[]{:S(2)}, u32[]{:S(2)}) collective-permute-start(f32[128,128]{1,0:T(8,128)S(1)} %copy-done.14), channel_id=1, source_target_pairs={{8,16},{16,8},{9,17},{17,9},{10,18},{18,10},{11,19},{19,11},{12,20... | collective-permute-start | bytes 196616 | tf_op jit(solution)/shard_map/ppermute | solution.py:64
  90.7 1.2 %collective-permute-done.9.refs_7_ = f32[960,128]{1,0:T(8,128)S(1)} collective-permute-done((f32[960,128]{1,0:T(8,128)}, f32[960,128]{1,0:T(8,128)S(1)}, u32[]{:S(2)}, u32[]{:S(2)}) %collective-permute-start.9) | collective-permute-done | bytes 491552 | tf_op jit(solution)/shard_map/ppermute | solution.py:64
  92.0 0.0 copy-done
  92.0 0.8 copy-done.1
  92.7 13.9 %grid_step.1 = (f32[16,32,256]{2,1,0:T(8,128)}, f32[16,32,256]{2,1,0:T(8,128)}, f32[1024,128]{1,0:T(8,128)}) custom-call(s32[256]{0:T(256)} %refs_0_.4, f32[256,128]{1,0:T(8,128)} %get-tuple-element.58.refs_1_, f32[16,32,256]{2,1,0:T(8,128)} %refs_2_.2, f32[16,32,256]{2,1,0:T(8,128)} %get-tuple-element.59.refs_1_.refs_3_, ...), custom_call_target="tpu_custom_call" | custom-call | flops 31948800 | bytes 8388608 | tf_op jit(solution)/shard_map/grid_step/pallas_call | solution.py:791
  106.7 0.0 collective-permute-done.10
  106.7 0.0 copy-start.4
  106.7 0.0 collective-permute-done.11
  106.7 0.0 copy-start.5
  106.7 0.0 collective-permute-done.12
  106.7 0.0 copy-start.6
  106.7 0.0 collective-permute-done.13
  106.7 0.0 copy-start.7
  106.7 0.5 copy-done.4
  107.3 0.0 copy-done.5
  107.3 0.0 copy-done.6
  107.4 0.0 copy-done.7
  107.4 4.3 %gather_forces.1 = f32[3,32768]{1,0:T(4,128)} custom-call(s32[7,32]{1,0:T(8,128)} %send_index_ref.3, f32[256,4,128]{2,1,0:T(4,128)} %bitcast.17, f32[256,4,128]{2,1,0:T(4,128)} %bitcast.19, f32[32,4,128]{2,1,0:T(4,128)} %bitcast.21, f32[240,4,128]{2,1,0:T(4,128)} %bitcast.15, f32[240,4,128]{2,1,0:T(4,128)} %bitcast.16, f32[32,4,128]{2,1,0:T(4,128)} %bitcast.22, ...), custom_call_target="tpu_custom_call" | custom-call | tf_op jit(solution)/shard_map/gather_forces/pallas_call | solution.py:853
  (5 shorter events, 0.0 us)
Async XLA Ops:
  7.0 8.4 %collective-permute-start = (f32[128,128]{1,0:T(8,128)}, f32[128,128]{1,0:T(8,128)S(1)}, u32[]{:S(2)}, u32[]{:S(2)}) collective-permute-start(f32[128,128]{1,0:T(8,128)} %get-tuple-element.42), channel_id=1, source_target_pairs={{0,1},{1,0},{2,3},{3,2},{4,5},{5,4},{6,7},{7,6},{8,9},{9,8},{10,11... | collective-permute-start | bytes 196616 | tf_op jit(solution)/shard_map/ppermute | solution.py:64
  7.7 9.8 %collective-permute-start.1 = (f32[128,128]{1,0:T(8,128)}, f32[128,128]{1,0:T(8,128)S(1)}, u32[]{:S(2)}, u32[]{:S(2)}) collective-permute-start(f32[128,128]{1,0:T(8,128)} %get-tuple-element.43), channel_id=1, source_target_pairs={{1,2},{2,1},{3,4},{4,3},{5,6},{6,5},{9,10},{10,9},{11,12},{12,11},... | collective-permute-start | bytes 196616 | tf_op jit(solution)/shard_map/ppermute | solution.py:64
  10.8 6.7 %collective-permute-start.2 = (f32[128,128]{1,0:T(8,128)}, f32[128,128]{1,0:T(8,128)S(1)}, u32[]{:S(2)}, u32[]{:S(2)}) collective-permute-start(f32[128,128]{1,0:T(8,128)} %get-tuple-element.44), channel_id=1, source_target_pairs={{0,2},{1,3},{2,0},{3,1},{4,6},{5,7},{6,4},{7,5},{8,10},{9,11},{10,... | collective-permute-start | bytes 196616 | tf_op jit(solution)/shard_map/ppermute | solution.py:64
  11.1 6.5 %collective-permute-start.3 = (f32[128,128]{1,0:T(8,128)}, f32[128,128]{1,0:T(8,128)S(1)}, u32[]{:S(2)}, u32[]{:S(2)}) collective-permute-start(f32[128,128]{1,0:T(8,128)} %get-tuple-element.45), channel_id=1, source_target_pairs={{2,4},{3,5},{4,2},{5,3},{10,12},{11,13},{12,10},{13,11},{18,20},{1... | collective-permute-start | bytes 196616 | tf_op jit(solution)/shard_map/ppermute | solution.py:64
  14.1 3.4 %collective-permute-start.4 = (f32[128,128]{1,0:T(8,128)}, f32[128,128]{1,0:T(8,128)S(1)}, u32[]{:S(2)}, u32[]{:S(2)}) collective-permute-start(f32[128,128]{1,0:T(8,128)} %get-tuple-element.46), channel_id=1, source_target_pairs={{0,8},{8,0},{16,24},{24,16},{1,9},{9,1},{17,25},{25,17},{2,10},{10... | collective-permute-start | bytes 196616 | tf_op jit(solution)/shard_map/ppermute | solution.py:64
  15.4 8.5 %copy-start.8 = (f32[128,128]{1,0:T(8,128)}, f32[128,128]{1,0:T(8,128)S(1)}, u32[]{:S(2)}) copy-start(f32[128,128]{1,0:T(8,128)S(1)} %collective-permute-done.refs_5_) | copy-start | bytes 196612
  15.4 6.1 %collective-permute-start.5 = (f32[128,128]{1,0:T(8,128)}, f32[128,128]{1,0:T(8,128)S(1)}, u32[]{:S(2)}, u32[]{:S(2)}) collective-permute-start(f32[128,128]{1,0:T(8,128)} %get-tuple-element.47), channel_id=1, source_target_pairs={{8,16},{16,8},{9,17},{17,9},{10,18},{18,10},{11,19},{19,11},{12,20... | collective-permute-start | bytes 196616 | tf_op jit(solution)/shard_map/ppermute | solution.py:64
  17.5 6.4 %copy-start.9 = (f32[128,128]{1,0:T(8,128)}, f32[128,128]{1,0:T(8,128)S(1)}, u32[]{:S(2)}) copy-start(f32[128,128]{1,0:T(8,128)S(1)} %collective-permute-done.1.refs_6_) | copy-start | bytes 196612
  17.5 6.4 %copy-start.10 = (f32[128,128]{1,0:T(8,128)}, f32[128,128]{1,0:T(8,128)S(1)}, u32[]{:S(2)}) copy-start(f32[128,128]{1,0:T(8,128)S(1)} %collective-permute-done.2.refs_7_) | copy-start | bytes 196612
  17.6 6.4 %copy-start.11 = (f32[128,128]{1,0:T(8,128)}, f32[128,128]{1,0:T(8,128)S(1)}, u32[]{:S(2)}) copy-start(f32[128,128]{1,0:T(8,128)S(1)} %collective-permute-done.3.refs_8_) | copy-start | bytes 196612
  17.6 6.3 %copy-start.12 = (f32[128,128]{1,0:T(8,128)}, f32[128,128]{1,0:T(8,128)S(1)}, u32[]{:S(2)}) copy-start(f32[128,128]{1,0:T(8,128)S(1)} %collective-permute-done.4.refs_9_) | copy-start | bytes 196612
  21.5 2.4 %copy-start.13 = (f32[128,128]{1,0:T(8,128)}, f32[128,128]{1,0:T(8,128)S(1)}, u32[]{:S(2)}) copy-start(f32[128,128]{1,0:T(8,128)S(1)} %collective-permute-done.5.refs_10_) | copy-start | bytes 196612
  21.5 53.0 %collective-permute-start.6 = (f32[28,32,128]{2,1,0:T(8,128)}, f32[28,32,128]{2,1,0:T(8,128)S(1)}, u32[]{:S(2)}, u32[]{:S(2)}) collective-permute-start(f32[28,32,128]{2,1,0:T(8,128)} %get-tuple-element.61), channel_id=1, source_target_pairs={{0,8},{8,0},{16,24},{24,16},{1,9},{9,1},{17,25},{25,17},{2,10},{10... | collective-permute-start | bytes 1376264 | tf_op jit(solution)/shard_map/ppermute | solution.py:64
  21.5 53.0 %collective-permute-start.7 = (f32[28,32,128]{2,1,0:T(8,128)}, f32[28,32,128]{2,1,0:T(8,128)S(1)}, u32[]{:S(2)}, u32[]{:S(2)}) collective-permute-start(f32[28,32,128]{2,1,0:T(8,128)} %get-tuple-element.62), channel_id=1, source_target_pairs={{8,16},{16,8},{9,17},{17,9},{10,18},{18,10},{11,19},{19,11},{12,20... | collective-permute-start | bytes 1376264 | tf_op jit(solution)/shard_map/ppermute | solution.py:64
  74.5 0.8 copy-start.2
  74.5 0.9 copy-start.3
  75.5 7.4 %copy-start.17 = (f32[128,128]{1,0:T(8,128)S(1)}, f32[128,128]{1,0:T(8,128)}, u32[]{:S(2)}) copy-start(f32[128,128]{1,0:T(8,128)} %get-tuple-element.69) | copy-start | bytes 196612
  75.5 8.8 %copy-start.16 = (f32[128,128]{1,0:T(8,128)S(1)}, f32[128,128]{1,0:T(8,128)}, u32[]{:S(2)}) copy-start(f32[128,128]{1,0:T(8,128)} %get-tuple-element.70) | copy-start | bytes 196612
  75.5 10.7 %copy-start.15 = (f32[128,128]{1,0:T(8,128)S(1)}, f32[128,128]{1,0:T(8,128)}, u32[]{:S(2)}) copy-start(f32[128,128]{1,0:T(8,128)} %get-tuple-element.71) | copy-start | bytes 196612
  75.5 11.2 %copy-start.14 = (f32[128,128]{1,0:T(8,128)S(1)}, f32[128,128]{1,0:T(8,128)}, u32[]{:S(2)}) copy-start(f32[128,128]{1,0:T(8,128)} %get-tuple-element.72) | copy-start | bytes 196612
  78.2 8.5 %collective-permute-start.8 = (f32[960,128]{1,0:T(8,128)}, f32[960,128]{1,0:T(8,128)S(1)}, u32[]{:S(2)}, u32[]{:S(2)}) collective-permute-start(f32[960,128]{1,0:T(8,128)} %get-tuple-element.65), channel_id=1, source_target_pairs={{0,1},{1,0},{2,3},{3,2},{4,5},{5,4},{6,7},{7,6},{8,9},{9,8},{10,11... | collective-permute-start | bytes 1474568 | tf_op jit(solution)/shard_map/ppermute | solution.py:64
  80.9 11.0 %collective-permute-start.9 = (f32[960,128]{1,0:T(8,128)}, f32[960,128]{1,0:T(8,128)S(1)}, u32[]{:S(2)}, u32[]{:S(2)}) collective-permute-start(f32[960,128]{1,0:T(8,128)} %get-tuple-element.66), channel_id=1, source_target_pairs={{1,2},{2,1},{3,4},{4,3},{5,6},{6,5},{9,10},{10,9},{11,12},{12,11},... | collective-permute-start | bytes 1474568 | tf_op jit(solution)/shard_map/ppermute | solution.py:64
  82.8 23.8 %collective-permute-start.10 = (f32[128,128]{1,0:T(8,128)S(1)}, f32[128,128]{1,0:T(8,128)S(1)}, u32[]{:S(2)}, u32[]{:S(2)}) collective-permute-start(f32[128,128]{1,0:T(8,128)S(1)} %copy-done.17), channel_id=1, source_target_pairs={{0,2},{1,3},{2,0},{3,1},{4,6},{5,7},{6,4},{7,5},{8,10},{9,11},{10,... | collective-permute-start | bytes 196616 | tf_op jit(solution)/shard_map/ppermute | solution.py:64
  84.3 22.4 %collective-permute-start.11 = (f32[128,128]{1,0:T(8,128)S(1)}, f32[128,128]{1,0:T(8,128)S(1)}, u32[]{:S(2)}, u32[]{:S(2)}) collective-permute-start(f32[128,128]{1,0:T(8,128)S(1)} %copy-done.16), channel_id=1, source_target_pairs={{2,4},{3,5},{4,2},{5,3},{10,12},{11,13},{12,10},{13,11},{18,20},{1... | collective-permute-start | bytes 196616 | tf_op jit(solution)/shard_map/ppermute | solution.py:64
  86.2 20.5 %collective-permute-start.12 = (f32[128,128]{1,0:T(8,128)S(1)}, f32[128,128]{1,0:T(8,128)S(1)}, u32[]{:S(2)}, u32[]{:S(2)}) collective-permute-start(f32[128,128]{1,0:T(8,128)S(1)} %copy-done.15), channel_id=1, source_target_pairs={{0,8},{8,0},{16,24},{24,16},{1,9},{9,1},{17,25},{25,17},{2,10},{10... | collective-permute-start | bytes 196616 | tf_op jit(solution)/shard_map/ppermute | solution.py:64
  86.7 5.3 %copy-start = (f32[960,128]{1,0:T(8,128)}, f32[960,128]{1,0:T(8,128)S(1)}, u32[]{:S(2)}) copy-start(f32[960,128]{1,0:T(8,128)S(1)} %collective-permute-done.8.refs_6_) | copy-start | bytes 1474564
  86.7 20.0 %collective-permute-start.13 = (f32[128,128]{1,0:T(8,128)S(1)}, f32[128,128]{1,0:T(8,128)S(1)}, u32[]{:S(2)}, u32[]{:S(2)}) collective-permute-start(f32[128,128]{1,0:T(8,128)S(1)} %copy-done.14), channel_id=1, source_target_pairs={{8,16},{16,8},{9,17},{17,9},{10,18},{18,10},{11,19},{19,11},{12,20... | collective-permute-start | bytes 196616 | tf_op jit(solution)/shard_map/ppermute | solution.py:64
  92.0 0.8 copy-start.1
  106.7 0.6 copy-start.4
  106.7 0.6 copy-start.5
  106.7 0.6 copy-start.6
  106.7 0.6 copy-start.7

commit v16 on v15

--- a/solution.py
+++ b/solution.py
@@ -31,6 +31,7 @@
 
 
 VMEM_LIMIT = 60 * 1024 * 1024
+ROOMY_LIMIT = 48 * 1024 * 1024
 
 
 def start_copies(pairs, sems):
@@ -300,7 +301,7 @@
     pairs = own_rows.shape[0]
     smem = pl.BlockSpec(memory_space=pltpu.SMEM)
     vmem = pl.BlockSpec(memory_space=pltpu.VMEM)
-    hbm = pl.BlockSpec(memory_space=pltpu.HBM)
+    hbm = pl.BlockSpec(memory_space=pl.ANY)
     operands = (*selections(), own)
     return pl.pallas_call(
         pair_kernel,
@@ -323,7 +324,7 @@
             pltpu.VMEM((128, 128), jnp.float32),
             *[pltpu.VMEM((128 * UNROLL, 256), jnp.bfloat16)] * 2,
         ],
-        compiler_params=pltpu.CompilerParams(vmem_limit_bytes=VMEM_LIMIT),
+        compiler_params=pltpu.CompilerParams(vmem_limit_bytes=ROOMY_LIMIT),
         cost_estimate=pl.CostEstimate(
             flops=pairs * 128 * 128 * 20, bytes_accessed=4 * 1024 * 1024, transcendentals=0
         ),
@@ -333,43 +334,31 @@
 
 def prepare_kernel(
     fill_ref,
-    cell_ref,
     send_index_ref,
     send_count_ref,
-    cell_row_ref,
     pair_dir_ref,
     pair_slot_ref,
     position_hbm,
     charge_hbm,
-    ion_hbm,
-    start_hbm,
-    screen_hbm,
     row_ref,
     own_ref,
     masked_ref,
-    inverse_ref,
-    source_ref,
     *refs,
 ):
-    out_refs, edge_refs, scratch = (refs[:-10], refs[-10:-8], refs[-8:])
-    sum_ref, deposit_ref, position_ref, charge_ref, ion_ref, start_ref, screen_ref, sems = scratch
-    copies = start_copies(
-        (
-            (position_hbm, position_ref),
-            (charge_hbm, charge_ref),
-            (ion_hbm, ion_ref),
-            (start_hbm, start_ref),
-            (screen_hbm, screen_ref),
-        ),
-        sems,
-    )
-    copies[0].wait()
-    copies[1].wait()
+    out_refs, (position_ref, charge_ref, sems) = (refs[:-3], refs[-3:])
+    copies = start_copies(((position_hbm, position_ref), (charge_hbm, charge_ref)), sems)
     clusters = charge_ref.shape[0]
-    cells_x, cells_y, _ = ion_ref.shape
     slots = send_index_ref.shape[1]
     lane = lax.broadcasted_iota(jnp.int32, (1, 128), 1)
     row = lax.broadcasted_iota(jnp.int32, (4, 128), 0)
+    ups = upward()
+    direction = pair_dir_ref[...]
+    way = lax.shift_right_arithmetic(direction - 1, 1)
+    flip = jnp.where(way == 0, ups[0], jnp.where(way == 1, ups[1], ups[2]))
+    position = 1 + 2 * way + lax.bitwise_xor(lax.bitwise_and(direction - 1, 1), flip)
+    row_ref[...] = jnp.where(direction == 0, 0, position) * slots + pair_slot_ref[...]
+    for copy in copies:
+        copy.wait()
 
     def collect(step, _):
         for turn in range(8):
@@ -379,19 +368,9 @@
             place = position_ref[:, pl.ds(pl.multiple_of(cluster * 128, 128), 128)]
             own_ref[cluster, 0:3, :] = place
             own_ref[cluster, 3:4, :] = masked
-        at = pl.ds(pl.multiple_of(step * 8, 8), 8)
-        total = jnp.sum(masked_ref[at, :], axis=1, keepdims=True)
-        sum_ref[at, :] = jnp.broadcast_to(deposit_scale * total, (8, 128))
-        return 0
-
-    lax.fori_loop(0, clusters // 8, collect, 0, unroll=4)
-
-    ups = upward()
-    direction = pair_dir_ref[...]
-    way = lax.shift_right_arithmetic(direction - 1, 1)
-    flip = jnp.where(way == 0, ups[0], jnp.where(way == 1, ups[1], ups[2]))
-    position = 1 + 2 * way + lax.bitwise_xor(lax.bitwise_and(direction - 1, 1), flip)
-    row_ref[...] = jnp.where(direction == 0, 0, position) * slots + pair_slot_ref[...]
+        return 0
+
+    lax.fori_loop(0, clusters // 8, collect, 0, unroll=2)
 
     def fill_messages(step, _):
         for position, out_ref in enumerate(out_refs):
@@ -406,6 +385,67 @@
         return 0
 
     lax.fori_loop(0, slots // 2, fill_messages, 0)
+
+
+def prepare(fill, send_index, send_count, pair_dir, pair_slot, positions, charges):
+    clusters = charges.shape[0]
+    directions, slots = send_index.shape
+    smem = pl.BlockSpec(memory_space=pltpu.SMEM)
+    vmem = pl.BlockSpec(memory_space=pltpu.VMEM)
+    return pl.pallas_call(
+        prepare_kernel,
+        out_shape=(
+            jax.ShapeDtypeStruct(pair_dir.shape, jnp.int32),
+            jax.ShapeDtypeStruct((clusters, 4, 128), jnp.float32),
+            jax.ShapeDtypeStruct((clusters, 128), jnp.float32),
+            *[jax.ShapeDtypeStruct((slots * 4, 128), jnp.float32)] * directions,
+        ),
+        in_specs=[smem] * 3 + [vmem] * 2 + [pl.BlockSpec(memory_space=pltpu.HBM)] * 2,
+        out_specs=(vmem,) * (3 + directions),
+        scratch_shapes=[
+            *[pltpu.VMEM(operand.shape, jnp.float32) for operand in (positions, charges)],
+            pltpu.SemaphoreType.DMA((2,)),
+        ],
+        compiler_params=pltpu.CompilerParams(vmem_limit_bytes=VMEM_LIMIT),
+        name="prepare",
+    )(fill, send_index, send_count, pair_dir, pair_slot, positions, charges)
+
+
+def sources_kernel(
+    cell_ref,
+    cell_row_ref,
+    masked_hbm,
+    ion_hbm,
+    start_hbm,
+    screen_hbm,
+    inverse_ref,
+    source_ref,
+    *refs,
+):
+    edge_refs, refs = (refs[:2], refs[2:])
+    sum_ref, deposit_ref, masked_ref, ion_ref, start_ref, screen_ref, sems = refs
+    copies = start_copies(
+        (
+            (masked_hbm, masked_ref),
+            (ion_hbm, ion_ref),
+            (start_hbm, start_ref),
+            (screen_hbm, screen_ref),
+        ),
+        sems,
+    )
+    copies[0].wait()
+    clusters = masked_ref.shape[0]
+    cells_x, cells_y, _ = ion_ref.shape
+    lane = lax.broadcasted_iota(jnp.int32, (1, 128), 1)
+    ups = upward()
+
+    def add_up(step, _):
+        at = pl.ds(pl.multiple_of(step * 8, 8), 8)
+        total = jnp.sum(masked_ref[at, :], axis=1, keepdims=True)
+        sum_ref[at, :] = jnp.broadcast_to(deposit_scale * total, (8, 128))
+        return 0
+
+    lax.fori_loop(0, clusters // 8, add_up, 0, unroll=8)
 
     def place(step, _):
         for turn in range(8):
@@ -429,7 +469,7 @@
         deposit_ref[first : first + block, :] = added[:, :128] + (
             added[:, 128:256] + added[:, 256:]
         )
-    for copy in copies[2:]:
+    for copy in copies[1:]:
         copy.wait()
     inverse_ref[...] = 1.0 / (6.0 + screen_ref[...])
     for index in range(cells_x):
@@ -452,62 +492,29 @@
             edge += 1
 
 
-def prepare(
-    fill,
-    cell,
-    send_index,
-    send_count,
-    pair_dir,
-    pair_slot,
-    positions,
-    charges,
-    ions,
-    start,
-    screen,
-):
-    clusters = charges.shape[0]
-    directions, slots = send_index.shape
+def sources_of(cell, masked, ions, start, screen):
+    clusters = masked.shape[0]
     cells_y = ions.shape[1]
     smem = pl.BlockSpec(memory_space=pltpu.SMEM)
     vmem = pl.BlockSpec(memory_space=pltpu.VMEM)
+    edge = jax.ShapeDtypeStruct((2 * sum(HALO_WIDTHS), cells_y, 128), jnp.float32)
     return pl.pallas_call(
-        prepare_kernel,
-        out_shape=(
-            jax.ShapeDtypeStruct(pair_dir.shape, jnp.int32),
-            jax.ShapeDtypeStruct((clusters, 4, 128), jnp.float32),
-            jax.ShapeDtypeStruct((clusters, 128), jnp.float32),
-            jax.ShapeDtypeStruct(ions.shape, jnp.float32),
-            jax.ShapeDtypeStruct(ions.shape, jnp.float32),
-            *[jax.ShapeDtypeStruct((slots * 4, 128), jnp.float32)] * directions,
-            *[jax.ShapeDtypeStruct((2 * sum(HALO_WIDTHS), cells_y, 128), jnp.float32)] * 2,
-        ),
-        in_specs=[smem] * 4 + [vmem] * 3 + [pl.BlockSpec(memory_space=pltpu.HBM)] * 5,
-        out_specs=(vmem,) * (7 + directions),
+        sources_kernel,
+        out_shape=(*[jax.ShapeDtypeStruct(ions.shape, jnp.float32)] * 2, edge, edge),
+        in_specs=[smem, vmem] + [pl.BlockSpec(memory_space=pltpu.HBM)] * 4,
+        out_specs=(vmem,) * 4,
         scratch_shapes=[
             pltpu.VMEM((clusters, 128), jnp.float32),
             pltpu.VMEM((ions.size // 128, 128), jnp.float32),
-            *[
-                pltpu.VMEM(operand.shape, jnp.float32)
-                for operand in (positions, charges, ions, start, screen)
-            ],
-            pltpu.SemaphoreType.DMA((5,)),
+            *[pltpu.VMEM(operand.shape, jnp.float32) for operand in (masked, ions, start, screen)],
+            pltpu.SemaphoreType.DMA((4,)),
         ],
         compiler_params=pltpu.CompilerParams(vmem_limit_bytes=VMEM_LIMIT),
-        name="prepare",
-    )(
-        fill,
-        cell,
-        send_index,
-        send_count,
-        cell.reshape(1, clusters),
-        pair_dir,
-        pair_slot,
-        positions,
-        charges,
-        ions,
-        start,
-        screen,
-    )
+        cost_estimate=pl.CostEstimate(
+            flops=20_000_000, bytes_accessed=4 << 20, transcendentals=0
+        ),
+        name="sources",
+    )(cell, cell.reshape(1, clusters), masked, ions, start, screen)
 
 
 def line_rows(cells_y):
@@ -565,14 +572,14 @@
     return pl.pallas_call(
         pack_rows_kernel,
         out_shape=(shape, shape),
-        in_specs=[pl.BlockSpec(memory_space=pltpu.HBM)] * 8,
+        in_specs=[pl.BlockSpec(memory_space=pl.ANY)] * 8,
         out_specs=(vmem, vmem),
         scratch_shapes=[
             *[pltpu.VMEM((2, cells_x, 8, cells_z), jnp.float32)] * 4,
             *[pltpu.VMEM((2, edges[0].shape[0], 8, 128), jnp.float32)] * 2,
             pltpu.SemaphoreType.DMA((14,)),
         ],
-        compiler_params=pltpu.CompilerParams(vmem_limit_bytes=VMEM_LIMIT),
+        compiler_params=pltpu.CompilerParams(vmem_limit_bytes=ROOMY_LIMIT),
         name="pack_rows",
     )(*fields, *edges, *reactions)
 
@@ -618,19 +625,23 @@
     moves += zip(hbm_refs, field_refs, strict=True)
     moves += zip(edge_hbms, edge_refs, strict=True)
     moves.append((masked_hbm, masked_ref))
-    for copy in start_copies(moves, sems):
+    copies = start_copies(moves, sems)
+    extended = (start_ref, inverse_ref, source_ref, ion_ref)
+    for copy in copies[:2]:
         copy.wait()
-    extended = (start_ref, inverse_ref, source_ref, ion_ref)
-
-    def fill(index, _):
-        for field, target_ref in enumerate(extended):
+    for field, target_ref in enumerate(extended):
+        copies[2 + field].wait()
+
+        def fill(index, _, field=field, target_ref=target_ref):
             plane = field_refs[field][index]
             for half in range(2):
                 value = plane[:, 128 * half : 128 * half + 128]
                 fill_line(target_ref, DEPTH + index, half, field, value, rim_ref)
-        return 0
-
-    lax.fori_loop(0, cells_x, fill, 0, unroll=2)
+            return 0
+
+        lax.fori_loop(0, cells_x, fill, 0, unroll=4)
+    for copy in copies[6:]:
+        copy.wait()
     for field, target_ref in enumerate(extended):
         width = HALO_WIDTHS[field]
         for phase, edge_ref in enumerate(edge_refs):
@@ -795,7 +806,7 @@
             jax.ShapeDtypeStruct(fields[0].shape, jnp.float32),
             jax.ShapeDtypeStruct((clusters * 4, 128), jnp.float32),
         ),
-        in_specs=[smem] + [pl.BlockSpec(memory_space=pltpu.HBM)] * 9,
+        in_specs=[smem] + [pl.BlockSpec(memory_space=pl.ANY)] * 9,
         out_specs=(vmem,) * 3,
         scratch_shapes=[pltpu.VMEM(block, jnp.float32)] * 10
         + [pltpu.VMEM((clusters, 128), jnp.float32)] * 3
@@ -803,7 +814,7 @@
         + [pltpu.VMEM(field.shape, jnp.float32) for field in fields]
         + [pltpu.VMEM(masked.shape, jnp.float32), pltpu.SemaphoreType.DMA((9,))]
         + [pltpu.VMEM(edge.shape, jnp.float32) for edge in edges],
-        compiler_params=pltpu.CompilerParams(vmem_limit_bytes=VMEM_LIMIT),
+        compiler_params=pltpu.CompilerParams(vmem_limit_bytes=ROOMY_LIMIT),
         cost_estimate=pl.CostEstimate(
             flops=block[0] * block[1] * 100, bytes_accessed=8 << 20, transcendentals=0
         ),
@@ -813,8 +824,8 @@
 
 def gather_forces_kernel(send_index_ref, *refs):
     fetched = len(SWAPS) + 3
-    out_ref, sum_ref = refs[fetched : fetched + 2]
-    own_ref, field_ref, *back_refs = refs[fetched + 2 : -1]
+    out_ref, extra_ref = refs[fetched : fetched + 2]
+    sum_ref, field_ref, *back_refs = refs[fetched + 2 : -1]
     copies = start_copies(
         [
             (source.at[0 : target.shape[0]], target)
@@ -822,25 +833,27 @@
         ],
         refs[-1],
     )
+    extra_ref[...] = jnp.zeros_like(extra_ref)
     for copy in copies:
         copy.wait()
-    clusters = own_ref.shape[0]
+    clusters = sum_ref.shape[0]
     slots = send_index_ref.shape[1]
-    sum_ref[...] = own_ref[...] + field_ref[...]
     ups = upward()
 
     def visit(slot, _):
         for position, back_ref in enumerate(back_refs):
             cluster = send_index_ref[sent_row(position, ups) if position else 0, slot]
-            sum_ref[cluster] += back_ref[slot]
-        return 0
-
-    lax.fori_loop(0, slots, visit, 0)
+            target_ref = extra_ref if position % 2 else sum_ref
+            target_ref[cluster] += back_ref[slot]
+        return 0
+
+    lax.fori_loop(0, slots, visit, 0, unroll=2)
 
     def write(step, _):
         for turn in range(8):
             cluster = step * 8 + turn
-            out_ref[:, pl.ds(pl.multiple_of(cluster * 128, 128), 128)] = sum_ref[cluster][0:3]
+            total = (sum_ref[cluster] + extra_ref[cluster]) + field_ref[cluster]
+            out_ref[:, pl.ds(pl.multiple_of(cluster * 128, 128), 128)] = total[0:3]
         return 0
 
     lax.fori_loop(0, clusters // 8, write, 0)
@@ -853,14 +866,14 @@
     return pl.pallas_call(
         gather_forces_kernel,
         out_shape=jax.ShapeDtypeStruct((3, clusters * 128), jnp.float32),
-        in_specs=[smem] + [pl.BlockSpec(memory_space=pltpu.HBM)] * (2 + len(backs)),
+        in_specs=[smem] + [pl.BlockSpec(memory_space=pl.ANY)] * (2 + len(backs)),
         out_specs=vmem,
         scratch_shapes=[
             *[pltpu.VMEM(part.shape, jnp.float32) for part in (own, own, field)],
             *[pltpu.VMEM((send_index.shape[1], 4, 128), jnp.float32)] * len(backs),
             pltpu.SemaphoreType.DMA((2 + len(backs),)),
         ],
-        compiler_params=pltpu.CompilerParams(vmem_limit_bytes=VMEM_LIMIT),
+        compiler_params=pltpu.CompilerParams(vmem_limit_bytes=ROOMY_LIMIT),
         name="gather_forces",
     )(send_index, own, field, *backs)
 
@@ -883,23 +896,21 @@
     psize = charges.shape[0] // clusters
     slots = send_index.shape[1]
     base = slots * 4
-    other_rows, own, masked, inverse, source, local, *messages = prepare(
+    other_rows, own, masked, local, *messages = prepare(
         cluster_fill,
-        cluster_cell,
         send_index,
         send_count,
         pair_dir.reshape(-1, 128),
         pair_slot.reshape(-1, 128),
         positions,
         charges.reshape(clusters, psize),
-        ion_density,
-        potential_prev,
-        screening,
-    )
-    edges = messages[len(SWAPS) :]
+    )
+    inverse, source, *edges = sources_of(
+        cluster_cell, masked, ion_density, potential_prev, screening
+    )
     arrived = [local] + [
         swapped(message, *swap)
-        for message, swap in zip(messages[: len(SWAPS)], SWAPS, strict=True)
+        for message, swap in zip(messages, SWAPS, strict=True)
     ]
     fields = (potential_prev, inverse, source, ion_density)
     arrived, edges = lax.optimization_barrier((arrived, edges))

time: 114 us -> 107 us (0.939); the launches traced: 112 us -> 107 us
  Pallas kernels: 77.8 us -> 75.2 us
  waiting for transfers between devices: 5.18 us -> 3.05 us
    pallas_call x0 -> x1, Pallas kernels: none -> 4.44 us  [sources_of(): pl.pallas_call(sources_kernel, out_shape=(*[jax.ShapeDtypeStruct(ions.sha...]
    ppermute x14, waiting for transfers between devices: 5.18 us -> 3.05 us  [swapped(): return lax.ppermute(shard, axis, pairs)]
    pallas_call x1, Pallas kernels: 6.34 us -> 4.23 us  [prepare(): pl.pallas_call(prepare_kernel, out_shape=(jax.ShapeDtypeStruct(pair_dir.s...]
    pallas_call x1, Pallas kernels: 2.71 us -> 0.65 us  [pack_rows(): pl.pallas_call(pack_rows_kernel, out_shape=(shape, shape), in_specs=[pl.B...]
    unnamed x36 -> x30, local copies, waits for them, and re-layouts: 2.34 us -> 2.83 us
  transfers between devices with their start and end apart: 14 -> 14, of which waited for: 2 -> 1; matrix products, arithmetic and copies ran while one was open for 0% -> 0% of each run, Pallas kernels for 58% -> 63%
where the time goes in v16:
time: 107 us
  Pallas kernels  75.2 us (70%)
  starting transfers between devices  24.5 us (23%)
  waiting for transfers between devices  3.05 us (3%)
  local copies, waits for them, and re-layouts  2.83 us (3%)
    pallas_call x1, Pallas kernels, pair_forces(): pl.pallas_call(pair_kernel, out_shape=(jax.ShapeDtypeStruct(own.shape, jn...  49.6 us
    ppermute x14, starting transfers between devices, swapped(): return lax.ppermute(shard, axis, pairs)  24.5 us
    pallas_call x1, Pallas kernels, grid_step(): pl.pallas_call(functools.partial(grid_kernel, base), out_shape=(jax.Shape...  12.9 us
    pallas_call x1, Pallas kernels, sources_of(): pl.pallas_call(sources_kernel, out_shape=(*[jax.ShapeDtypeStruct(ions.sha...  4.44 us
    pallas_call x1, Pallas kernels, prepare(): pl.pallas_call(prepare_kernel, out_shape=(jax.ShapeDtypeStruct(pair_dir.s...  4.23 us
    pallas_call x1, Pallas kernels, gather_forces(): pl.pallas_call(gather_forces_kernel, out_shape=jax.ShapeDtypeStruct((3, c...  3.33 us
    ppermute x14, waiting for transfers between devices, swapped(): return lax.ppermute(shard, axis, pairs)  3.05 us
    unnamed x30, local copies, waits for them, and re-layouts  2.83 us
  transfers between devices with their start and end apart: 14, of which 1 were waited for; matrix products, arithmetic and copies ran while one was open for 0% of the time, Pallas kernels for 63%

profile of v16, /device:TPU:13, one launch (start us, length us, event | category | flops | bytes accessed | tf_op | source)
XLA Modules:
  0.0 106.5 jit_solution(14350860632696283389)
XLA Ops:
  0.6 4.2 %prepare.1 = (s32[8,128]{1,0:T(8,128)}, f32[256,4,128]{2,1,0:T(4,128)}, f32[256,128]{1,0:T(8,128)}, f32[128,128]{1,0:T(8,128)}, f32[128,128]{1,0:T(8,128)}, /*in...) custom-call(s32[256]{0:T(256)} %fill_ref.1, ...), custom_call_target="tpu_custom_call" | custom-call | tf_op jit(solution)/shard_map/prepare/pallas_call | solution.py:395
  4.9 0.7 collective-permute-start
  5.6 3.1 %collective-permute-start.1 = (f32[128,128]{1,0:T(8,128)}, f32[128,128]{1,0:T(8,128)S(1)}, u32[]{:S(2)}, u32[]{:S(2)}) collective-permute-start(f32[128,128]{1,0:T(8,128)} %get-tuple-element.43), channel_id=1, source_target_pairs={{1,2},{2,1},{3,4},{4,3},{5,6},{6,5},{9,10},{10,9},{11,12},{12,11},... | collective-permute-start | bytes 196616 | tf_op jit(solution)/shard_map/ppermute | solution.py:65
  8.7 0.2 collective-permute-start.2
  9.0 3.0 %collective-permute-start.3 = (f32[128,128]{1,0:T(8,128)}, f32[128,128]{1,0:T(8,128)S(1)}, u32[]{:S(2)}, u32[]{:S(2)}) collective-permute-start(f32[128,128]{1,0:T(8,128)} %get-tuple-element.45), channel_id=1, source_target_pairs={{2,4},{3,5},{4,2},{5,3},{10,12},{11,13},{12,10},{13,11},{18,20},{1... | collective-permute-start | bytes 196616 | tf_op jit(solution)/shard_map/ppermute | solution.py:65
  12.0 1.3 %collective-permute-start.4 = (f32[128,128]{1,0:T(8,128)}, f32[128,128]{1,0:T(8,128)S(1)}, u32[]{:S(2)}, u32[]{:S(2)}) collective-permute-start(f32[128,128]{1,0:T(8,128)} %get-tuple-element.46), channel_id=1, source_target_pairs={{0,8},{8,0},{16,24},{24,16},{1,9},{9,1},{17,25},{25,17},{2,10},{10... | collective-permute-start | bytes 196616 | tf_op jit(solution)/shard_map/ppermute | solution.py:65
  13.3 0.0 collective-permute-done.refs_5_
  13.3 2.1 %collective-permute-start.5 = (f32[128,128]{1,0:T(8,128)}, f32[128,128]{1,0:T(8,128)S(1)}, u32[]{:S(2)}, u32[]{:S(2)}) collective-permute-start(f32[128,128]{1,0:T(8,128)} %get-tuple-element.47), channel_id=1, source_target_pairs={{8,16},{16,8},{9,17},{17,9},{10,18},{18,10},{11,19},{19,11},{12,20... | collective-permute-start | bytes 196616 | tf_op jit(solution)/shard_map/ppermute | solution.py:65
  15.4 0.0 copy-start.5
  15.4 0.0 copy-start.7
  15.4 0.0 copy-start.8
  15.4 0.0 copy-start.9
  15.4 0.0 copy-start.10
  15.5 4.4 %sources.1 = (f32[16,32,256]{2,1,0:T(8,128)}, f32[16,32,256]{2,1,0:T(8,128)}, f32[28,32,128]{2,1,0:T(8,128)}, f32[28,32,128]{2,1,0:T(8,128)}) custom-call(s32[256]{0:T(256)} %refs_0_.4, s32[1,256]{1,0:T(1,128)} %bitcast.25, f32[256,128]{1,0:T(8,128)} %get-tuple-element.48.masked_hbm.refs_1_, f32[16,32,256]{2,1,0:T(8,128)} %refs_5_.1, ...), custom_call_target="tpu_custom_call" | custom-call | flops 20000000 | bytes 4194304 | tf_op jit(solution)/shard_map/sources/pallas_call | solution.py:501
  19.9 0.0 collective-permute-done.1.refs_6_
  19.9 0.0 collective-permute-done.2.refs_7_
  19.9 0.0 collective-permute-done.3.refs_8_
  19.9 0.0 collective-permute-done.4.refs_9_
  19.9 0.0 collective-permute-done.5.refs_10_
  19.9 0.0 copy-start.14
  20.0 0.0 copy-start.13
  20.0 0.1 collective-permute-start.6
  20.0 4.1 %collective-permute-start.7 = (f32[28,32,128]{2,1,0:T(8,128)}, f32[28,32,128]{2,1,0:T(8,128)S(1)}, u32[]{:S(2)}, u32[]{:S(2)}) collective-permute-start(f32[28,32,128]{2,1,0:T(8,128)} %get-tuple-element.62), channel_id=1, source_target_pairs={{8,16},{16,8},{9,17},{17,9},{10,18},{18,10},{11,19},{19,11},{12,20... | collective-permute-start | bytes 1376264 | tf_op jit(solution)/shard_map/ppermute | solution.py:65
  24.1 0.0 copy-done.5
  24.1 0.0 copy-done.7
  24.2 0.0 copy-done.8
  24.2 0.0 copy-done.9
  24.2 0.0 copy-done.10
  24.2 0.0 copy-done.14
  24.2 0.0 copy-done.13
  24.2 0.0 copy-start
  24.2 0.0 copy-start.1
  24.2 49.6 %pair_forces.1 = (f32[1024,128]{1,0:T(8,128)S(1)}, f32[128,128]{1,0:T(8,128)S(1)}, f32[128,128]{1,0:T(8,128)S(1)}, f32[128,128]{1,0:T(8,128)S(1)}, f32[128,128]{...) custom-call(s32[1024]{0:T(1024)S(1)} %copy-done.13, s32[1024]{0:T(1024)S(1)} %bitcast.26, ...), custom_call_target="tpu_custom_call" | custom-call | flops 335544320 | bytes 4194304 | tf_op jit(solution)/shard_map/pair_forces/pallas_call | solution.py:306
  73.9 0.0 collective-permute-done.6.refs_4_.refs_8_
  73.9 0.0 collective-permute-done.7.refs_5_.refs_9_
  73.9 0.0 copy-done
  73.9 0.0 copy-done.1
  73.9 0.0 copy-start.2
  73.9 1.0 copy-done.2
  74.9 0.0 copy-start.4
  74.9 1.0 copy-done.4
  76.0 0.0 copy-start.3
  76.0 0.0 copy-start.6
  76.0 0.6 pack_rows.1
  76.6 2.1 %collective-permute-start.8 = (f32[960,128]{1,0:T(8,128)S(1)}, f32[960,128]{1,0:T(8,128)S(1)}, u32[]{:S(2)}, u32[]{:S(2)}) collective-permute-start(f32[960,128]{1,0:T(8,128)S(1)} %get-tuple-element.65), channel_id=1, source_target_pairs={{0,1},{1,0},{2,3},{3,2},{4,5},{5,4},{6,7},{7,6},{8,9},{9,8},{10,11... | collective-permute-start | bytes 1474568 | tf_op jit(solution)/shard_map/ppermute | solution.py:65
  78.7 1.9 %collective-permute-start.9 = (f32[960,128]{1,0:T(8,128)S(1)}, f32[960,128]{1,0:T(8,128)S(1)}, u32[]{:S(2)}, u32[]{:S(2)}) collective-permute-start(f32[960,128]{1,0:T(8,128)S(1)} %get-tuple-element.66), channel_id=1, source_target_pairs={{1,2},{2,1},{3,4},{4,3},{5,6},{6,5},{9,10},{10,9},{11,12},{12,11},... | collective-permute-start | bytes 1474568 | tf_op jit(solution)/shard_map/ppermute | solution.py:65
  80.6 1.4 %collective-permute-start.10 = (f32[128,128]{1,0:T(8,128)S(1)}, f32[128,128]{1,0:T(8,128)S(1)}, u32[]{:S(2)}, u32[]{:S(2)}) collective-permute-start(f32[128,128]{1,0:T(8,128)S(1)} %get-tuple-element.69), channel_id=1, source_target_pairs={{0,2},{1,3},{2,0},{3,1},{4,6},{5,7},{6,4},{7,5},{8,10},{9,11},{10,... | collective-permute-start | bytes 196616 | tf_op jit(solution)/shard_map/ppermute | solution.py:65
  82.1 1.9 %collective-permute-start.11 = (f32[128,128]{1,0:T(8,128)S(1)}, f32[128,128]{1,0:T(8,128)S(1)}, u32[]{:S(2)}, u32[]{:S(2)}) collective-permute-start(f32[128,128]{1,0:T(8,128)S(1)} %get-tuple-element.70), channel_id=1, source_target_pairs={{2,4},{3,5},{4,2},{5,3},{10,12},{11,13},{12,10},{13,11},{18,20},{1... | collective-permute-start | bytes 196616 | tf_op jit(solution)/shard_map/ppermute | solution.py:65
  84.0 0.0 copy-start.12
  84.0 0.1 collective-permute-start.12
  84.1 0.0 collective-permute-done.8.refs_6_
  84.1 2.5 %collective-permute-start.13 = (f32[128,128]{1,0:T(8,128)S(1)}, f32[128,128]{1,0:T(8,128)S(1)}, u32[]{:S(2)}, u32[]{:S(2)}) collective-permute-start(f32[128,128]{1,0:T(8,128)S(1)} %get-tuple-element.72), channel_id=1, source_target_pairs={{8,16},{16,8},{9,17},{17,9},{10,18},{18,10},{11,19},{19,11},{12,20... | collective-permute-start | bytes 196616 | tf_op jit(solution)/shard_map/ppermute | solution.py:65
  86.5 3.0 %collective-permute-done.9.refs_7_ = f32[960,128]{1,0:T(8,128)S(1)} collective-permute-done((f32[960,128]{1,0:T(8,128)S(1)}, f32[960,128]{1,0:T(8,128)S(1)}, u32[]{:S(2)}, u32[]{:S(2)}) %collective-permute-start.9) | collective-permute-done | bytes 491552 | tf_op jit(solution)/shard_map/ppermute | solution.py:65
  89.6 0.0 copy-done.3
  89.6 0.0 copy-done.6
  89.6 0.0 copy-done.12
  89.6 12.9 %grid_step.1 = (f32[16,32,256]{2,1,0:T(8,128)}, f32[16,32,256]{2,1,0:T(8,128)}, f32[1024,128]{1,0:T(8,128)S(1)}) custom-call(s32[256]{0:T(256)S(1)} %copy-done.12, f32[256,128]{1,0:T(8,128)S(1)} %copy-done.6, f32[16,32,256]{2,1,0:T(8,128)S(1)} %copy-done, f32[16,32,256]{2,1,0:T(8,128)S(1)} %copy-done.3, f32[16,32,256]{2,1,0:T(8,128)S(1)} %copy-done.4, ...), custom_call_target="tpu_custom_call" | custom-call | flops 31948800 | bytes 8388608 | tf_op jit(solution)/shard_map/grid_step/pallas_call | solution.py:802
  102.5 0.0 collective-permute-done.10
  102.5 0.0 collective-permute-done.11
  102.5 0.0 collective-permute-done.12
  102.5 0.0 collective-permute-done.13
  102.5 0.0 copy-start.11
  102.5 0.7 copy-done.11
  103.2 3.3 %gather_forces.1 = f32[3,32768]{1,0:T(4,128)} custom-call(s32[7,32]{1,0:T(8,128)S(1)} %copy-done.11, f32[256,4,128]{2,1,0:T(4,128)S(1)} %bitcast.17, f32[256,4,128]{2,1,0:T(4,128)S(1)} %bitcast.19, f32[32,4,128]{2,1,0:T(4,128)S(1)} %bitcast.20, f32[240,4,128]{2,1,0:T(4,128)S(1)} %bitcast.15, f32[240,4,128]{2,1,0:T(4,128)S(1)} %bitcast.16, ...), custom_call_target="tpu_custom_call" | custom-call | tf_op jit(solution)/shard_map/gather_forces/pallas_call | solution.py:866
Async XLA Ops:
  4.9 8.4 %collective-permute-start = (f32[128,128]{1,0:T(8,128)}, f32[128,128]{1,0:T(8,128)S(1)}, u32[]{:S(2)}, u32[]{:S(2)}) collective-permute-start(f32[128,128]{1,0:T(8,128)} %get-tuple-element.42), channel_id=1, source_target_pairs={{0,1},{1,0},{2,3},{3,2},{4,5},{5,4},{6,7},{7,6},{8,9},{9,8},{10,11... | collective-permute-start | bytes 196616 | tf_op jit(solution)/shard_map/ppermute | solution.py:65
  5.6 14.3 %collective-permute-start.1 = (f32[128,128]{1,0:T(8,128)}, f32[128,128]{1,0:T(8,128)S(1)}, u32[]{:S(2)}, u32[]{:S(2)}) collective-permute-start(f32[128,128]{1,0:T(8,128)} %get-tuple-element.43), channel_id=1, source_target_pairs={{1,2},{2,1},{3,4},{4,3},{5,6},{6,5},{9,10},{10,9},{11,12},{12,11},... | collective-permute-start | bytes 196616 | tf_op jit(solution)/shard_map/ppermute | solution.py:65
  8.7 11.2 %collective-permute-start.2 = (f32[128,128]{1,0:T(8,128)}, f32[128,128]{1,0:T(8,128)S(1)}, u32[]{:S(2)}, u32[]{:S(2)}) collective-permute-start(f32[128,128]{1,0:T(8,128)} %get-tuple-element.44), channel_id=1, source_target_pairs={{0,2},{1,3},{2,0},{3,1},{4,6},{5,7},{6,4},{7,5},{8,10},{9,11},{10,... | collective-permute-start | bytes 196616 | tf_op jit(solution)/shard_map/ppermute | solution.py:65
  9.0 11.0 %collective-permute-start.3 = (f32[128,128]{1,0:T(8,128)}, f32[128,128]{1,0:T(8,128)S(1)}, u32[]{:S(2)}, u32[]{:S(2)}) collective-permute-start(f32[128,128]{1,0:T(8,128)} %get-tuple-element.45), channel_id=1, source_target_pairs={{2,4},{3,5},{4,2},{5,3},{10,12},{11,13},{12,10},{13,11},{18,20},{1... | collective-permute-start | bytes 196616 | tf_op jit(solution)/shard_map/ppermute | solution.py:65
  12.0 7.9 %collective-permute-start.4 = (f32[128,128]{1,0:T(8,128)}, f32[128,128]{1,0:T(8,128)S(1)}, u32[]{:S(2)}, u32[]{:S(2)}) collective-permute-start(f32[128,128]{1,0:T(8,128)} %get-tuple-element.46), channel_id=1, source_target_pairs={{0,8},{8,0},{16,24},{24,16},{1,9},{9,1},{17,25},{25,17},{2,10},{10... | collective-permute-start | bytes 196616 | tf_op jit(solution)/shard_map/ppermute | solution.py:65
  13.3 6.7 %collective-permute-start.5 = (f32[128,128]{1,0:T(8,128)}, f32[128,128]{1,0:T(8,128)S(1)}, u32[]{:S(2)}, u32[]{:S(2)}) collective-permute-start(f32[128,128]{1,0:T(8,128)} %get-tuple-element.47), channel_id=1, source_target_pairs={{8,16},{16,8},{9,17},{17,9},{10,18},{18,10},{11,19},{19,11},{12,20... | collective-permute-start | bytes 196616 | tf_op jit(solution)/shard_map/ppermute | solution.py:65
  15.4 8.7 %copy-start.5 = (f32[256,4,128]{2,1,0:T(4,128)S(1)}, f32[256,4,128]{2,1,0:T(4,128)}, u32[]{:S(2)}) copy-start(f32[256,4,128]{2,1,0:T(4,128)} %get-tuple-element.40) | copy-start | bytes 1572868
  15.4 8.7 %copy-start.7 = (bf16[128,1024]{1,0:T(8,128)(2,1)S(1)}, bf16[128,1024]{1,0:T(8,128)(2,1)}, u32[]{:S(2)}) copy-start(bf16[128,1024]{1,0:T(8,128)(2,1)} %constant.6.clone.refs_0_) | copy-start | bytes 786436
  15.4 8.7 %copy-start.8 = (bf16[256,128]{1,0:T(8,128)(2,1)S(1)}, bf16[256,128]{1,0:T(8,128)(2,1)}, u32[]{:S(2)}) copy-start(bf16[256,128]{1,0:T(8,128)(2,1)} %constant.7.clone.refs_1_) | copy-start | bytes 196612
  15.4 8.7 %copy-start.9 = (f32[128,128]{1,0:T(8,128)S(1)}, f32[128,128]{1,0:T(8,128)}, u32[]{:S(2)}) copy-start(f32[128,128]{1,0:T(8,128)} %get-tuple-element.51.refs_4_) | copy-start | bytes 196612
  15.4 8.7 %copy-start.10 = (bf16[128,128]{1,0:T(8,128)(2,1)S(1)}, bf16[128,128]{1,0:T(8,128)(2,1)}, u32[]{:S(2)}) copy-start(bf16[128,128]{1,0:T(8,128)(2,1)} %constant.8.clone.refs_2_) | copy-start | bytes 98308
  19.9 4.2 %copy-start.14 = (s32[8,128]{1,0:T(8,128)S(1)}, s32[8,128]{1,0:T(8,128)}, u32[]{:S(2)}) copy-start(s32[8,128]{1,0:T(8,128)} %get-tuple-element.39) | copy-start | bytes 12292
  20.0 4.2 %copy-start.13 = (s32[1024]{0:T(1024)S(1)}, s32[1024]{0:T(1024)}, u32[]{:S(2)}) copy-start(s32[1024]{0:T(1024)} %own_rows_ref.1) | copy-start | bytes 12292
  20.0 53.9 %collective-permute-start.6 = (f32[28,32,128]{2,1,0:T(8,128)}, f32[28,32,128]{2,1,0:T(8,128)S(1)}, u32[]{:S(2)}, u32[]{:S(2)}) collective-permute-start(f32[28,32,128]{2,1,0:T(8,128)} %get-tuple-element.61), channel_id=1, source_target_pairs={{0,8},{8,0},{16,24},{24,16},{1,9},{9,1},{17,25},{25,17},{2,10},{10... | collective-permute-start | bytes 1376264 | tf_op jit(solution)/shard_map/ppermute | solution.py:65
  20.0 53.8 %collective-permute-start.7 = (f32[28,32,128]{2,1,0:T(8,128)}, f32[28,32,128]{2,1,0:T(8,128)S(1)}, u32[]{:S(2)}, u32[]{:S(2)}) collective-permute-start(f32[28,32,128]{2,1,0:T(8,128)} %get-tuple-element.62), channel_id=1, source_target_pairs={{8,16},{16,8},{9,17},{17,9},{10,18},{18,10},{11,19},{19,11},{12,20... | collective-permute-start | bytes 1376264 | tf_op jit(solution)/shard_map/ppermute | solution.py:65
  24.2 49.7 %copy-start = (f32[16,32,256]{2,1,0:T(8,128)S(1)}, f32[16,32,256]{2,1,0:T(8,128)}, u32[]{:S(2)}) copy-start(f32[16,32,256]{2,1,0:T(8,128)} %refs_2_.2) | copy-start | bytes 1572868
  24.2 49.7 %copy-start.1 = (f32[16,32,256]{2,1,0:T(8,128)S(1)}, f32[16,32,256]{2,1,0:T(8,128)}, u32[]{:S(2)}) copy-start(f32[16,32,256]{2,1,0:T(8,128)} %refs_5_.1) | copy-start | bytes 1572868
  73.9 1.0 copy-start.2
  74.9 1.0 copy-start.4
  76.0 13.6 %copy-start.3 = (f32[16,32,256]{2,1,0:T(8,128)S(1)}, f32[16,32,256]{2,1,0:T(8,128)}, u32[]{:S(2)}) copy-start(f32[16,32,256]{2,1,0:T(8,128)} %get-tuple-element.59.refs_1_.refs_3_) | copy-start | bytes 1572868
  76.0 13.6 %copy-start.6 = (f32[256,128]{1,0:T(8,128)S(1)}, f32[256,128]{1,0:T(8,128)}, u32[]{:S(2)}) copy-start(f32[256,128]{1,0:T(8,128)} %get-tuple-element.48.masked_hbm.refs_1_) | copy-start | bytes 393220
  76.6 7.4 %collective-permute-start.8 = (f32[960,128]{1,0:T(8,128)S(1)}, f32[960,128]{1,0:T(8,128)S(1)}, u32[]{:S(2)}, u32[]{:S(2)}) collective-permute-start(f32[960,128]{1,0:T(8,128)S(1)} %get-tuple-element.65), channel_id=1, source_target_pairs={{0,1},{1,0},{2,3},{3,2},{4,5},{5,4},{6,7},{7,6},{8,9},{9,8},{10,11... | collective-permute-start | bytes 1474568 | tf_op jit(solution)/shard_map/ppermute | solution.py:65
  78.7 10.8 %collective-permute-start.9 = (f32[960,128]{1,0:T(8,128)S(1)}, f32[960,128]{1,0:T(8,128)S(1)}, u32[]{:S(2)}, u32[]{:S(2)}) collective-permute-start(f32[960,128]{1,0:T(8,128)S(1)} %get-tuple-element.66), channel_id=1, source_target_pairs={{1,2},{2,1},{3,4},{4,3},{5,6},{6,5},{9,10},{10,9},{11,12},{12,11},... | collective-permute-start | bytes 1474568 | tf_op jit(solution)/shard_map/ppermute | solution.py:65
  80.6 21.8 %collective-permute-start.10 = (f32[128,128]{1,0:T(8,128)S(1)}, f32[128,128]{1,0:T(8,128)S(1)}, u32[]{:S(2)}, u32[]{:S(2)}) collective-permute-start(f32[128,128]{1,0:T(8,128)S(1)} %get-tuple-element.69), channel_id=1, source_target_pairs={{0,2},{1,3},{2,0},{3,1},{4,6},{5,7},{6,4},{7,5},{8,10},{9,11},{10,... | collective-permute-start | bytes 196616 | tf_op jit(solution)/shard_map/ppermute | solution.py:65
  82.1 20.4 %collective-permute-start.11 = (f32[128,128]{1,0:T(8,128)S(1)}, f32[128,128]{1,0:T(8,128)S(1)}, u32[]{:S(2)}, u32[]{:S(2)}) collective-permute-start(f32[128,128]{1,0:T(8,128)S(1)} %get-tuple-element.70), channel_id=1, source_target_pairs={{2,4},{3,5},{4,2},{5,3},{10,12},{11,13},{12,10},{13,11},{18,20},{1... | collective-permute-start | bytes 196616 | tf_op jit(solution)/shard_map/ppermute | solution.py:65
  84.0 5.6 %copy-start.12 = (s32[256]{0:T(256)S(1)}, s32[256]{0:T(256)}, u32[]{:S(2)}) copy-start(s32[256]{0:T(256)} %refs_0_.4) | copy-start | bytes 3076
  84.0 18.5 %collective-permute-start.12 = (f32[128,128]{1,0:T(8,128)S(1)}, f32[128,128]{1,0:T(8,128)S(1)}, u32[]{:S(2)}, u32[]{:S(2)}) collective-permute-start(f32[128,128]{1,0:T(8,128)S(1)} %get-tuple-element.71), channel_id=1, source_target_pairs={{0,8},{8,0},{16,24},{24,16},{1,9},{9,1},{17,25},{25,17},{2,10},{10... | collective-permute-start | bytes 196616 | tf_op jit(solution)/shard_map/ppermute | solution.py:65
  84.1 18.4 %collective-permute-start.13 = (f32[128,128]{1,0:T(8,128)S(1)}, f32[128,128]{1,0:T(8,128)S(1)}, u32[]{:S(2)}, u32[]{:S(2)}) collective-permute-start(f32[128,128]{1,0:T(8,128)S(1)} %get-tuple-element.72), channel_id=1, source_target_pairs={{8,16},{16,8},{9,17},{17,9},{10,18},{18,10},{11,19},{19,11},{12,20... | collective-permute-start | bytes 196616 | tf_op jit(solution)/shard_map/ppermute | solution.py:65
  102.5 0.7 copy-start.11

commit v17 on v16

--- a/solution.py
+++ b/solution.py
@@ -11,6 +11,8 @@
 SWEEPS = 4
 UNROLL = 8
 CHUNKS = 4
+AHEAD = 2
+BEHIND = 4
 HALO_WIDTHS = (SWEEPS + 1, SWEEPS, SWEEPS, 1)
 DEPTH = SWEEPS + 1
 CELL_BITS = 8
@@ -231,37 +233,40 @@
         own_sum_ref[row_block(own), :] += to_own[:, :128] + to_own[:, 128:]
         other_sum_ref[row_block(other), :] += to_other[:, :128] + to_other[:, 128:]
 
-    def half_step(step, side, dist):
+    def half_step(step, side, dists):
         last = jnp.maximum(step - 1, 0) * UNROLL
         waiting = []
         for index in range(UNROLL):
             own = own_rows_ref[last + index]
             other = other_rows_ref[last + index]
-            later = distances(jnp.minimum(step * UNROLL + index + 1, groups * UNROLL - 1))
-            weights(dist, index, 0, weight_refs[1 - side])
+            coming = step * UNROLL + index + AHEAD
+            later = distances(jnp.minimum(coming, groups * UNROLL - 1))
+            weights(dists[0], index, 0, weight_refs[1 - side])
             to_own = own_product(other, weight_refs[side], index)
-            weights(dist, index, 1, weight_refs[1 - side])
-            weights(dist, index, 2, weight_refs[1 - side])
+            weights(dists[0], index, 1, weight_refs[1 - side])
+            weights(dists[0], index, 2, weight_refs[1 - side])
             to_other = other_product(own, weight_refs[side], index)
-            weights(dist, index, 3, weight_refs[1 - side])
-            dist = later
+            weights(dists[0], index, 3, weight_refs[1 - side])
+            dists = [*dists[1:], later]
             waiting.append((own, other, to_own, to_other))
-            if len(waiting) > 2:
+            if len(waiting) > BEHIND:
                 add_rows(*waiting.pop(0))
         for entry in waiting:
             add_rows(*entry)
-        return dist
+        return dists
 
     def visit(step, _):
-        dist = dist_ref[...]
+        dists = [dist_ref[index] for index in range(AHEAD)]
         for side in range(2):
-            dist = half_step(step * 2 + side, side, dist)
-        dist_ref[...] = dist
-        return 0
-
-    dist_ref[...] = distances(0)
+            dists = half_step(step * 2 + side, side, dists)
+        for index in range(AHEAD):
+            dist_ref[index] = dists[index]
+        return 0
+
+    for index in range(AHEAD):
+        dist_ref[index] = distances(index)
     lax.fori_loop(0, groups // 2, visit, 0)
-    half_step(groups, 0, dist_ref[...])
+    half_step(groups, 0, [dist_ref[index] for index in range(AHEAD)])
 
     def finish(data_ref, out_ref, sum_ref, base, step, _):
         start = pl.multiple_of(step * 8, 8)
@@ -321,7 +326,7 @@
             pltpu.VMEM((others * 16, 128), jnp.bfloat16),
             pltpu.VMEM((clusters * 16, 128), jnp.float32),
             pltpu.VMEM((others * 16, 128), jnp.float32),
-            pltpu.VMEM((128, 128), jnp.float32),
+            pltpu.VMEM((AHEAD, 128, 128), jnp.float32),
             *[pltpu.VMEM((128 * UNROLL, 256), jnp.bfloat16)] * 2,
         ],
         compiler_params=pltpu.CompilerParams(vmem_limit_bytes=ROOMY_LIMIT),

time: 107 us -> 107 us (level)
  no operation moved by 1% of the time
where the time goes in v17:
time: 107 us
  Pallas kernels  75.3 us (70%)
  starting transfers between devices  24.5 us (23%)
  waiting for transfers between devices  3.08 us (3%)
  local copies, waits for them, and re-layouts  2.83 us (3%)
    pallas_call x1, Pallas kernels, pair_forces(): pl.pallas_call(pair_kernel, out_shape=(jax.ShapeDtypeStruct(own.shape, jn...  49.7 us
    ppermute x14, starting transfers between devices, swapped(): return lax.ppermute(shard, axis, pairs)  24.5 us
    pallas_call x1, Pallas kernels, grid_step(): pl.pallas_call(functools.partial(grid_kernel, base), out_shape=(jax.Shape...  12.9 us
    pallas_call x1, Pallas kernels, sources_of(): pl.pallas_call(sources_kernel, out_shape=(*[jax.ShapeDtypeStruct(ions.sha...  4.44 us
    pallas_call x1, Pallas kernels, prepare(): pl.pallas_call(prepare_kernel, out_shape=(jax.ShapeDtypeStruct(pair_dir.s...  4.23 us
    pallas_call x1, Pallas kernels, gather_forces(): pl.pallas_call(gather_forces_kernel, out_shape=jax.ShapeDtypeStruct((3, c...  3.33 us
    ppermute x14, waiting for transfers between devices, swapped(): return lax.ppermute(shard, axis, pairs)  3.08 us
    unnamed x30, local copies, waits for them, and re-layouts  2.83 us
  transfers between devices with their start and end apart: 14, of which 1 were waited for; matrix products, arithmetic and copies ran while one was open for 0% of the time, Pallas kernels for 63%

profile of v17, /device:TPU:13, one launch (start us, length us, event | category | flops | bytes accessed | tf_op | source)
XLA Modules:
  0.0 106.7 jit_solution(13950192899080021934)
XLA Ops:
  0.6 4.2 %prepare.1 = (s32[8,128]{1,0:T(8,128)}, f32[256,4,128]{2,1,0:T(4,128)}, f32[256,128]{1,0:T(8,128)}, f32[128,128]{1,0:T(8,128)}, f32[128,128]{1,0:T(8,128)}, /*in...) custom-call(s32[256]{0:T(256)} %fill_ref.1, ...), custom_call_target="tpu_custom_call" | custom-call | tf_op jit(solution)/shard_map/prepare/pallas_call | solution.py:400
  4.9 0.7 collective-permute-start
  5.6 3.1 %collective-permute-start.1 = (f32[128,128]{1,0:T(8,128)}, f32[128,128]{1,0:T(8,128)S(1)}, u32[]{:S(2)}, u32[]{:S(2)}) collective-permute-start(f32[128,128]{1,0:T(8,128)} %get-tuple-element.43), channel_id=1, source_target_pairs={{1,2},{2,1},{3,4},{4,3},{5,6},{6,5},{9,10},{10,9},{11,12},{12,11},... | collective-permute-start | bytes 196616 | tf_op jit(solution)/shard_map/ppermute | solution.py:67
  8.7 0.2 collective-permute-start.2
  9.0 3.0 %collective-permute-start.3 = (f32[128,128]{1,0:T(8,128)}, f32[128,128]{1,0:T(8,128)S(1)}, u32[]{:S(2)}, u32[]{:S(2)}) collective-permute-start(f32[128,128]{1,0:T(8,128)} %get-tuple-element.45), channel_id=1, source_target_pairs={{2,4},{3,5},{4,2},{5,3},{10,12},{11,13},{12,10},{13,11},{18,20},{1... | collective-permute-start | bytes 196616 | tf_op jit(solution)/shard_map/ppermute | solution.py:67
  12.0 1.3 %collective-permute-start.4 = (f32[128,128]{1,0:T(8,128)}, f32[128,128]{1,0:T(8,128)S(1)}, u32[]{:S(2)}, u32[]{:S(2)}) collective-permute-start(f32[128,128]{1,0:T(8,128)} %get-tuple-element.46), channel_id=1, source_target_pairs={{0,8},{8,0},{16,24},{24,16},{1,9},{9,1},{17,25},{25,17},{2,10},{10... | collective-permute-start | bytes 196616 | tf_op jit(solution)/shard_map/ppermute | solution.py:67
  13.3 0.0 collective-permute-done.refs_5_
  13.3 2.1 %collective-permute-start.5 = (f32[128,128]{1,0:T(8,128)}, f32[128,128]{1,0:T(8,128)S(1)}, u32[]{:S(2)}, u32[]{:S(2)}) collective-permute-start(f32[128,128]{1,0:T(8,128)} %get-tuple-element.47), channel_id=1, source_target_pairs={{8,16},{16,8},{9,17},{17,9},{10,18},{18,10},{11,19},{19,11},{12,20... | collective-permute-start | bytes 196616 | tf_op jit(solution)/shard_map/ppermute | solution.py:67
  15.4 0.0 copy-start.5
  15.4 0.0 copy-start.7
  15.4 0.0 copy-start.8
  15.4 0.0 copy-start.9
  15.4 0.0 copy-start.10
  15.5 4.4 %sources.1 = (f32[16,32,256]{2,1,0:T(8,128)}, f32[16,32,256]{2,1,0:T(8,128)}, f32[28,32,128]{2,1,0:T(8,128)}, f32[28,32,128]{2,1,0:T(8,128)}) custom-call(s32[256]{0:T(256)} %refs_0_.4, s32[1,256]{1,0:T(1,128)} %bitcast.25, f32[256,128]{1,0:T(8,128)} %get-tuple-element.48.masked_hbm.refs_1_, f32[16,32,256]{2,1,0:T(8,128)} %refs_5_.1, ...), custom_call_target="tpu_custom_call" | custom-call | flops 20000000 | bytes 4194304 | tf_op jit(solution)/shard_map/sources/pallas_call | solution.py:506
  19.9 0.0 collective-permute-done.1.refs_6_
  19.9 0.0 collective-permute-done.2.refs_7_
  19.9 0.0 collective-permute-done.3.refs_8_
  19.9 0.0 collective-permute-done.4.refs_9_
  19.9 0.0 collective-permute-done.5.refs_10_
  19.9 0.0 copy-start.14
  20.0 0.0 copy-start.13
  20.0 0.1 collective-permute-start.6
  20.0 4.1 %collective-permute-start.7 = (f32[28,32,128]{2,1,0:T(8,128)}, f32[28,32,128]{2,1,0:T(8,128)S(1)}, u32[]{:S(2)}, u32[]{:S(2)}) collective-permute-start(f32[28,32,128]{2,1,0:T(8,128)} %get-tuple-element.62), channel_id=1, source_target_pairs={{8,16},{16,8},{9,17},{17,9},{10,18},{18,10},{11,19},{19,11},{12,20... | collective-permute-start | bytes 1376264 | tf_op jit(solution)/shard_map/ppermute | solution.py:67
  24.1 0.0 copy-done.5
  24.1 0.0 copy-done.7
  24.2 0.0 copy-done.8
  24.2 0.0 copy-done.9
  24.2 0.0 copy-done.10
  24.2 0.0 copy-done.14
  24.2 0.0 copy-done.13
  24.2 0.0 copy-start
  24.2 0.0 copy-start.1
  24.2 49.7 %pair_forces.1 = (f32[1024,128]{1,0:T(8,128)S(1)}, f32[128,128]{1,0:T(8,128)S(1)}, f32[128,128]{1,0:T(8,128)S(1)}, f32[128,128]{1,0:T(8,128)S(1)}, f32[128,128]{...) custom-call(s32[1024]{0:T(1024)S(1)} %copy-done.13, s32[1024]{0:T(1024)S(1)} %bitcast.26, ...), custom_call_target="tpu_custom_call" | custom-call | flops 335544320 | bytes 4194304 | tf_op jit(solution)/shard_map/pair_forces/pallas_call | solution.py:311
  74.0 0.0 collective-permute-done.6.refs_4_.refs_8_
  74.0 0.0 collective-permute-done.7.refs_5_.refs_9_
  74.0 0.0 copy-done
  74.0 0.0 copy-done.1
  74.0 0.0 copy-start.2
  74.0 1.0 copy-done.2
  75.1 0.0 copy-start.4
  75.1 1.0 copy-done.4
  76.1 0.0 copy-start.3
  76.1 0.0 copy-start.6
  76.1 0.6 pack_rows.1
  76.8 2.1 %collective-permute-start.8 = (f32[960,128]{1,0:T(8,128)S(1)}, f32[960,128]{1,0:T(8,128)S(1)}, u32[]{:S(2)}, u32[]{:S(2)}) collective-permute-start(f32[960,128]{1,0:T(8,128)S(1)} %get-tuple-element.65), channel_id=1, source_target_pairs={{0,1},{1,0},{2,3},{3,2},{4,5},{5,4},{6,7},{7,6},{8,9},{9,8},{10,11... | collective-permute-start | bytes 1474568 | tf_op jit(solution)/shard_map/ppermute | solution.py:67
  78.9 1.9 %collective-permute-start.9 = (f32[960,128]{1,0:T(8,128)S(1)}, f32[960,128]{1,0:T(8,128)S(1)}, u32[]{:S(2)}, u32[]{:S(2)}) collective-permute-start(f32[960,128]{1,0:T(8,128)S(1)} %get-tuple-element.66), channel_id=1, source_target_pairs={{1,2},{2,1},{3,4},{4,3},{5,6},{6,5},{9,10},{10,9},{11,12},{12,11},... | collective-permute-start | bytes 1474568 | tf_op jit(solution)/shard_map/ppermute | solution.py:67
  80.8 1.4 %collective-permute-start.10 = (f32[128,128]{1,0:T(8,128)S(1)}, f32[128,128]{1,0:T(8,128)S(1)}, u32[]{:S(2)}, u32[]{:S(2)}) collective-permute-start(f32[128,128]{1,0:T(8,128)S(1)} %get-tuple-element.69), channel_id=1, source_target_pairs={{0,2},{1,3},{2,0},{3,1},{4,6},{5,7},{6,4},{7,5},{8,10},{9,11},{10,... | collective-permute-start | bytes 196616 | tf_op jit(solution)/shard_map/ppermute | solution.py:67
  82.2 1.9 %collective-permute-start.11 = (f32[128,128]{1,0:T(8,128)S(1)}, f32[128,128]{1,0:T(8,128)S(1)}, u32[]{:S(2)}, u32[]{:S(2)}) collective-permute-start(f32[128,128]{1,0:T(8,128)S(1)} %get-tuple-element.70), channel_id=1, source_target_pairs={{2,4},{3,5},{4,2},{5,3},{10,12},{11,13},{12,10},{13,11},{18,20},{1... | collective-permute-start | bytes 196616 | tf_op jit(solution)/shard_map/ppermute | solution.py:67
  84.1 0.0 copy-start.12
  84.2 0.1 collective-permute-start.12
  84.2 0.0 collective-permute-done.8.refs_6_
  84.2 2.4 %collective-permute-start.13 = (f32[128,128]{1,0:T(8,128)S(1)}, f32[128,128]{1,0:T(8,128)S(1)}, u32[]{:S(2)}, u32[]{:S(2)}) collective-permute-start(f32[128,128]{1,0:T(8,128)S(1)} %get-tuple-element.72), channel_id=1, source_target_pairs={{8,16},{16,8},{9,17},{17,9},{10,18},{18,10},{11,19},{19,11},{12,20... | collective-permute-start | bytes 196616 | tf_op jit(solution)/shard_map/ppermute | solution.py:67
  86.7 3.0 %collective-permute-done.9.refs_7_ = f32[960,128]{1,0:T(8,128)S(1)} collective-permute-done((f32[960,128]{1,0:T(8,128)S(1)}, f32[960,128]{1,0:T(8,128)S(1)}, u32[]{:S(2)}, u32[]{:S(2)}) %collective-permute-start.9) | collective-permute-done | bytes 491552 | tf_op jit(solution)/shard_map/ppermute | solution.py:67
  89.7 0.0 copy-done.3
  89.7 0.0 copy-done.6
  89.7 0.0 copy-done.12
  89.7 12.9 %grid_step.1 = (f32[16,32,256]{2,1,0:T(8,128)}, f32[16,32,256]{2,1,0:T(8,128)}, f32[1024,128]{1,0:T(8,128)S(1)}) custom-call(s32[256]{0:T(256)S(1)} %copy-done.12, f32[256,128]{1,0:T(8,128)S(1)} %copy-done.6, f32[16,32,256]{2,1,0:T(8,128)S(1)} %copy-done, f32[16,32,256]{2,1,0:T(8,128)S(1)} %copy-done.3, f32[16,32,256]{2,1,0:T(8,128)S(1)} %copy-done.4, ...), custom_call_target="tpu_custom_call" | custom-call | flops 31948800 | bytes 8388608 | tf_op jit(solution)/shard_map/grid_step/pallas_call | solution.py:807
  102.6 0.0 collective-permute-done.10
  102.6 0.0 collective-permute-done.11
  102.6 0.0 collective-permute-done.12
  102.7 0.0 collective-permute-done.13
  102.7 0.0 copy-start.11
  102.7 0.7 copy-done.11
  103.4 3.3 %gather_forces.1 = f32[3,32768]{1,0:T(4,128)} custom-call(s32[7,32]{1,0:T(8,128)S(1)} %copy-done.11, f32[256,4,128]{2,1,0:T(4,128)S(1)} %bitcast.17, f32[256,4,128]{2,1,0:T(4,128)S(1)} %bitcast.19, f32[32,4,128]{2,1,0:T(4,128)S(1)} %bitcast.20, f32[240,4,128]{2,1,0:T(4,128)S(1)} %bitcast.15, f32[240,4,128]{2,1,0:T(4,128)S(1)} %bitcast.16, ...), custom_call_target="tpu_custom_call" | custom-call | tf_op jit(solution)/shard_map/gather_forces/pallas_call | solution.py:871
Async XLA Ops:
  4.9 8.4 %collective-permute-start = (f32[128,128]{1,0:T(8,128)}, f32[128,128]{1,0:T(8,128)S(1)}, u32[]{:S(2)}, u32[]{:S(2)}) collective-permute-start(f32[128,128]{1,0:T(8,128)} %get-tuple-element.42), channel_id=1, source_target_pairs={{0,1},{1,0},{2,3},{3,2},{4,5},{5,4},{6,7},{7,6},{8,9},{9,8},{10,11... | collective-permute-start | bytes 196616 | tf_op jit(solution)/shard_map/ppermute | solution.py:67
  5.6 14.3 %collective-permute-start.1 = (f32[128,128]{1,0:T(8,128)}, f32[128,128]{1,0:T(8,128)S(1)}, u32[]{:S(2)}, u32[]{:S(2)}) collective-permute-start(f32[128,128]{1,0:T(8,128)} %get-tuple-element.43), channel_id=1, source_target_pairs={{1,2},{2,1},{3,4},{4,3},{5,6},{6,5},{9,10},{10,9},{11,12},{12,11},... | collective-permute-start | bytes 196616 | tf_op jit(solution)/shard_map/ppermute | solution.py:67
  8.7 11.2 %collective-permute-start.2 = (f32[128,128]{1,0:T(8,128)}, f32[128,128]{1,0:T(8,128)S(1)}, u32[]{:S(2)}, u32[]{:S(2)}) collective-permute-start(f32[128,128]{1,0:T(8,128)} %get-tuple-element.44), channel_id=1, source_target_pairs={{0,2},{1,3},{2,0},{3,1},{4,6},{5,7},{6,4},{7,5},{8,10},{9,11},{10,... | collective-permute-start | bytes 196616 | tf_op jit(solution)/shard_map/ppermute | solution.py:67
  9.0 11.0 %collective-permute-start.3 = (f32[128,128]{1,0:T(8,128)}, f32[128,128]{1,0:T(8,128)S(1)}, u32[]{:S(2)}, u32[]{:S(2)}) collective-permute-start(f32[128,128]{1,0:T(8,128)} %get-tuple-element.45), channel_id=1, source_target_pairs={{2,4},{3,5},{4,2},{5,3},{10,12},{11,13},{12,10},{13,11},{18,20},{1... | collective-permute-start | bytes 196616 | tf_op jit(solution)/shard_map/ppermute | solution.py:67
  12.0 7.9 %collective-permute-start.4 = (f32[128,128]{1,0:T(8,128)}, f32[128,128]{1,0:T(8,128)S(1)}, u32[]{:S(2)}, u32[]{:S(2)}) collective-permute-start(f32[128,128]{1,0:T(8,128)} %get-tuple-element.46), channel_id=1, source_target_pairs={{0,8},{8,0},{16,24},{24,16},{1,9},{9,1},{17,25},{25,17},{2,10},{10... | collective-permute-start | bytes 196616 | tf_op jit(solution)/shard_map/ppermute | solution.py:67
  13.3 6.7 %collective-permute-start.5 = (f32[128,128]{1,0:T(8,128)}, f32[128,128]{1,0:T(8,128)S(1)}, u32[]{:S(2)}, u32[]{:S(2)}) collective-permute-start(f32[128,128]{1,0:T(8,128)} %get-tuple-element.47), channel_id=1, source_target_pairs={{8,16},{16,8},{9,17},{17,9},{10,18},{18,10},{11,19},{19,11},{12,20... | collective-permute-start | bytes 196616 | tf_op jit(solution)/shard_map/ppermute | solution.py:67
  15.4 8.7 %copy-start.5 = (f32[256,4,128]{2,1,0:T(4,128)S(1)}, f32[256,4,128]{2,1,0:T(4,128)}, u32[]{:S(2)}) copy-start(f32[256,4,128]{2,1,0:T(4,128)} %get-tuple-element.40) | copy-start | bytes 1572868
  15.4 8.7 %copy-start.7 = (bf16[128,1024]{1,0:T(8,128)(2,1)S(1)}, bf16[128,1024]{1,0:T(8,128)(2,1)}, u32[]{:S(2)}) copy-start(bf16[128,1024]{1,0:T(8,128)(2,1)} %constant.6.clone.refs_0_) | copy-start | bytes 786436
  15.4 8.7 %copy-start.8 = (bf16[256,128]{1,0:T(8,128)(2,1)S(1)}, bf16[256,128]{1,0:T(8,128)(2,1)}, u32[]{:S(2)}) copy-start(bf16[256,128]{1,0:T(8,128)(2,1)} %constant.7.clone.refs_1_) | copy-start | bytes 196612
  15.4 8.7 %copy-start.9 = (f32[128,128]{1,0:T(8,128)S(1)}, f32[128,128]{1,0:T(8,128)}, u32[]{:S(2)}) copy-start(f32[128,128]{1,0:T(8,128)} %get-tuple-element.51.refs_4_) | copy-start | bytes 196612
  15.4 8.7 %copy-start.10 = (bf16[128,128]{1,0:T(8,128)(2,1)S(1)}, bf16[128,128]{1,0:T(8,128)(2,1)}, u32[]{:S(2)}) copy-start(bf16[128,128]{1,0:T(8,128)(2,1)} %constant.8.clone.refs_2_) | copy-start | bytes 98308
  19.9 4.2 %copy-start.14 = (s32[8,128]{1,0:T(8,128)S(1)}, s32[8,128]{1,0:T(8,128)}, u32[]{:S(2)}) copy-start(s32[8,128]{1,0:T(8,128)} %get-tuple-element.39) | copy-start | bytes 12292
  20.0 4.2 %copy-start.13 = (s32[1024]{0:T(1024)S(1)}, s32[1024]{0:T(1024)}, u32[]{:S(2)}) copy-start(s32[1024]{0:T(1024)} %own_rows_ref.1) | copy-start | bytes 12292
  20.0 54.0 %collective-permute-start.6 = (f32[28,32,128]{2,1,0:T(8,128)}, f32[28,32,128]{2,1,0:T(8,128)S(1)}, u32[]{:S(2)}, u32[]{:S(2)}) collective-permute-start(f32[28,32,128]{2,1,0:T(8,128)} %get-tuple-element.61), channel_id=1, source_target_pairs={{0,8},{8,0},{16,24},{24,16},{1,9},{9,1},{17,25},{25,17},{2,10},{10... | collective-permute-start | bytes 1376264 | tf_op jit(solution)/shard_map/ppermute | solution.py:67
  20.0 53.9 %collective-permute-start.7 = (f32[28,32,128]{2,1,0:T(8,128)}, f32[28,32,128]{2,1,0:T(8,128)S(1)}, u32[]{:S(2)}, u32[]{:S(2)}) collective-permute-start(f32[28,32,128]{2,1,0:T(8,128)} %get-tuple-element.62), channel_id=1, source_target_pairs={{8,16},{16,8},{9,17},{17,9},{10,18},{18,10},{11,19},{19,11},{12,20... | collective-permute-start | bytes 1376264 | tf_op jit(solution)/shard_map/ppermute | solution.py:67
  24.2 49.8 %copy-start = (f32[16,32,256]{2,1,0:T(8,128)S(1)}, f32[16,32,256]{2,1,0:T(8,128)}, u32[]{:S(2)}) copy-start(f32[16,32,256]{2,1,0:T(8,128)} %refs_2_.2) | copy-start | bytes 1572868
  24.2 49.8 %copy-start.1 = (f32[16,32,256]{2,1,0:T(8,128)S(1)}, f32[16,32,256]{2,1,0:T(8,128)}, u32[]{:S(2)}) copy-start(f32[16,32,256]{2,1,0:T(8,128)} %refs_5_.1) | copy-start | bytes 1572868
  74.0 1.0 copy-start.2
  75.1 1.0 copy-start.4
  76.1 13.6 %copy-start.3 = (f32[16,32,256]{2,1,0:T(8,128)S(1)}, f32[16,32,256]{2,1,0:T(8,128)}, u32[]{:S(2)}) copy-start(f32[16,32,256]{2,1,0:T(8,128)} %get-tuple-element.59.refs_1_.refs_3_) | copy-start | bytes 1572868
  76.1 13.6 %copy-start.6 = (f32[256,128]{1,0:T(8,128)S(1)}, f32[256,128]{1,0:T(8,128)}, u32[]{:S(2)}) copy-start(f32[256,128]{1,0:T(8,128)} %get-tuple-element.48.masked_hbm.refs_1_) | copy-start | bytes 393220
  76.8 7.5 %collective-permute-start.8 = (f32[960,128]{1,0:T(8,128)S(1)}, f32[960,128]{1,0:T(8,128)S(1)}, u32[]{:S(2)}, u32[]{:S(2)}) collective-permute-start(f32[960,128]{1,0:T(8,128)S(1)} %get-tuple-element.65), channel_id=1, source_target_pairs={{0,1},{1,0},{2,3},{3,2},{4,5},{5,4},{6,7},{7,6},{8,9},{9,8},{10,11... | collective-permute-start | bytes 1474568 | tf_op jit(solution)/shard_map/ppermute | solution.py:67
  78.9 10.8 %collective-permute-start.9 = (f32[960,128]{1,0:T(8,128)S(1)}, f32[960,128]{1,0:T(8,128)S(1)}, u32[]{:S(2)}, u32[]{:S(2)}) collective-permute-start(f32[960,128]{1,0:T(8,128)S(1)} %get-tuple-element.66), channel_id=1, source_target_pairs={{1,2},{2,1},{3,4},{4,3},{5,6},{6,5},{9,10},{10,9},{11,12},{12,11},... | collective-permute-start | bytes 1474568 | tf_op jit(solution)/shard_map/ppermute | solution.py:67
  80.8 21.8 %collective-permute-start.10 = (f32[128,128]{1,0:T(8,128)S(1)}, f32[128,128]{1,0:T(8,128)S(1)}, u32[]{:S(2)}, u32[]{:S(2)}) collective-permute-start(f32[128,128]{1,0:T(8,128)S(1)} %get-tuple-element.69), channel_id=1, source_target_pairs={{0,2},{1,3},{2,0},{3,1},{4,6},{5,7},{6,4},{7,5},{8,10},{9,11},{10,... | collective-permute-start | bytes 196616 | tf_op jit(solution)/shard_map/ppermute | solution.py:67
  82.2 20.4 %collective-permute-start.11 = (f32[128,128]{1,0:T(8,128)S(1)}, f32[128,128]{1,0:T(8,128)S(1)}, u32[]{:S(2)}, u32[]{:S(2)}) collective-permute-start(f32[128,128]{1,0:T(8,128)S(1)} %get-tuple-element.70), channel_id=1, source_target_pairs={{2,4},{3,5},{4,2},{5,3},{10,12},{11,13},{12,10},{13,11},{18,20},{1... | collective-permute-start | bytes 196616 | tf_op jit(solution)/shard_map/ppermute | solution.py:67
  84.1 5.6 %copy-start.12 = (s32[256]{0:T(256)S(1)}, s32[256]{0:T(256)}, u32[]{:S(2)}) copy-start(s32[256]{0:T(256)} %refs_0_.4) | copy-start | bytes 3076
  84.2 18.5 %collective-permute-start.12 = (f32[128,128]{1,0:T(8,128)S(1)}, f32[128,128]{1,0:T(8,128)S(1)}, u32[]{:S(2)}, u32[]{:S(2)}) collective-permute-start(f32[128,128]{1,0:T(8,128)S(1)} %get-tuple-element.71), channel_id=1, source_target_pairs={{0,8},{8,0},{16,24},{24,16},{1,9},{9,1},{17,25},{25,17},{2,10},{10... | collective-permute-start | bytes 196616 | tf_op jit(solution)/shard_map/ppermute | solution.py:67
  84.2 18.4 %collective-permute-start.13 = (f32[128,128]{1,0:T(8,128)S(1)}, f32[128,128]{1,0:T(8,128)S(1)}, u32[]{:S(2)}, u32[]{:S(2)}) collective-permute-start(f32[128,128]{1,0:T(8,128)S(1)} %get-tuple-element.72), channel_id=1, source_target_pairs={{8,16},{16,8},{9,17},{17,9},{10,18},{18,10},{11,19},{19,11},{12,20... | collective-permute-start | bytes 196616 | tf_op jit(solution)/shard_map/ppermute | solution.py:67
  102.7 0.7 copy-start.11

commit v18 on v17

--- a/solution.py
+++ b/solution.py
@@ -527,27 +527,19 @@
 
 
 def pack_rows_kernel(*refs):
-    field_hbms, edge_hbms, reaction_hbms, out_refs = (refs[:4], refs[4:6], refs[6:8], refs[8:10])
-    near_refs, edge_refs, sems = (refs[10:14], refs[14:16], refs[16])
-    cells_x, cells_y, _ = field_hbms[0].shape
-    base = reaction_hbms[0].shape[0]
+    field_refs, edge_refs, reaction_refs, out_refs = (refs[:4], refs[4:6], refs[6:8], refs[8:10])
+    cells_x, cells_y, _ = field_refs[0].shape
+    base = reaction_refs[0].shape[0]
     ups = upward()
-    moves = [
-        (reaction, out_ref.at[0:base])
-        for reaction, out_ref in zip(reaction_hbms, out_refs, strict=True)
-    ]
-    for source, target in zip(field_hbms + edge_hbms, near_refs + edge_refs, strict=True):
-        moves.append((source.at[:, 0:8], target.at[0]))
-        moves.append((source.at[:, cells_y - 8 : cells_y], target.at[1]))
-    for copy in start_copies(moves, sems):
-        copy.wait()
+    for reaction_ref, out_ref in zip(reaction_refs, out_refs, strict=True):
+        out_ref[0:base, :] = reaction_ref[...]
 
     def fill(out_ref, after):
         for field, width in enumerate(HALO_WIDTHS):
             offset = sum(HALO_WIDTHS[:field])
-            rows = slice(8 - width, 8) if after else slice(0, width)
+            rows = slice(cells_y - width, cells_y) if after else slice(0, width)
             for index in range(cells_x):
-                value = near_refs[field][after, index, rows, :]
+                value = field_refs[field][index, rows, :]
                 for half in range(2):
                     at = base + ((DEPTH + index) * 2 + half) * 16 + offset
                     out_ref[at : at + width, :] = value[:, 128 * half : 128 * half + 128]
@@ -559,7 +551,7 @@
                     plane = (DEPTH - width) + higher * (cells_x + width) + step
                     for half in range(2):
                         at = pl.ds(base + (plane * 2 + half) * 16 + offset, width)
-                        out_ref[at, :] = edge_ref[after, 2 * (offset + step) + half, rows, :]
+                        out_ref[at, :] = edge_ref[2 * (offset + step) + half, rows, :]
 
     for up in range(2):
 
@@ -571,19 +563,14 @@
 
 def pack_rows(fields, edges, reactions):
     vmem = pl.BlockSpec(memory_space=pltpu.VMEM)
-    cells_x, _, cells_z = fields[0].shape
+    cells_x = fields[0].shape[0]
     rows = reactions[0].shape[0] + (cells_x + 2 * DEPTH) * 32
     shape = jax.ShapeDtypeStruct((rows, 128), jnp.float32)
     return pl.pallas_call(
         pack_rows_kernel,
         out_shape=(shape, shape),
-        in_specs=[pl.BlockSpec(memory_space=pl.ANY)] * 8,
+        in_specs=[vmem] * 8,
         out_specs=(vmem, vmem),
-        scratch_shapes=[
-            *[pltpu.VMEM((2, cells_x, 8, cells_z), jnp.float32)] * 4,
-            *[pltpu.VMEM((2, edges[0].shape[0], 8, 128), jnp.float32)] * 2,
-            pltpu.SemaphoreType.DMA((14,)),
-        ],
         compiler_params=pltpu.CompilerParams(vmem_limit_bytes=ROOMY_LIMIT),
         name="pack_rows",
     )(*fields, *edges, *reactions)
@@ -610,32 +597,21 @@
 
 
 def grid_kernel(base, *refs):
-    cell_ref, masked_hbm = refs[:2]
-    hbm_refs, edge_hbms = (refs[2:6], refs[8:10])
+    cell_ref, masked_ref = refs[:2]
+    field_refs, rims, edge_refs = (refs[2:6], refs[6:8], refs[8:10])
     potential_ref, next_ref, force_ref = refs[10:13]
     start_ref, inverse_ref, source_ref, ion_ref = refs[13:17]
     updates, resids, final_ref, pick_refs = (refs[17:20], refs[20:22], refs[22], refs[23:26])
-    rim_ref, field_refs, masked_ref, sems = (refs[26], refs[27:31], refs[31], refs[32])
-    edge_refs = refs[33:35]
+    rim_ref = refs[26]
     cells_x, cells_y, _ = field_refs[0].shape
     rows = line_rows(cells_y)
-    inner = cells_y + 2 * DEPTH - 2
     clusters = masked_ref.shape[0]
     ups = upward()
     size = (cells_x + 2 * DEPTH) * 32
-    moves = [
-        (rim.at[base : base + size], rim_ref.at[pl.ds(pl.multiple_of(side * size, size), size)])
-        for rim, side in zip(refs[6:8], (ups[0], 1 - ups[0]), strict=True)
-    ]
-    moves += zip(hbm_refs, field_refs, strict=True)
-    moves += zip(edge_hbms, edge_refs, strict=True)
-    moves.append((masked_hbm, masked_ref))
-    copies = start_copies(moves, sems)
+    for rim, side in zip(rims, (ups[0], 1 - ups[0]), strict=True):
+        rim_ref[pl.ds(pl.multiple_of(side * size, size), size), :] = rim[base : base + size, :]
     extended = (start_ref, inverse_ref, source_ref, ion_ref)
-    for copy in copies[:2]:
-        copy.wait()
     for field, target_ref in enumerate(extended):
-        copies[2 + field].wait()
 
         def fill(index, _, field=field, target_ref=target_ref):
             plane = field_refs[field][index]
@@ -645,8 +621,6 @@
             return 0
 
         lax.fori_loop(0, cells_x, fill, 0, unroll=4)
-    for copy in copies[6:]:
-        copy.wait()
     for field, target_ref in enumerate(extended):
         width = HALO_WIDTHS[field]
         for phase, edge_ref in enumerate(edge_refs):
@@ -662,27 +636,26 @@
 
             lax.fori_loop(0, width, fill_edge, 0, unroll=True)
 
-    def beyond(values):
-        lane = lax.broadcasted_iota(jnp.int32, values[0].shape, 1)
-        right = [pltpu.roll(value, 127, 1) for value in values]
-        left = [pltpu.roll(value, 1, 1) for value in values]
-        above = [jnp.where(lane == 127, right[1], right[0]), jnp.where(lane == 127, 0.0, right[1])]
-        below = [jnp.where(lane == 0, 0.0, left[0]), jnp.where(lane == 0, left[0], left[1])]
+    lane = lax.broadcasted_iota(jnp.int32, (2 * rows, 128), 1)
+    blank = jnp.zeros((rows, 128), jnp.float32)
+
+    def beyond(value):
+        right = pltpu.roll(value, 127, 1)
+        left = pltpu.roll(value, 1, 1)
+        above = jnp.where(lane == 127, jnp.concatenate([right[rows:], blank], axis=0), right)
+        below = jnp.where(lane == 0, jnp.concatenate([blank, left[:rows]], axis=0), left)
         return (below, above)
 
-    def wide(plane, half, shift=0):
-        return pl.ds((plane * 2 + half) * rows + 1 + shift, inner)
+    def whole(plane, shift=0):
+        return pl.ds(plane * 2 * rows + shift, 2 * rows)
 
     def around(ref, plane):
-        here = [ref[wide(plane, half), :] for half in range(2)]
+        here = ref[whole(plane), :]
         below, above = beyond(here)
-        sums = [
-            (ref[wide(plane - 1, half), :] + ref[wide(plane + 1, half), :])
-            + (ref[wide(plane, half, -1), :] + ref[wide(plane, half, 1), :])
-            + (below[half] + above[half])
-            for half in range(2)
-        ]
-        return (here, sums)
+        sums = (ref[whole(plane - 1), :] + ref[whole(plane + 1), :]) + (
+            ref[whole(plane, -1), :] + ref[whole(plane, 1), :]
+        )
+        return (here, sums + (below + above))
 
     middle = 0.5 * (highest_eig + lowest_eig)
     spread = 0.5 * (highest_eig - lowest_eig)
@@ -690,9 +663,8 @@
 
     def sweep_first(plane, _):
         here, sums = around(start_ref, plane)
-        for half in range(2):
-            at = wide(plane, half)
-            updates[0][at, :] = source_ref[at, :] - here[half] + inverse_ref[at, :] * sums[half]
+        at = whole(plane)
+        updates[0][at, :] = source_ref[at, :] - here + inverse_ref[at, :] * sums
         return 0
 
     lax.fori_loop(1, cells_x + 2 * DEPTH - 1, sweep_first, 0, unroll=2)
@@ -706,53 +678,48 @@
 
         def sweep(plane, _, turn=turn, keep=keep, gain=gain):
             here, sums = around(updates[turn - 1], plane)
-            for half in range(2):
-                at = wide(plane, half)
-                resid = inverse_ref[at, :] * sums[half]
-                if turn > 1:
-                    resid = resid + (resids[turn - 2][at, :] - here[half])
-                update = keep * here[half] + gain * resid
-                if turn + 1 < SWEEPS:
-                    resids[turn - 1][at, :] = resid
-                    updates[turn][at, :] = update
-                else:
-                    final_ref[at, :] = (start_ref[at, :] + updates[0][at, :]) + (
-                        (updates[1][at, :] + here[half]) + update
-                    )
+            at = whole(plane)
+            resid = inverse_ref[at, :] * sums
+            if turn > 1:
+                resid = resid + (resids[turn - 2][at, :] - here)
+            update = keep * here + gain * resid
+            if turn + 1 < SWEEPS:
+                resids[turn - 1][at, :] = resid
+                updates[turn][at, :] = update
+            else:
+                final_ref[at, :] = (start_ref[at, :] + updates[0][at, :]) + (
+                    (updates[1][at, :] + here) + update
+                )
             return 0
 
         first = 1 + turn
         lax.fori_loop(first, cells_x + 2 * DEPTH - first, sweep, 0, unroll=2)
 
-    def local(plane, half, shift=0):
-        return pl.ds((plane * 2 + half) * rows + DEPTH + shift, cells_y)
-
     def advance(index, _):
         plane = index + DEPTH
-        pots = [final_ref[local(plane, half), :] for half in range(2)]
-        ions = [ion_ref[local(plane, half), :] for half in range(2)]
-        pot_below, pot_above = beyond(pots)
-        ion_below, ion_above = beyond(ions)
+        pot = final_ref[whole(plane, DEPTH), :]
+        ion = ion_ref[whole(plane, DEPTH), :]
+        steps = [
+            (final_ref[at, :], ion_ref[at, :])
+            for at in (
+                whole(plane - 1, DEPTH),
+                whole(plane + 1, DEPTH),
+                whole(plane, DEPTH - 1),
+                whole(plane, DEPTH + 1),
+            )
+        ]
+        steps += zip(beyond(pot), beyond(ion), strict=True)
+        total = 0.0
+        for low, high in zip(steps[0::2], steps[1::2], strict=True):
+            total = total + (
+                face_flux(pot, high[0], ion, high[1]) - face_flux(low[0], pot, low[1], ion)
+            )
+        result = ion - time_step * total
         for half in range(2):
-            pot, ion = (pots[half], ions[half])
-            steps = [
-                (final_ref[at, :], ion_ref[at, :])
-                for at in (
-                    local(plane - 1, half),
-                    local(plane + 1, half),
-                    local(plane, half, -1),
-                    local(plane, half, 1),
-                )
-            ]
-            steps += [(pot_below[half], ion_below[half]), (pot_above[half], ion_above[half])]
-            total = 0.0
-            for low, high in zip(steps[0::2], steps[1::2], strict=True):
-                total = total + (
-                    face_flux(pot, high[0], ion, high[1]) - face_flux(low[0], pot, low[1], ion)
-                )
             lanes = slice(128 * half, 128 * half + 128)
-            next_ref[index, :, lanes] = ion - time_step * total
-            potential_ref[index, :, lanes] = pot
+            kept = slice(rows * half, rows * half + cells_y)
+            next_ref[index, :, lanes] = result[kept]
+            potential_ref[index, :, lanes] = pot[kept]
         return 0
 
     lax.fori_loop(0, cells_x, advance, 0)
@@ -811,14 +778,11 @@
             jax.ShapeDtypeStruct(fields[0].shape, jnp.float32),
             jax.ShapeDtypeStruct((clusters * 4, 128), jnp.float32),
         ),
-        in_specs=[smem] + [pl.BlockSpec(memory_space=pl.ANY)] * 9,
+        in_specs=[smem] + [vmem] * 9,
         out_specs=(vmem,) * 3,
         scratch_shapes=[pltpu.VMEM(block, jnp.float32)] * 10
         + [pltpu.VMEM((clusters, 128), jnp.float32)] * 3
-        + [pltpu.VMEM(((cells_x + 2 * DEPTH) * 64, 128), jnp.float32)]
-        + [pltpu.VMEM(field.shape, jnp.float32) for field in fields]
-        + [pltpu.VMEM(masked.shape, jnp.float32), pltpu.SemaphoreType.DMA((9,))]
-        + [pltpu.VMEM(edge.shape, jnp.float32) for edge in edges],
+        + [pltpu.VMEM(((cells_x + 2 * DEPTH) * 64, 128), jnp.float32)],
         compiler_params=pltpu.CompilerParams(vmem_limit_bytes=ROOMY_LIMIT),
         cost_estimate=pl.CostEstimate(
             flops=block[0] * block[1] * 100, bytes_accessed=8 << 20, transcendentals=0
@@ -828,19 +792,10 @@
 
 
 def gather_forces_kernel(send_index_ref, *refs):
-    fetched = len(SWAPS) + 3
-    out_ref, extra_ref = refs[fetched : fetched + 2]
-    sum_ref, field_ref, *back_refs = refs[fetched + 2 : -1]
-    copies = start_copies(
-        [
-            (source.at[0 : target.shape[0]], target)
-            for source, target in zip(refs[:fetched], refs[fetched + 2 : -1], strict=True)
-        ],
-        refs[-1],
-    )
-    extra_ref[...] = jnp.zeros_like(extra_ref)
-    for copy in copies:
-        copy.wait()
+    own_ref, field_ref, *back_refs = refs[:-3]
+    out_ref, sum_ref, extra_ref = refs[-3:]
+    sum_ref[...] = own_ref[...]
+    extra_ref[...] = field_ref[...]
     clusters = sum_ref.shape[0]
     slots = send_index_ref.shape[1]
     ups = upward()
@@ -857,7 +812,7 @@
     def write(step, _):
         for turn in range(8):
             cluster = step * 8 + turn
-            total = (sum_ref[cluster] + extra_ref[cluster]) + field_ref[cluster]
+            total = sum_ref[cluster] + extra_ref[cluster]
             out_ref[:, pl.ds(pl.multiple_of(cluster * 128, 128), 128)] = total[0:3]
         return 0
 
@@ -871,13 +826,9 @@
     return pl.pallas_call(
         gather_forces_kernel,
         out_shape=jax.ShapeDtypeStruct((3, clusters * 128), jnp.float32),
-        in_specs=[smem] + [pl.BlockSpec(memory_space=pl.ANY)] * (2 + len(backs)),
+        in_specs=[smem] + [vmem] * (2 + len(backs)),
         out_specs=vmem,
-        scratch_shapes=[
-            *[pltpu.VMEM(part.shape, jnp.float32) for part in (own, own, field)],
-            *[pltpu.VMEM((send_index.shape[1], 4, 128), jnp.float32)] * len(backs),
-            pltpu.SemaphoreType.DMA((2 + len(backs),)),
-        ],
+        scratch_shapes=[pltpu.VMEM(own.shape, jnp.float32)] * 2,
         compiler_params=pltpu.CompilerParams(vmem_limit_bytes=ROOMY_LIMIT),
         name="gather_forces",
     )(send_index, own, field, *backs)

time: 107 us -> 105 us (0.981)
  Pallas kernels: 75.3 us -> 73.2 us
where the time goes in v18:
time: 105 us
  Pallas kernels  73.2 us (70%)
  starting transfers between devices  24.5 us (23%)
  waiting for transfers between devices  3.04 us (3%)
  local copies, waits for them, and re-layouts  2.83 us (3%)
    pallas_call x1, Pallas kernels, pair_forces(): pl.pallas_call(pair_kernel, out_shape=(jax.ShapeDtypeStruct(own.shape, jn...  49.8 us
    ppermute x14, starting transfers between devices, swapped(): return lax.ppermute(shard, axis, pairs)  24.5 us
    pallas_call x1, Pallas kernels, grid_step(): pl.pallas_call(functools.partial(grid_kernel, base), out_shape=(jax.Shape...  12 us
    pallas_call x1, Pallas kernels, sources_of(): pl.pallas_call(sources_kernel, out_shape=(*[jax.ShapeDtypeStruct(ions.sha...  4.44 us
    pallas_call x1, Pallas kernels, prepare(): pl.pallas_call(prepare_kernel, out_shape=(jax.ShapeDtypeStruct(pair_dir.s...  4.23 us
    ppermute x14, waiting for transfers between devices, swapped(): return lax.ppermute(shard, axis, pairs)  3.04 us
    unnamed x30, local copies, waits for them, and re-layouts  2.83 us
    pallas_call x1, Pallas kernels, gather_forces(): pl.pallas_call(gather_forces_kernel, out_shape=jax.ShapeDtypeStruct((3, c...  2.6 us
  transfers between devices with their start and end apart: 14, of which 1 were waited for; matrix products, arithmetic and copies ran while one was open for 0% of the time, Pallas kernels for 63%

profile of v18, /device:TPU:13, one launch (start us, length us, event | category | flops | bytes accessed | tf_op | source)
XLA Modules:
  0.0 104.5 jit_solution(2943351798192562399)
XLA Ops:
  0.6 4.2 %prepare.1 = (s32[8,128]{1,0:T(8,128)}, f32[256,4,128]{2,1,0:T(4,128)}, f32[256,128]{1,0:T(8,128)}, f32[128,128]{1,0:T(8,128)}, f32[128,128]{1,0:T(8,128)}, /*in...) custom-call(s32[256]{0:T(256)} %fill_ref.1, ...), custom_call_target="tpu_custom_call" | custom-call | tf_op jit(solution)/shard_map/prepare/pallas_call | solution.py:400
  4.9 0.7 collective-permute-start
  5.6 3.1 %collective-permute-start.1 = (f32[128,128]{1,0:T(8,128)}, f32[128,128]{1,0:T(8,128)S(1)}, u32[]{:S(2)}, u32[]{:S(2)}) collective-permute-start(f32[128,128]{1,0:T(8,128)} %get-tuple-element.43), channel_id=1, source_target_pairs={{1,2},{2,1},{3,4},{4,3},{5,6},{6,5},{9,10},{10,9},{11,12},{12,11},... | collective-permute-start | bytes 196616 | tf_op jit(solution)/shard_map/ppermute | solution.py:67
  8.7 0.2 collective-permute-start.2
  9.0 3.0 %collective-permute-start.3 = (f32[128,128]{1,0:T(8,128)}, f32[128,128]{1,0:T(8,128)S(1)}, u32[]{:S(2)}, u32[]{:S(2)}) collective-permute-start(f32[128,128]{1,0:T(8,128)} %get-tuple-element.45), channel_id=1, source_target_pairs={{2,4},{3,5},{4,2},{5,3},{10,12},{11,13},{12,10},{13,11},{18,20},{1... | collective-permute-start | bytes 196616 | tf_op jit(solution)/shard_map/ppermute | solution.py:67
  12.0 1.3 %collective-permute-start.4 = (f32[128,128]{1,0:T(8,128)}, f32[128,128]{1,0:T(8,128)S(1)}, u32[]{:S(2)}, u32[]{:S(2)}) collective-permute-start(f32[128,128]{1,0:T(8,128)} %get-tuple-element.46), channel_id=1, source_target_pairs={{0,8},{8,0},{16,24},{24,16},{1,9},{9,1},{17,25},{25,17},{2,10},{10... | collective-permute-start | bytes 196616 | tf_op jit(solution)/shard_map/ppermute | solution.py:67
  13.3 0.0 collective-permute-done.refs_5_
  13.3 2.1 %collective-permute-start.5 = (f32[128,128]{1,0:T(8,128)}, f32[128,128]{1,0:T(8,128)S(1)}, u32[]{:S(2)}, u32[]{:S(2)}) collective-permute-start(f32[128,128]{1,0:T(8,128)} %get-tuple-element.47), channel_id=1, source_target_pairs={{8,16},{16,8},{9,17},{17,9},{10,18},{18,10},{11,19},{19,11},{12,20... | collective-permute-start | bytes 196616 | tf_op jit(solution)/shard_map/ppermute | solution.py:67
  15.4 0.0 copy-start.5
  15.4 0.0 copy-start.7
  15.4 0.0 copy-start.8
  15.4 0.0 copy-start.9
  15.4 0.0 copy-start.10
  15.5 4.4 %sources.1 = (f32[16,32,256]{2,1,0:T(8,128)}, f32[16,32,256]{2,1,0:T(8,128)}, f32[28,32,128]{2,1,0:T(8,128)}, f32[28,32,128]{2,1,0:T(8,128)}) custom-call(s32[256]{0:T(256)} %refs_0_.4, s32[1,256]{1,0:T(1,128)} %bitcast.25, f32[256,128]{1,0:T(8,128)} %get-tuple-element.48.masked_hbm.refs_1_, f32[16,32,256]{2,1,0:T(8,128)} %refs_5_.1, ...), custom_call_target="tpu_custom_call" | custom-call | flops 20000000 | bytes 4194304 | tf_op jit(solution)/shard_map/sources/pallas_call | solution.py:506
  19.9 0.0 collective-permute-done.1.refs_6_
  19.9 0.0 collective-permute-done.2.refs_7_
  19.9 0.0 collective-permute-done.3.refs_8_
  19.9 0.0 collective-permute-done.4.refs_9_
  19.9 0.0 collective-permute-done.5.refs_10_
  19.9 0.0 copy-start.14
  20.0 0.0 copy-start.13
  20.0 0.1 collective-permute-start.6
  20.0 4.1 %collective-permute-start.7 = (f32[28,32,128]{2,1,0:T(8,128)}, f32[28,32,128]{2,1,0:T(8,128)S(1)}, u32[]{:S(2)}, u32[]{:S(2)}) collective-permute-start(f32[28,32,128]{2,1,0:T(8,128)} %get-tuple-element.62), channel_id=1, source_target_pairs={{8,16},{16,8},{9,17},{17,9},{10,18},{18,10},{11,19},{19,11},{12,20... | collective-permute-start | bytes 1376264 | tf_op jit(solution)/shard_map/ppermute | solution.py:67
  24.1 0.0 copy-done.5
  24.1 0.0 copy-done.7
  24.2 0.0 copy-done.8
  24.2 0.0 copy-done.9
  24.2 0.0 copy-done.10
  24.2 0.0 copy-done.14
  24.2 0.0 copy-done.13
  24.2 0.0 copy-start
  24.2 0.0 copy-start.1
  24.2 49.8 %pair_forces.1 = (f32[1024,128]{1,0:T(8,128)S(1)}, f32[128,128]{1,0:T(8,128)S(1)}, f32[128,128]{1,0:T(8,128)S(1)}, f32[128,128]{1,0:T(8,128)S(1)}, f32[128,128]{...) custom-call(s32[1024]{0:T(1024)S(1)} %copy-done.13, s32[1024]{0:T(1024)S(1)} %bitcast.26, ...), custom_call_target="tpu_custom_call" | custom-call | flops 335544320 | bytes 4194304 | tf_op jit(solution)/shard_map/pair_forces/pallas_call | solution.py:311
  74.0 0.0 collective-permute-done.6.refs_4_.refs_8_
  74.0 0.0 collective-permute-done.7.refs_5_.refs_9_
  74.0 0.0 copy-done
  74.0 0.0 copy-done.1
  74.0 0.0 copy-start.2
  74.0 1.0 copy-done.2
  75.1 0.0 copy-start.4
  75.1 1.0 copy-done.4
  76.1 0.0 copy-start.3
  76.1 0.0 copy-start.6
  76.1 0.2 pack_rows.1
  76.3 2.1 %collective-permute-start.8 = (f32[960,128]{1,0:T(8,128)S(1)}, f32[960,128]{1,0:T(8,128)S(1)}, u32[]{:S(2)}, u32[]{:S(2)}) collective-permute-start(f32[960,128]{1,0:T(8,128)S(1)} %get-tuple-element.65), channel_id=1, source_target_pairs={{0,1},{1,0},{2,3},{3,2},{4,5},{5,4},{6,7},{7,6},{8,9},{9,8},{10,11... | collective-permute-start | bytes 1474568 | tf_op jit(solution)/shard_map/ppermute | solution.py:67
  78.4 1.9 %collective-permute-start.9 = (f32[960,128]{1,0:T(8,128)S(1)}, f32[960,128]{1,0:T(8,128)S(1)}, u32[]{:S(2)}, u32[]{:S(2)}) collective-permute-start(f32[960,128]{1,0:T(8,128)S(1)} %get-tuple-element.66), channel_id=1, source_target_pairs={{1,2},{2,1},{3,4},{4,3},{5,6},{6,5},{9,10},{10,9},{11,12},{12,11},... | collective-permute-start | bytes 1474568 | tf_op jit(solution)/shard_map/ppermute | solution.py:67
  80.3 1.4 %collective-permute-start.10 = (f32[128,128]{1,0:T(8,128)S(1)}, f32[128,128]{1,0:T(8,128)S(1)}, u32[]{:S(2)}, u32[]{:S(2)}) collective-permute-start(f32[128,128]{1,0:T(8,128)S(1)} %get-tuple-element.69), channel_id=1, source_target_pairs={{0,2},{1,3},{2,0},{3,1},{4,6},{5,7},{6,4},{7,5},{8,10},{9,11},{10,... | collective-permute-start | bytes 196616 | tf_op jit(solution)/shard_map/ppermute | solution.py:67
  81.7 1.9 %collective-permute-start.11 = (f32[128,128]{1,0:T(8,128)S(1)}, f32[128,128]{1,0:T(8,128)S(1)}, u32[]{:S(2)}, u32[]{:S(2)}) collective-permute-start(f32[128,128]{1,0:T(8,128)S(1)} %get-tuple-element.70), channel_id=1, source_target_pairs={{2,4},{3,5},{4,2},{5,3},{10,12},{11,13},{12,10},{13,11},{18,20},{1... | collective-permute-start | bytes 196616 | tf_op jit(solution)/shard_map/ppermute | solution.py:67
  83.6 0.0 copy-start.12
  83.6 0.1 collective-permute-start.12
  83.7 0.0 collective-permute-done.8.refs_6_
  83.7 2.5 %collective-permute-start.13 = (f32[128,128]{1,0:T(8,128)S(1)}, f32[128,128]{1,0:T(8,128)S(1)}, u32[]{:S(2)}, u32[]{:S(2)}) collective-permute-start(f32[128,128]{1,0:T(8,128)S(1)} %get-tuple-element.72), channel_id=1, source_target_pairs={{8,16},{16,8},{9,17},{17,9},{10,18},{18,10},{11,19},{19,11},{12,20... | collective-permute-start | bytes 196616 | tf_op jit(solution)/shard_map/ppermute | solution.py:67
  86.2 3.0 %collective-permute-done.9.refs_7_ = f32[960,128]{1,0:T(8,128)S(1)} collective-permute-done((f32[960,128]{1,0:T(8,128)S(1)}, f32[960,128]{1,0:T(8,128)S(1)}, u32[]{:S(2)}, u32[]{:S(2)}) %collective-permute-start.9) | collective-permute-done | bytes 491552 | tf_op jit(solution)/shard_map/ppermute | solution.py:67
  89.2 0.0 copy-done.3
  89.2 0.0 copy-done.6
  89.2 0.0 copy-done.12
  89.2 12.0 %grid_step.1 = (f32[16,32,256]{2,1,0:T(8,128)}, f32[16,32,256]{2,1,0:T(8,128)}, f32[1024,128]{1,0:T(8,128)S(1)}) custom-call(s32[256]{0:T(256)S(1)} %copy-done.12, f32[256,128]{1,0:T(8,128)S(1)} %copy-done.6, f32[16,32,256]{2,1,0:T(8,128)S(1)} %copy-done, f32[16,32,256]{2,1,0:T(8,128)S(1)} %copy-done.3, f32[16,32,256]{2,1,0:T(8,128)S(1)} %copy-done.4, ...), custom_call_target="tpu_custom_call" | custom-call | flops 31948800 | bytes 8388608 | tf_op jit(solution)/shard_map/grid_step/pallas_call | solution.py:774
  101.2 0.0 collective-permute-done.10
  101.2 0.0 collective-permute-done.11
  101.2 0.0 collective-permute-done.12
  101.2 0.0 collective-permute-done.13
  101.2 0.0 copy-start.11
  101.2 0.7 copy-done.11
  101.9 2.6 %gather_forces.1 = f32[3,32768]{1,0:T(4,128)} custom-call(s32[7,32]{1,0:T(8,128)S(1)} %copy-done.11, f32[256,4,128]{2,1,0:T(4,128)S(1)} %bitcast.17, f32[256,4,128]{2,1,0:T(4,128)S(1)} %bitcast.19, f32[32,4,128]{2,1,0:T(4,128)S(1)} %bitcast.20, f32[240,4,128]{2,1,0:T(4,128)S(1)} %bitcast.15, f32[240,4,128]{2,1,0:T(4,128)S(1)} %bitcast.16, ...), custom_call_target="tpu_custom_call" | custom-call | tf_op jit(solution)/shard_map/gather_forces/pallas_call | solution.py:826
Async XLA Ops:
  4.9 8.4 %collective-permute-start = (f32[128,128]{1,0:T(8,128)}, f32[128,128]{1,0:T(8,128)S(1)}, u32[]{:S(2)}, u32[]{:S(2)}) collective-permute-start(f32[128,128]{1,0:T(8,128)} %get-tuple-element.42), channel_id=1, source_target_pairs={{0,1},{1,0},{2,3},{3,2},{4,5},{5,4},{6,7},{7,6},{8,9},{9,8},{10,11... | collective-permute-start | bytes 196616 | tf_op jit(solution)/shard_map/ppermute | solution.py:67
  5.6 14.3 %collective-permute-start.1 = (f32[128,128]{1,0:T(8,128)}, f32[128,128]{1,0:T(8,128)S(1)}, u32[]{:S(2)}, u32[]{:S(2)}) collective-permute-start(f32[128,128]{1,0:T(8,128)} %get-tuple-element.43), channel_id=1, source_target_pairs={{1,2},{2,1},{3,4},{4,3},{5,6},{6,5},{9,10},{10,9},{11,12},{12,11},... | collective-permute-start | bytes 196616 | tf_op jit(solution)/shard_map/ppermute | solution.py:67
  8.7 11.2 %collective-permute-start.2 = (f32[128,128]{1,0:T(8,128)}, f32[128,128]{1,0:T(8,128)S(1)}, u32[]{:S(2)}, u32[]{:S(2)}) collective-permute-start(f32[128,128]{1,0:T(8,128)} %get-tuple-element.44), channel_id=1, source_target_pairs={{0,2},{1,3},{2,0},{3,1},{4,6},{5,7},{6,4},{7,5},{8,10},{9,11},{10,... | collective-permute-start | bytes 196616 | tf_op jit(solution)/shard_map/ppermute | solution.py:67
  9.0 11.0 %collective-permute-start.3 = (f32[128,128]{1,0:T(8,128)}, f32[128,128]{1,0:T(8,128)S(1)}, u32[]{:S(2)}, u32[]{:S(2)}) collective-permute-start(f32[128,128]{1,0:T(8,128)} %get-tuple-element.45), channel_id=1, source_target_pairs={{2,4},{3,5},{4,2},{5,3},{10,12},{11,13},{12,10},{13,11},{18,20},{1... | collective-permute-start | bytes 196616 | tf_op jit(solution)/shard_map/ppermute | solution.py:67
  12.0 7.9 %collective-permute-start.4 = (f32[128,128]{1,0:T(8,128)}, f32[128,128]{1,0:T(8,128)S(1)}, u32[]{:S(2)}, u32[]{:S(2)}) collective-permute-start(f32[128,128]{1,0:T(8,128)} %get-tuple-element.46), channel_id=1, source_target_pairs={{0,8},{8,0},{16,24},{24,16},{1,9},{9,1},{17,25},{25,17},{2,10},{10... | collective-permute-start | bytes 196616 | tf_op jit(solution)/shard_map/ppermute | solution.py:67
  13.3 6.7 %collective-permute-start.5 = (f32[128,128]{1,0:T(8,128)}, f32[128,128]{1,0:T(8,128)S(1)}, u32[]{:S(2)}, u32[]{:S(2)}) collective-permute-start(f32[128,128]{1,0:T(8,128)} %get-tuple-element.47), channel_id=1, source_target_pairs={{8,16},{16,8},{9,17},{17,9},{10,18},{18,10},{11,19},{19,11},{12,20... | collective-permute-start | bytes 196616 | tf_op jit(solution)/shard_map/ppermute | solution.py:67
  15.4 8.7 %copy-start.5 = (f32[256,4,128]{2,1,0:T(4,128)S(1)}, f32[256,4,128]{2,1,0:T(4,128)}, u32[]{:S(2)}) copy-start(f32[256,4,128]{2,1,0:T(4,128)} %get-tuple-element.40) | copy-start | bytes 1572868
  15.4 8.7 %copy-start.7 = (bf16[128,1024]{1,0:T(8,128)(2,1)S(1)}, bf16[128,1024]{1,0:T(8,128)(2,1)}, u32[]{:S(2)}) copy-start(bf16[128,1024]{1,0:T(8,128)(2,1)} %constant.6.clone.refs_0_) | copy-start | bytes 786436
  15.4 8.7 %copy-start.8 = (bf16[256,128]{1,0:T(8,128)(2,1)S(1)}, bf16[256,128]{1,0:T(8,128)(2,1)}, u32[]{:S(2)}) copy-start(bf16[256,128]{1,0:T(8,128)(2,1)} %constant.7.clone.refs_1_) | copy-start | bytes 196612
  15.4 8.7 %copy-start.9 = (f32[128,128]{1,0:T(8,128)S(1)}, f32[128,128]{1,0:T(8,128)}, u32[]{:S(2)}) copy-start(f32[128,128]{1,0:T(8,128)} %get-tuple-element.51.refs_4_) | copy-start | bytes 196612
  15.4 8.7 %copy-start.10 = (bf16[128,128]{1,0:T(8,128)(2,1)S(1)}, bf16[128,128]{1,0:T(8,128)(2,1)}, u32[]{:S(2)}) copy-start(bf16[128,128]{1,0:T(8,128)(2,1)} %constant.8.clone.refs_2_) | copy-start | bytes 98308
  19.9 4.2 %copy-start.14 = (s32[8,128]{1,0:T(8,128)S(1)}, s32[8,128]{1,0:T(8,128)}, u32[]{:S(2)}) copy-start(s32[8,128]{1,0:T(8,128)} %get-tuple-element.39) | copy-start | bytes 12292
  20.0 4.2 %copy-start.13 = (s32[1024]{0:T(1024)S(1)}, s32[1024]{0:T(1024)}, u32[]{:S(2)}) copy-start(s32[1024]{0:T(1024)} %own_rows_ref.1) | copy-start | bytes 12292
  20.0 54.0 %collective-permute-start.6 = (f32[28,32,128]{2,1,0:T(8,128)}, f32[28,32,128]{2,1,0:T(8,128)S(1)}, u32[]{:S(2)}, u32[]{:S(2)}) collective-permute-start(f32[28,32,128]{2,1,0:T(8,128)} %get-tuple-element.61), channel_id=1, source_target_pairs={{0,8},{8,0},{16,24},{24,16},{1,9},{9,1},{17,25},{25,17},{2,10},{10... | collective-permute-start | bytes 1376264 | tf_op jit(solution)/shard_map/ppermute | solution.py:67
  20.0 54.0 %collective-permute-start.7 = (f32[28,32,128]{2,1,0:T(8,128)}, f32[28,32,128]{2,1,0:T(8,128)S(1)}, u32[]{:S(2)}, u32[]{:S(2)}) collective-permute-start(f32[28,32,128]{2,1,0:T(8,128)} %get-tuple-element.62), channel_id=1, source_target_pairs={{8,16},{16,8},{9,17},{17,9},{10,18},{18,10},{11,19},{19,11},{12,20... | collective-permute-start | bytes 1376264 | tf_op jit(solution)/shard_map/ppermute | solution.py:67
  24.2 49.8 %copy-start = (f32[16,32,256]{2,1,0:T(8,128)S(1)}, f32[16,32,256]{2,1,0:T(8,128)}, u32[]{:S(2)}) copy-start(f32[16,32,256]{2,1,0:T(8,128)} %refs_2_.2) | copy-start | bytes 1572868
  24.2 49.8 %copy-start.1 = (f32[16,32,256]{2,1,0:T(8,128)S(1)}, f32[16,32,256]{2,1,0:T(8,128)}, u32[]{:S(2)}) copy-start(f32[16,32,256]{2,1,0:T(8,128)} %refs_5_.1) | copy-start | bytes 1572868
  74.0 1.0 copy-start.2
  75.1 1.0 copy-start.4
  76.1 13.1 %copy-start.3 = (f32[16,32,256]{2,1,0:T(8,128)S(1)}, f32[16,32,256]{2,1,0:T(8,128)}, u32[]{:S(2)}) copy-start(f32[16,32,256]{2,1,0:T(8,128)} %get-tuple-element.59.refs_1_.refs_3_) | copy-start | bytes 1572868
  76.1 13.1 %copy-start.6 = (f32[256,128]{1,0:T(8,128)S(1)}, f32[256,128]{1,0:T(8,128)}, u32[]{:S(2)}) copy-start(f32[256,128]{1,0:T(8,128)} %get-tuple-element.48.masked_hbm.refs_1_) | copy-start | bytes 393220
  76.3 7.4 %collective-permute-start.8 = (f32[960,128]{1,0:T(8,128)S(1)}, f32[960,128]{1,0:T(8,128)S(1)}, u32[]{:S(2)}, u32[]{:S(2)}) collective-permute-start(f32[960,128]{1,0:T(8,128)S(1)} %get-tuple-element.65), channel_id=1, source_target_pairs={{0,1},{1,0},{2,3},{3,2},{4,5},{5,4},{6,7},{7,6},{8,9},{9,8},{10,11... | collective-permute-start | bytes 1474568 | tf_op jit(solution)/shard_map/ppermute | solution.py:67
  78.4 10.8 %collective-permute-start.9 = (f32[960,128]{1,0:T(8,128)S(1)}, f32[960,128]{1,0:T(8,128)S(1)}, u32[]{:S(2)}, u32[]{:S(2)}) collective-permute-start(f32[960,128]{1,0:T(8,128)S(1)} %get-tuple-element.66), channel_id=1, source_target_pairs={{1,2},{2,1},{3,4},{4,3},{5,6},{6,5},{9,10},{10,9},{11,12},{12,11},... | collective-permute-start | bytes 1474568 | tf_op jit(solution)/shard_map/ppermute | solution.py:67
  80.3 20.9 %collective-permute-start.10 = (f32[128,128]{1,0:T(8,128)S(1)}, f32[128,128]{1,0:T(8,128)S(1)}, u32[]{:S(2)}, u32[]{:S(2)}) collective-permute-start(f32[128,128]{1,0:T(8,128)S(1)} %get-tuple-element.69), channel_id=1, source_target_pairs={{0,2},{1,3},{2,0},{3,1},{4,6},{5,7},{6,4},{7,5},{8,10},{9,11},{10,... | collective-permute-start | bytes 196616 | tf_op jit(solution)/shard_map/ppermute | solution.py:67
  81.7 19.5 %collective-permute-start.11 = (f32[128,128]{1,0:T(8,128)S(1)}, f32[128,128]{1,0:T(8,128)S(1)}, u32[]{:S(2)}, u32[]{:S(2)}) collective-permute-start(f32[128,128]{1,0:T(8,128)S(1)} %get-tuple-element.70), channel_id=1, source_target_pairs={{2,4},{3,5},{4,2},{5,3},{10,12},{11,13},{12,10},{13,11},{18,20},{1... | collective-permute-start | bytes 196616 | tf_op jit(solution)/shard_map/ppermute | solution.py:67
  83.6 5.6 %copy-start.12 = (s32[256]{0:T(256)S(1)}, s32[256]{0:T(256)}, u32[]{:S(2)}) copy-start(s32[256]{0:T(256)} %refs_0_.4) | copy-start | bytes 3076
  83.6 17.6 %collective-permute-start.12 = (f32[128,128]{1,0:T(8,128)S(1)}, f32[128,128]{1,0:T(8,128)S(1)}, u32[]{:S(2)}, u32[]{:S(2)}) collective-permute-start(f32[128,128]{1,0:T(8,128)S(1)} %get-tuple-element.71), channel_id=1, source_target_pairs={{0,8},{8,0},{16,24},{24,16},{1,9},{9,1},{17,25},{25,17},{2,10},{10... | collective-permute-start | bytes 196616 | tf_op jit(solution)/shard_map/ppermute | solution.py:67
  83.7 17.5 %collective-permute-start.13 = (f32[128,128]{1,0:T(8,128)S(1)}, f32[128,128]{1,0:T(8,128)S(1)}, u32[]{:S(2)}, u32[]{:S(2)}) collective-permute-start(f32[128,128]{1,0:T(8,128)S(1)} %get-tuple-element.72), channel_id=1, source_target_pairs={{8,16},{16,8},{9,17},{17,9},{10,18},{18,10},{11,19},{19,11},{12,20... | collective-permute-start | bytes 196616 | tf_op jit(solution)/shard_map/ppermute | solution.py:67
  101.2 0.7 copy-start.11

commit v19 on v18

--- a/solution.py
+++ b/solution.py
@@ -9,6 +9,7 @@
 from jax.sharding import PartitionSpec as P
 
 SWEEPS = 4
+QUAD = 4
 UNROLL = 8
 CHUNKS = 4
 AHEAD = 2
@@ -93,6 +94,7 @@
     near = np.zeros((128, 1024), np.float32)
     far = np.zeros((256, 128), np.float32)
     moment = np.zeros((128, 128), np.float32)
+    column = np.zeros((128, QUAD * 256), np.float32)
     for cluster in range(8):
         for index, kind in enumerate(near_kinds):
             near[kind * 8 + cluster, cluster * 128 + index] = 1.0
@@ -100,18 +102,22 @@
             far[cluster * 32 + index, kind * 8 + cluster] = 1.0
         for kind in range(12):
             moment[cluster * 16 + kind, kind * 8 + cluster] = 1.0
-    return tuple(jnp.asarray(part, jnp.bfloat16) for part in (near, far, moment))
+            for turn in range(QUAD):
+                lane = (cluster % QUAD + turn) % QUAD * 32 + kind
+                target = turn * 256 + cluster // QUAD * 128 + lane
+                column[kind * 8 + cluster, target] = 1.0
+    return tuple(jnp.asarray(part, jnp.bfloat16) for part in (near, far, moment, column))
 
 
 def pair_kernel(own_rows_ref, other_rows_ref, *refs):
     sources = len(SWAPS) + 1
-    fetched = sources + 4
+    fetched = sources + 5
     hbm_refs = refs[:fetched]
     own_out_ref = refs[fetched]
     other_out_refs = refs[fetched + 1 : fetched + 1 + sources]
     refs = refs[fetched + 1 + sources :]
-    near_sel_ref, far_sel_ref, moment_sel_ref, own_ref = refs[:4]
-    other_refs = refs[4:fetched]
+    near_sel_ref, far_sel_ref, moment_sel_ref, column_sel_ref, own_ref = refs[:5]
+    other_refs = refs[5:fetched]
     sems = refs[fetched]
     copies = start_copies(
         [
@@ -134,6 +140,7 @@
     slots = other_out_refs[0].shape[0] // 4
     others = slots * sources
     groups = own_rows_ref.shape[0] // UNROLL
+    groups_of_other = others // QUAD
     ones = jnp.ones((8, 128), jnp.float32)
     zeros = jnp.zeros((8, 128), jnp.float32)
 
@@ -175,18 +182,23 @@
             far_sel_ref[...], place_pieces(comps, -2.0, softening).astype(jnp.bfloat16)
         )
         moments = jnp.concatenate(moment_pieces(comps, charge) + [zeros] * 4, axis=0)
-        other_moment_ref[pl.ds(pl.multiple_of(start * 16, 128), 128), :] = selected(
-            moment_sel_ref[...], moments.astype(jnp.bfloat16)
-        )
+        tiles = selected(moments.T, column_sel_ref[...])
+        for turn in range(QUAD):
+            for half in range(2):
+                group = turn * groups_of_other + source * (slots // QUAD) + step * 2 + half
+                column = 256 * turn + 128 * half
+                other_moment_ref[pl.ds(pl.multiple_of(group * 128, 128), 128), :] = tiles[
+                    :, column : column + 128
+                ]
         return 0
 
     own_sum_ref[...] = jnp.zeros_like(own_sum_ref)
     other_sum_ref[...] = jnp.zeros_like(other_sum_ref)
     weight_refs[0][...] = jnp.zeros_like(weight_refs[0])
-    for copy in copies[:4]:
+    for copy in copies[:5]:
         copy.wait()
     lax.fori_loop(0, clusters // 8, near_rows, 0, unroll=4)
-    for copy in copies[4:]:
+    for copy in copies[5:]:
         copy.wait()
     for source in range(sources):
         lax.fori_loop(0, slots // 8, functools.partial(far_rows, source), 0, unroll=4)
@@ -213,14 +225,30 @@
     def row_block(index):
         return pl.ds(pl.multiple_of(index * 16, 16), 16)
 
-    def own_product(other, weight_ref, index):
-        both = weight_ref[128 * index : 128 * index + 128]
-        return lax.dot_general(
-            other_moment_ref[row_block(other), :],
-            jnp.concatenate([both[:, :128], both[:, 128:]], axis=0),
-            (((1,), (1,)), ((), ())),
-            preferred_element_type=jnp.float32,
+    quarter_row = lax.shift_right_logical(lax.broadcasted_iota(jnp.int32, (1, 128), 1), 5)
+    masks = [jnp.where(quarter_row == turn, 1.0, 0.0).astype(jnp.bfloat16) for turn in range(QUAD)]
+
+    def turned(index, turn):
+        rotation = lax.bitwise_and(turn - index, 3)
+        group = rotation * groups_of_other + lax.shift_right_logical(index, 2)
+        return other_moment_ref[pl.ds(pl.multiple_of(group * 128, 128), 128), :] * masks[turn]
+
+    def own_products(others, weight_ref, first):
+        levels = [
+            jnp.concatenate(
+                [
+                    weight_ref[128 * (first + turn) : 128 * (first + turn) + 128, lanes]
+                    for turn in range(QUAD)
+                ],
+                axis=1,
+            )
+            for lanes in (slice(0, 128), slice(128, 256))
+        ]
+        columns = jnp.concatenate([turned(other, turn) for turn, other in enumerate(others)], axis=0)
+        both = jnp.dot(
+            jnp.concatenate(levels, axis=0), columns, preferred_element_type=jnp.float32
         )
+        return (both[:128] + both[128:]).T
 
     def other_product(own, weight_ref, index):
         return jnp.dot(
@@ -229,8 +257,8 @@
             preferred_element_type=jnp.float32,
         )
 
-    def add_rows(own, other, to_own, to_other):
-        own_sum_ref[row_block(own), :] += to_own[:, :128] + to_own[:, 128:]
+    def add_rows(own, other, turn, to_own, to_other):
+        own_sum_ref[row_block(own), :] += to_own[32 * turn : 32 * turn + 16]
         other_sum_ref[row_block(other), :] += to_other[:, :128] + to_other[:, 128:]
 
     def half_step(step, side, dists):
@@ -242,13 +270,16 @@
             coming = step * UNROLL + index + AHEAD
             later = distances(jnp.minimum(coming, groups * UNROLL - 1))
             weights(dists[0], index, 0, weight_refs[1 - side])
-            to_own = own_product(other, weight_refs[side], index)
+            turn = index % QUAD
+            if turn == 0:
+                others_now = [other_rows_ref[last + index + place] for place in range(QUAD)]
+                to_own = own_products(others_now, weight_refs[side], index)
             weights(dists[0], index, 1, weight_refs[1 - side])
             weights(dists[0], index, 2, weight_refs[1 - side])
             to_other = other_product(own, weight_refs[side], index)
             weights(dists[0], index, 3, weight_refs[1 - side])
             dists = [*dists[1:], later]
-            waiting.append((own, other, to_own, to_other))
+            waiting.append((own, other, turn, to_own, to_other))
             if len(waiting) > BEHIND:
                 add_rows(*waiting.pop(0))
         for entry in waiting:
@@ -314,7 +345,7 @@
             jax.ShapeDtypeStruct(own.shape, jnp.float32),
             *[jax.ShapeDtypeStruct((slots * 4, 128), jnp.float32)] * len(arrived),
         ),
-        in_specs=[smem, smem] + [hbm] * (4 + len(arrived)),
+        in_specs=[smem, smem] + [hbm] * (5 + len(arrived)),
         out_specs=(vmem,) * (len(arrived) + 1),
         scratch_shapes=[
             *[pltpu.VMEM(operand.shape, operand.dtype) for operand in operands],
@@ -323,7 +354,7 @@
             pltpu.VMEM((clusters * 128, 128), jnp.bfloat16),
             pltpu.VMEM((others * 32, 128), jnp.bfloat16),
             pltpu.VMEM((clusters * 16, 128), jnp.bfloat16),
-            pltpu.VMEM((others * 16, 128), jnp.bfloat16),
+            pltpu.VMEM((others * 128, 128), jnp.bfloat16),
             pltpu.VMEM((clusters * 16, 128), jnp.float32),
             pltpu.VMEM((others * 16, 128), jnp.float32),
             pltpu.VMEM((AHEAD, 128, 128), jnp.float32),

time: 105 us -> 113 us (1.076)
  Pallas kernels: 73.2 us -> 81.8 us
    pallas_call x1, Pallas kernels: 49.8 us -> 58.4 us  [pair_forces(): pl.pallas_call(pair_kernel, out_shape=(jax.ShapeDtypeStruct(own.shape, jn...]
    unnamed x30 -> x32, local copies, waits for them, and re-layouts: 2.83 us -> 1.8 us
  transfers between devices with their start and end apart: 14 -> 14, of which waited for: 1 -> 1; matrix products, arithmetic and copies ran while one was open for 0% -> 0% of each run, Pallas kernels for 63% -> 67%
where the time goes in v19:
time: 113 us; the launch traced here: 112 us
  Pallas kernels  81.8 us (72%)
  starting transfers between devices  24.4 us (22%)
  waiting for transfers between devices  3.1 us (3%)
  local copies, waits for them, and re-layouts  1.8 us (2%)
    pallas_call x1, Pallas kernels, pair_forces(): pl.pallas_call(pair_kernel, out_shape=(jax.ShapeDtypeStruct(own.shape, jn...  58.4 us
    ppermute x14, starting transfers between devices, swapped(): return lax.ppermute(shard, axis, pairs)  24.4 us
    pallas_call x1, Pallas kernels, grid_step(): pl.pallas_call(functools.partial(grid_kernel, base), out_shape=(jax.Shape...  12 us
    pallas_call x1, Pallas kernels, sources_of(): pl.pallas_call(sources_kernel, out_shape=(*[jax.ShapeDtypeStruct(ions.sha...  4.45 us
    pallas_call x1, Pallas kernels, prepare(): pl.pallas_call(prepare_kernel, out_shape=(jax.ShapeDtypeStruct(pair_dir.s...  4.24 us
    ppermute x14, waiting for transfers between devices, swapped(): return lax.ppermute(shard, axis, pairs)  3.1 us
    pallas_call x1, Pallas kernels, gather_forces(): pl.pallas_call(gather_forces_kernel, out_shape=jax.ShapeDtypeStruct((3, c...  2.6 us
  transfers between devices with their start and end apart: 14, of which 1 were waited for; matrix products, arithmetic and copies ran while one was open for 0% of the time, Pallas kernels for 67%

profile of v19, /device:TPU:13, one launch (start us, length us, event | category | flops | bytes accessed | tf_op | source)
XLA Modules:
  0.0 112.2 jit_solution(17204877453306390088)
XLA Ops:
  0.6 4.2 %prepare.1 = (s32[8,128]{1,0:T(8,128)}, f32[256,4,128]{2,1,0:T(4,128)}, f32[256,128]{1,0:T(8,128)}, f32[128,128]{1,0:T(8,128)}, f32[128,128]{1,0:T(8,128)}, /*in...) custom-call(s32[256]{0:T(256)} %fill_ref.1, ...), custom_call_target="tpu_custom_call" | custom-call | tf_op jit(solution)/shard_map/prepare/pallas_call | solution.py:431
  4.9 0.7 collective-permute-start
  5.6 3.1 %collective-permute-start.1 = (f32[128,128]{1,0:T(8,128)}, f32[128,128]{1,0:T(8,128)S(1)}, u32[]{:S(2)}, u32[]{:S(2)}) collective-permute-start(f32[128,128]{1,0:T(8,128)} %get-tuple-element.43), channel_id=1, source_target_pairs={{1,2},{2,1},{3,4},{4,3},{5,6},{6,5},{9,10},{10,9},{11,12},{12,11},... | collective-permute-start | bytes 196616 | tf_op jit(solution)/shard_map/ppermute | solution.py:68
  8.7 0.2 collective-permute-start.2
  9.0 3.0 %collective-permute-start.3 = (f32[128,128]{1,0:T(8,128)}, f32[128,128]{1,0:T(8,128)S(1)}, u32[]{:S(2)}, u32[]{:S(2)}) collective-permute-start(f32[128,128]{1,0:T(8,128)} %get-tuple-element.45), channel_id=1, source_target_pairs={{2,4},{3,5},{4,2},{5,3},{10,12},{11,13},{12,10},{13,11},{18,20},{1... | collective-permute-start | bytes 196616 | tf_op jit(solution)/shard_map/ppermute | solution.py:68
  12.0 1.3 %collective-permute-start.4 = (f32[128,128]{1,0:T(8,128)}, f32[128,128]{1,0:T(8,128)S(1)}, u32[]{:S(2)}, u32[]{:S(2)}) collective-permute-start(f32[128,128]{1,0:T(8,128)} %get-tuple-element.46), channel_id=1, source_target_pairs={{0,8},{8,0},{16,24},{24,16},{1,9},{9,1},{17,25},{25,17},{2,10},{10... | collective-permute-start | bytes 196616 | tf_op jit(solution)/shard_map/ppermute | solution.py:68
  13.3 0.0 collective-permute-done.refs_6_
  13.3 2.1 %collective-permute-start.5 = (f32[128,128]{1,0:T(8,128)}, f32[128,128]{1,0:T(8,128)S(1)}, u32[]{:S(2)}, u32[]{:S(2)}) collective-permute-start(f32[128,128]{1,0:T(8,128)} %get-tuple-element.47), channel_id=1, source_target_pairs={{8,16},{16,8},{9,17},{17,9},{10,18},{18,10},{11,19},{19,11},{12,20... | collective-permute-start | bytes 196616 | tf_op jit(solution)/shard_map/ppermute | solution.py:68
  15.4 0.0 copy-start.5
  15.4 0.0 copy-start.7
  15.4 0.0 copy-start.8
  15.4 0.0 copy-start.9
  15.5 0.0 copy-start.10
  15.5 0.0 copy-start.11
  15.5 4.4 %sources.1 = (f32[16,32,256]{2,1,0:T(8,128)}, f32[16,32,256]{2,1,0:T(8,128)}, f32[28,32,128]{2,1,0:T(8,128)}, f32[28,32,128]{2,1,0:T(8,128)}) custom-call(s32[256]{0:T(256)} %refs_0_.4, s32[1,256]{1,0:T(1,128)} %bitcast.25, f32[256,128]{1,0:T(8,128)} %get-tuple-element.48.masked_hbm.refs_1_, f32[16,32,256]{2,1,0:T(8,128)} %refs_5_.1, ...), custom_call_target="tpu_custom_call" | custom-call | flops 20000000 | bytes 4194304 | tf_op jit(solution)/shard_map/sources/pallas_call | solution.py:537
  19.9 0.0 collective-permute-done.1.refs_7_
  19.9 0.0 collective-permute-done.2.refs_8_
  20.0 0.0 collective-permute-done.3.refs_9_
  20.0 0.0 collective-permute-done.4.refs_10_
  20.0 0.0 collective-permute-done.5.refs_11_
  20.0 0.0 copy-start.15
  20.0 0.0 copy-start.14
  20.0 0.1 collective-permute-start.6
  20.1 4.1 %collective-permute-start.7 = (f32[28,32,128]{2,1,0:T(8,128)}, f32[28,32,128]{2,1,0:T(8,128)S(1)}, u32[]{:S(2)}, u32[]{:S(2)}) collective-permute-start(f32[28,32,128]{2,1,0:T(8,128)} %get-tuple-element.62), channel_id=1, source_target_pairs={{8,16},{16,8},{9,17},{17,9},{10,18},{18,10},{11,19},{19,11},{12,20... | collective-permute-start | bytes 1376264 | tf_op jit(solution)/shard_map/ppermute | solution.py:68
  24.2 0.0 copy-done.5
  24.2 0.0 copy-done.7
  24.2 0.0 copy-done.8
  24.2 0.0 copy-done.9
  24.2 0.0 copy-done.10
  24.2 0.0 copy-done.11
  24.2 0.0 copy-done.15
  24.2 0.0 copy-done.14
  24.3 0.0 copy-start
  24.3 0.0 copy-start.1
  24.3 0.0 copy-start.2
  24.3 58.4 %pair_forces.1 = (f32[1024,128]{1,0:T(8,128)S(1)}, f32[128,128]{1,0:T(8,128)S(1)}, f32[128,128]{1,0:T(8,128)S(1)}, f32[128,128]{1,0:T(8,128)S(1)}, f32[128,128]{...) custom-call(s32[1024]{0:T(1024)S(1)} %copy-done.14, s32[1024]{0:T(1024)S(1)} %bitcast.26, ...), custom_call_target="tpu_custom_call" | custom-call | flops 335544320 | bytes 4194304 | tf_op jit(solution)/shard_map/pair_forces/pallas_call | solution.py:342
  82.7 0.0 collective-permute-done.6.refs_4_.refs_8_
  82.7 0.0 collective-permute-done.7.refs_5_.refs_9_
  82.7 0.0 copy-done
  82.7 0.0 copy-done.1
  82.7 0.0 copy-done.2
  82.7 0.0 copy-start.3
  82.7 1.0 copy-done.3
  83.8 0.2 pack_rows.1
  83.9 2.1 %collective-permute-start.8 = (f32[960,128]{1,0:T(8,128)S(1)}, f32[960,128]{1,0:T(8,128)S(1)}, u32[]{:S(2)}, u32[]{:S(2)}) collective-permute-start(f32[960,128]{1,0:T(8,128)S(1)} %get-tuple-element.65), channel_id=1, source_target_pairs={{0,1},{1,0},{2,3},{3,2},{4,5},{5,4},{6,7},{7,6},{8,9},{9,8},{10,11... | collective-permute-start | bytes 1474568 | tf_op jit(solution)/shard_map/ppermute | solution.py:68
  86.0 1.9 %collective-permute-start.9 = (f32[960,128]{1,0:T(8,128)S(1)}, f32[960,128]{1,0:T(8,128)S(1)}, u32[]{:S(2)}, u32[]{:S(2)}) collective-permute-start(f32[960,128]{1,0:T(8,128)S(1)} %get-tuple-element.66), channel_id=1, source_target_pairs={{1,2},{2,1},{3,4},{4,3},{5,6},{6,5},{9,10},{10,9},{11,12},{12,11},... | collective-permute-start | bytes 1474568 | tf_op jit(solution)/shard_map/ppermute | solution.py:68
  87.9 1.4 %collective-permute-start.10 = (f32[128,128]{1,0:T(8,128)S(1)}, f32[128,128]{1,0:T(8,128)S(1)}, u32[]{:S(2)}, u32[]{:S(2)}) collective-permute-start(f32[128,128]{1,0:T(8,128)S(1)} %get-tuple-element.69), channel_id=1, source_target_pairs={{0,2},{1,3},{2,0},{3,1},{4,6},{5,7},{6,4},{7,5},{8,10},{9,11},{10,... | collective-permute-start | bytes 196616 | tf_op jit(solution)/shard_map/ppermute | solution.py:68
  89.4 1.9 %collective-permute-start.11 = (f32[128,128]{1,0:T(8,128)S(1)}, f32[128,128]{1,0:T(8,128)S(1)}, u32[]{:S(2)}, u32[]{:S(2)}) collective-permute-start(f32[128,128]{1,0:T(8,128)S(1)} %get-tuple-element.70), channel_id=1, source_target_pairs={{2,4},{3,5},{4,2},{5,3},{10,12},{11,13},{12,10},{13,11},{18,20},{1... | collective-permute-start | bytes 196616 | tf_op jit(solution)/shard_map/ppermute | solution.py:68
  91.3 0.0 copy-start.13
  91.3 0.1 collective-permute-start.12
  91.4 0.0 collective-permute-done.8.refs_6_
  91.4 2.4 %collective-permute-start.13 = (f32[128,128]{1,0:T(8,128)S(1)}, f32[128,128]{1,0:T(8,128)S(1)}, u32[]{:S(2)}, u32[]{:S(2)}) collective-permute-start(f32[128,128]{1,0:T(8,128)S(1)} %get-tuple-element.72), channel_id=1, source_target_pairs={{8,16},{16,8},{9,17},{17,9},{10,18},{18,10},{11,19},{19,11},{12,20... | collective-permute-start | bytes 196616 | tf_op jit(solution)/shard_map/ppermute | solution.py:68
  93.8 3.1 %collective-permute-done.9.refs_7_ = f32[960,128]{1,0:T(8,128)S(1)} collective-permute-done((f32[960,128]{1,0:T(8,128)S(1)}, f32[960,128]{1,0:T(8,128)S(1)}, u32[]{:S(2)}, u32[]{:S(2)}) %collective-permute-start.9) | collective-permute-done | bytes 491552 | tf_op jit(solution)/shard_map/ppermute | solution.py:68
  96.8 0.0 copy-done.4
  96.9 0.0 copy-done.6
  96.9 0.0 copy-done.13
  96.9 12.0 %grid_step.1 = (f32[16,32,256]{2,1,0:T(8,128)}, f32[16,32,256]{2,1,0:T(8,128)}, f32[1024,128]{1,0:T(8,128)S(1)}) custom-call(s32[256]{0:T(256)S(1)} %copy-done.13, f32[256,128]{1,0:T(8,128)S(1)} %copy-done.6, f32[16,32,256]{2,1,0:T(8,128)S(1)} %copy-done, f32[16,32,256]{2,1,0:T(8,128)S(1)} %copy-done.2, f32[16,32,256]{2,1,0:T(8,128)S(1)} %copy-done.4, ...), custom_call_target="tpu_custom_call" | custom-call | flops 31948800 | bytes 8388608 | tf_op jit(solution)/shard_map/grid_step/pallas_call | solution.py:805
  108.8 0.0 collective-permute-done.10
  108.8 0.0 collective-permute-done.11
  108.9 0.0 collective-permute-done.12
  108.9 0.0 collective-permute-done.13
  108.9 0.0 copy-start.12
  108.9 0.7 copy-done.12
  109.6 2.6 %gather_forces.1 = f32[3,32768]{1,0:T(4,128)} custom-call(s32[7,32]{1,0:T(8,128)S(1)} %copy-done.12, f32[256,4,128]{2,1,0:T(4,128)S(1)} %bitcast.18, f32[256,4,128]{2,1,0:T(4,128)S(1)} %bitcast.19, f32[32,4,128]{2,1,0:T(4,128)S(1)} %bitcast.20, f32[240,4,128]{2,1,0:T(4,128)S(1)} %bitcast.15, f32[240,4,128]{2,1,0:T(4,128)S(1)} %bitcast.16, ...), custom_call_target="tpu_custom_call" | custom-call | tf_op jit(solution)/shard_map/gather_forces/pallas_call | solution.py:857
  (2 shorter events, 0.0 us)
Async XLA Ops:
  4.9 8.4 %collective-permute-start = (f32[128,128]{1,0:T(8,128)}, f32[128,128]{1,0:T(8,128)S(1)}, u32[]{:S(2)}, u32[]{:S(2)}) collective-permute-start(f32[128,128]{1,0:T(8,128)} %get-tuple-element.42), channel_id=1, source_target_pairs={{0,1},{1,0},{2,3},{3,2},{4,5},{5,4},{6,7},{7,6},{8,9},{9,8},{10,11... | collective-permute-start | bytes 196616 | tf_op jit(solution)/shard_map/ppermute | solution.py:68
  5.6 14.3 %collective-permute-start.1 = (f32[128,128]{1,0:T(8,128)}, f32[128,128]{1,0:T(8,128)S(1)}, u32[]{:S(2)}, u32[]{:S(2)}) collective-permute-start(f32[128,128]{1,0:T(8,128)} %get-tuple-element.43), channel_id=1, source_target_pairs={{1,2},{2,1},{3,4},{4,3},{5,6},{6,5},{9,10},{10,9},{11,12},{12,11},... | collective-permute-start | bytes 196616 | tf_op jit(solution)/shard_map/ppermute | solution.py:68
  8.7 11.2 %collective-permute-start.2 = (f32[128,128]{1,0:T(8,128)}, f32[128,128]{1,0:T(8,128)S(1)}, u32[]{:S(2)}, u32[]{:S(2)}) collective-permute-start(f32[128,128]{1,0:T(8,128)} %get-tuple-element.44), channel_id=1, source_target_pairs={{0,2},{1,3},{2,0},{3,1},{4,6},{5,7},{6,4},{7,5},{8,10},{9,11},{10,... | collective-permute-start | bytes 196616 | tf_op jit(solution)/shard_map/ppermute | solution.py:68
  9.0 11.0 %collective-permute-start.3 = (f32[128,128]{1,0:T(8,128)}, f32[128,128]{1,0:T(8,128)S(1)}, u32[]{:S(2)}, u32[]{:S(2)}) collective-permute-start(f32[128,128]{1,0:T(8,128)} %get-tuple-element.45), channel_id=1, source_target_pairs={{2,4},{3,5},{4,2},{5,3},{10,12},{11,13},{12,10},{13,11},{18,20},{1... | collective-permute-start | bytes 196616 | tf_op jit(solution)/shard_map/ppermute | solution.py:68
  12.0 7.9 %collective-permute-start.4 = (f32[128,128]{1,0:T(8,128)}, f32[128,128]{1,0:T(8,128)S(1)}, u32[]{:S(2)}, u32[]{:S(2)}) collective-permute-start(f32[128,128]{1,0:T(8,128)} %get-tuple-element.46), channel_id=1, source_target_pairs={{0,8},{8,0},{16,24},{24,16},{1,9},{9,1},{17,25},{25,17},{2,10},{10... | collective-permute-start | bytes 196616 | tf_op jit(solution)/shard_map/ppermute | solution.py:68
  13.3 6.7 %collective-permute-start.5 = (f32[128,128]{1,0:T(8,128)}, f32[128,128]{1,0:T(8,128)S(1)}, u32[]{:S(2)}, u32[]{:S(2)}) collective-permute-start(f32[128,128]{1,0:T(8,128)} %get-tuple-element.47), channel_id=1, source_target_pairs={{8,16},{16,8},{9,17},{17,9},{10,18},{18,10},{11,19},{19,11},{12,20... | collective-permute-start | bytes 196616 | tf_op jit(solution)/shard_map/ppermute | solution.py:68
  15.4 8.8 %copy-start.5 = (f32[256,4,128]{2,1,0:T(4,128)S(1)}, f32[256,4,128]{2,1,0:T(4,128)}, u32[]{:S(2)}) copy-start(f32[256,4,128]{2,1,0:T(4,128)} %get-tuple-element.40) | copy-start | bytes 1572868
  15.4 8.8 %copy-start.7 = (bf16[128,1024]{1,0:T(8,128)(2,1)S(1)}, bf16[128,1024]{1,0:T(8,128)(2,1)}, u32[]{:S(2)}) copy-start(bf16[128,1024]{1,0:T(8,128)(2,1)} %constant.11.clone.refs_3_) | copy-start | bytes 786436
  15.4 8.8 %copy-start.8 = (bf16[128,1024]{1,0:T(8,128)(2,1)S(1)}, bf16[128,1024]{1,0:T(8,128)(2,1)}, u32[]{:S(2)}) copy-start(bf16[128,1024]{1,0:T(8,128)(2,1)} %constant.8.clone.refs_0_) | copy-start | bytes 786436
  15.4 8.8 %copy-start.9 = (bf16[256,128]{1,0:T(8,128)(2,1)S(1)}, bf16[256,128]{1,0:T(8,128)(2,1)}, u32[]{:S(2)}) copy-start(bf16[256,128]{1,0:T(8,128)(2,1)} %constant.9.clone.refs_1_) | copy-start | bytes 196612
  15.5 8.8 %copy-start.10 = (f32[128,128]{1,0:T(8,128)S(1)}, f32[128,128]{1,0:T(8,128)}, u32[]{:S(2)}) copy-start(f32[128,128]{1,0:T(8,128)} %get-tuple-element.51.refs_5_) | copy-start | bytes 196612
  15.5 8.8 %copy-start.11 = (bf16[128,128]{1,0:T(8,128)(2,1)S(1)}, bf16[128,128]{1,0:T(8,128)(2,1)}, u32[]{:S(2)}) copy-start(bf16[128,128]{1,0:T(8,128)(2,1)} %constant.10.clone.refs_2_) | copy-start | bytes 98308
  20.0 4.2 %copy-start.15 = (s32[8,128]{1,0:T(8,128)S(1)}, s32[8,128]{1,0:T(8,128)}, u32[]{:S(2)}) copy-start(s32[8,128]{1,0:T(8,128)} %get-tuple-element.39) | copy-start | bytes 12292
  20.0 4.2 %copy-start.14 = (s32[1024]{0:T(1024)S(1)}, s32[1024]{0:T(1024)}, u32[]{:S(2)}) copy-start(s32[1024]{0:T(1024)} %own_rows_ref.1) | copy-start | bytes 12292
  20.0 62.7 %collective-permute-start.6 = (f32[28,32,128]{2,1,0:T(8,128)}, f32[28,32,128]{2,1,0:T(8,128)S(1)}, u32[]{:S(2)}, u32[]{:S(2)}) collective-permute-start(f32[28,32,128]{2,1,0:T(8,128)} %get-tuple-element.61), channel_id=1, source_target_pairs={{0,8},{8,0},{16,24},{24,16},{1,9},{9,1},{17,25},{25,17},{2,10},{10... | collective-permute-start | bytes 1376264 | tf_op jit(solution)/shard_map/ppermute | solution.py:68
  20.1 62.6 %collective-permute-start.7 = (f32[28,32,128]{2,1,0:T(8,128)}, f32[28,32,128]{2,1,0:T(8,128)S(1)}, u32[]{:S(2)}, u32[]{:S(2)}) collective-permute-start(f32[28,32,128]{2,1,0:T(8,128)} %get-tuple-element.62), channel_id=1, source_target_pairs={{8,16},{16,8},{9,17},{17,9},{10,18},{18,10},{11,19},{19,11},{12,20... | collective-permute-start | bytes 1376264 | tf_op jit(solution)/shard_map/ppermute | solution.py:68
  24.3 58.4 %copy-start = (f32[16,32,256]{2,1,0:T(8,128)S(1)}, f32[16,32,256]{2,1,0:T(8,128)}, u32[]{:S(2)}) copy-start(f32[16,32,256]{2,1,0:T(8,128)} %refs_2_.2) | copy-start | bytes 1572868
  24.3 58.4 %copy-start.1 = (f32[16,32,256]{2,1,0:T(8,128)S(1)}, f32[16,32,256]{2,1,0:T(8,128)}, u32[]{:S(2)}) copy-start(f32[16,32,256]{2,1,0:T(8,128)} %refs_5_.1) | copy-start | bytes 1572868
  24.3 58.4 %copy-start.2 = (f32[16,32,256]{2,1,0:T(8,128)S(1)}, f32[16,32,256]{2,1,0:T(8,128)}, u32[]{:S(2)}) copy-start(f32[16,32,256]{2,1,0:T(8,128)} %get-tuple-element.59.refs_1_.refs_3_) | copy-start | bytes 1572868
  82.7 1.0 copy-start.3
  83.8 13.1 %copy-start.4 = (f32[16,32,256]{2,1,0:T(8,128)S(1)}, f32[16,32,256]{2,1,0:T(8,128)}, u32[]{:S(2)}) copy-start(f32[16,32,256]{2,1,0:T(8,128)} %get-tuple-element.60.refs_2_.refs_4_) | copy-start | bytes 1572868
  83.8 13.1 %copy-start.6 = (f32[256,128]{1,0:T(8,128)S(1)}, f32[256,128]{1,0:T(8,128)}, u32[]{:S(2)}) copy-start(f32[256,128]{1,0:T(8,128)} %get-tuple-element.48.masked_hbm.refs_1_) | copy-start | bytes 393220
  83.9 7.4 %collective-permute-start.8 = (f32[960,128]{1,0:T(8,128)S(1)}, f32[960,128]{1,0:T(8,128)S(1)}, u32[]{:S(2)}, u32[]{:S(2)}) collective-permute-start(f32[960,128]{1,0:T(8,128)S(1)} %get-tuple-element.65), channel_id=1, source_target_pairs={{0,1},{1,0},{2,3},{3,2},{4,5},{5,4},{6,7},{7,6},{8,9},{9,8},{10,11... | collective-permute-start | bytes 1474568 | tf_op jit(solution)/shard_map/ppermute | solution.py:68
  86.0 10.8 %collective-permute-start.9 = (f32[960,128]{1,0:T(8,128)S(1)}, f32[960,128]{1,0:T(8,128)S(1)}, u32[]{:S(2)}, u32[]{:S(2)}) collective-permute-start(f32[960,128]{1,0:T(8,128)S(1)} %get-tuple-element.66), channel_id=1, source_target_pairs={{1,2},{2,1},{3,4},{4,3},{5,6},{6,5},{9,10},{10,9},{11,12},{12,11},... | collective-permute-start | bytes 1474568 | tf_op jit(solution)/shard_map/ppermute | solution.py:68
  87.9 20.9 %collective-permute-start.10 = (f32[128,128]{1,0:T(8,128)S(1)}, f32[128,128]{1,0:T(8,128)S(1)}, u32[]{:S(2)}, u32[]{:S(2)}) collective-permute-start(f32[128,128]{1,0:T(8,128)S(1)} %get-tuple-element.69), channel_id=1, source_target_pairs={{0,2},{1,3},{2,0},{3,1},{4,6},{5,7},{6,4},{7,5},{8,10},{9,11},{10,... | collective-permute-start | bytes 196616 | tf_op jit(solution)/shard_map/ppermute | solution.py:68
  89.4 19.5 %collective-permute-start.11 = (f32[128,128]{1,0:T(8,128)S(1)}, f32[128,128]{1,0:T(8,128)S(1)}, u32[]{:S(2)}, u32[]{:S(2)}) collective-permute-start(f32[128,128]{1,0:T(8,128)S(1)} %get-tuple-element.70), channel_id=1, source_target_pairs={{2,4},{3,5},{4,2},{5,3},{10,12},{11,13},{12,10},{13,11},{18,20},{1... | collective-permute-start | bytes 196616 | tf_op jit(solution)/shard_map/ppermute | solution.py:68
  91.3 5.6 %copy-start.13 = (s32[256]{0:T(256)S(1)}, s32[256]{0:T(256)}, u32[]{:S(2)}) copy-start(s32[256]{0:T(256)} %refs_0_.4) | copy-start | bytes 3076
  91.3 17.6 %collective-permute-start.12 = (f32[128,128]{1,0:T(8,128)S(1)}, f32[128,128]{1,0:T(8,128)S(1)}, u32[]{:S(2)}, u32[]{:S(2)}) collective-permute-start(f32[128,128]{1,0:T(8,128)S(1)} %get-tuple-element.71), channel_id=1, source_target_pairs={{0,8},{8,0},{16,24},{24,16},{1,9},{9,1},{17,25},{25,17},{2,10},{10... | collective-permute-start | bytes 196616 | tf_op jit(solution)/shard_map/ppermute | solution.py:68
  91.4 17.5 %collective-permute-start.13 = (f32[128,128]{1,0:T(8,128)S(1)}, f32[128,128]{1,0:T(8,128)S(1)}, u32[]{:S(2)}, u32[]{:S(2)}) collective-permute-start(f32[128,128]{1,0:T(8,128)S(1)} %get-tuple-element.72), channel_id=1, source_target_pairs={{8,16},{16,8},{9,17},{17,9},{10,18},{18,10},{11,19},{19,11},{12,20... | collective-permute-start | bytes 196616 | tf_op jit(solution)/shard_map/ppermute | solution.py:68
  108.9 0.7 copy-start.12

commit v20 on v18

--- a/solution.py
+++ b/solution.py
@@ -13,6 +13,7 @@
 CHUNKS = 4
 AHEAD = 2
 BEHIND = 4
+BATCH = 4
 HALO_WIDTHS = (SWEEPS + 1, SWEEPS, SWEEPS, 1)
 DEPTH = SWEEPS + 1
 CELL_BITS = 8
@@ -154,42 +155,46 @@
             left.astype(jnp.bfloat16), right, preferred_element_type=jnp.float32
         ).astype(jnp.bfloat16)
 
+    def stacked(moments):
+        return jnp.concatenate(moments + [zeros] * 4, axis=0).astype(jnp.bfloat16)
+
     def near_rows(step, _):
-        start = pl.multiple_of(step * 8, 8)
-        *comps, charge = components(own_ref, start)
-        moments = jnp.concatenate(moment_pieces(comps, charge) + [zeros] * 4, axis=0)
-        own_moment_ref[pl.ds(pl.multiple_of(start * 16, 128), 128), :] = selected(
-            moment_sel_ref[...], moments.astype(jnp.bfloat16)
-        )
-        tiles = selected(place_pieces(comps, 1.0, 0.0).T, near_sel_ref[...])
-        for index in range(8):
-            at = pl.ds(pl.multiple_of((start + index) * 128, 128), 128)
-            near_ref[at, :] = tiles[:, 128 * index : 128 * index + 128]
-        return 0
-
-    def far_rows(source, step, _):
-        local = pl.multiple_of(step * 8, 8)
-        start = source * slots + local
-        *comps, charge = components(other_refs[source], local)
-        far_ref[pl.ds(pl.multiple_of(start * 32, 256), 256), :] = selected(
-            far_sel_ref[...], place_pieces(comps, -2.0, softening).astype(jnp.bfloat16)
-        )
-        moments = jnp.concatenate(moment_pieces(comps, charge) + [zeros] * 4, axis=0)
-        other_moment_ref[pl.ds(pl.multiple_of(start * 16, 128), 128), :] = selected(
-            moment_sel_ref[...], moments.astype(jnp.bfloat16)
-        )
-        return 0
+        starts = [pl.multiple_of(step * 8 * BATCH + 8 * index, 8) for index in range(BATCH)]
+        parts = [components(own_ref, start) for start in starts]
+        turned = [place_pieces(part[:3], 1.0, 0.0).T.astype(jnp.bfloat16) for part in parts]
+        moments = [stacked(moment_pieces(part[:3], part[3])) for part in parts]
+        placed = [selected(moment_sel_ref[...], moment) for moment in moments]
+        for start, rows in zip(starts, placed, strict=True):
+            own_moment_ref[pl.ds(pl.multiple_of(start * 16, 128), 128), :] = rows
+        for start, pieces in zip(starts, turned, strict=True):
+            tiles = selected(pieces, near_sel_ref[...])
+            for index in range(8):
+                at = pl.ds(pl.multiple_of((start + index) * 128, 128), 128)
+                near_ref[at, :] = tiles[:, 128 * index : 128 * index + 128]
+        return 0
+
+    def far_rows(source):
+        locals_ = range(0, slots, 8)
+        parts = [components(other_refs[source], local) for local in locals_]
+        pieces = [place_pieces(part[:3], -2.0, softening).astype(jnp.bfloat16) for part in parts]
+        moments = [stacked(moment_pieces(part[:3], part[3])) for part in parts]
+        rows = [selected(far_sel_ref[...], piece) for piece in pieces]
+        placed = [selected(moment_sel_ref[...], moment) for moment in moments]
+        for local, row, moment in zip(locals_, rows, placed, strict=True):
+            start = source * slots + local
+            far_ref[start * 32 : start * 32 + 256, :] = row
+            other_moment_ref[start * 16 : start * 16 + 128, :] = moment
 
     own_sum_ref[...] = jnp.zeros_like(own_sum_ref)
     other_sum_ref[...] = jnp.zeros_like(other_sum_ref)
     weight_refs[0][...] = jnp.zeros_like(weight_refs[0])
     for copy in copies[:4]:
         copy.wait()
-    lax.fori_loop(0, clusters // 8, near_rows, 0, unroll=4)
+    lax.fori_loop(0, clusters // (8 * BATCH), near_rows, 0)
     for copy in copies[4:]:
         copy.wait()
     for source in range(sources):
-        lax.fori_loop(0, slots // 8, functools.partial(far_rows, source), 0, unroll=4)
+        far_rows(source)
     def distances(pair):
         own = own_rows_ref[pair]
         other = other_rows_ref[pair]
@@ -269,35 +274,37 @@
     half_step(groups, 0, [dist_ref[index] for index in range(AHEAD)])
 
     def finish(data_ref, out_ref, sum_ref, base, step, _):
-        start = pl.multiple_of(step * 8, 8)
-        *comps, charge = components(data_ref, start)
-
-        def total(part):
+        starts = [pl.multiple_of(step * 8 * BATCH + 8 * index, 8) for index in range(BATCH)]
+        parts = [components(data_ref, start) for start in starts]
+
+        def total(start, part):
             terms = [
                 sum_ref[pl.ds(base + start * 16 + 4 * level + part, 8, stride=16), :]
                 for level in range(3)
             ]
             return terms[0] + (terms[1] + terms[2])
 
-        weight = total(3)
-        scale = coulomb_scale * charge
-        for part, comp in enumerate(comps):
-            out_ref[pl.ds(4 * start + part, 8, stride=4), :] = scale * (comp * weight - total(part))
-        out_ref[pl.ds(4 * start + 3, 8, stride=4), :] = zeros
+        totals = [[total(start, part) for part in range(4)] for start in starts]
+        for start, (*comps, charge), sums in zip(starts, parts, totals, strict=True):
+            scale = coulomb_scale * charge
+            for part, comp in enumerate(comps):
+                out_ref[pl.ds(4 * start + part, 8, stride=4), :] = scale * (
+                    comp * sums[3] - sums[part]
+                )
+            out_ref[pl.ds(4 * start + 3, 8, stride=4), :] = zeros
         return 0
 
     lax.fori_loop(
-        0, clusters // 8, functools.partial(finish, own_ref, own_out_ref, own_sum_ref, 0), 0, unroll=4
+        0,
+        clusters // (8 * BATCH),
+        functools.partial(finish, own_ref, own_out_ref, own_sum_ref, 0),
+        0,
     )
     for source in range(sources):
         body = functools.partial(
-            finish,
-            other_refs[source],
-            other_out_refs[source],
-            other_sum_ref,
-            source * slots * 16,
+            finish, other_refs[source], other_out_refs[source], other_sum_ref, source * slots * 16
         )
-        lax.fori_loop(0, slots // 8, body, 0, unroll=4)
+        lax.fori_loop(0, slots // (8 * BATCH), body, 0)
 
 
 def pair_forces(own_rows, other_rows, own, arrived, slots):
@@ -751,7 +758,7 @@
         pick_refs[2][at, :] = along_z
         return 0
 
-    lax.fori_loop(0, clusters, pick, 0, unroll=8)
+    lax.fori_loop(0, clusters, pick, 0, unroll=16)
 
     def spread_out(step, _):
         start = pl.multiple_of(step * 8, 8)

time: 105 us -> 105 us (level)
  no operation moved by 1% of the time
where the time goes in v20:
time: 105 us; the launch traced here: 104 us
  Pallas kernels  72.9 us (69%)
  starting transfers between devices  24.5 us (23%)
  waiting for transfers between devices  3.04 us (3%)
  local copies, waits for them, and re-layouts  2.83 us (3%)
    pallas_call x1, Pallas kernels, pair_forces(): pl.pallas_call(pair_kernel, out_shape=(jax.ShapeDtypeStruct(own.shape, jn...  49.6 us
    ppermute x14, starting transfers between devices, swapped(): return lax.ppermute(shard, axis, pairs)  24.5 us
    pallas_call x1, Pallas kernels, grid_step(): pl.pallas_call(functools.partial(grid_kernel, base), out_shape=(jax.Shape...  11.9 us
    pallas_call x1, Pallas kernels, sources_of(): pl.pallas_call(sources_kernel, out_shape=(*[jax.ShapeDtypeStruct(ions.sha...  4.44 us
    pallas_call x1, Pallas kernels, prepare(): pl.pallas_call(prepare_kernel, out_shape=(jax.ShapeDtypeStruct(pair_dir.s...  4.23 us
    ppermute x14, waiting for transfers between devices, swapped(): return lax.ppermute(shard, axis, pairs)  3.04 us
    unnamed x30, local copies, waits for them, and re-layouts  2.83 us
    pallas_call x1, Pallas kernels, gather_forces(): pl.pallas_call(gather_forces_kernel, out_shape=jax.ShapeDtypeStruct((3, c...  2.6 us
  transfers between devices with their start and end apart: 14, of which 1 were waited for; matrix products, arithmetic and copies ran while one was open for 0% of the time, Pallas kernels for 63%

profile of v20, /device:TPU:13, one launch (start us, length us, event | category | flops | bytes accessed | tf_op | source)
XLA Modules:
  0.0 104.2 jit_solution(7182760177302324366)
XLA Ops:
  0.6 4.2 %prepare.1 = (s32[8,128]{1,0:T(8,128)}, f32[256,4,128]{2,1,0:T(4,128)}, f32[256,128]{1,0:T(8,128)}, f32[128,128]{1,0:T(8,128)}, f32[128,128]{1,0:T(8,128)}, /*in...) custom-call(s32[256]{0:T(256)} %fill_ref.1, ...), custom_call_target="tpu_custom_call" | custom-call | tf_op jit(solution)/shard_map/prepare/pallas_call | solution.py:407
  4.9 0.7 collective-permute-start
  5.6 3.1 %collective-permute-start.1 = (f32[128,128]{1,0:T(8,128)}, f32[128,128]{1,0:T(8,128)S(1)}, u32[]{:S(2)}, u32[]{:S(2)}) collective-permute-start(f32[128,128]{1,0:T(8,128)} %get-tuple-element.43), channel_id=1, source_target_pairs={{1,2},{2,1},{3,4},{4,3},{5,6},{6,5},{9,10},{10,9},{11,12},{12,11},... | collective-permute-start | bytes 196616 | tf_op jit(solution)/shard_map/ppermute | solution.py:68
  8.7 0.2 collective-permute-start.2
  9.0 3.0 %collective-permute-start.3 = (f32[128,128]{1,0:T(8,128)}, f32[128,128]{1,0:T(8,128)S(1)}, u32[]{:S(2)}, u32[]{:S(2)}) collective-permute-start(f32[128,128]{1,0:T(8,128)} %get-tuple-element.45), channel_id=1, source_target_pairs={{2,4},{3,5},{4,2},{5,3},{10,12},{11,13},{12,10},{13,11},{18,20},{1... | collective-permute-start | bytes 196616 | tf_op jit(solution)/shard_map/ppermute | solution.py:68
  12.0 1.3 %collective-permute-start.4 = (f32[128,128]{1,0:T(8,128)}, f32[128,128]{1,0:T(8,128)S(1)}, u32[]{:S(2)}, u32[]{:S(2)}) collective-permute-start(f32[128,128]{1,0:T(8,128)} %get-tuple-element.46), channel_id=1, source_target_pairs={{0,8},{8,0},{16,24},{24,16},{1,9},{9,1},{17,25},{25,17},{2,10},{10... | collective-permute-start | bytes 196616 | tf_op jit(solution)/shard_map/ppermute | solution.py:68
  13.3 0.0 collective-permute-done.refs_5_
  13.3 2.1 %collective-permute-start.5 = (f32[128,128]{1,0:T(8,128)}, f32[128,128]{1,0:T(8,128)S(1)}, u32[]{:S(2)}, u32[]{:S(2)}) collective-permute-start(f32[128,128]{1,0:T(8,128)} %get-tuple-element.47), channel_id=1, source_target_pairs={{8,16},{16,8},{9,17},{17,9},{10,18},{18,10},{11,19},{19,11},{12,20... | collective-permute-start | bytes 196616 | tf_op jit(solution)/shard_map/ppermute | solution.py:68
  15.4 0.0 copy-start.5
  15.4 0.0 copy-start.7
  15.4 0.0 copy-start.8
  15.4 0.0 copy-start.9
  15.4 0.0 copy-start.10
  15.5 4.4 %sources.1 = (f32[16,32,256]{2,1,0:T(8,128)}, f32[16,32,256]{2,1,0:T(8,128)}, f32[28,32,128]{2,1,0:T(8,128)}, f32[28,32,128]{2,1,0:T(8,128)}) custom-call(s32[256]{0:T(256)} %refs_0_.4, s32[1,256]{1,0:T(1,128)} %bitcast.25, f32[256,128]{1,0:T(8,128)} %get-tuple-element.48.masked_hbm.refs_1_, f32[16,32,256]{2,1,0:T(8,128)} %refs_5_.1, ...), custom_call_target="tpu_custom_call" | custom-call | flops 20000000 | bytes 4194304 | tf_op jit(solution)/shard_map/sources/pallas_call | solution.py:513
  19.9 0.0 collective-permute-done.1.refs_6_
  19.9 0.0 collective-permute-done.2.refs_7_
  19.9 0.0 collective-permute-done.3.refs_8_
  19.9 0.0 collective-permute-done.4.refs_9_
  19.9 0.0 collective-permute-done.5.refs_10_
  19.9 0.0 copy-start.14
  20.0 0.0 copy-start.13
  20.0 0.1 collective-permute-start.6
  20.0 4.1 %collective-permute-start.7 = (f32[28,32,128]{2,1,0:T(8,128)}, f32[28,32,128]{2,1,0:T(8,128)S(1)}, u32[]{:S(2)}, u32[]{:S(2)}) collective-permute-start(f32[28,32,128]{2,1,0:T(8,128)} %get-tuple-element.62), channel_id=1, source_target_pairs={{8,16},{16,8},{9,17},{17,9},{10,18},{18,10},{11,19},{19,11},{12,20... | collective-permute-start | bytes 1376264 | tf_op jit(solution)/shard_map/ppermute | solution.py:68
  24.1 0.0 copy-done.5
  24.1 0.0 copy-done.7
  24.2 0.0 copy-done.8
  24.2 0.0 copy-done.9
  24.2 0.0 copy-done.10
  24.2 0.0 copy-done.14
  24.2 0.0 copy-done.13
  24.2 0.0 copy-start
  24.2 0.0 copy-start.1
  24.2 49.6 %pair_forces.1 = (f32[1024,128]{1,0:T(8,128)S(1)}, f32[128,128]{1,0:T(8,128)S(1)}, f32[128,128]{1,0:T(8,128)S(1)}, f32[128,128]{1,0:T(8,128)S(1)}, f32[128,128]{...) custom-call(s32[1024]{0:T(1024)S(1)} %copy-done.13, s32[1024]{0:T(1024)S(1)} %bitcast.26, ...), custom_call_target="tpu_custom_call" | custom-call | flops 335544320 | bytes 4194304 | tf_op jit(solution)/shard_map/pair_forces/pallas_call | solution.py:318
  73.8 0.0 collective-permute-done.6.refs_4_.refs_8_
  73.8 0.0 collective-permute-done.7.refs_5_.refs_9_
  73.8 0.0 copy-done
  73.8 0.0 copy-done.1
  73.8 0.0 copy-start.2
  73.9 1.0 copy-done.2
  74.9 0.0 copy-start.4
  74.9 1.0 copy-done.4
  75.9 0.0 copy-start.3
  75.9 0.0 copy-start.6
  75.9 0.2 pack_rows.1
  76.1 2.1 %collective-permute-start.8 = (f32[960,128]{1,0:T(8,128)S(1)}, f32[960,128]{1,0:T(8,128)S(1)}, u32[]{:S(2)}, u32[]{:S(2)}) collective-permute-start(f32[960,128]{1,0:T(8,128)S(1)} %get-tuple-element.65), channel_id=1, source_target_pairs={{0,1},{1,0},{2,3},{3,2},{4,5},{5,4},{6,7},{7,6},{8,9},{9,8},{10,11... | collective-permute-start | bytes 1474568 | tf_op jit(solution)/shard_map/ppermute | solution.py:68
  78.2 1.9 %collective-permute-start.9 = (f32[960,128]{1,0:T(8,128)S(1)}, f32[960,128]{1,0:T(8,128)S(1)}, u32[]{:S(2)}, u32[]{:S(2)}) collective-permute-start(f32[960,128]{1,0:T(8,128)S(1)} %get-tuple-element.66), channel_id=1, source_target_pairs={{1,2},{2,1},{3,4},{4,3},{5,6},{6,5},{9,10},{10,9},{11,12},{12,11},... | collective-permute-start | bytes 1474568 | tf_op jit(solution)/shard_map/ppermute | solution.py:68
  80.1 1.4 %collective-permute-start.10 = (f32[128,128]{1,0:T(8,128)S(1)}, f32[128,128]{1,0:T(8,128)S(1)}, u32[]{:S(2)}, u32[]{:S(2)}) collective-permute-start(f32[128,128]{1,0:T(8,128)S(1)} %get-tuple-element.69), channel_id=1, source_target_pairs={{0,2},{1,3},{2,0},{3,1},{4,6},{5,7},{6,4},{7,5},{8,10},{9,11},{10,... | collective-permute-start | bytes 196616 | tf_op jit(solution)/shard_map/ppermute | solution.py:68
  81.5 1.9 %collective-permute-start.11 = (f32[128,128]{1,0:T(8,128)S(1)}, f32[128,128]{1,0:T(8,128)S(1)}, u32[]{:S(2)}, u32[]{:S(2)}) collective-permute-start(f32[128,128]{1,0:T(8,128)S(1)} %get-tuple-element.70), channel_id=1, source_target_pairs={{2,4},{3,5},{4,2},{5,3},{10,12},{11,13},{12,10},{13,11},{18,20},{1... | collective-permute-start | bytes 196616 | tf_op jit(solution)/shard_map/ppermute | solution.py:68
  83.5 0.0 copy-start.12
  83.5 0.1 collective-permute-start.12
  83.5 0.0 collective-permute-done.8.refs_6_
  83.6 2.5 %collective-permute-start.13 = (f32[128,128]{1,0:T(8,128)S(1)}, f32[128,128]{1,0:T(8,128)S(1)}, u32[]{:S(2)}, u32[]{:S(2)}) collective-permute-start(f32[128,128]{1,0:T(8,128)S(1)} %get-tuple-element.72), channel_id=1, source_target_pairs={{8,16},{16,8},{9,17},{17,9},{10,18},{18,10},{11,19},{19,11},{12,20... | collective-permute-start | bytes 196616 | tf_op jit(solution)/shard_map/ppermute | solution.py:68
  86.0 3.0 %collective-permute-done.9.refs_7_ = f32[960,128]{1,0:T(8,128)S(1)} collective-permute-done((f32[960,128]{1,0:T(8,128)S(1)}, f32[960,128]{1,0:T(8,128)S(1)}, u32[]{:S(2)}, u32[]{:S(2)}) %collective-permute-start.9) | collective-permute-done | bytes 491552 | tf_op jit(solution)/shard_map/ppermute | solution.py:68
  89.0 0.0 copy-done.3
  89.0 0.0 copy-done.6
  89.0 0.0 copy-done.12
  89.0 11.9 %grid_step.1 = (f32[16,32,256]{2,1,0:T(8,128)}, f32[16,32,256]{2,1,0:T(8,128)}, f32[1024,128]{1,0:T(8,128)S(1)}) custom-call(s32[256]{0:T(256)S(1)} %copy-done.12, f32[256,128]{1,0:T(8,128)S(1)} %copy-done.6, f32[16,32,256]{2,1,0:T(8,128)S(1)} %copy-done, f32[16,32,256]{2,1,0:T(8,128)S(1)} %copy-done.3, f32[16,32,256]{2,1,0:T(8,128)S(1)} %copy-done.4, ...), custom_call_target="tpu_custom_call" | custom-call | flops 31948800 | bytes 8388608 | tf_op jit(solution)/shard_map/grid_step/pallas_call | solution.py:781
  100.9 0.0 collective-permute-done.10
  100.9 0.0 collective-permute-done.11
  100.9 0.0 collective-permute-done.12
  100.9 0.0 collective-permute-done.13
  101.0 0.0 copy-start.11
  101.0 0.7 copy-done.11
  101.6 2.6 %gather_forces.1 = f32[3,32768]{1,0:T(4,128)} custom-call(s32[7,32]{1,0:T(8,128)S(1)} %copy-done.11, f32[256,4,128]{2,1,0:T(4,128)S(1)} %bitcast.17, f32[256,4,128]{2,1,0:T(4,128)S(1)} %bitcast.19, f32[32,4,128]{2,1,0:T(4,128)S(1)} %bitcast.20, f32[240,4,128]{2,1,0:T(4,128)S(1)} %bitcast.15, f32[240,4,128]{2,1,0:T(4,128)S(1)} %bitcast.16, ...), custom_call_target="tpu_custom_call" | custom-call | tf_op jit(solution)/shard_map/gather_forces/pallas_call | solution.py:833
Async XLA Ops:
  4.9 8.4 %collective-permute-start = (f32[128,128]{1,0:T(8,128)}, f32[128,128]{1,0:T(8,128)S(1)}, u32[]{:S(2)}, u32[]{:S(2)}) collective-permute-start(f32[128,128]{1,0:T(8,128)} %get-tuple-element.42), channel_id=1, source_target_pairs={{0,1},{1,0},{2,3},{3,2},{4,5},{5,4},{6,7},{7,6},{8,9},{9,8},{10,11... | collective-permute-start | bytes 196616 | tf_op jit(solution)/shard_map/ppermute | solution.py:68
  5.6 14.3 %collective-permute-start.1 = (f32[128,128]{1,0:T(8,128)}, f32[128,128]{1,0:T(8,128)S(1)}, u32[]{:S(2)}, u32[]{:S(2)}) collective-permute-start(f32[128,128]{1,0:T(8,128)} %get-tuple-element.43), channel_id=1, source_target_pairs={{1,2},{2,1},{3,4},{4,3},{5,6},{6,5},{9,10},{10,9},{11,12},{12,11},... | collective-permute-start | bytes 196616 | tf_op jit(solution)/shard_map/ppermute | solution.py:68
  8.7 11.2 %collective-permute-start.2 = (f32[128,128]{1,0:T(8,128)}, f32[128,128]{1,0:T(8,128)S(1)}, u32[]{:S(2)}, u32[]{:S(2)}) collective-permute-start(f32[128,128]{1,0:T(8,128)} %get-tuple-element.44), channel_id=1, source_target_pairs={{0,2},{1,3},{2,0},{3,1},{4,6},{5,7},{6,4},{7,5},{8,10},{9,11},{10,... | collective-permute-start | bytes 196616 | tf_op jit(solution)/shard_map/ppermute | solution.py:68
  9.0 11.0 %collective-permute-start.3 = (f32[128,128]{1,0:T(8,128)}, f32[128,128]{1,0:T(8,128)S(1)}, u32[]{:S(2)}, u32[]{:S(2)}) collective-permute-start(f32[128,128]{1,0:T(8,128)} %get-tuple-element.45), channel_id=1, source_target_pairs={{2,4},{3,5},{4,2},{5,3},{10,12},{11,13},{12,10},{13,11},{18,20},{1... | collective-permute-start | bytes 196616 | tf_op jit(solution)/shard_map/ppermute | solution.py:68
  12.0 7.9 %collective-permute-start.4 = (f32[128,128]{1,0:T(8,128)}, f32[128,128]{1,0:T(8,128)S(1)}, u32[]{:S(2)}, u32[]{:S(2)}) collective-permute-start(f32[128,128]{1,0:T(8,128)} %get-tuple-element.46), channel_id=1, source_target_pairs={{0,8},{8,0},{16,24},{24,16},{1,9},{9,1},{17,25},{25,17},{2,10},{10... | collective-permute-start | bytes 196616 | tf_op jit(solution)/shard_map/ppermute | solution.py:68
  13.3 6.7 %collective-permute-start.5 = (f32[128,128]{1,0:T(8,128)}, f32[128,128]{1,0:T(8,128)S(1)}, u32[]{:S(2)}, u32[]{:S(2)}) collective-permute-start(f32[128,128]{1,0:T(8,128)} %get-tuple-element.47), channel_id=1, source_target_pairs={{8,16},{16,8},{9,17},{17,9},{10,18},{18,10},{11,19},{19,11},{12,20... | collective-permute-start | bytes 196616 | tf_op jit(solution)/shard_map/ppermute | solution.py:68
  15.4 8.7 %copy-start.5 = (f32[256,4,128]{2,1,0:T(4,128)S(1)}, f32[256,4,128]{2,1,0:T(4,128)}, u32[]{:S(2)}) copy-start(f32[256,4,128]{2,1,0:T(4,128)} %get-tuple-element.40) | copy-start | bytes 1572868
  15.4 8.7 %copy-start.7 = (bf16[128,1024]{1,0:T(8,128)(2,1)S(1)}, bf16[128,1024]{1,0:T(8,128)(2,1)}, u32[]{:S(2)}) copy-start(bf16[128,1024]{1,0:T(8,128)(2,1)} %constant.6.clone.refs_0_) | copy-start | bytes 786436
  15.4 8.7 %copy-start.8 = (bf16[256,128]{1,0:T(8,128)(2,1)S(1)}, bf16[256,128]{1,0:T(8,128)(2,1)}, u32[]{:S(2)}) copy-start(bf16[256,128]{1,0:T(8,128)(2,1)} %constant.7.clone.refs_1_) | copy-start | bytes 196612
  15.4 8.7 %copy-start.9 = (f32[128,128]{1,0:T(8,128)S(1)}, f32[128,128]{1,0:T(8,128)}, u32[]{:S(2)}) copy-start(f32[128,128]{1,0:T(8,128)} %get-tuple-element.51.refs_4_) | copy-start | bytes 196612
  15.4 8.7 %copy-start.10 = (bf16[128,128]{1,0:T(8,128)(2,1)S(1)}, bf16[128,128]{1,0:T(8,128)(2,1)}, u32[]{:S(2)}) copy-start(bf16[128,128]{1,0:T(8,128)(2,1)} %constant.8.clone.refs_2_) | copy-start | bytes 98308
  19.9 4.2 %copy-start.14 = (s32[8,128]{1,0:T(8,128)S(1)}, s32[8,128]{1,0:T(8,128)}, u32[]{:S(2)}) copy-start(s32[8,128]{1,0:T(8,128)} %get-tuple-element.39) | copy-start | bytes 12292
  20.0 4.2 %copy-start.13 = (s32[1024]{0:T(1024)S(1)}, s32[1024]{0:T(1024)}, u32[]{:S(2)}) copy-start(s32[1024]{0:T(1024)} %own_rows_ref.1) | copy-start | bytes 12292
  20.0 53.8 %collective-permute-start.6 = (f32[28,32,128]{2,1,0:T(8,128)}, f32[28,32,128]{2,1,0:T(8,128)S(1)}, u32[]{:S(2)}, u32[]{:S(2)}) collective-permute-start(f32[28,32,128]{2,1,0:T(8,128)} %get-tuple-element.61), channel_id=1, source_target_pairs={{0,8},{8,0},{16,24},{24,16},{1,9},{9,1},{17,25},{25,17},{2,10},{10... | collective-permute-start | bytes 1376264 | tf_op jit(solution)/shard_map/ppermute | solution.py:68
  20.0 53.8 %collective-permute-start.7 = (f32[28,32,128]{2,1,0:T(8,128)}, f32[28,32,128]{2,1,0:T(8,128)S(1)}, u32[]{:S(2)}, u32[]{:S(2)}) collective-permute-start(f32[28,32,128]{2,1,0:T(8,128)} %get-tuple-element.62), channel_id=1, source_target_pairs={{8,16},{16,8},{9,17},{17,9},{10,18},{18,10},{11,19},{19,11},{12,20... | collective-permute-start | bytes 1376264 | tf_op jit(solution)/shard_map/ppermute | solution.py:68
  24.2 49.6 %copy-start = (f32[16,32,256]{2,1,0:T(8,128)S(1)}, f32[16,32,256]{2,1,0:T(8,128)}, u32[]{:S(2)}) copy-start(f32[16,32,256]{2,1,0:T(8,128)} %refs_2_.2) | copy-start | bytes 1572868
  24.2 49.6 %copy-start.1 = (f32[16,32,256]{2,1,0:T(8,128)S(1)}, f32[16,32,256]{2,1,0:T(8,128)}, u32[]{:S(2)}) copy-start(f32[16,32,256]{2,1,0:T(8,128)} %refs_5_.1) | copy-start | bytes 1572868
  73.8 1.0 %copy-start.2 = (f32[16,32,256]{2,1,0:T(8,128)S(1)}, f32[16,32,256]{2,1,0:T(8,128)}, u32[]{:S(2)}) copy-start(f32[16,32,256]{2,1,0:T(8,128)} %get-tuple-element.59.refs_1_.refs_3_) | copy-start | bytes 1572868
  74.9 1.0 copy-start.4
  75.9 13.1 %copy-start.3 = (f32[16,32,256]{2,1,0:T(8,128)S(1)}, f32[16,32,256]{2,1,0:T(8,128)}, u32[]{:S(2)}) copy-start(f32[16,32,256]{2,1,0:T(8,128)} %get-tuple-element.59.refs_1_.refs_3_) | copy-start | bytes 1572868
  75.9 13.1 %copy-start.6 = (f32[256,128]{1,0:T(8,128)S(1)}, f32[256,128]{1,0:T(8,128)}, u32[]{:S(2)}) copy-start(f32[256,128]{1,0:T(8,128)} %get-tuple-element.48.masked_hbm.refs_1_) | copy-start | bytes 393220
  76.1 7.4 %collective-permute-start.8 = (f32[960,128]{1,0:T(8,128)S(1)}, f32[960,128]{1,0:T(8,128)S(1)}, u32[]{:S(2)}, u32[]{:S(2)}) collective-permute-start(f32[960,128]{1,0:T(8,128)S(1)} %get-tuple-element.65), channel_id=1, source_target_pairs={{0,1},{1,0},{2,3},{3,2},{4,5},{5,4},{6,7},{7,6},{8,9},{9,8},{10,11... | collective-permute-start | bytes 1474568 | tf_op jit(solution)/shard_map/ppermute | solution.py:68
  78.2 10.8 %collective-permute-start.9 = (f32[960,128]{1,0:T(8,128)S(1)}, f32[960,128]{1,0:T(8,128)S(1)}, u32[]{:S(2)}, u32[]{:S(2)}) collective-permute-start(f32[960,128]{1,0:T(8,128)S(1)} %get-tuple-element.66), channel_id=1, source_target_pairs={{1,2},{2,1},{3,4},{4,3},{5,6},{6,5},{9,10},{10,9},{11,12},{12,11},... | collective-permute-start | bytes 1474568 | tf_op jit(solution)/shard_map/ppermute | solution.py:68
  80.1 20.8 %collective-permute-start.10 = (f32[128,128]{1,0:T(8,128)S(1)}, f32[128,128]{1,0:T(8,128)S(1)}, u32[]{:S(2)}, u32[]{:S(2)}) collective-permute-start(f32[128,128]{1,0:T(8,128)S(1)} %get-tuple-element.69), channel_id=1, source_target_pairs={{0,2},{1,3},{2,0},{3,1},{4,6},{5,7},{6,4},{7,5},{8,10},{9,11},{10,... | collective-permute-start | bytes 196616 | tf_op jit(solution)/shard_map/ppermute | solution.py:68
  81.5 19.4 %collective-permute-start.11 = (f32[128,128]{1,0:T(8,128)S(1)}, f32[128,128]{1,0:T(8,128)S(1)}, u32[]{:S(2)}, u32[]{:S(2)}) collective-permute-start(f32[128,128]{1,0:T(8,128)S(1)} %get-tuple-element.70), channel_id=1, source_target_pairs={{2,4},{3,5},{4,2},{5,3},{10,12},{11,13},{12,10},{13,11},{18,20},{1... | collective-permute-start | bytes 196616 | tf_op jit(solution)/shard_map/ppermute | solution.py:68
  83.5 5.6 %copy-start.12 = (s32[256]{0:T(256)S(1)}, s32[256]{0:T(256)}, u32[]{:S(2)}) copy-start(s32[256]{0:T(256)} %refs_0_.4) | copy-start | bytes 3076
  83.5 17.5 %collective-permute-start.12 = (f32[128,128]{1,0:T(8,128)S(1)}, f32[128,128]{1,0:T(8,128)S(1)}, u32[]{:S(2)}, u32[]{:S(2)}) collective-permute-start(f32[128,128]{1,0:T(8,128)S(1)} %get-tuple-element.71), channel_id=1, source_target_pairs={{0,8},{8,0},{16,24},{24,16},{1,9},{9,1},{17,25},{25,17},{2,10},{10... | collective-permute-start | bytes 196616 | tf_op jit(solution)/shard_map/ppermute | solution.py:68
  83.6 17.4 %collective-permute-start.13 = (f32[128,128]{1,0:T(8,128)S(1)}, f32[128,128]{1,0:T(8,128)S(1)}, u32[]{:S(2)}, u32[]{:S(2)}) collective-permute-start(f32[128,128]{1,0:T(8,128)S(1)} %get-tuple-element.72), channel_id=1, source_target_pairs={{8,16},{16,8},{9,17},{17,9},{10,18},{18,10},{11,19},{19,11},{12,20... | collective-permute-start | bytes 196616 | tf_op jit(solution)/shard_map/ppermute | solution.py:68
  101.0 0.7 copy-start.11

commit v21 on v20

--- a/solution.py
+++ b/solution.py
@@ -9,7 +9,7 @@
 from jax.sharding import PartitionSpec as P
 
 SWEEPS = 4
-UNROLL = 8
+UNROLL = 16
 CHUNKS = 4
 AHEAD = 2
 BEHIND = 4

time: 105 us -> 102 us (0.971)
  Pallas kernels: 72.9 us -> 70.5 us
    pallas_call x1, Pallas kernels: 49.6 us -> 47.2 us  [pair_forces(): pl.pallas_call(pair_kernel, out_shape=(jax.ShapeDtypeStruct(own.shape, jn...]
  transfers between devices with their start and end apart: 14 -> 14, of which waited for: 1 -> 1; matrix products, arithmetic and copies ran while one was open for 0% -> 0% of each run, Pallas kernels for 63% -> 62%
where the time goes in v21:
time: 102 us
  Pallas kernels  70.5 us (69%)
  starting transfers between devices  24.5 us (24%)
  waiting for transfers between devices  3.04 us (3%)
  local copies, waits for them, and re-layouts  2.83 us (3%)
    pallas_call x1, Pallas kernels, pair_forces(): pl.pallas_call(pair_kernel, out_shape=(jax.ShapeDtypeStruct(own.shape, jn...  47.2 us
    ppermute x14, starting transfers between devices, swapped(): return lax.ppermute(shard, axis, pairs)  24.5 us
    pallas_call x1, Pallas kernels, grid_step(): pl.pallas_call(functools.partial(grid_kernel, base), out_shape=(jax.Shape...  11.9 us
    pallas_call x1, Pallas kernels, sources_of(): pl.pallas_call(sources_kernel, out_shape=(*[jax.ShapeDtypeStruct(ions.sha...  4.44 us
    pallas_call x1, Pallas kernels, prepare(): pl.pallas_call(prepare_kernel, out_shape=(jax.ShapeDtypeStruct(pair_dir.s...  4.23 us
    ppermute x14, waiting for transfers between devices, swapped(): return lax.ppermute(shard, axis, pairs)  3.04 us
    unnamed x30, local copies, waits for them, and re-layouts  2.83 us
    pallas_call x1, Pallas kernels, gather_forces(): pl.pallas_call(gather_forces_kernel, out_shape=jax.ShapeDtypeStruct((3, c...  2.6 us
  transfers between devices with their start and end apart: 14, of which 1 were waited for; matrix products, arithmetic and copies ran while one was open for 0% of the time, Pallas kernels for 62%

profile of v21, /device:TPU:13, one launch (start us, length us, event | category | flops | bytes accessed | tf_op | source)
XLA Modules:
  0.0 101.8 jit_solution(14005915176517456939)
XLA Ops:
  0.6 4.2 %prepare.1 = (s32[8,128]{1,0:T(8,128)}, f32[256,4,128]{2,1,0:T(4,128)}, f32[256,128]{1,0:T(8,128)}, f32[128,128]{1,0:T(8,128)}, f32[128,128]{1,0:T(8,128)}, /*in...) custom-call(s32[256]{0:T(256)} %fill_ref.1, ...), custom_call_target="tpu_custom_call" | custom-call | tf_op jit(solution)/shard_map/prepare/pallas_call | solution.py:407
  4.9 0.7 collective-permute-start
  5.6 3.1 %collective-permute-start.1 = (f32[128,128]{1,0:T(8,128)}, f32[128,128]{1,0:T(8,128)S(1)}, u32[]{:S(2)}, u32[]{:S(2)}) collective-permute-start(f32[128,128]{1,0:T(8,128)} %get-tuple-element.43), channel_id=1, source_target_pairs={{1,2},{2,1},{3,4},{4,3},{5,6},{6,5},{9,10},{10,9},{11,12},{12,11},... | collective-permute-start | bytes 196616 | tf_op jit(solution)/shard_map/ppermute | solution.py:68
  8.7 0.2 collective-permute-start.2
  9.0 3.0 %collective-permute-start.3 = (f32[128,128]{1,0:T(8,128)}, f32[128,128]{1,0:T(8,128)S(1)}, u32[]{:S(2)}, u32[]{:S(2)}) collective-permute-start(f32[128,128]{1,0:T(8,128)} %get-tuple-element.45), channel_id=1, source_target_pairs={{2,4},{3,5},{4,2},{5,3},{10,12},{11,13},{12,10},{13,11},{18,20},{1... | collective-permute-start | bytes 196616 | tf_op jit(solution)/shard_map/ppermute | solution.py:68
  12.0 1.3 %collective-permute-start.4 = (f32[128,128]{1,0:T(8,128)}, f32[128,128]{1,0:T(8,128)S(1)}, u32[]{:S(2)}, u32[]{:S(2)}) collective-permute-start(f32[128,128]{1,0:T(8,128)} %get-tuple-element.46), channel_id=1, source_target_pairs={{0,8},{8,0},{16,24},{24,16},{1,9},{9,1},{17,25},{25,17},{2,10},{10... | collective-permute-start | bytes 196616 | tf_op jit(solution)/shard_map/ppermute | solution.py:68
  13.3 0.0 collective-permute-done.refs_5_
  13.3 2.1 %collective-permute-start.5 = (f32[128,128]{1,0:T(8,128)}, f32[128,128]{1,0:T(8,128)S(1)}, u32[]{:S(2)}, u32[]{:S(2)}) collective-permute-start(f32[128,128]{1,0:T(8,128)} %get-tuple-element.47), channel_id=1, source_target_pairs={{8,16},{16,8},{9,17},{17,9},{10,18},{18,10},{11,19},{19,11},{12,20... | collective-permute-start | bytes 196616 | tf_op jit(solution)/shard_map/ppermute | solution.py:68
  15.4 0.0 copy-start.5
  15.4 0.0 copy-start.7
  15.4 0.0 copy-start.8
  15.4 0.0 copy-start.9
  15.4 0.0 copy-start.10
  15.5 4.4 %sources.1 = (f32[16,32,256]{2,1,0:T(8,128)}, f32[16,32,256]{2,1,0:T(8,128)}, f32[28,32,128]{2,1,0:T(8,128)}, f32[28,32,128]{2,1,0:T(8,128)}) custom-call(s32[256]{0:T(256)} %refs_0_.4, s32[1,256]{1,0:T(1,128)} %bitcast.25, f32[256,128]{1,0:T(8,128)} %get-tuple-element.48.masked_hbm.refs_1_, f32[16,32,256]{2,1,0:T(8,128)} %refs_5_.1, ...), custom_call_target="tpu_custom_call" | custom-call | flops 20000000 | bytes 4194304 | tf_op jit(solution)/shard_map/sources/pallas_call | solution.py:513
  19.9 0.0 collective-permute-done.1.refs_6_
  19.9 0.0 collective-permute-done.2.refs_7_
  19.9 0.0 collective-permute-done.3.refs_8_
  19.9 0.0 collective-permute-done.4.refs_9_
  19.9 0.0 collective-permute-done.5.refs_10_
  19.9 0.0 copy-start.14
  20.0 0.0 copy-start.13
  20.0 0.1 collective-permute-start.6
  20.0 4.1 %collective-permute-start.7 = (f32[28,32,128]{2,1,0:T(8,128)}, f32[28,32,128]{2,1,0:T(8,128)S(1)}, u32[]{:S(2)}, u32[]{:S(2)}) collective-permute-start(f32[28,32,128]{2,1,0:T(8,128)} %get-tuple-element.62), channel_id=1, source_target_pairs={{8,16},{16,8},{9,17},{17,9},{10,18},{18,10},{11,19},{19,11},{12,20... | collective-permute-start | bytes 1376264 | tf_op jit(solution)/shard_map/ppermute | solution.py:68
  24.1 0.0 copy-done.5
  24.1 0.0 copy-done.7
  24.2 0.0 copy-done.8
  24.2 0.0 copy-done.9
  24.2 0.0 copy-done.10
  24.2 0.0 copy-done.14
  24.2 0.0 copy-done.13
  24.2 0.0 copy-start
  24.2 0.0 copy-start.1
  24.2 47.2 %pair_forces.1 = (f32[1024,128]{1,0:T(8,128)S(1)}, f32[128,128]{1,0:T(8,128)S(1)}, f32[128,128]{1,0:T(8,128)S(1)}, f32[128,128]{1,0:T(8,128)S(1)}, f32[128,128]{...) custom-call(s32[1024]{0:T(1024)S(1)} %copy-done.13, s32[1024]{0:T(1024)S(1)} %bitcast.26, ...), custom_call_target="tpu_custom_call" | custom-call | flops 335544320 | bytes 4194304 | tf_op jit(solution)/shard_map/pair_forces/pallas_call | solution.py:318
  71.4 0.0 collective-permute-done.6.refs_4_.refs_8_
  71.4 0.0 collective-permute-done.7.refs_5_.refs_9_
  71.4 0.0 copy-done
  71.4 0.0 copy-done.1
  71.4 0.0 copy-start.2
  71.4 1.0 %copy-done.2 = f32[16,32,256]{2,1,0:T(8,128)S(1)} copy-done((f32[16,32,256]{2,1,0:T(8,128)S(1)}, f32[16,32,256]{2,1,0:T(8,128)}, u32[]{:S(2)}) %copy-start.2) | copy-done | bytes 524312
  72.5 0.0 copy-start.4
  72.5 1.0 %copy-done.4 = f32[16,32,256]{2,1,0:T(8,128)S(1)} copy-done((f32[16,32,256]{2,1,0:T(8,128)S(1)}, f32[16,32,256]{2,1,0:T(8,128)}, u32[]{:S(2)}) %copy-start.4) | copy-done | bytes 524312
  73.5 0.0 copy-start.3
  73.5 0.0 copy-start.6
  73.5 0.2 pack_rows.1
  73.7 2.1 %collective-permute-start.8 = (f32[960,128]{1,0:T(8,128)S(1)}, f32[960,128]{1,0:T(8,128)S(1)}, u32[]{:S(2)}, u32[]{:S(2)}) collective-permute-start(f32[960,128]{1,0:T(8,128)S(1)} %get-tuple-element.65), channel_id=1, source_target_pairs={{0,1},{1,0},{2,3},{3,2},{4,5},{5,4},{6,7},{7,6},{8,9},{9,8},{10,11... | collective-permute-start | bytes 1474568 | tf_op jit(solution)/shard_map/ppermute | solution.py:68
  75.8 1.9 %collective-permute-start.9 = (f32[960,128]{1,0:T(8,128)S(1)}, f32[960,128]{1,0:T(8,128)S(1)}, u32[]{:S(2)}, u32[]{:S(2)}) collective-permute-start(f32[960,128]{1,0:T(8,128)S(1)} %get-tuple-element.66), channel_id=1, source_target_pairs={{1,2},{2,1},{3,4},{4,3},{5,6},{6,5},{9,10},{10,9},{11,12},{12,11},... | collective-permute-start | bytes 1474568 | tf_op jit(solution)/shard_map/ppermute | solution.py:68
  77.7 1.4 %collective-permute-start.10 = (f32[128,128]{1,0:T(8,128)S(1)}, f32[128,128]{1,0:T(8,128)S(1)}, u32[]{:S(2)}, u32[]{:S(2)}) collective-permute-start(f32[128,128]{1,0:T(8,128)S(1)} %get-tuple-element.69), channel_id=1, source_target_pairs={{0,2},{1,3},{2,0},{3,1},{4,6},{5,7},{6,4},{7,5},{8,10},{9,11},{10,... | collective-permute-start | bytes 196616 | tf_op jit(solution)/shard_map/ppermute | solution.py:68
  79.1 1.9 %collective-permute-start.11 = (f32[128,128]{1,0:T(8,128)S(1)}, f32[128,128]{1,0:T(8,128)S(1)}, u32[]{:S(2)}, u32[]{:S(2)}) collective-permute-start(f32[128,128]{1,0:T(8,128)S(1)} %get-tuple-element.70), channel_id=1, source_target_pairs={{2,4},{3,5},{4,2},{5,3},{10,12},{11,13},{12,10},{13,11},{18,20},{1... | collective-permute-start | bytes 196616 | tf_op jit(solution)/shard_map/ppermute | solution.py:68
  81.0 0.0 copy-start.12
  81.0 0.1 collective-permute-start.12
  81.1 0.0 collective-permute-done.8.refs_6_
  81.1 2.5 %collective-permute-start.13 = (f32[128,128]{1,0:T(8,128)S(1)}, f32[128,128]{1,0:T(8,128)S(1)}, u32[]{:S(2)}, u32[]{:S(2)}) collective-permute-start(f32[128,128]{1,0:T(8,128)S(1)} %get-tuple-element.72), channel_id=1, source_target_pairs={{8,16},{16,8},{9,17},{17,9},{10,18},{18,10},{11,19},{19,11},{12,20... | collective-permute-start | bytes 196616 | tf_op jit(solution)/shard_map/ppermute | solution.py:68
  83.6 3.0 %collective-permute-done.9.refs_7_ = f32[960,128]{1,0:T(8,128)S(1)} collective-permute-done((f32[960,128]{1,0:T(8,128)S(1)}, f32[960,128]{1,0:T(8,128)S(1)}, u32[]{:S(2)}, u32[]{:S(2)}) %collective-permute-start.9) | collective-permute-done | bytes 491552 | tf_op jit(solution)/shard_map/ppermute | solution.py:68
  86.6 0.0 copy-done.3
  86.6 0.0 copy-done.6
  86.6 0.0 copy-done.12
  86.6 11.9 %grid_step.1 = (f32[16,32,256]{2,1,0:T(8,128)}, f32[16,32,256]{2,1,0:T(8,128)}, f32[1024,128]{1,0:T(8,128)S(1)}) custom-call(s32[256]{0:T(256)S(1)} %copy-done.12, f32[256,128]{1,0:T(8,128)S(1)} %copy-done.6, f32[16,32,256]{2,1,0:T(8,128)S(1)} %copy-done, f32[16,32,256]{2,1,0:T(8,128)S(1)} %copy-done.3, f32[16,32,256]{2,1,0:T(8,128)S(1)} %copy-done.4, ...), custom_call_target="tpu_custom_call" | custom-call | flops 31948800 | bytes 8388608 | tf_op jit(solution)/shard_map/grid_step/pallas_call | solution.py:781
  98.5 0.0 collective-permute-done.10
  98.5 0.0 collective-permute-done.11
  98.5 0.0 collective-permute-done.12
  98.5 0.0 collective-permute-done.13
  98.5 0.0 copy-start.11
  98.6 0.7 copy-done.11
  99.2 2.6 %gather_forces.1 = f32[3,32768]{1,0:T(4,128)} custom-call(s32[7,32]{1,0:T(8,128)S(1)} %copy-done.11, f32[256,4,128]{2,1,0:T(4,128)S(1)} %bitcast.17, f32[256,4,128]{2,1,0:T(4,128)S(1)} %bitcast.19, f32[32,4,128]{2,1,0:T(4,128)S(1)} %bitcast.20, f32[240,4,128]{2,1,0:T(4,128)S(1)} %bitcast.15, f32[240,4,128]{2,1,0:T(4,128)S(1)} %bitcast.16, ...), custom_call_target="tpu_custom_call" | custom-call | tf_op jit(solution)/shard_map/gather_forces/pallas_call | solution.py:833
Async XLA Ops:
  4.9 8.4 %collective-permute-start = (f32[128,128]{1,0:T(8,128)}, f32[128,128]{1,0:T(8,128)S(1)}, u32[]{:S(2)}, u32[]{:S(2)}) collective-permute-start(f32[128,128]{1,0:T(8,128)} %get-tuple-element.42), channel_id=1, source_target_pairs={{0,1},{1,0},{2,3},{3,2},{4,5},{5,4},{6,7},{7,6},{8,9},{9,8},{10,11... | collective-permute-start | bytes 196616 | tf_op jit(solution)/shard_map/ppermute | solution.py:68
  5.6 14.3 %collective-permute-start.1 = (f32[128,128]{1,0:T(8,128)}, f32[128,128]{1,0:T(8,128)S(1)}, u32[]{:S(2)}, u32[]{:S(2)}) collective-permute-start(f32[128,128]{1,0:T(8,128)} %get-tuple-element.43), channel_id=1, source_target_pairs={{1,2},{2,1},{3,4},{4,3},{5,6},{6,5},{9,10},{10,9},{11,12},{12,11},... | collective-permute-start | bytes 196616 | tf_op jit(solution)/shard_map/ppermute | solution.py:68
  8.7 11.2 %collective-permute-start.2 = (f32[128,128]{1,0:T(8,128)}, f32[128,128]{1,0:T(8,128)S(1)}, u32[]{:S(2)}, u32[]{:S(2)}) collective-permute-start(f32[128,128]{1,0:T(8,128)} %get-tuple-element.44), channel_id=1, source_target_pairs={{0,2},{1,3},{2,0},{3,1},{4,6},{5,7},{6,4},{7,5},{8,10},{9,11},{10,... | collective-permute-start | bytes 196616 | tf_op jit(solution)/shard_map/ppermute | solution.py:68
  9.0 11.0 %collective-permute-start.3 = (f32[128,128]{1,0:T(8,128)}, f32[128,128]{1,0:T(8,128)S(1)}, u32[]{:S(2)}, u32[]{:S(2)}) collective-permute-start(f32[128,128]{1,0:T(8,128)} %get-tuple-element.45), channel_id=1, source_target_pairs={{2,4},{3,5},{4,2},{5,3},{10,12},{11,13},{12,10},{13,11},{18,20},{1... | collective-permute-start | bytes 196616 | tf_op jit(solution)/shard_map/ppermute | solution.py:68
  12.0 7.9 %collective-permute-start.4 = (f32[128,128]{1,0:T(8,128)}, f32[128,128]{1,0:T(8,128)S(1)}, u32[]{:S(2)}, u32[]{:S(2)}) collective-permute-start(f32[128,128]{1,0:T(8,128)} %get-tuple-element.46), channel_id=1, source_target_pairs={{0,8},{8,0},{16,24},{24,16},{1,9},{9,1},{17,25},{25,17},{2,10},{10... | collective-permute-start | bytes 196616 | tf_op jit(solution)/shard_map/ppermute | solution.py:68
  13.3 6.7 %collective-permute-start.5 = (f32[128,128]{1,0:T(8,128)}, f32[128,128]{1,0:T(8,128)S(1)}, u32[]{:S(2)}, u32[]{:S(2)}) collective-permute-start(f32[128,128]{1,0:T(8,128)} %get-tuple-element.47), channel_id=1, source_target_pairs={{8,16},{16,8},{9,17},{17,9},{10,18},{18,10},{11,19},{19,11},{12,20... | collective-permute-start | bytes 196616 | tf_op jit(solution)/shard_map/ppermute | solution.py:68
  15.4 8.7 %copy-start.5 = (f32[256,4,128]{2,1,0:T(4,128)S(1)}, f32[256,4,128]{2,1,0:T(4,128)}, u32[]{:S(2)}) copy-start(f32[256,4,128]{2,1,0:T(4,128)} %get-tuple-element.40) | copy-start | bytes 1572868
  15.4 8.7 %copy-start.7 = (bf16[128,1024]{1,0:T(8,128)(2,1)S(1)}, bf16[128,1024]{1,0:T(8,128)(2,1)}, u32[]{:S(2)}) copy-start(bf16[128,1024]{1,0:T(8,128)(2,1)} %constant.6.clone.refs_0_) | copy-start | bytes 786436
  15.4 8.7 %copy-start.8 = (bf16[256,128]{1,0:T(8,128)(2,1)S(1)}, bf16[256,128]{1,0:T(8,128)(2,1)}, u32[]{:S(2)}) copy-start(bf16[256,128]{1,0:T(8,128)(2,1)} %constant.7.clone.refs_1_) | copy-start | bytes 196612
  15.4 8.7 %copy-start.9 = (f32[128,128]{1,0:T(8,128)S(1)}, f32[128,128]{1,0:T(8,128)}, u32[]{:S(2)}) copy-start(f32[128,128]{1,0:T(8,128)} %get-tuple-element.51.refs_4_) | copy-start | bytes 196612
  15.4 8.7 %copy-start.10 = (bf16[128,128]{1,0:T(8,128)(2,1)S(1)}, bf16[128,128]{1,0:T(8,128)(2,1)}, u32[]{:S(2)}) copy-start(bf16[128,128]{1,0:T(8,128)(2,1)} %constant.8.clone.refs_2_) | copy-start | bytes 98308
  19.9 4.2 %copy-start.14 = (s32[8,128]{1,0:T(8,128)S(1)}, s32[8,128]{1,0:T(8,128)}, u32[]{:S(2)}) copy-start(s32[8,128]{1,0:T(8,128)} %get-tuple-element.39) | copy-start | bytes 12292
  20.0 4.2 %copy-start.13 = (s32[1024]{0:T(1024)S(1)}, s32[1024]{0:T(1024)}, u32[]{:S(2)}) copy-start(s32[1024]{0:T(1024)} %own_rows_ref.1) | copy-start | bytes 12292
  20.0 51.4 %collective-permute-start.6 = (f32[28,32,128]{2,1,0:T(8,128)}, f32[28,32,128]{2,1,0:T(8,128)S(1)}, u32[]{:S(2)}, u32[]{:S(2)}) collective-permute-start(f32[28,32,128]{2,1,0:T(8,128)} %get-tuple-element.61), channel_id=1, source_target_pairs={{0,8},{8,0},{16,24},{24,16},{1,9},{9,1},{17,25},{25,17},{2,10},{10... | collective-permute-start | bytes 1376264 | tf_op jit(solution)/shard_map/ppermute | solution.py:68
  20.0 51.4 %collective-permute-start.7 = (f32[28,32,128]{2,1,0:T(8,128)}, f32[28,32,128]{2,1,0:T(8,128)S(1)}, u32[]{:S(2)}, u32[]{:S(2)}) collective-permute-start(f32[28,32,128]{2,1,0:T(8,128)} %get-tuple-element.62), channel_id=1, source_target_pairs={{8,16},{16,8},{9,17},{17,9},{10,18},{18,10},{11,19},{19,11},{12,20... | collective-permute-start | bytes 1376264 | tf_op jit(solution)/shard_map/ppermute | solution.py:68
  24.2 47.2 %copy-start = (f32[16,32,256]{2,1,0:T(8,128)S(1)}, f32[16,32,256]{2,1,0:T(8,128)}, u32[]{:S(2)}) copy-start(f32[16,32,256]{2,1,0:T(8,128)} %refs_2_.2) | copy-start | bytes 1572868
  24.2 47.2 %copy-start.1 = (f32[16,32,256]{2,1,0:T(8,128)S(1)}, f32[16,32,256]{2,1,0:T(8,128)}, u32[]{:S(2)}) copy-start(f32[16,32,256]{2,1,0:T(8,128)} %refs_5_.1) | copy-start | bytes 1572868
  71.4 1.0 %copy-start.2 = (f32[16,32,256]{2,1,0:T(8,128)S(1)}, f32[16,32,256]{2,1,0:T(8,128)}, u32[]{:S(2)}) copy-start(f32[16,32,256]{2,1,0:T(8,128)} %get-tuple-element.59.refs_1_.refs_3_) | copy-start | bytes 1572868
  72.5 1.0 %copy-start.4 = (f32[16,32,256]{2,1,0:T(8,128)S(1)}, f32[16,32,256]{2,1,0:T(8,128)}, u32[]{:S(2)}) copy-start(f32[16,32,256]{2,1,0:T(8,128)} %get-tuple-element.60.refs_2_.refs_4_) | copy-start | bytes 1572868
  73.5 13.1 %copy-start.3 = (f32[16,32,256]{2,1,0:T(8,128)S(1)}, f32[16,32,256]{2,1,0:T(8,128)}, u32[]{:S(2)}) copy-start(f32[16,32,256]{2,1,0:T(8,128)} %get-tuple-element.59.refs_1_.refs_3_) | copy-start | bytes 1572868
  73.5 13.1 %copy-start.6 = (f32[256,128]{1,0:T(8,128)S(1)}, f32[256,128]{1,0:T(8,128)}, u32[]{:S(2)}) copy-start(f32[256,128]{1,0:T(8,128)} %get-tuple-element.48.masked_hbm.refs_1_) | copy-start | bytes 393220
  73.7 7.4 %collective-permute-start.8 = (f32[960,128]{1,0:T(8,128)S(1)}, f32[960,128]{1,0:T(8,128)S(1)}, u32[]{:S(2)}, u32[]{:S(2)}) collective-permute-start(f32[960,128]{1,0:T(8,128)S(1)} %get-tuple-element.65), channel_id=1, source_target_pairs={{0,1},{1,0},{2,3},{3,2},{4,5},{5,4},{6,7},{7,6},{8,9},{9,8},{10,11... | collective-permute-start | bytes 1474568 | tf_op jit(solution)/shard_map/ppermute | solution.py:68
  75.8 10.8 %collective-permute-start.9 = (f32[960,128]{1,0:T(8,128)S(1)}, f32[960,128]{1,0:T(8,128)S(1)}, u32[]{:S(2)}, u32[]{:S(2)}) collective-permute-start(f32[960,128]{1,0:T(8,128)S(1)} %get-tuple-element.66), channel_id=1, source_target_pairs={{1,2},{2,1},{3,4},{4,3},{5,6},{6,5},{9,10},{10,9},{11,12},{12,11},... | collective-permute-start | bytes 1474568 | tf_op jit(solution)/shard_map/ppermute | solution.py:68
  77.7 20.8 %collective-permute-start.10 = (f32[128,128]{1,0:T(8,128)S(1)}, f32[128,128]{1,0:T(8,128)S(1)}, u32[]{:S(2)}, u32[]{:S(2)}) collective-permute-start(f32[128,128]{1,0:T(8,128)S(1)} %get-tuple-element.69), channel_id=1, source_target_pairs={{0,2},{1,3},{2,0},{3,1},{4,6},{5,7},{6,4},{7,5},{8,10},{9,11},{10,... | collective-permute-start | bytes 196616 | tf_op jit(solution)/shard_map/ppermute | solution.py:68
  79.1 19.4 %collective-permute-start.11 = (f32[128,128]{1,0:T(8,128)S(1)}, f32[128,128]{1,0:T(8,128)S(1)}, u32[]{:S(2)}, u32[]{:S(2)}) collective-permute-start(f32[128,128]{1,0:T(8,128)S(1)} %get-tuple-element.70), channel_id=1, source_target_pairs={{2,4},{3,5},{4,2},{5,3},{10,12},{11,13},{12,10},{13,11},{18,20},{1... | collective-permute-start | bytes 196616 | tf_op jit(solution)/shard_map/ppermute | solution.py:68
  81.0 5.6 %copy-start.12 = (s32[256]{0:T(256)S(1)}, s32[256]{0:T(256)}, u32[]{:S(2)}) copy-start(s32[256]{0:T(256)} %refs_0_.4) | copy-start | bytes 3076
  81.0 17.5 %collective-permute-start.12 = (f32[128,128]{1,0:T(8,128)S(1)}, f32[128,128]{1,0:T(8,128)S(1)}, u32[]{:S(2)}, u32[]{:S(2)}) collective-permute-start(f32[128,128]{1,0:T(8,128)S(1)} %get-tuple-element.71), channel_id=1, source_target_pairs={{0,8},{8,0},{16,24},{24,16},{1,9},{9,1},{17,25},{25,17},{2,10},{10... | collective-permute-start | bytes 196616 | tf_op jit(solution)/shard_map/ppermute | solution.py:68
  81.1 17.4 %collective-permute-start.13 = (f32[128,128]{1,0:T(8,128)S(1)}, f32[128,128]{1,0:T(8,128)S(1)}, u32[]{:S(2)}, u32[]{:S(2)}) collective-permute-start(f32[128,128]{1,0:T(8,128)S(1)} %get-tuple-element.72), channel_id=1, source_target_pairs={{8,16},{16,8},{9,17},{17,9},{10,18},{18,10},{11,19},{19,11},{12,20... | collective-permute-start | bytes 196616 | tf_op jit(solution)/shard_map/ppermute | solution.py:68
  98.5 0.7 copy-start.11
